TPU v7x, 32 devices: a whole 2x2x4 slice. The times are simulated.
32 devices in a mesh: dp: 4 (over y, x), grid: 8 (over z, core).
Axes of the slice: x: 2, y: 2, z: 4, core: 2. Of those that a mesh axis runs over, the one named last changes fastest.
Arguments:
- embeddings: bfloat16 [10240, 768], P(('dp', 'grid')), may hold values from -6 to 6
- cluster: int32 [10240, 1], P(('dp', 'grid')), may hold values from 0 to 3; in each aligned block of 320 rows (0 to 319, 320 to 639, ...) at most 160 rows name the same one
- order_key: int32 [10240], P(('dp', 'grid')), may hold values from 0 to 10239, each once
Outputs:
- best: float32 [10240], P(('dp', 'grid'))
Inputs may be any that keep to these rules, and one draw needn't show every extreme that they name: In the rows of one device at most 160 rows name one cluster, and on some device one cluster is named by exactly 160 rows; every cluster is named. `order_key`: each number of 0 to 10239 appears once.
All inputs are finite; a program needn't handle non-finite values.
Results may differ from a plain program's by a relative error of at most 0.0012.
Values may be sent and summed in bfloat16 or wider, within the bound.
No kernel may reach another device: no remote copies, remote signals or barrier semaphores. Data moves between devices by JAX's collectives and lax.ppermute only.
A program may use at most 128 MiB of HBM per device.

v0:
```python
import jax
import jax.numpy as jnp
from jax import lax
from jax.sharding import PartitionSpec as P

epsilon = 1e-06


def shards(embeddings, cluster, order_key):
    rows = embeddings.shape[0]
    width = embeddings.shape[1]
    owners = lax.axis_size("dp")
    values = embeddings.astype(jnp.float32)
    units = (values * lax.rsqrt(jnp.sum(values * values, axis=1, keepdims=True) + epsilon)).astype(
        jnp.bfloat16
    )
    labels = cluster[:, 0]
    depth = rows // 2
    onehot = (labels[:, None] == jnp.arange(owners, dtype=jnp.int32)[None, :]).astype(jnp.int32)
    before = jnp.cumsum(onehot, axis=0) - onehot
    places = jnp.sum(before * onehot, axis=1)
    flat = labels * depth + places
    send_units = (
        jnp.zeros((owners * depth, width), jnp.bfloat16)
        .at[flat]
        .set(units)
        .reshape(owners, depth, width)
    )
    send_keys = (
        jnp.full((owners * depth,), -1, jnp.int32).at[flat].set(order_key).reshape(owners, depth)
    )
    got_units, got_keys = (
        lax.all_to_all(send_units, "dp", split_axis=0, concat_axis=0, tiled=True),
        lax.all_to_all(send_keys, "dp", split_axis=0, concat_axis=0, tiled=True),
    )
    mine = got_units.reshape(owners * depth, width)
    mine_keys = got_keys.reshape(owners * depth)
    initial = jnp.full((owners * depth,), -1.0, jnp.float32)
    other_units = lax.all_gather(mine, "grid", axis=0, tiled=True)
    other_keys = lax.all_gather(mine_keys, "grid", axis=0, tiled=True)
    sims = jnp.einsum("qe,ke->qk", mine, other_units, preferred_element_type=jnp.float32)
    allowed = (other_keys[None, :] >= 0) & (other_keys[None, :] < mine_keys[:, None])
    scores = jnp.maximum(initial, jnp.max(jnp.where(allowed, sims, jnp.float32(-1.0)), axis=1))
    returned = lax.all_to_all(
        scores.reshape(owners, depth), "dp", split_axis=0, concat_axis=0, tiled=True
    )
    return returned.reshape(owners * depth)[flat]


def solution(mesh):
    placed = (P(("dp", "grid"), None), P(("dp", "grid"), None), P(("dp", "grid")))
    return jax.shard_map(
        shards, mesh=mesh, in_specs=placed, out_specs=P(("dp", "grid")), check_vma=False
    )
```

profile of v0, /device:TPU:0, one launch (start us, length us, event | category | flops | bytes accessed | tf_op | source)
XLA Modules:
  0.0 137.3 jit_solution(4906086970229508415)
XLA Ops:
  6.5 0.0 all-gather.3.cloned.1.call-start
  6.5 0.7 reduce
  7.3 1.2 reduce-window.6
  8.5 0.2 slice_reduce_fusion
  8.7 0.2 reduce-window.9
  8.9 0.1 add_bitcast_fusion
  9.0 0.7 fusion.10
  9.7 1.2 fusion
  10.9 2.8 %scatter_custom_fusion.1 = bf16[640,768]{1,0:T(8,128)(2,1)S(1)} fusion(s32[320]{0:T(512)S(1)} %fusion.10, bf16[320,768]{1,0:T(8,128)(2,1)} %param.3, f32[320]{0:T(512)S(1)} %add_rsqrt_fusion, bf16[]{:T(256)} %constant.6.clone.1), kind=kCustom, calls=%fused_computation.8 | custom fusion | flops 737280 | bytes 1476610 | tf_op jit(solution)/shard_map/scatter | solution.py:26
  13.7 18.7 %all_to_all.20 = bf16[4,160,768]{2,1,0:T(8,128)(2,1)} all-to-all(bf16[4,160,768]{2,1,0:T(8,128)(2,1)S(1)} %bitcast.18), channel_id=1, replica_groups=mesh['dp'=4,'grid'=8] {'dp'}, dimensions={0} | all-to-all | bytes 1966080 | tf_op jit(solution)/shard_map/all_to_all | solution.py:33
  32.4 0.0 all-gather.3.cloned.1.call-update
  32.4 3.1 %scatter_custom_fusion = s32[640]{0:T(1024)S(1)} fusion(s32[320]{0:T(512)S(1)} %fusion.10, s32[320]{0:T(512)} %param.5, s32[]{:T(128)} %constant.10.clone.1), kind=kCustom, calls=%fused_computation.25 | custom fusion | bytes 3072 | tf_op jit(solution)/shard_map/scatter | solution.py:30
  35.5 0.1 all_to_all.13
  35.6 7.0 %all_to_all.21 = s32[4,1,160]{2,1,0:T(1,128)S(1)} all-to-all(s32[4,1,160]{2,1,0:T(1,128)S(1)} %all_to_all.13), channel_id=1, replica_groups=mesh['dp'=4,'grid'=8] {'dp'}, dimensions={0} | all-to-all | bytes 5120 | tf_op jit(solution)/shard_map/all_to_all | solution.py:34
  42.6 0.1 reshape.88
  42.7 0.1 reshape.59
  42.8 15.2 %all-gather = s32[8,1,640]{2,1,0:T(1,128)S(1)} all-gather(s32[1,1,640]{2,1,0:T(1,128)S(1)} %reshape.88), channel_id=1, replica_groups=mesh['dp'=4,'grid'=8] {'grid'}, dimensions={0}, use_global_device_ids=true | all-gather | bytes 23040 | tf_op jit(solution)/shard_map/all_gather | solution.py:40
  58.1 52.0 %all-gather.3.cloned.1.call-done = bf16[5120,768]{1,0:T(8,128)(2,1)} async-done(((bf16[640,768]{1,0:T(8,128)(2,1)}), bf16[5120,768]{1,0:T(8,128)(2,1)}) %all-gather.3.cloned.1.call-update) | async-done | bytes 7864336 | tf_op jit(solution)/shard_map/all_gather | solution.py:39
  110.0 8.5 %select_reduce_fusion = f32[640]{0:T(1024)S(1)} fusion(bf16[640,768]{1,0:T(8,128)(2,1)} %bitcast.17, bf16[5120,768]{1,0:T(8,128)(2,1)} %all-gather.3.cloned.1.call-done, s32[5120]{0:T(1024)S(1)} %bitcast.20, s32[640]{0:T(1024)S(1)} %reshape.59, pred[5120]{0:T(1024)(128)(4,1)S(1)} %broadcast_compare_fusion), kind=kOutput, calls=%fused_computation.3 | convolution fusion | flops 5046271488 | bytes 8878080 | tf_op jit(solution)/shard_map/qe,ke->qk/dot_general | solution.py:41
  118.6 0.7 max_broadcast_in_dim.15
  119.2 3.6 %all-to-all-start.2 = ((f32[4,1,160]{2,1,0:T(1,128)}), f32[4,1,160]{2,1,0:T(1,128)S(1)}, u32[]{:S(2)}, u32[]{:S(2)}) async-start(f32[4,1,160]{2,1,0:T(1,128)} %max_broadcast_in_dim.15), calls=%async_computation.2 | async-start | bytes 8192 | tf_op jit(solution)/shard_map/all_to_all | solution.py:44
  122.9 4.7 %all-to-all-done.2 = f32[4,1,160]{2,1,0:T(1,128)S(1)} async-done(((f32[4,1,160]{2,1,0:T(1,128)}), f32[4,1,160]{2,1,0:T(1,128)S(1)}, u32[]{:S(2)}, u32[]{:S(2)}) %all-to-all-start.2) | async-done | bytes 2592 | tf_op jit(solution)/shard_map/all_to_all | solution.py:44
  127.6 0.1 reshape.62
  127.6 2.8 %gather_fusion = f32[320]{0:T(512)} fusion(f32[640]{0:T(1024)S(1)} %reshape.62, s32[1024]{0:T(1024)S(1)} %pad_clamp_fusion), kind=kCustom, calls=%fused_computation | custom fusion | bytes 3840 | tf_op jit(solution)/shard_map/gather | solution.py:47
  (11 shorter events, 0.1 us)
Async XLA Ops:
  6.5 103.5 %all-gather.3.cloned.1.call-start = ((), (), s32[]{:S(2)}) async-start(), calls=%async_computation.3 | async-start | bytes 8847360 | tf_op jit(solution)/shard_map/all_gather | solution.py:39
  119.2 8.3 %all-to-all-start.2 = ((f32[4,1,160]{2,1,0:T(1,128)}), f32[4,1,160]{2,1,0:T(1,128)S(1)}, u32[]{:S(2)}, u32[]{:S(2)}) async-start(f32[4,1,160]{2,1,0:T(1,128)} %max_broadcast_in_dim.15), calls=%async_computation.2 | async-start | bytes 8192 | tf_op jit(solution)/shard_map/all_to_all | solution.py:44
Sparse Core Ops, SparseCore 0:
  32.6 77.4 all-gather.2
where the time goes:
time: 138 us; the launch traced here: 137 us
  waiting for transfers between devices  56.6 us (41%)
  blocking collectives  40.9 us (30%)
  between operations  13.5 us (10%)
  matrix products  8.51 us (6%)
  local copies, waits for them, and re-layouts  7.11 us (5%)
  other arithmetic  7 us (5%)
  starting transfers between devices  3.63 us (3%)
    all_gather x1, waiting for transfers between devices, shards(): other_units = lax.all_gather(mine, 'grid', axis=0, tiled=True)  52 us
    all_to_all x1, blocking collectives, shards(): lax.all_to_all(send_units, 'dp', split_axis=0, concat_axis=0, tiled=True)  18.7 us
    all_gather x1, blocking collectives, shards(): other_keys = lax.all_gather(mine_keys, 'grid', axis=0, tiled=True)  15.2 us
    dot_general x1, matrix products, shards(): jnp.einsum('qe,ke->qk', mine, other_units, preferred_element_type=jnp.flo...  8.51 us
    all_to_all x1, blocking collectives, shards(): lax.all_to_all(send_keys, 'dp', split_axis=0, concat_axis=0, tiled=True)  7.01 us
    all_to_all x1, waiting for transfers between devices, shards(): lax.all_to_all(scores.reshape(owners, depth), 'dp', split_axis=0, concat_...  4.67 us
    all_to_all x1, starting transfers between devices, shards(): lax.all_to_all(scores.reshape(owners, depth), 'dp', split_axis=0, concat_...  3.63 us
    scatter x1, local copies, waits for them, and re-layouts, shards(): jnp.full((owners * depth,), -1, jnp.int32).at[flat].set(order_key)  3.08 us
  transfers between devices with their start and end apart: 2, of which 2 were waited for; matrix products, arithmetic and copies ran while one was open for 2% of the time, Pallas kernels for 0%

commit v1 on v0

v1 whole, which is shorter than its diff:
```python
import functools

import jax
import jax.numpy as jnp
from jax import lax
from jax.experimental import pallas as pl
from jax.experimental.pallas import tpu as pltpu
from jax.sharding import PartitionSpec as P

EPSILON = 1e-06
EXTRA = 16
LANES = 128
BOTH = ("dp", "grid")


def up(value, multiple):
    return -(-value // multiple) * multiple


def turned_to_row(column, rows):
    padded = up(rows, LANES)
    if padded != rows:
        column = jnp.concatenate([column, jnp.zeros((padded - rows, LANES), column.dtype)], axis=0)
    return column.T[0:1, :rows]


def turned_to_column(row, rows):
    return jnp.broadcast_to(row, (LANES, row.shape[1])).T[:rows]


def codes(block, rows, span):
    parts = block[rows : rows + EXTRA, : up(rows, LANES)].astype(jnp.float32)
    return parts[2:3] * (4.0 * span) + parts[0:1] * 256.0 + parts[1:2]


def prepare_kernel(embeddings, cluster, order_key, block):
    rows, width = embeddings.shape
    values = embeddings[...].astype(jnp.float32)
    scale = lax.rsqrt(jnp.sum(values * values, axis=1, keepdims=True) + EPSILON)
    block[0:rows, :] = (values * scale).astype(jnp.bfloat16)
    labels = turned_to_row(
        jnp.broadcast_to(cluster[...].astype(jnp.float32), (rows, LANES)), rows
    )
    keys = order_key[...]
    high = (keys >> 8).astype(jnp.float32)
    low = (keys & 255).astype(jnp.float32)
    parts = jnp.concatenate(
        [high, low, labels + 1.0, jnp.zeros((EXTRA - 3, rows), jnp.float32)], axis=0
    )
    parts = jnp.concatenate([parts, jnp.zeros((EXTRA, width - rows), jnp.float32)], axis=1)
    block[rows : rows + EXTRA, :] = parts.astype(jnp.bfloat16)


def prepare(embeddings, cluster, order_key):
    rows, width = embeddings.shape
    return pl.pallas_call(
        prepare_kernel,
        out_shape=jax.ShapeDtypeStruct((rows + EXTRA, width), jnp.bfloat16),
        compiler_params=pltpu.CompilerParams(vmem_limit_bytes=16 << 20),
        cost_estimate=pl.CostEstimate(
            flops=4 * rows * width, bytes_accessed=4 * rows * width, transcendentals=rows
        ),
    )(embeddings, cluster, order_key.reshape(1, rows))


def similarities(ours, held):
    return lax.dot_general(
        ours, held, (((1,), (1,)), ((), ())), preferred_element_type=jnp.float32
    )


def lane_tiles_max(values):
    best = values[:, :LANES]
    for at in range(LANES, values.shape[1], LANES):
        best = jnp.maximum(best, values[:, at : at + LANES])
    return best


def row_from_partial(partial, rows):
    padded = up(rows, LANES)
    if padded != rows:
        partial = jnp.concatenate(
            [partial, jnp.zeros((padded - rows, LANES), partial.dtype)], axis=0
        )
    return jnp.max(partial.T, axis=0, keepdims=True)[:, :rows]


def meet(block, rows, span, held, held_codes, to_block, to_held):
    total = held.shape[0]
    step = 64
    column = turned_to_column(codes(block, rows, span), rows)
    partials = []
    best_held = jnp.full((8, total), -1.0, jnp.float32)
    for at in range(0, rows, step):
        sims = similarities(block[at : at + step, :], held[...])
        wide = jnp.concatenate([column[at : at + step]] * (total // LANES), axis=1)
        gap = wide - held_codes
        if to_block and to_held:
            sims = jnp.where(jnp.abs(gap) < span, sims, -1.0)
            later = gap > 0.0
            partials.append(lane_tiles_max(jnp.where(later, sims, -1.0)))
            other = jnp.where(later, -1.0, sims)
        elif to_block:
            partials.append(
                lane_tiles_max(jnp.where((gap > 0.0) & (gap < span), sims, -1.0))
            )
        else:
            other = jnp.where((gap < 0.0) & (gap > -span), sims, -1.0)
        if to_held:
            for row in range(0, step, 8):
                best_held = jnp.maximum(best_held, other[row : row + 8])
    mine = row_from_partial(jnp.concatenate(partials, axis=0), rows) if to_block else None
    return mine, jnp.max(best_held, axis=0, keepdims=True) if to_held else None


def plane_kernel(rows, span, *refs):
    blocks, partner, held, held_codes, best = refs[:-4], refs[-4], refs[-3], refs[-2], refs[-1]
    for at, block in enumerate(blocks):
        held[at * rows : (at + 1) * rows, :] = block[0:rows, :]
    row = jnp.concatenate([codes(block, rows, span)[:, :rows] for block in blocks], axis=1)
    held_codes[...] = row
    mine, _ = meet(blocks[0], rows, span, held, row, True, False)
    _, theirs = meet(partner, rows, span, held, row, False, True)
    best[...] = jnp.concatenate(
        [jnp.maximum(theirs[:, :rows], mine), theirs[:, rows:]], axis=1
    )


def plane(blocks, partner, rows, span):
    width = partner.shape[1]
    total = len(blocks) * rows
    row = jax.ShapeDtypeStruct((1, total), jnp.float32)
    return pl.pallas_call(
        functools.partial(plane_kernel, rows, span),
        out_shape=(jax.ShapeDtypeStruct((total, width), jnp.bfloat16), row, row),
        compiler_params=pltpu.CompilerParams(vmem_limit_bytes=32 << 20),
        cost_estimate=pl.CostEstimate(
            flops=4 * rows * total * width, bytes_accessed=4 * total * width, transcendentals=0
        ),
    )(*blocks, partner)


def line_kernel(rows, span, held, held_codes, best, block, new_best, block_best):
    mine, theirs = meet(block, rows, span, held, held_codes[...], True, True)
    new_best[...] = jnp.maximum(best[...], theirs)
    block_best[...] = mine


def line(held, held_codes, best, block, rows, span):
    total, width = held.shape
    return pl.pallas_call(
        functools.partial(line_kernel, rows, span),
        out_shape=(
            jax.ShapeDtypeStruct((1, total), jnp.float32),
            jax.ShapeDtypeStruct((1, rows), jnp.float32),
        ),
        compiler_params=pltpu.CompilerParams(vmem_limit_bytes=32 << 20),
        cost_estimate=pl.CostEstimate(
            flops=2 * rows * total * width, bytes_accessed=2 * total * width, transcendentals=0
        ),
    )(held, held_codes, best, block)


def line_rounds(chips):
    if chips == 4:
        return [[(0, 2), (3, 1), (1, 0)], [(0, 3), (3, 2), (2, 1)]]
    rounds = []
    for shift in range(1, chips // 2 + 1):
        senders = chips // 2 if 2 * shift == chips else chips
        rounds.append([(s, (s + shift) % chips) for s in range(senders)])
    return rounds


def solution(mesh):
    groups, members = mesh.shape["dp"], mesh.shape["grid"]
    chips = members // 2

    def moves(pairs):
        return [(a * members + b, c * members + d) for (a, b), (c, d) in pairs]

    def back(pairs):
        return [(target, source) for source, target in pairs]

    everyone = [(p, g) for p in range(groups) for g in range(members)]
    other_core = moves([((p, g), (p, g ^ 1)) for p, g in everyone])

    def other_group(p, shift):
        return p ^ shift if groups & (groups - 1) == 0 else (p + shift) % groups

    across = [
        moves([((p, g), (other_group(p, shift), g)) for p, g in everyone])
        for shift in range(1, groups)
    ]
    rounds = line_rounds(chips)

    def along(pairs, cross):
        return moves(
            [
                ((p, 2 * s + c), (p, 2 * t + (c ^ cross)))
                for p in range(groups)
                for s, t in pairs
                for c in range(2)
            ]
        )

    def shards(embeddings, cluster, order_key):
        rows = embeddings.shape[0]
        span = 256
        while span < rows * groups * members:
            span *= 2
        chip = lax.axis_index("grid") // 2
        block = prepare(embeddings, cluster, order_key)
        partner = lax.ppermute(block, BOTH, other_core)
        from_line = [lax.ppermute(block, BOTH, along(pairs, 0)) for pairs in rounds]
        from_plane = [lax.ppermute(block, BOTH, pairs) for pairs in across]
        held, held_codes, best = plane([block] + from_plane, partner, rows, span)
        results = []
        for pairs, near in zip(rounds, from_line):
            far = lax.ppermute(near, BOTH, other_core)
            senders = functools.reduce(jnp.logical_or, [chip == s for s, _ in pairs])
            for cross, arrived in ((0, near), (1, far)):
                best, found = line(held, held_codes, best, arrived, rows, span)
                found = lax.ppermute(found, BOTH, back(along(pairs, cross)))
                results.append(jnp.where(senders, found, -1.0))
        for at, pairs in enumerate(across):
            part = best[:, (at + 1) * rows : (at + 2) * rows]
            results.append(lax.ppermute(part, BOTH, back(pairs)))
        return functools.reduce(jnp.maximum, results, best[:, :rows]).reshape(rows)

    placed = (P(BOTH, None), P(BOTH, None), P(BOTH))
    return jax.shard_map(
        shards, mesh=mesh, in_specs=placed, out_specs=P(BOTH), check_vma=False
    )
```

time: 138 us -> 73.3 us (0.53)
  blocking collectives: 40.9 us -> 0 us
  waiting for transfers between devices: 56.6 us -> 23.6 us
  starting transfers between devices: 3.63 us -> 26.7 us
  Pallas kernels: 0 us -> 19.3 us
  between operations: 13.5 us -> 0.18 us
  matrix products: 8.51 us -> 0 us
  other arithmetic: 7 us -> 0.6 us
  local copies, waits for them, and re-layouts: 7.11 us -> 2.6 us
    all_gather x1 -> x0, waiting for transfers between devices: 52 us -> none  [shards(): other_units = lax.all_gather(mine, 'grid', axis=0, tiled=True)]
    ppermute x0 -> x15, starting transfers between devices: none -> 26.7 us  [the longest x4 10.4 us: shards(): found = lax.ppermute(found, BOTH, back(along(pairs, cross)))]
    all_to_all x2 -> x0, blocking collectives: 25.7 us -> none  [the longest x1 18.7 us: shards(): lax.all_to_all(send_units, 'dp', split_axis=0, concat_axis=0, tiled=True)]
    ppermute x0 -> x15, waiting for transfers between devices: none -> 23.6 us  [the longest x2 13.7 us: shards(): from_line = [lax.ppermute(block, BOTH, along(pairs, 0)) for pairs in rounds]]
    pallas_call x0 -> x6, Pallas kernels: none -> 19.3 us  [the longest x4 12.9 us: line(): pl.pallas_call(functools.partial(line_kernel, rows, span), out_shape=(jax...]
    all_gather x1 -> x0, blocking collectives: 15.2 us -> none  [shards(): other_keys = lax.all_gather(mine_keys, 'grid', axis=0, tiled=True)]
    dot_general x1 -> x0, matrix products: 8.51 us -> none  [shards(): jnp.einsum('qe,ke->qk', mine, other_units, preferred_element_type=jnp.flo...]
    all_to_all x1 -> x0, waiting for transfers between devices: 4.67 us -> none  [shards(): lax.all_to_all(scores.reshape(owners, depth), 'dp', split_axis=0, concat_...]
  transfers between devices with their start and end apart: 2 -> 15, of which waited for: 2 -> 6; matrix products, arithmetic and copies ran while one was open for 2% -> 0% of each run, Pallas kernels for 0% -> 26%
where the time goes in v1:
time: 73.3 us; the launch traced here: 73 us
  starting transfers between devices  26.7 us (36%)
  waiting for transfers between devices  23.6 us (32%)
  Pallas kernels  19.3 us (26%)
  local copies, waits for them, and re-layouts  2.6 us (4%)
    ppermute x2, waiting for transfers between devices, shards(): from_line = [lax.ppermute(block, BOTH, along(pairs, 0)) for pairs in rounds]  13.7 us
    pallas_call x4, Pallas kernels, line(): pl.pallas_call(functools.partial(line_kernel, rows, span), out_shape=(jax...  12.9 us
    ppermute x4, starting transfers between devices, shards(): found = lax.ppermute(found, BOTH, back(along(pairs, cross)))  10.4 us
    ppermute x3, waiting for transfers between devices, shards(): from_plane = [lax.ppermute(block, BOTH, pairs) for pairs in across]  8.03 us
    ppermute x2, starting transfers between devices, shards(): from_line = [lax.ppermute(block, BOTH, along(pairs, 0)) for pairs in rounds]  7.8 us
    pallas_call x1, Pallas kernels, plane(): pl.pallas_call(functools.partial(plane_kernel, rows, span), out_shape=(ja...  6.14 us
    ppermute x3, starting transfers between devices, shards(): from_plane = [lax.ppermute(block, BOTH, pairs) for pairs in across]  5.05 us
    ppermute x3, starting transfers between devices, shards(): results.append(lax.ppermute(part, BOTH, back(pairs)))  3.5 us
  transfers between devices with their start and end apart: 15, of which 6 were waited for; matrix products, arithmetic and copies ran while one was open for 0% of the time, Pallas kernels for 26%

profile of v1, /device:TPU:0, one launch (start us, length us, event | category | flops | bytes accessed | tf_op | source)
XLA Modules:
  0.0 73.0 jit_solution(11823180343373404868)
XLA Ops:
  0.0 0.8 %copy.4.cluster = s32[320,1]{1,0:T(8,128)S(1)} copy(s32[320,1]{0,1:T(1,128)} %param.4) | data formatting | bytes 2560 | tf_op args[1]
  0.8 0.7 reshape.6.order_key
  1.5 1.0 %copy-done = bf16[320,768]{1,0:T(8,128)(2,1)S(1)} copy-done((bf16[320,768]{1,0:T(8,128)(2,1)S(1)}, bf16[320,768]{1,0:T(8,128)(2,1)}, u32[]{:S(2)}) %copy-start) | copy-done | bytes 491544
  2.8 3.0 %collective-permute-start = (bf16[336,768]{1,0:T(8,128)(2,1)S(1)}, bf16[336,768]{1,0:T(8,128)(2,1)S(1)}, u32[]{:S(2)}, u32[]{:S(2)}) collective-permute-start(bf16[336,768]{1,0:T(8,128)(2,1)S(1)} %shard_map.37.refs_0_), channel_id=1, source_target_pairs={{0,8},{1,9},{2,10},{3,11},{4,12},{5,13},{6,14},{7,15},{8,0},{9,1},... | collective-permute-start | bytes 1548296 | tf_op jit(solution)/shard_map/ppermute | solution.py:215
  5.8 4.5 %collective-permute-start.4 = (bf16[336,768]{1,0:T(8,128)(2,1)S(1)}, bf16[336,768]{1,0:T(8,128)(2,1)S(1)}, u32[]{:S(2)}, u32[]{:S(2)}) collective-permute-start(bf16[336,768]{1,0:T(8,128)(2,1)S(1)} %shard_map.37.refs_0_), channel_id=1, source_target_pairs={{0,4},{1,5},{6,2},{7,3},{2,0},{3,1},{8,12},{9,13},{14,10},{15,11},... | collective-permute-start | bytes 1548296 | tf_op jit(solution)/shard_map/ppermute | solution.py:214
  10.3 3.3 %collective-permute-start.6 = (bf16[336,768]{1,0:T(8,128)(2,1)S(1)}, bf16[336,768]{1,0:T(8,128)(2,1)S(1)}, u32[]{:S(2)}, u32[]{:S(2)}) collective-permute-start(bf16[336,768]{1,0:T(8,128)(2,1)S(1)} %shard_map.37.refs_0_), channel_id=1, source_target_pairs={{0,6},{1,7},{6,4},{7,5},{4,2},{5,3},{8,14},{9,15},{14,12},{15,13},... | collective-permute-start | bytes 1548296 | tf_op jit(solution)/shard_map/ppermute | solution.py:214
  13.6 1.6 %collective-permute-start.1 = (bf16[336,768]{1,0:T(8,128)(2,1)S(1)}, bf16[336,768]{1,0:T(8,128)(2,1)S(1)}, u32[]{:S(2)}, u32[]{:S(2)}) collective-permute-start(bf16[336,768]{1,0:T(8,128)(2,1)S(1)} %shard_map.37.refs_0_), channel_id=1, source_target_pairs={{0,16},{1,17},{2,18},{3,19},{4,20},{5,21},{6,22},{7,23},{8,24},{9,... | collective-permute-start | bytes 1548296 | tf_op jit(solution)/shard_map/ppermute | solution.py:215
  15.7 2.7 %collective-permute-done.refs_1_ = bf16[336,768]{1,0:T(8,128)(2,1)S(1)} collective-permute-done((bf16[336,768]{1,0:T(8,128)(2,1)S(1)}, bf16[336,768]{1,0:T(8,128)(2,1)S(1)}, u32[]{:S(2)}, u32[]{:S(2)}) %collective-permute-start) | collective-permute-done | bytes 516128 | tf_op jit(solution)/shard_map/ppermute | solution.py:215
  18.4 4.1 %collective-permute-done.4.block = bf16[336,768]{1,0:T(8,128)(2,1)S(1)} collective-permute-done((bf16[336,768]{1,0:T(8,128)(2,1)S(1)}, bf16[336,768]{1,0:T(8,128)(2,1)S(1)}, u32[]{:S(2)}, u32[]{:S(2)}) %collective-permute-start.4) | collective-permute-done | bytes 516128 | tf_op jit(solution)/shard_map/ppermute | solution.py:214
  22.5 9.6 %collective-permute-done.6.block = bf16[336,768]{1,0:T(8,128)(2,1)S(1)} collective-permute-done((bf16[336,768]{1,0:T(8,128)(2,1)S(1)}, bf16[336,768]{1,0:T(8,128)(2,1)S(1)}, u32[]{:S(2)}, u32[]{:S(2)}) %collective-permute-start.6) | collective-permute-done | bytes 516128 | tf_op jit(solution)/shard_map/ppermute | solution.py:214
  32.1 5.3 %collective-permute-done.1.refs_2_ = bf16[336,768]{1,0:T(8,128)(2,1)S(1)} collective-permute-done((bf16[336,768]{1,0:T(8,128)(2,1)S(1)}, bf16[336,768]{1,0:T(8,128)(2,1)S(1)}, u32[]{:S(2)}, u32[]{:S(2)}) %collective-permute-start.1) | collective-permute-done | bytes 516128 | tf_op jit(solution)/shard_map/ppermute | solution.py:215
  37.4 6.1 %shard_map.38 = (bf16[1280,768]{1,0:T(8,128)(2,1)S(1)}, f32[1,1280]{1,0:T(1,128)S(1)}, f32[1,1280]{1,0:T(1,128)S(1)}) custom-call(bf16[336,768]{1,0:T(8,128)(2,1)S(1)} %shard_map.37.refs_0_, bf16[336,768]{1,0:T(8,128)(2,1)S(1)} %collective-permute-done.refs_1_, bf16[336,768]{1,0:T(8,128)(2,1)S(1)} %collective-permute-done.1.refs_2_, ...), custom_call_target="tpu_custom_call" | custom-call | flops 1258291200 | bytes 3932160 | tf_op jit(solution)/shard_map/pallas_call | solution.py:133
  43.6 3.2 %shard_map.39 = (f32[1,1280]{1,0:T(1,128)S(1)}, f32[1,320]{1,0:T(1,128)S(1)}) custom-call(bf16[1280,768]{1,0:T(8,128)(2,1)S(1)} %get-tuple-element.16.held, f32[1,1280]{1,0:T(1,128)S(1)} %get-tuple-element.17.held_codes, f32[1,1280]{1,0:T(1,128)S(1)} %get-tuple-element.18.best, bf16[336,768]{1,0:T(8,128)(2,1)S(1)} %collective-permute-done.4.block), custom_call_target="tpu_custom_call" | custom-call | flops 629145600 | bytes 1966080 | tf_op jit(solution)/shard_map/pallas_call | solution.py:151
  46.8 2.1 %collective-permute-start.8 = (f32[1,320]{1,0:T(1,128)S(1)}, f32[1,320]{1,0:T(1,128)S(1)}, u32[]{:S(2)}, u32[]{:S(2)}) collective-permute-start(f32[1,320]{1,0:T(1,128)S(1)} %get-tuple-element.23), channel_id=1, source_target_pairs={{4,0},{5,1},{2,6},{3,7},{0,2},{1,3},{12,8},{13,9},{10,14},{11,15},... | collective-permute-start | bytes 3848 | tf_op jit(solution)/shard_map/ppermute | solution.py:223
  48.9 3.2 %shard_map.40 = (f32[1,1280]{1,0:T(1,128)S(1)}, f32[1,320]{1,0:T(1,128)S(1)}) custom-call(bf16[1280,768]{1,0:T(8,128)(2,1)S(1)} %get-tuple-element.16.held, f32[1,1280]{1,0:T(1,128)S(1)} %get-tuple-element.17.held_codes, f32[1,1280]{1,0:T(1,128)S(1)} %get-tuple-element.19.best, bf16[336,768]{1,0:T(8,128)(2,1)S(1)} %collective-permute-done.5.block), custom_call_target="tpu_custom_call" | custom-call | flops 629145600 | bytes 1966080 | tf_op jit(solution)/shard_map/pallas_call | solution.py:151
  52.1 3.2 %shard_map.41 = (f32[1,1280]{1,0:T(1,128)S(1)}, f32[1,320]{1,0:T(1,128)S(1)}) custom-call(bf16[1280,768]{1,0:T(8,128)(2,1)S(1)} %get-tuple-element.16.held, f32[1,1280]{1,0:T(1,128)S(1)} %get-tuple-element.17.held_codes, f32[1,1280]{1,0:T(1,128)S(1)} %get-tuple-element.20.best, bf16[336,768]{1,0:T(8,128)(2,1)S(1)} %collective-permute-done.6.block), custom_call_target="tpu_custom_call" | custom-call | flops 629145600 | bytes 1966080 | tf_op jit(solution)/shard_map/pallas_call | solution.py:151
  55.4 3.2 %shard_map.42 = (f32[1,1280]{1,0:T(1,128)S(1)}, f32[1,320]{1,0:T(1,128)S(1)}) custom-call(bf16[1280,768]{1,0:T(8,128)(2,1)S(1)} %get-tuple-element.16.held, f32[1,1280]{1,0:T(1,128)S(1)} %get-tuple-element.17.held_codes, f32[1,1280]{1,0:T(1,128)S(1)} %get-tuple-element.21.best, bf16[336,768]{1,0:T(8,128)(2,1)S(1)} %collective-permute-done.7.block), custom_call_target="tpu_custom_call" | custom-call | flops 629145600 | bytes 1966080 | tf_op jit(solution)/shard_map/pallas_call | solution.py:151
  59.2 1.5 %collective-permute-start.13 = (f32[1,320]{1,0:T(1,128)S(1)}, f32[1,320]{1,0:T(1,128)S(1)}, u32[]{:S(2)}, u32[]{:S(2)}) collective-permute-start(f32[1,320]{1,0:T(1,128)S(1)} %get-tuple-element.29), channel_id=1, source_target_pairs={{16,0},{17,1},{18,2},{19,3},{20,4},{21,5},{22,6},{23,7},{24,8},{25... | collective-permute-start | bytes 3848 | tf_op jit(solution)/shard_map/ppermute | solution.py:227
  60.7 1.4 %collective-permute-start.14 = (f32[1,320]{1,0:T(1,128)S(1)}, f32[1,320]{1,0:T(1,128)S(1)}, u32[]{:S(2)}, u32[]{:S(2)}) collective-permute-start(f32[1,320]{1,0:T(1,128)S(1)} %get-tuple-element.28), channel_id=1, source_target_pairs={{24,0},{25,1},{26,2},{27,3},{28,4},{29,5},{30,6},{31,7},{16,8},{17... | collective-permute-start | bytes 3848 | tf_op jit(solution)/shard_map/ppermute | solution.py:227
  62.2 1.3 %collective-permute-start.11 = (f32[1,320]{1,0:T(1,128)S(1)}, f32[1,320]{1,0:T(1,128)S(1)}, u32[]{:S(2)}, u32[]{:S(2)}) collective-permute-start(f32[1,320]{1,0:T(1,128)S(1)} %get-tuple-element.26), channel_id=1, source_target_pairs={{7,0},{6,1},{5,6},{4,7},{3,4},{2,5},{15,8},{14,9},{13,14},{12,15},... | collective-permute-start | bytes 3848 | tf_op jit(solution)/shard_map/ppermute | solution.py:223
  63.5 1.3 %collective-permute-start.10 = (f32[1,320]{1,0:T(1,128)S(1)}, f32[1,320]{1,0:T(1,128)S(1)}, u32[]{:S(2)}, u32[]{:S(2)}) collective-permute-start(f32[1,320]{1,0:T(1,128)S(1)} %get-tuple-element.25), channel_id=1, source_target_pairs={{6,0},{7,1},{4,6},{5,7},{2,4},{3,5},{14,8},{15,9},{12,14},{13,15},... | collective-permute-start | bytes 3848 | tf_op jit(solution)/shard_map/ppermute | solution.py:223
  64.8 5.7 %collective-permute-start.9 = (f32[1,320]{1,0:T(1,128)S(1)}, f32[1,320]{1,0:T(1,128)S(1)}, u32[]{:S(2)}, u32[]{:S(2)}) collective-permute-start(f32[1,320]{1,0:T(1,128)S(1)} %get-tuple-element.24), channel_id=1, source_target_pairs={{5,0},{4,1},{3,6},{2,7},{1,2},{0,3},{13,8},{12,9},{11,14},{10,15},... | collective-permute-start | bytes 3848 | tf_op jit(solution)/shard_map/ppermute | solution.py:223
  70.7 1.6 %collective-permute-done.9 = f32[1,320]{1,0:T(1,128)S(1)} collective-permute-done((f32[1,320]{1,0:T(1,128)S(1)}, f32[1,320]{1,0:T(1,128)S(1)}, u32[]{:S(2)}, u32[]{:S(2)}) %collective-permute-start.9) | collective-permute-done | bytes 1312 | tf_op jit(solution)/shard_map/ppermute | solution.py:223
  72.4 0.6 maximum_reduce_fusion
  (18 shorter events, 1.6 us)
Async XLA Ops:
  1.5 1.0 %copy-start = (bf16[320,768]{1,0:T(8,128)(2,1)S(1)}, bf16[320,768]{1,0:T(8,128)(2,1)}, u32[]{:S(2)}) copy-start(bf16[320,768]{1,0:T(8,128)(2,1)} %embeddings.1) | copy-start | bytes 1474564
  2.8 15.6 %collective-permute-start = (bf16[336,768]{1,0:T(8,128)(2,1)S(1)}, bf16[336,768]{1,0:T(8,128)(2,1)S(1)}, u32[]{:S(2)}, u32[]{:S(2)}) collective-permute-start(bf16[336,768]{1,0:T(8,128)(2,1)S(1)} %shard_map.37.refs_0_), channel_id=1, source_target_pairs={{0,8},{1,9},{2,10},{3,11},{4,12},{5,13},{6,14},{7,15},{8,0},{9,1},... | collective-permute-start | bytes 1548296 | tf_op jit(solution)/shard_map/ppermute | solution.py:215
  5.8 16.7 %collective-permute-start.4 = (bf16[336,768]{1,0:T(8,128)(2,1)S(1)}, bf16[336,768]{1,0:T(8,128)(2,1)S(1)}, u32[]{:S(2)}, u32[]{:S(2)}) collective-permute-start(bf16[336,768]{1,0:T(8,128)(2,1)S(1)} %shard_map.37.refs_0_), channel_id=1, source_target_pairs={{0,4},{1,5},{6,2},{7,3},{2,0},{3,1},{8,12},{9,13},{14,10},{15,11},... | collective-permute-start | bytes 1548296 | tf_op jit(solution)/shard_map/ppermute | solution.py:214
  10.3 21.8 %collective-permute-start.6 = (bf16[336,768]{1,0:T(8,128)(2,1)S(1)}, bf16[336,768]{1,0:T(8,128)(2,1)S(1)}, u32[]{:S(2)}, u32[]{:S(2)}) collective-permute-start(bf16[336,768]{1,0:T(8,128)(2,1)S(1)} %shard_map.37.refs_0_), channel_id=1, source_target_pairs={{0,6},{1,7},{6,4},{7,5},{4,2},{5,3},{8,14},{9,15},{14,12},{15,13},... | collective-permute-start | bytes 1548296 | tf_op jit(solution)/shard_map/ppermute | solution.py:214
  13.6 23.8 %collective-permute-start.1 = (bf16[336,768]{1,0:T(8,128)(2,1)S(1)}, bf16[336,768]{1,0:T(8,128)(2,1)S(1)}, u32[]{:S(2)}, u32[]{:S(2)}) collective-permute-start(bf16[336,768]{1,0:T(8,128)(2,1)S(1)} %shard_map.37.refs_0_), channel_id=1, source_target_pairs={{0,16},{1,17},{2,18},{3,19},{4,20},{5,21},{6,22},{7,23},{8,24},{9,... | collective-permute-start | bytes 1548296 | tf_op jit(solution)/shard_map/ppermute | solution.py:215
  15.2 22.2 %collective-permute-start.2 = (bf16[336,768]{1,0:T(8,128)(2,1)S(1)}, bf16[336,768]{1,0:T(8,128)(2,1)S(1)}, u32[]{:S(2)}, u32[]{:S(2)}) collective-permute-start(bf16[336,768]{1,0:T(8,128)(2,1)S(1)} %shard_map.37.refs_0_), channel_id=1, source_target_pairs={{0,24},{1,25},{2,26},{3,27},{4,28},{5,29},{6,30},{7,31},{8,16},{9,... | collective-permute-start | bytes 1548296 | tf_op jit(solution)/shard_map/ppermute | solution.py:215
  18.4 19.0 %collective-permute-start.3 = (bf16[336,768]{1,0:T(8,128)(2,1)S(1)}, bf16[336,768]{1,0:T(8,128)(2,1)S(1)}, u32[]{:S(2)}, u32[]{:S(2)}) collective-permute-start(bf16[336,768]{1,0:T(8,128)(2,1)S(1)} %shard_map.37.refs_0_), channel_id=1, source_target_pairs={{0,1},{1,0},{2,3},{3,2},{4,5},{5,4},{6,7},{7,6},{8,9},{9,8},{10,11... | collective-permute-start | bytes 1548296 | tf_op jit(solution)/shard_map/ppermute | solution.py:213
  22.5 26.4 %collective-permute-start.5 = (bf16[336,768]{1,0:T(8,128)(2,1)S(1)}, bf16[336,768]{1,0:T(8,128)(2,1)S(1)}, u32[]{:S(2)}, u32[]{:S(2)}) collective-permute-start(bf16[336,768]{1,0:T(8,128)(2,1)S(1)} %collective-permute-done.4.block), channel_id=1, source_target_pairs={{0,1},{1,0},{2,3},{3,2},{4,5},{5,4},{6,7},{7,6},{8,9},{9,8},{10,11... | collective-permute-start | bytes 1548296 | tf_op jit(solution)/shard_map/ppermute | solution.py:219
  32.1 23.3 %collective-permute-start.7 = (bf16[336,768]{1,0:T(8,128)(2,1)S(1)}, bf16[336,768]{1,0:T(8,128)(2,1)S(1)}, u32[]{:S(2)}, u32[]{:S(2)}) collective-permute-start(bf16[336,768]{1,0:T(8,128)(2,1)S(1)} %collective-permute-done.6.block), channel_id=1, source_target_pairs={{0,1},{1,0},{2,3},{3,2},{4,5},{5,4},{6,7},{7,6},{8,9},{9,8},{10,11... | collective-permute-start | bytes 1548296 | tf_op jit(solution)/shard_map/ppermute | solution.py:219
  46.8 16.6 %collective-permute-start.8 = (f32[1,320]{1,0:T(1,128)S(1)}, f32[1,320]{1,0:T(1,128)S(1)}, u32[]{:S(2)}, u32[]{:S(2)}) collective-permute-start(f32[1,320]{1,0:T(1,128)S(1)} %get-tuple-element.23), channel_id=1, source_target_pairs={{4,0},{5,1},{2,6},{3,7},{0,2},{1,3},{12,8},{13,9},{10,14},{11,15},... | collective-permute-start | bytes 3848 | tf_op jit(solution)/shard_map/ppermute | solution.py:223
  58.7 6.1 %collective-permute-start.12 = (f32[1,320]{1,0:T(1,128)S(1)}, f32[1,320]{1,0:T(1,128)S(1)}, u32[]{:S(2)}, u32[]{:S(2)}) collective-permute-start(f32[1,320]{1,0:T(1,128)S(1)} %get-tuple-element.27), channel_id=1, source_target_pairs={{8,0},{9,1},{10,2},{11,3},{12,4},{13,5},{14,6},{15,7},{0,8},{1,9},... | collective-permute-start | bytes 3848 | tf_op jit(solution)/shard_map/ppermute | solution.py:227
  59.2 11.3 %collective-permute-start.13 = (f32[1,320]{1,0:T(1,128)S(1)}, f32[1,320]{1,0:T(1,128)S(1)}, u32[]{:S(2)}, u32[]{:S(2)}) collective-permute-start(f32[1,320]{1,0:T(1,128)S(1)} %get-tuple-element.29), channel_id=1, source_target_pairs={{16,0},{17,1},{18,2},{19,3},{20,4},{21,5},{22,6},{23,7},{24,8},{25... | collective-permute-start | bytes 3848 | tf_op jit(solution)/shard_map/ppermute | solution.py:227
  60.7 9.8 %collective-permute-start.14 = (f32[1,320]{1,0:T(1,128)S(1)}, f32[1,320]{1,0:T(1,128)S(1)}, u32[]{:S(2)}, u32[]{:S(2)}) collective-permute-start(f32[1,320]{1,0:T(1,128)S(1)} %get-tuple-element.28), channel_id=1, source_target_pairs={{24,0},{25,1},{26,2},{27,3},{28,4},{29,5},{30,6},{31,7},{16,8},{17... | collective-permute-start | bytes 3848 | tf_op jit(solution)/shard_map/ppermute | solution.py:227
  62.2 8.4 %collective-permute-start.11 = (f32[1,320]{1,0:T(1,128)S(1)}, f32[1,320]{1,0:T(1,128)S(1)}, u32[]{:S(2)}, u32[]{:S(2)}) collective-permute-start(f32[1,320]{1,0:T(1,128)S(1)} %get-tuple-element.26), channel_id=1, source_target_pairs={{7,0},{6,1},{5,6},{4,7},{3,4},{2,5},{15,8},{14,9},{13,14},{12,15},... | collective-permute-start | bytes 3848 | tf_op jit(solution)/shard_map/ppermute | solution.py:223
  63.5 7.3 %collective-permute-start.10 = (f32[1,320]{1,0:T(1,128)S(1)}, f32[1,320]{1,0:T(1,128)S(1)}, u32[]{:S(2)}, u32[]{:S(2)}) collective-permute-start(f32[1,320]{1,0:T(1,128)S(1)} %get-tuple-element.25), channel_id=1, source_target_pairs={{6,0},{7,1},{4,6},{5,7},{2,4},{3,5},{14,8},{15,9},{12,14},{13,15},... | collective-permute-start | bytes 3848 | tf_op jit(solution)/shard_map/ppermute | solution.py:223
  64.8 7.6 %collective-permute-start.9 = (f32[1,320]{1,0:T(1,128)S(1)}, f32[1,320]{1,0:T(1,128)S(1)}, u32[]{:S(2)}, u32[]{:S(2)}) collective-permute-start(f32[1,320]{1,0:T(1,128)S(1)} %get-tuple-element.24), channel_id=1, source_target_pairs={{5,0},{4,1},{3,6},{2,7},{1,2},{0,3},{13,8},{12,9},{11,14},{10,15},... | collective-permute-start | bytes 3848 | tf_op jit(solution)/shard_map/ppermute | solution.py:223

commit v2 on v0

v2 whole, which is shorter than its diff:
```python
import functools

import jax
import jax.numpy as jnp
from jax import lax
from jax.experimental import pallas as pl
from jax.experimental.pallas import tpu as pltpu
from jax.sharding import PartitionSpec as P

EPSILON = 1e-06
EXTRA = 16
LANES = 128
TILE = 256
BOTH = ("dp", "grid")


def up(value, multiple):
    return -(-value // multiple) * multiple


def turned_to_column(row, rows):
    return jnp.broadcast_to(row, (LANES, row.shape[1])).T[:rows]


def codes(block, rows, span):
    parts = block[rows : rows + EXTRA, : up(rows, LANES)].astype(jnp.float32)
    return parts[2:3] * (4.0 * span) + parts[0:1] * 256.0 + parts[1:2]


def prepare_kernel(embeddings, cluster, order_key, block):
    rows, width = embeddings.shape
    values = embeddings[...].astype(jnp.float32)
    scale = lax.rsqrt(jnp.sum(values * values, axis=1, keepdims=True) + EPSILON)
    block[0:rows, :] = (values * scale).astype(jnp.bfloat16)
    keys = order_key[...].reshape(1, rows)
    parts = [keys >> 8, keys & 255, cluster[...] + 1]
    parts = [part.astype(jnp.float32) for part in parts]
    parts = jnp.concatenate(parts + [jnp.zeros((EXTRA - 3, rows), jnp.float32)], axis=0)
    parts = jnp.concatenate([parts, jnp.zeros((EXTRA, width - rows), jnp.float32)], axis=1)
    block[rows : rows + EXTRA, :] = parts.astype(jnp.bfloat16)


def prepare(embeddings, cluster, order_key):
    rows, width = embeddings.shape
    return pl.pallas_call(
        prepare_kernel,
        out_shape=jax.ShapeDtypeStruct((rows + EXTRA, width), jnp.bfloat16),
        compiler_params=pltpu.CompilerParams(vmem_limit_bytes=16 << 20),
        cost_estimate=pl.CostEstimate(
            flops=4 * rows * width, bytes_accessed=4 * rows * width, transcendentals=rows
        ),
    )(embeddings, cluster.reshape(1, rows), order_key)


def row_from_partial(partial, rows):
    padded = up(rows, LANES)
    if padded != rows:
        partial = jnp.concatenate(
            [partial, jnp.zeros((padded - rows, LANES), partial.dtype)], axis=0
        )
    return jnp.max(partial.T, axis=0, keepdims=True)[:, :rows]


def meet(block, rows, span, held, held_codes, to_block, to_held):
    column = turned_to_column(codes(block, rows, span), rows)
    partial = jnp.full((rows, LANES), -1.0, jnp.float32)
    best_held = []
    for at in range(0, held.shape[0], TILE):
        sims = lax.dot_general(
            block[0:rows, :],
            held[at : at + TILE, :],
            (((1,), (1,)), ((), ())),
            preferred_element_type=jnp.float32,
        )
        for lane in range(0, TILE, LANES):
            part = sims[:, lane : lane + LANES]
            gap = column - held_codes[:, at + lane : at + lane + LANES]
            if to_block and to_held:
                part = jnp.where(jnp.abs(gap) < span, part, -1.0)
                later = gap > 0.0
                partial = jnp.maximum(partial, jnp.where(later, part, -1.0))
                other = jnp.where(later, -1.0, part)
            elif to_block:
                partial = jnp.maximum(
                    partial, jnp.where((gap > 0.0) & (gap < span), part, -1.0)
                )
            else:
                other = jnp.where((gap < 0.0) & (gap > -span), part, -1.0)
            if to_held:
                best_held.append(jnp.max(other, axis=0, keepdims=True))
    return (
        row_from_partial(partial, rows) if to_block else None,
        jnp.concatenate(best_held, axis=1) if to_held else None,
    )


def meet_kernel(rows, span, count, modes, holders, earlier, split, *refs):
    blocks, refs = refs[:count], refs[count:]
    holds, refs = refs[:holders], refs[holders:]
    bests, refs = refs[: holders * earlier], refs[holders * earlier :]
    outs, found, held = refs[:holders], refs[holders:-1], refs[-1]
    if split:
        found, joined = found[:-1], found[-1]
        top = 0
        for piece in blocks[-split:]:
            joined[top : top + piece.shape[0], :] = piece[...]
            top += piece.shape[0]
        blocks = blocks[:-split] + (joined,)
    total = held.shape[0]
    row = []
    for at, block in enumerate(holds):
        held[at * rows : (at + 1) * rows, :] = block[0:rows, :]
        row.append(codes(block, rows, span)[:, :rows])
    if total > holders * rows:
        held[holders * rows :, :] = jnp.zeros((total - holders * rows, held.shape[1]), held.dtype)
        row.append(jnp.zeros((1, total - holders * rows), jnp.float32))
    row = jnp.concatenate(row, axis=1)
    best = None
    at = 0
    for block, (to_block, to_held) in zip(blocks, modes):
        mine, theirs = meet(block, rows, span, held, row, to_block, to_held)
        if to_block:
            found[at][...] = mine
            at += 1
        if to_held:
            best = theirs if best is None else jnp.maximum(best, theirs)
    top = 0
    for out in found[at:]:
        out[...] = blocks[-1][top : top + out.shape[0], :]
        top += out.shape[0]
    for at, out in enumerate(outs):
        part = best[:, at * rows : (at + 1) * rows]
        if earlier:
            part = jnp.maximum(part, bests[at][...])
        out[...] = part


def meeting(blocks, modes, holds, bests, rows, span, keep=(), split=0):
    width = blocks[0].shape[1]
    holders = len(holds)
    total = up(holders * rows, TILE)
    row = jax.ShapeDtypeStruct((1, rows), jnp.float32)
    count = holders + sum(to_block for to_block, _ in modes)
    kept = tuple(jax.ShapeDtypeStruct((height, width), jnp.bfloat16) for height in keep)
    joined = [pltpu.VMEM((rows + EXTRA, width), jnp.bfloat16)] if split else []
    results = pl.pallas_call(
        functools.partial(
            meet_kernel, rows, span, len(blocks), modes, holders, 1 if bests else 0, split
        ),
        out_shape=(row,) * count + kept,
        scratch_shapes=joined + [pltpu.VMEM((total, width), jnp.bfloat16)],
        compiler_params=pltpu.CompilerParams(vmem_limit_bytes=32 << 20),
        cost_estimate=pl.CostEstimate(flops=rows, bytes_accessed=rows, transcendentals=0),
    )(*blocks, *holds, *bests)
    return list(results[:holders]), list(results[holders:count]), list(results[count:])


OWN = (True, False)
HELD = (False, True)
TWO = (True, True)


def line_rounds(chips):
    if chips == 4:
        return [[(0, 2), (3, 1), (1, 0)], [(0, 3), (3, 2), (2, 1)]]
    rounds = []
    for shift in range(1, chips // 2 + 1):
        senders = chips // 2 if 2 * shift == chips else chips
        rounds.append([(s, (s + shift) % chips) for s in range(senders)])
    return rounds


def solution(mesh):
    groups, members = mesh.shape["dp"], mesh.shape["grid"]
    assert groups == 4 and members % 2 == 0
    chips = members // 2
    rounds = line_rounds(chips)

    def everywhere(target):
        return [
            (p * members + g, a * members + b)
            for p in range(groups)
            for g in range(members)
            for a, b in [target(p, g)]
        ]

    other_core = everywhere(lambda p, g: (p, g ^ 1))
    first = everywhere(lambda p, g: (p ^ (1 + g % 2), g))
    second = everywhere(lambda p, g: (p ^ (2 - g % 2), g))
    corner = everywhere(lambda p, g: (p ^ 3, g))

    def along(pairs, cross):
        return [
            (p * members + 2 * s + c, p * members + 2 * t + (c ^ cross))
            for p in range(groups)
            for s, t in pairs
            for c in range(2)
        ]

    def back(pairs):
        return [(target, source) for source, target in pairs]

    def shards(embeddings, cluster, order_key):
        rows = embeddings.shape[0]
        span = 256
        while span < rows * groups * members:
            span *= 2
        chip = lax.axis_index("grid") // 2
        block = prepare(embeddings, cluster, order_key)
        near = [lax.ppermute(block, BOTH, along(rounds[0], 0))]
        from_first = lax.ppermute(block, BOTH, first)
        near += [lax.ppermute(block, BOTH, along(pairs, 0)) for pairs in rounds[1:]]
        from_second = lax.ppermute(block, BOTH, second)
        from_corner = lax.ppermute(from_first, BOTH, second)
        partner = lax.optimization_barrier((block, from_first))[0]
        partner = lax.ppermute(partner, BOTH, other_core)

        results = []

        def give_back(found, pairs):
            senders = functools.reduce(jnp.logical_or, [chip == s for s, _ in pairs])
            for cross, part in enumerate(found):
                part = lax.ppermute(part, BOTH, back(along(pairs, cross)))
                results.append(jnp.where(senders, part, -1.0))

        three = [block, from_first, from_second]
        bests, (mine, one), pieces = meeting(
            [block, near[0]], [OWN, TWO], three, [], rows, span, keep=(rows // 2, rows // 2 + EXTRA)
        )
        results.append(mine)
        pieces = [lax.ppermute(piece, BOTH, other_core) for piece in pieces]
        corner_best, (mine, one_more), _ = meeting(
            [block, near[0]], [OWN, TWO], [from_corner], [], rows, span
        )
        results.append(mine)
        bests, (other,), _ = meeting(
            [partner] + pieces,
            [HELD, TWO],
            three + [from_corner],
            bests + corner_best,
            rows,
            span,
            split=len(pieces),
        )
        give_back([jnp.maximum(one, one_more), other], rounds[0])
        for pairs, one in zip(rounds[1:], near[1:]):
            found = []
            one, bests = lax.optimization_barrier((one, bests))
            for part in (one, lax.ppermute(one, BOTH, other_core)):
                bests, mine, _ = meeting([part], [TWO], three + [from_corner], bests, rows, span)
                found += mine
            give_back(found, pairs)
        results += [
            lax.ppermute(part, BOTH, pairs)
            for part, pairs in zip(bests[1:], (first, second, corner))
        ]
        return functools.reduce(jnp.maximum, results, bests[0]).reshape(rows)

    placed = (P(BOTH, None), P(BOTH, None), P(BOTH))
    return jax.shard_map(
        shards, mesh=mesh, in_specs=placed, out_specs=P(BOTH), check_vma=False
    )
```

time: 138 us -> 59 us (0.43)
  blocking collectives: 40.9 us -> 0 us
  waiting for transfers between devices: 56.6 us -> 16.6 us
  starting transfers between devices: 3.63 us -> 32.4 us
  between operations: 13.5 us -> 0.12 us
  matrix products: 8.51 us -> 0 us
  Pallas kernels: 0 us -> 6.67 us
  other arithmetic: 7 us -> 0.61 us
  local copies, waits for them, and re-layouts: 7.11 us -> 2.39 us
    all_gather x1 -> x0, waiting for transfers between devices: 52 us -> none  [shards(): other_units = lax.all_gather(mine, 'grid', axis=0, tiled=True)]
    ppermute x0 -> x16, starting transfers between devices: none -> 32.4 us  [the longest x4 12 us: give_back(): part = lax.ppermute(part, BOTH, back(along(pairs, cross)))]
    all_to_all x2 -> x0, blocking collectives: 25.7 us -> none  [the longest x1 18.7 us: shards(): lax.all_to_all(send_units, 'dp', split_axis=0, concat_axis=0, tiled=True)]
    ppermute x0 -> x16, waiting for transfers between devices: none -> 16.6 us  [the longest x1 6.27 us: shards(): near += [lax.ppermute(block, BOTH, along(pairs, 0)) for pairs in rounds[1:]]]
    all_gather x1 -> x0, blocking collectives: 15.2 us -> none  [shards(): other_keys = lax.all_gather(mine_keys, 'grid', axis=0, tiled=True)]
    dot_general x1 -> x0, matrix products: 8.51 us -> none  [shards(): jnp.einsum('qe,ke->qk', mine, other_units, preferred_element_type=jnp.flo...]
    pallas_call x0 -> x6, Pallas kernels: none -> 6.67 us  [the longest x5 6.49 us: meeting(): pl.pallas_call(functools.partial(meet_kernel, rows, span, len(blocks), mo...]
    all_to_all x1 -> x0, waiting for transfers between devices: 4.67 us -> none  [shards(): lax.all_to_all(scores.reshape(owners, depth), 'dp', split_axis=0, concat_...]
  transfers between devices with their start and end apart: 2 -> 16, of which waited for: 2 -> 5; matrix products, arithmetic and copies ran while one was open for 2% -> 0% of each run, Pallas kernels for 0% -> 11%
where the time goes in v2:
time: 59 us; the launch traced here: 58.7 us
  starting transfers between devices  32.4 us (55%)
  waiting for transfers between devices  16.6 us (28%)
  Pallas kernels  6.67 us (11%)
  local copies, waits for them, and re-layouts  2.39 us (4%)
  other arithmetic  0.61 us (1%)
    ppermute x4, starting transfers between devices, give_back(): part = lax.ppermute(part, BOTH, back(along(pairs, cross)))  12 us
    pallas_call x5, Pallas kernels, meeting(): pl.pallas_call(functools.partial(meet_kernel, rows, span, len(blocks), mo...  6.49 us
    ppermute x1, waiting for transfers between devices, shards(): near += [lax.ppermute(block, BOTH, along(pairs, 0)) for pairs in rounds[1:]]  6.27 us
    ppermute x1, waiting for transfers between devices, shards(): from_first = lax.ppermute(block, BOTH, first)  6.02 us
    ppermute x1, starting transfers between devices, shards(): near += [lax.ppermute(block, BOTH, along(pairs, 0)) for pairs in rounds[1:]]  5.67 us
    ppermute x1, starting transfers between devices, shards(): near = [lax.ppermute(block, BOTH, along(rounds[0], 0))]  4.49 us
    ppermute x3, starting transfers between devices, shards(): lax.ppermute(part, BOTH, pairs)  3.55 us
    ppermute x1, starting transfers between devices, shards(): from_first = lax.ppermute(block, BOTH, first)  3 us
  transfers between devices with their start and end apart: 16, of which 5 were waited for; matrix products, arithmetic and copies ran while one was open for 0% of the time, Pallas kernels for 11%

profile of v2, /device:TPU:0, one launch (start us, length us, event | category | flops | bytes accessed | tf_op | source)
XLA Modules:
  0.0 58.7 jit_solution(7748201918004660295)
XLA Ops:
  0.0 0.7 %copy-done.2 = s32[320,1]{0,1:T(1,128)S(1)} copy-done((s32[320,1]{0,1:T(1,128)S(1)}, s32[320,1]{0,1:T(1,128)}, u32[]{:S(2)}) %copy-start.2) | copy-done | bytes 1304
  0.7 1.0 %copy-done = bf16[320,768]{1,0:T(8,128)(2,1)S(1)} copy-done((bf16[320,768]{1,0:T(8,128)(2,1)S(1)}, bf16[320,768]{1,0:T(8,128)(2,1)}, u32[]{:S(2)}) %copy-start) | copy-done | bytes 491544
  1.7 0.7 %copy-done.1 = s32[320]{0:T(512)S(1)} copy-done((s32[320]{0:T(512)S(1)}, s32[320]{0:T(512)}, u32[]{:S(2)}) %copy-start.1) | copy-done | bytes 1304
  2.6 3.0 %collective-permute-start.1 = (bf16[336,768]{1,0:T(8,128)(2,1)S(1)}, bf16[336,768]{1,0:T(8,128)(2,1)S(1)}, u32[]{:S(2)}, u32[]{:S(2)}) collective-permute-start(bf16[336,768]{1,0:T(8,128)(2,1)S(1)} %shard_map.37.refs_0_.refs_2_.refs_3_.refs_1_), channel_id=1, source_target_pairs={{0,8},{1,17},{2,10},{3,19},{4,12},{5,21},{6,14},{7,23},{8,0},{9,25... | collective-permute-start | bytes 1548296 | tf_op jit(solution)/shard_map/ppermute | solution.py:211
  5.6 1.5 %collective-permute-start.4 = (bf16[336,768]{1,0:T(8,128)(2,1)S(1)}, bf16[336,768]{1,0:T(8,128)(2,1)S(1)}, u32[]{:S(2)}, u32[]{:S(2)}) collective-permute-start(bf16[336,768]{1,0:T(8,128)(2,1)S(1)} %shard_map.37.refs_0_.refs_2_.refs_3_.refs_1_), channel_id=1, source_target_pairs={{0,16},{1,9},{2,18},{3,11},{4,20},{5,13},{6,22},{7,15},{8,24},{9,1... | collective-permute-start | bytes 1548296 | tf_op jit(solution)/shard_map/ppermute | solution.py:213
  7.1 4.5 %collective-permute-start.3 = (bf16[336,768]{1,0:T(8,128)(2,1)S(1)}, bf16[336,768]{1,0:T(8,128)(2,1)S(1)}, u32[]{:S(2)}, u32[]{:S(2)}) collective-permute-start(bf16[336,768]{1,0:T(8,128)(2,1)S(1)} %shard_map.37.refs_0_.refs_2_.refs_3_.refs_1_), channel_id=1, source_target_pairs={{0,4},{1,5},{6,2},{7,3},{2,0},{3,1},{8,12},{9,13},{14,10},{15,11},... | collective-permute-start | bytes 1548296 | tf_op jit(solution)/shard_map/ppermute | solution.py:210
  11.6 6.0 %collective-permute-done.1.refs_3_.refs_4_.refs_2_ = bf16[336,768]{1,0:T(8,128)(2,1)S(1)} collective-permute-done((bf16[336,768]{1,0:T(8,128)(2,1)S(1)}, bf16[336,768]{1,0:T(8,128)(2,1)S(1)}, u32[]{:S(2)}, u32[]{:S(2)}) %collective-permute-start.1) | collective-permute-done | bytes 516128 | tf_op jit(solution)/shard_map/ppermute | solution.py:211
  17.6 1.6 %collective-permute-start.7 = (bf16[336,768]{1,0:T(8,128)(2,1)S(1)}, bf16[336,768]{1,0:T(8,128)(2,1)S(1)}, u32[]{:S(2)}, u32[]{:S(2)}) collective-permute-start(bf16[336,768]{1,0:T(8,128)(2,1)S(1)} %collective-permute-done.1.refs_3_.refs_4_.refs_2_), channel_id=1, source_target_pairs={{0,16},{1,9},{2,18},{3,11},{4,20},{5,13},{6,22},{7,15},{8,24},{9,1... | collective-permute-start | bytes 1548296 | tf_op jit(solution)/shard_map/ppermute | solution.py:214
  19.2 5.7 %collective-permute-start = (bf16[336,768]{1,0:T(8,128)(2,1)S(1)}, bf16[336,768]{1,0:T(8,128)(2,1)S(1)}, u32[]{:S(2)}, u32[]{:S(2)}) collective-permute-start(bf16[336,768]{1,0:T(8,128)(2,1)S(1)} %shard_map.37.refs_0_.refs_2_.refs_3_.refs_1_), channel_id=1, source_target_pairs={{0,6},{1,7},{6,4},{7,5},{4,2},{5,3},{8,14},{9,15},{14,12},{15,13},... | collective-permute-start | bytes 1548296 | tf_op jit(solution)/shard_map/ppermute | solution.py:212
  24.9 1.5 %shard_map.38 = (f32[1,320]{1,0:T(1,128)S(1)}, f32[1,320]{1,0:T(1,128)S(1)}, f32[1,320]{1,0:T(1,128)S(1)}, f32[1,320]{1,0:T(1,128)S(1)}, f32[1,320]{1,0:T(1,128)...) custom-call(bf16[336,768]{1,0:T(8,128)(2,1)S(1)} %shard_map.37.refs_0_.refs_2_.refs_3_.refs_1_, ...), custom_call_target="tpu_custom_call" | custom-call | flops 320 | bytes 320 | tf_op jit(solution)/shard_map/pallas_call | solution.py:146
  27.0 0.9 %shard_map.39 = (f32[1,320]{1,0:T(1,128)S(1)}, f32[1,320]{1,0:T(1,128)S(1)}, f32[1,320]{1,0:T(1,128)S(1)}) custom-call(bf16[336,768]{1,0:T(8,128)(2,1)S(1)} %shard_map.37.refs_0_.refs_2_.refs_3_.refs_1_, bf16[336,768]{1,0:T(8,128)(2,1)S(1)} %collective-permute-done.3.refs_1_, bf16[336,768]{1,0:T(8,128)(2,1)S(1)} %collective-permute-done.7.refs_2_.refs_6_.refs_4_), custom_call_target="tpu_custom_call" | custom-call | flops 320 | bytes 320 | tf_op jit(solution)/shard_map/pallas_call | solution.py:146
  28.4 1.8 %shard_map.40 = (f32[1,320]{1,0:T(1,128)S(1)}, f32[1,320]{1,0:T(1,128)S(1)}, f32[1,320]{1,0:T(1,128)S(1)}, f32[1,320]{1,0:T(1,128)S(1)}, f32[1,320]{1,0:T(1,128)S(1)}) custom-call(bf16[336,768]{1,0:T(8,128)(2,1)S(1)} %collective-permute-done.2.refs_0_, bf16[160,768]{1,0:T(8,128)(2,1)S(1)} %collective-permute-done.5.refs_1_, ...), custom_call_target="tpu_custom_call" | custom-call | flops 320 | bytes 320 | tf_op jit(solution)/shard_map/pallas_call | solution.py:146
  30.2 6.3 %collective-permute-done.refs_0_ = bf16[336,768]{1,0:T(8,128)(2,1)S(1)} collective-permute-done((bf16[336,768]{1,0:T(8,128)(2,1)S(1)}, bf16[336,768]{1,0:T(8,128)(2,1)S(1)}, u32[]{:S(2)}, u32[]{:S(2)}) %collective-permute-start) | collective-permute-done | bytes 516128 | tf_op jit(solution)/shard_map/ppermute | solution.py:212
  36.5 1.1 %shard_map.41 = (f32[1,320]{1,0:T(1,128)S(1)}, f32[1,320]{1,0:T(1,128)S(1)}, f32[1,320]{1,0:T(1,128)S(1)}, f32[1,320]{1,0:T(1,128)S(1)}, f32[1,320]{1,0:T(1,128)S(1)}) custom-call(bf16[336,768]{1,0:T(8,128)(2,1)S(1)} %collective-permute-done.refs_0_, bf16[336,768]{1,0:T(8,128)(2,1)S(1)} %shard_map.37.refs_0_.refs_2_.refs_3_.refs_1_, ...), custom_call_target="tpu_custom_call" | custom-call | flops 320 | bytes 320 | tf_op jit(solution)/shard_map/pallas_call | solution.py:146
  37.6 1.3 %collective-permute-start.11 = (f32[1,320]{1,0:T(1,128)S(1)}, f32[1,320]{1,0:T(1,128)S(1)}, u32[]{:S(2)}, u32[]{:S(2)}) collective-permute-start(f32[1,320]{1,0:T(1,128)S(1)} %get-tuple-element.62), channel_id=1, source_target_pairs={{6,0},{7,1},{4,6},{5,7},{2,4},{3,5},{14,8},{15,9},{12,14},{13,15},... | collective-permute-start | bytes 3848 | tf_op jit(solution)/shard_map/ppermute | solution.py:223
  38.9 4.4 %collective-permute-start.10 = (f32[1,320]{1,0:T(1,128)S(1)}, f32[1,320]{1,0:T(1,128)S(1)}, u32[]{:S(2)}, u32[]{:S(2)}) collective-permute-start(f32[1,320]{1,0:T(1,128)S(1)} %get-tuple-element.61), channel_id=1, source_target_pairs={{5,0},{4,1},{3,6},{2,7},{1,2},{0,3},{13,8},{12,9},{11,14},{10,15},... | collective-permute-start | bytes 3848 | tf_op jit(solution)/shard_map/ppermute | solution.py:223
  43.3 5.0 %collective-permute-start.9 = (f32[1,320]{1,0:T(1,128)S(1)}, f32[1,320]{1,0:T(1,128)S(1)}, u32[]{:S(2)}, u32[]{:S(2)}) collective-permute-start(f32[1,320]{1,0:T(1,128)S(1)} %max.32), channel_id=1, source_target_pairs={{4,0},{5,1},{2,6},{3,7},{0,2},{1,3},{12,8},{13,9},{10,14},{11,15},... | collective-permute-start | bytes 3848 | tf_op jit(solution)/shard_map/ppermute | solution.py:223
  48.3 1.1 %shard_map.42 = (f32[1,320]{1,0:T(1,128)S(1)}, f32[1,320]{1,0:T(1,128)S(1)}, f32[1,320]{1,0:T(1,128)S(1)}, f32[1,320]{1,0:T(1,128)S(1)}, f32[1,320]{1,0:T(1,128)S(1)}) custom-call(bf16[336,768]{1,0:T(8,128)(2,1)S(1)} %collective-permute-done.8.refs_0_, bf16[336,768]{1,0:T(8,128)(2,1)S(1)} %shard_map.37.refs_0_.refs_2_.refs_3_.refs_1_, ...), custom_call_target="tpu_custom_call" | custom-call | flops 320 | bytes 320 | tf_op jit(solution)/shard_map/pallas_call | solution.py:146
  49.5 1.3 %collective-permute-start.12 = (f32[1,320]{1,0:T(1,128)S(1)}, f32[1,320]{1,0:T(1,128)S(1)}, u32[]{:S(2)}, u32[]{:S(2)}) collective-permute-start(f32[1,320]{1,0:T(1,128)S(1)} %get-tuple-element.63), channel_id=1, source_target_pairs={{7,0},{6,1},{5,6},{4,7},{3,4},{2,5},{15,8},{14,9},{13,14},{12,15},... | collective-permute-start | bytes 3848 | tf_op jit(solution)/shard_map/ppermute | solution.py:223
  50.8 1.6 %collective-permute-start.13 = (f32[1,320]{1,0:T(1,128)S(1)}, f32[1,320]{1,0:T(1,128)S(1)}, u32[]{:S(2)}, u32[]{:S(2)}) collective-permute-start(f32[1,320]{1,0:T(1,128)S(1)} %get-tuple-element.64), channel_id=1, source_target_pairs={{0,8},{1,17},{2,10},{3,19},{4,12},{5,21},{6,14},{7,23},{8,0},{9,25... | collective-permute-start | bytes 3848 | tf_op jit(solution)/shard_map/ppermute | solution.py:254
  52.3 1.3 %collective-permute-start.14 = (f32[1,320]{1,0:T(1,128)S(1)}, f32[1,320]{1,0:T(1,128)S(1)}, u32[]{:S(2)}, u32[]{:S(2)}) collective-permute-start(f32[1,320]{1,0:T(1,128)S(1)} %get-tuple-element.65), channel_id=1, source_target_pairs={{0,16},{1,9},{2,18},{3,11},{4,20},{5,13},{6,22},{7,15},{8,24},{9,1... | collective-permute-start | bytes 3848 | tf_op jit(solution)/shard_map/ppermute | solution.py:254
  53.6 0.7 %collective-permute-start.15 = (f32[1,320]{1,0:T(1,128)S(1)}, f32[1,320]{1,0:T(1,128)S(1)}, u32[]{:S(2)}, u32[]{:S(2)}) collective-permute-start(f32[1,320]{1,0:T(1,128)S(1)} %get-tuple-element.66), channel_id=1, source_target_pairs={{0,24},{1,25},{2,26},{3,27},{4,28},{5,29},{6,30},{7,31},{8,16},{9,... | collective-permute-start | bytes 3848 | tf_op jit(solution)/shard_map/ppermute | solution.py:254
  54.3 1.8 %collective-permute-done.12 = f32[1,320]{1,0:T(1,128)S(1)} collective-permute-done((f32[1,320]{1,0:T(1,128)S(1)}, f32[1,320]{1,0:T(1,128)S(1)}, u32[]{:S(2)}, u32[]{:S(2)}) %collective-permute-start.12) | collective-permute-done | bytes 1312 | tf_op jit(solution)/shard_map/ppermute | solution.py:223
  56.2 1.9 %collective-permute-done.15 = f32[1,320]{1,0:T(1,128)S(1)} collective-permute-done((f32[1,320]{1,0:T(1,128)S(1)}, f32[1,320]{1,0:T(1,128)S(1)}, u32[]{:S(2)}, u32[]{:S(2)}) %collective-permute-start.15) | collective-permute-done | bytes 1312 | tf_op jit(solution)/shard_map/ppermute | solution.py:254
  (22 shorter events, 1.9 us)
Async XLA Ops:
  0.0 0.7 %copy-start.2 = (s32[320,1]{0,1:T(1,128)S(1)}, s32[320,1]{0,1:T(1,128)}, u32[]{:S(2)}) copy-start(s32[320,1]{0,1:T(1,128)} %param.4) | copy-start | bytes 3844
  0.7 1.0 %copy-start = (bf16[320,768]{1,0:T(8,128)(2,1)S(1)}, bf16[320,768]{1,0:T(8,128)(2,1)}, u32[]{:S(2)}) copy-start(bf16[320,768]{1,0:T(8,128)(2,1)} %embeddings.1) | copy-start | bytes 1474564
  1.7 0.7 %copy-start.1 = (s32[320]{0:T(512)S(1)}, s32[320]{0:T(512)}, u32[]{:S(2)}) copy-start(s32[320]{0:T(512)} %order_key.1) | copy-start | bytes 3844
  2.6 15.0 %collective-permute-start.1 = (bf16[336,768]{1,0:T(8,128)(2,1)S(1)}, bf16[336,768]{1,0:T(8,128)(2,1)S(1)}, u32[]{:S(2)}, u32[]{:S(2)}) collective-permute-start(bf16[336,768]{1,0:T(8,128)(2,1)S(1)} %shard_map.37.refs_0_.refs_2_.refs_3_.refs_1_), channel_id=1, source_target_pairs={{0,8},{1,17},{2,10},{3,19},{4,12},{5,21},{6,14},{7,23},{8,0},{9,25... | collective-permute-start | bytes 1548296 | tf_op jit(solution)/shard_map/ppermute | solution.py:211
  5.6 19.3 %collective-permute-start.4 = (bf16[336,768]{1,0:T(8,128)(2,1)S(1)}, bf16[336,768]{1,0:T(8,128)(2,1)S(1)}, u32[]{:S(2)}, u32[]{:S(2)}) collective-permute-start(bf16[336,768]{1,0:T(8,128)(2,1)S(1)} %shard_map.37.refs_0_.refs_2_.refs_3_.refs_1_), channel_id=1, source_target_pairs={{0,16},{1,9},{2,18},{3,11},{4,20},{5,13},{6,22},{7,15},{8,24},{9,1... | collective-permute-start | bytes 1548296 | tf_op jit(solution)/shard_map/ppermute | solution.py:213
  7.1 17.8 %collective-permute-start.3 = (bf16[336,768]{1,0:T(8,128)(2,1)S(1)}, bf16[336,768]{1,0:T(8,128)(2,1)S(1)}, u32[]{:S(2)}, u32[]{:S(2)}) collective-permute-start(bf16[336,768]{1,0:T(8,128)(2,1)S(1)} %shard_map.37.refs_0_.refs_2_.refs_3_.refs_1_), channel_id=1, source_target_pairs={{0,4},{1,5},{6,2},{7,3},{2,0},{3,1},{8,12},{9,13},{14,10},{15,11},... | collective-permute-start | bytes 1548296 | tf_op jit(solution)/shard_map/ppermute | solution.py:210
  17.6 9.4 %collective-permute-start.7 = (bf16[336,768]{1,0:T(8,128)(2,1)S(1)}, bf16[336,768]{1,0:T(8,128)(2,1)S(1)}, u32[]{:S(2)}, u32[]{:S(2)}) collective-permute-start(bf16[336,768]{1,0:T(8,128)(2,1)S(1)} %collective-permute-done.1.refs_3_.refs_4_.refs_2_), channel_id=1, source_target_pairs={{0,16},{1,9},{2,18},{3,11},{4,20},{5,13},{6,22},{7,15},{8,24},{9,1... | collective-permute-start | bytes 1548296 | tf_op jit(solution)/shard_map/ppermute | solution.py:214
  19.2 9.2 %collective-permute-start.2 = (bf16[336,768]{1,0:T(8,128)(2,1)S(1)}, bf16[336,768]{1,0:T(8,128)(2,1)S(1)}, u32[]{:S(2)}, u32[]{:S(2)}) collective-permute-start(bf16[336,768]{1,0:T(8,128)(2,1)S(1)} %shard_map.37.refs_0_.refs_2_.refs_3_.refs_1_), channel_id=1, source_target_pairs={{0,1},{1,0},{2,3},{3,2},{4,5},{5,4},{6,7},{7,6},{8,9},{9,8},{10,11... | collective-permute-start | bytes 1548296 | tf_op jit(solution)/shard_map/ppermute | solution.py:216
  19.2 17.3 %collective-permute-start = (bf16[336,768]{1,0:T(8,128)(2,1)S(1)}, bf16[336,768]{1,0:T(8,128)(2,1)S(1)}, u32[]{:S(2)}, u32[]{:S(2)}) collective-permute-start(bf16[336,768]{1,0:T(8,128)(2,1)S(1)} %shard_map.37.refs_0_.refs_2_.refs_3_.refs_1_), channel_id=1, source_target_pairs={{0,6},{1,7},{6,4},{7,5},{4,2},{5,3},{8,14},{9,15},{14,12},{15,13},... | collective-permute-start | bytes 1548296 | tf_op jit(solution)/shard_map/ppermute | solution.py:212
  26.4 2.0 %collective-permute-start.6 = (bf16[176,768]{1,0:T(8,128)(2,1)S(1)}, bf16[176,768]{1,0:T(8,128)(2,1)S(1)}, u32[]{:S(2)}, u32[]{:S(2)}) collective-permute-start(bf16[176,768]{1,0:T(8,128)(2,1)S(1)} %get-tuple-element.38), channel_id=1, source_target_pairs={{0,1},{1,0},{2,3},{3,2},{4,5},{5,4},{6,7},{7,6},{8,9},{9,8},{10,11... | collective-permute-start | bytes 811016 | tf_op jit(solution)/shard_map/ppermute | solution.py:231
  26.7 1.7 %collective-permute-start.5 = (bf16[160,768]{1,0:T(8,128)(2,1)S(1)}, bf16[160,768]{1,0:T(8,128)(2,1)S(1)}, u32[]{:S(2)}, u32[]{:S(2)}) collective-permute-start(bf16[160,768]{1,0:T(8,128)(2,1)S(1)} %get-tuple-element.37), channel_id=1, source_target_pairs={{0,1},{1,0},{2,3},{3,2},{4,5},{5,4},{6,7},{7,6},{8,9},{9,8},{10,11... | collective-permute-start | bytes 737288 | tf_op jit(solution)/shard_map/ppermute | solution.py:231
  36.5 11.8 %collective-permute-start.8 = (bf16[336,768]{1,0:T(8,128)(2,1)S(1)}, bf16[336,768]{1,0:T(8,128)(2,1)S(1)}, u32[]{:S(2)}, u32[]{:S(2)}) collective-permute-start(bf16[336,768]{1,0:T(8,128)(2,1)S(1)} %collective-permute-done.refs_0_), channel_id=1, source_target_pairs={{0,1},{1,0},{2,3},{3,2},{4,5},{5,4},{6,7},{7,6},{8,9},{9,8},{10,11... | collective-permute-start | bytes 1548296 | tf_op jit(solution)/shard_map/ppermute | solution.py:249
  37.6 14.7 %collective-permute-start.11 = (f32[1,320]{1,0:T(1,128)S(1)}, f32[1,320]{1,0:T(1,128)S(1)}, u32[]{:S(2)}, u32[]{:S(2)}) collective-permute-start(f32[1,320]{1,0:T(1,128)S(1)} %get-tuple-element.62), channel_id=1, source_target_pairs={{6,0},{7,1},{4,6},{5,7},{2,4},{3,5},{14,8},{15,9},{12,14},{13,15},... | collective-permute-start | bytes 3848 | tf_op jit(solution)/shard_map/ppermute | solution.py:223
  38.9 14.7 %collective-permute-start.10 = (f32[1,320]{1,0:T(1,128)S(1)}, f32[1,320]{1,0:T(1,128)S(1)}, u32[]{:S(2)}, u32[]{:S(2)}) collective-permute-start(f32[1,320]{1,0:T(1,128)S(1)} %get-tuple-element.61), channel_id=1, source_target_pairs={{5,0},{4,1},{3,6},{2,7},{1,2},{0,3},{13,8},{12,9},{11,14},{10,15},... | collective-permute-start | bytes 3848 | tf_op jit(solution)/shard_map/ppermute | solution.py:223
  43.3 11.0 %collective-permute-start.9 = (f32[1,320]{1,0:T(1,128)S(1)}, f32[1,320]{1,0:T(1,128)S(1)}, u32[]{:S(2)}, u32[]{:S(2)}) collective-permute-start(f32[1,320]{1,0:T(1,128)S(1)} %max.32), channel_id=1, source_target_pairs={{4,0},{5,1},{2,6},{3,7},{0,2},{1,3},{12,8},{13,9},{10,14},{11,15},... | collective-permute-start | bytes 3848 | tf_op jit(solution)/shard_map/ppermute | solution.py:223
  49.5 6.7 %collective-permute-start.12 = (f32[1,320]{1,0:T(1,128)S(1)}, f32[1,320]{1,0:T(1,128)S(1)}, u32[]{:S(2)}, u32[]{:S(2)}) collective-permute-start(f32[1,320]{1,0:T(1,128)S(1)} %get-tuple-element.63), channel_id=1, source_target_pairs={{7,0},{6,1},{5,6},{4,7},{3,4},{2,5},{15,8},{14,9},{13,14},{12,15},... | collective-permute-start | bytes 3848 | tf_op jit(solution)/shard_map/ppermute | solution.py:223
  50.8 5.4 %collective-permute-start.13 = (f32[1,320]{1,0:T(1,128)S(1)}, f32[1,320]{1,0:T(1,128)S(1)}, u32[]{:S(2)}, u32[]{:S(2)}) collective-permute-start(f32[1,320]{1,0:T(1,128)S(1)} %get-tuple-element.64), channel_id=1, source_target_pairs={{0,8},{1,17},{2,10},{3,19},{4,12},{5,21},{6,14},{7,23},{8,0},{9,25... | collective-permute-start | bytes 3848 | tf_op jit(solution)/shard_map/ppermute | solution.py:254
  52.3 3.8 %collective-permute-start.14 = (f32[1,320]{1,0:T(1,128)S(1)}, f32[1,320]{1,0:T(1,128)S(1)}, u32[]{:S(2)}, u32[]{:S(2)}) collective-permute-start(f32[1,320]{1,0:T(1,128)S(1)} %get-tuple-element.65), channel_id=1, source_target_pairs={{0,16},{1,9},{2,18},{3,11},{4,20},{5,13},{6,22},{7,15},{8,24},{9,1... | collective-permute-start | bytes 3848 | tf_op jit(solution)/shard_map/ppermute | solution.py:254
  53.6 4.5 %collective-permute-start.15 = (f32[1,320]{1,0:T(1,128)S(1)}, f32[1,320]{1,0:T(1,128)S(1)}, u32[]{:S(2)}, u32[]{:S(2)}) collective-permute-start(f32[1,320]{1,0:T(1,128)S(1)} %get-tuple-element.66), channel_id=1, source_target_pairs={{0,24},{1,25},{2,26},{3,27},{4,28},{5,29},{6,30},{7,31},{8,16},{9,... | collective-permute-start | bytes 3848 | tf_op jit(solution)/shard_map/ppermute | solution.py:254

commit v3 on v2

v3 whole, which is shorter than its diff:
```python
import functools

import jax
import jax.numpy as jnp
from jax import lax
from jax.experimental import pallas as pl
from jax.experimental.pallas import tpu as pltpu
from jax.sharding import PartitionSpec as P

EPSILON = 1e-06
EXTRA = 16
LANES = 128
TILE = 256
BOTH = ("dp", "grid")


def up(value, multiple):
    return -(-value // multiple) * multiple


def turned_to_column(row, rows):
    return jnp.broadcast_to(row, (LANES, row.shape[1])).T[:rows]


def codes(block, rows, span):
    parts = block[rows : rows + EXTRA, : up(rows, LANES)].astype(jnp.float32)
    return parts[2:3] * (4.0 * span) + parts[0:1] * 256.0 + parts[1:2]


def prepare_kernel(
    embeddings_hbm, cluster_hbm, order_key_hbm, block, embeddings, cluster, order_key, arrived
):
    copies = [
        pltpu.make_async_copy(source, target, arrived.at[at])
        for at, (source, target) in enumerate(
            (
                (embeddings_hbm, embeddings),
                (cluster_hbm, cluster),
                (order_key_hbm, order_key),
            )
        )
    ]
    for copy in copies:
        copy.start()
    for copy in copies:
        copy.wait()
    rows, width = embeddings.shape
    values = embeddings[...].astype(jnp.float32)
    scale = lax.rsqrt(jnp.sum(values * values, axis=1, keepdims=True) + EPSILON)
    block[0:rows, :] = (values * scale).astype(jnp.bfloat16)
    keys = order_key[...].reshape(1, rows)
    parts = [keys >> 8, keys & 255, cluster[...] + 1]
    parts = [part.astype(jnp.float32) for part in parts]
    parts = jnp.concatenate(parts + [jnp.zeros((EXTRA - 3, rows), jnp.float32)], axis=0)
    parts = jnp.concatenate([parts, jnp.zeros((EXTRA, width - rows), jnp.float32)], axis=1)
    block[rows : rows + EXTRA, :] = parts.astype(jnp.bfloat16)


def prepare(embeddings, cluster, order_key):
    rows, width = embeddings.shape
    inputs = (embeddings, cluster.reshape(1, rows), order_key)
    return pl.pallas_call(
        prepare_kernel,
        in_specs=[pl.BlockSpec(memory_space=pltpu.HBM)] * 3,
        out_shape=jax.ShapeDtypeStruct((rows + EXTRA, width), jnp.bfloat16),
        scratch_shapes=[pltpu.VMEM(array.shape, array.dtype) for array in inputs]
        + [pltpu.SemaphoreType.DMA((3,))],
        compiler_params=pltpu.CompilerParams(vmem_limit_bytes=56 << 20),
        cost_estimate=pl.CostEstimate(flops=rows, bytes_accessed=rows, transcendentals=0),
    )(*inputs)


def row_from_partial(partial, rows):
    padded = up(rows, LANES)
    if padded != rows:
        partial = jnp.concatenate(
            [partial, jnp.zeros((padded - rows, LANES), partial.dtype)], axis=0
        )
    return jnp.max(partial.T, axis=0, keepdims=True)[:, :rows]


def meet(block, rows, span, held, held_codes, to_block, to_held):
    column = turned_to_column(codes(block, rows, span), rows)
    partial = jnp.full((rows, LANES), -1.0, jnp.float32)
    best_held = []
    for at in range(0, held.shape[0], TILE):
        tile = min(TILE, held.shape[0] - at)
        sims = lax.dot_general(
            block[0:rows, :],
            held[at : at + tile, :],
            (((1,), (1,)), ((), ())),
            preferred_element_type=jnp.float32,
        )
        for lane in range(0, tile, LANES):
            part = sims[:, lane : lane + LANES]
            gap = column - held_codes[:, at + lane : at + lane + LANES]
            if to_block and to_held:
                part = jnp.where(jnp.abs(gap) < span, part, -1.0)
                later = gap > 0.0
                partial = jnp.maximum(partial, jnp.where(later, part, -1.0))
                other = jnp.where(later, -1.0, part)
            elif to_block:
                partial = jnp.maximum(
                    partial, jnp.where((gap > 0.0) & (gap < span), part, -1.0)
                )
            else:
                other = jnp.where((gap < 0.0) & (gap > -span), part, -1.0)
            if to_held:
                best_held.append(jnp.max(other, axis=0, keepdims=True))
    return (
        row_from_partial(partial, rows) if to_block else None,
        jnp.concatenate(best_held, axis=1) if to_held else None,
    )


def assemble(whole, pieces):
    top = 0
    for piece in pieces:
        whole[top : top + piece.shape[0], :] = piece[...]
        top += piece.shape[0]


def meet_kernel(rows, span, sizes, modes, groups, *refs):
    kinds = []
    for size in sizes:
        kinds.append(refs[:size])
        refs = refs[size:]
    blocks, holds, bests, outs, found, kept, scratch = kinds
    held, scratch = scratch[0], iter(scratch[1:])

    def whole(block):
        if len(block) == 1:
            return block[0]
        joined = next(scratch)
        assemble(joined, block)
        return joined

    blocks = [whole(block) for block in regrouped(blocks, groups[0])]
    holds = [whole(block) for block in regrouped(holds, groups[1])]
    total = held.shape[0]
    row = []
    for at, block in enumerate(holds):
        held[at * rows : (at + 1) * rows, :] = block[0:rows, :]
        row.append(codes(block, rows, span)[:, :rows])
    rest = total - len(holds) * rows
    if rest:
        held[total - rest :, :] = jnp.zeros((rest, held.shape[1]), held.dtype)
        row.append(jnp.zeros((1, rest), jnp.float32))
    row = jnp.concatenate(row, axis=1)
    best = None
    found = iter(found)
    for block, (to_block, to_held) in zip(blocks, modes):
        mine, theirs = meet(block, rows, span, held, row, to_block, to_held)
        if to_block:
            next(found)[...] = mine
        if to_held:
            best = theirs if best is None else jnp.maximum(best, theirs)
    if kept:
        top = 0
        for out in kept:
            out[...] = blocks[-1][top : top + out.shape[0], :]
            top += out.shape[0]
    parts = [best[:, at * rows : (at + 1) * rows] for at in range(len(holds))]
    if bests:
        parts = [jnp.maximum(part, earlier[...]) for part, earlier in zip(parts, bests)]
    for out, places in zip(outs, groups[2]):
        if len(places) == 1:
            out[...] = parts[places[0]]
        else:
            out[...] = jnp.concatenate([parts[place] for place in places], axis=1)


def regrouped(flat, lengths):
    flat = iter(flat)
    return [[next(flat) for _ in range(length)] for length in lengths]


def meeting(blocks, modes, holds, bests, rows, span, keep=(), together=None):
    width = blocks[0][0].shape[1]
    together = together or [(at,) for at in range(len(holds))]
    lengths = [[len(block) for block in some] for some in (blocks, holds)]
    flat = [[piece for block in some for piece in block] for some in (blocks, holds)]
    outs = [jax.ShapeDtypeStruct((1, rows * len(some)), jnp.float32) for some in together]
    found = [jax.ShapeDtypeStruct((1, rows), jnp.float32)] * sum(mode[0] for mode in modes)
    kept = [jax.ShapeDtypeStruct((height, width), jnp.bfloat16) for height in keep]
    split = sum(length > 1 for some in lengths for length in some)
    scratch = [pltpu.VMEM((up(len(holds) * rows, LANES), width), jnp.bfloat16)]
    scratch += [pltpu.VMEM((rows + EXTRA, width), jnp.bfloat16)] * split
    kinds = flat + [bests, outs, found, kept, scratch]
    results = pl.pallas_call(
        functools.partial(
            meet_kernel, rows, span, [len(kind) for kind in kinds], modes, lengths + [together]
        ),
        out_shape=outs + found + kept,
        scratch_shapes=scratch,
        compiler_params=pltpu.CompilerParams(vmem_limit_bytes=32 << 20),
        cost_estimate=pl.CostEstimate(flops=rows, bytes_accessed=rows, transcendentals=0),
    )(*flat[0], *flat[1], *bests)
    return regrouped(results, [len(outs), len(found), len(kept)])


OWN = (True, False)
HELD = (False, True)
TWO = (True, True)


def line_rounds(chips):
    if chips == 4:
        return [[(0, 2), (3, 1), (1, 0)], [(0, 3), (3, 2), (2, 1)]]
    rounds = []
    for shift in range(1, chips // 2 + 1):
        senders = chips // 2 if 2 * shift == chips else chips
        rounds.append([(s, (s + shift) % chips) for s in range(senders)])
    return rounds


def solution(mesh):
    groups, members = mesh.shape["dp"], mesh.shape["grid"]
    assert groups == 4 and members % 2 == 0
    chips = members // 2
    rounds = line_rounds(chips)

    def everywhere(target):
        return [
            (p * members + g, a * members + b)
            for p in range(groups)
            for g in range(members)
            for a, b in [target(p, g)]
        ]

    other_core = everywhere(lambda p, g: (p, g ^ 1))
    first = everywhere(lambda p, g: (p ^ (1 + g % 2), g))
    second = everywhere(lambda p, g: (p ^ (2 - g % 2), g))

    def along(pairs):
        return [
            (p * members + 2 * s + c, p * members + 2 * t + c)
            for p in range(groups)
            for s, t in pairs
            for c in range(2)
        ]

    def back(pairs):
        return [(target, source) for source, target in pairs]

    def shards(embeddings, cluster, order_key):
        rows = embeddings.shape[0]
        span = 256
        while span < rows * groups * members:
            span *= 2
        chip = lax.axis_index("grid") // 2
        block = prepare(embeddings, cluster, order_key)
        halves = (rows // 2, rows // 2 + EXTRA)
        own = [block]
        near = [[lax.ppermute(block, BOTH, along(pairs))] for pairs in rounds]
        from_first = [lax.ppermute(block, BOTH, first)]
        from_second = [lax.ppermute(block, BOTH, second)]
        from_corner = [
            lax.ppermute(piece, BOTH, second)
            for piece in (from_first[0][: halves[0]], from_first[0][halves[0] :])
        ]
        partner = lax.optimization_barrier((block, from_first[0]))[0]
        partner = [lax.ppermute(partner, BOTH, other_core)]

        results = []

        def give_back(mine, theirs, pairs):
            mine = jnp.maximum(mine, lax.ppermute(theirs, BOTH, other_core))
            mine = lax.ppermute(mine, BOTH, back(along(pairs)))
            senders = functools.reduce(jnp.logical_or, [chip == s for s, _ in pairs])
            results.append(jnp.where(senders, mine, -1.0))

        bests, (mine, one), pieces = meeting(
            [own, near[0]], [OWN, TWO], [own, from_first], [], rows, span, keep=halves
        )
        results.append(mine)
        pieces = [lax.ppermute(piece, BOTH, other_core) for piece in pieces]
        more_bests, (mine, one_more), _ = meeting(
            [own, near[0]], [OWN, TWO], [from_second, from_corner], [], rows, span
        )
        results.append(mine)
        held = [own, from_first, from_second, from_corner]
        bests, (other,), _ = meeting(
            [partner, pieces], [HELD, TWO], held, bests + more_bests, rows, span
        )
        give_back(jnp.maximum(one, one_more), other, rounds[0])
        for at, (pairs, one) in enumerate(zip(rounds[1:], near[1:])):
            one, bests = lax.optimization_barrier((one, bests))
            far = [lax.ppermute(piece, BOTH, other_core) for piece in one]
            bests, (mine,), _ = meeting([one], [TWO], held, bests, rows, span)
            last = at == len(rounds) - 2
            bests, (theirs,), _ = meeting(
                [far], [TWO], held, bests, rows, span, together=[(0,), (1, 3), (2,)] if last else None
            )
            give_back(mine, theirs, pairs)
        from_x = lax.ppermute(bests[1], BOTH, first)
        results.append(from_x[:, :rows])
        onward = jnp.maximum(bests[2], from_x[:, rows:])
        results.append(lax.ppermute(onward, BOTH, second))
        return functools.reduce(jnp.maximum, results, bests[0]).reshape(rows)

    placed = (P(BOTH, None), P(BOTH, None), P(BOTH))
    return jax.shard_map(
        shards, mesh=mesh, in_specs=placed, out_specs=P(BOTH), check_vma=False
    )
```

time: 59 us -> 49.4 us (0.84)
  waiting for transfers between devices: 16.6 us -> 11.2 us
  starting transfers between devices: 32.4 us -> 28.6 us
  local copies, waits for them, and re-layouts: 2.39 us -> 0.04 us
  Pallas kernels: 6.67 us -> 8.5 us
    ppermute x14, waiting for transfers between devices: 16.1 us -> 11.2 us  [the longest x2 5.67 us: shards(): lax.ppermute(piece, BOTH, second)]
    ppermute x14, starting transfers between devices: 31.8 us -> 28.5 us  [the longest x2 13.1 us: shards(): near = [[lax.ppermute(block, BOTH, along(pairs))] for pairs in rounds]]
    unnamed x6 -> x2, local copies, waits for them, and re-layouts: 2.39 us -> 0.01 us
    pallas_call x6, Pallas kernels: 6.67 us -> 8.5 us  [the longest x5 6.47 us: meeting(): pl.pallas_call(functools.partial(meet_kernel, rows, span, [len(kind) for...]
  transfers between devices with their start and end apart: 16 -> 16, of which waited for: 5 -> 6; matrix products, arithmetic and copies ran while one was open for 0% -> 0% of each run, Pallas kernels for 11% -> 13%
where the time goes in v3:
time: 49.4 us; the launch traced here: 49.2 us
  starting transfers between devices  28.6 us (58%)
  waiting for transfers between devices  11.2 us (23%)
  Pallas kernels  8.5 us (17%)
  other arithmetic  0.69 us (1%)
    ppermute x2, starting transfers between devices, shards(): near = [[lax.ppermute(block, BOTH, along(pairs))] for pairs in rounds]  13.1 us
    pallas_call x5, Pallas kernels, meeting(): pl.pallas_call(functools.partial(meet_kernel, rows, span, [len(kind) for...  6.47 us
    ppermute x2, waiting for transfers between devices, shards(): lax.ppermute(piece, BOTH, second)  5.67 us
    ppermute x2, waiting for transfers between devices, give_back(): mine = lax.ppermute(mine, BOTH, back(along(pairs)))  3.26 us
    ppermute x2, starting transfers between devices, give_back(): mine = lax.ppermute(mine, BOTH, back(along(pairs)))  3.2 us
    ppermute x1, starting transfers between devices, shards(): from_first = [lax.ppermute(block, BOTH, first)]  3 us
    ppermute x2, starting transfers between devices, shards(): lax.ppermute(piece, BOTH, second)  2.73 us
    ppermute x1, starting transfers between devices, shards(): results.append(lax.ppermute(onward, BOTH, second))  2.62 us
  transfers between devices with their start and end apart: 16, of which 6 were waited for; matrix products, arithmetic and copies ran while one was open for 0% of the time, Pallas kernels for 13%

profile of v3, /device:TPU:0, one launch (start us, length us, event | category | flops | bytes accessed | tf_op | source)
XLA Modules:
  0.0 49.2 jit_solution(2024738520767014281)
XLA Ops:
  0.0 2.0 %shard_map.37.refs_0_.refs_2_.refs_3_.refs_1_ = bf16[336,768]{1,0:T(8,128)(2,1)} custom-call(bf16[320,768]{1,0:T(8,128)(2,1)} %embeddings_hbm.1, s32[1,320]{1,0:T(1,128)} %bitcast.1, s32[320]{0:T(512)} %order_key_hbm.1), custom_call_target="tpu_custom_call" | custom-call | flops 320 | bytes 320 | tf_op jit(solution)/shard_map/pallas_call | solution.py:62
  2.1 3.0 %collective-permute-start.1 = (bf16[336,768]{1,0:T(8,128)(2,1)}, bf16[336,768]{1,0:T(8,128)(2,1)S(1)}, u32[]{:S(2)}, u32[]{:S(2)}) collective-permute-start(bf16[336,768]{1,0:T(8,128)(2,1)} %shard_map.37.refs_0_.refs_2_.refs_3_.refs_1_), channel_id=1, source_target_pairs={{0,8},{1,17},{2,10},{3,19},{4,12},{5,21},{6,14},{7,23},{8,0},{9,25... | collective-permute-start | bytes 1548296 | tf_op jit(solution)/shard_map/ppermute | solution.py:256
  5.1 4.5 %collective-permute-start.3 = (bf16[336,768]{1,0:T(8,128)(2,1)}, bf16[336,768]{1,0:T(8,128)(2,1)S(1)}, u32[]{:S(2)}, u32[]{:S(2)}) collective-permute-start(bf16[336,768]{1,0:T(8,128)(2,1)} %shard_map.37.refs_0_.refs_2_.refs_3_.refs_1_), channel_id=1, source_target_pairs={{0,4},{1,5},{6,2},{7,3},{2,0},{3,1},{8,12},{9,13},{14,10},{15,11},... | collective-permute-start | bytes 1548296 | tf_op jit(solution)/shard_map/ppermute | solution.py:255
  9.6 1.6 %collective-permute-start.6 = (bf16[336,768]{1,0:T(8,128)(2,1)}, bf16[336,768]{1,0:T(8,128)(2,1)S(1)}, u32[]{:S(2)}, u32[]{:S(2)}) collective-permute-start(bf16[336,768]{1,0:T(8,128)(2,1)} %shard_map.37.refs_0_.refs_2_.refs_3_.refs_1_), channel_id=1, source_target_pairs={{0,16},{1,9},{2,18},{3,11},{4,20},{5,13},{6,22},{7,15},{8,24},{9,1... | collective-permute-start | bytes 1548296 | tf_op jit(solution)/shard_map/ppermute | solution.py:257
  11.1 1.9 %collective-permute-done.1.refs_3_.refs_4_.refs_2_ = bf16[336,768]{1,0:T(8,128)(2,1)S(1)} collective-permute-done((bf16[336,768]{1,0:T(8,128)(2,1)}, bf16[336,768]{1,0:T(8,128)(2,1)S(1)}, u32[]{:S(2)}, u32[]{:S(2)}) %collective-permute-start.1) | collective-permute-done | bytes 516128 | tf_op jit(solution)/shard_map/ppermute | solution.py:256
  13.1 8.6 %collective-permute-start = (bf16[336,768]{1,0:T(8,128)(2,1)}, bf16[336,768]{1,0:T(8,128)(2,1)S(1)}, u32[]{:S(2)}, u32[]{:S(2)}) collective-permute-start(bf16[336,768]{1,0:T(8,128)(2,1)} %shard_map.37.refs_0_.refs_2_.refs_3_.refs_1_), channel_id=1, source_target_pairs={{0,6},{1,7},{6,4},{7,5},{4,2},{5,3},{8,14},{9,15},{14,12},{15,13},... | collective-permute-start | bytes 1548296 | tf_op jit(solution)/shard_map/ppermute | solution.py:255
  21.7 2.6 %collective-permute-start.7 = (bf16[160,768]{1,0:T(8,128)(2,1)S(1)}, bf16[160,768]{1,0:T(8,128)(2,1)S(1)}, u32[]{:S(2)}, u32[]{:S(2)}) collective-permute-start(bf16[160,768]{1,0:T(8,128)(2,1)S(1)} %slice.16), channel_id=1, source_target_pairs={{0,16},{1,9},{2,18},{3,11},{4,20},{5,13},{6,22},{7,15},{8,24},{9,1... | collective-permute-start | bytes 737288 | tf_op jit(solution)/shard_map/ppermute | solution.py:259
  24.5 1.2 %shard_map.38 = (f32[1,320]{1,0:T(1,128)S(1)}, f32[1,320]{1,0:T(1,128)S(1)}, f32[1,320]{1,0:T(1,128)S(1)}, f32[1,320]{1,0:T(1,128)S(1)}, bf16[160,768]{1,0:T(8,128)(2,1)S(1)}, /*index=5*/bf16[176,768]{1,0:T(8,128)(2,1)S(1)}) custom-call(bf16[336,768]{1,0:T(8,128)(2,1)S(1)} %copy-done, bf16[336,768]{1,0:T(8,128)(2,1)S(1)} %collective-permute-done.3.refs_1_, ...), custom_call_target="tpu_custom_call" | custom-call | flops 320 | bytes 320 | tf_op jit(solution)/shard_map/pallas_call | solution.py:190
  25.8 2.8 %collective-permute-done.7.refs_3_.refs_6_.refs_4_ = bf16[160,768]{1,0:T(8,128)(2,1)S(1)} collective-permute-done((bf16[160,768]{1,0:T(8,128)(2,1)S(1)}, bf16[160,768]{1,0:T(8,128)(2,1)S(1)}, u32[]{:S(2)}, u32[]{:S(2)}) %collective-permute-start.7) | collective-permute-done | bytes 245792 | tf_op jit(solution)/shard_map/ppermute | solution.py:259
  28.6 2.9 %collective-permute-done.8.refs_4_.refs_7_.refs_5_ = bf16[176,768]{1,0:T(8,128)(2,1)S(1)} collective-permute-done((bf16[176,768]{1,0:T(8,128)(2,1)S(1)}, bf16[176,768]{1,0:T(8,128)(2,1)S(1)}, u32[]{:S(2)}, u32[]{:S(2)}) %collective-permute-start.8) | collective-permute-done | bytes 270368 | tf_op jit(solution)/shard_map/ppermute | solution.py:259
  31.5 1.2 %shard_map.39 = (f32[1,320]{1,0:T(1,128)S(1)}, f32[1,320]{1,0:T(1,128)S(1)}, f32[1,320]{1,0:T(1,128)S(1)}, f32[1,320]{1,0:T(1,128)S(1)}) custom-call(bf16[336,768]{1,0:T(8,128)(2,1)S(1)} %copy-done, bf16[336,768]{1,0:T(8,128)(2,1)S(1)} %collective-permute-done.3.refs_1_, bf16[336,768]{1,0:T(8,128)(2,1)S(1)} %collective-permute-done.6.refs_2_.refs_5_.refs_3_, ...), custom_call_target="tpu_custom_call" | custom-call | flops 320 | bytes 320 | tf_op jit(solution)/shard_map/pallas_call | solution.py:190
  32.7 1.8 %shard_map.40 = (f32[1,320]{1,0:T(1,128)S(1)}, f32[1,320]{1,0:T(1,128)S(1)}, f32[1,320]{1,0:T(1,128)S(1)}, f32[1,320]{1,0:T(1,128)S(1)}, f32[1,320]{1,0:T(1,128)S(1)}) custom-call(bf16[336,768]{1,0:T(8,128)(2,1)S(1)} %collective-permute-done.2.refs_0_, bf16[160,768]{1,0:T(8,128)(2,1)S(1)} %collective-permute-done.4.refs_1_, ...), custom_call_target="tpu_custom_call" | custom-call | flops 320 | bytes 320 | tf_op jit(solution)/shard_map/pallas_call | solution.py:190
  34.6 0.5 %collective-permute-start.10 = (f32[1,320]{1,0:T(1,128)S(1)}, f32[1,320]{1,0:T(1,128)S(1)}, u32[]{:S(2)}, u32[]{:S(2)}) collective-permute-start(f32[1,320]{1,0:T(1,128)S(1)} %get-tuple-element.60), channel_id=1, source_target_pairs={{0,1},{1,0},{2,3},{3,2},{4,5},{5,4},{6,7},{7,6},{8,9},{9,8},{10,11... | collective-permute-start | bytes 3848 | tf_op jit(solution)/shard_map/ppermute | solution.py:268
  35.1 1.1 %shard_map.41 = (f32[1,320]{1,0:T(1,128)S(1)}, f32[1,320]{1,0:T(1,128)S(1)}, f32[1,320]{1,0:T(1,128)S(1)}, f32[1,320]{1,0:T(1,128)S(1)}, f32[1,320]{1,0:T(1,128)S(1)}) custom-call(bf16[336,768]{1,0:T(8,128)(2,1)S(1)} %collective-permute-done.refs_0_, bf16[336,768]{1,0:T(8,128)(2,1)S(1)} %copy-done, ...), custom_call_target="tpu_custom_call" | custom-call | flops 320 | bytes 320 | tf_op jit(solution)/shard_map/pallas_call | solution.py:190
  36.2 0.3 collective-permute-done.9.refs_0_
  36.5 1.1 %shard_map.42 = (f32[1,320]{1,0:T(1,128)S(1)}, f32[1,640]{1,0:T(1,128)S(1)}, f32[1,320]{1,0:T(1,128)S(1)}, f32[1,320]{1,0:T(1,128)S(1)}) custom-call(bf16[336,768]{1,0:T(8,128)(2,1)S(1)} %collective-permute-done.9.refs_0_, bf16[336,768]{1,0:T(8,128)(2,1)S(1)} %copy-done, bf16[336,768]{1,0:T(8,128)(2,1)S(1)} %collective-permute-done.1.refs_3_.refs_4_.refs_2_, ...), custom_call_target="tpu_custom_call" | custom-call | flops 320 | bytes 320 | tf_op jit(solution)/shard_map/pallas_call | solution.py:190
  37.6 0.2 collective-permute-start.12
  37.8 1.5 %collective-permute-start.14 = (f32[1,640]{1,0:T(1,128)S(1)}, f32[1,640]{1,0:T(1,128)S(1)}, u32[]{:S(2)}, u32[]{:S(2)}) collective-permute-start(f32[1,640]{1,0:T(1,128)S(1)} %get-tuple-element.63), channel_id=1, source_target_pairs={{0,8},{1,17},{2,10},{3,19},{4,12},{5,21},{6,14},{7,23},{8,0},{9,25... | collective-permute-start | bytes 7688 | tf_op jit(solution)/shard_map/ppermute | solution.py:296
  39.3 1.9 %collective-permute-start.11 = (f32[1,320]{1,0:T(1,128)S(1)}, f32[1,320]{1,0:T(1,128)S(1)}, u32[]{:S(2)}, u32[]{:S(2)}) collective-permute-start(f32[1,320]{1,0:T(1,128)S(1)} %maximum_maximum_fusion), channel_id=1, source_target_pairs={{4,0},{5,1},{2,6},{3,7},{0,2},{1,3},{12,8},{13,9},{10,14},{11,15},... | collective-permute-start | bytes 3848 | tf_op jit(solution)/shard_map/ppermute | solution.py:269
  41.3 1.3 %collective-permute-start.13 = (f32[1,320]{1,0:T(1,128)S(1)}, f32[1,320]{1,0:T(1,128)S(1)}, u32[]{:S(2)}, u32[]{:S(2)}) collective-permute-start(f32[1,320]{1,0:T(1,128)S(1)} %max.35), channel_id=1, source_target_pairs={{6,0},{7,1},{4,6},{5,7},{2,4},{3,5},{14,8},{15,9},{12,14},{13,15},... | collective-permute-start | bytes 3848 | tf_op jit(solution)/shard_map/ppermute | solution.py:269
  42.7 2.6 %collective-permute-start.15 = (f32[1,320]{1,0:T(1,128)S(1)}, f32[1,320]{1,0:T(1,128)S(1)}, u32[]{:S(2)}, u32[]{:S(2)}) collective-permute-start(f32[1,320]{1,0:T(1,128)S(1)} %slice_maximum_fusion), channel_id=1, source_target_pairs={{0,16},{1,9},{2,18},{3,11},{4,20},{5,13},{6,22},{7,15},{8,24},{9,1... | collective-permute-start | bytes 3848 | tf_op jit(solution)/shard_map/ppermute | solution.py:299
  45.3 0.4 collective-permute-done.11
  45.7 2.9 %collective-permute-done.13 = f32[1,320]{1,0:T(1,128)S(1)} collective-permute-done((f32[1,320]{1,0:T(1,128)S(1)}, f32[1,320]{1,0:T(1,128)S(1)}, u32[]{:S(2)}, u32[]{:S(2)}) %collective-permute-start.13) | collective-permute-done | bytes 1312 | tf_op jit(solution)/shard_map/ppermute | solution.py:269
  48.6 0.6 %maximum_reduce_fusion = f32[320]{0:T(512)} fusion(f32[1,320]{1,0:T(1,128)S(1)} %collective-permute-done.15, f32[1,640]{1,0:T(1,128)S(1)} %collective-permute-done.14, f32[1,320]{1,0:T(1,128)S(1)} %collective-permute-done.13, pred[]{:T(512)S(6)} %or.12, f32[1,320]{1,0:T(1,128)S(1)} %collective-permute-done.11, pred[]{:T(512)S(6)} %or.11, ...), kind=kLoop, calls=%fused_computation.6 | loop fusion | flops 2560 | bytes 10242 | tf_op jit(solution)/shard_map/max | solution.py:300
  (22 shorter events, 0.4 us)
Async XLA Ops:
  2.0 22.5 %copy-start = (bf16[336,768]{1,0:T(8,128)(2,1)S(1)}, bf16[336,768]{1,0:T(8,128)(2,1)}, u32[]{:S(2)}) copy-start(bf16[336,768]{1,0:T(8,128)(2,1)} %shard_map.37.refs_0_.refs_2_.refs_3_.refs_1_) | copy-start | bytes 1548292
  2.1 11.0 %collective-permute-start.1 = (bf16[336,768]{1,0:T(8,128)(2,1)}, bf16[336,768]{1,0:T(8,128)(2,1)S(1)}, u32[]{:S(2)}, u32[]{:S(2)}) collective-permute-start(bf16[336,768]{1,0:T(8,128)(2,1)} %shard_map.37.refs_0_.refs_2_.refs_3_.refs_1_), channel_id=1, source_target_pairs={{0,8},{1,17},{2,10},{3,19},{4,12},{5,21},{6,14},{7,23},{8,0},{9,25... | collective-permute-start | bytes 1548296 | tf_op jit(solution)/shard_map/ppermute | solution.py:256
  5.1 19.4 %collective-permute-start.3 = (bf16[336,768]{1,0:T(8,128)(2,1)}, bf16[336,768]{1,0:T(8,128)(2,1)S(1)}, u32[]{:S(2)}, u32[]{:S(2)}) collective-permute-start(bf16[336,768]{1,0:T(8,128)(2,1)} %shard_map.37.refs_0_.refs_2_.refs_3_.refs_1_), channel_id=1, source_target_pairs={{0,4},{1,5},{6,2},{7,3},{2,0},{3,1},{8,12},{9,13},{14,10},{15,11},... | collective-permute-start | bytes 1548296 | tf_op jit(solution)/shard_map/ppermute | solution.py:255
  9.6 16.2 %collective-permute-start.6 = (bf16[336,768]{1,0:T(8,128)(2,1)}, bf16[336,768]{1,0:T(8,128)(2,1)S(1)}, u32[]{:S(2)}, u32[]{:S(2)}) collective-permute-start(bf16[336,768]{1,0:T(8,128)(2,1)} %shard_map.37.refs_0_.refs_2_.refs_3_.refs_1_), channel_id=1, source_target_pairs={{0,16},{1,9},{2,18},{3,11},{4,20},{5,13},{6,22},{7,15},{8,24},{9,1... | collective-permute-start | bytes 1548296 | tf_op jit(solution)/shard_map/ppermute | solution.py:257
  13.1 19.6 %collective-permute-start.2 = (bf16[336,768]{1,0:T(8,128)(2,1)}, bf16[336,768]{1,0:T(8,128)(2,1)S(1)}, u32[]{:S(2)}, u32[]{:S(2)}) collective-permute-start(bf16[336,768]{1,0:T(8,128)(2,1)} %shard_map.37.refs_0_.refs_2_.refs_3_.refs_1_), channel_id=1, source_target_pairs={{0,1},{1,0},{2,3},{3,2},{4,5},{5,4},{6,7},{7,6},{8,9},{9,8},{10,11... | collective-permute-start | bytes 1548296 | tf_op jit(solution)/shard_map/ppermute | solution.py:263
  13.1 21.5 %collective-permute-start = (bf16[336,768]{1,0:T(8,128)(2,1)}, bf16[336,768]{1,0:T(8,128)(2,1)S(1)}, u32[]{:S(2)}, u32[]{:S(2)}) collective-permute-start(bf16[336,768]{1,0:T(8,128)(2,1)} %shard_map.37.refs_0_.refs_2_.refs_3_.refs_1_), channel_id=1, source_target_pairs={{0,6},{1,7},{6,4},{7,5},{4,2},{5,3},{8,14},{9,15},{14,12},{15,13},... | collective-permute-start | bytes 1548296 | tf_op jit(solution)/shard_map/ppermute | solution.py:255
  21.7 6.8 %collective-permute-start.7 = (bf16[160,768]{1,0:T(8,128)(2,1)S(1)}, bf16[160,768]{1,0:T(8,128)(2,1)S(1)}, u32[]{:S(2)}, u32[]{:S(2)}) collective-permute-start(bf16[160,768]{1,0:T(8,128)(2,1)S(1)} %slice.16), channel_id=1, source_target_pairs={{0,16},{1,9},{2,18},{3,11},{4,20},{5,13},{6,22},{7,15},{8,24},{9,1... | collective-permute-start | bytes 737288 | tf_op jit(solution)/shard_map/ppermute | solution.py:259
  24.4 7.0 %collective-permute-start.8 = (bf16[176,768]{1,0:T(8,128)(2,1)S(1)}, bf16[176,768]{1,0:T(8,128)(2,1)S(1)}, u32[]{:S(2)}, u32[]{:S(2)}) collective-permute-start(bf16[176,768]{1,0:T(8,128)(2,1)S(1)} %slice.17), channel_id=1, source_target_pairs={{0,16},{1,9},{2,18},{3,11},{4,20},{5,13},{6,22},{7,15},{8,24},{9,1... | collective-permute-start | bytes 811016 | tf_op jit(solution)/shard_map/ppermute | solution.py:259
  25.7 7.0 %collective-permute-start.5 = (bf16[176,768]{1,0:T(8,128)(2,1)S(1)}, bf16[176,768]{1,0:T(8,128)(2,1)S(1)}, u32[]{:S(2)}, u32[]{:S(2)}) collective-permute-start(bf16[176,768]{1,0:T(8,128)(2,1)S(1)} %get-tuple-element.37), channel_id=1, source_target_pairs={{0,1},{1,0},{2,3},{3,2},{4,5},{5,4},{6,7},{7,6},{8,9},{9,8},{10,11... | collective-permute-start | bytes 811016 | tf_op jit(solution)/shard_map/ppermute | solution.py:277
  28.6 4.1 %collective-permute-start.4 = (bf16[160,768]{1,0:T(8,128)(2,1)S(1)}, bf16[160,768]{1,0:T(8,128)(2,1)S(1)}, u32[]{:S(2)}, u32[]{:S(2)}) collective-permute-start(bf16[160,768]{1,0:T(8,128)(2,1)S(1)} %get-tuple-element.36), channel_id=1, source_target_pairs={{0,1},{1,0},{2,3},{3,2},{4,5},{5,4},{6,7},{7,6},{8,9},{9,8},{10,11... | collective-permute-start | bytes 737288 | tf_op jit(solution)/shard_map/ppermute | solution.py:277
  34.5 2.0 %collective-permute-start.9 = (bf16[336,768]{1,0:T(8,128)(2,1)S(1)}, bf16[336,768]{1,0:T(8,128)(2,1)S(1)}, u32[]{:S(2)}, u32[]{:S(2)}) collective-permute-start(bf16[336,768]{1,0:T(8,128)(2,1)S(1)} %collective-permute-done.refs_0_), channel_id=1, source_target_pairs={{0,1},{1,0},{2,3},{3,2},{4,5},{5,4},{6,7},{7,6},{8,9},{9,8},{10,11... | collective-permute-start | bytes 1548296 | tf_op jit(solution)/shard_map/ppermute | solution.py:289
  34.6 4.7 %collective-permute-start.10 = (f32[1,320]{1,0:T(1,128)S(1)}, f32[1,320]{1,0:T(1,128)S(1)}, u32[]{:S(2)}, u32[]{:S(2)}) collective-permute-start(f32[1,320]{1,0:T(1,128)S(1)} %get-tuple-element.60), channel_id=1, source_target_pairs={{0,1},{1,0},{2,3},{3,2},{4,5},{5,4},{6,7},{7,6},{8,9},{9,8},{10,11... | collective-permute-start | bytes 3848 | tf_op jit(solution)/shard_map/ppermute | solution.py:268
  37.6 3.6 %collective-permute-start.12 = (f32[1,320]{1,0:T(1,128)S(1)}, f32[1,320]{1,0:T(1,128)S(1)}, u32[]{:S(2)}, u32[]{:S(2)}) collective-permute-start(f32[1,320]{1,0:T(1,128)S(1)} %get-tuple-element.62), channel_id=1, source_target_pairs={{0,1},{1,0},{2,3},{3,2},{4,5},{5,4},{6,7},{7,6},{8,9},{9,8},{10,11... | collective-permute-start | bytes 3848 | tf_op jit(solution)/shard_map/ppermute | solution.py:268
  37.8 4.7 %collective-permute-start.14 = (f32[1,640]{1,0:T(1,128)S(1)}, f32[1,640]{1,0:T(1,128)S(1)}, u32[]{:S(2)}, u32[]{:S(2)}) collective-permute-start(f32[1,640]{1,0:T(1,128)S(1)} %get-tuple-element.63), channel_id=1, source_target_pairs={{0,8},{1,17},{2,10},{3,19},{4,12},{5,21},{6,14},{7,23},{8,0},{9,25... | collective-permute-start | bytes 7688 | tf_op jit(solution)/shard_map/ppermute | solution.py:296
  39.3 6.4 %collective-permute-start.11 = (f32[1,320]{1,0:T(1,128)S(1)}, f32[1,320]{1,0:T(1,128)S(1)}, u32[]{:S(2)}, u32[]{:S(2)}) collective-permute-start(f32[1,320]{1,0:T(1,128)S(1)} %maximum_maximum_fusion), channel_id=1, source_target_pairs={{4,0},{5,1},{2,6},{3,7},{0,2},{1,3},{12,8},{13,9},{10,14},{11,15},... | collective-permute-start | bytes 3848 | tf_op jit(solution)/shard_map/ppermute | solution.py:269
  41.3 7.3 %collective-permute-start.13 = (f32[1,320]{1,0:T(1,128)S(1)}, f32[1,320]{1,0:T(1,128)S(1)}, u32[]{:S(2)}, u32[]{:S(2)}) collective-permute-start(f32[1,320]{1,0:T(1,128)S(1)} %max.35), channel_id=1, source_target_pairs={{6,0},{7,1},{4,6},{5,7},{2,4},{3,5},{14,8},{15,9},{12,14},{13,15},... | collective-permute-start | bytes 3848 | tf_op jit(solution)/shard_map/ppermute | solution.py:269
  42.7 5.9 %collective-permute-start.15 = (f32[1,320]{1,0:T(1,128)S(1)}, f32[1,320]{1,0:T(1,128)S(1)}, u32[]{:S(2)}, u32[]{:S(2)}) collective-permute-start(f32[1,320]{1,0:T(1,128)S(1)} %slice_maximum_fusion), channel_id=1, source_target_pairs={{0,16},{1,9},{2,18},{3,11},{4,20},{5,13},{6,22},{7,15},{8,24},{9,1... | collective-permute-start | bytes 3848 | tf_op jit(solution)/shard_map/ppermute | solution.py:299

commit v4 on v3

--- a/solution.py
+++ b/solution.py
@@ -219,6 +219,7 @@
     assert groups == 4 and members % 2 == 0
     chips = members // 2
     rounds = line_rounds(chips)
+    rounds += [[]] * (len(rounds) % 2)
 
     def everywhere(target):
         return [
@@ -232,12 +233,12 @@
     first = everywhere(lambda p, g: (p ^ (1 + g % 2), g))
     second = everywhere(lambda p, g: (p ^ (2 - g % 2), g))
 
-    def along(pairs):
+    def along(pairs, *cores):
         return [
             (p * members + 2 * s + c, p * members + 2 * t + c)
             for p in range(groups)
             for s, t in pairs
-            for c in range(2)
+            for c in cores
         ]
 
     def back(pairs):
@@ -248,27 +249,19 @@
         span = 256
         while span < rows * groups * members:
             span *= 2
-        chip = lax.axis_index("grid") // 2
+        chip, core = lax.axis_index("grid") // 2, lax.axis_index("grid") % 2
         block = prepare(embeddings, cluster, order_key)
         halves = (rows // 2, rows // 2 + EXTRA)
         own = [block]
-        near = [[lax.ppermute(block, BOTH, along(pairs))] for pairs in rounds]
+        near = [[lax.ppermute(block, BOTH, along(pairs, 0, 1))] for pairs in rounds]
         from_first = [lax.ppermute(block, BOTH, first)]
-        from_second = [lax.ppermute(block, BOTH, second)]
-        from_corner = [
-            lax.ppermute(piece, BOTH, second)
-            for piece in (from_first[0][: halves[0]], from_first[0][halves[0] :])
-        ]
-        partner = lax.optimization_barrier((block, from_first[0]))[0]
-        partner = [lax.ppermute(partner, BOTH, other_core)]
+        from_corner = [lax.ppermute(from_first[0], BOTH, second)]
+        later = lax.optimization_barrier((block, from_first[0]))[0]
+        from_second = [lax.ppermute(later, BOTH, second)]
+        partner = [lax.ppermute(later, BOTH, other_core)]
 
         results = []
-
-        def give_back(mine, theirs, pairs):
-            mine = jnp.maximum(mine, lax.ppermute(theirs, BOTH, other_core))
-            mine = lax.ppermute(mine, BOTH, back(along(pairs)))
-            senders = functools.reduce(jnp.logical_or, [chip == s for s, _ in pairs])
-            results.append(jnp.where(senders, mine, -1.0))
+        turned = []
 
         bests, (mine, one), pieces = meeting(
             [own, near[0]], [OWN, TWO], [own, from_first], [], rows, span, keep=halves
@@ -283,7 +276,7 @@
         bests, (other,), _ = meeting(
             [partner, pieces], [HELD, TWO], held, bests + more_bests, rows, span
         )
-        give_back(jnp.maximum(one, one_more), other, rounds[0])
+        turned.append(jnp.concatenate([jnp.maximum(one, one_more), other], axis=1))
         for at, (pairs, one) in enumerate(zip(rounds[1:], near[1:])):
             one, bests = lax.optimization_barrier((one, bests))
             far = [lax.ppermute(piece, BOTH, other_core) for piece in one]
@@ -292,7 +285,20 @@
             bests, (theirs,), _ = meeting(
                 [far], [TWO], held, bests, rows, span, together=[(0,), (1, 3), (2,)] if last else None
             )
-            give_back(mine, theirs, pairs)
+            turned.append(jnp.concatenate([mine, theirs], axis=1))
+        for at in range(0, len(rounds), 2):
+            even, odd = turned[at], turned[at + 1]
+            sent = lax.ppermute(jnp.where(core == 0, odd, even), BOTH, other_core)
+            kept = jnp.where(core == 0, even, odd)
+            kept = jnp.maximum(kept, jnp.concatenate([sent[:, rows:], sent[:, :rows]], axis=1))
+            pairs = along(rounds[at], 0) + along(rounds[at + 1], 1)
+            kept = lax.ppermute(kept, BOTH, back(pairs))
+            sender = functools.reduce(
+                jnp.logical_or,
+                [(chip == s) & (core == c) for c in range(2) for s, _ in rounds[at + c]],
+            )
+            kept = jnp.where(sender, kept, -1.0)
+            results += [kept[:, :rows], lax.ppermute(kept[:, rows:], BOTH, other_core)]
         from_x = lax.ppermute(bests[1], BOTH, first)
         results.append(from_x[:, :rows])
         onward = jnp.maximum(bests[2], from_x[:, rows:])

time: 49.4 us -> 45.9 us (0.929)
  starting transfers between devices: 28.6 us -> 22.3 us
  waiting for transfers between devices: 11.2 us -> 12.8 us
  local copies, waits for them, and re-layouts: 0.04 us -> 1.19 us
    ppermute x10 -> x8, starting transfers between devices: 21.3 us -> 16.7 us  [the longest x2 10.5 us: shards(): near = [[lax.ppermute(block, BOTH, along(pairs, 0, 1))] for pairs in rounds]]
    ppermute x1, starting transfers between devices: 2.62 us -> 0.52 us  [shards(): results.append(lax.ppermute(onward, BOTH, second))]
    unnamed x2 -> x4, local copies, waits for them, and re-layouts: 0.01 us -> 1.04 us
    ppermute x1, waiting for transfers between devices: 1.93 us -> 2.79 us  [shards(): from_first = [lax.ppermute(block, BOTH, first)]]
    ppermute x1, waiting for transfers between devices: 0.28 us -> 0.79 us  [shards(): far = [lax.ppermute(piece, BOTH, other_core) for piece in one]]
    ppermute x2, starting transfers between devices: 0.07 us -> 0.58 us  [shards(): pieces = [lax.ppermute(piece, BOTH, other_core) for piece in pieces]]
    ppermute x10 -> x8, waiting for transfers between devices: 8.94 us -> 9.08 us  [the longest x1 3.79 us: shards(): from_corner = [lax.ppermute(from_first[0], BOTH, second)]]
  transfers between devices with their start and end apart: 16 -> 14, of which waited for: 6 -> 8; matrix products, arithmetic and copies ran while one was open for 0% -> 1% of each run, Pallas kernels for 13% -> 12%
where the time goes in v4:
time: 45.9 us; the launch traced here: 45.7 us
  starting transfers between devices  22.3 us (49%)
  waiting for transfers between devices  12.8 us (28%)
  Pallas kernels  8.46 us (18%)
  local copies, waits for them, and re-layouts  1.19 us (3%)
  other arithmetic  0.84 us (2%)
    ppermute x2, starting transfers between devices, shards(): near = [[lax.ppermute(block, BOTH, along(pairs, 0, 1))] for pairs in rounds]  10.5 us
    pallas_call x5, Pallas kernels, meeting(): pl.pallas_call(functools.partial(meet_kernel, rows, span, [len(kind) for...  6.43 us
    ppermute x1, waiting for transfers between devices, shards(): from_corner = [lax.ppermute(from_first[0], BOTH, second)]  3.79 us
    ppermute x1, starting transfers between devices, shards(): kept = lax.ppermute(kept, BOTH, back(pairs))  3.44 us
    ppermute x1, starting transfers between devices, shards(): from_first = [lax.ppermute(block, BOTH, first)]  3 us
    ppermute x1, waiting for transfers between devices, shards(): from_first = [lax.ppermute(block, BOTH, first)]  2.79 us
    ppermute x1, waiting for transfers between devices, shards(): kept = lax.ppermute(kept, BOTH, back(pairs))  2.32 us
    ppermute x2, waiting for transfers between devices, shards(): near = [[lax.ppermute(block, BOTH, along(pairs, 0, 1))] for pairs in rounds]  2.29 us
  transfers between devices with their start and end apart: 14, of which 8 were waited for; matrix products, arithmetic and copies ran while one was open for 1% of the time, Pallas kernels for 12%

profile of v4, /device:TPU:0, one launch (start us, length us, event | category | flops | bytes accessed | tf_op | source)
XLA Modules:
  0.0 45.7 jit_solution(10072247176990561234)
XLA Ops:
  0.0 2.0 %shard_map.37.refs_0_.refs_2_.refs_3_.refs_1_ = bf16[336,768]{1,0:T(8,128)(2,1)} custom-call(bf16[320,768]{1,0:T(8,128)(2,1)} %embeddings_hbm.1, s32[1,320]{1,0:T(1,128)} %bitcast.1, s32[320]{0:T(512)} %order_key_hbm.1), custom_call_target="tpu_custom_call" | custom-call | flops 320 | bytes 320 | tf_op jit(solution)/shard_map/pallas_call | solution.py:62
  2.0 3.0 %collective-permute-start.1 = (bf16[336,768]{1,0:T(8,128)(2,1)}, bf16[336,768]{1,0:T(8,128)(2,1)S(1)}, u32[]{:S(2)}, u32[]{:S(2)}) collective-permute-start(bf16[336,768]{1,0:T(8,128)(2,1)} %shard_map.37.refs_0_.refs_2_.refs_3_.refs_1_), channel_id=1, source_target_pairs={{0,8},{1,17},{2,10},{3,19},{4,12},{5,21},{6,14},{7,23},{8,0},{9,25... | collective-permute-start | bytes 1548296 | tf_op jit(solution)/shard_map/ppermute | solution.py:257
  5.0 4.5 %collective-permute-start.3 = (bf16[336,768]{1,0:T(8,128)(2,1)}, bf16[336,768]{1,0:T(8,128)(2,1)S(1)}, u32[]{:S(2)}, u32[]{:S(2)}) collective-permute-start(bf16[336,768]{1,0:T(8,128)(2,1)} %shard_map.37.refs_0_.refs_2_.refs_3_.refs_1_), channel_id=1, source_target_pairs={{0,4},{1,5},{6,2},{7,3},{2,0},{3,1},{8,12},{9,13},{14,10},{15,11},... | collective-permute-start | bytes 1548296 | tf_op jit(solution)/shard_map/ppermute | solution.py:256
  9.5 2.8 %collective-permute-done.1.refs_3_.refs_4_.refs_2_ = bf16[336,768]{1,0:T(8,128)(2,1)S(1)} collective-permute-done((bf16[336,768]{1,0:T(8,128)(2,1)}, bf16[336,768]{1,0:T(8,128)(2,1)S(1)}, u32[]{:S(2)}, u32[]{:S(2)}) %collective-permute-start.1) | collective-permute-done | bytes 516128 | tf_op jit(solution)/shard_map/ppermute | solution.py:257
  12.3 2.0 %collective-permute-start.6 = (bf16[336,768]{1,0:T(8,128)(2,1)}, bf16[336,768]{1,0:T(8,128)(2,1)S(1)}, u32[]{:S(2)}, u32[]{:S(2)}) collective-permute-start(bf16[336,768]{1,0:T(8,128)(2,1)} %shard_map.37.refs_0_.refs_2_.refs_3_.refs_1_), channel_id=1, source_target_pairs={{0,16},{1,9},{2,18},{3,11},{4,20},{5,13},{6,22},{7,15},{8,24},{9,1... | collective-permute-start | bytes 1548296 | tf_op jit(solution)/shard_map/ppermute | solution.py:260
  14.4 6.0 %collective-permute-start = (bf16[336,768]{1,0:T(8,128)(2,1)}, bf16[336,768]{1,0:T(8,128)(2,1)S(1)}, u32[]{:S(2)}, u32[]{:S(2)}) collective-permute-start(bf16[336,768]{1,0:T(8,128)(2,1)} %shard_map.37.refs_0_.refs_2_.refs_3_.refs_1_), channel_id=1, source_target_pairs={{0,6},{1,7},{6,4},{7,5},{4,2},{5,3},{8,14},{9,15},{14,12},{15,13},... | collective-permute-start | bytes 1548296 | tf_op jit(solution)/shard_map/ppermute | solution.py:256
  20.4 0.2 collective-permute-done.3.refs_1_
  20.6 1.0 %copy-done = bf16[336,768]{1,0:T(8,128)(2,1)S(1)} copy-done((bf16[336,768]{1,0:T(8,128)(2,1)S(1)}, bf16[336,768]{1,0:T(8,128)(2,1)}, u32[]{:S(2)}) %copy-start) | copy-done | bytes 516120
  21.6 1.2 %shard_map.38 = (f32[1,320]{1,0:T(1,128)S(1)}, f32[1,320]{1,0:T(1,128)S(1)}, f32[1,320]{1,0:T(1,128)S(1)}, f32[1,320]{1,0:T(1,128)S(1)}, bf16[160,768]{1,0:T(8,128)(2,1)S(1)}, /*index=5*/bf16[176,768]{1,0:T(8,128)(2,1)S(1)}) custom-call(bf16[336,768]{1,0:T(8,128)(2,1)S(1)} %copy-done, bf16[336,768]{1,0:T(8,128)(2,1)S(1)} %collective-permute-done.3.refs_1_, ...), custom_call_target="tpu_custom_call" | custom-call | flops 320 | bytes 320 | tf_op jit(solution)/shard_map/pallas_call | solution.py:190
  23.0 0.4 collective-permute-start.4
  23.4 3.8 %collective-permute-done.7.refs_3_.refs_6_.refs_4_ = bf16[336,768]{1,0:T(8,128)(2,1)S(1)} collective-permute-done((bf16[336,768]{1,0:T(8,128)(2,1)S(1)}, bf16[336,768]{1,0:T(8,128)(2,1)S(1)}, u32[]{:S(2)}, u32[]{:S(2)}) %collective-permute-start.7) | collective-permute-done | bytes 516128 | tf_op jit(solution)/shard_map/ppermute | solution.py:258
  27.2 1.2 %shard_map.39 = (f32[1,320]{1,0:T(1,128)S(1)}, f32[1,320]{1,0:T(1,128)S(1)}, f32[1,320]{1,0:T(1,128)S(1)}, f32[1,320]{1,0:T(1,128)S(1)}) custom-call(bf16[336,768]{1,0:T(8,128)(2,1)S(1)} %copy-done.1, bf16[336,768]{1,0:T(8,128)(2,1)S(1)} %collective-permute-done.3.refs_1_, bf16[336,768]{1,0:T(8,128)(2,1)S(1)} %collective-permute-done.6.refs_2_.refs_5_.refs_3_, ...), custom_call_target="tpu_custom_call" | custom-call | flops 320 | bytes 320 | tf_op jit(solution)/shard_map/pallas_call | solution.py:190
  28.4 1.8 %shard_map.40 = (f32[1,320]{1,0:T(1,128)S(1)}, f32[1,320]{1,0:T(1,128)S(1)}, f32[1,320]{1,0:T(1,128)S(1)}, f32[1,320]{1,0:T(1,128)S(1)}, f32[1,320]{1,0:T(1,128)S(1)}) custom-call(bf16[336,768]{1,0:T(8,128)(2,1)S(1)} %collective-permute-done.2.refs_0_, bf16[160,768]{1,0:T(8,128)(2,1)S(1)} %collective-permute-done.4.refs_1_, ...), custom_call_target="tpu_custom_call" | custom-call | flops 320 | bytes 320 | tf_op jit(solution)/shard_map/pallas_call | solution.py:190
  30.2 2.1 %collective-permute-done.refs_0_ = bf16[336,768]{1,0:T(8,128)(2,1)S(1)} collective-permute-done((bf16[336,768]{1,0:T(8,128)(2,1)}, bf16[336,768]{1,0:T(8,128)(2,1)S(1)}, u32[]{:S(2)}, u32[]{:S(2)}) %collective-permute-start) | collective-permute-done | bytes 516128 | tf_op jit(solution)/shard_map/ppermute | solution.py:256
  32.4 1.1 %shard_map.41 = (f32[1,320]{1,0:T(1,128)S(1)}, f32[1,320]{1,0:T(1,128)S(1)}, f32[1,320]{1,0:T(1,128)S(1)}, f32[1,320]{1,0:T(1,128)S(1)}, f32[1,320]{1,0:T(1,128)S(1)}) custom-call(bf16[336,768]{1,0:T(8,128)(2,1)S(1)} %collective-permute-done.refs_0_, bf16[336,768]{1,0:T(8,128)(2,1)S(1)} %copy-done.1, ...), custom_call_target="tpu_custom_call" | custom-call | flops 320 | bytes 320 | tf_op jit(solution)/shard_map/pallas_call | solution.py:190
  33.5 0.8 %collective-permute-done.8.refs_0_ = bf16[336,768]{1,0:T(8,128)(2,1)S(1)} collective-permute-done((bf16[336,768]{1,0:T(8,128)(2,1)S(1)}, bf16[336,768]{1,0:T(8,128)(2,1)S(1)}, u32[]{:S(2)}, u32[]{:S(2)}) %collective-permute-start.8) | collective-permute-done | bytes 516128 | tf_op jit(solution)/shard_map/ppermute | solution.py:282
  34.3 1.1 %shard_map.42 = (f32[1,320]{1,0:T(1,128)S(1)}, f32[1,640]{1,0:T(1,128)S(1)}, f32[1,320]{1,0:T(1,128)S(1)}, f32[1,320]{1,0:T(1,128)S(1)}) custom-call(bf16[336,768]{1,0:T(8,128)(2,1)S(1)} %collective-permute-done.8.refs_0_, bf16[336,768]{1,0:T(8,128)(2,1)S(1)} %copy-done.1, bf16[336,768]{1,0:T(8,128)(2,1)S(1)} %collective-permute-done.1.refs_3_.refs_4_.refs_2_, ...), custom_call_target="tpu_custom_call" | custom-call | flops 320 | bytes 320 | tf_op jit(solution)/shard_map/pallas_call | solution.py:190
  35.6 1.5 %collective-permute-start.12 = (f32[1,640]{1,0:T(1,128)S(1)}, f32[1,640]{1,0:T(1,128)S(1)}, u32[]{:S(2)}, u32[]{:S(2)}) collective-permute-start(f32[1,640]{1,0:T(1,128)S(1)} %get-tuple-element.63), channel_id=1, source_target_pairs={{0,8},{1,17},{2,10},{3,19},{4,12},{5,21},{6,14},{7,23},{8,0},{9,25... | collective-permute-start | bytes 7688 | tf_op jit(solution)/shard_map/ppermute | solution.py:302
  37.3 3.4 %collective-permute-start.10 = (f32[1,640]{1,0:T(1,128)S(1)}, f32[1,640]{1,0:T(1,128)S(1)}, u32[]{:S(2)}, u32[]{:S(2)}) collective-permute-start(f32[1,640]{1,0:T(1,128)S(1)} %fusion), channel_id=1, source_target_pairs={{4,0},{2,6},{0,2},{12,8},{10,14},{8,10},{20,16},{18,22},{16,18},{2... | collective-permute-start | bytes 7688 | tf_op jit(solution)/shard_map/ppermute | solution.py:295
  40.8 0.5 %collective-permute-start.13 = (f32[1,320]{1,0:T(1,128)S(1)}, f32[1,320]{1,0:T(1,128)S(1)}, u32[]{:S(2)}, u32[]{:S(2)}) collective-permute-start(f32[1,320]{1,0:T(1,128)S(1)} %slice_maximum_fusion), channel_id=1, source_target_pairs={{0,16},{1,9},{2,18},{3,11},{4,20},{5,13},{6,22},{7,15},{8,24},{9,1... | collective-permute-start | bytes 3848 | tf_op jit(solution)/shard_map/ppermute | solution.py:305
  41.3 2.3 %collective-permute-done.10 = f32[1,640]{1,0:T(1,128)S(1)} collective-permute-done((f32[1,640]{1,0:T(1,128)S(1)}, f32[1,640]{1,0:T(1,128)S(1)}, u32[]{:S(2)}, u32[]{:S(2)}) %collective-permute-start.10) | collective-permute-done | bytes 2592 | tf_op jit(solution)/shard_map/ppermute | solution.py:295
  43.7 0.5 %collective-permute-start.11 = (f32[1,320]{1,0:T(1,128)S(1)}, f32[1,320]{1,0:T(1,128)S(1)}, u32[]{:S(2)}, u32[]{:S(2)}) collective-permute-start(f32[1,320]{1,0:T(1,128)S(1)} %slice.27), channel_id=1, source_target_pairs={{0,1},{1,0},{2,3},{3,2},{4,5},{5,4},{6,7},{7,6},{8,9},{9,8},{10,11... | collective-permute-start | bytes 3848 | tf_op jit(solution)/shard_map/ppermute | solution.py:301
  44.4 0.7 %collective-permute-done.11 = f32[1,320]{1,0:T(1,128)S(1)} collective-permute-done((f32[1,320]{1,0:T(1,128)S(1)}, f32[1,320]{1,0:T(1,128)S(1)}, u32[]{:S(2)}, u32[]{:S(2)}) %collective-permute-start.11) | collective-permute-done | bytes 1312 | tf_op jit(solution)/shard_map/ppermute | solution.py:301
  45.1 0.6 %fusion.3 = f32[320]{0:T(512)} fusion(f32[1,320]{1,0:T(1,128)S(1)} %collective-permute-done.13, f32[1,640]{1,0:T(1,128)S(1)} %collective-permute-done.12, f32[1,320]{1,0:T(1,128)S(1)} %collective-permute-done.11, f32[1,640]{1,0:T(1,128)S(1)} %broadcast_select_fusion.2, f32[1,320]{1,0:T(1,128)S(1)} %get-tuple-element.57, f32[1,320]{1,0:T(1,128)S(1)} %get-tuple-element.55, ...), kind=kLoop, calls=%fused_computation.11 | loop fusion | flops 1920 | bytes 10240 | tf_op jit(solution)/shard_map/max | solution.py:306
  (22 shorter events, 0.9 us)
Async XLA Ops:
  2.0 10.3 %collective-permute-start.1 = (bf16[336,768]{1,0:T(8,128)(2,1)}, bf16[336,768]{1,0:T(8,128)(2,1)S(1)}, u32[]{:S(2)}, u32[]{:S(2)}) collective-permute-start(bf16[336,768]{1,0:T(8,128)(2,1)} %shard_map.37.refs_0_.refs_2_.refs_3_.refs_1_), channel_id=1, source_target_pairs={{0,8},{1,17},{2,10},{3,19},{4,12},{5,21},{6,14},{7,23},{8,0},{9,25... | collective-permute-start | bytes 1548296 | tf_op jit(solution)/shard_map/ppermute | solution.py:257
  5.0 15.5 %collective-permute-start.3 = (bf16[336,768]{1,0:T(8,128)(2,1)}, bf16[336,768]{1,0:T(8,128)(2,1)S(1)}, u32[]{:S(2)}, u32[]{:S(2)}) collective-permute-start(bf16[336,768]{1,0:T(8,128)(2,1)} %shard_map.37.refs_0_.refs_2_.refs_3_.refs_1_), channel_id=1, source_target_pairs={{0,4},{1,5},{6,2},{7,3},{2,0},{3,1},{8,12},{9,13},{14,10},{15,11},... | collective-permute-start | bytes 1548296 | tf_op jit(solution)/shard_map/ppermute | solution.py:256
  12.3 10.6 %collective-permute-start.6 = (bf16[336,768]{1,0:T(8,128)(2,1)}, bf16[336,768]{1,0:T(8,128)(2,1)S(1)}, u32[]{:S(2)}, u32[]{:S(2)}) collective-permute-start(bf16[336,768]{1,0:T(8,128)(2,1)} %shard_map.37.refs_0_.refs_2_.refs_3_.refs_1_), channel_id=1, source_target_pairs={{0,16},{1,9},{2,18},{3,11},{4,20},{5,13},{6,22},{7,15},{8,24},{9,1... | collective-permute-start | bytes 1548296 | tf_op jit(solution)/shard_map/ppermute | solution.py:260
  14.4 12.8 %collective-permute-start.7 = (bf16[336,768]{1,0:T(8,128)(2,1)S(1)}, bf16[336,768]{1,0:T(8,128)(2,1)S(1)}, u32[]{:S(2)}, u32[]{:S(2)}) collective-permute-start(bf16[336,768]{1,0:T(8,128)(2,1)S(1)} %collective-permute-done.1.refs_3_.refs_4_.refs_2_), channel_id=1, source_target_pairs={{0,16},{1,9},{2,18},{3,11},{4,20},{5,13},{6,22},{7,15},{8,24},{9,1... | collective-permute-start | bytes 1548296 | tf_op jit(solution)/shard_map/ppermute | solution.py:258
  14.4 14.0 %collective-permute-start.2 = (bf16[336,768]{1,0:T(8,128)(2,1)}, bf16[336,768]{1,0:T(8,128)(2,1)S(1)}, u32[]{:S(2)}, u32[]{:S(2)}) collective-permute-start(bf16[336,768]{1,0:T(8,128)(2,1)} %shard_map.37.refs_0_.refs_2_.refs_3_.refs_1_), channel_id=1, source_target_pairs={{0,1},{1,0},{2,3},{3,2},{4,5},{5,4},{6,7},{7,6},{8,9},{9,8},{10,11... | collective-permute-start | bytes 1548296 | tf_op jit(solution)/shard_map/ppermute | solution.py:261
  14.4 18.0 %collective-permute-start = (bf16[336,768]{1,0:T(8,128)(2,1)}, bf16[336,768]{1,0:T(8,128)(2,1)S(1)}, u32[]{:S(2)}, u32[]{:S(2)}) collective-permute-start(bf16[336,768]{1,0:T(8,128)(2,1)} %shard_map.37.refs_0_.refs_2_.refs_3_.refs_1_), channel_id=1, source_target_pairs={{0,6},{1,7},{6,4},{7,5},{4,2},{5,3},{8,14},{9,15},{14,12},{15,13},... | collective-permute-start | bytes 1548296 | tf_op jit(solution)/shard_map/ppermute | solution.py:256
  20.6 1.0 %copy-start = (bf16[336,768]{1,0:T(8,128)(2,1)S(1)}, bf16[336,768]{1,0:T(8,128)(2,1)}, u32[]{:S(2)}) copy-start(bf16[336,768]{1,0:T(8,128)(2,1)} %shard_map.37.refs_0_.refs_2_.refs_3_.refs_1_) | copy-start | bytes 1548292
  21.6 5.6 %copy-start.1 = (bf16[336,768]{1,0:T(8,128)(2,1)S(1)}, bf16[336,768]{1,0:T(8,128)(2,1)}, u32[]{:S(2)}) copy-start(bf16[336,768]{1,0:T(8,128)(2,1)} %shard_map.37.refs_0_.refs_2_.refs_3_.refs_1_) | copy-start | bytes 1548292
  22.8 5.6 %collective-permute-start.5 = (bf16[176,768]{1,0:T(8,128)(2,1)S(1)}, bf16[176,768]{1,0:T(8,128)(2,1)S(1)}, u32[]{:S(2)}, u32[]{:S(2)}) collective-permute-start(bf16[176,768]{1,0:T(8,128)(2,1)S(1)} %get-tuple-element.37), channel_id=1, source_target_pairs={{0,1},{1,0},{2,3},{3,2},{4,5},{5,4},{6,7},{7,6},{8,9},{9,8},{10,11... | collective-permute-start | bytes 811016 | tf_op jit(solution)/shard_map/ppermute | solution.py:270
  23.0 5.4 %collective-permute-start.4 = (bf16[160,768]{1,0:T(8,128)(2,1)S(1)}, bf16[160,768]{1,0:T(8,128)(2,1)S(1)}, u32[]{:S(2)}, u32[]{:S(2)}) collective-permute-start(bf16[160,768]{1,0:T(8,128)(2,1)S(1)} %get-tuple-element.36), channel_id=1, source_target_pairs={{0,1},{1,0},{2,3},{3,2},{4,5},{5,4},{6,7},{7,6},{8,9},{9,8},{10,11... | collective-permute-start | bytes 737288 | tf_op jit(solution)/shard_map/ppermute | solution.py:270
  32.4 1.9 %collective-permute-start.8 = (bf16[336,768]{1,0:T(8,128)(2,1)S(1)}, bf16[336,768]{1,0:T(8,128)(2,1)S(1)}, u32[]{:S(2)}, u32[]{:S(2)}) collective-permute-start(bf16[336,768]{1,0:T(8,128)(2,1)S(1)} %collective-permute-done.refs_0_), channel_id=1, source_target_pairs={{0,1},{1,0},{2,3},{3,2},{4,5},{5,4},{6,7},{7,6},{8,9},{9,8},{10,11... | collective-permute-start | bytes 1548296 | tf_op jit(solution)/shard_map/ppermute | solution.py:282
  35.5 1.6 %collective-permute-start.9 = (f32[1,640]{1,0:T(1,128)S(1)}, f32[1,640]{1,0:T(1,128)S(1)}, u32[]{:S(2)}, u32[]{:S(2)}) collective-permute-start(f32[1,640]{1,0:T(1,128)S(1)} %broadcast_select_fusion), channel_id=1, source_target_pairs={{0,1},{1,0},{2,3},{3,2},{4,5},{5,4},{6,7},{7,6},{8,9},{9,8},{10,11... | collective-permute-start | bytes 7688 | tf_op jit(solution)/shard_map/ppermute | solution.py:291
  35.6 5.1 %collective-permute-start.12 = (f32[1,640]{1,0:T(1,128)S(1)}, f32[1,640]{1,0:T(1,128)S(1)}, u32[]{:S(2)}, u32[]{:S(2)}) collective-permute-start(f32[1,640]{1,0:T(1,128)S(1)} %get-tuple-element.63), channel_id=1, source_target_pairs={{0,8},{1,17},{2,10},{3,19},{4,12},{5,21},{6,14},{7,23},{8,0},{9,25... | collective-permute-start | bytes 7688 | tf_op jit(solution)/shard_map/ppermute | solution.py:302
  37.3 6.4 %collective-permute-start.10 = (f32[1,640]{1,0:T(1,128)S(1)}, f32[1,640]{1,0:T(1,128)S(1)}, u32[]{:S(2)}, u32[]{:S(2)}) collective-permute-start(f32[1,640]{1,0:T(1,128)S(1)} %fusion), channel_id=1, source_target_pairs={{4,0},{2,6},{0,2},{12,8},{10,14},{8,10},{20,16},{18,22},{16,18},{2... | collective-permute-start | bytes 7688 | tf_op jit(solution)/shard_map/ppermute | solution.py:295
  40.8 3.6 %collective-permute-start.13 = (f32[1,320]{1,0:T(1,128)S(1)}, f32[1,320]{1,0:T(1,128)S(1)}, u32[]{:S(2)}, u32[]{:S(2)}) collective-permute-start(f32[1,320]{1,0:T(1,128)S(1)} %slice_maximum_fusion), channel_id=1, source_target_pairs={{0,16},{1,9},{2,18},{3,11},{4,20},{5,13},{6,22},{7,15},{8,24},{9,1... | collective-permute-start | bytes 3848 | tf_op jit(solution)/shard_map/ppermute | solution.py:305
  43.7 1.3 %collective-permute-start.11 = (f32[1,320]{1,0:T(1,128)S(1)}, f32[1,320]{1,0:T(1,128)S(1)}, u32[]{:S(2)}, u32[]{:S(2)}) collective-permute-start(f32[1,320]{1,0:T(1,128)S(1)} %slice.27), channel_id=1, source_target_pairs={{0,1},{1,0},{2,3},{3,2},{4,5},{5,4},{6,7},{7,6},{8,9},{9,8},{10,11... | collective-permute-start | bytes 3848 | tf_op jit(solution)/shard_map/ppermute | solution.py:301

commit v5 on v3

--- a/solution.py
+++ b/solution.py
@@ -23,7 +23,7 @@
 
 
 def codes(block, rows, span):
-    parts = block[rows : rows + EXTRA, : up(rows, LANES)].astype(jnp.float32)
+    parts = block[block.shape[0] - EXTRA :, : up(rows, LANES)].astype(jnp.float32)
     return parts[2:3] * (4.0 * span) + parts[0:1] * 256.0 + parts[1:2]
 
 
@@ -113,11 +113,11 @@
     )
 
 
-def assemble(whole, pieces):
-    top = 0
+def assemble(whole, top, end, pieces):
     for piece in pieces:
-        whole[top : top + piece.shape[0], :] = piece[...]
-        top += piece.shape[0]
+        height = min(piece.shape[0], end - top)
+        whole[top : top + height, :] = piece[0:height, :]
+        top += height
 
 
 def meet_kernel(rows, span, sizes, modes, groups, *refs):
@@ -132,16 +132,16 @@
         if len(block) == 1:
             return block[0]
         joined = next(scratch)
-        assemble(joined, block)
+        assemble(joined, 0, joined.shape[0], block)
         return joined
 
     blocks = [whole(block) for block in regrouped(blocks, groups[0])]
-    holds = [whole(block) for block in regrouped(holds, groups[1])]
+    holds = regrouped(holds, groups[1])
     total = held.shape[0]
     row = []
     for at, block in enumerate(holds):
-        held[at * rows : (at + 1) * rows, :] = block[0:rows, :]
-        row.append(codes(block, rows, span)[:, :rows])
+        assemble(held, at * rows, (at + 1) * rows, block)
+        row.append(codes(block[-1], rows, span)[:, :rows])
     rest = total - len(holds) * rows
     if rest:
         held[total - rest :, :] = jnp.zeros((rest, held.shape[1]), held.dtype)
@@ -183,7 +183,7 @@
     outs = [jax.ShapeDtypeStruct((1, rows * len(some)), jnp.float32) for some in together]
     found = [jax.ShapeDtypeStruct((1, rows), jnp.float32)] * sum(mode[0] for mode in modes)
     kept = [jax.ShapeDtypeStruct((height, width), jnp.bfloat16) for height in keep]
-    split = sum(length > 1 for some in lengths for length in some)
+    split = sum(length > 1 for length in lengths[0])
     scratch = [pltpu.VMEM((up(len(holds) * rows, LANES), width), jnp.bfloat16)]
     scratch += [pltpu.VMEM((rows + EXTRA, width), jnp.bfloat16)] * split
     kinds = flat + [bests, outs, found, kept, scratch]
@@ -218,7 +218,6 @@
     groups, members = mesh.shape["dp"], mesh.shape["grid"]
     assert groups == 4 and members % 2 == 0
     chips = members // 2
-    rounds = line_rounds(chips)
 
     def everywhere(target):
         return [
@@ -232,13 +231,17 @@
     first = everywhere(lambda p, g: (p ^ (1 + g % 2), g))
     second = everywhere(lambda p, g: (p ^ (2 - g % 2), g))
 
-    def along(pairs):
-        return [
+    rounds = line_rounds(chips)
+    rounds += [[]] * (len(rounds) % 2)
+    rounds = [
+        [
             (p * members + 2 * s + c, p * members + 2 * t + c)
             for p in range(groups)
-            for s, t in pairs
             for c in range(2)
+            for s, t in rounds[at + c]
         ]
+        for at in range(0, len(rounds), 2)
+    ]
 
     def back(pairs):
         return [(target, source) for source, target in pairs]
@@ -248,51 +251,53 @@
         span = 256
         while span < rows * groups * members:
             span *= 2
-        chip = lax.axis_index("grid") // 2
         block = prepare(embeddings, cluster, order_key)
         halves = (rows // 2, rows // 2 + EXTRA)
         own = [block]
-        near = [[lax.ppermute(block, BOTH, along(pairs))] for pairs in rounds]
-        from_first = [lax.ppermute(block, BOTH, first)]
-        from_second = [lax.ppermute(block, BOTH, second)]
-        from_corner = [
-            lax.ppermute(piece, BOTH, second)
-            for piece in (from_first[0][: halves[0]], from_first[0][halves[0] :])
-        ]
-        partner = lax.optimization_barrier((block, from_first[0]))[0]
-        partner = [lax.ppermute(partner, BOTH, other_core)]
-
-        results = []
-
-        def give_back(mine, theirs, pairs):
-            mine = jnp.maximum(mine, lax.ppermute(theirs, BOTH, other_core))
-            mine = lax.ppermute(mine, BOTH, back(along(pairs)))
-            senders = functools.reduce(jnp.logical_or, [chip == s for s, _ in pairs])
-            results.append(jnp.where(senders, mine, -1.0))
-
+        parts = (block[: halves[0]], block[halves[0] :])
+        partner = lax.ppermute(block, BOTH, other_core)
+        near = [[lax.ppermute(block, BOTH, pairs)] for pairs in rounds]
+        from_first = [lax.ppermute(part, BOTH, first) for part in parts]
+        near_other = [[lax.ppermute(partner, BOTH, pairs)] for pairs in rounds]
+        from_corner = [lax.ppermute(part, BOTH, second) for part in from_first]
+        later = lax.optimization_barrier((block, *from_first))[0]
+        from_second = [lax.ppermute(later, BOTH, second)]
+        held = [own, from_first, from_second, from_corner]
+
+        results, kept, sent = [], [], []
         bests, (mine, one), pieces = meeting(
-            [own, near[0]], [OWN, TWO], [own, from_first], [], rows, span, keep=halves
+            [own, near[0]], [OWN, TWO], held[:2], [], rows, span, keep=halves
         )
         results.append(mine)
         pieces = [lax.ppermute(piece, BOTH, other_core) for piece in pieces]
         more_bests, (mine, one_more), _ = meeting(
-            [own, near[0]], [OWN, TWO], [from_second, from_corner], [], rows, span
+            [own, near[0]], [OWN, TWO], held[2:], [], rows, span
         )
         results.append(mine)
-        held = [own, from_first, from_second, from_corner]
-        bests, (other,), _ = meeting(
-            [partner, pieces], [HELD, TWO], held, bests + more_bests, rows, span
-        )
-        give_back(jnp.maximum(one, one_more), other, rounds[0])
-        for at, (pairs, one) in enumerate(zip(rounds[1:], near[1:])):
-            one, bests = lax.optimization_barrier((one, bests))
-            far = [lax.ppermute(piece, BOTH, other_core) for piece in one]
-            bests, (mine,), _ = meeting([one], [TWO], held, bests, rows, span)
-            last = at == len(rounds) - 2
-            bests, (theirs,), _ = meeting(
+        kept.append(jnp.maximum(one, one_more))
+        bests, found, _ = meeting(
+            [[partner], pieces], [HELD, TWO], held, bests + more_bests, rows, span
+        )
+        sent += found
+        rest = [blocks for both in zip(near, near_other) for blocks in both][1:]
+        for at, one in enumerate(rest):
+            (one,), bests = lax.optimization_barrier((one, bests))
+            far = [lax.ppermute(one, BOTH, other_core)]
+            bests, found, _ = meeting([[one]], [TWO], held, bests, rows, span)
+            kept += found
+            last = at == len(rest) - 1
+            bests, found, _ = meeting(
                 [far], [TWO], held, bests, rows, span, together=[(0,), (1, 3), (2,)] if last else None
             )
-            give_back(mine, theirs, pairs)
+            sent += found
+        sent = lax.ppermute(jnp.concatenate(sent, axis=1), BOTH, other_core)
+        kept = jnp.maximum(jnp.concatenate(kept, axis=1), sent)
+        for at, pairs in enumerate(rounds):
+            found = lax.ppermute(kept[:, 2 * at * rows : 2 * (at + 1) * rows], BOTH, back(pairs))
+            me = lax.axis_index(BOTH)
+            sender = functools.reduce(jnp.logical_or, [me == source for source, _ in pairs])
+            found = jnp.where(sender, found, -1.0)
+            results += [found[:, :rows], lax.ppermute(found[:, rows:], BOTH, other_core)]
         from_x = lax.ppermute(bests[1], BOTH, first)
         results.append(from_x[:, :rows])
         onward = jnp.maximum(bests[2], from_x[:, rows:])

time: 49.4 us -> 47.5 us (0.962)
  starting transfers between devices: 28.6 us -> 19.6 us
  waiting for transfers between devices: 11.2 us -> 17.2 us
  local copies, waits for them, and re-layouts: 0.04 us -> 1.07 us
    ppermute x12, starting transfers between devices: 24.4 us -> 17.1 us  [the longest x1 4.49 us: shards(): near = [[lax.ppermute(block, BOTH, pairs)] for pairs in rounds]]
    ppermute x12, waiting for transfers between devices: 11.2 us -> 17.1 us  [the longest x2 7.19 us: shards(): from_corner = [lax.ppermute(part, BOTH, second) for part in from_first]]
    ppermute x1, starting transfers between devices: 2.62 us -> 1.27 us  [shards(): results.append(lax.ppermute(onward, BOTH, second))]
    slice x2 -> x3, local copies, waits for them, and re-layouts: 0.04 us -> 1.06 us  [the longest x2 0.99 us: shards(): parts = (block[:halves[0]], block[halves[0]:])]
    ppermute x1, starting transfers between devices: 1.49 us -> 0.58 us  [shards(): from_x = lax.ppermute(bests[1], BOTH, first)]
    ppermute x2, starting transfers between devices: 0.07 us -> 0.67 us  [shards(): pieces = [lax.ppermute(piece, BOTH, other_core) for piece in pieces]]
  transfers between devices with their start and end apart: 16 -> 16, of which waited for: 6 -> 7; matrix products, arithmetic and copies ran while one was open for 0% -> 3% of each run, Pallas kernels for 13% -> 11%
where the time goes in v5:
time: 47.5 us; the launch traced here: 47.2 us
  starting transfers between devices  19.6 us (41%)
  waiting for transfers between devices  17.2 us (36%)
  Pallas kernels  8.42 us (18%)
  local copies, waits for them, and re-layouts  1.07 us (2%)
  other arithmetic  0.83 us (2%)
    ppermute x2, waiting for transfers between devices, shards(): from_corner = [lax.ppermute(part, BOTH, second) for part in from_first]  7.19 us
    pallas_call x5, Pallas kernels, meeting(): pl.pallas_call(functools.partial(meet_kernel, rows, span, [len(kind) for...  6.39 us
    ppermute x2, waiting for transfers between devices, shards(): from_first = [lax.ppermute(part, BOTH, first) for part in parts]  5.66 us
    ppermute x1, starting transfers between devices, shards(): near = [[lax.ppermute(block, BOTH, pairs)] for pairs in rounds]  4.49 us
    ppermute x2, starting transfers between devices, shards(): from_first = [lax.ppermute(part, BOTH, first) for part in parts]  3.21 us
    ppermute x1, starting transfers between devices, shards(): lax.ppermute(kept[:, 2 * at * rows:2 * (at + 1) * rows], BOTH, back(pairs))  2.77 us
    ppermute x1, waiting for transfers between devices, shards(): lax.ppermute(kept[:, 2 * at * rows:2 * (at + 1) * rows], BOTH, back(pairs))  2.23 us
    ppermute x2, starting transfers between devices, shards(): from_corner = [lax.ppermute(part, BOTH, second) for part in from_first]  2.09 us
  transfers between devices with their start and end apart: 16, of which 7 were waited for; matrix products, arithmetic and copies ran while one was open for 3% of the time, Pallas kernels for 11%

profile of v5, /device:TPU:0, one launch (start us, length us, event | category | flops | bytes accessed | tf_op | source)
XLA Modules:
  0.0 47.2 jit_solution(608795496087270275)
XLA Ops:
  0.0 2.0 %shard_map.37.refs_0_.refs_2_.refs_3_.refs_1_ = bf16[336,768]{1,0:T(8,128)(2,1)} custom-call(bf16[320,768]{1,0:T(8,128)(2,1)} %embeddings_hbm.1, s32[1,320]{1,0:T(1,128)} %bitcast.1, s32[320]{0:T(512)} %order_key_hbm.1), custom_call_target="tpu_custom_call" | custom-call | flops 320 | bytes 320 | tf_op jit(solution)/shard_map/pallas_call | solution.py:62
  2.6 1.0 %slice.25 = bf16[176,768]{1,0:T(8,128)(2,1)S(1)} slice(bf16[336,768]{1,0:T(8,128)(2,1)} %shard_map.37.refs_0_.refs_2_.refs_3_.refs_1_), slice={[160:336], [0:768]} | slice | bytes 540672 | tf_op jit(solution)/shard_map/slice | solution.py:257
  3.5 2.6 %collective-permute-start.4 = (bf16[176,768]{1,0:T(8,128)(2,1)S(1)}, bf16[176,768]{1,0:T(8,128)(2,1)S(1)}, u32[]{:S(2)}, u32[]{:S(2)}) collective-permute-start(bf16[176,768]{1,0:T(8,128)(2,1)S(1)} %slice.25), channel_id=1, source_target_pairs={{0,8},{1,17},{2,10},{3,19},{4,12},{5,21},{6,14},{7,23},{8,0},{9,25... | collective-permute-start | bytes 811016 | tf_op jit(solution)/shard_map/ppermute | solution.py:260
  6.2 4.5 %collective-permute-start.2 = (bf16[336,768]{1,0:T(8,128)(2,1)S(1)}, bf16[336,768]{1,0:T(8,128)(2,1)S(1)}, u32[]{:S(2)}, u32[]{:S(2)}) collective-permute-start(bf16[336,768]{1,0:T(8,128)(2,1)S(1)} %copy-done), channel_id=1, source_target_pairs={{0,4},{6,2},{2,0},{1,7},{7,5},{5,3},{8,12},{14,10},{10,8},{9,15},{... | collective-permute-start | bytes 1548296 | tf_op jit(solution)/shard_map/ppermute | solution.py:259
  10.7 0.6 %collective-permute-start.3 = (bf16[160,768]{1,0:T(8,128)(2,1)S(1)}, bf16[160,768]{1,0:T(8,128)(2,1)S(1)}, u32[]{:S(2)}, u32[]{:S(2)}) collective-permute-start(bf16[160,768]{1,0:T(8,128)(2,1)S(1)} %slice.24), channel_id=1, source_target_pairs={{0,8},{1,17},{2,10},{3,19},{4,12},{5,21},{6,14},{7,23},{8,0},{9,25... | collective-permute-start | bytes 737288 | tf_op jit(solution)/shard_map/ppermute | solution.py:260
  11.3 5.7 %collective-permute-done.3.refs_3_.refs_4_.refs_2_ = bf16[160,768]{1,0:T(8,128)(2,1)S(1)} collective-permute-done((bf16[160,768]{1,0:T(8,128)(2,1)S(1)}, bf16[160,768]{1,0:T(8,128)(2,1)S(1)}, u32[]{:S(2)}, u32[]{:S(2)}) %collective-permute-start.3) | collective-permute-done | bytes 245792 | tf_op jit(solution)/shard_map/ppermute | solution.py:260
  16.9 1.5 %collective-permute-start.7 = (bf16[336,768]{1,0:T(8,128)(2,1)S(1)}, bf16[336,768]{1,0:T(8,128)(2,1)S(1)}, u32[]{:S(2)}, u32[]{:S(2)}) collective-permute-start(bf16[336,768]{1,0:T(8,128)(2,1)S(1)} %copy-done), channel_id=1, source_target_pairs={{0,16},{1,9},{2,18},{3,11},{4,20},{5,13},{6,22},{7,15},{8,24},{9,1... | collective-permute-start | bytes 1548296 | tf_op jit(solution)/shard_map/ppermute | solution.py:264
  18.5 1.9 %collective-permute-start.1 = (bf16[336,768]{1,0:T(8,128)(2,1)S(1)}, bf16[336,768]{1,0:T(8,128)(2,1)S(1)}, u32[]{:S(2)}, u32[]{:S(2)}) collective-permute-start(bf16[336,768]{1,0:T(8,128)(2,1)S(1)} %collective-permute-done.refs_0_), channel_id=1, source_target_pairs={{0,4},{6,2},{2,0},{1,7},{7,5},{5,3},{8,12},{14,10},{10,8},{9,15},{... | collective-permute-start | bytes 1548296 | tf_op jit(solution)/shard_map/ppermute | solution.py:261
  21.0 1.5 %collective-permute-start.9 = (bf16[176,768]{1,0:T(8,128)(2,1)S(1)}, bf16[176,768]{1,0:T(8,128)(2,1)S(1)}, u32[]{:S(2)}, u32[]{:S(2)}) collective-permute-start(bf16[176,768]{1,0:T(8,128)(2,1)S(1)} %collective-permute-done.4.refs_4_.refs_5_.refs_3_), channel_id=1, source_target_pairs={{0,16},{1,9},{2,18},{3,11},{4,20},{5,13},{6,22},{7,15},{8,24},{9,1... | collective-permute-start | bytes 811016 | tf_op jit(solution)/shard_map/ppermute | solution.py:262
  22.5 1.2 %shard_map.38 = (f32[1,320]{1,0:T(1,128)S(1)}, f32[1,320]{1,0:T(1,128)S(1)}, f32[1,320]{1,0:T(1,128)S(1)}, f32[1,320]{1,0:T(1,128)S(1)}, bf16[160,768]{1,0:T(8,128)(2,1)S(1)}, /*index=5*/bf16[176,768]{1,0:T(8,128)(2,1)S(1)}) custom-call(bf16[336,768]{1,0:T(8,128)(2,1)S(1)} %copy-done, bf16[336,768]{1,0:T(8,128)(2,1)S(1)} %collective-permute-done.2.refs_1_, ...), custom_call_target="tpu_custom_call" | custom-call | flops 320 | bytes 320 | tf_op jit(solution)/shard_map/pallas_call | solution.py:190
  23.7 0.7 %collective-permute-start.6 = (bf16[176,768]{1,0:T(8,128)(2,1)S(1)}, bf16[176,768]{1,0:T(8,128)(2,1)S(1)}, u32[]{:S(2)}, u32[]{:S(2)}) collective-permute-start(bf16[176,768]{1,0:T(8,128)(2,1)S(1)} %get-tuple-element.36), channel_id=1, source_target_pairs={{0,1},{1,0},{2,3},{3,2},{4,5},{5,4},{6,7},{7,6},{8,9},{9,8},{10,11... | collective-permute-start | bytes 811016 | tf_op jit(solution)/shard_map/ppermute | solution.py:272
  24.4 4.3 %collective-permute-done.8.refs_3_.refs_7_.refs_5_ = bf16[160,768]{1,0:T(8,128)(2,1)S(1)} collective-permute-done((bf16[160,768]{1,0:T(8,128)(2,1)S(1)}, bf16[160,768]{1,0:T(8,128)(2,1)S(1)}, u32[]{:S(2)}, u32[]{:S(2)}) %collective-permute-start.8) | collective-permute-done | bytes 245792 | tf_op jit(solution)/shard_map/ppermute | solution.py:262
  28.7 2.9 %collective-permute-done.9.refs_4_.refs_8_.refs_6_ = bf16[176,768]{1,0:T(8,128)(2,1)S(1)} collective-permute-done((bf16[176,768]{1,0:T(8,128)(2,1)S(1)}, bf16[176,768]{1,0:T(8,128)(2,1)S(1)}, u32[]{:S(2)}, u32[]{:S(2)}) %collective-permute-start.9) | collective-permute-done | bytes 270368 | tf_op jit(solution)/shard_map/ppermute | solution.py:262
  31.6 1.2 %shard_map.39 = (f32[1,320]{1,0:T(1,128)S(1)}, f32[1,320]{1,0:T(1,128)S(1)}, f32[1,320]{1,0:T(1,128)S(1)}, f32[1,320]{1,0:T(1,128)S(1)}) custom-call(bf16[336,768]{1,0:T(8,128)(2,1)S(1)} %copy-done, bf16[336,768]{1,0:T(8,128)(2,1)S(1)} %collective-permute-done.2.refs_1_, bf16[336,768]{1,0:T(8,128)(2,1)S(1)} %collective-permute-done.7.refs_2_.refs_6_.refs_4_, ...), custom_call_target="tpu_custom_call" | custom-call | flops 320 | bytes 320 | tf_op jit(solution)/shard_map/pallas_call | solution.py:190
  32.8 1.8 %shard_map.40 = (f32[1,320]{1,0:T(1,128)S(1)}, f32[1,320]{1,0:T(1,128)S(1)}, f32[1,320]{1,0:T(1,128)S(1)}, f32[1,320]{1,0:T(1,128)S(1)}, f32[1,320]{1,0:T(1,128)S(1)}) custom-call(bf16[336,768]{1,0:T(8,128)(2,1)S(1)} %collective-permute-done.refs_0_, bf16[160,768]{1,0:T(8,128)(2,1)S(1)} %collective-permute-done.5.refs_1_, ...), custom_call_target="tpu_custom_call" | custom-call | flops 320 | bytes 320 | tf_op jit(solution)/shard_map/pallas_call | solution.py:190
  34.7 1.1 %shard_map.41 = (f32[1,320]{1,0:T(1,128)S(1)}, f32[1,320]{1,0:T(1,128)S(1)}, f32[1,320]{1,0:T(1,128)S(1)}, f32[1,320]{1,0:T(1,128)S(1)}, f32[1,320]{1,0:T(1,128)S(1)}) custom-call(bf16[336,768]{1,0:T(8,128)(2,1)S(1)} %collective-permute-done.1.refs_0_, bf16[336,768]{1,0:T(8,128)(2,1)S(1)} %copy-done, ...), custom_call_target="tpu_custom_call" | custom-call | flops 320 | bytes 320 | tf_op jit(solution)/shard_map/pallas_call | solution.py:190
  35.8 0.7 %collective-permute-done.10.refs_0_ = bf16[336,768]{1,0:T(8,128)(2,1)S(1)} collective-permute-done((bf16[336,768]{1,0:T(8,128)(2,1)S(1)}, bf16[336,768]{1,0:T(8,128)(2,1)S(1)}, u32[]{:S(2)}, u32[]{:S(2)}) %collective-permute-start.10) | collective-permute-done | bytes 516128 | tf_op jit(solution)/shard_map/ppermute | solution.py:285
  36.6 1.1 %shard_map.42 = (f32[1,320]{1,0:T(1,128)S(1)}, f32[1,640]{1,0:T(1,128)S(1)}, f32[1,320]{1,0:T(1,128)S(1)}, f32[1,320]{1,0:T(1,128)S(1)}) custom-call(bf16[336,768]{1,0:T(8,128)(2,1)S(1)} %collective-permute-done.10.refs_0_, bf16[336,768]{1,0:T(8,128)(2,1)S(1)} %copy-done, bf16[160,768]{1,0:T(8,128)(2,1)S(1)} %collective-permute-done.3.refs_3_.refs_4_.refs_2_, ...), custom_call_target="tpu_custom_call" | custom-call | flops 320 | bytes 320 | tf_op jit(solution)/shard_map/pallas_call | solution.py:190
  37.9 0.6 %collective-permute-start.14 = (f32[1,640]{1,0:T(1,128)S(1)}, f32[1,640]{1,0:T(1,128)S(1)}, u32[]{:S(2)}, u32[]{:S(2)}) collective-permute-start(f32[1,640]{1,0:T(1,128)S(1)} %get-tuple-element.63), channel_id=1, source_target_pairs={{0,8},{1,17},{2,10},{3,19},{4,12},{5,21},{6,14},{7,23},{8,0},{9,25... | collective-permute-start | bytes 7688 | tf_op jit(solution)/shard_map/ppermute | solution.py:301
  39.0 2.8 %collective-permute-start.12 = (f32[1,640]{1,0:T(1,128)S(1)}, f32[1,640]{1,0:T(1,128)S(1)}, u32[]{:S(2)}, u32[]{:S(2)}) collective-permute-start(f32[1,640]{1,0:T(1,128)S(1)} %maximum_maximum_fusion), channel_id=1, source_target_pairs={{4,0},{2,6},{0,2},{7,1},{5,7},{3,5},{12,8},{10,14},{8,10},{15,9},{... | collective-permute-start | bytes 7688 | tf_op jit(solution)/shard_map/ppermute | solution.py:296
  41.9 1.3 %collective-permute-start.15 = (f32[1,320]{1,0:T(1,128)S(1)}, f32[1,320]{1,0:T(1,128)S(1)}, u32[]{:S(2)}, u32[]{:S(2)}) collective-permute-start(f32[1,320]{1,0:T(1,128)S(1)} %slice_maximum_fusion), channel_id=1, source_target_pairs={{0,16},{1,9},{2,18},{3,11},{4,20},{5,13},{6,22},{7,15},{8,24},{9,1... | collective-permute-start | bytes 3848 | tf_op jit(solution)/shard_map/ppermute | solution.py:304
  43.1 2.2 %collective-permute-done.12 = f32[1,640]{1,0:T(1,128)S(1)} collective-permute-done((f32[1,640]{1,0:T(1,128)S(1)}, f32[1,640]{1,0:T(1,128)S(1)}, u32[]{:S(2)}, u32[]{:S(2)}) %collective-permute-start.12) | collective-permute-done | bytes 2592 | tf_op jit(solution)/shard_map/ppermute | solution.py:296
  45.8 0.8 %collective-permute-done.13 = f32[1,320]{1,0:T(1,128)S(1)} collective-permute-done((f32[1,320]{1,0:T(1,128)S(1)}, f32[1,320]{1,0:T(1,128)S(1)}, u32[]{:S(2)}, u32[]{:S(2)}) %collective-permute-start.13) | collective-permute-done | bytes 1312 | tf_op jit(solution)/shard_map/ppermute | solution.py:300
  46.6 0.6 %fusion.2 = f32[320]{0:T(512)} fusion(f32[1,320]{1,0:T(1,128)S(1)} %collective-permute-done.15, f32[1,640]{1,0:T(1,128)S(1)} %collective-permute-done.14, f32[1,320]{1,0:T(1,128)S(1)} %collective-permute-done.13, f32[1,640]{1,0:T(1,128)S(1)} %broadcast_select_fusion, f32[1,320]{1,0:T(1,128)S(1)} %get-tuple-element.57, f32[1,320]{1,0:T(1,128)S(1)} %get-tuple-element.55, ...), kind=kLoop, calls=%fused_computation.8 | loop fusion | flops 1920 | bytes 10240 | tf_op jit(solution)/shard_map/max | solution.py:305
  (25 shorter events, 2.5 us)
Async XLA Ops:
  2.0 4.1 %copy-start = (bf16[336,768]{1,0:T(8,128)(2,1)S(1)}, bf16[336,768]{1,0:T(8,128)(2,1)}, u32[]{:S(2)}) copy-start(bf16[336,768]{1,0:T(8,128)(2,1)} %shard_map.37.refs_0_.refs_2_.refs_3_.refs_1_) | copy-start | bytes 1548292
  2.1 16.4 %collective-permute-start = (bf16[336,768]{1,0:T(8,128)(2,1)}, bf16[336,768]{1,0:T(8,128)(2,1)S(1)}, u32[]{:S(2)}, u32[]{:S(2)}) collective-permute-start(bf16[336,768]{1,0:T(8,128)(2,1)} %shard_map.37.refs_0_.refs_2_.refs_3_.refs_1_), channel_id=1, source_target_pairs={{0,1},{1,0},{2,3},{3,2},{4,5},{5,4},{6,7},{7,6},{8,9},{9,8},{10,11... | collective-permute-start | bytes 1548296 | tf_op jit(solution)/shard_map/ppermute | solution.py:258
  3.5 13.4 %collective-permute-start.4 = (bf16[176,768]{1,0:T(8,128)(2,1)S(1)}, bf16[176,768]{1,0:T(8,128)(2,1)S(1)}, u32[]{:S(2)}, u32[]{:S(2)}) collective-permute-start(bf16[176,768]{1,0:T(8,128)(2,1)S(1)} %slice.25), channel_id=1, source_target_pairs={{0,8},{1,17},{2,10},{3,19},{4,12},{5,21},{6,14},{7,23},{8,0},{9,25... | collective-permute-start | bytes 811016 | tf_op jit(solution)/shard_map/ppermute | solution.py:260
  6.2 16.4 %collective-permute-start.2 = (bf16[336,768]{1,0:T(8,128)(2,1)S(1)}, bf16[336,768]{1,0:T(8,128)(2,1)S(1)}, u32[]{:S(2)}, u32[]{:S(2)}) collective-permute-start(bf16[336,768]{1,0:T(8,128)(2,1)S(1)} %copy-done), channel_id=1, source_target_pairs={{0,4},{6,2},{2,0},{1,7},{7,5},{5,3},{8,12},{14,10},{10,8},{9,15},{... | collective-permute-start | bytes 1548296 | tf_op jit(solution)/shard_map/ppermute | solution.py:259
  10.7 6.3 %collective-permute-start.3 = (bf16[160,768]{1,0:T(8,128)(2,1)S(1)}, bf16[160,768]{1,0:T(8,128)(2,1)S(1)}, u32[]{:S(2)}, u32[]{:S(2)}) collective-permute-start(bf16[160,768]{1,0:T(8,128)(2,1)S(1)} %slice.24), channel_id=1, source_target_pairs={{0,8},{1,17},{2,10},{3,19},{4,12},{5,21},{6,14},{7,23},{8,0},{9,25... | collective-permute-start | bytes 737288 | tf_op jit(solution)/shard_map/ppermute | solution.py:260
  16.9 14.6 %collective-permute-start.7 = (bf16[336,768]{1,0:T(8,128)(2,1)S(1)}, bf16[336,768]{1,0:T(8,128)(2,1)S(1)}, u32[]{:S(2)}, u32[]{:S(2)}) collective-permute-start(bf16[336,768]{1,0:T(8,128)(2,1)S(1)} %copy-done), channel_id=1, source_target_pairs={{0,16},{1,9},{2,18},{3,11},{4,20},{5,13},{6,22},{7,15},{8,24},{9,1... | collective-permute-start | bytes 1548296 | tf_op jit(solution)/shard_map/ppermute | solution.py:264
  18.5 16.1 %collective-permute-start.1 = (bf16[336,768]{1,0:T(8,128)(2,1)S(1)}, bf16[336,768]{1,0:T(8,128)(2,1)S(1)}, u32[]{:S(2)}, u32[]{:S(2)}) collective-permute-start(bf16[336,768]{1,0:T(8,128)(2,1)S(1)} %collective-permute-done.refs_0_), channel_id=1, source_target_pairs={{0,4},{6,2},{2,0},{1,7},{7,5},{5,3},{8,12},{14,10},{10,8},{9,15},{... | collective-permute-start | bytes 1548296 | tf_op jit(solution)/shard_map/ppermute | solution.py:261
  20.4 8.3 %collective-permute-start.8 = (bf16[160,768]{1,0:T(8,128)(2,1)S(1)}, bf16[160,768]{1,0:T(8,128)(2,1)S(1)}, u32[]{:S(2)}, u32[]{:S(2)}) collective-permute-start(bf16[160,768]{1,0:T(8,128)(2,1)S(1)} %collective-permute-done.3.refs_3_.refs_4_.refs_2_), channel_id=1, source_target_pairs={{0,16},{1,9},{2,18},{3,11},{4,20},{5,13},{6,22},{7,15},{8,24},{9,1... | collective-permute-start | bytes 737288 | tf_op jit(solution)/shard_map/ppermute | solution.py:262
  21.0 10.6 %collective-permute-start.9 = (bf16[176,768]{1,0:T(8,128)(2,1)S(1)}, bf16[176,768]{1,0:T(8,128)(2,1)S(1)}, u32[]{:S(2)}, u32[]{:S(2)}) collective-permute-start(bf16[176,768]{1,0:T(8,128)(2,1)S(1)} %collective-permute-done.4.refs_4_.refs_5_.refs_3_), channel_id=1, source_target_pairs={{0,16},{1,9},{2,18},{3,11},{4,20},{5,13},{6,22},{7,15},{8,24},{9,1... | collective-permute-start | bytes 811016 | tf_op jit(solution)/shard_map/ppermute | solution.py:262
  23.7 9.1 %collective-permute-start.6 = (bf16[176,768]{1,0:T(8,128)(2,1)S(1)}, bf16[176,768]{1,0:T(8,128)(2,1)S(1)}, u32[]{:S(2)}, u32[]{:S(2)}) collective-permute-start(bf16[176,768]{1,0:T(8,128)(2,1)S(1)} %get-tuple-element.36), channel_id=1, source_target_pairs={{0,1},{1,0},{2,3},{3,2},{4,5},{5,4},{6,7},{7,6},{8,9},{9,8},{10,11... | collective-permute-start | bytes 811016 | tf_op jit(solution)/shard_map/ppermute | solution.py:272
  28.7 4.1 %collective-permute-start.5 = (bf16[160,768]{1,0:T(8,128)(2,1)S(1)}, bf16[160,768]{1,0:T(8,128)(2,1)S(1)}, u32[]{:S(2)}, u32[]{:S(2)}) collective-permute-start(bf16[160,768]{1,0:T(8,128)(2,1)S(1)} %get-tuple-element.35), channel_id=1, source_target_pairs={{0,1},{1,0},{2,3},{3,2},{4,5},{5,4},{6,7},{7,6},{8,9},{9,8},{10,11... | collective-permute-start | bytes 737288 | tf_op jit(solution)/shard_map/ppermute | solution.py:272
  34.6 2.0 %collective-permute-start.10 = (bf16[336,768]{1,0:T(8,128)(2,1)S(1)}, bf16[336,768]{1,0:T(8,128)(2,1)S(1)}, u32[]{:S(2)}, u32[]{:S(2)}) collective-permute-start(bf16[336,768]{1,0:T(8,128)(2,1)S(1)} %collective-permute-done.1.refs_0_), channel_id=1, source_target_pairs={{0,1},{1,0},{2,3},{3,2},{4,5},{5,4},{6,7},{7,6},{8,9},{9,8},{10,11... | collective-permute-start | bytes 1548296 | tf_op jit(solution)/shard_map/ppermute | solution.py:285
  37.8 1.2 %collective-permute-start.11 = (f32[1,640]{1,0:T(1,128)S(1)}, f32[1,640]{1,0:T(1,128)S(1)}, u32[]{:S(2)}, u32[]{:S(2)}) collective-permute-start(f32[1,640]{1,0:T(1,128)S(1)} %pad_maximum_fusion), channel_id=1, source_target_pairs={{0,1},{1,0},{2,3},{3,2},{4,5},{5,4},{6,7},{7,6},{8,9},{9,8},{10,11... | collective-permute-start | bytes 7688 | tf_op jit(solution)/shard_map/ppermute | solution.py:293
  37.9 3.9 %collective-permute-start.14 = (f32[1,640]{1,0:T(1,128)S(1)}, f32[1,640]{1,0:T(1,128)S(1)}, u32[]{:S(2)}, u32[]{:S(2)}) collective-permute-start(f32[1,640]{1,0:T(1,128)S(1)} %get-tuple-element.63), channel_id=1, source_target_pairs={{0,8},{1,17},{2,10},{3,19},{4,12},{5,21},{6,14},{7,23},{8,0},{9,25... | collective-permute-start | bytes 7688 | tf_op jit(solution)/shard_map/ppermute | solution.py:301
  39.0 6.4 %collective-permute-start.12 = (f32[1,640]{1,0:T(1,128)S(1)}, f32[1,640]{1,0:T(1,128)S(1)}, u32[]{:S(2)}, u32[]{:S(2)}) collective-permute-start(f32[1,640]{1,0:T(1,128)S(1)} %maximum_maximum_fusion), channel_id=1, source_target_pairs={{4,0},{2,6},{0,2},{7,1},{5,7},{3,5},{12,8},{10,14},{8,10},{15,9},{... | collective-permute-start | bytes 7688 | tf_op jit(solution)/shard_map/ppermute | solution.py:296
  41.9 3.9 %collective-permute-start.15 = (f32[1,320]{1,0:T(1,128)S(1)}, f32[1,320]{1,0:T(1,128)S(1)}, u32[]{:S(2)}, u32[]{:S(2)}) collective-permute-start(f32[1,320]{1,0:T(1,128)S(1)} %slice_maximum_fusion), channel_id=1, source_target_pairs={{0,16},{1,9},{2,18},{3,11},{4,20},{5,13},{6,22},{7,15},{8,24},{9,1... | collective-permute-start | bytes 3848 | tf_op jit(solution)/shard_map/ppermute | solution.py:304
  45.5 1.2 %collective-permute-start.13 = (f32[1,320]{1,0:T(1,128)S(1)}, f32[1,320]{1,0:T(1,128)S(1)}, u32[]{:S(2)}, u32[]{:S(2)}) collective-permute-start(f32[1,320]{1,0:T(1,128)S(1)} %slice.27), channel_id=1, source_target_pairs={{0,1},{1,0},{2,3},{3,2},{4,5},{5,4},{6,7},{7,6},{8,9},{9,8},{10,11... | collective-permute-start | bytes 3848 | tf_op jit(solution)/shard_map/ppermute | solution.py:300

commit v6 on v5

--- a/solution.py
+++ b/solution.py
@@ -28,8 +28,13 @@
 
 
 def prepare_kernel(
-    embeddings_hbm, cluster_hbm, order_key_hbm, block, embeddings, cluster, order_key, arrived
+    embeddings_hbm,
+    cluster_hbm,
+    order_key_hbm,
+    block,
+    *refs,
 ):
+    *parts_out, embeddings, cluster, order_key, arrived = refs
     copies = [
         pltpu.make_async_copy(source, target, arrived.at[at])
         for at, (source, target) in enumerate(
@@ -54,15 +59,22 @@
     parts = jnp.concatenate(parts + [jnp.zeros((EXTRA - 3, rows), jnp.float32)], axis=0)
     parts = jnp.concatenate([parts, jnp.zeros((EXTRA, width - rows), jnp.float32)], axis=1)
     block[rows : rows + EXTRA, :] = parts.astype(jnp.bfloat16)
-
-
-def prepare(embeddings, cluster, order_key):
+    top = 0
+    for out in parts_out:
+        out[...] = block[top : top + out.shape[0], :]
+        top += out.shape[0]
+
+
+def prepare(embeddings, cluster, order_key, heights):
     rows, width = embeddings.shape
     inputs = (embeddings, cluster.reshape(1, rows), order_key)
     return pl.pallas_call(
         prepare_kernel,
         in_specs=[pl.BlockSpec(memory_space=pltpu.HBM)] * 3,
-        out_shape=jax.ShapeDtypeStruct((rows + EXTRA, width), jnp.bfloat16),
+        out_shape=[
+            jax.ShapeDtypeStruct((height, width), jnp.bfloat16)
+            for height in (rows + EXTRA, *heights)
+        ],
         scratch_shapes=[pltpu.VMEM(array.shape, array.dtype) for array in inputs]
         + [pltpu.SemaphoreType.DMA((3,))],
         compiler_params=pltpu.CompilerParams(vmem_limit_bytes=56 << 20),
@@ -251,17 +263,15 @@
         span = 256
         while span < rows * groups * members:
             span *= 2
-        block = prepare(embeddings, cluster, order_key)
         halves = (rows // 2, rows // 2 + EXTRA)
+        block, *parts = prepare(embeddings, cluster, order_key, halves)
         own = [block]
-        parts = (block[: halves[0]], block[halves[0] :])
         partner = lax.ppermute(block, BOTH, other_core)
         near = [[lax.ppermute(block, BOTH, pairs)] for pairs in rounds]
         from_first = [lax.ppermute(part, BOTH, first) for part in parts]
         near_other = [[lax.ppermute(partner, BOTH, pairs)] for pairs in rounds]
         from_corner = [lax.ppermute(part, BOTH, second) for part in from_first]
-        later = lax.optimization_barrier((block, *from_first))[0]
-        from_second = [lax.ppermute(later, BOTH, second)]
+        from_second = [lax.ppermute(block, BOTH, second)]
         held = [own, from_first, from_second, from_corner]
 
         results, kept, sent = [], [], []

time: 47.5 us -> 45.4 us (0.956)
  waiting for transfers between devices: 17.2 us -> 13 us
  starting transfers between devices: 19.6 us -> 21.5 us
    ppermute x2, waiting for transfers between devices: 7.19 us -> 3.73 us  [shards(): from_corner = [lax.ppermute(part, BOTH, second) for part in from_first]]
    ppermute x2, starting transfers between devices: 3.21 us -> 2.09 us  [shards(): from_first = [lax.ppermute(part, BOTH, first) for part in parts]]
    unnamed x2 -> x4, local copies, waits for them, and re-layouts: 0.01 us -> 1.04 us
    ppermute x1, starting transfers between devices: 4.49 us -> 5.5 us  [shards(): near = [[lax.ppermute(block, BOTH, pairs)] for pairs in rounds]]
    slice x2 -> x0, local copies, waits for them, and re-layouts: 0.99 us -> none  [shards(): parts = (block[:halves[0]], block[halves[0]:])]
    ppermute x1, starting transfers between devices: 0.58 us -> 1.54 us  [shards(): from_x = lax.ppermute(bests[1], BOTH, first)]
    ppermute x2, starting transfers between devices: 2.09 us -> 3.04 us  [shards(): from_corner = [lax.ppermute(part, BOTH, second) for part in from_first]]
    ppermute x1, waiting for transfers between devices: 2.23 us -> 1.32 us  [shards(): lax.ppermute(kept[:, 2 * at * rows:2 * (at + 1) * rows], BOTH, back(pairs))]
  transfers between devices with their start and end apart: 16 -> 16, of which waited for: 7 -> 8; matrix products, arithmetic and copies ran while one was open for 3% -> 1% of each run, Pallas kernels for 11% -> 12%
where the time goes in v6:
time: 45.4 us; the launch traced here: 45.1 us
  starting transfers between devices  21.5 us (47%)
  waiting for transfers between devices  13 us (29%)
  Pallas kernels  8.58 us (19%)
  local copies, waits for them, and re-layouts  1.12 us (2%)
  other arithmetic  0.83 us (2%)
    pallas_call x5, Pallas kernels, meeting(): pl.pallas_call(functools.partial(meet_kernel, rows, span, [len(kind) for...  6.39 us
    ppermute x2, waiting for transfers between devices, shards(): from_first = [lax.ppermute(part, BOTH, first) for part in parts]  6.04 us
    ppermute x1, starting transfers between devices, shards(): near = [[lax.ppermute(block, BOTH, pairs)] for pairs in rounds]  5.5 us
    ppermute x2, waiting for transfers between devices, shards(): from_corner = [lax.ppermute(part, BOTH, second) for part in from_first]  3.73 us
    ppermute x1, starting transfers between devices, shards(): lax.ppermute(kept[:, 2 * at * rows:2 * (at + 1) * rows], BOTH, back(pairs))  3.46 us
    ppermute x2, starting transfers between devices, shards(): from_corner = [lax.ppermute(part, BOTH, second) for part in from_first]  3.04 us
    pallas_call x1, Pallas kernels, prepare(): pl.pallas_call(prepare_kernel, in_specs=[pl.BlockSpec(memory_space=pltpu....  2.19 us
    ppermute x2, starting transfers between devices, shards(): from_first = [lax.ppermute(part, BOTH, first) for part in parts]  2.09 us
  transfers between devices with their start and end apart: 16, of which 8 were waited for; matrix products, arithmetic and copies ran while one was open for 1% of the time, Pallas kernels for 12%

profile of v6, /device:TPU:0, one launch (start us, length us, event | category | flops | bytes accessed | tf_op | source)
XLA Modules:
  0.0 45.1 jit_solution(15129213637004511133)
XLA Ops:
  0.0 2.2 %shard_map.37 = (bf16[336,768]{1,0:T(8,128)(2,1)}, bf16[160,768]{1,0:T(8,128)(2,1)}, bf16[176,768]{1,0:T(8,128)(2,1)}) custom-call(bf16[320,768]{1,0:T(8,128)(2,1)} %embeddings_hbm.1, s32[1,320]{1,0:T(1,128)} %bitcast.1, s32[320]{0:T(512)} %order_key_hbm.1), custom_call_target="tpu_custom_call" | custom-call | flops 320 | bytes 320 | tf_op jit(solution)/shard_map/pallas_call | solution.py:71
  2.7 5.5 %collective-permute-start.2 = (bf16[336,768]{1,0:T(8,128)(2,1)}, bf16[336,768]{1,0:T(8,128)(2,1)S(1)}, u32[]{:S(2)}, u32[]{:S(2)}) collective-permute-start(bf16[336,768]{1,0:T(8,128)(2,1)} %get-tuple-element.37.refs_0_.refs_2_.refs_3_.refs_1_), channel_id=1, source_target_pairs={{0,4},{6,2},{2,0},{1,7},{7,5},{5,3},{8,12},{14,10},{10,8},{9,15},{... | collective-permute-start | bytes 1548296 | tf_op jit(solution)/shard_map/ppermute | solution.py:270
  8.2 1.6 %collective-permute-start.3 = (bf16[160,768]{1,0:T(8,128)(2,1)}, bf16[160,768]{1,0:T(8,128)(2,1)S(1)}, u32[]{:S(2)}, u32[]{:S(2)}) collective-permute-start(bf16[160,768]{1,0:T(8,128)(2,1)} %get-tuple-element.38), channel_id=1, source_target_pairs={{0,8},{1,17},{2,10},{3,19},{4,12},{5,21},{6,14},{7,23},{8,0},{9,25... | collective-permute-start | bytes 737288 | tf_op jit(solution)/shard_map/ppermute | solution.py:271
  10.3 1.5 %collective-permute-start.7 = (bf16[336,768]{1,0:T(8,128)(2,1)}, bf16[336,768]{1,0:T(8,128)(2,1)S(1)}, u32[]{:S(2)}, u32[]{:S(2)}) collective-permute-start(bf16[336,768]{1,0:T(8,128)(2,1)} %get-tuple-element.37.refs_0_.refs_2_.refs_3_.refs_1_), channel_id=1, source_target_pairs={{0,16},{1,9},{2,18},{3,11},{4,20},{5,13},{6,22},{7,15},{8,24},{9,1... | collective-permute-start | bytes 1548296 | tf_op jit(solution)/shard_map/ppermute | solution.py:274
  11.8 1.9 %collective-permute-start.1 = (bf16[336,768]{1,0:T(8,128)(2,1)S(1)}, bf16[336,768]{1,0:T(8,128)(2,1)S(1)}, u32[]{:S(2)}, u32[]{:S(2)}) collective-permute-start(bf16[336,768]{1,0:T(8,128)(2,1)S(1)} %collective-permute-done.refs_0_), channel_id=1, source_target_pairs={{0,4},{6,2},{2,0},{1,7},{7,5},{5,3},{8,12},{14,10},{10,8},{9,15},{... | collective-permute-start | bytes 1548296 | tf_op jit(solution)/shard_map/ppermute | solution.py:272
  13.8 1.8 %collective-permute-done.3.refs_3_.refs_4_.refs_2_ = bf16[160,768]{1,0:T(8,128)(2,1)S(1)} collective-permute-done((bf16[160,768]{1,0:T(8,128)(2,1)}, bf16[160,768]{1,0:T(8,128)(2,1)S(1)}, u32[]{:S(2)}, u32[]{:S(2)}) %collective-permute-start.3) | collective-permute-done | bytes 245792 | tf_op jit(solution)/shard_map/ppermute | solution.py:271
  15.5 1.5 %collective-permute-start.8 = (bf16[160,768]{1,0:T(8,128)(2,1)S(1)}, bf16[160,768]{1,0:T(8,128)(2,1)S(1)}, u32[]{:S(2)}, u32[]{:S(2)}) collective-permute-start(bf16[160,768]{1,0:T(8,128)(2,1)S(1)} %collective-permute-done.3.refs_3_.refs_4_.refs_2_), channel_id=1, source_target_pairs={{0,16},{1,9},{2,18},{3,11},{4,20},{5,13},{6,22},{7,15},{8,24},{9,1... | collective-permute-start | bytes 737288 | tf_op jit(solution)/shard_map/ppermute | solution.py:273
  17.0 4.3 %collective-permute-done.4.refs_4_.refs_5_.refs_3_ = bf16[176,768]{1,0:T(8,128)(2,1)S(1)} collective-permute-done((bf16[176,768]{1,0:T(8,128)(2,1)}, bf16[176,768]{1,0:T(8,128)(2,1)S(1)}, u32[]{:S(2)}, u32[]{:S(2)}) %collective-permute-start.4) | collective-permute-done | bytes 270368 | tf_op jit(solution)/shard_map/ppermute | solution.py:271
  21.3 1.5 %collective-permute-start.9 = (bf16[176,768]{1,0:T(8,128)(2,1)S(1)}, bf16[176,768]{1,0:T(8,128)(2,1)S(1)}, u32[]{:S(2)}, u32[]{:S(2)}) collective-permute-start(bf16[176,768]{1,0:T(8,128)(2,1)S(1)} %collective-permute-done.4.refs_4_.refs_5_.refs_3_), channel_id=1, source_target_pairs={{0,16},{1,9},{2,18},{3,11},{4,20},{5,13},{6,22},{7,15},{8,24},{9,1... | collective-permute-start | bytes 811016 | tf_op jit(solution)/shard_map/ppermute | solution.py:273
  22.8 1.0 %copy-done = bf16[336,768]{1,0:T(8,128)(2,1)S(1)} copy-done((bf16[336,768]{1,0:T(8,128)(2,1)S(1)}, bf16[336,768]{1,0:T(8,128)(2,1)}, u32[]{:S(2)}) %copy-start) | copy-done | bytes 516120
  23.9 1.2 %shard_map.38 = (f32[1,320]{1,0:T(1,128)S(1)}, f32[1,320]{1,0:T(1,128)S(1)}, f32[1,320]{1,0:T(1,128)S(1)}, f32[1,320]{1,0:T(1,128)S(1)}, bf16[160,768]{1,0:T(8,128)(2,1)S(1)}, /*index=5*/bf16[176,768]{1,0:T(8,128)(2,1)S(1)}) custom-call(bf16[336,768]{1,0:T(8,128)(2,1)S(1)} %copy-done, bf16[336,768]{1,0:T(8,128)(2,1)S(1)} %collective-permute-done.2.refs_1_, ...), custom_call_target="tpu_custom_call" | custom-call | flops 320 | bytes 320 | tf_op jit(solution)/shard_map/pallas_call | solution.py:202
  25.2 0.8 %collective-permute-done.8.refs_3_.refs_7_.refs_5_ = bf16[160,768]{1,0:T(8,128)(2,1)S(1)} collective-permute-done((bf16[160,768]{1,0:T(8,128)(2,1)S(1)}, bf16[160,768]{1,0:T(8,128)(2,1)S(1)}, u32[]{:S(2)}, u32[]{:S(2)}) %collective-permute-start.8) | collective-permute-done | bytes 245792 | tf_op jit(solution)/shard_map/ppermute | solution.py:273
  26.0 2.9 %collective-permute-done.9.refs_4_.refs_8_.refs_6_ = bf16[176,768]{1,0:T(8,128)(2,1)S(1)} collective-permute-done((bf16[176,768]{1,0:T(8,128)(2,1)S(1)}, bf16[176,768]{1,0:T(8,128)(2,1)S(1)}, u32[]{:S(2)}, u32[]{:S(2)}) %collective-permute-start.9) | collective-permute-done | bytes 270368 | tf_op jit(solution)/shard_map/ppermute | solution.py:273
  28.9 1.2 %shard_map.39 = (f32[1,320]{1,0:T(1,128)S(1)}, f32[1,320]{1,0:T(1,128)S(1)}, f32[1,320]{1,0:T(1,128)S(1)}, f32[1,320]{1,0:T(1,128)S(1)}) custom-call(bf16[336,768]{1,0:T(8,128)(2,1)S(1)} %copy-done, bf16[336,768]{1,0:T(8,128)(2,1)S(1)} %collective-permute-done.2.refs_1_, bf16[336,768]{1,0:T(8,128)(2,1)S(1)} %collective-permute-done.7.refs_2_.refs_6_.refs_4_, ...), custom_call_target="tpu_custom_call" | custom-call | flops 320 | bytes 320 | tf_op jit(solution)/shard_map/pallas_call | solution.py:202
  30.1 1.8 %shard_map.40 = (f32[1,320]{1,0:T(1,128)S(1)}, f32[1,320]{1,0:T(1,128)S(1)}, f32[1,320]{1,0:T(1,128)S(1)}, f32[1,320]{1,0:T(1,128)S(1)}, f32[1,320]{1,0:T(1,128)S(1)}) custom-call(bf16[336,768]{1,0:T(8,128)(2,1)S(1)} %collective-permute-done.refs_0_, bf16[160,768]{1,0:T(8,128)(2,1)S(1)} %collective-permute-done.5.refs_1_, ...), custom_call_target="tpu_custom_call" | custom-call | flops 320 | bytes 320 | tf_op jit(solution)/shard_map/pallas_call | solution.py:202
  32.1 1.1 %shard_map.41 = (f32[1,320]{1,0:T(1,128)S(1)}, f32[1,320]{1,0:T(1,128)S(1)}, f32[1,320]{1,0:T(1,128)S(1)}, f32[1,320]{1,0:T(1,128)S(1)}, f32[1,320]{1,0:T(1,128)S(1)}) custom-call(bf16[336,768]{1,0:T(8,128)(2,1)S(1)} %collective-permute-done.1.refs_0_, bf16[336,768]{1,0:T(8,128)(2,1)S(1)} %copy-done.1, ...), custom_call_target="tpu_custom_call" | custom-call | flops 320 | bytes 320 | tf_op jit(solution)/shard_map/pallas_call | solution.py:202
  33.2 0.7 %collective-permute-done.10.refs_0_ = bf16[336,768]{1,0:T(8,128)(2,1)S(1)} collective-permute-done((bf16[336,768]{1,0:T(8,128)(2,1)S(1)}, bf16[336,768]{1,0:T(8,128)(2,1)S(1)}, u32[]{:S(2)}, u32[]{:S(2)}) %collective-permute-start.10) | collective-permute-done | bytes 516128 | tf_op jit(solution)/shard_map/ppermute | solution.py:295
  34.0 1.1 %shard_map.42 = (f32[1,320]{1,0:T(1,128)S(1)}, f32[1,640]{1,0:T(1,128)S(1)}, f32[1,320]{1,0:T(1,128)S(1)}, f32[1,320]{1,0:T(1,128)S(1)}) custom-call(bf16[336,768]{1,0:T(8,128)(2,1)S(1)} %collective-permute-done.10.refs_0_, bf16[336,768]{1,0:T(8,128)(2,1)S(1)} %copy-done.1, bf16[160,768]{1,0:T(8,128)(2,1)S(1)} %collective-permute-done.3.refs_3_.refs_4_.refs_2_, ...), custom_call_target="tpu_custom_call" | custom-call | flops 320 | bytes 320 | tf_op jit(solution)/shard_map/pallas_call | solution.py:202
  35.3 1.5 %collective-permute-start.14 = (f32[1,640]{1,0:T(1,128)S(1)}, f32[1,640]{1,0:T(1,128)S(1)}, u32[]{:S(2)}, u32[]{:S(2)}) collective-permute-start(f32[1,640]{1,0:T(1,128)S(1)} %get-tuple-element.67), channel_id=1, source_target_pairs={{0,8},{1,17},{2,10},{3,19},{4,12},{5,21},{6,14},{7,23},{8,0},{9,25... | collective-permute-start | bytes 7688 | tf_op jit(solution)/shard_map/ppermute | solution.py:311
  36.9 3.5 %collective-permute-start.12 = (f32[1,640]{1,0:T(1,128)S(1)}, f32[1,640]{1,0:T(1,128)S(1)}, u32[]{:S(2)}, u32[]{:S(2)}) collective-permute-start(f32[1,640]{1,0:T(1,128)S(1)} %maximum_maximum_fusion), channel_id=1, source_target_pairs={{4,0},{2,6},{0,2},{7,1},{5,7},{3,5},{12,8},{10,14},{8,10},{15,9},{... | collective-permute-start | bytes 7688 | tf_op jit(solution)/shard_map/ppermute | solution.py:306
  40.5 1.5 %collective-permute-start.15 = (f32[1,320]{1,0:T(1,128)S(1)}, f32[1,320]{1,0:T(1,128)S(1)}, u32[]{:S(2)}, u32[]{:S(2)}) collective-permute-start(f32[1,320]{1,0:T(1,128)S(1)} %slice_maximum_fusion), channel_id=1, source_target_pairs={{0,16},{1,9},{2,18},{3,11},{4,20},{5,13},{6,22},{7,15},{8,24},{9,1... | collective-permute-start | bytes 3848 | tf_op jit(solution)/shard_map/ppermute | solution.py:314
  42.0 1.3 %collective-permute-done.12 = f32[1,640]{1,0:T(1,128)S(1)} collective-permute-done((f32[1,640]{1,0:T(1,128)S(1)}, f32[1,640]{1,0:T(1,128)S(1)}, u32[]{:S(2)}, u32[]{:S(2)}) %collective-permute-start.12) | collective-permute-done | bytes 2592 | tf_op jit(solution)/shard_map/ppermute | solution.py:306
  43.4 0.6 %collective-permute-done.15 = f32[1,320]{1,0:T(1,128)S(1)} collective-permute-done((f32[1,320]{1,0:T(1,128)S(1)}, f32[1,320]{1,0:T(1,128)S(1)}, u32[]{:S(2)}, u32[]{:S(2)}) %collective-permute-start.15) | collective-permute-done | bytes 1312 | tf_op jit(solution)/shard_map/ppermute | solution.py:314
  44.5 0.6 %fusion.2 = f32[320]{0:T(512)} fusion(f32[1,320]{1,0:T(1,128)S(1)} %collective-permute-done.15, f32[1,640]{1,0:T(1,128)S(1)} %collective-permute-done.14, f32[1,320]{1,0:T(1,128)S(1)} %collective-permute-done.13, f32[1,640]{1,0:T(1,128)S(1)} %broadcast_select_fusion, f32[1,320]{1,0:T(1,128)S(1)} %get-tuple-element.61, f32[1,320]{1,0:T(1,128)S(1)} %get-tuple-element.59, ...), kind=kLoop, calls=%fused_computation.8 | loop fusion | flops 1920 | bytes 10240 | tf_op jit(solution)/shard_map/max | solution.py:315
  (25 shorter events, 2.2 us)
Async XLA Ops:
  2.2 9.6 %collective-permute-start = (bf16[336,768]{1,0:T(8,128)(2,1)}, bf16[336,768]{1,0:T(8,128)(2,1)S(1)}, u32[]{:S(2)}, u32[]{:S(2)}) collective-permute-start(bf16[336,768]{1,0:T(8,128)(2,1)} %get-tuple-element.37.refs_0_.refs_2_.refs_3_.refs_1_), channel_id=1, source_target_pairs={{0,1},{1,0},{2,3},{3,2},{4,5},{5,4},{6,7},{7,6},{8,9},{9,8},{10,11... | collective-permute-start | bytes 1548296 | tf_op jit(solution)/shard_map/ppermute | solution.py:269
  2.7 20.1 %collective-permute-start.2 = (bf16[336,768]{1,0:T(8,128)(2,1)}, bf16[336,768]{1,0:T(8,128)(2,1)S(1)}, u32[]{:S(2)}, u32[]{:S(2)}) collective-permute-start(bf16[336,768]{1,0:T(8,128)(2,1)} %get-tuple-element.37.refs_0_.refs_2_.refs_3_.refs_1_), channel_id=1, source_target_pairs={{0,4},{6,2},{2,0},{1,7},{7,5},{5,3},{8,12},{14,10},{10,8},{9,15},{... | collective-permute-start | bytes 1548296 | tf_op jit(solution)/shard_map/ppermute | solution.py:270
  8.2 7.3 %collective-permute-start.3 = (bf16[160,768]{1,0:T(8,128)(2,1)}, bf16[160,768]{1,0:T(8,128)(2,1)S(1)}, u32[]{:S(2)}, u32[]{:S(2)}) collective-permute-start(bf16[160,768]{1,0:T(8,128)(2,1)} %get-tuple-element.38), channel_id=1, source_target_pairs={{0,8},{1,17},{2,10},{3,19},{4,12},{5,21},{6,14},{7,23},{8,0},{9,25... | collective-permute-start | bytes 737288 | tf_op jit(solution)/shard_map/ppermute | solution.py:271
  9.8 11.5 %collective-permute-start.4 = (bf16[176,768]{1,0:T(8,128)(2,1)}, bf16[176,768]{1,0:T(8,128)(2,1)S(1)}, u32[]{:S(2)}, u32[]{:S(2)}) collective-permute-start(bf16[176,768]{1,0:T(8,128)(2,1)} %get-tuple-element.39), channel_id=1, source_target_pairs={{0,8},{1,17},{2,10},{3,19},{4,12},{5,21},{6,14},{7,23},{8,0},{9,25... | collective-permute-start | bytes 811016 | tf_op jit(solution)/shard_map/ppermute | solution.py:271
  10.3 15.7 %collective-permute-start.7 = (bf16[336,768]{1,0:T(8,128)(2,1)}, bf16[336,768]{1,0:T(8,128)(2,1)S(1)}, u32[]{:S(2)}, u32[]{:S(2)}) collective-permute-start(bf16[336,768]{1,0:T(8,128)(2,1)} %get-tuple-element.37.refs_0_.refs_2_.refs_3_.refs_1_), channel_id=1, source_target_pairs={{0,16},{1,9},{2,18},{3,11},{4,20},{5,13},{6,22},{7,15},{8,24},{9,1... | collective-permute-start | bytes 1548296 | tf_op jit(solution)/shard_map/ppermute | solution.py:274
  11.8 20.1 %collective-permute-start.1 = (bf16[336,768]{1,0:T(8,128)(2,1)S(1)}, bf16[336,768]{1,0:T(8,128)(2,1)S(1)}, u32[]{:S(2)}, u32[]{:S(2)}) collective-permute-start(bf16[336,768]{1,0:T(8,128)(2,1)S(1)} %collective-permute-done.refs_0_), channel_id=1, source_target_pairs={{0,4},{6,2},{2,0},{1,7},{7,5},{5,3},{8,12},{14,10},{10,8},{9,15},{... | collective-permute-start | bytes 1548296 | tf_op jit(solution)/shard_map/ppermute | solution.py:272
  15.5 10.5 %collective-permute-start.8 = (bf16[160,768]{1,0:T(8,128)(2,1)S(1)}, bf16[160,768]{1,0:T(8,128)(2,1)S(1)}, u32[]{:S(2)}, u32[]{:S(2)}) collective-permute-start(bf16[160,768]{1,0:T(8,128)(2,1)S(1)} %collective-permute-done.3.refs_3_.refs_4_.refs_2_), channel_id=1, source_target_pairs={{0,16},{1,9},{2,18},{3,11},{4,20},{5,13},{6,22},{7,15},{8,24},{9,1... | collective-permute-start | bytes 737288 | tf_op jit(solution)/shard_map/ppermute | solution.py:273
  21.3 7.6 %collective-permute-start.9 = (bf16[176,768]{1,0:T(8,128)(2,1)S(1)}, bf16[176,768]{1,0:T(8,128)(2,1)S(1)}, u32[]{:S(2)}, u32[]{:S(2)}) collective-permute-start(bf16[176,768]{1,0:T(8,128)(2,1)S(1)} %collective-permute-done.4.refs_4_.refs_5_.refs_3_), channel_id=1, source_target_pairs={{0,16},{1,9},{2,18},{3,11},{4,20},{5,13},{6,22},{7,15},{8,24},{9,1... | collective-permute-start | bytes 811016 | tf_op jit(solution)/shard_map/ppermute | solution.py:273
  22.8 1.0 %copy-start = (bf16[336,768]{1,0:T(8,128)(2,1)S(1)}, bf16[336,768]{1,0:T(8,128)(2,1)}, u32[]{:S(2)}) copy-start(bf16[336,768]{1,0:T(8,128)(2,1)} %get-tuple-element.37.refs_0_.refs_2_.refs_3_.refs_1_) | copy-start | bytes 1548292
  25.1 5.1 %collective-permute-start.6 = (bf16[176,768]{1,0:T(8,128)(2,1)S(1)}, bf16[176,768]{1,0:T(8,128)(2,1)S(1)}, u32[]{:S(2)}, u32[]{:S(2)}) collective-permute-start(bf16[176,768]{1,0:T(8,128)(2,1)S(1)} %get-tuple-element.41), channel_id=1, source_target_pairs={{0,1},{1,0},{2,3},{3,2},{4,5},{5,4},{6,7},{7,6},{8,9},{9,8},{10,11... | collective-permute-start | bytes 811016 | tf_op jit(solution)/shard_map/ppermute | solution.py:282
  26.0 4.1 %collective-permute-start.5 = (bf16[160,768]{1,0:T(8,128)(2,1)S(1)}, bf16[160,768]{1,0:T(8,128)(2,1)S(1)}, u32[]{:S(2)}, u32[]{:S(2)}) collective-permute-start(bf16[160,768]{1,0:T(8,128)(2,1)S(1)} %get-tuple-element.40), channel_id=1, source_target_pairs={{0,1},{1,0},{2,3},{3,2},{4,5},{5,4},{6,7},{7,6},{8,9},{9,8},{10,11... | collective-permute-start | bytes 737288 | tf_op jit(solution)/shard_map/ppermute | solution.py:282
  30.1 2.0 %copy-start.1 = (bf16[336,768]{1,0:T(8,128)(2,1)S(1)}, bf16[336,768]{1,0:T(8,128)(2,1)}, u32[]{:S(2)}) copy-start(bf16[336,768]{1,0:T(8,128)(2,1)} %get-tuple-element.37.refs_0_.refs_2_.refs_3_.refs_1_) | copy-start | bytes 1548292
  32.0 2.0 %collective-permute-start.10 = (bf16[336,768]{1,0:T(8,128)(2,1)S(1)}, bf16[336,768]{1,0:T(8,128)(2,1)S(1)}, u32[]{:S(2)}, u32[]{:S(2)}) collective-permute-start(bf16[336,768]{1,0:T(8,128)(2,1)S(1)} %collective-permute-done.1.refs_0_), channel_id=1, source_target_pairs={{0,1},{1,0},{2,3},{3,2},{4,5},{5,4},{6,7},{7,6},{8,9},{9,8},{10,11... | collective-permute-start | bytes 1548296 | tf_op jit(solution)/shard_map/ppermute | solution.py:295
  35.1 1.7 %collective-permute-start.11 = (f32[1,640]{1,0:T(1,128)S(1)}, f32[1,640]{1,0:T(1,128)S(1)}, u32[]{:S(2)}, u32[]{:S(2)}) collective-permute-start(f32[1,640]{1,0:T(1,128)S(1)} %pad_maximum_fusion), channel_id=1, source_target_pairs={{0,1},{1,0},{2,3},{3,2},{4,5},{5,4},{6,7},{7,6},{8,9},{9,8},{10,11... | collective-permute-start | bytes 7688 | tf_op jit(solution)/shard_map/ppermute | solution.py:303
  35.3 5.1 %collective-permute-start.14 = (f32[1,640]{1,0:T(1,128)S(1)}, f32[1,640]{1,0:T(1,128)S(1)}, u32[]{:S(2)}, u32[]{:S(2)}) collective-permute-start(f32[1,640]{1,0:T(1,128)S(1)} %get-tuple-element.67), channel_id=1, source_target_pairs={{0,8},{1,17},{2,10},{3,19},{4,12},{5,21},{6,14},{7,23},{8,0},{9,25... | collective-permute-start | bytes 7688 | tf_op jit(solution)/shard_map/ppermute | solution.py:311
  36.9 6.4 %collective-permute-start.12 = (f32[1,640]{1,0:T(1,128)S(1)}, f32[1,640]{1,0:T(1,128)S(1)}, u32[]{:S(2)}, u32[]{:S(2)}) collective-permute-start(f32[1,640]{1,0:T(1,128)S(1)} %maximum_maximum_fusion), channel_id=1, source_target_pairs={{4,0},{2,6},{0,2},{7,1},{5,7},{3,5},{12,8},{10,14},{8,10},{15,9},{... | collective-permute-start | bytes 7688 | tf_op jit(solution)/shard_map/ppermute | solution.py:306
  40.5 3.6 %collective-permute-start.15 = (f32[1,320]{1,0:T(1,128)S(1)}, f32[1,320]{1,0:T(1,128)S(1)}, u32[]{:S(2)}, u32[]{:S(2)}) collective-permute-start(f32[1,320]{1,0:T(1,128)S(1)} %slice_maximum_fusion), channel_id=1, source_target_pairs={{0,16},{1,9},{2,18},{3,11},{4,20},{5,13},{6,22},{7,15},{8,24},{9,1... | collective-permute-start | bytes 3848 | tf_op jit(solution)/shard_map/ppermute | solution.py:314
  43.4 1.2 %collective-permute-start.13 = (f32[1,320]{1,0:T(1,128)S(1)}, f32[1,320]{1,0:T(1,128)S(1)}, u32[]{:S(2)}, u32[]{:S(2)}) collective-permute-start(f32[1,320]{1,0:T(1,128)S(1)} %slice.17), channel_id=1, source_target_pairs={{0,1},{1,0},{2,3},{3,2},{4,5},{5,4},{6,7},{7,6},{8,9},{9,8},{10,11... | collective-permute-start | bytes 3848 | tf_op jit(solution)/shard_map/ppermute | solution.py:310

commit v7 on v6

--- a/solution.py
+++ b/solution.py
@@ -27,34 +27,14 @@
     return parts[2:3] * (4.0 * span) + parts[0:1] * 256.0 + parts[1:2]
 
 
-def prepare_kernel(
-    embeddings_hbm,
-    cluster_hbm,
-    order_key_hbm,
-    block,
-    *refs,
-):
-    *parts_out, embeddings, cluster, order_key, arrived = refs
-    copies = [
-        pltpu.make_async_copy(source, target, arrived.at[at])
-        for at, (source, target) in enumerate(
-            (
-                (embeddings_hbm, embeddings),
-                (cluster_hbm, cluster),
-                (order_key_hbm, order_key),
-            )
-        )
-    ]
-    for copy in copies:
-        copy.start()
-    for copy in copies:
-        copy.wait()
+def prepare_kernel(span, embeddings, named, block, *parts_out):
     rows, width = embeddings.shape
     values = embeddings[...].astype(jnp.float32)
     scale = lax.rsqrt(jnp.sum(values * values, axis=1, keepdims=True) + EPSILON)
     block[0:rows, :] = (values * scale).astype(jnp.bfloat16)
-    keys = order_key[...].reshape(1, rows)
-    parts = [keys >> 8, keys & 255, cluster[...] + 1]
+    names = named[...].reshape(1, rows)
+    keys = names & (span - 1)
+    parts = [keys >> 8, keys & 255, (names >> (span.bit_length() - 1)) + 1]
     parts = [part.astype(jnp.float32) for part in parts]
     parts = jnp.concatenate(parts + [jnp.zeros((EXTRA - 3, rows), jnp.float32)], axis=0)
     parts = jnp.concatenate([parts, jnp.zeros((EXTRA, width - rows), jnp.float32)], axis=1)
@@ -65,21 +45,18 @@
         top += out.shape[0]
 
 
-def prepare(embeddings, cluster, order_key, heights):
+def prepare(embeddings, cluster, order_key, span, heights):
     rows, width = embeddings.shape
-    inputs = (embeddings, cluster.reshape(1, rows), order_key)
+    named = cluster[:, 0] * span + order_key
     return pl.pallas_call(
-        prepare_kernel,
-        in_specs=[pl.BlockSpec(memory_space=pltpu.HBM)] * 3,
+        functools.partial(prepare_kernel, span),
         out_shape=[
             jax.ShapeDtypeStruct((height, width), jnp.bfloat16)
             for height in (rows + EXTRA, *heights)
         ],
-        scratch_shapes=[pltpu.VMEM(array.shape, array.dtype) for array in inputs]
-        + [pltpu.SemaphoreType.DMA((3,))],
-        compiler_params=pltpu.CompilerParams(vmem_limit_bytes=56 << 20),
+        compiler_params=pltpu.CompilerParams(vmem_limit_bytes=16 << 20),
         cost_estimate=pl.CostEstimate(flops=rows, bytes_accessed=rows, transcendentals=0),
-    )(*inputs)
+    )(embeddings, named)
 
 
 def row_from_partial(partial, rows):
@@ -264,7 +241,7 @@
         while span < rows * groups * members:
             span *= 2
         halves = (rows // 2, rows // 2 + EXTRA)
-        block, *parts = prepare(embeddings, cluster, order_key, halves)
+        block, *parts = prepare(embeddings, cluster, order_key, span, halves)
         own = [block]
         partner = lax.ppermute(block, BOTH, other_core)
         near = [[lax.ppermute(block, BOTH, pairs)] for pairs in rounds]

time: 45.4 us -> 44.9 us (0.989)
  Pallas kernels: 8.58 us -> 6.58 us
  waiting for transfers between devices: 13 us -> 13.8 us
  other arithmetic: 0.83 us -> 1.55 us
    pallas_call x1, Pallas kernels: 2.19 us -> 0.18 us  [prepare(): pl.pallas_call(functools.partial(prepare_kernel, span), out_shape=[jax.Sh...]
    ppermute x2, waiting for transfers between devices: 3.73 us -> 4.78 us  [shards(): from_corner = [lax.ppermute(part, BOTH, second) for part in from_first]]
    mul x0 -> x1, other arithmetic: none -> 0.71 us  [prepare(): named = cluster[:, 0] * span + order_key]
where the time goes in v7:
time: 44.9 us; the launch traced here: 44.7 us
  starting transfers between devices  21.5 us (48%)
  waiting for transfers between devices  13.8 us (31%)
  Pallas kernels  6.58 us (15%)
  other arithmetic  1.55 us (3%)
  local copies, waits for them, and re-layouts  1.1 us (2%)
    pallas_call x5, Pallas kernels, meeting(): pl.pallas_call(functools.partial(meet_kernel, rows, span, [len(kind) for...  6.4 us
    ppermute x2, waiting for transfers between devices, shards(): from_first = [lax.ppermute(part, BOTH, first) for part in parts]  5.82 us
    ppermute x1, starting transfers between devices, shards(): near = [[lax.ppermute(block, BOTH, pairs)] for pairs in rounds]  5.51 us
    ppermute x2, waiting for transfers between devices, shards(): from_corner = [lax.ppermute(part, BOTH, second) for part in from_first]  4.78 us
    ppermute x1, starting transfers between devices, shards(): lax.ppermute(kept[:, 2 * at * rows:2 * (at + 1) * rows], BOTH, back(pairs))  3.47 us
    ppermute x2, starting transfers between devices, shards(): from_corner = [lax.ppermute(part, BOTH, second) for part in from_first]  3.04 us
    ppermute x2, starting transfers between devices, shards(): from_first = [lax.ppermute(part, BOTH, first) for part in parts]  2.09 us
    ppermute x1, starting transfers between devices, shards(): near_other = [[lax.ppermute(partner, BOTH, pairs)] for pairs in rounds]  1.91 us
  transfers between devices with their start and end apart: 16, of which 8 were waited for; matrix products, arithmetic and copies ran while one was open for 1% of the time, Pallas kernels for 12%

profile of v7, /device:TPU:0, one launch (start us, length us, event | category | flops | bytes accessed | tf_op | source)
XLA Modules:
  0.0 44.7 jit_solution(10200715468875081077)
XLA Ops:
  0.0 0.7 %multiply_reduce_fusion = s32[320]{0:T(512)S(1)} fusion(s32[320,1]{0,1:T(1,128)} %param.4), kind=kLoop, calls=%fused_computation.8 | loop fusion | flops 320 | bytes 2560 | tf_op jit(solution)/shard_map/mul | solution.py:50
  0.7 1.0 %copy-done = bf16[320,768]{1,0:T(8,128)(2,1)S(1)} copy-done((bf16[320,768]{1,0:T(8,128)(2,1)S(1)}, bf16[320,768]{1,0:T(8,128)(2,1)}, u32[]{:S(2)}) %copy-start) | copy-done | bytes 491544
  2.5 5.5 %collective-permute-start.2 = (bf16[336,768]{1,0:T(8,128)(2,1)S(1)}, bf16[336,768]{1,0:T(8,128)(2,1)S(1)}, u32[]{:S(2)}, u32[]{:S(2)}) collective-permute-start(bf16[336,768]{1,0:T(8,128)(2,1)S(1)} %get-tuple-element.37.refs_0_.refs_2_.refs_3_.refs_1_), channel_id=1, source_target_pairs={{0,4},{6,2},{2,0},{1,7},{7,5},{5,3},{8,12},{14,10},{10,8},{9,15},{... | collective-permute-start | bytes 1548296 | tf_op jit(solution)/shard_map/ppermute | solution.py:247
  8.0 1.6 %collective-permute-start.3 = (bf16[160,768]{1,0:T(8,128)(2,1)S(1)}, bf16[160,768]{1,0:T(8,128)(2,1)S(1)}, u32[]{:S(2)}, u32[]{:S(2)}) collective-permute-start(bf16[160,768]{1,0:T(8,128)(2,1)S(1)} %get-tuple-element.38), channel_id=1, source_target_pairs={{0,8},{1,17},{2,10},{3,19},{4,12},{5,21},{6,14},{7,23},{8,0},{9,25... | collective-permute-start | bytes 737288 | tf_op jit(solution)/shard_map/ppermute | solution.py:248
  10.1 1.5 %collective-permute-start.7 = (bf16[336,768]{1,0:T(8,128)(2,1)S(1)}, bf16[336,768]{1,0:T(8,128)(2,1)S(1)}, u32[]{:S(2)}, u32[]{:S(2)}) collective-permute-start(bf16[336,768]{1,0:T(8,128)(2,1)S(1)} %get-tuple-element.37.refs_0_.refs_2_.refs_3_.refs_1_), channel_id=1, source_target_pairs={{0,16},{1,9},{2,18},{3,11},{4,20},{5,13},{6,22},{7,15},{8,24},{9,1... | collective-permute-start | bytes 1548296 | tf_op jit(solution)/shard_map/ppermute | solution.py:251
  11.6 1.9 %collective-permute-start.1 = (bf16[336,768]{1,0:T(8,128)(2,1)S(1)}, bf16[336,768]{1,0:T(8,128)(2,1)S(1)}, u32[]{:S(2)}, u32[]{:S(2)}) collective-permute-start(bf16[336,768]{1,0:T(8,128)(2,1)S(1)} %collective-permute-done.refs_0_), channel_id=1, source_target_pairs={{0,4},{6,2},{2,0},{1,7},{7,5},{5,3},{8,12},{14,10},{10,8},{9,15},{... | collective-permute-start | bytes 1548296 | tf_op jit(solution)/shard_map/ppermute | solution.py:249
  13.5 1.6 %collective-permute-done.3.refs_3_.refs_4_.refs_2_ = bf16[160,768]{1,0:T(8,128)(2,1)S(1)} collective-permute-done((bf16[160,768]{1,0:T(8,128)(2,1)S(1)}, bf16[160,768]{1,0:T(8,128)(2,1)S(1)}, u32[]{:S(2)}, u32[]{:S(2)}) %collective-permute-start.3) | collective-permute-done | bytes 245792 | tf_op jit(solution)/shard_map/ppermute | solution.py:248
  15.1 1.5 %collective-permute-start.8 = (bf16[160,768]{1,0:T(8,128)(2,1)S(1)}, bf16[160,768]{1,0:T(8,128)(2,1)S(1)}, u32[]{:S(2)}, u32[]{:S(2)}) collective-permute-start(bf16[160,768]{1,0:T(8,128)(2,1)S(1)} %collective-permute-done.3.refs_3_.refs_4_.refs_2_), channel_id=1, source_target_pairs={{0,16},{1,9},{2,18},{3,11},{4,20},{5,13},{6,22},{7,15},{8,24},{9,1... | collective-permute-start | bytes 737288 | tf_op jit(solution)/shard_map/ppermute | solution.py:250
  16.6 4.3 %collective-permute-done.4.refs_4_.refs_5_.refs_3_ = bf16[176,768]{1,0:T(8,128)(2,1)S(1)} collective-permute-done((bf16[176,768]{1,0:T(8,128)(2,1)S(1)}, bf16[176,768]{1,0:T(8,128)(2,1)S(1)}, u32[]{:S(2)}, u32[]{:S(2)}) %collective-permute-start.4) | collective-permute-done | bytes 270368 | tf_op jit(solution)/shard_map/ppermute | solution.py:248
  20.9 1.5 %collective-permute-start.9 = (bf16[176,768]{1,0:T(8,128)(2,1)S(1)}, bf16[176,768]{1,0:T(8,128)(2,1)S(1)}, u32[]{:S(2)}, u32[]{:S(2)}) collective-permute-start(bf16[176,768]{1,0:T(8,128)(2,1)S(1)} %collective-permute-done.4.refs_4_.refs_5_.refs_3_), channel_id=1, source_target_pairs={{0,16},{1,9},{2,18},{3,11},{4,20},{5,13},{6,22},{7,15},{8,24},{9,1... | collective-permute-start | bytes 811016 | tf_op jit(solution)/shard_map/ppermute | solution.py:250
  22.4 1.2 %shard_map.38 = (f32[1,320]{1,0:T(1,128)S(1)}, f32[1,320]{1,0:T(1,128)S(1)}, f32[1,320]{1,0:T(1,128)S(1)}, f32[1,320]{1,0:T(1,128)S(1)}, bf16[160,768]{1,0:T(8,128)(2,1)S(1)}, /*index=5*/bf16[176,768]{1,0:T(8,128)(2,1)S(1)}) custom-call(bf16[336,768]{1,0:T(8,128)(2,1)S(1)} %get-tuple-element.37.refs_0_.refs_2_.refs_3_.refs_1_, ...), custom_call_target="tpu_custom_call" | custom-call | flops 320 | bytes 320 | tf_op jit(solution)/shard_map/pallas_call | solution.py:179
  23.7 1.9 %collective-permute-done.8.refs_3_.refs_7_.refs_5_ = bf16[160,768]{1,0:T(8,128)(2,1)S(1)} collective-permute-done((bf16[160,768]{1,0:T(8,128)(2,1)S(1)}, bf16[160,768]{1,0:T(8,128)(2,1)S(1)}, u32[]{:S(2)}, u32[]{:S(2)}) %collective-permute-start.8) | collective-permute-done | bytes 245792 | tf_op jit(solution)/shard_map/ppermute | solution.py:250
  25.6 2.9 %collective-permute-done.9.refs_4_.refs_8_.refs_6_ = bf16[176,768]{1,0:T(8,128)(2,1)S(1)} collective-permute-done((bf16[176,768]{1,0:T(8,128)(2,1)S(1)}, bf16[176,768]{1,0:T(8,128)(2,1)S(1)}, u32[]{:S(2)}, u32[]{:S(2)}) %collective-permute-start.9) | collective-permute-done | bytes 270368 | tf_op jit(solution)/shard_map/ppermute | solution.py:250
  28.5 1.2 %shard_map.39 = (f32[1,320]{1,0:T(1,128)S(1)}, f32[1,320]{1,0:T(1,128)S(1)}, f32[1,320]{1,0:T(1,128)S(1)}, f32[1,320]{1,0:T(1,128)S(1)}) custom-call(bf16[336,768]{1,0:T(8,128)(2,1)S(1)} %get-tuple-element.37.refs_0_.refs_2_.refs_3_.refs_1_, bf16[336,768]{1,0:T(8,128)(2,1)S(1)} %collective-permute-done.2.refs_1_, ...), custom_call_target="tpu_custom_call" | custom-call | flops 320 | bytes 320 | tf_op jit(solution)/shard_map/pallas_call | solution.py:179
  29.7 1.8 %shard_map.40 = (f32[1,320]{1,0:T(1,128)S(1)}, f32[1,320]{1,0:T(1,128)S(1)}, f32[1,320]{1,0:T(1,128)S(1)}, f32[1,320]{1,0:T(1,128)S(1)}, f32[1,320]{1,0:T(1,128)S(1)}) custom-call(bf16[336,768]{1,0:T(8,128)(2,1)S(1)} %collective-permute-done.refs_0_, bf16[160,768]{1,0:T(8,128)(2,1)S(1)} %collective-permute-done.5.refs_1_, ...), custom_call_target="tpu_custom_call" | custom-call | flops 320 | bytes 320 | tf_op jit(solution)/shard_map/pallas_call | solution.py:179
  31.6 1.1 %shard_map.41 = (f32[1,320]{1,0:T(1,128)S(1)}, f32[1,320]{1,0:T(1,128)S(1)}, f32[1,320]{1,0:T(1,128)S(1)}, f32[1,320]{1,0:T(1,128)S(1)}, f32[1,320]{1,0:T(1,128)S(1)}) custom-call(bf16[336,768]{1,0:T(8,128)(2,1)S(1)} %collective-permute-done.1.refs_0_, bf16[336,768]{1,0:T(8,128)(2,1)S(1)} %get-tuple-element.37.refs_0_.refs_2_.refs_3_.refs_1_, ...), custom_call_target="tpu_custom_call" | custom-call | flops 320 | bytes 320 | tf_op jit(solution)/shard_map/pallas_call | solution.py:179
  32.7 0.8 %collective-permute-done.10.refs_0_ = bf16[336,768]{1,0:T(8,128)(2,1)S(1)} collective-permute-done((bf16[336,768]{1,0:T(8,128)(2,1)S(1)}, bf16[336,768]{1,0:T(8,128)(2,1)S(1)}, u32[]{:S(2)}, u32[]{:S(2)}) %collective-permute-start.10) | collective-permute-done | bytes 516128 | tf_op jit(solution)/shard_map/ppermute | solution.py:272
  33.5 1.1 %shard_map.42 = (f32[1,320]{1,0:T(1,128)S(1)}, f32[1,640]{1,0:T(1,128)S(1)}, f32[1,320]{1,0:T(1,128)S(1)}, f32[1,320]{1,0:T(1,128)S(1)}) custom-call(bf16[336,768]{1,0:T(8,128)(2,1)S(1)} %collective-permute-done.10.refs_0_, bf16[336,768]{1,0:T(8,128)(2,1)S(1)} %get-tuple-element.37.refs_0_.refs_2_.refs_3_.refs_1_, ...), custom_call_target="tpu_custom_call" | custom-call | flops 320 | bytes 320 | tf_op jit(solution)/shard_map/pallas_call | solution.py:179
  34.8 1.5 %collective-permute-start.14 = (f32[1,640]{1,0:T(1,128)S(1)}, f32[1,640]{1,0:T(1,128)S(1)}, u32[]{:S(2)}, u32[]{:S(2)}) collective-permute-start(f32[1,640]{1,0:T(1,128)S(1)} %get-tuple-element.67), channel_id=1, source_target_pairs={{0,8},{1,17},{2,10},{3,19},{4,12},{5,21},{6,14},{7,23},{8,0},{9,25... | collective-permute-start | bytes 7688 | tf_op jit(solution)/shard_map/ppermute | solution.py:288
  36.4 3.5 %collective-permute-start.12 = (f32[1,640]{1,0:T(1,128)S(1)}, f32[1,640]{1,0:T(1,128)S(1)}, u32[]{:S(2)}, u32[]{:S(2)}) collective-permute-start(f32[1,640]{1,0:T(1,128)S(1)} %maximum_maximum_fusion), channel_id=1, source_target_pairs={{4,0},{2,6},{0,2},{7,1},{5,7},{3,5},{12,8},{10,14},{8,10},{15,9},{... | collective-permute-start | bytes 7688 | tf_op jit(solution)/shard_map/ppermute | solution.py:283
  40.0 1.5 %collective-permute-start.15 = (f32[1,320]{1,0:T(1,128)S(1)}, f32[1,320]{1,0:T(1,128)S(1)}, u32[]{:S(2)}, u32[]{:S(2)}) collective-permute-start(f32[1,320]{1,0:T(1,128)S(1)} %slice_maximum_fusion), channel_id=1, source_target_pairs={{0,16},{1,9},{2,18},{3,11},{4,20},{5,13},{6,22},{7,15},{8,24},{9,1... | collective-permute-start | bytes 3848 | tf_op jit(solution)/shard_map/ppermute | solution.py:291
  41.5 1.3 %collective-permute-done.12 = f32[1,640]{1,0:T(1,128)S(1)} collective-permute-done((f32[1,640]{1,0:T(1,128)S(1)}, f32[1,640]{1,0:T(1,128)S(1)}, u32[]{:S(2)}, u32[]{:S(2)}) %collective-permute-start.12) | collective-permute-done | bytes 2592 | tf_op jit(solution)/shard_map/ppermute | solution.py:283
  42.9 0.7 %collective-permute-done.15 = f32[1,320]{1,0:T(1,128)S(1)} collective-permute-done((f32[1,320]{1,0:T(1,128)S(1)}, f32[1,320]{1,0:T(1,128)S(1)}, u32[]{:S(2)}, u32[]{:S(2)}) %collective-permute-start.15) | collective-permute-done | bytes 1312 | tf_op jit(solution)/shard_map/ppermute | solution.py:291
  44.1 0.6 %fusion.2 = f32[320]{0:T(512)} fusion(f32[1,320]{1,0:T(1,128)S(1)} %collective-permute-done.15, f32[1,640]{1,0:T(1,128)S(1)} %collective-permute-done.14, f32[1,320]{1,0:T(1,128)S(1)} %collective-permute-done.13, f32[1,640]{1,0:T(1,128)S(1)} %broadcast_select_fusion, f32[1,320]{1,0:T(1,128)S(1)} %get-tuple-element.61, f32[1,320]{1,0:T(1,128)S(1)} %get-tuple-element.59, ...), kind=kLoop, calls=%fused_computation.9 | loop fusion | flops 1920 | bytes 10240 | tf_op jit(solution)/shard_map/max | solution.py:292
  (27 shorter events, 2.4 us)
Async XLA Ops:
  0.0 0.7 %copy-start.1 = (s32[320]{0:T(512)S(1)}, s32[320]{0:T(512)}, u32[]{:S(2)}) copy-start(s32[320]{0:T(512)} %param.5) | copy-start | bytes 3844
  0.7 1.0 %copy-start = (bf16[320,768]{1,0:T(8,128)(2,1)S(1)}, bf16[320,768]{1,0:T(8,128)(2,1)}, u32[]{:S(2)}) copy-start(bf16[320,768]{1,0:T(8,128)(2,1)} %embeddings.1) | copy-start | bytes 1474564
  2.0 9.6 %collective-permute-start = (bf16[336,768]{1,0:T(8,128)(2,1)S(1)}, bf16[336,768]{1,0:T(8,128)(2,1)S(1)}, u32[]{:S(2)}, u32[]{:S(2)}) collective-permute-start(bf16[336,768]{1,0:T(8,128)(2,1)S(1)} %get-tuple-element.37.refs_0_.refs_2_.refs_3_.refs_1_), channel_id=1, source_target_pairs={{0,1},{1,0},{2,3},{3,2},{4,5},{5,4},{6,7},{7,6},{8,9},{9,8},{10,11... | collective-permute-start | bytes 1548296 | tf_op jit(solution)/shard_map/ppermute | solution.py:246
  2.5 19.9 %collective-permute-start.2 = (bf16[336,768]{1,0:T(8,128)(2,1)S(1)}, bf16[336,768]{1,0:T(8,128)(2,1)S(1)}, u32[]{:S(2)}, u32[]{:S(2)}) collective-permute-start(bf16[336,768]{1,0:T(8,128)(2,1)S(1)} %get-tuple-element.37.refs_0_.refs_2_.refs_3_.refs_1_), channel_id=1, source_target_pairs={{0,4},{6,2},{2,0},{1,7},{7,5},{5,3},{8,12},{14,10},{10,8},{9,15},{... | collective-permute-start | bytes 1548296 | tf_op jit(solution)/shard_map/ppermute | solution.py:247
  8.0 7.1 %collective-permute-start.3 = (bf16[160,768]{1,0:T(8,128)(2,1)S(1)}, bf16[160,768]{1,0:T(8,128)(2,1)S(1)}, u32[]{:S(2)}, u32[]{:S(2)}) collective-permute-start(bf16[160,768]{1,0:T(8,128)(2,1)S(1)} %get-tuple-element.38), channel_id=1, source_target_pairs={{0,8},{1,17},{2,10},{3,19},{4,12},{5,21},{6,14},{7,23},{8,0},{9,25... | collective-permute-start | bytes 737288 | tf_op jit(solution)/shard_map/ppermute | solution.py:248
  9.5 11.3 %collective-permute-start.4 = (bf16[176,768]{1,0:T(8,128)(2,1)S(1)}, bf16[176,768]{1,0:T(8,128)(2,1)S(1)}, u32[]{:S(2)}, u32[]{:S(2)}) collective-permute-start(bf16[176,768]{1,0:T(8,128)(2,1)S(1)} %get-tuple-element.39), channel_id=1, source_target_pairs={{0,8},{1,17},{2,10},{3,19},{4,12},{5,21},{6,14},{7,23},{8,0},{9,25... | collective-permute-start | bytes 811016 | tf_op jit(solution)/shard_map/ppermute | solution.py:248
  10.1 15.5 %collective-permute-start.7 = (bf16[336,768]{1,0:T(8,128)(2,1)S(1)}, bf16[336,768]{1,0:T(8,128)(2,1)S(1)}, u32[]{:S(2)}, u32[]{:S(2)}) collective-permute-start(bf16[336,768]{1,0:T(8,128)(2,1)S(1)} %get-tuple-element.37.refs_0_.refs_2_.refs_3_.refs_1_), channel_id=1, source_target_pairs={{0,16},{1,9},{2,18},{3,11},{4,20},{5,13},{6,22},{7,15},{8,24},{9,1... | collective-permute-start | bytes 1548296 | tf_op jit(solution)/shard_map/ppermute | solution.py:251
  11.6 19.9 %collective-permute-start.1 = (bf16[336,768]{1,0:T(8,128)(2,1)S(1)}, bf16[336,768]{1,0:T(8,128)(2,1)S(1)}, u32[]{:S(2)}, u32[]{:S(2)}) collective-permute-start(bf16[336,768]{1,0:T(8,128)(2,1)S(1)} %collective-permute-done.refs_0_), channel_id=1, source_target_pairs={{0,4},{6,2},{2,0},{1,7},{7,5},{5,3},{8,12},{14,10},{10,8},{9,15},{... | collective-permute-start | bytes 1548296 | tf_op jit(solution)/shard_map/ppermute | solution.py:249
  15.1 10.5 %collective-permute-start.8 = (bf16[160,768]{1,0:T(8,128)(2,1)S(1)}, bf16[160,768]{1,0:T(8,128)(2,1)S(1)}, u32[]{:S(2)}, u32[]{:S(2)}) collective-permute-start(bf16[160,768]{1,0:T(8,128)(2,1)S(1)} %collective-permute-done.3.refs_3_.refs_4_.refs_2_), channel_id=1, source_target_pairs={{0,16},{1,9},{2,18},{3,11},{4,20},{5,13},{6,22},{7,15},{8,24},{9,1... | collective-permute-start | bytes 737288 | tf_op jit(solution)/shard_map/ppermute | solution.py:250
  20.9 7.6 %collective-permute-start.9 = (bf16[176,768]{1,0:T(8,128)(2,1)S(1)}, bf16[176,768]{1,0:T(8,128)(2,1)S(1)}, u32[]{:S(2)}, u32[]{:S(2)}) collective-permute-start(bf16[176,768]{1,0:T(8,128)(2,1)S(1)} %collective-permute-done.4.refs_4_.refs_5_.refs_3_), channel_id=1, source_target_pairs={{0,16},{1,9},{2,18},{3,11},{4,20},{5,13},{6,22},{7,15},{8,24},{9,1... | collective-permute-start | bytes 811016 | tf_op jit(solution)/shard_map/ppermute | solution.py:250
  23.6 6.1 %collective-permute-start.6 = (bf16[176,768]{1,0:T(8,128)(2,1)S(1)}, bf16[176,768]{1,0:T(8,128)(2,1)S(1)}, u32[]{:S(2)}, u32[]{:S(2)}) collective-permute-start(bf16[176,768]{1,0:T(8,128)(2,1)S(1)} %get-tuple-element.41), channel_id=1, source_target_pairs={{0,1},{1,0},{2,3},{3,2},{4,5},{5,4},{6,7},{7,6},{8,9},{9,8},{10,11... | collective-permute-start | bytes 811016 | tf_op jit(solution)/shard_map/ppermute | solution.py:259
  25.6 4.1 %collective-permute-start.5 = (bf16[160,768]{1,0:T(8,128)(2,1)S(1)}, bf16[160,768]{1,0:T(8,128)(2,1)S(1)}, u32[]{:S(2)}, u32[]{:S(2)}) collective-permute-start(bf16[160,768]{1,0:T(8,128)(2,1)S(1)} %get-tuple-element.40), channel_id=1, source_target_pairs={{0,1},{1,0},{2,3},{3,2},{4,5},{5,4},{6,7},{7,6},{8,9},{9,8},{10,11... | collective-permute-start | bytes 737288 | tf_op jit(solution)/shard_map/ppermute | solution.py:259
  31.5 2.0 %collective-permute-start.10 = (bf16[336,768]{1,0:T(8,128)(2,1)S(1)}, bf16[336,768]{1,0:T(8,128)(2,1)S(1)}, u32[]{:S(2)}, u32[]{:S(2)}) collective-permute-start(bf16[336,768]{1,0:T(8,128)(2,1)S(1)} %collective-permute-done.1.refs_0_), channel_id=1, source_target_pairs={{0,1},{1,0},{2,3},{3,2},{4,5},{5,4},{6,7},{7,6},{8,9},{9,8},{10,11... | collective-permute-start | bytes 1548296 | tf_op jit(solution)/shard_map/ppermute | solution.py:272
  34.7 1.7 %collective-permute-start.11 = (f32[1,640]{1,0:T(1,128)S(1)}, f32[1,640]{1,0:T(1,128)S(1)}, u32[]{:S(2)}, u32[]{:S(2)}) collective-permute-start(f32[1,640]{1,0:T(1,128)S(1)} %pad_maximum_fusion), channel_id=1, source_target_pairs={{0,1},{1,0},{2,3},{3,2},{4,5},{5,4},{6,7},{7,6},{8,9},{9,8},{10,11... | collective-permute-start | bytes 7688 | tf_op jit(solution)/shard_map/ppermute | solution.py:280
  34.8 5.1 %collective-permute-start.14 = (f32[1,640]{1,0:T(1,128)S(1)}, f32[1,640]{1,0:T(1,128)S(1)}, u32[]{:S(2)}, u32[]{:S(2)}) collective-permute-start(f32[1,640]{1,0:T(1,128)S(1)} %get-tuple-element.67), channel_id=1, source_target_pairs={{0,8},{1,17},{2,10},{3,19},{4,12},{5,21},{6,14},{7,23},{8,0},{9,25... | collective-permute-start | bytes 7688 | tf_op jit(solution)/shard_map/ppermute | solution.py:288
  36.4 6.4 %collective-permute-start.12 = (f32[1,640]{1,0:T(1,128)S(1)}, f32[1,640]{1,0:T(1,128)S(1)}, u32[]{:S(2)}, u32[]{:S(2)}) collective-permute-start(f32[1,640]{1,0:T(1,128)S(1)} %maximum_maximum_fusion), channel_id=1, source_target_pairs={{4,0},{2,6},{0,2},{7,1},{5,7},{3,5},{12,8},{10,14},{8,10},{15,9},{... | collective-permute-start | bytes 7688 | tf_op jit(solution)/shard_map/ppermute | solution.py:283
  40.0 3.6 %collective-permute-start.15 = (f32[1,320]{1,0:T(1,128)S(1)}, f32[1,320]{1,0:T(1,128)S(1)}, u32[]{:S(2)}, u32[]{:S(2)}) collective-permute-start(f32[1,320]{1,0:T(1,128)S(1)} %slice_maximum_fusion), channel_id=1, source_target_pairs={{0,16},{1,9},{2,18},{3,11},{4,20},{5,13},{6,22},{7,15},{8,24},{9,1... | collective-permute-start | bytes 3848 | tf_op jit(solution)/shard_map/ppermute | solution.py:291
  42.9 1.2 %collective-permute-start.13 = (f32[1,320]{1,0:T(1,128)S(1)}, f32[1,320]{1,0:T(1,128)S(1)}, u32[]{:S(2)}, u32[]{:S(2)}) collective-permute-start(f32[1,320]{1,0:T(1,128)S(1)} %slice.17), channel_id=1, source_target_pairs={{0,1},{1,0},{2,3},{3,2},{4,5},{5,4},{6,7},{7,6},{8,9},{9,8},{10,11... | collective-permute-start | bytes 3848 | tf_op jit(solution)/shard_map/ppermute | solution.py:287

commit v8 on v7

--- a/solution.py
+++ b/solution.py
@@ -34,7 +34,7 @@
     block[0:rows, :] = (values * scale).astype(jnp.bfloat16)
     names = named[...].reshape(1, rows)
     keys = names & (span - 1)
-    parts = [keys >> 8, keys & 255, (names >> (span.bit_length() - 1)) + 1]
+    parts = [keys >> 8, keys & 255, names >> (span.bit_length() - 1)]
     parts = [part.astype(jnp.float32) for part in parts]
     parts = jnp.concatenate(parts + [jnp.zeros((EXTRA - 3, rows), jnp.float32)], axis=0)
     parts = jnp.concatenate([parts, jnp.zeros((EXTRA, width - rows), jnp.float32)], axis=1)
@@ -45,9 +45,8 @@
         top += out.shape[0]
 
 
-def prepare(embeddings, cluster, order_key, span, heights):
+def prepare(embeddings, named, span, heights=()):
     rows, width = embeddings.shape
-    named = cluster[:, 0] * span + order_key
     return pl.pallas_call(
         functools.partial(prepare_kernel, span),
         out_shape=[
@@ -240,32 +239,40 @@
         span = 256
         while span < rows * groups * members:
             span *= 2
-        halves = (rows // 2, rows // 2 + EXTRA)
-        block, *parts = prepare(embeddings, cluster, order_key, span, halves)
+        heights = (rows // 5 * 4, rows // 5 + EXTRA)
+        named = (cluster[:, 0] + 1) * span + order_key
+        partner = lax.ppermute(embeddings, BOTH, other_core)
+        raw = [lax.ppermute(embeddings, BOTH, pairs) for pairs in rounds]
+        block, *parts = prepare(embeddings, named, span, heights)
         own = [block]
-        partner = lax.ppermute(block, BOTH, other_core)
-        near = [[lax.ppermute(block, BOTH, pairs)] for pairs in rounds]
         from_first = [lax.ppermute(part, BOTH, first) for part in parts]
+        from_second = [lax.ppermute(block, BOTH, second)]
+        (partner,) = prepare(partner, lax.ppermute(named, BOTH, other_core), span)
         near_other = [[lax.ppermute(partner, BOTH, pairs)] for pairs in rounds]
         from_corner = [lax.ppermute(part, BOTH, second) for part in from_first]
-        from_second = [lax.ppermute(block, BOTH, second)]
+        near = [
+            prepare(rows_of, lax.ppermute(named, BOTH, pairs), span, heights)
+            for rows_of, pairs in zip(raw, rounds)
+        ]
+        pieces = [lax.ppermute(piece, BOTH, other_core) for piece in near[0][1:]]
+        near = [blocks[:1] for blocks in near]
         held = [own, from_first, from_second, from_corner]
 
         results, kept, sent = [], [], []
-        bests, (mine, one), pieces = meeting(
-            [own, near[0]], [OWN, TWO], held[:2], [], rows, span, keep=halves
+        bests, (mine, one), _ = meeting(
+            [own, near[0]], [OWN, TWO], held[:3], [], rows, span
         )
         results.append(mine)
-        pieces = [lax.ppermute(piece, BOTH, other_core) for piece in pieces]
-        more_bests, (mine, one_more), _ = meeting(
-            [own, near[0]], [OWN, TWO], held[2:], [], rows, span
+        bests, (other,), _ = meeting(
+            [[partner], pieces], [HELD, TWO], held[:3], bests, rows, span
+        )
+        corner_best, (mine, one_more, other_more), _ = meeting(
+            [own, near[0], [partner], pieces], [OWN, TWO, HELD, TWO], held[3:], [], rows, span
         )
         results.append(mine)
+        bests += corner_best
         kept.append(jnp.maximum(one, one_more))
-        bests, found, _ = meeting(
-            [[partner], pieces], [HELD, TWO], held, bests + more_bests, rows, span
-        )
-        sent += found
+        sent.append(jnp.maximum(other, other_more))
         rest = [blocks for both in zip(near, near_other) for blocks in both][1:]
         for at, one in enumerate(rest):
             (one,), bests = lax.optimization_barrier((one, bests))

time: 44.9 us -> 55.5 us (1.24)
  starting transfers between devices: 21.5 us -> 27.1 us
  waiting for transfers between devices: 13.8 us -> 18.1 us
  Pallas kernels: 6.58 us -> 7.16 us
    ppermute x4 -> x6, waiting for transfers between devices: 0.01 us -> 8.2 us  [the longest x1 7.37 us: shards(): lax.ppermute(named, BOTH, pairs)]
    ppermute x2, waiting for transfers between devices: 4.78 us -> 1.83 us  [shards(): from_corner = [lax.ppermute(part, BOTH, second) for part in from_first]]
    ppermute x4 -> x6, starting transfers between devices: 6.16 us -> 9.08 us  [the longest x1 5.62 us: shards(): raw = [lax.ppermute(embeddings, BOTH, pairs) for pairs in rounds]]
    ppermute x2, starting transfers between devices: 3.04 us -> 4.19 us  [shards(): from_corner = [lax.ppermute(part, BOTH, second) for part in from_first]]
    ppermute x2, starting transfers between devices: 2.09 us -> 3.05 us  [shards(): from_first = [lax.ppermute(part, BOTH, first) for part in parts]]
  transfers between devices with their start and end apart: 16 -> 18, of which waited for: 8 -> 9; matrix products, arithmetic and copies ran while one was open for 1% -> 2% of each run, Pallas kernels for 12% -> 11%
where the time goes in v8:
time: 55.5 us; the launch traced here: 55.2 us
  starting transfers between devices  27.1 us (49%)
  waiting for transfers between devices  18.1 us (33%)
  Pallas kernels  7.16 us (13%)
  other arithmetic  1.54 us (3%)
  local copies, waits for them, and re-layouts  1.1 us (2%)
    ppermute x1, waiting for transfers between devices, shards(): lax.ppermute(named, BOTH, pairs)  7.37 us
    pallas_call x5, Pallas kernels, meeting(): pl.pallas_call(functools.partial(meet_kernel, rows, span, [len(kind) for...  6.62 us
    ppermute x1, starting transfers between devices, shards(): raw = [lax.ppermute(embeddings, BOTH, pairs) for pairs in rounds]  5.62 us
    ppermute x2, waiting for transfers between devices, shards(): from_first = [lax.ppermute(part, BOTH, first) for part in parts]  5.48 us
    ppermute x2, starting transfers between devices, shards(): from_corner = [lax.ppermute(part, BOTH, second) for part in from_first]  4.19 us
    ppermute x1, starting transfers between devices, shards(): lax.ppermute(kept[:, 2 * at * rows:2 * (at + 1) * rows], BOTH, back(pairs))  3.75 us
    ppermute x2, starting transfers between devices, shards(): from_first = [lax.ppermute(part, BOTH, first) for part in parts]  3.05 us
    ppermute x1, starting transfers between devices, shards(): lax.ppermute(named, BOTH, pairs)  1.92 us
  transfers between devices with their start and end apart: 18, of which 9 were waited for; matrix products, arithmetic and copies ran while one was open for 2% of the time, Pallas kernels for 11%

profile of v8, /device:TPU:0, one launch (start us, length us, event | category | flops | bytes accessed | tf_op | source)
XLA Modules:
  0.0 55.2 jit_solution(5171736552513483847)
XLA Ops:
  0.5 5.6 %collective-permute-start.3 = (bf16[320,768]{1,0:T(8,128)(2,1)}, bf16[320,768]{1,0:T(8,128)(2,1)S(1)}, u32[]{:S(2)}, u32[]{:S(2)}) collective-permute-start(bf16[320,768]{1,0:T(8,128)(2,1)} %embeddings.1), channel_id=1, source_target_pairs={{0,4},{6,2},{2,0},{1,7},{7,5},{5,3},{8,12},{14,10},{10,8},{9,15},{... | collective-permute-start | bytes 1474568 | tf_op jit(solution)/shard_map/ppermute | solution.py:245
  6.8 1.0 %copy-done = bf16[320,768]{1,0:T(8,128)(2,1)S(1)} copy-done((bf16[320,768]{1,0:T(8,128)(2,1)S(1)}, bf16[320,768]{1,0:T(8,128)(2,1)}, u32[]{:S(2)}) %copy-start) | copy-done | bytes 491544
  8.0 1.6 %collective-permute-start.7 = (bf16[256,768]{1,0:T(8,128)(2,1)S(1)}, bf16[256,768]{1,0:T(8,128)(2,1)S(1)}, u32[]{:S(2)}, u32[]{:S(2)}) collective-permute-start(bf16[256,768]{1,0:T(8,128)(2,1)S(1)} %get-tuple-element.41), channel_id=1, source_target_pairs={{0,8},{1,17},{2,10},{3,19},{4,12},{5,21},{6,14},{7,23},{8,0},{9,25... | collective-permute-start | bytes 1179656 | tf_op jit(solution)/shard_map/ppermute | solution.py:248
  9.6 1.5 %collective-permute-start.9 = (bf16[336,768]{1,0:T(8,128)(2,1)S(1)}, bf16[336,768]{1,0:T(8,128)(2,1)S(1)}, u32[]{:S(2)}, u32[]{:S(2)}) collective-permute-start(bf16[336,768]{1,0:T(8,128)(2,1)S(1)} %get-tuple-element.40.refs_0_.refs_2_.refs_3_.refs_1_), channel_id=1, source_target_pairs={{0,16},{1,9},{2,18},{3,11},{4,20},{5,13},{6,22},{7,15},{8,24},{9,1... | collective-permute-start | bytes 1548296 | tf_op jit(solution)/shard_map/ppermute | solution.py:249
  11.7 0.8 %collective-permute-done.1.named = s32[320]{0:T(512)S(1)} collective-permute-done((s32[320]{0:T(512)S(1)}, s32[320]{0:T(512)S(1)}, u32[]{:S(2)}, u32[]{:S(2)}) %collective-permute-start.1) | collective-permute-done | bytes 1312 | tf_op jit(solution)/shard_map/ppermute | solution.py:250
  12.7 1.9 %collective-permute-start.2 = (bf16[336,768]{1,0:T(8,128)(2,1)S(1)}, bf16[336,768]{1,0:T(8,128)(2,1)S(1)}, u32[]{:S(2)}, u32[]{:S(2)}) collective-permute-start(bf16[336,768]{1,0:T(8,128)(2,1)S(1)} %shard_map.37.refs_0_.refs_2_), channel_id=1, source_target_pairs={{0,4},{6,2},{2,0},{1,7},{7,5},{5,3},{8,12},{14,10},{10,8},{9,15},{... | collective-permute-start | bytes 1548296 | tf_op jit(solution)/shard_map/ppermute | solution.py:251
  14.6 1.9 %collective-permute-start.4 = (s32[320]{0:T(512)S(1)}, s32[320]{0:T(512)S(1)}, u32[]{:S(2)}, u32[]{:S(2)}) collective-permute-start(s32[320]{0:T(512)S(1)} %add.15.named), channel_id=1, source_target_pairs={{0,4},{6,2},{2,0},{1,7},{7,5},{5,3},{8,12},{14,10},{10,8},{9,15},{... | collective-permute-start | bytes 3848 | tf_op jit(solution)/shard_map/ppermute | solution.py:254
  16.5 2.1 %collective-permute-done.7.refs_3_.refs_4_.refs_2_ = bf16[256,768]{1,0:T(8,128)(2,1)S(1)} collective-permute-done((bf16[256,768]{1,0:T(8,128)(2,1)S(1)}, bf16[256,768]{1,0:T(8,128)(2,1)S(1)}, u32[]{:S(2)}, u32[]{:S(2)}) %collective-permute-start.7) | collective-permute-done | bytes 393248 | tf_op jit(solution)/shard_map/ppermute | solution.py:248
  18.6 2.7 %collective-permute-start.10 = (bf16[256,768]{1,0:T(8,128)(2,1)S(1)}, bf16[256,768]{1,0:T(8,128)(2,1)S(1)}, u32[]{:S(2)}, u32[]{:S(2)}) collective-permute-start(bf16[256,768]{1,0:T(8,128)(2,1)S(1)} %collective-permute-done.7.refs_3_.refs_4_.refs_2_), channel_id=1, source_target_pairs={{0,16},{1,9},{2,18},{3,11},{4,20},{5,13},{6,22},{7,15},{8,24},{9,1... | collective-permute-start | bytes 1179656 | tf_op jit(solution)/shard_map/ppermute | solution.py:252
  21.3 7.4 %collective-permute-done.4.named = s32[320]{0:T(512)S(1)} collective-permute-done((s32[320]{0:T(512)S(1)}, s32[320]{0:T(512)S(1)}, u32[]{:S(2)}, u32[]{:S(2)}) %collective-permute-start.4) | collective-permute-done | bytes 1312 | tf_op jit(solution)/shard_map/ppermute | solution.py:254
  29.4 1.5 %collective-permute-start.8 = (bf16[80,768]{1,0:T(8,128)(2,1)S(1)}, bf16[80,768]{1,0:T(8,128)(2,1)S(1)}, u32[]{:S(2)}, u32[]{:S(2)}) collective-permute-start(bf16[80,768]{1,0:T(8,128)(2,1)S(1)} %get-tuple-element.42), channel_id=1, source_target_pairs={{0,8},{1,17},{2,10},{3,19},{4,12},{5,21},{6,14},{7,23},{8,0},{9,25... | collective-permute-start | bytes 368648 | tf_op jit(solution)/shard_map/ppermute | solution.py:248
  30.9 3.4 %collective-permute-done.8.refs_4_.refs_5_.refs_3_ = bf16[80,768]{1,0:T(8,128)(2,1)S(1)} collective-permute-done((bf16[80,768]{1,0:T(8,128)(2,1)S(1)}, bf16[80,768]{1,0:T(8,128)(2,1)S(1)}, u32[]{:S(2)}, u32[]{:S(2)}) %collective-permute-start.8) | collective-permute-done | bytes 122912 | tf_op jit(solution)/shard_map/ppermute | solution.py:248
  34.2 1.5 %collective-permute-start.11 = (bf16[80,768]{1,0:T(8,128)(2,1)S(1)}, bf16[80,768]{1,0:T(8,128)(2,1)S(1)}, u32[]{:S(2)}, u32[]{:S(2)}) collective-permute-start(bf16[80,768]{1,0:T(8,128)(2,1)S(1)} %collective-permute-done.8.refs_4_.refs_5_.refs_3_), channel_id=1, source_target_pairs={{0,16},{1,9},{2,18},{3,11},{4,20},{5,13},{6,22},{7,15},{8,24},{9,1... | collective-permute-start | bytes 368648 | tf_op jit(solution)/shard_map/ppermute | solution.py:252
  35.8 1.5 %shard_map.40 = (f32[1,320]{1,0:T(1,128)S(1)}, f32[1,320]{1,0:T(1,128)S(1)}, f32[1,320]{1,0:T(1,128)S(1)}, f32[1,320]{1,0:T(1,128)S(1)}, f32[1,320]{1,0:T(1,128)S(1)}) custom-call(bf16[336,768]{1,0:T(8,128)(2,1)S(1)} %get-tuple-element.40.refs_0_.refs_2_.refs_3_.refs_1_, bf16[336,768]{1,0:T(8,128)(2,1)S(1)} %get-tuple-element.43.refs_1_, ...), custom_call_target="tpu_custom_call" | custom-call | flops 320 | bytes 320 | tf_op jit(solution)/shard_map/pallas_call | solution.py:178
  37.3 1.8 %collective-permute-done.11.refs_6_ = bf16[80,768]{1,0:T(8,128)(2,1)S(1)} collective-permute-done((bf16[80,768]{1,0:T(8,128)(2,1)S(1)}, bf16[80,768]{1,0:T(8,128)(2,1)S(1)}, u32[]{:S(2)}, u32[]{:S(2)}) %collective-permute-start.11) | collective-permute-done | bytes 122912 | tf_op jit(solution)/shard_map/ppermute | solution.py:252
  39.1 1.4 %shard_map.42 = (f32[1,320]{1,0:T(1,128)S(1)}, f32[1,320]{1,0:T(1,128)S(1)}, f32[1,320]{1,0:T(1,128)S(1)}, f32[1,320]{1,0:T(1,128)S(1)}) custom-call(bf16[336,768]{1,0:T(8,128)(2,1)S(1)} %get-tuple-element.40.refs_0_.refs_2_.refs_3_.refs_1_, bf16[336,768]{1,0:T(8,128)(2,1)S(1)} %get-tuple-element.43.refs_1_, bf16[336,768]{1,0:T(8,128)(2,1)S(1)} %shard_map.37.refs_0_.refs_2_, ...), custom_call_target="tpu_custom_call" | custom-call | flops 320 | bytes 320 | tf_op jit(solution)/shard_map/pallas_call | solution.py:178
  40.5 1.5 %shard_map.41 = (f32[1,320]{1,0:T(1,128)S(1)}, f32[1,320]{1,0:T(1,128)S(1)}, f32[1,320]{1,0:T(1,128)S(1)}, f32[1,320]{1,0:T(1,128)S(1)}) custom-call(bf16[336,768]{1,0:T(8,128)(2,1)S(1)} %shard_map.37.refs_0_.refs_2_, bf16[256,768]{1,0:T(8,128)(2,1)S(1)} %collective-permute-done.5.refs_1_.refs_3_, ...), custom_call_target="tpu_custom_call" | custom-call | flops 320 | bytes 320 | tf_op jit(solution)/shard_map/pallas_call | solution.py:178
  42.2 1.1 %shard_map.43 = (f32[1,320]{1,0:T(1,128)S(1)}, f32[1,320]{1,0:T(1,128)S(1)}, f32[1,320]{1,0:T(1,128)S(1)}, f32[1,320]{1,0:T(1,128)S(1)}, f32[1,320]{1,0:T(1,128)S(1)}) custom-call(bf16[336,768]{1,0:T(8,128)(2,1)S(1)} %collective-permute-done.2.refs_0_, bf16[336,768]{1,0:T(8,128)(2,1)S(1)} %get-tuple-element.40.refs_0_.refs_2_.refs_3_.refs_1_, ...), custom_call_target="tpu_custom_call" | custom-call | flops 320 | bytes 320 | tf_op jit(solution)/shard_map/pallas_call | solution.py:178
  43.3 0.7 %collective-permute-done.12.refs_0_ = bf16[336,768]{1,0:T(8,128)(2,1)S(1)} collective-permute-done((bf16[336,768]{1,0:T(8,128)(2,1)S(1)}, bf16[336,768]{1,0:T(8,128)(2,1)S(1)}, u32[]{:S(2)}, u32[]{:S(2)}) %collective-permute-start.12) | collective-permute-done | bytes 516128 | tf_op jit(solution)/shard_map/ppermute | solution.py:279
  44.0 1.1 %shard_map.44 = (f32[1,320]{1,0:T(1,128)S(1)}, f32[1,640]{1,0:T(1,128)S(1)}, f32[1,320]{1,0:T(1,128)S(1)}, f32[1,320]{1,0:T(1,128)S(1)}) custom-call(bf16[336,768]{1,0:T(8,128)(2,1)S(1)} %collective-permute-done.12.refs_0_, bf16[336,768]{1,0:T(8,128)(2,1)S(1)} %get-tuple-element.40.refs_0_.refs_2_.refs_3_.refs_1_, ...), custom_call_target="tpu_custom_call" | custom-call | flops 320 | bytes 320 | tf_op jit(solution)/shard_map/pallas_call | solution.py:178
  45.4 1.5 %collective-permute-start.16 = (f32[1,640]{1,0:T(1,128)S(1)}, f32[1,640]{1,0:T(1,128)S(1)}, u32[]{:S(2)}, u32[]{:S(2)}) collective-permute-start(f32[1,640]{1,0:T(1,128)S(1)} %get-tuple-element.69), channel_id=1, source_target_pairs={{0,8},{1,17},{2,10},{3,19},{4,12},{5,21},{6,14},{7,23},{8,0},{9,25... | collective-permute-start | bytes 7688 | tf_op jit(solution)/shard_map/ppermute | solution.py:295
  47.0 3.7 %collective-permute-start.14 = (f32[1,640]{1,0:T(1,128)S(1)}, f32[1,640]{1,0:T(1,128)S(1)}, u32[]{:S(2)}, u32[]{:S(2)}) collective-permute-start(f32[1,640]{1,0:T(1,128)S(1)} %maximum_maximum_fusion), channel_id=1, source_target_pairs={{4,0},{2,6},{0,2},{7,1},{5,7},{3,5},{12,8},{10,14},{8,10},{15,9},{... | collective-permute-start | bytes 7688 | tf_op jit(solution)/shard_map/ppermute | solution.py:290
  50.8 1.5 %collective-permute-start.17 = (f32[1,320]{1,0:T(1,128)S(1)}, f32[1,320]{1,0:T(1,128)S(1)}, u32[]{:S(2)}, u32[]{:S(2)}) collective-permute-start(f32[1,320]{1,0:T(1,128)S(1)} %slice_maximum_fusion), channel_id=1, source_target_pairs={{0,16},{1,9},{2,18},{3,11},{4,20},{5,13},{6,22},{7,15},{8,24},{9,1... | collective-permute-start | bytes 3848 | tf_op jit(solution)/shard_map/ppermute | solution.py:298
  52.3 1.0 %collective-permute-done.14 = f32[1,640]{1,0:T(1,128)S(1)} collective-permute-done((f32[1,640]{1,0:T(1,128)S(1)}, f32[1,640]{1,0:T(1,128)S(1)}, u32[]{:S(2)}, u32[]{:S(2)}) %collective-permute-start.14) | collective-permute-done | bytes 2592 | tf_op jit(solution)/shard_map/ppermute | solution.py:290
  (34 shorter events, 5.1 us)
Async XLA Ops:
  0.0 6.8 %copy-start.1 = (s32[320]{0:T(512)S(1)}, s32[320]{0:T(512)}, u32[]{:S(2)}) copy-start(s32[320]{0:T(512)} %param.5) | copy-start | bytes 3844
  0.0 12.5 %collective-permute-start = (bf16[320,768]{1,0:T(8,128)(2,1)}, bf16[320,768]{1,0:T(8,128)(2,1)S(1)}, u32[]{:S(2)}, u32[]{:S(2)}) collective-permute-start(bf16[320,768]{1,0:T(8,128)(2,1)} %embeddings.1), channel_id=1, source_target_pairs={{0,1},{1,0},{2,3},{3,2},{4,5},{5,4},{6,7},{7,6},{8,9},{9,8},{10,11... | collective-permute-start | bytes 1474568 | tf_op jit(solution)/shard_map/ppermute | solution.py:244
  0.5 28.2 %collective-permute-start.3 = (bf16[320,768]{1,0:T(8,128)(2,1)}, bf16[320,768]{1,0:T(8,128)(2,1)S(1)}, u32[]{:S(2)}, u32[]{:S(2)}) collective-permute-start(bf16[320,768]{1,0:T(8,128)(2,1)} %embeddings.1), channel_id=1, source_target_pairs={{0,4},{6,2},{2,0},{1,7},{7,5},{5,3},{8,12},{14,10},{10,8},{9,15},{... | collective-permute-start | bytes 1474568 | tf_op jit(solution)/shard_map/ppermute | solution.py:245
  6.8 1.0 %copy-start = (bf16[320,768]{1,0:T(8,128)(2,1)S(1)}, bf16[320,768]{1,0:T(8,128)(2,1)}, u32[]{:S(2)}) copy-start(bf16[320,768]{1,0:T(8,128)(2,1)} %embeddings.1) | copy-start | bytes 1474564
  8.0 10.6 %collective-permute-start.7 = (bf16[256,768]{1,0:T(8,128)(2,1)S(1)}, bf16[256,768]{1,0:T(8,128)(2,1)S(1)}, u32[]{:S(2)}, u32[]{:S(2)}) collective-permute-start(bf16[256,768]{1,0:T(8,128)(2,1)S(1)} %get-tuple-element.41), channel_id=1, source_target_pairs={{0,8},{1,17},{2,10},{3,19},{4,12},{5,21},{6,14},{7,23},{8,0},{9,25... | collective-permute-start | bytes 1179656 | tf_op jit(solution)/shard_map/ppermute | solution.py:248
  9.6 26.2 %collective-permute-start.9 = (bf16[336,768]{1,0:T(8,128)(2,1)S(1)}, bf16[336,768]{1,0:T(8,128)(2,1)S(1)}, u32[]{:S(2)}, u32[]{:S(2)}) collective-permute-start(bf16[336,768]{1,0:T(8,128)(2,1)S(1)} %get-tuple-element.40.refs_0_.refs_2_.refs_3_.refs_1_), channel_id=1, source_target_pairs={{0,16},{1,9},{2,18},{3,11},{4,20},{5,13},{6,22},{7,15},{8,24},{9,1... | collective-permute-start | bytes 1548296 | tf_op jit(solution)/shard_map/ppermute | solution.py:249
  11.1 1.4 %collective-permute-start.1 = (s32[320]{0:T(512)S(1)}, s32[320]{0:T(512)S(1)}, u32[]{:S(2)}, u32[]{:S(2)}) collective-permute-start(s32[320]{0:T(512)S(1)} %add.15.named), channel_id=1, source_target_pairs={{0,1},{1,0},{2,3},{3,2},{4,5},{5,4},{6,7},{7,6},{8,9},{9,8},{10,11... | collective-permute-start | bytes 3848 | tf_op jit(solution)/shard_map/ppermute | solution.py:250
  12.7 29.4 %collective-permute-start.2 = (bf16[336,768]{1,0:T(8,128)(2,1)S(1)}, bf16[336,768]{1,0:T(8,128)(2,1)S(1)}, u32[]{:S(2)}, u32[]{:S(2)}) collective-permute-start(bf16[336,768]{1,0:T(8,128)(2,1)S(1)} %shard_map.37.refs_0_.refs_2_), channel_id=1, source_target_pairs={{0,4},{6,2},{2,0},{1,7},{7,5},{5,3},{8,12},{14,10},{10,8},{9,15},{... | collective-permute-start | bytes 1548296 | tf_op jit(solution)/shard_map/ppermute | solution.py:251
  14.6 14.1 %collective-permute-start.4 = (s32[320]{0:T(512)S(1)}, s32[320]{0:T(512)S(1)}, u32[]{:S(2)}, u32[]{:S(2)}) collective-permute-start(s32[320]{0:T(512)S(1)} %add.15.named), channel_id=1, source_target_pairs={{0,4},{6,2},{2,0},{1,7},{7,5},{5,3},{8,12},{14,10},{10,8},{9,15},{... | collective-permute-start | bytes 3848 | tf_op jit(solution)/shard_map/ppermute | solution.py:254
  18.6 20.5 %collective-permute-start.10 = (bf16[256,768]{1,0:T(8,128)(2,1)S(1)}, bf16[256,768]{1,0:T(8,128)(2,1)S(1)}, u32[]{:S(2)}, u32[]{:S(2)}) collective-permute-start(bf16[256,768]{1,0:T(8,128)(2,1)S(1)} %collective-permute-done.7.refs_3_.refs_4_.refs_2_), channel_id=1, source_target_pairs={{0,16},{1,9},{2,18},{3,11},{4,20},{5,13},{6,22},{7,15},{8,24},{9,1... | collective-permute-start | bytes 1179656 | tf_op jit(solution)/shard_map/ppermute | solution.py:252
  28.9 10.3 %collective-permute-start.5 = (bf16[256,768]{1,0:T(8,128)(2,1)S(1)}, bf16[256,768]{1,0:T(8,128)(2,1)S(1)}, u32[]{:S(2)}, u32[]{:S(2)}) collective-permute-start(bf16[256,768]{1,0:T(8,128)(2,1)S(1)} %get-tuple-element.38), channel_id=1, source_target_pairs={{0,1},{1,0},{2,3},{3,2},{4,5},{5,4},{6,7},{7,6},{8,9},{9,8},{10,11... | collective-permute-start | bytes 1179656 | tf_op jit(solution)/shard_map/ppermute | solution.py:257
  29.4 4.9 %collective-permute-start.8 = (bf16[80,768]{1,0:T(8,128)(2,1)S(1)}, bf16[80,768]{1,0:T(8,128)(2,1)S(1)}, u32[]{:S(2)}, u32[]{:S(2)}) collective-permute-start(bf16[80,768]{1,0:T(8,128)(2,1)S(1)} %get-tuple-element.42), channel_id=1, source_target_pairs={{0,8},{1,17},{2,10},{3,19},{4,12},{5,21},{6,14},{7,23},{8,0},{9,25... | collective-permute-start | bytes 368648 | tf_op jit(solution)/shard_map/ppermute | solution.py:248
  34.2 4.9 %collective-permute-start.11 = (bf16[80,768]{1,0:T(8,128)(2,1)S(1)}, bf16[80,768]{1,0:T(8,128)(2,1)S(1)}, u32[]{:S(2)}, u32[]{:S(2)}) collective-permute-start(bf16[80,768]{1,0:T(8,128)(2,1)S(1)} %collective-permute-done.8.refs_4_.refs_5_.refs_3_), channel_id=1, source_target_pairs={{0,16},{1,9},{2,18},{3,11},{4,20},{5,13},{6,22},{7,15},{8,24},{9,1... | collective-permute-start | bytes 368648 | tf_op jit(solution)/shard_map/ppermute | solution.py:252
  35.8 3.4 %collective-permute-start.6 = (bf16[80,768]{1,0:T(8,128)(2,1)S(1)}, bf16[80,768]{1,0:T(8,128)(2,1)S(1)}, u32[]{:S(2)}, u32[]{:S(2)}) collective-permute-start(bf16[80,768]{1,0:T(8,128)(2,1)S(1)} %get-tuple-element.39), channel_id=1, source_target_pairs={{0,1},{1,0},{2,3},{3,2},{4,5},{5,4},{6,7},{7,6},{8,9},{9,8},{10,11... | collective-permute-start | bytes 368648 | tf_op jit(solution)/shard_map/ppermute | solution.py:257
  42.1 2.0 %collective-permute-start.12 = (bf16[336,768]{1,0:T(8,128)(2,1)S(1)}, bf16[336,768]{1,0:T(8,128)(2,1)S(1)}, u32[]{:S(2)}, u32[]{:S(2)}) collective-permute-start(bf16[336,768]{1,0:T(8,128)(2,1)S(1)} %collective-permute-done.2.refs_0_), channel_id=1, source_target_pairs={{0,1},{1,0},{2,3},{3,2},{4,5},{5,4},{6,7},{7,6},{8,9},{9,8},{10,11... | collective-permute-start | bytes 1548296 | tf_op jit(solution)/shard_map/ppermute | solution.py:279
  45.2 1.7 %collective-permute-start.13 = (f32[1,640]{1,0:T(1,128)S(1)}, f32[1,640]{1,0:T(1,128)S(1)}, u32[]{:S(2)}, u32[]{:S(2)}) collective-permute-start(f32[1,640]{1,0:T(1,128)S(1)} %pad_maximum_fusion), channel_id=1, source_target_pairs={{0,1},{1,0},{2,3},{3,2},{4,5},{5,4},{6,7},{7,6},{8,9},{9,8},{10,11... | collective-permute-start | bytes 7688 | tf_op jit(solution)/shard_map/ppermute | solution.py:287
  45.4 5.4 %collective-permute-start.16 = (f32[1,640]{1,0:T(1,128)S(1)}, f32[1,640]{1,0:T(1,128)S(1)}, u32[]{:S(2)}, u32[]{:S(2)}) collective-permute-start(f32[1,640]{1,0:T(1,128)S(1)} %get-tuple-element.69), channel_id=1, source_target_pairs={{0,8},{1,17},{2,10},{3,19},{4,12},{5,21},{6,14},{7,23},{8,0},{9,25... | collective-permute-start | bytes 7688 | tf_op jit(solution)/shard_map/ppermute | solution.py:295
  47.0 6.4 %collective-permute-start.14 = (f32[1,640]{1,0:T(1,128)S(1)}, f32[1,640]{1,0:T(1,128)S(1)}, u32[]{:S(2)}, u32[]{:S(2)}) collective-permute-start(f32[1,640]{1,0:T(1,128)S(1)} %maximum_maximum_fusion), channel_id=1, source_target_pairs={{4,0},{2,6},{0,2},{7,1},{5,7},{3,5},{12,8},{10,14},{8,10},{15,9},{... | collective-permute-start | bytes 7688 | tf_op jit(solution)/shard_map/ppermute | solution.py:290
  50.8 3.6 %collective-permute-start.17 = (f32[1,320]{1,0:T(1,128)S(1)}, f32[1,320]{1,0:T(1,128)S(1)}, u32[]{:S(2)}, u32[]{:S(2)}) collective-permute-start(f32[1,320]{1,0:T(1,128)S(1)} %slice_maximum_fusion), channel_id=1, source_target_pairs={{0,16},{1,9},{2,18},{3,11},{4,20},{5,13},{6,22},{7,15},{8,24},{9,1... | collective-permute-start | bytes 3848 | tf_op jit(solution)/shard_map/ppermute | solution.py:298
  53.4 1.2 %collective-permute-start.15 = (f32[1,320]{1,0:T(1,128)S(1)}, f32[1,320]{1,0:T(1,128)S(1)}, u32[]{:S(2)}, u32[]{:S(2)}) collective-permute-start(f32[1,320]{1,0:T(1,128)S(1)} %slice.17), channel_id=1, source_target_pairs={{0,1},{1,0},{2,3},{3,2},{4,5},{5,4},{6,7},{7,6},{8,9},{9,8},{10,11... | collective-permute-start | bytes 3848 | tf_op jit(solution)/shard_map/ppermute | solution.py:294

commit v9 on v8

--- a/solution.py
+++ b/solution.py
@@ -27,11 +27,22 @@
     return parts[2:3] * (4.0 * span) + parts[0:1] * 256.0 + parts[1:2]
 
 
+def unit_rows(rows, out):
+    values = rows[...].astype(jnp.float32)
+    scale = lax.rsqrt(jnp.sum(values * values, axis=1, keepdims=True) + EPSILON)
+    out[0 : rows.shape[0], :] = (values * scale).astype(jnp.bfloat16)
+
+
+def give_parts(block, outs):
+    top = 0
+    for out in outs:
+        out[...] = block[top : top + out.shape[0], :]
+        top += out.shape[0]
+
+
 def prepare_kernel(span, embeddings, named, block, *parts_out):
     rows, width = embeddings.shape
-    values = embeddings[...].astype(jnp.float32)
-    scale = lax.rsqrt(jnp.sum(values * values, axis=1, keepdims=True) + EPSILON)
-    block[0:rows, :] = (values * scale).astype(jnp.bfloat16)
+    unit_rows(embeddings, block)
     names = named[...].reshape(1, rows)
     keys = names & (span - 1)
     parts = [keys >> 8, keys & 255, names >> (span.bit_length() - 1)]
@@ -39,23 +50,28 @@
     parts = jnp.concatenate(parts + [jnp.zeros((EXTRA - 3, rows), jnp.float32)], axis=0)
     parts = jnp.concatenate([parts, jnp.zeros((EXTRA, width - rows), jnp.float32)], axis=1)
     block[rows : rows + EXTRA, :] = parts.astype(jnp.bfloat16)
-    top = 0
-    for out in parts_out:
-        out[...] = block[top : top + out.shape[0], :]
-        top += out.shape[0]
-
-
-def prepare(embeddings, named, span, heights=()):
-    rows, width = embeddings.shape
+    codes_out, *parts_out = parts_out
+    codes_out[0:EXTRA, :] = block[rows : rows + EXTRA, :]
+    give_parts(block, parts_out)
+
+
+def complete_kernel(rows_of, named, block, *parts_out):
+    unit_rows(rows_of, block)
+    block[rows_of.shape[0] :, :] = named[0:EXTRA, :]
+    give_parts(block, parts_out)
+
+
+def with_units(kernel, rows_of, named, heights=()):
+    rows, width = rows_of.shape
     return pl.pallas_call(
-        functools.partial(prepare_kernel, span),
+        kernel,
         out_shape=[
             jax.ShapeDtypeStruct((height, width), jnp.bfloat16)
             for height in (rows + EXTRA, *heights)
         ],
         compiler_params=pltpu.CompilerParams(vmem_limit_bytes=16 << 20),
         cost_estimate=pl.CostEstimate(flops=rows, bytes_accessed=rows, transcendentals=0),
-    )(embeddings, named)
+    )(rows_of, named)
 
 
 def row_from_partial(partial, rows):
@@ -104,6 +120,8 @@
 def assemble(whole, top, end, pieces):
     for piece in pieces:
         height = min(piece.shape[0], end - top)
+        if height == 0:
+            break
         whole[top : top + height, :] = piece[0:height, :]
         top += height
 
@@ -239,19 +257,21 @@
         span = 256
         while span < rows * groups * members:
             span *= 2
-        heights = (rows // 5 * 4, rows // 5 + EXTRA)
+        heights = (rows - 16, 16 + EXTRA)
         named = (cluster[:, 0] + 1) * span + order_key
         partner = lax.ppermute(embeddings, BOTH, other_core)
         raw = [lax.ppermute(embeddings, BOTH, pairs) for pairs in rounds]
-        block, *parts = prepare(embeddings, named, span, heights)
+        block, codes_of, *parts = with_units(
+            functools.partial(prepare_kernel, span), embeddings, named, (EXTRA,) + heights
+        )
         own = [block]
         from_first = [lax.ppermute(part, BOTH, first) for part in parts]
         from_second = [lax.ppermute(block, BOTH, second)]
-        (partner,) = prepare(partner, lax.ppermute(named, BOTH, other_core), span)
+        (partner,) = with_units(complete_kernel, partner, lax.ppermute(codes_of, BOTH, other_core))
         near_other = [[lax.ppermute(partner, BOTH, pairs)] for pairs in rounds]
         from_corner = [lax.ppermute(part, BOTH, second) for part in from_first]
         near = [
-            prepare(rows_of, lax.ppermute(named, BOTH, pairs), span, heights)
+            with_units(complete_kernel, rows_of, lax.ppermute(codes_of, BOTH, pairs), (rows, EXTRA))
             for rows_of, pairs in zip(raw, rounds)
         ]
         pieces = [lax.ppermute(piece, BOTH, other_core) for piece in near[0][1:]]

time: 55.5 us -> 48.9 us (0.88)
  starting transfers between devices: 27.1 us -> 22.5 us
  waiting for transfers between devices: 18.1 us -> 16.1 us
    ppermute x2, waiting for transfers between devices: 8.19 us -> 2.61 us  [the longest x1 2.61 us: shards(): lax.ppermute(codes_of, BOTH, pairs)]
    ppermute x1, waiting for transfers between devices: 1.01 us -> 4.04 us  [shards(): lax.ppermute(kept[:, 2 * at * rows:2 * (at + 1) * rows], BOTH, back(pairs))]
    ppermute x2, starting transfers between devices: 4.19 us -> 1.81 us  [shards(): from_corner = [lax.ppermute(part, BOTH, second) for part in from_first]]
    ppermute x1, starting transfers between devices: 3.75 us -> 1.91 us  [shards(): lax.ppermute(kept[:, 2 * at * rows:2 * (at + 1) * rows], BOTH, back(pairs))]
    ppermute x1, starting transfers between devices: 1.52 us -> 0.33 us  [shards(): results.append(lax.ppermute(onward, BOTH, second))]
    ppermute x2, starting transfers between devices: 3.05 us -> 4.01 us  [shards(): from_first = [lax.ppermute(part, BOTH, first) for part in parts]]
    ppermute x1, waiting for transfers between devices: 0.18 us -> 1.13 us  [shards(): lax.ppermute(found[:, rows:], BOTH, other_core)]
    ppermute x1, waiting for transfers between devices: 0.69 us -> 0.01 us  [shards(): results.append(lax.ppermute(onward, BOTH, second))]
  transfers between devices with their start and end apart: 18 -> 18, of which waited for: 9 -> 7; matrix products, arithmetic and copies ran while one was open for 2% -> 2% of each run, Pallas kernels for 11% -> 12%
where the time goes in v9:
time: 48.9 us; the launch traced here: 48.6 us
  starting transfers between devices  22.5 us (46%)
  waiting for transfers between devices  16.1 us (33%)
  Pallas kernels  7.18 us (15%)
  other arithmetic  1.54 us (3%)
  local copies, waits for them, and re-layouts  1.1 us (2%)
    pallas_call x5, Pallas kernels, meeting(): pl.pallas_call(functools.partial(meet_kernel, rows, span, [len(kind) for...  6.64 us
    ppermute x1, starting transfers between devices, shards(): raw = [lax.ppermute(embeddings, BOTH, pairs) for pairs in rounds]  6.07 us
    ppermute x2, waiting for transfers between devices, shards(): from_first = [lax.ppermute(part, BOTH, first) for part in parts]  5.25 us
    ppermute x1, waiting for transfers between devices, shards(): lax.ppermute(kept[:, 2 * at * rows:2 * (at + 1) * rows], BOTH, back(pairs))  4.04 us
    ppermute x2, starting transfers between devices, shards(): from_first = [lax.ppermute(part, BOTH, first) for part in parts]  4.01 us
    ppermute x1, waiting for transfers between devices, shards(): lax.ppermute(codes_of, BOTH, pairs)  2.61 us
    ppermute x2, waiting for transfers between devices, shards(): from_corner = [lax.ppermute(part, BOTH, second) for part in from_first]  2.26 us
    ppermute x1, starting transfers between devices, shards(): from_x = lax.ppermute(bests[1], BOTH, first)  2.07 us
  transfers between devices with their start and end apart: 18, of which 7 were waited for; matrix products, arithmetic and copies ran while one was open for 2% of the time, Pallas kernels for 12%

profile of v9, /device:TPU:0, one launch (start us, length us, event | category | flops | bytes accessed | tf_op | source)
XLA Modules:
  0.0 48.6 jit_solution(8993981807685507362)
XLA Ops:
  0.0 6.1 %collective-permute-start.3 = (bf16[320,768]{1,0:T(8,128)(2,1)}, bf16[320,768]{1,0:T(8,128)(2,1)S(1)}, u32[]{:S(2)}, u32[]{:S(2)}) collective-permute-start(bf16[320,768]{1,0:T(8,128)(2,1)} %embeddings.1), channel_id=1, source_target_pairs={{0,4},{6,2},{2,0},{1,7},{7,5},{5,3},{8,12},{14,10},{10,8},{9,15},{... | collective-permute-start | bytes 1474568 | tf_op jit(solution)/shard_map/ppermute | solution.py:263
  6.1 0.7 %collective-permute-start = (bf16[320,768]{1,0:T(8,128)(2,1)}, bf16[320,768]{1,0:T(8,128)(2,1)S(1)}, u32[]{:S(2)}, u32[]{:S(2)}) collective-permute-start(bf16[320,768]{1,0:T(8,128)(2,1)} %embeddings.1), channel_id=1, source_target_pairs={{0,1},{1,0},{2,3},{3,2},{4,5},{5,4},{6,7},{7,6},{8,9},{9,8},{10,11... | collective-permute-start | bytes 1474568 | tf_op jit(solution)/shard_map/ppermute | solution.py:262
  6.7 0.7 %multiply_reduce_fusion = s32[320]{0:T(512)S(1)} fusion(s32[320,1]{0,1:T(1,128)} %param.4), kind=kLoop, calls=%fused_computation.8 | loop fusion | flops 640 | bytes 2560 | tf_op jit(solution)/shard_map/mul | solution.py:261
  7.5 1.0 %copy-done = bf16[320,768]{1,0:T(8,128)(2,1)S(1)} copy-done((bf16[320,768]{1,0:T(8,128)(2,1)S(1)}, bf16[320,768]{1,0:T(8,128)(2,1)}, u32[]{:S(2)}) %copy-start) | copy-done | bytes 491544
  8.7 1.6 %collective-permute-start.7 = (bf16[304,768]{1,0:T(8,128)(2,1)S(1)}, bf16[304,768]{1,0:T(8,128)(2,1)S(1)}, u32[]{:S(2)}, u32[]{:S(2)}) collective-permute-start(bf16[304,768]{1,0:T(8,128)(2,1)S(1)} %get-tuple-element.43), channel_id=1, source_target_pairs={{0,8},{1,17},{2,10},{3,19},{4,12},{5,21},{6,14},{7,23},{8,0},{9,25... | collective-permute-start | bytes 1400840 | tf_op jit(solution)/shard_map/ppermute | solution.py:268
  10.2 1.5 %collective-permute-start.9 = (bf16[336,768]{1,0:T(8,128)(2,1)S(1)}, bf16[336,768]{1,0:T(8,128)(2,1)S(1)}, u32[]{:S(2)}, u32[]{:S(2)}) collective-permute-start(bf16[336,768]{1,0:T(8,128)(2,1)S(1)} %get-tuple-element.42.refs_0_.refs_2_.refs_3_.refs_1_), channel_id=1, source_target_pairs={{0,16},{1,9},{2,18},{3,11},{4,20},{5,13},{6,22},{7,15},{8,24},{9,1... | collective-permute-start | bytes 1548296 | tf_op jit(solution)/shard_map/ppermute | solution.py:269
  11.8 1.9 %collective-permute-start.4 = (bf16[16,768]{1,0:T(8,128)(2,1)S(1)}, bf16[16,768]{1,0:T(8,128)(2,1)S(1)}, u32[]{:S(2)}, u32[]{:S(2)}) collective-permute-start(bf16[16,768]{1,0:T(8,128)(2,1)S(1)} %get-tuple-element.39), channel_id=1, source_target_pairs={{0,4},{6,2},{2,0},{1,7},{7,5},{5,3},{8,12},{14,10},{10,8},{9,15},{... | collective-permute-start | bytes 73736 | tf_op jit(solution)/shard_map/ppermute | solution.py:274
  13.9 1.9 %collective-permute-start.2 = (bf16[336,768]{1,0:T(8,128)(2,1)S(1)}, bf16[336,768]{1,0:T(8,128)(2,1)S(1)}, u32[]{:S(2)}, u32[]{:S(2)}) collective-permute-start(bf16[336,768]{1,0:T(8,128)(2,1)S(1)} %shard_map.38.refs_0_.refs_2_), channel_id=1, source_target_pairs={{0,4},{6,2},{2,0},{1,7},{7,5},{5,3},{8,12},{14,10},{10,8},{9,15},{... | collective-permute-start | bytes 1548296 | tf_op jit(solution)/shard_map/ppermute | solution.py:271
  15.8 2.6 %collective-permute-done.4.named = bf16[16,768]{1,0:T(8,128)(2,1)S(1)} collective-permute-done((bf16[16,768]{1,0:T(8,128)(2,1)S(1)}, bf16[16,768]{1,0:T(8,128)(2,1)S(1)}, u32[]{:S(2)}, u32[]{:S(2)}) %collective-permute-start.4) | collective-permute-done | bytes 24608 | tf_op jit(solution)/shard_map/ppermute | solution.py:274
  18.7 2.6 %collective-permute-done.7.refs_3_.refs_4_.refs_2_ = bf16[304,768]{1,0:T(8,128)(2,1)S(1)} collective-permute-done((bf16[304,768]{1,0:T(8,128)(2,1)S(1)}, bf16[304,768]{1,0:T(8,128)(2,1)S(1)}, u32[]{:S(2)}, u32[]{:S(2)}) %collective-permute-start.7) | collective-permute-done | bytes 466976 | tf_op jit(solution)/shard_map/ppermute | solution.py:268
  21.3 1.5 %collective-permute-start.10 = (bf16[304,768]{1,0:T(8,128)(2,1)S(1)}, bf16[304,768]{1,0:T(8,128)(2,1)S(1)}, u32[]{:S(2)}, u32[]{:S(2)}) collective-permute-start(bf16[304,768]{1,0:T(8,128)(2,1)S(1)} %collective-permute-done.7.refs_3_.refs_4_.refs_2_), channel_id=1, source_target_pairs={{0,16},{1,9},{2,18},{3,11},{4,20},{5,13},{6,22},{7,15},{8,24},{9,1... | collective-permute-start | bytes 1400840 | tf_op jit(solution)/shard_map/ppermute | solution.py:272
  22.8 2.5 %collective-permute-start.8 = (bf16[32,768]{1,0:T(8,128)(2,1)S(1)}, bf16[32,768]{1,0:T(8,128)(2,1)S(1)}, u32[]{:S(2)}, u32[]{:S(2)}) collective-permute-start(bf16[32,768]{1,0:T(8,128)(2,1)S(1)} %get-tuple-element.44), channel_id=1, source_target_pairs={{0,8},{1,17},{2,10},{3,19},{4,12},{5,21},{6,14},{7,23},{8,0},{9,25... | collective-permute-start | bytes 147464 | tf_op jit(solution)/shard_map/ppermute | solution.py:268
  25.2 2.7 %collective-permute-done.8.refs_4_.refs_5_.refs_3_ = bf16[32,768]{1,0:T(8,128)(2,1)S(1)} collective-permute-done((bf16[32,768]{1,0:T(8,128)(2,1)S(1)}, bf16[32,768]{1,0:T(8,128)(2,1)S(1)}, u32[]{:S(2)}, u32[]{:S(2)}) %collective-permute-start.8) | collective-permute-done | bytes 49184 | tf_op jit(solution)/shard_map/ppermute | solution.py:268
  28.2 1.5 %shard_map.40 = (f32[1,320]{1,0:T(1,128)S(1)}, f32[1,320]{1,0:T(1,128)S(1)}, f32[1,320]{1,0:T(1,128)S(1)}, f32[1,320]{1,0:T(1,128)S(1)}, f32[1,320]{1,0:T(1,128)S(1)}) custom-call(bf16[336,768]{1,0:T(8,128)(2,1)S(1)} %get-tuple-element.42.refs_0_.refs_2_.refs_3_.refs_1_, bf16[336,768]{1,0:T(8,128)(2,1)S(1)} %get-tuple-element.45.refs_1_, ...), custom_call_target="tpu_custom_call" | custom-call | flops 320 | bytes 320 | tf_op jit(solution)/shard_map/pallas_call | solution.py:196
  29.7 2.3 %collective-permute-done.11.refs_6_ = bf16[32,768]{1,0:T(8,128)(2,1)S(1)} collective-permute-done((bf16[32,768]{1,0:T(8,128)(2,1)S(1)}, bf16[32,768]{1,0:T(8,128)(2,1)S(1)}, u32[]{:S(2)}, u32[]{:S(2)}) %collective-permute-start.11) | collective-permute-done | bytes 49184 | tf_op jit(solution)/shard_map/ppermute | solution.py:272
  32.0 1.4 %shard_map.42 = (f32[1,320]{1,0:T(1,128)S(1)}, f32[1,320]{1,0:T(1,128)S(1)}, f32[1,320]{1,0:T(1,128)S(1)}, f32[1,320]{1,0:T(1,128)S(1)}) custom-call(bf16[336,768]{1,0:T(8,128)(2,1)S(1)} %get-tuple-element.42.refs_0_.refs_2_.refs_3_.refs_1_, bf16[336,768]{1,0:T(8,128)(2,1)S(1)} %get-tuple-element.45.refs_1_, bf16[336,768]{1,0:T(8,128)(2,1)S(1)} %shard_map.38.refs_0_.refs_2_, ...), custom_call_target="tpu_custom_call" | custom-call | flops 320 | bytes 320 | tf_op jit(solution)/shard_map/pallas_call | solution.py:196
  33.4 1.5 %shard_map.41 = (f32[1,320]{1,0:T(1,128)S(1)}, f32[1,320]{1,0:T(1,128)S(1)}, f32[1,320]{1,0:T(1,128)S(1)}, f32[1,320]{1,0:T(1,128)S(1)}) custom-call(bf16[336,768]{1,0:T(8,128)(2,1)S(1)} %shard_map.38.refs_0_.refs_2_, bf16[320,768]{1,0:T(8,128)(2,1)S(1)} %collective-permute-done.5.refs_1_.refs_3_, ...), custom_call_target="tpu_custom_call" | custom-call | flops 320 | bytes 320 | tf_op jit(solution)/shard_map/pallas_call | solution.py:196
  35.1 1.1 %shard_map.43 = (f32[1,320]{1,0:T(1,128)S(1)}, f32[1,320]{1,0:T(1,128)S(1)}, f32[1,320]{1,0:T(1,128)S(1)}, f32[1,320]{1,0:T(1,128)S(1)}, f32[1,320]{1,0:T(1,128)S(1)}) custom-call(bf16[336,768]{1,0:T(8,128)(2,1)S(1)} %collective-permute-done.2.refs_0_, bf16[336,768]{1,0:T(8,128)(2,1)S(1)} %get-tuple-element.42.refs_0_.refs_2_.refs_3_.refs_1_, ...), custom_call_target="tpu_custom_call" | custom-call | flops 320 | bytes 320 | tf_op jit(solution)/shard_map/pallas_call | solution.py:196
  36.2 0.7 %collective-permute-done.12.refs_0_ = bf16[336,768]{1,0:T(8,128)(2,1)S(1)} collective-permute-done((bf16[336,768]{1,0:T(8,128)(2,1)S(1)}, bf16[336,768]{1,0:T(8,128)(2,1)S(1)}, u32[]{:S(2)}, u32[]{:S(2)}) %collective-permute-start.12) | collective-permute-done | bytes 516128 | tf_op jit(solution)/shard_map/ppermute | solution.py:299
  36.9 1.1 %shard_map.44 = (f32[1,320]{1,0:T(1,128)S(1)}, f32[1,640]{1,0:T(1,128)S(1)}, f32[1,320]{1,0:T(1,128)S(1)}, f32[1,320]{1,0:T(1,128)S(1)}) custom-call(bf16[336,768]{1,0:T(8,128)(2,1)S(1)} %collective-permute-done.12.refs_0_, bf16[336,768]{1,0:T(8,128)(2,1)S(1)} %get-tuple-element.42.refs_0_.refs_2_.refs_3_.refs_1_, ...), custom_call_target="tpu_custom_call" | custom-call | flops 320 | bytes 320 | tf_op jit(solution)/shard_map/pallas_call | solution.py:196
  38.2 2.1 %collective-permute-start.16 = (f32[1,640]{1,0:T(1,128)S(1)}, f32[1,640]{1,0:T(1,128)S(1)}, u32[]{:S(2)}, u32[]{:S(2)}) collective-permute-start(f32[1,640]{1,0:T(1,128)S(1)} %get-tuple-element.71), channel_id=1, source_target_pairs={{0,8},{1,17},{2,10},{3,19},{4,12},{5,21},{6,14},{7,23},{8,0},{9,25... | collective-permute-start | bytes 7688 | tf_op jit(solution)/shard_map/ppermute | solution.py:315
  40.4 1.9 %collective-permute-start.14 = (f32[1,640]{1,0:T(1,128)S(1)}, f32[1,640]{1,0:T(1,128)S(1)}, u32[]{:S(2)}, u32[]{:S(2)}) collective-permute-start(f32[1,640]{1,0:T(1,128)S(1)} %maximum_maximum_fusion), channel_id=1, source_target_pairs={{4,0},{2,6},{0,2},{7,1},{5,7},{3,5},{12,8},{10,14},{8,10},{15,9},{... | collective-permute-start | bytes 7688 | tf_op jit(solution)/shard_map/ppermute | solution.py:310
  42.7 4.0 %collective-permute-done.14 = f32[1,640]{1,0:T(1,128)S(1)} collective-permute-done((f32[1,640]{1,0:T(1,128)S(1)}, f32[1,640]{1,0:T(1,128)S(1)}, u32[]{:S(2)}, u32[]{:S(2)}) %collective-permute-start.14) | collective-permute-done | bytes 2592 | tf_op jit(solution)/shard_map/ppermute | solution.py:310
  46.9 1.1 %collective-permute-done.15 = f32[1,320]{1,0:T(1,128)S(1)} collective-permute-done((f32[1,320]{1,0:T(1,128)S(1)}, f32[1,320]{1,0:T(1,128)S(1)}, u32[]{:S(2)}, u32[]{:S(2)}) %collective-permute-start.15) | collective-permute-done | bytes 1312 | tf_op jit(solution)/shard_map/ppermute | solution.py:314
  (34 shorter events, 2.4 us)
Async XLA Ops:
  0.0 7.4 %copy-start.1 = (s32[320]{0:T(512)S(1)}, s32[320]{0:T(512)}, u32[]{:S(2)}) copy-start(s32[320]{0:T(512)} %param.5) | copy-start | bytes 3844
  0.0 18.4 %collective-permute-start.3 = (bf16[320,768]{1,0:T(8,128)(2,1)}, bf16[320,768]{1,0:T(8,128)(2,1)S(1)}, u32[]{:S(2)}, u32[]{:S(2)}) collective-permute-start(bf16[320,768]{1,0:T(8,128)(2,1)} %embeddings.1), channel_id=1, source_target_pairs={{0,4},{6,2},{2,0},{1,7},{7,5},{5,3},{8,12},{14,10},{10,8},{9,15},{... | collective-permute-start | bytes 1474568 | tf_op jit(solution)/shard_map/ppermute | solution.py:263
  6.1 7.6 %collective-permute-start = (bf16[320,768]{1,0:T(8,128)(2,1)}, bf16[320,768]{1,0:T(8,128)(2,1)S(1)}, u32[]{:S(2)}, u32[]{:S(2)}) collective-permute-start(bf16[320,768]{1,0:T(8,128)(2,1)} %embeddings.1), channel_id=1, source_target_pairs={{0,1},{1,0},{2,3},{3,2},{4,5},{5,4},{6,7},{7,6},{8,9},{9,8},{10,11... | collective-permute-start | bytes 1474568 | tf_op jit(solution)/shard_map/ppermute | solution.py:262
  7.5 1.0 %copy-start = (bf16[320,768]{1,0:T(8,128)(2,1)S(1)}, bf16[320,768]{1,0:T(8,128)(2,1)}, u32[]{:S(2)}) copy-start(bf16[320,768]{1,0:T(8,128)(2,1)} %embeddings.1) | copy-start | bytes 1474564
  8.7 12.6 %collective-permute-start.7 = (bf16[304,768]{1,0:T(8,128)(2,1)S(1)}, bf16[304,768]{1,0:T(8,128)(2,1)S(1)}, u32[]{:S(2)}, u32[]{:S(2)}) collective-permute-start(bf16[304,768]{1,0:T(8,128)(2,1)S(1)} %get-tuple-element.43), channel_id=1, source_target_pairs={{0,8},{1,17},{2,10},{3,19},{4,12},{5,21},{6,14},{7,23},{8,0},{9,25... | collective-permute-start | bytes 1400840 | tf_op jit(solution)/shard_map/ppermute | solution.py:268
  10.2 1.5 %collective-permute-start.1 = (bf16[16,768]{1,0:T(8,128)(2,1)S(1)}, bf16[16,768]{1,0:T(8,128)(2,1)S(1)}, u32[]{:S(2)}, u32[]{:S(2)}) collective-permute-start(bf16[16,768]{1,0:T(8,128)(2,1)S(1)} %get-tuple-element.39), channel_id=1, source_target_pairs={{0,1},{1,0},{2,3},{3,2},{4,5},{5,4},{6,7},{7,6},{8,9},{9,8},{10,11... | collective-permute-start | bytes 73736 | tf_op jit(solution)/shard_map/ppermute | solution.py:270
  10.2 18.0 %collective-permute-start.9 = (bf16[336,768]{1,0:T(8,128)(2,1)S(1)}, bf16[336,768]{1,0:T(8,128)(2,1)S(1)}, u32[]{:S(2)}, u32[]{:S(2)}) collective-permute-start(bf16[336,768]{1,0:T(8,128)(2,1)S(1)} %get-tuple-element.42.refs_0_.refs_2_.refs_3_.refs_1_), channel_id=1, source_target_pairs={{0,16},{1,9},{2,18},{3,11},{4,20},{5,13},{6,22},{7,15},{8,24},{9,1... | collective-permute-start | bytes 1548296 | tf_op jit(solution)/shard_map/ppermute | solution.py:269
  11.8 6.7 %collective-permute-start.4 = (bf16[16,768]{1,0:T(8,128)(2,1)S(1)}, bf16[16,768]{1,0:T(8,128)(2,1)S(1)}, u32[]{:S(2)}, u32[]{:S(2)}) collective-permute-start(bf16[16,768]{1,0:T(8,128)(2,1)S(1)} %get-tuple-element.39), channel_id=1, source_target_pairs={{0,4},{6,2},{2,0},{1,7},{7,5},{5,3},{8,12},{14,10},{10,8},{9,15},{... | collective-permute-start | bytes 73736 | tf_op jit(solution)/shard_map/ppermute | solution.py:274
  13.9 21.1 %collective-permute-start.2 = (bf16[336,768]{1,0:T(8,128)(2,1)S(1)}, bf16[336,768]{1,0:T(8,128)(2,1)S(1)}, u32[]{:S(2)}, u32[]{:S(2)}) collective-permute-start(bf16[336,768]{1,0:T(8,128)(2,1)S(1)} %shard_map.38.refs_0_.refs_2_), channel_id=1, source_target_pairs={{0,4},{6,2},{2,0},{1,7},{7,5},{5,3},{8,12},{14,10},{10,8},{9,15},{... | collective-permute-start | bytes 1548296 | tf_op jit(solution)/shard_map/ppermute | solution.py:271
  18.6 13.4 %collective-permute-start.5 = (bf16[320,768]{1,0:T(8,128)(2,1)S(1)}, bf16[320,768]{1,0:T(8,128)(2,1)S(1)}, u32[]{:S(2)}, u32[]{:S(2)}) collective-permute-start(bf16[320,768]{1,0:T(8,128)(2,1)S(1)} %get-tuple-element.40), channel_id=1, source_target_pairs={{0,1},{1,0},{2,3},{3,2},{4,5},{5,4},{6,7},{7,6},{8,9},{9,8},{10,11... | collective-permute-start | bytes 1474568 | tf_op jit(solution)/shard_map/ppermute | solution.py:277
  21.3 10.7 %collective-permute-start.10 = (bf16[304,768]{1,0:T(8,128)(2,1)S(1)}, bf16[304,768]{1,0:T(8,128)(2,1)S(1)}, u32[]{:S(2)}, u32[]{:S(2)}) collective-permute-start(bf16[304,768]{1,0:T(8,128)(2,1)S(1)} %collective-permute-done.7.refs_3_.refs_4_.refs_2_), channel_id=1, source_target_pairs={{0,16},{1,9},{2,18},{3,11},{4,20},{5,13},{6,22},{7,15},{8,24},{9,1... | collective-permute-start | bytes 1400840 | tf_op jit(solution)/shard_map/ppermute | solution.py:272
  22.8 5.1 %collective-permute-start.8 = (bf16[32,768]{1,0:T(8,128)(2,1)S(1)}, bf16[32,768]{1,0:T(8,128)(2,1)S(1)}, u32[]{:S(2)}, u32[]{:S(2)}) collective-permute-start(bf16[32,768]{1,0:T(8,128)(2,1)S(1)} %get-tuple-element.44), channel_id=1, source_target_pairs={{0,8},{1,17},{2,10},{3,19},{4,12},{5,21},{6,14},{7,23},{8,0},{9,25... | collective-permute-start | bytes 147464 | tf_op jit(solution)/shard_map/ppermute | solution.py:268
  27.9 4.1 %collective-permute-start.11 = (bf16[32,768]{1,0:T(8,128)(2,1)S(1)}, bf16[32,768]{1,0:T(8,128)(2,1)S(1)}, u32[]{:S(2)}, u32[]{:S(2)}) collective-permute-start(bf16[32,768]{1,0:T(8,128)(2,1)S(1)} %collective-permute-done.8.refs_4_.refs_5_.refs_3_), channel_id=1, source_target_pairs={{0,16},{1,9},{2,18},{3,11},{4,20},{5,13},{6,22},{7,15},{8,24},{9,1... | collective-permute-start | bytes 147464 | tf_op jit(solution)/shard_map/ppermute | solution.py:272
  28.2 3.8 %collective-permute-start.6 = (bf16[16,768]{1,0:T(8,128)(2,1)S(1)}, bf16[16,768]{1,0:T(8,128)(2,1)S(1)}, u32[]{:S(2)}, u32[]{:S(2)}) collective-permute-start(bf16[16,768]{1,0:T(8,128)(2,1)S(1)} %get-tuple-element.41), channel_id=1, source_target_pairs={{0,1},{1,0},{2,3},{3,2},{4,5},{5,4},{6,7},{7,6},{8,9},{9,8},{10,11... | collective-permute-start | bytes 73736 | tf_op jit(solution)/shard_map/ppermute | solution.py:277
  34.9 2.0 %collective-permute-start.12 = (bf16[336,768]{1,0:T(8,128)(2,1)S(1)}, bf16[336,768]{1,0:T(8,128)(2,1)S(1)}, u32[]{:S(2)}, u32[]{:S(2)}) collective-permute-start(bf16[336,768]{1,0:T(8,128)(2,1)S(1)} %collective-permute-done.2.refs_0_), channel_id=1, source_target_pairs={{0,1},{1,0},{2,3},{3,2},{4,5},{5,4},{6,7},{7,6},{8,9},{9,8},{10,11... | collective-permute-start | bytes 1548296 | tf_op jit(solution)/shard_map/ppermute | solution.py:299
  38.1 2.2 %collective-permute-start.13 = (f32[1,640]{1,0:T(1,128)S(1)}, f32[1,640]{1,0:T(1,128)S(1)}, u32[]{:S(2)}, u32[]{:S(2)}) collective-permute-start(f32[1,640]{1,0:T(1,128)S(1)} %pad_maximum_fusion), channel_id=1, source_target_pairs={{0,1},{1,0},{2,3},{3,2},{4,5},{5,4},{6,7},{7,6},{8,9},{9,8},{10,11... | collective-permute-start | bytes 7688 | tf_op jit(solution)/shard_map/ppermute | solution.py:307
  38.2 4.1 %collective-permute-start.16 = (f32[1,640]{1,0:T(1,128)S(1)}, f32[1,640]{1,0:T(1,128)S(1)}, u32[]{:S(2)}, u32[]{:S(2)}) collective-permute-start(f32[1,640]{1,0:T(1,128)S(1)} %get-tuple-element.71), channel_id=1, source_target_pairs={{0,8},{1,17},{2,10},{3,19},{4,12},{5,21},{6,14},{7,23},{8,0},{9,25... | collective-permute-start | bytes 7688 | tf_op jit(solution)/shard_map/ppermute | solution.py:315
  40.4 6.4 %collective-permute-start.14 = (f32[1,640]{1,0:T(1,128)S(1)}, f32[1,640]{1,0:T(1,128)S(1)}, u32[]{:S(2)}, u32[]{:S(2)}) collective-permute-start(f32[1,640]{1,0:T(1,128)S(1)} %maximum_maximum_fusion), channel_id=1, source_target_pairs={{4,0},{2,6},{0,2},{7,1},{5,7},{3,5},{12,8},{10,14},{8,10},{15,9},{... | collective-permute-start | bytes 7688 | tf_op jit(solution)/shard_map/ppermute | solution.py:310
  42.4 4.5 %collective-permute-start.17 = (f32[1,320]{1,0:T(1,128)S(1)}, f32[1,320]{1,0:T(1,128)S(1)}, u32[]{:S(2)}, u32[]{:S(2)}) collective-permute-start(f32[1,320]{1,0:T(1,128)S(1)} %slice_maximum_fusion), channel_id=1, source_target_pairs={{0,16},{1,9},{2,18},{3,11},{4,20},{5,13},{6,22},{7,15},{8,24},{9,1... | collective-permute-start | bytes 3848 | tf_op jit(solution)/shard_map/ppermute | solution.py:318
  46.8 1.2 %collective-permute-start.15 = (f32[1,320]{1,0:T(1,128)S(1)}, f32[1,320]{1,0:T(1,128)S(1)}, u32[]{:S(2)}, u32[]{:S(2)}) collective-permute-start(f32[1,320]{1,0:T(1,128)S(1)} %slice.17), channel_id=1, source_target_pairs={{0,1},{1,0},{2,3},{3,2},{4,5},{5,4},{6,7},{7,6},{8,9},{9,8},{10,11... | collective-permute-start | bytes 3848 | tf_op jit(solution)/shard_map/ppermute | solution.py:314

commit v10 on v9

--- a/solution.py
+++ b/solution.py
@@ -257,19 +257,22 @@
         span = 256
         while span < rows * groups * members:
             span *= 2
-        heights = (rows - 16, 16 + EXTRA)
+        halves = rows // 2
         named = (cluster[:, 0] + 1) * span + order_key
         partner = lax.ppermute(embeddings, BOTH, other_core)
         raw = [lax.ppermute(embeddings, BOTH, pairs) for pairs in rounds]
-        block, codes_of, *parts = with_units(
-            functools.partial(prepare_kernel, span), embeddings, named, (EXTRA,) + heights
+        block, codes_of = with_units(
+            functools.partial(prepare_kernel, span), embeddings, named, (EXTRA,)
         )
         own = [block]
-        from_first = [lax.ppermute(part, BOTH, first) for part in parts]
+        from_first = [lax.ppermute(block, BOTH, first)]
         from_second = [lax.ppermute(block, BOTH, second)]
         (partner,) = with_units(complete_kernel, partner, lax.ppermute(codes_of, BOTH, other_core))
         near_other = [[lax.ppermute(partner, BOTH, pairs)] for pairs in rounds]
-        from_corner = [lax.ppermute(part, BOTH, second) for part in from_first]
+        from_corner = [
+            lax.ppermute(part, BOTH, second)
+            for part in (from_first[0][:halves], from_first[0][halves:])
+        ]
         near = [
             with_units(complete_kernel, rows_of, lax.ppermute(codes_of, BOTH, pairs), (rows, EXTRA))
             for rows_of, pairs in zip(raw, rounds)
@@ -286,6 +289,8 @@
         bests, (other,), _ = meeting(
             [[partner], pieces], [HELD, TWO], held[:3], bests, rows, span
         )
+        *from_corner, bests = lax.optimization_barrier((*from_corner, bests))
+        held[3] = from_corner
         corner_best, (mine, one_more, other_more), _ = meeting(
             [own, near[0], [partner], pieces], [OWN, TWO, HELD, TWO], held[3:], [], rows, span
         )

time: 48.9 us -> 45.9 us (0.939)
  waiting for transfers between devices: 16.1 us -> 13.2 us
    ppermute x4 -> x3, starting transfers between devices: 5.82 us -> 3.71 us  [the longest x2 2.16 us: shards(): lax.ppermute(part, BOTH, second)]
    ppermute x1, waiting for transfers between devices: 4.04 us -> 2.34 us  [shards(): lax.ppermute(kept[:, 2 * at * rows:2 * (at + 1) * rows], BOTH, back(pairs))]
    ppermute x1, starting transfers between devices: 0.33 us -> 1.98 us  [shards(): results.append(lax.ppermute(onward, BOTH, second))]
    ppermute x4 -> x3, waiting for transfers between devices: 7.51 us -> 6.02 us  [the longest x2 3.88 us: shards(): lax.ppermute(part, BOTH, second)]
    ppermute x1, starting transfers between devices: 0.01 us -> 0.88 us  [shards(): lax.ppermute(codes_of, BOTH, other_core)]
    ppermute x1, starting transfers between devices: 1.52 us -> 0.65 us  [shards(): from_second = [lax.ppermute(block, BOTH, second)]]
    ppermute x2, starting transfers between devices: 0.07 us -> 0.84 us  [shards(): pieces = [lax.ppermute(piece, BOTH, other_core) for piece in near[0][1:]]]
  transfers between devices with their start and end apart: 18 -> 17, of which waited for: 7 -> 7; matrix products, arithmetic and copies ran while one was open for 2% -> 2% of each run, Pallas kernels for 12% -> 13%
where the time goes in v10:
time: 45.9 us; the launch traced here: 45.6 us
  starting transfers between devices  22.3 us (49%)
  waiting for transfers between devices  13.2 us (29%)
  Pallas kernels  7.17 us (16%)
  other arithmetic  1.54 us (3%)
  local copies, waits for them, and re-layouts  1.14 us (2%)
    pallas_call x5, Pallas kernels, meeting(): pl.pallas_call(functools.partial(meet_kernel, rows, span, [len(kind) for...  6.63 us
    ppermute x1, starting transfers between devices, shards(): raw = [lax.ppermute(embeddings, BOTH, pairs) for pairs in rounds]  5.62 us
    ppermute x2, waiting for transfers between devices, shards(): lax.ppermute(part, BOTH, second)  3.88 us
    ppermute x1, waiting for transfers between devices, shards(): lax.ppermute(codes_of, BOTH, pairs)  2.74 us
    ppermute x1, waiting for transfers between devices, shards(): lax.ppermute(kept[:, 2 * at * rows:2 * (at + 1) * rows], BOTH, back(pairs))  2.34 us
    ppermute x1, starting transfers between devices, shards(): from_x = lax.ppermute(bests[1], BOTH, first)  2.19 us
    ppermute x2, starting transfers between devices, shards(): lax.ppermute(part, BOTH, second)  2.16 us
    ppermute x1, waiting for transfers between devices, shards(): from_first = [lax.ppermute(block, BOTH, first)]  2.14 us
  transfers between devices with their start and end apart: 17, of which 7 were waited for; matrix products, arithmetic and copies ran while one was open for 2% of the time, Pallas kernels for 13%

profile of v10, /device:TPU:0, one launch (start us, length us, event | category | flops | bytes accessed | tf_op | source)
XLA Modules:
  0.0 45.6 jit_solution(1425624465832036923)
XLA Ops:
  0.5 5.6 %collective-permute-start.6 = (bf16[320,768]{1,0:T(8,128)(2,1)}, bf16[320,768]{1,0:T(8,128)(2,1)S(1)}, u32[]{:S(2)}, u32[]{:S(2)}) collective-permute-start(bf16[320,768]{1,0:T(8,128)(2,1)} %embeddings.1), channel_id=1, source_target_pairs={{0,4},{6,2},{2,0},{1,7},{7,5},{5,3},{8,12},{14,10},{10,8},{9,15},{... | collective-permute-start | bytes 1474568 | tf_op jit(solution)/shard_map/ppermute | solution.py:263
  6.1 0.7 %multiply_reduce_fusion = s32[320]{0:T(512)S(1)} fusion(s32[320,1]{0,1:T(1,128)} %param.4), kind=kLoop, calls=%fused_computation.8 | loop fusion | flops 640 | bytes 2560 | tf_op jit(solution)/shard_map/mul | solution.py:261
  6.8 1.0 %copy-done = bf16[320,768]{1,0:T(8,128)(2,1)S(1)} copy-done((bf16[320,768]{1,0:T(8,128)(2,1)S(1)}, bf16[320,768]{1,0:T(8,128)(2,1)}, u32[]{:S(2)}) %copy-start) | copy-done | bytes 491544
  8.0 1.6 %collective-permute-start.3 = (bf16[336,768]{1,0:T(8,128)(2,1)S(1)}, bf16[336,768]{1,0:T(8,128)(2,1)S(1)}, u32[]{:S(2)}, u32[]{:S(2)}) collective-permute-start(bf16[336,768]{1,0:T(8,128)(2,1)S(1)} %get-tuple-element.43.refs_0_.refs_2_.refs_3_.refs_1_), channel_id=1, source_target_pairs={{0,8},{1,17},{2,10},{3,19},{4,12},{5,21},{6,14},{7,23},{8,0},{9,25... | collective-permute-start | bytes 1548296 | tf_op jit(solution)/shard_map/ppermute | solution.py:268
  9.6 0.9 %collective-permute-start.1 = (bf16[16,768]{1,0:T(8,128)(2,1)S(1)}, bf16[16,768]{1,0:T(8,128)(2,1)S(1)}, u32[]{:S(2)}, u32[]{:S(2)}) collective-permute-start(bf16[16,768]{1,0:T(8,128)(2,1)S(1)} %get-tuple-element.42), channel_id=1, source_target_pairs={{0,1},{1,0},{2,3},{3,2},{4,5},{5,4},{6,7},{7,6},{8,9},{9,8},{10,11... | collective-permute-start | bytes 73736 | tf_op jit(solution)/shard_map/ppermute | solution.py:270
  10.5 0.6 %collective-permute-start.10 = (bf16[336,768]{1,0:T(8,128)(2,1)S(1)}, bf16[336,768]{1,0:T(8,128)(2,1)S(1)}, u32[]{:S(2)}, u32[]{:S(2)}) collective-permute-start(bf16[336,768]{1,0:T(8,128)(2,1)S(1)} %get-tuple-element.43.refs_0_.refs_2_.refs_3_.refs_1_), channel_id=1, source_target_pairs={{0,16},{1,9},{2,18},{3,11},{4,20},{5,13},{6,22},{7,15},{8,24},{9,1... | collective-permute-start | bytes 1548296 | tf_op jit(solution)/shard_map/ppermute | solution.py:269
  11.3 1.9 %collective-permute-start.7 = (bf16[16,768]{1,0:T(8,128)(2,1)S(1)}, bf16[16,768]{1,0:T(8,128)(2,1)S(1)}, u32[]{:S(2)}, u32[]{:S(2)}) collective-permute-start(bf16[16,768]{1,0:T(8,128)(2,1)S(1)} %get-tuple-element.42), channel_id=1, source_target_pairs={{0,4},{6,2},{2,0},{1,7},{7,5},{5,3},{8,12},{14,10},{10,8},{9,15},{... | collective-permute-start | bytes 73736 | tf_op jit(solution)/shard_map/ppermute | solution.py:277
  13.4 1.9 %collective-permute-start.2 = (bf16[336,768]{1,0:T(8,128)(2,1)S(1)}, bf16[336,768]{1,0:T(8,128)(2,1)S(1)}, u32[]{:S(2)}, u32[]{:S(2)}) collective-permute-start(bf16[336,768]{1,0:T(8,128)(2,1)S(1)} %shard_map.38.refs_0_.refs_2_), channel_id=1, source_target_pairs={{0,4},{6,2},{2,0},{1,7},{7,5},{5,3},{8,12},{14,10},{10,8},{9,15},{... | collective-permute-start | bytes 1548296 | tf_op jit(solution)/shard_map/ppermute | solution.py:271
  15.3 2.7 %collective-permute-done.7.named = bf16[16,768]{1,0:T(8,128)(2,1)S(1)} collective-permute-done((bf16[16,768]{1,0:T(8,128)(2,1)S(1)}, bf16[16,768]{1,0:T(8,128)(2,1)S(1)}, u32[]{:S(2)}, u32[]{:S(2)}) %collective-permute-start.7) | collective-permute-done | bytes 24608 | tf_op jit(solution)/shard_map/ppermute | solution.py:277
  18.3 0.8 %collective-permute-start.8 = (bf16[320,768]{1,0:T(8,128)(2,1)S(1)}, bf16[320,768]{1,0:T(8,128)(2,1)S(1)}, u32[]{:S(2)}, u32[]{:S(2)}) collective-permute-start(bf16[320,768]{1,0:T(8,128)(2,1)S(1)} %get-tuple-element.44), channel_id=1, source_target_pairs={{0,1},{1,0},{2,3},{3,2},{4,5},{5,4},{6,7},{7,6},{8,9},{9,8},{10,11... | collective-permute-start | bytes 1474568 | tf_op jit(solution)/shard_map/ppermute | solution.py:280
  19.1 2.1 %collective-permute-done.3.refs_3_.refs_4_.refs_2_ = bf16[336,768]{1,0:T(8,128)(2,1)S(1)} collective-permute-done((bf16[336,768]{1,0:T(8,128)(2,1)S(1)}, bf16[336,768]{1,0:T(8,128)(2,1)S(1)}, u32[]{:S(2)}, u32[]{:S(2)}) %collective-permute-start.3) | collective-permute-done | bytes 516128 | tf_op jit(solution)/shard_map/ppermute | solution.py:268
  21.3 2.0 %collective-permute-start.5 = (bf16[176,768]{1,0:T(8,128)(2,1)S(1)}, bf16[176,768]{1,0:T(8,128)(2,1)S(1)}, u32[]{:S(2)}, u32[]{:S(2)}) collective-permute-start(bf16[176,768]{1,0:T(8,128)(2,1)S(1)} %slice.25), channel_id=1, source_target_pairs={{0,16},{1,9},{2,18},{3,11},{4,20},{5,13},{6,22},{7,15},{8,24},{9,1... | collective-permute-start | bytes 811016 | tf_op jit(solution)/shard_map/ppermute | solution.py:273
  23.5 1.5 %shard_map.40 = (f32[1,320]{1,0:T(1,128)S(1)}, f32[1,320]{1,0:T(1,128)S(1)}, f32[1,320]{1,0:T(1,128)S(1)}, f32[1,320]{1,0:T(1,128)S(1)}, f32[1,320]{1,0:T(1,128)S(1)}) custom-call(bf16[336,768]{1,0:T(8,128)(2,1)S(1)} %get-tuple-element.43.refs_0_.refs_2_.refs_3_.refs_1_, bf16[336,768]{1,0:T(8,128)(2,1)S(1)} %get-tuple-element.46.refs_1_, ...), custom_call_target="tpu_custom_call" | custom-call | flops 320 | bytes 320 | tf_op jit(solution)/shard_map/pallas_call | solution.py:196
  25.0 1.5 %shard_map.41 = (f32[1,320]{1,0:T(1,128)S(1)}, f32[1,320]{1,0:T(1,128)S(1)}, f32[1,320]{1,0:T(1,128)S(1)}, f32[1,320]{1,0:T(1,128)S(1)}) custom-call(bf16[336,768]{1,0:T(8,128)(2,1)S(1)} %shard_map.38.refs_0_.refs_2_, bf16[320,768]{1,0:T(8,128)(2,1)S(1)} %collective-permute-done.8.refs_1_.refs_3_, ...), custom_call_target="tpu_custom_call" | custom-call | flops 320 | bytes 320 | tf_op jit(solution)/shard_map/pallas_call | solution.py:196
  26.6 3.9 %collective-permute-done.4.refs_5_.refs_4_ = bf16[160,768]{1,0:T(8,128)(2,1)S(1)} collective-permute-done((bf16[160,768]{1,0:T(8,128)(2,1)S(1)}, bf16[160,768]{1,0:T(8,128)(2,1)S(1)}, u32[]{:S(2)}, u32[]{:S(2)}) %collective-permute-start.4) | collective-permute-done | bytes 245792 | tf_op jit(solution)/shard_map/ppermute | solution.py:273
  30.4 1.4 %shard_map.42 = (f32[1,320]{1,0:T(1,128)S(1)}, f32[1,320]{1,0:T(1,128)S(1)}, f32[1,320]{1,0:T(1,128)S(1)}, f32[1,320]{1,0:T(1,128)S(1)}) custom-call(bf16[336,768]{1,0:T(8,128)(2,1)S(1)} %get-tuple-element.43.refs_0_.refs_2_.refs_3_.refs_1_, bf16[336,768]{1,0:T(8,128)(2,1)S(1)} %get-tuple-element.46.refs_1_, bf16[336,768]{1,0:T(8,128)(2,1)S(1)} %shard_map.38.refs_0_.refs_2_, ...), custom_call_target="tpu_custom_call" | custom-call | flops 320 | bytes 320 | tf_op jit(solution)/shard_map/pallas_call | solution.py:196
  32.0 1.1 %shard_map.43 = (f32[1,320]{1,0:T(1,128)S(1)}, f32[1,320]{1,0:T(1,128)S(1)}, f32[1,320]{1,0:T(1,128)S(1)}, f32[1,320]{1,0:T(1,128)S(1)}, f32[1,320]{1,0:T(1,128)S(1)}) custom-call(bf16[336,768]{1,0:T(8,128)(2,1)S(1)} %collective-permute-done.2.refs_0_, bf16[336,768]{1,0:T(8,128)(2,1)S(1)} %get-tuple-element.43.refs_0_.refs_2_.refs_3_.refs_1_, ...), custom_call_target="tpu_custom_call" | custom-call | flops 320 | bytes 320 | tf_op jit(solution)/shard_map/pallas_call | solution.py:196
  33.0 0.7 %collective-permute-done.11.refs_0_ = bf16[336,768]{1,0:T(8,128)(2,1)S(1)} collective-permute-done((bf16[336,768]{1,0:T(8,128)(2,1)S(1)}, bf16[336,768]{1,0:T(8,128)(2,1)S(1)}, u32[]{:S(2)}, u32[]{:S(2)}) %collective-permute-start.11) | collective-permute-done | bytes 516128 | tf_op jit(solution)/shard_map/ppermute | solution.py:304
  33.8 1.1 %shard_map.44 = (f32[1,320]{1,0:T(1,128)S(1)}, f32[1,640]{1,0:T(1,128)S(1)}, f32[1,320]{1,0:T(1,128)S(1)}, f32[1,320]{1,0:T(1,128)S(1)}) custom-call(bf16[336,768]{1,0:T(8,128)(2,1)S(1)} %collective-permute-done.11.refs_0_, bf16[336,768]{1,0:T(8,128)(2,1)S(1)} %get-tuple-element.43.refs_0_.refs_2_.refs_3_.refs_1_, ...), custom_call_target="tpu_custom_call" | custom-call | flops 320 | bytes 320 | tf_op jit(solution)/shard_map/pallas_call | solution.py:196
  35.1 2.2 %collective-permute-start.15 = (f32[1,640]{1,0:T(1,128)S(1)}, f32[1,640]{1,0:T(1,128)S(1)}, u32[]{:S(2)}, u32[]{:S(2)}) collective-permute-start(f32[1,640]{1,0:T(1,128)S(1)} %get-tuple-element.77), channel_id=1, source_target_pairs={{0,8},{1,17},{2,10},{3,19},{4,12},{5,21},{6,14},{7,23},{8,0},{9,25... | collective-permute-start | bytes 7688 | tf_op jit(solution)/shard_map/ppermute | solution.py:320
  37.4 2.0 %collective-permute-start.13 = (f32[1,640]{1,0:T(1,128)S(1)}, f32[1,640]{1,0:T(1,128)S(1)}, u32[]{:S(2)}, u32[]{:S(2)}) collective-permute-start(f32[1,640]{1,0:T(1,128)S(1)} %maximum_maximum_fusion), channel_id=1, source_target_pairs={{4,0},{2,6},{0,2},{7,1},{5,7},{3,5},{12,8},{10,14},{8,10},{15,9},{... | collective-permute-start | bytes 7688 | tf_op jit(solution)/shard_map/ppermute | solution.py:315
  39.5 2.0 %collective-permute-start.16 = (f32[1,320]{1,0:T(1,128)S(1)}, f32[1,320]{1,0:T(1,128)S(1)}, u32[]{:S(2)}, u32[]{:S(2)}) collective-permute-start(f32[1,320]{1,0:T(1,128)S(1)} %slice_maximum_fusion), channel_id=1, source_target_pairs={{0,16},{1,9},{2,18},{3,11},{4,20},{5,13},{6,22},{7,15},{8,24},{9,1... | collective-permute-start | bytes 3848 | tf_op jit(solution)/shard_map/ppermute | solution.py:323
  41.4 2.3 %collective-permute-done.13 = f32[1,640]{1,0:T(1,128)S(1)} collective-permute-done((f32[1,640]{1,0:T(1,128)S(1)}, f32[1,640]{1,0:T(1,128)S(1)}, u32[]{:S(2)}, u32[]{:S(2)}) %collective-permute-start.13) | collective-permute-done | bytes 2592 | tf_op jit(solution)/shard_map/ppermute | solution.py:315
  43.9 1.1 %collective-permute-done.14 = f32[1,320]{1,0:T(1,128)S(1)} collective-permute-done((f32[1,320]{1,0:T(1,128)S(1)}, f32[1,320]{1,0:T(1,128)S(1)}, u32[]{:S(2)}, u32[]{:S(2)}) %collective-permute-start.14) | collective-permute-done | bytes 1312 | tf_op jit(solution)/shard_map/ppermute | solution.py:319
  (34 shorter events, 2.6 us)
Async XLA Ops:
  0.0 6.8 %copy-start.1 = (s32[320]{0:T(512)S(1)}, s32[320]{0:T(512)}, u32[]{:S(2)}) copy-start(s32[320]{0:T(512)} %param.5) | copy-start | bytes 3844
  0.0 13.2 %collective-permute-start = (bf16[320,768]{1,0:T(8,128)(2,1)}, bf16[320,768]{1,0:T(8,128)(2,1)S(1)}, u32[]{:S(2)}, u32[]{:S(2)}) collective-permute-start(bf16[320,768]{1,0:T(8,128)(2,1)} %embeddings.1), channel_id=1, source_target_pairs={{0,1},{1,0},{2,3},{3,2},{4,5},{5,4},{6,7},{7,6},{8,9},{9,8},{10,11... | collective-permute-start | bytes 1474568 | tf_op jit(solution)/shard_map/ppermute | solution.py:262
  0.5 17.6 %collective-permute-start.6 = (bf16[320,768]{1,0:T(8,128)(2,1)}, bf16[320,768]{1,0:T(8,128)(2,1)S(1)}, u32[]{:S(2)}, u32[]{:S(2)}) collective-permute-start(bf16[320,768]{1,0:T(8,128)(2,1)} %embeddings.1), channel_id=1, source_target_pairs={{0,4},{6,2},{2,0},{1,7},{7,5},{5,3},{8,12},{14,10},{10,8},{9,15},{... | collective-permute-start | bytes 1474568 | tf_op jit(solution)/shard_map/ppermute | solution.py:263
  6.8 1.0 %copy-start = (bf16[320,768]{1,0:T(8,128)(2,1)S(1)}, bf16[320,768]{1,0:T(8,128)(2,1)}, u32[]{:S(2)}) copy-start(bf16[320,768]{1,0:T(8,128)(2,1)} %embeddings.1) | copy-start | bytes 1474564
  8.0 13.2 %collective-permute-start.3 = (bf16[336,768]{1,0:T(8,128)(2,1)S(1)}, bf16[336,768]{1,0:T(8,128)(2,1)S(1)}, u32[]{:S(2)}, u32[]{:S(2)}) collective-permute-start(bf16[336,768]{1,0:T(8,128)(2,1)S(1)} %get-tuple-element.43.refs_0_.refs_2_.refs_3_.refs_1_), channel_id=1, source_target_pairs={{0,8},{1,17},{2,10},{3,19},{4,12},{5,21},{6,14},{7,23},{8,0},{9,25... | collective-permute-start | bytes 1548296 | tf_op jit(solution)/shard_map/ppermute | solution.py:268
  9.6 1.7 %collective-permute-start.1 = (bf16[16,768]{1,0:T(8,128)(2,1)S(1)}, bf16[16,768]{1,0:T(8,128)(2,1)S(1)}, u32[]{:S(2)}, u32[]{:S(2)}) collective-permute-start(bf16[16,768]{1,0:T(8,128)(2,1)S(1)} %get-tuple-element.42), channel_id=1, source_target_pairs={{0,1},{1,0},{2,3},{3,2},{4,5},{5,4},{6,7},{7,6},{8,9},{9,8},{10,11... | collective-permute-start | bytes 73736 | tf_op jit(solution)/shard_map/ppermute | solution.py:270
  10.5 13.0 %collective-permute-start.10 = (bf16[336,768]{1,0:T(8,128)(2,1)S(1)}, bf16[336,768]{1,0:T(8,128)(2,1)S(1)}, u32[]{:S(2)}, u32[]{:S(2)}) collective-permute-start(bf16[336,768]{1,0:T(8,128)(2,1)S(1)} %get-tuple-element.43.refs_0_.refs_2_.refs_3_.refs_1_), channel_id=1, source_target_pairs={{0,16},{1,9},{2,18},{3,11},{4,20},{5,13},{6,22},{7,15},{8,24},{9,1... | collective-permute-start | bytes 1548296 | tf_op jit(solution)/shard_map/ppermute | solution.py:269
  11.3 6.8 %collective-permute-start.7 = (bf16[16,768]{1,0:T(8,128)(2,1)S(1)}, bf16[16,768]{1,0:T(8,128)(2,1)S(1)}, u32[]{:S(2)}, u32[]{:S(2)}) collective-permute-start(bf16[16,768]{1,0:T(8,128)(2,1)S(1)} %get-tuple-element.42), channel_id=1, source_target_pairs={{0,4},{6,2},{2,0},{1,7},{7,5},{5,3},{8,12},{14,10},{10,8},{9,15},{... | collective-permute-start | bytes 73736 | tf_op jit(solution)/shard_map/ppermute | solution.py:277
  13.4 18.4 %collective-permute-start.2 = (bf16[336,768]{1,0:T(8,128)(2,1)S(1)}, bf16[336,768]{1,0:T(8,128)(2,1)S(1)}, u32[]{:S(2)}, u32[]{:S(2)}) collective-permute-start(bf16[336,768]{1,0:T(8,128)(2,1)S(1)} %shard_map.38.refs_0_.refs_2_), channel_id=1, source_target_pairs={{0,4},{6,2},{2,0},{1,7},{7,5},{5,3},{8,12},{14,10},{10,8},{9,15},{... | collective-permute-start | bytes 1548296 | tf_op jit(solution)/shard_map/ppermute | solution.py:271
  18.3 6.7 %collective-permute-start.8 = (bf16[320,768]{1,0:T(8,128)(2,1)S(1)}, bf16[320,768]{1,0:T(8,128)(2,1)S(1)}, u32[]{:S(2)}, u32[]{:S(2)}) collective-permute-start(bf16[320,768]{1,0:T(8,128)(2,1)S(1)} %get-tuple-element.44), channel_id=1, source_target_pairs={{0,1},{1,0},{2,3},{3,2},{4,5},{5,4},{6,7},{7,6},{8,9},{9,8},{10,11... | collective-permute-start | bytes 1474568 | tf_op jit(solution)/shard_map/ppermute | solution.py:280
  21.3 9.2 %collective-permute-start.5 = (bf16[176,768]{1,0:T(8,128)(2,1)S(1)}, bf16[176,768]{1,0:T(8,128)(2,1)S(1)}, u32[]{:S(2)}, u32[]{:S(2)}) collective-permute-start(bf16[176,768]{1,0:T(8,128)(2,1)S(1)} %slice.25), channel_id=1, source_target_pairs={{0,16},{1,9},{2,18},{3,11},{4,20},{5,13},{6,22},{7,15},{8,24},{9,1... | collective-permute-start | bytes 811016 | tf_op jit(solution)/shard_map/ppermute | solution.py:273
  23.3 7.1 %collective-permute-start.4 = (bf16[160,768]{1,0:T(8,128)(2,1)S(1)}, bf16[160,768]{1,0:T(8,128)(2,1)S(1)}, u32[]{:S(2)}, u32[]{:S(2)}) collective-permute-start(bf16[160,768]{1,0:T(8,128)(2,1)S(1)} %slice.24), channel_id=1, source_target_pairs={{0,16},{1,9},{2,18},{3,11},{4,20},{5,13},{6,22},{7,15},{8,24},{9,1... | collective-permute-start | bytes 737288 | tf_op jit(solution)/shard_map/ppermute | solution.py:273
  23.5 1.6 %collective-permute-start.9 = (bf16[16,768]{1,0:T(8,128)(2,1)S(1)}, bf16[16,768]{1,0:T(8,128)(2,1)S(1)}, u32[]{:S(2)}, u32[]{:S(2)}) collective-permute-start(bf16[16,768]{1,0:T(8,128)(2,1)S(1)} %get-tuple-element.45), channel_id=1, source_target_pairs={{0,1},{1,0},{2,3},{3,2},{4,5},{5,4},{6,7},{7,6},{8,9},{9,8},{10,11... | collective-permute-start | bytes 73736 | tf_op jit(solution)/shard_map/ppermute | solution.py:280
  31.8 2.0 %collective-permute-start.11 = (bf16[336,768]{1,0:T(8,128)(2,1)S(1)}, bf16[336,768]{1,0:T(8,128)(2,1)S(1)}, u32[]{:S(2)}, u32[]{:S(2)}) collective-permute-start(bf16[336,768]{1,0:T(8,128)(2,1)S(1)} %collective-permute-done.2.refs_0_), channel_id=1, source_target_pairs={{0,1},{1,0},{2,3},{3,2},{4,5},{5,4},{6,7},{7,6},{8,9},{9,8},{10,11... | collective-permute-start | bytes 1548296 | tf_op jit(solution)/shard_map/ppermute | solution.py:304
  35.0 2.3 %collective-permute-start.12 = (f32[1,640]{1,0:T(1,128)S(1)}, f32[1,640]{1,0:T(1,128)S(1)}, u32[]{:S(2)}, u32[]{:S(2)}) collective-permute-start(f32[1,640]{1,0:T(1,128)S(1)} %pad_maximum_fusion), channel_id=1, source_target_pairs={{0,1},{1,0},{2,3},{3,2},{4,5},{5,4},{6,7},{7,6},{8,9},{9,8},{10,11... | collective-permute-start | bytes 7688 | tf_op jit(solution)/shard_map/ppermute | solution.py:312
  35.1 4.2 %collective-permute-start.15 = (f32[1,640]{1,0:T(1,128)S(1)}, f32[1,640]{1,0:T(1,128)S(1)}, u32[]{:S(2)}, u32[]{:S(2)}) collective-permute-start(f32[1,640]{1,0:T(1,128)S(1)} %get-tuple-element.77), channel_id=1, source_target_pairs={{0,8},{1,17},{2,10},{3,19},{4,12},{5,21},{6,14},{7,23},{8,0},{9,25... | collective-permute-start | bytes 7688 | tf_op jit(solution)/shard_map/ppermute | solution.py:320
  37.4 6.4 %collective-permute-start.13 = (f32[1,640]{1,0:T(1,128)S(1)}, f32[1,640]{1,0:T(1,128)S(1)}, u32[]{:S(2)}, u32[]{:S(2)}) collective-permute-start(f32[1,640]{1,0:T(1,128)S(1)} %maximum_maximum_fusion), channel_id=1, source_target_pairs={{4,0},{2,6},{0,2},{7,1},{5,7},{3,5},{12,8},{10,14},{8,10},{15,9},{... | collective-permute-start | bytes 7688 | tf_op jit(solution)/shard_map/ppermute | solution.py:315
  39.5 4.4 %collective-permute-start.16 = (f32[1,320]{1,0:T(1,128)S(1)}, f32[1,320]{1,0:T(1,128)S(1)}, u32[]{:S(2)}, u32[]{:S(2)}) collective-permute-start(f32[1,320]{1,0:T(1,128)S(1)} %slice_maximum_fusion), channel_id=1, source_target_pairs={{0,16},{1,9},{2,18},{3,11},{4,20},{5,13},{6,22},{7,15},{8,24},{9,1... | collective-permute-start | bytes 3848 | tf_op jit(solution)/shard_map/ppermute | solution.py:323
  43.9 1.2 %collective-permute-start.14 = (f32[1,320]{1,0:T(1,128)S(1)}, f32[1,320]{1,0:T(1,128)S(1)}, u32[]{:S(2)}, u32[]{:S(2)}) collective-permute-start(f32[1,320]{1,0:T(1,128)S(1)} %slice.27), channel_id=1, source_target_pairs={{0,1},{1,0},{2,3},{3,2},{4,5},{5,4},{6,7},{7,6},{8,9},{9,8},{10,11... | collective-permute-start | bytes 3848 | tf_op jit(solution)/shard_map/ppermute | solution.py:319

commit v11 on v9

v11 whole, which is shorter than its diff:
```python
import functools

import jax
import jax.numpy as jnp
from jax import lax
from jax.experimental import pallas as pl
from jax.experimental.pallas import tpu as pltpu
from jax.sharding import PartitionSpec as P

EPSILON = 1e-06
EXTRA = 16
CODES = 3
LANES = 128
TILE = 256
BOTH = ("dp", "grid")


def up(value, multiple):
    return -(-value // multiple) * multiple


def turned_to_column(row, rows):
    return jnp.broadcast_to(row, (LANES, row.shape[1])).T[:rows]


def codes(block, rows, span, first=0):
    parts = block[block.shape[0] - EXTRA :, : up(rows, LANES)].astype(jnp.float32)
    parts = parts[first : first + CODES]
    return parts[2:3] * (4.0 * span) + parts[0:1] * 256.0 + parts[1:2]


def unit_rows(rows, out):
    values = rows[...].astype(jnp.float32)
    scale = lax.rsqrt(jnp.sum(values * values, axis=1, keepdims=True) + EPSILON)
    out[0 : rows.shape[0], :] = (values * scale).astype(jnp.bfloat16)


def give_parts(block, outs):
    top = 0
    for out in outs:
        out[...] = block[top : top + out.shape[0], :]
        top += out.shape[0]


def prepare_kernel(span, embeddings, named, block, *parts_out):
    rows, width = embeddings.shape
    unit_rows(embeddings, block)
    names = named[...].reshape(1, rows)
    keys = names & (span - 1)
    parts = [keys >> 8, keys & 255, names >> (span.bit_length() - 1)]
    parts = [part.astype(jnp.float32) for part in parts]
    parts = jnp.concatenate(parts + [jnp.zeros((EXTRA - 3, rows), jnp.float32)], axis=0)
    parts = jnp.concatenate([parts, jnp.zeros((EXTRA, width - rows), jnp.float32)], axis=1)
    block[rows : rows + EXTRA, :] = parts.astype(jnp.bfloat16)
    codes_out, *parts_out = parts_out
    codes_out[0:EXTRA, :] = block[rows : rows + EXTRA, :]
    give_parts(block, parts_out)


def complete_kernel(rows_of, codes_of, other_codes, block):
    rows, width = rows_of.shape
    unit_rows(rows_of, block)
    named = [part[...].astype(jnp.float32)[0:CODES] for part in (codes_of, other_codes)]
    named = jnp.concatenate(named + [jnp.zeros((EXTRA - 2 * CODES, width), jnp.float32)], axis=0)
    block[rows:, :] = named.astype(jnp.bfloat16)


def unit_kernel(rows_of, block, *parts_out):
    unit_rows(rows_of, block)
    give_parts(block, parts_out)


def with_units(kernel, heights, rows_of, *others):
    rows, width = rows_of.shape
    return pl.pallas_call(
        kernel,
        out_shape=[jax.ShapeDtypeStruct((height, width), jnp.bfloat16) for height in heights],
        compiler_params=pltpu.CompilerParams(vmem_limit_bytes=16 << 20),
        cost_estimate=pl.CostEstimate(flops=rows, bytes_accessed=rows, transcendentals=0),
    )(rows_of, *others)


def row_from_partial(partial, rows):
    padded = up(rows, LANES)
    if padded != rows:
        partial = jnp.concatenate(
            [partial, jnp.zeros((padded - rows, LANES), partial.dtype)], axis=0
        )
    return jnp.max(partial.T, axis=0, keepdims=True)[:, :rows]


def products(block, rows, held, at, tile):
    return lax.dot_general(
        block[0:rows, :],
        held[at : at + tile, :],
        (((1,), (1,)), ((), ())),
        preferred_element_type=jnp.float32,
    )


def meet(sims_of, row, rows, span, held_codes, to_block, to_held):
    column = turned_to_column(row, rows)
    partial = jnp.full((rows, LANES), -1.0, jnp.float32)
    best_held = []
    for at in range(0, held_codes.shape[1], TILE):
        tile = min(TILE, held_codes.shape[1] - at)
        sims = sims_of(at, tile)
        for lane in range(0, tile, LANES):
            part = sims[:, lane : lane + LANES]
            gap = column - held_codes[:, at + lane : at + lane + LANES]
            if to_block and to_held:
                part = jnp.where(jnp.abs(gap) < span, part, -1.0)
                later = gap > 0.0
                partial = jnp.maximum(partial, jnp.where(later, part, -1.0))
                other = jnp.where(later, -1.0, part)
            elif to_block:
                partial = jnp.maximum(
                    partial, jnp.where((gap > 0.0) & (gap < span), part, -1.0)
                )
            else:
                other = jnp.where((gap < 0.0) & (gap > -span), part, -1.0)
            if to_held:
                best_held.append(jnp.max(other, axis=0, keepdims=True))
    return (
        row_from_partial(partial, rows) if to_block else None,
        jnp.concatenate(best_held, axis=1) if to_held else None,
    )


def assemble(whole, top, end, pieces):
    for piece in pieces:
        height = min(piece.shape[0], end - top)
        if height == 0:
            break
        whole[top : top + height, :] = piece[0:height, :]
        top += height


def hold(held, holds, rows):
    for at, block in enumerate(holds):
        assemble(held, at * rows, (at + 1) * rows, block)
    rest = held.shape[0] - len(holds) * rows
    if rest:
        held[len(holds) * rows :, :] = jnp.zeros((rest, held.shape[1]), held.dtype)


def products_kernel(rows, lengths, *refs):
    *refs, out, held = refs
    block, *holds = regrouped(refs, lengths)
    hold(held, holds, rows)
    for at in range(0, held.shape[0], TILE):
        tile = min(TILE, held.shape[0] - at)
        top = 0
        for piece in block:
            height = piece.shape[0]
            out[top : top + height, at : at + tile] = products(piece, height, held, at, tile)
            top += height


def all_products(block, holds, rows):
    width = block[0].shape[1]
    total = up(len(holds) * rows, LANES)
    parts = [block, *holds]
    return pl.pallas_call(
        functools.partial(products_kernel, rows, [len(part) for part in parts]),
        out_shape=jax.ShapeDtypeStruct((rows, total), jnp.float32),
        scratch_shapes=[pltpu.VMEM((total, width), jnp.bfloat16)],
        compiler_params=pltpu.CompilerParams(vmem_limit_bytes=32 << 20),
        cost_estimate=pl.CostEstimate(flops=5 * rows * total * width // 4, bytes_accessed=rows, transcendentals=0),
    )(*[piece for part in parts for piece in part])


def meet_kernel(rows, span, sizes, modes, lengths, together, *refs):
    blocks, holds, bests, given, outs, found, scratch = regrouped(refs, sizes)
    (held,) = scratch
    holds = regrouped(holds, lengths)
    hold(held, holds, rows)
    row = [codes(block[-1], rows, span)[:, :rows] for block in holds]
    rest = held.shape[0] - len(holds) * rows
    if rest:
        row.append(jnp.zeros((1, rest), jnp.float32))
    row = jnp.concatenate(row, axis=1)
    best = None
    found = iter(found)

    def join(sims_of, own_row, to_block, to_held):
        nonlocal best
        mine, theirs = meet(sims_of, own_row, rows, span, row, to_block, to_held)
        if to_block:
            next(found)[...] = mine
        if to_held:
            best = theirs if best is None else jnp.maximum(best, theirs)

    for block, mode in zip(blocks, modes):
        join(
            lambda at, tile, block=block: products(block, rows, held, at, tile),
            codes(block, rows, span),
            *mode,
        )
    for sims, block in zip(given, blocks):
        join(
            lambda at, tile, sims=sims: sims[:, at : at + tile],
            codes(block, rows, span, first=CODES),
            *TWO,
        )
    parts = [best[:, at * rows : (at + 1) * rows] for at in range(len(holds))]
    if bests:
        parts = [jnp.maximum(part, earlier[...]) for part, earlier in zip(parts, bests)]
    for out, places in zip(outs, together):
        if len(places) == 1:
            out[...] = parts[places[0]]
        else:
            out[...] = jnp.concatenate([parts[place] for place in places], axis=1)


def regrouped(flat, lengths):
    flat = iter(flat)
    return [[next(flat) for _ in range(length)] for length in lengths]


def meeting(blocks, modes, holds, bests, rows, span, given=(), together=None):
    width = blocks[0].shape[1]
    together = together or [(at,) for at in range(len(holds))]
    flat = [piece for block in holds for piece in block]
    outs = [jax.ShapeDtypeStruct((1, rows * len(some)), jnp.float32) for some in together]
    count = sum(mode[0] for mode in modes) + len(given)
    found = [jax.ShapeDtypeStruct((1, rows), jnp.float32)] * count
    scratch = [pltpu.VMEM((up(len(holds) * rows, LANES), width), jnp.bfloat16)]
    kinds = [blocks, flat, bests, given, outs, found, scratch]
    results = pl.pallas_call(
        functools.partial(
            meet_kernel,
            rows,
            span,
            [len(kind) for kind in kinds],
            modes,
            [len(block) for block in holds],
            together,
        ),
        out_shape=outs + found,
        scratch_shapes=scratch,
        compiler_params=pltpu.CompilerParams(vmem_limit_bytes=32 << 20),
        cost_estimate=pl.CostEstimate(flops=rows, bytes_accessed=rows, transcendentals=0),
    )(*blocks, *flat, *bests, *given)
    return regrouped(results, [len(outs), len(found)])


OWN = (True, False)
HELD = (False, True)
TWO = (True, True)


def line_rounds(chips):
    if chips == 4:
        return [[(0, 2), (3, 1), (1, 0)], [(0, 3), (3, 2), (2, 1)]]
    rounds = []
    for shift in range(1, chips // 2 + 1):
        senders = chips // 2 if 2 * shift == chips else chips
        rounds.append([(s, (s + shift) % chips) for s in range(senders)])
    return rounds


def solution(mesh):
    groups, members = mesh.shape["dp"], mesh.shape["grid"]
    assert groups == 4 and members % 2 == 0
    chips = members // 2

    def everywhere(target):
        return [
            (p * members + g, a * members + b)
            for p in range(groups)
            for g in range(members)
            for a, b in [target(p, g)]
        ]

    other_core = everywhere(lambda p, g: (p, g ^ 1))
    first = everywhere(lambda p, g: (p ^ (1 + g % 2), g))
    second = everywhere(lambda p, g: (p ^ (2 - g % 2), g))

    rounds = line_rounds(chips)
    rounds += [[]] * (len(rounds) % 2)
    rounds = [
        [
            (p * members + 2 * s + c, p * members + 2 * t + c)
            for p in range(groups)
            for c in range(2)
            for s, t in rounds[at + c]
        ]
        for at in range(0, len(rounds), 2)
    ]

    def back(pairs):
        return [(target, source) for source, target in pairs]

    def shards(embeddings, cluster, order_key):
        rows = embeddings.shape[0]
        span = 256
        while span < rows * groups * members:
            span *= 2
        halves = (rows // 2, rows // 2 + EXTRA)
        uneven = (rows // 2 + EXTRA, rows // 2 - EXTRA)
        named = (cluster[:, 0] + 1) * span + order_key
        partner = lax.ppermute(embeddings, BOTH, other_core)
        raw = [lax.ppermute(embeddings, BOTH, pairs) for pairs in rounds]
        block, codes_of, *parts = with_units(
            functools.partial(prepare_kernel, span),
            (rows + EXTRA, EXTRA, *halves),
            embeddings,
            named,
        )
        own = [block]
        from_first = [lax.ppermute(part, BOTH, first) for part in parts]
        from_second = [lax.ppermute(block, BOTH, second)]
        other_codes = lax.ppermute(codes_of, BOTH, other_core)
        (partner,) = with_units(complete_kernel, (rows + EXTRA,), partner, other_codes, codes_of)
        near_other = [lax.ppermute(partner, BOTH, pairs) for pairs in rounds]
        from_corner = [lax.ppermute(part, BOTH, second) for part in from_first]
        near = [with_units(unit_kernel, (rows, *uneven), rows_of) for rows_of in raw]
        far = [[lax.ppermute(piece, BOTH, other_core) for piece in blocks[1:]] for blocks in near]

        results, kept, sent = [], [], []
        bests, found = meeting(
            [block, partner], [OWN, HELD], [own, from_first, from_second], [], rows, span
        )
        results += found
        *from_corner, bests = lax.optimization_barrier((*from_corner, bests))
        corner_best, found = meeting([block, partner], [OWN, HELD], [from_corner], [], rows, span)
        results += found
        bests += corner_best
        held = [own, from_first, from_second, from_corner]
        for at, one in enumerate(near_other):
            sims_near = all_products(near[at][:1], held, rows)
            *far[at], sims_near = lax.optimization_barrier((*far[at], sims_near))
            sims_far = all_products(far[at], held, rows)
            one, bests, sims_near, sims_far = lax.optimization_barrier(
                (one, bests, sims_near, sims_far)
            )
            far_other = lax.ppermute(one, BOTH, other_core)
            bests, found = meeting([one], [TWO], held, bests, rows, span, given=[sims_near])
            kept += found
            last = at == len(rounds) - 1
            bests, found = meeting(
                [far_other],
                [TWO],
                held,
                bests,
                rows,
                span,
                given=[sims_far],
                together=[(0,), (1, 3), (2,)] if last else None,
            )
            sent += found
        sent = lax.ppermute(jnp.concatenate(sent, axis=1), BOTH, other_core)
        kept = jnp.maximum(jnp.concatenate(kept, axis=1), sent)
        for at, pairs in enumerate(rounds):
            found = lax.ppermute(kept[:, 2 * at * rows : 2 * (at + 1) * rows], BOTH, back(pairs))
            me = lax.axis_index(BOTH)
            sender = functools.reduce(jnp.logical_or, [me == source for source, _ in pairs])
            found = jnp.where(sender, found, -1.0)
            results += [found[:, rows:], lax.ppermute(found[:, :rows], BOTH, other_core)]
        from_x = lax.ppermute(bests[1], BOTH, first)
        results.append(from_x[:, :rows])
        onward = jnp.maximum(bests[2], from_x[:, rows:])
        results.append(lax.ppermute(onward, BOTH, second))
        return functools.reduce(jnp.maximum, results, bests[0]).reshape(rows)

    placed = (P(BOTH, None), P(BOTH, None), P(BOTH))
    return jax.shard_map(
        shards, mesh=mesh, in_specs=placed, out_specs=P(BOTH), check_vma=False
    )
```

time: 48.9 us -> 52.4 us (1.072)
  starting transfers between devices: 22.5 us -> 18.5 us
  Pallas kernels: 7.18 us -> 10.1 us
  local copies, waits for them, and re-layouts: 1.1 us -> 3.41 us
  waiting for transfers between devices: 16.1 us -> 17.5 us
  other arithmetic: 1.54 us -> 2.28 us
    ppermute x2, waiting for transfers between devices: 5.25 us -> 8.33 us  [shards(): from_first = [lax.ppermute(part, BOTH, first) for part in parts]]
    ppermute x7 -> x6, waiting for transfers between devices: 4.49 us -> 1.99 us  [the longest x1 1.13 us: shards(): lax.ppermute(found[:, :rows], BOTH, other_core)]
    unnamed x4 -> x10, local copies, waits for them, and re-layouts: 1.03 us -> 3.4 us
    pallas_call x0 -> x2, Pallas kernels: none -> 2.25 us  [all_products(): pl.pallas_call(functools.partial(products_kernel, rows, [len(part) for pa...]
    ppermute x2, starting transfers between devices: 4.01 us -> 2.03 us  [shards(): from_first = [lax.ppermute(part, BOTH, first) for part in parts]]
    ppermute x2, waiting for transfers between devices: 2.26 us -> 3.36 us  [shards(): from_corner = [lax.ppermute(part, BOTH, second) for part in from_first]]
    ppermute x7 -> x6, starting transfers between devices: 3.98 us -> 3.26 us  [the longest x1 1.92 us: shards(): near_other = [lax.ppermute(partner, BOTH, pairs) for pairs in rounds]]
    ppermute x2, starting transfers between devices: 1.81 us -> 1.1 us  [shards(): from_corner = [lax.ppermute(part, BOTH, second) for part in from_first]]
  transfers between devices with their start and end apart: 18 -> 17, of which waited for: 7 -> 6; matrix products, arithmetic and copies ran while one was open for 2% -> 3% of each run, Pallas kernels for 12% -> 14%
where the time goes in v11:
time: 52.4 us; the launch traced here: 51.9 us
  starting transfers between devices  18.5 us (35%)
  waiting for transfers between devices  17.5 us (33%)
  Pallas kernels  10.1 us (19%)
  local copies, waits for them, and re-layouts  3.41 us (7%)
  other arithmetic  2.28 us (4%)
    ppermute x2, waiting for transfers between devices, shards(): from_first = [lax.ppermute(part, BOTH, first) for part in parts]  8.33 us
    pallas_call x4, Pallas kernels, meeting(): pl.pallas_call(functools.partial(meet_kernel, rows, span, [len(kind) for...  7.26 us
    ppermute x1, starting transfers between devices, shards(): raw = [lax.ppermute(embeddings, BOTH, pairs) for pairs in rounds]  5.49 us
    ppermute x1, waiting for transfers between devices, shards(): lax.ppermute(kept[:, 2 * at * rows:2 * (at + 1) * rows], BOTH, back(pairs))  3.78 us
    unnamed x10, local copies, waits for them, and re-layouts  3.4 us
    ppermute x2, waiting for transfers between devices, shards(): from_corner = [lax.ppermute(part, BOTH, second) for part in from_first]  3.36 us
    pallas_call x2, Pallas kernels, all_products(): pl.pallas_call(functools.partial(products_kernel, rows, [len(part) for pa...  2.25 us
    ppermute x2, starting transfers between devices, shards(): from_first = [lax.ppermute(part, BOTH, first) for part in parts]  2.03 us
  transfers between devices with their start and end apart: 17, of which 6 were waited for; matrix products, arithmetic and copies ran while one was open for 3% of the time, Pallas kernels for 14%

profile of v11, /device:TPU:0, one launch (start us, length us, event | category | flops | bytes accessed | tf_op | source)
XLA Modules:
  0.0 51.9 jit_solution(7711547732606164578)
XLA Ops:
  0.5 5.5 %collective-permute-start.8 = (bf16[320,768]{1,0:T(8,128)(2,1)}, bf16[320,768]{1,0:T(8,128)(2,1)S(1)}, u32[]{:S(2)}, u32[]{:S(2)}) collective-permute-start(bf16[320,768]{1,0:T(8,128)(2,1)} %embeddings.1), channel_id=1, source_target_pairs={{0,4},{6,2},{2,0},{1,7},{7,5},{5,3},{8,12},{14,10},{10,8},{9,15},{... | collective-permute-start | bytes 1474568 | tf_op jit(solution)/shard_map/ppermute | solution.py:304
  5.9 0.7 %multiply_reduce_fusion = s32[320]{0:T(512)S(1)} fusion(s32[320,1]{0,1:T(1,128)} %param.4), kind=kLoop, calls=%fused_computation.8 | loop fusion | flops 640 | bytes 2560 | tf_op jit(solution)/shard_map/mul | solution.py:302
  6.6 0.7 %add.15.named = s32[320]{0:T(512)S(1)} add(s32[320]{0:T(512)S(1)} %multiply_reduce_fusion, s32[320]{0:T(512)} %param.5) | non-fusion elementwise | flops 320 | bytes 3840 | tf_op jit(solution)/shard_map/add | solution.py:302
  7.3 1.0 %copy-done.4 = bf16[320,768]{1,0:T(8,128)(2,1)S(1)} copy-done((bf16[320,768]{1,0:T(8,128)(2,1)S(1)}, bf16[320,768]{1,0:T(8,128)(2,1)}, u32[]{:S(2)}) %copy-start.4) | copy-done | bytes 491544
  8.5 1.6 %collective-permute-start.7 = (bf16[336,768]{1,0:T(8,128)(2,1)S(1)}, bf16[336,768]{1,0:T(8,128)(2,1)S(1)}, u32[]{:S(2)}, u32[]{:S(2)}) collective-permute-start(bf16[336,768]{1,0:T(8,128)(2,1)S(1)} %get-tuple-element.47.refs_0_.refs_2_.refs_1_), channel_id=1, source_target_pairs={{0,16},{1,9},{2,18},{3,11},{4,20},{5,13},{6,22},{7,15},{8,24},{9,1... | collective-permute-start | bytes 1548296 | tf_op jit(solution)/shard_map/ppermute | solution.py:313
  10.1 1.5 %collective-permute-start.5 = (bf16[176,768]{1,0:T(8,128)(2,1)S(1)}, bf16[176,768]{1,0:T(8,128)(2,1)S(1)}, u32[]{:S(2)}, u32[]{:S(2)}) collective-permute-start(bf16[176,768]{1,0:T(8,128)(2,1)S(1)} %get-tuple-element.46), channel_id=1, source_target_pairs={{0,8},{1,17},{2,10},{3,19},{4,12},{5,21},{6,14},{7,23},{8,0},{9,25... | collective-permute-start | bytes 811016 | tf_op jit(solution)/shard_map/ppermute | solution.py:312
  11.6 0.7 %collective-permute-start.1 = (bf16[16,768]{1,0:T(8,128)(2,1)S(1)}, bf16[16,768]{1,0:T(8,128)(2,1)S(1)}, u32[]{:S(2)}, u32[]{:S(2)}) collective-permute-start(bf16[16,768]{1,0:T(8,128)(2,1)S(1)} %get-tuple-element.44.other_codes), channel_id=1, source_target_pairs={{0,1},{1,0},{2,3},{3,2},{4,5},{5,4},{6,7},{7,6},{8,9},{9,8},{10,11... | collective-permute-start | bytes 73736 | tf_op jit(solution)/shard_map/ppermute | solution.py:314
  12.3 0.8 %collective-permute-done.1.codes_of = bf16[16,768]{1,0:T(8,128)(2,1)S(1)} collective-permute-done((bf16[16,768]{1,0:T(8,128)(2,1)S(1)}, bf16[16,768]{1,0:T(8,128)(2,1)S(1)}, u32[]{:S(2)}, u32[]{:S(2)}) %collective-permute-start.1) | collective-permute-done | bytes 24608 | tf_op jit(solution)/shard_map/ppermute | solution.py:314
  13.9 1.9 %collective-permute-start.2 = (bf16[336,768]{1,0:T(8,128)(2,1)S(1)}, bf16[336,768]{1,0:T(8,128)(2,1)}, u32[]{:S(2)}, u32[]{:S(2)}) collective-permute-start(bf16[336,768]{1,0:T(8,128)(2,1)S(1)} %shard_map.38.refs_1_), channel_id=1, source_target_pairs={{0,4},{6,2},{2,0},{1,7},{7,5},{5,3},{8,12},{14,10},{10,8},{9,15},{... | collective-permute-start | bytes 1548296 | tf_op jit(solution)/shard_map/ppermute | solution.py:316
  15.8 3.7 %collective-permute-done.5.refs_4_.refs_3_ = bf16[176,768]{1,0:T(8,128)(2,1)S(1)} collective-permute-done((bf16[176,768]{1,0:T(8,128)(2,1)S(1)}, bf16[176,768]{1,0:T(8,128)(2,1)S(1)}, u32[]{:S(2)}, u32[]{:S(2)}) %collective-permute-start.5) | collective-permute-done | bytes 270368 | tf_op jit(solution)/shard_map/ppermute | solution.py:312
  20.0 4.6 %collective-permute-done.3.refs_3_.refs_2_ = bf16[160,768]{1,0:T(8,128)(2,1)S(1)} collective-permute-done((bf16[160,768]{1,0:T(8,128)(2,1)S(1)}, bf16[160,768]{1,0:T(8,128)(2,1)S(1)}, u32[]{:S(2)}, u32[]{:S(2)}) %collective-permute-start.3) | collective-permute-done | bytes 245792 | tf_op jit(solution)/shard_map/ppermute | solution.py:312
  26.0 1.4 %shard_map.39 = (f32[1,320]{1,0:T(1,128)S(1)}, f32[1,320]{1,0:T(1,128)S(1)}, f32[1,320]{1,0:T(1,128)S(1)}, f32[1,320]{1,0:T(1,128)S(1)}) custom-call(bf16[336,768]{1,0:T(8,128)(2,1)S(1)} %get-tuple-element.47.refs_0_.refs_2_.refs_1_, bf16[336,768]{1,0:T(8,128)(2,1)S(1)} %shard_map.38.refs_1_, bf16[336,768]{1,0:T(8,128)(2,1)S(1)} %get-tuple-element.47.refs_0_.refs_2_.refs_1_, ...), custom_call_target="tpu_custom_call" | custom-call | flops 320 | bytes 320 | tf_op jit(solution)/shard_map/pallas_call | solution.py:230
  27.5 3.4 %collective-permute-done.4.refs_2_.refs_5_.refs_6_ = bf16[160,768]{1,0:T(8,128)(2,1)S(1)} collective-permute-done((bf16[160,768]{1,0:T(8,128)(2,1)S(1)}, bf16[160,768]{1,0:T(8,128)(2,1)S(1)}, u32[]{:S(2)}, u32[]{:S(2)}) %collective-permute-start.4) | collective-permute-done | bytes 245792 | tf_op jit(solution)/shard_map/ppermute | solution.py:317
  30.8 0.7 %shard_map.40 = (f32[1,320]{1,0:T(1,128)S(1)}, f32[1,320]{1,0:T(1,128)S(1)}) custom-call(bf16[336,768]{1,0:T(8,128)(2,1)S(1)} %get-tuple-element.47.refs_0_.refs_2_.refs_1_, bf16[336,768]{1,0:T(8,128)(2,1)S(1)} %shard_map.38.refs_1_, bf16[160,768]{1,0:T(8,128)(2,1)S(1)} %collective-permute-done.4.refs_2_.refs_5_.refs_6_, ...), custom_call_target="tpu_custom_call" | custom-call | flops 320 | bytes 320 | tf_op jit(solution)/shard_map/pallas_call | solution.py:230
  31.5 0.8 %shard_map.42.refs_11_ = f32[320,1280]{1,0:T(8,128)S(1)} custom-call(bf16[320,768]{1,0:T(8,128)(2,1)S(1)} %get-tuple-element.59.refs_0_, bf16[336,768]{1,0:T(8,128)(2,1)S(1)} %get-tuple-element.47.refs_0_.refs_2_.refs_1_, bf16[160,768]{1,0:T(8,128)(2,1)S(1)} %collective-permute-done.3.refs_3_.refs_2_, ...), custom_call_target="tpu_custom_call" | custom-call | flops 393216000 | bytes 320 | tf_op jit(solution)/shard_map/pallas_call | solution.py:164
  32.4 1.4 %shard_map.43.refs_11_ = f32[320,1280]{1,0:T(8,128)S(1)} custom-call(bf16[176,768]{1,0:T(8,128)(2,1)S(1)} %collective-permute-done.9.refs_0_, bf16[144,768]{1,0:T(8,128)(2,1)S(1)} %collective-permute-done.10.refs_1_, bf16[336,768]{1,0:T(8,128)(2,1)S(1)} %get-tuple-element.47.refs_0_.refs_2_.refs_1_, ...), custom_call_target="tpu_custom_call" | custom-call | flops 393216000 | bytes 320 | tf_op jit(solution)/shard_map/pallas_call | solution.py:164
  34.0 1.4 %copy-done.1 = f32[320,1280]{1,0:T(8,128)S(1)} copy-done((f32[320,1280]{1,0:T(8,128)S(1)}, f32[320,1280]{1,0:T(8,128)}, u32[]{:S(2)}) %copy-start.1) | copy-done | bytes 1638424
  35.4 0.9 %copy-done.3 = bf16[160,768]{1,0:T(8,128)(2,1)S(1)} copy-done((bf16[160,768]{1,0:T(8,128)(2,1)S(1)}, bf16[160,768]{1,0:T(8,128)(2,1)}, u32[]{:S(2)}) %copy-start.3) | copy-done | bytes 245784
  36.4 2.6 %shard_map.44 = (f32[1,320]{1,0:T(1,128)S(1)}, f32[1,320]{1,0:T(1,128)S(1)}, f32[1,320]{1,0:T(1,128)S(1)}, f32[1,320]{1,0:T(1,128)S(1)}, f32[1,320]{1,0:T(1,128)S(1)}, /*index=5*/f32[1,320]{1,0:T(1,128)S(1)}) custom-call(bf16[336,768]{1,0:T(8,128)(2,1)} %collective-permute-done.2.refs_0_, bf16[336,768]{1,0:T(8,128)(2,1)S(1)} %get-tuple-element.47.refs_0_.refs_2_.refs_1_, ...), custom_call_target="tpu_custom_call" | custom-call | flops 320 | bytes 320 | tf_op jit(solution)/shard_map/pallas_call | solution.py:230
  38.9 2.6 %shard_map.45 = (f32[1,320]{1,0:T(1,128)S(1)}, f32[1,640]{1,0:T(1,128)S(1)}, f32[1,320]{1,0:T(1,128)S(1)}, f32[1,320]{1,0:T(1,128)S(1)}, f32[1,320]{1,0:T(1,128)S(1)}) custom-call(bf16[336,768]{1,0:T(8,128)(2,1)} %collective-permute-done.11.refs_0_, bf16[336,768]{1,0:T(8,128)(2,1)S(1)} %get-tuple-element.47.refs_0_.refs_2_.refs_1_, ...), custom_call_target="tpu_custom_call" | custom-call | flops 320 | bytes 320 | tf_op jit(solution)/shard_map/pallas_call | solution.py:230
  42.0 1.6 %collective-permute-start.15 = (f32[1,640]{1,0:T(1,128)S(1)}, f32[1,640]{1,0:T(1,128)S(1)}, u32[]{:S(2)}, u32[]{:S(2)}) collective-permute-start(f32[1,640]{1,0:T(1,128)S(1)} %get-tuple-element.81), channel_id=1, source_target_pairs={{0,8},{1,17},{2,10},{3,19},{4,12},{5,21},{6,14},{7,23},{8,0},{9,25... | collective-permute-start | bytes 7688 | tf_op jit(solution)/shard_map/ppermute | solution.py:361
  43.7 1.9 %collective-permute-start.13 = (f32[1,640]{1,0:T(1,128)S(1)}, f32[1,640]{1,0:T(1,128)S(1)}, u32[]{:S(2)}, u32[]{:S(2)}) collective-permute-start(f32[1,640]{1,0:T(1,128)S(1)} %maximum_maximum_fusion), channel_id=1, source_target_pairs={{4,0},{2,6},{0,2},{7,1},{5,7},{3,5},{12,8},{10,14},{8,10},{15,9},{... | collective-permute-start | bytes 7688 | tf_op jit(solution)/shard_map/ppermute | solution.py:356
  46.3 3.8 %collective-permute-done.13 = f32[1,640]{1,0:T(1,128)S(1)} collective-permute-done((f32[1,640]{1,0:T(1,128)S(1)}, f32[1,640]{1,0:T(1,128)S(1)}, u32[]{:S(2)}, u32[]{:S(2)}) %collective-permute-start.13) | collective-permute-done | bytes 2592 | tf_op jit(solution)/shard_map/ppermute | solution.py:356
  50.1 1.1 %collective-permute-done.14 = f32[1,320]{1,0:T(1,128)S(1)} collective-permute-done((f32[1,320]{1,0:T(1,128)S(1)}, f32[1,320]{1,0:T(1,128)S(1)}, u32[]{:S(2)}, u32[]{:S(2)}) %collective-permute-start.14) | collective-permute-done | bytes 1312 | tf_op jit(solution)/shard_map/ppermute | solution.py:360
  (37 shorter events, 5.3 us)
Async XLA Ops:
  0.0 13.7 %collective-permute-start = (bf16[320,768]{1,0:T(8,128)(2,1)}, bf16[320,768]{1,0:T(8,128)(2,1)S(1)}, u32[]{:S(2)}, u32[]{:S(2)}) collective-permute-start(bf16[320,768]{1,0:T(8,128)(2,1)} %embeddings.1), channel_id=1, source_target_pairs={{0,1},{1,0},{2,3},{3,2},{4,5},{5,4},{6,7},{7,6},{8,9},{9,8},{10,11... | collective-permute-start | bytes 1474568 | tf_op jit(solution)/shard_map/ppermute | solution.py:303
  0.5 24.8 %collective-permute-start.8 = (bf16[320,768]{1,0:T(8,128)(2,1)}, bf16[320,768]{1,0:T(8,128)(2,1)S(1)}, u32[]{:S(2)}, u32[]{:S(2)}) collective-permute-start(bf16[320,768]{1,0:T(8,128)(2,1)} %embeddings.1), channel_id=1, source_target_pairs={{0,4},{6,2},{2,0},{1,7},{7,5},{5,3},{8,12},{14,10},{10,8},{9,15},{... | collective-permute-start | bytes 1474568 | tf_op jit(solution)/shard_map/ppermute | solution.py:304
  7.3 1.0 %copy-start.4 = (bf16[320,768]{1,0:T(8,128)(2,1)S(1)}, bf16[320,768]{1,0:T(8,128)(2,1)}, u32[]{:S(2)}) copy-start(bf16[320,768]{1,0:T(8,128)(2,1)} %embeddings.1) | copy-start | bytes 1474564
  8.5 17.0 %collective-permute-start.7 = (bf16[336,768]{1,0:T(8,128)(2,1)S(1)}, bf16[336,768]{1,0:T(8,128)(2,1)S(1)}, u32[]{:S(2)}, u32[]{:S(2)}) collective-permute-start(bf16[336,768]{1,0:T(8,128)(2,1)S(1)} %get-tuple-element.47.refs_0_.refs_2_.refs_1_), channel_id=1, source_target_pairs={{0,16},{1,9},{2,18},{3,11},{4,20},{5,13},{6,22},{7,15},{8,24},{9,1... | collective-permute-start | bytes 1548296 | tf_op jit(solution)/shard_map/ppermute | solution.py:313
  10.1 9.4 %collective-permute-start.5 = (bf16[176,768]{1,0:T(8,128)(2,1)S(1)}, bf16[176,768]{1,0:T(8,128)(2,1)S(1)}, u32[]{:S(2)}, u32[]{:S(2)}) collective-permute-start(bf16[176,768]{1,0:T(8,128)(2,1)S(1)} %get-tuple-element.46), channel_id=1, source_target_pairs={{0,8},{1,17},{2,10},{3,19},{4,12},{5,21},{6,14},{7,23},{8,0},{9,25... | collective-permute-start | bytes 811016 | tf_op jit(solution)/shard_map/ppermute | solution.py:312
  11.6 1.6 %collective-permute-start.1 = (bf16[16,768]{1,0:T(8,128)(2,1)S(1)}, bf16[16,768]{1,0:T(8,128)(2,1)S(1)}, u32[]{:S(2)}, u32[]{:S(2)}) collective-permute-start(bf16[16,768]{1,0:T(8,128)(2,1)S(1)} %get-tuple-element.44.other_codes), channel_id=1, source_target_pairs={{0,1},{1,0},{2,3},{3,2},{4,5},{5,4},{6,7},{7,6},{8,9},{9,8},{10,11... | collective-permute-start | bytes 73736 | tf_op jit(solution)/shard_map/ppermute | solution.py:314
  13.2 11.5 %collective-permute-start.3 = (bf16[160,768]{1,0:T(8,128)(2,1)S(1)}, bf16[160,768]{1,0:T(8,128)(2,1)S(1)}, u32[]{:S(2)}, u32[]{:S(2)}) collective-permute-start(bf16[160,768]{1,0:T(8,128)(2,1)S(1)} %get-tuple-element.45), channel_id=1, source_target_pairs={{0,8},{1,17},{2,10},{3,19},{4,12},{5,21},{6,14},{7,23},{8,0},{9,25... | collective-permute-start | bytes 737288 | tf_op jit(solution)/shard_map/ppermute | solution.py:312
  13.9 20.0 %collective-permute-start.2 = (bf16[336,768]{1,0:T(8,128)(2,1)S(1)}, bf16[336,768]{1,0:T(8,128)(2,1)}, u32[]{:S(2)}, u32[]{:S(2)}) collective-permute-start(bf16[336,768]{1,0:T(8,128)(2,1)S(1)} %shard_map.38.refs_1_), channel_id=1, source_target_pairs={{0,4},{6,2},{2,0},{1,7},{7,5},{5,3},{8,12},{14,10},{10,8},{9,15},{... | collective-permute-start | bytes 1548296 | tf_op jit(solution)/shard_map/ppermute | solution.py:316
  19.5 11.3 %collective-permute-start.6 = (bf16[176,768]{1,0:T(8,128)(2,1)S(1)}, bf16[176,768]{1,0:T(8,128)(2,1)S(1)}, u32[]{:S(2)}, u32[]{:S(2)}) collective-permute-start(bf16[176,768]{1,0:T(8,128)(2,1)S(1)} %collective-permute-done.5.refs_4_.refs_3_), channel_id=1, source_target_pairs={{0,16},{1,9},{2,18},{3,11},{4,20},{5,13},{6,22},{7,15},{8,24},{9,1... | collective-permute-start | bytes 811016 | tf_op jit(solution)/shard_map/ppermute | solution.py:317
  24.6 6.2 %collective-permute-start.4 = (bf16[160,768]{1,0:T(8,128)(2,1)S(1)}, bf16[160,768]{1,0:T(8,128)(2,1)S(1)}, u32[]{:S(2)}, u32[]{:S(2)}) collective-permute-start(bf16[160,768]{1,0:T(8,128)(2,1)S(1)} %collective-permute-done.3.refs_3_.refs_2_), channel_id=1, source_target_pairs={{0,16},{1,9},{2,18},{3,11},{4,20},{5,13},{6,22},{7,15},{8,24},{9,1... | collective-permute-start | bytes 737288 | tf_op jit(solution)/shard_map/ppermute | solution.py:317
  25.4 7.0 %collective-permute-start.9 = (bf16[176,768]{1,0:T(8,128)(2,1)S(1)}, bf16[176,768]{1,0:T(8,128)(2,1)S(1)}, u32[]{:S(2)}, u32[]{:S(2)}) collective-permute-start(bf16[176,768]{1,0:T(8,128)(2,1)S(1)} %get-tuple-element.57), channel_id=1, source_target_pairs={{0,1},{1,0},{2,3},{3,2},{4,5},{5,4},{6,7},{7,6},{8,9},{9,8},{10,11... | collective-permute-start | bytes 811016 | tf_op jit(solution)/shard_map/ppermute | solution.py:319
  25.5 6.9 %collective-permute-start.10 = (bf16[144,768]{1,0:T(8,128)(2,1)S(1)}, bf16[144,768]{1,0:T(8,128)(2,1)S(1)}, u32[]{:S(2)}, u32[]{:S(2)}) collective-permute-start(bf16[144,768]{1,0:T(8,128)(2,1)S(1)} %get-tuple-element.58), channel_id=1, source_target_pairs={{0,1},{1,0},{2,3},{3,2},{4,5},{5,4},{6,7},{7,6},{8,9},{9,8},{10,11... | collective-permute-start | bytes 663560 | tf_op jit(solution)/shard_map/ppermute | solution.py:319
  30.8 1.6 %copy-start.2 = (bf16[160,768]{1,0:T(8,128)(2,1)}, bf16[160,768]{1,0:T(8,128)(2,1)S(1)}, u32[]{:S(2)}) copy-start(bf16[160,768]{1,0:T(8,128)(2,1)S(1)} %collective-permute-done.4.refs_2_.refs_5_.refs_6_) | copy-start | bytes 737284
  32.4 1.5 %copy-start = (f32[320,1280]{1,0:T(8,128)}, f32[320,1280]{1,0:T(8,128)S(1)}, u32[]{:S(2)}) copy-start(f32[320,1280]{1,0:T(8,128)S(1)} %shard_map.42.refs_11_) | copy-start | bytes 4915204
  33.9 5.1 %collective-permute-start.11 = (bf16[336,768]{1,0:T(8,128)(2,1)}, bf16[336,768]{1,0:T(8,128)(2,1)}, u32[]{:S(2)}, u32[]{:S(2)}) collective-permute-start(bf16[336,768]{1,0:T(8,128)(2,1)} %collective-permute-done.2.refs_0_), channel_id=1, source_target_pairs={{0,1},{1,0},{2,3},{3,2},{4,5},{5,4},{6,7},{7,6},{8,9},{9,8},{10,11... | collective-permute-start | bytes 1548296 | tf_op jit(solution)/shard_map/ppermute | solution.py:338
  34.0 1.4 %copy-start.1 = (f32[320,1280]{1,0:T(8,128)S(1)}, f32[320,1280]{1,0:T(8,128)}, u32[]{:S(2)}) copy-start(f32[320,1280]{1,0:T(8,128)} %copy-done) | copy-start | bytes 4915204
  35.4 0.9 %copy-start.3 = (bf16[160,768]{1,0:T(8,128)(2,1)S(1)}, bf16[160,768]{1,0:T(8,128)(2,1)}, u32[]{:S(2)}) copy-start(bf16[160,768]{1,0:T(8,128)(2,1)} %copy-done.2) | copy-start | bytes 737284
  41.6 2.1 %collective-permute-start.12 = (f32[1,640]{1,0:T(1,128)S(1)}, f32[1,640]{1,0:T(1,128)S(1)}, u32[]{:S(2)}, u32[]{:S(2)}) collective-permute-start(f32[1,640]{1,0:T(1,128)S(1)} %pad_maximum_fusion), channel_id=1, source_target_pairs={{0,1},{1,0},{2,3},{3,2},{4,5},{5,4},{6,7},{7,6},{8,9},{9,8},{10,11... | collective-permute-start | bytes 7688 | tf_op jit(solution)/shard_map/ppermute | solution.py:353
  42.0 3.6 %collective-permute-start.15 = (f32[1,640]{1,0:T(1,128)S(1)}, f32[1,640]{1,0:T(1,128)S(1)}, u32[]{:S(2)}, u32[]{:S(2)}) collective-permute-start(f32[1,640]{1,0:T(1,128)S(1)} %get-tuple-element.81), channel_id=1, source_target_pairs={{0,8},{1,17},{2,10},{3,19},{4,12},{5,21},{6,14},{7,23},{8,0},{9,25... | collective-permute-start | bytes 7688 | tf_op jit(solution)/shard_map/ppermute | solution.py:361
  43.7 6.4 %collective-permute-start.13 = (f32[1,640]{1,0:T(1,128)S(1)}, f32[1,640]{1,0:T(1,128)S(1)}, u32[]{:S(2)}, u32[]{:S(2)}) collective-permute-start(f32[1,640]{1,0:T(1,128)S(1)} %maximum_maximum_fusion), channel_id=1, source_target_pairs={{4,0},{2,6},{0,2},{7,1},{5,7},{3,5},{12,8},{10,14},{8,10},{15,9},{... | collective-permute-start | bytes 7688 | tf_op jit(solution)/shard_map/ppermute | solution.py:356
  45.7 4.4 %collective-permute-start.16 = (f32[1,320]{1,0:T(1,128)S(1)}, f32[1,320]{1,0:T(1,128)S(1)}, u32[]{:S(2)}, u32[]{:S(2)}) collective-permute-start(f32[1,320]{1,0:T(1,128)S(1)} %slice_maximum_fusion), channel_id=1, source_target_pairs={{0,16},{1,9},{2,18},{3,11},{4,20},{5,13},{6,22},{7,15},{8,24},{9,1... | collective-permute-start | bytes 3848 | tf_op jit(solution)/shard_map/ppermute | solution.py:364
  50.1 1.2 %collective-permute-start.14 = (f32[1,320]{1,0:T(1,128)S(1)}, f32[1,320]{1,0:T(1,128)S(1)}, u32[]{:S(2)}, u32[]{:S(2)}) collective-permute-start(f32[1,320]{1,0:T(1,128)S(1)} %slice.17), channel_id=1, source_target_pairs={{0,1},{1,0},{2,3},{3,2},{4,5},{5,4},{6,7},{7,6},{8,9},{9,8},{10,11... | collective-permute-start | bytes 3848 | tf_op jit(solution)/shard_map/ppermute | solution.py:360

commit v12 on v11

v12 whole, which is shorter than its diff:
```python
import functools

import jax
import jax.numpy as jnp
from jax import lax
from jax.experimental import pallas as pl
from jax.experimental.pallas import tpu as pltpu
from jax.sharding import PartitionSpec as P

EPSILON = 1e-06
EXTRA = 16
CODES = 3
LANES = 128
TILE = 256
CHUNK = 32
BOTH = ("dp", "grid")


def up(value, multiple):
    return -(-value // multiple) * multiple


def turned_to_column(row, rows):
    return jnp.broadcast_to(row, (LANES, row.shape[1])).T[:rows]


def codes(block, rows, span, first=0):
    parts = block[block.shape[0] - EXTRA :, : up(rows, LANES)].astype(jnp.float32)
    parts = parts[first : first + CODES]
    return parts[2:3] * (4.0 * span) + parts[0:1] * 256.0 + parts[1:2]


def unit_rows(rows, out):
    values = rows[...].astype(jnp.float32)
    scale = lax.rsqrt(jnp.sum(values * values, axis=1, keepdims=True) + EPSILON)
    out[0 : rows.shape[0], :] = (values * scale).astype(jnp.bfloat16)


def give_parts(block, outs):
    for out, top in zip(outs, (0, block.shape[0] - outs[-1].shape[0])):
        out[...] = block[top : top + out.shape[0], :]


def prepare_kernel(span, embeddings, named, block, *parts_out):
    rows, width = embeddings.shape
    unit_rows(embeddings, block)
    names = named[...].reshape(1, rows)
    keys = names & (span - 1)
    parts = [keys >> 8, keys & 255, names >> (span.bit_length() - 1)]
    parts = [part.astype(jnp.float32) for part in parts]
    parts = jnp.concatenate(parts + [jnp.zeros((EXTRA - 3, rows), jnp.float32)], axis=0)
    parts = jnp.concatenate([parts, jnp.zeros((EXTRA, width - rows), jnp.float32)], axis=1)
    block[rows : rows + EXTRA, :] = parts.astype(jnp.bfloat16)
    codes_out, *parts_out = parts_out
    codes_out[0:EXTRA, :] = block[rows : rows + EXTRA, :]
    give_parts(block, parts_out)


def complete_kernel(rows_of, codes_of, other_codes, block):
    rows, width = rows_of.shape
    unit_rows(rows_of, block)
    named = [part[...].astype(jnp.float32)[0:CODES] for part in (codes_of, other_codes)]
    named = jnp.concatenate(named + [jnp.zeros((EXTRA - 2 * CODES, width), jnp.float32)], axis=0)
    block[rows:, :] = named.astype(jnp.bfloat16)


def unit_kernel(rows_of, block, *parts_out):
    unit_rows(rows_of, block)
    give_parts(block, parts_out)


def with_units(kernel, heights, rows_of, *others):
    rows, width = rows_of.shape
    return pl.pallas_call(
        kernel,
        out_shape=[jax.ShapeDtypeStruct((height, width), jnp.bfloat16) for height in heights],
        compiler_params=pltpu.CompilerParams(vmem_limit_bytes=16 << 20),
        cost_estimate=pl.CostEstimate(flops=rows, bytes_accessed=rows, transcendentals=0),
    )(rows_of, *others)


def row_from_partial(partial, rows):
    padded = up(rows, LANES)
    if padded != rows:
        partial = jnp.concatenate(
            [partial, jnp.zeros((padded - rows, LANES), partial.dtype)], axis=0
        )
    return jnp.max(partial.T, axis=0, keepdims=True)[:, :rows]


def meet(units, row, rows, span, held, held_codes, to_block, to_held):
    column = turned_to_column(row, rows)
    starts = range(0, rows, CHUNK)
    partial = [jnp.full((CHUNK, LANES), -1.0, jnp.float32) for _ in starts]
    best_held = []
    for at in range(0, held.shape[0], TILE):
        sims = lax.dot_general(
            units,
            held[at : at + TILE, :],
            (((1,), (1,)), ((), ())),
            preferred_element_type=jnp.float32,
        )
        best = [jnp.full((CHUNK, LANES), -1.0, jnp.float32) for _ in range(0, TILE, LANES)]
        for place, top in enumerate(starts):
            mine = column[top : top + CHUNK]
            for lane in range(0, TILE, LANES):
                part = sims[top : top + CHUNK, lane : lane + LANES]
                gap = mine - held_codes[:, at + lane : at + lane + LANES]
                if to_block and to_held:
                    part = jnp.where(jnp.abs(gap) < span, part, -1.0)
                    later = gap > 0.0
                    ours, theirs = jnp.where(later, part, -1.0), jnp.where(later, -1.0, part)
                elif to_block:
                    ours = jnp.where((gap > 0.0) & (gap < span), part, -1.0)
                else:
                    theirs = jnp.where((gap < 0.0) & (gap > -span), part, -1.0)
                if to_block:
                    partial[place] = jnp.maximum(partial[place], ours)
                if to_held:
                    best[lane // LANES] = jnp.maximum(best[lane // LANES], theirs)
        best_held += [jnp.max(some, axis=0, keepdims=True) for some in best]
    return (
        row_from_partial(jnp.concatenate(partial, axis=0), rows) if to_block else None,
        jnp.concatenate(best_held, axis=1) if to_held else None,
    )


def assemble(whole, top, rows, pieces, extra):
    first, *others = pieces
    height = min(first.shape[0], rows)
    whole[top : top + height, :] = first[0:height, :]
    for last in others:
        height = last.shape[0] - extra
        whole[top + rows - height : top + rows, :] = last[0:height, :]


def gather_kernel(rows, span, lengths, *refs):
    *pieces, held, row = refs
    holds = regrouped(pieces, lengths)
    for at, block in enumerate(holds):
        assemble(held, at * rows, rows, block, EXTRA)
    row[...] = jnp.concatenate(
        [codes(block[-1], rows, span)[:, :rows] for block in holds], axis=1
    )


def gather(holds, rows, span):
    width = holds[0][0].shape[1]
    total = len(holds) * rows
    return pl.pallas_call(
        functools.partial(gather_kernel, rows, span, [len(block) for block in holds]),
        out_shape=[
            jax.ShapeDtypeStruct((total, width), jnp.bfloat16),
            jax.ShapeDtypeStruct((1, total), jnp.float32),
        ],
        compiler_params=pltpu.CompilerParams(vmem_limit_bytes=16 << 20),
        cost_estimate=pl.CostEstimate(flops=rows, bytes_accessed=rows, transcendentals=0),
    )(*[piece for block in holds for piece in block])


def regrouped(flat, lengths):
    flat = iter(flat)
    return [[next(flat) for _ in range(length)] for length in lengths]


def plane_kernel(rows, span, block, partner, held, row, best, mine):
    mine[...], _ = meet(
        block[0:rows, :], codes(block, rows, span), rows, span, held, row[...], *OWN
    )
    _, best[...] = meet(
        partner[0:rows, :], codes(partner, rows, span), rows, span, held, row[...], *HELD
    )


def line_kernel(rows, span, count, together, *refs):
    pieces, (second, held, row, best, *outs, found, joined) = refs[:count], refs[count:]
    if count > 1:
        assemble(joined, 0, rows, pieces, 0)
    units = joined if count > 1 else pieces[0]
    results = [
        meet(
            block[0:rows, :],
            codes(second, rows, span, first=place),
            rows,
            span,
            held,
            row[...],
            *TWO,
        )
        for block, place in ((units, CODES), (second, 0))
    ]
    found[...] = jnp.concatenate([mine for mine, _ in results], axis=1)
    best = jnp.maximum(best[...], jnp.maximum(results[0][1], results[1][1]))
    for out, places in zip(outs, together):
        out[...] = jnp.concatenate(
            [best[:, place * rows : (place + 1) * rows] for place in places], axis=1
        )


def plane(block, partner, held, row, rows, span):
    total, width = held.shape
    return pl.pallas_call(
        functools.partial(plane_kernel, rows, span),
        out_shape=[
            jax.ShapeDtypeStruct((1, total), jnp.float32),
            jax.ShapeDtypeStruct((1, rows), jnp.float32),
        ],
        compiler_params=pltpu.CompilerParams(vmem_limit_bytes=32 << 20),
        cost_estimate=pl.CostEstimate(flops=8 * rows * total * width, bytes_accessed=rows, transcendentals=0),
    )(block, partner, held, row)


def line(pieces, second, held, row, best, rows, span, together):
    total, width = held.shape
    outs = [jax.ShapeDtypeStruct((1, rows * len(some)), jnp.float32) for some in together]
    *bests, found = pl.pallas_call(
        functools.partial(line_kernel, rows, span, len(pieces), together),
        out_shape=outs + [jax.ShapeDtypeStruct((1, 2 * rows), jnp.float32)],
        scratch_shapes=[pltpu.VMEM((rows, width), jnp.bfloat16)],
        compiler_params=pltpu.CompilerParams(vmem_limit_bytes=32 << 20),
        cost_estimate=pl.CostEstimate(flops=rows, bytes_accessed=rows, transcendentals=0),
    )(*pieces, second, held, row, best)
    return bests, found


OWN = (True, False)
HELD = (False, True)
TWO = (True, True)


def line_rounds(chips):
    if chips == 4:
        return [[(0, 2), (3, 1), (1, 0)], [(0, 3), (3, 2), (2, 1)]]
    rounds = []
    for shift in range(1, chips // 2 + 1):
        senders = chips // 2 if 2 * shift == chips else chips
        rounds.append([(s, (s + shift) % chips) for s in range(senders)])
    return rounds


def solution(mesh):
    groups, members = mesh.shape["dp"], mesh.shape["grid"]
    assert groups == 4 and members % 2 == 0
    chips = members // 2

    def everywhere(target):
        return [
            (p * members + g, a * members + b)
            for p in range(groups)
            for g in range(members)
            for a, b in [target(p, g)]
        ]

    other_core = everywhere(lambda p, g: (p, g ^ 1))
    first = everywhere(lambda p, g: (p ^ (1 + g % 2), g))
    second = everywhere(lambda p, g: (p ^ (2 - g % 2), g))

    rounds = line_rounds(chips)
    rounds += [[]] * (len(rounds) % 2)
    rounds = [
        [
            (p * members + 2 * s + c, p * members + 2 * t + c)
            for p in range(groups)
            for c in range(2)
            for s, t in rounds[at + c]
        ]
        for at in range(0, len(rounds), 2)
    ]

    def back(pairs):
        return [(target, source) for source, target in pairs]

    def shards(embeddings, cluster, order_key):
        rows = embeddings.shape[0]
        span = 256
        while span < rows * groups * members:
            span *= 2
        halves = (rows // 2, rows // 2 + EXTRA)
        named = (cluster[:, 0] + 1) * span + order_key
        partner = lax.ppermute(embeddings, BOTH, other_core)
        raw = [lax.ppermute(embeddings, BOTH, pairs) for pairs in rounds]
        block, codes_of, *parts = with_units(
            functools.partial(prepare_kernel, span),
            (rows + EXTRA, EXTRA, *halves),
            embeddings,
            named,
        )
        from_first = [lax.ppermute(part, BOTH, first) for part in parts]
        from_second = [lax.ppermute(block, BOTH, second)]
        other_codes = lax.ppermute(codes_of, BOTH, other_core)
        (partner,) = with_units(complete_kernel, (rows + EXTRA,), partner, other_codes, codes_of)
        near_other = [lax.ppermute(partner, BOTH, pairs) for pairs in rounds]
        from_corner = [lax.ppermute(part, BOTH, second) for part in from_first]
        near = [
            list(with_units(unit_kernel, (rows, rows // 2, rows // 2), rows_of))
            for rows_of in raw
        ]
        far = [[lax.ppermute(piece, BOTH, other_core) for piece in blocks[1:]] for blocks in near]

        results, kept, sent = [], [], []
        held, row = gather([[block], from_first, from_second, from_corner], rows, span)
        held, *far[0] = lax.optimization_barrier((held, *far[0]))
        best, mine = plane(block, partner, held, row, rows, span)
        results.append(mine)
        whole, last = [tuple(range(groups))], [(0,), (1, 3), (2,)]
        for at, second_near in enumerate(near_other):
            second_near, best = lax.optimization_barrier((second_near, best))
            second_far = lax.ppermute(second_near, BOTH, other_core)
            (best,), found = line(near[at][:1], second_near, held, row, best, rows, span, whole)
            kept.append(found)
            bests, found = line(
                far[at],
                second_far,
                held,
                row,
                best,
                rows,
                span,
                last if at == len(rounds) - 1 else whole,
            )
            best = bests[0]
            sent.append(found)
        sent = lax.ppermute(jnp.concatenate(sent, axis=1), BOTH, other_core)
        kept = jnp.maximum(jnp.concatenate(kept, axis=1), sent)
        for at, pairs in enumerate(rounds):
            found = lax.ppermute(kept[:, 2 * at * rows : 2 * (at + 1) * rows], BOTH, back(pairs))
            me = lax.axis_index(BOTH)
            sender = functools.reduce(jnp.logical_or, [me == source for source, _ in pairs])
            found = jnp.where(sender, found, -1.0)
            results += [found[:, :rows], lax.ppermute(found[:, rows:], BOTH, other_core)]
        from_x = lax.ppermute(bests[1], BOTH, first)
        results.append(from_x[:, :rows])
        onward = jnp.maximum(bests[2], from_x[:, rows:])
        results.append(lax.ppermute(onward, BOTH, second))
        return functools.reduce(jnp.maximum, results, bests[0]).reshape(rows)

    placed = (P(BOTH, None), P(BOTH, None), P(BOTH))
    return jax.shard_map(
        shards, mesh=mesh, in_specs=placed, out_specs=P(BOTH), check_vma=False
    )
```

time: 52.4 us -> 46.1 us (0.88)
  waiting for transfers between devices: 17.5 us -> 11.3 us
  starting transfers between devices: 18.5 us -> 24.3 us
  Pallas kernels: 10.1 us -> 6.22 us
  local copies, waits for them, and re-layouts: 3.41 us -> 1.8 us
    ppermute x2, waiting for transfers between devices: 8.33 us -> 4 us  [shards(): from_first = [lax.ppermute(part, BOTH, first) for part in parts]]
    pallas_call x6 -> x4, Pallas kernels: 9.51 us -> 5.68 us  [the longest x2 3.9 us: line(): pl.pallas_call(functools.partial(line_kernel, rows, span, len(pieces), to...]
    ppermute x2, starting transfers between devices: 1.1 us -> 3.91 us  [shards(): from_corner = [lax.ppermute(part, BOTH, second) for part in from_first]]
    unnamed x10, local copies, waits for them, and re-layouts: 3.4 us -> 1.73 us
    ppermute x1, waiting for transfers between devices: 3.78 us -> 2.51 us  [shards(): lax.ppermute(kept[:, 2 * at * rows:2 * (at + 1) * rows], BOTH, back(pairs))]
    ppermute x1, starting transfers between devices: 0.59 us -> 1.61 us  [shards(): results.append(lax.ppermute(onward, BOTH, second))]
    ppermute x1, waiting for transfers between devices: 0.85 us -> 0.01 us  [shards(): other_codes = lax.ppermute(codes_of, BOTH, other_core)]
    ppermute x2, starting transfers between devices: 2.03 us -> 2.81 us  [shards(): from_first = [lax.ppermute(part, BOTH, first) for part in parts]]
  transfers between devices with their start and end apart: 17 -> 17, of which waited for: 6 -> 6; matrix products, arithmetic and copies ran while one was open for 3% -> 3% of each run, Pallas kernels for 14% -> 9%
where the time goes in v12:
time: 46.1 us; the launch traced here: 45.8 us
  starting transfers between devices  24.3 us (53%)
  waiting for transfers between devices  11.3 us (25%)
  Pallas kernels  6.22 us (13%)
  other arithmetic  2.07 us (4%)
  local copies, waits for them, and re-layouts  1.8 us (4%)
    ppermute x1, starting transfers between devices, shards(): raw = [lax.ppermute(embeddings, BOTH, pairs) for pairs in rounds]  5.93 us
    ppermute x2, waiting for transfers between devices, shards(): from_first = [lax.ppermute(part, BOTH, first) for part in parts]  4 us
    ppermute x2, starting transfers between devices, shards(): from_corner = [lax.ppermute(part, BOTH, second) for part in from_first]  3.91 us
    pallas_call x2, Pallas kernels, line(): pl.pallas_call(functools.partial(line_kernel, rows, span, len(pieces), to...  3.9 us
    ppermute x2, waiting for transfers between devices, shards(): from_corner = [lax.ppermute(part, BOTH, second) for part in from_first]  3.62 us
    ppermute x2, starting transfers between devices, shards(): from_first = [lax.ppermute(part, BOTH, first) for part in parts]  2.81 us
    ppermute x1, waiting for transfers between devices, shards(): lax.ppermute(kept[:, 2 * at * rows:2 * (at + 1) * rows], BOTH, back(pairs))  2.51 us
    ppermute x1, starting transfers between devices, shards(): lax.ppermute(kept[:, 2 * at * rows:2 * (at + 1) * rows], BOTH, back(pairs))  2.17 us
  transfers between devices with their start and end apart: 17, of which 6 were waited for; matrix products, arithmetic and copies ran while one was open for 3% of the time, Pallas kernels for 9%

profile of v12, /device:TPU:0, one launch (start us, length us, event | category | flops | bytes accessed | tf_op | source)
XLA Modules:
  0.0 45.8 jit_solution(8950450132515898382)
XLA Ops:
  0.0 5.9 %collective-permute-start.5 = (bf16[320,768]{1,0:T(8,128)(2,1)}, bf16[320,768]{1,0:T(8,128)(2,1)S(1)}, u32[]{:S(2)}, u32[]{:S(2)}) collective-permute-start(bf16[320,768]{1,0:T(8,128)(2,1)} %embeddings.1), channel_id=1, source_target_pairs={{0,4},{6,2},{2,0},{1,7},{7,5},{5,3},{8,12},{14,10},{10,8},{9,15},{... | collective-permute-start | bytes 1474568 | tf_op jit(solution)/shard_map/ppermute | solution.py:281
  6.6 0.7 %multiply_reduce_fusion = s32[320]{0:T(512)S(1)} fusion(s32[320,1]{0,1:T(1,128)} %param.4), kind=kLoop, calls=%fused_computation.6 | loop fusion | flops 640 | bytes 2560 | tf_op jit(solution)/shard_map/mul | solution.py:279
  7.3 0.7 %add.15.named = s32[320]{0:T(512)S(1)} add(s32[320]{0:T(512)S(1)} %multiply_reduce_fusion, s32[320]{0:T(512)} %param.5) | non-fusion elementwise | flops 320 | bytes 3840 | tf_op jit(solution)/shard_map/add | solution.py:279
  8.0 1.0 %copy-done = bf16[320,768]{1,0:T(8,128)(2,1)S(1)} copy-done((bf16[320,768]{1,0:T(8,128)(2,1)S(1)}, bf16[320,768]{1,0:T(8,128)(2,1)}, u32[]{:S(2)}) %copy-start) | copy-done | bytes 491544
  9.2 1.6 %collective-permute-start = (bf16[160,768]{1,0:T(8,128)(2,1)S(1)}, bf16[160,768]{1,0:T(8,128)(2,1)S(1)}, u32[]{:S(2)}, u32[]{:S(2)}) collective-permute-start(bf16[160,768]{1,0:T(8,128)(2,1)S(1)} %get-tuple-element.28), channel_id=1, source_target_pairs={{0,8},{1,17},{2,10},{3,19},{4,12},{5,21},{6,14},{7,23},{8,0},{9,25... | collective-permute-start | bytes 737288 | tf_op jit(solution)/shard_map/ppermute | solution.py:288
  10.8 1.3 %collective-permute-start.1 = (bf16[176,768]{1,0:T(8,128)(2,1)S(1)}, bf16[176,768]{1,0:T(8,128)(2,1)S(1)}, u32[]{:S(2)}, u32[]{:S(2)}) collective-permute-start(bf16[176,768]{1,0:T(8,128)(2,1)S(1)} %get-tuple-element.29), channel_id=1, source_target_pairs={{0,8},{1,17},{2,10},{3,19},{4,12},{5,21},{6,14},{7,23},{8,0},{9,25... | collective-permute-start | bytes 811016 | tf_op jit(solution)/shard_map/ppermute | solution.py:288
  12.0 1.5 %collective-permute-start.2 = (bf16[336,768]{1,0:T(8,128)(2,1)S(1)}, bf16[336,768]{1,0:T(8,128)(2,1)S(1)}, u32[]{:S(2)}, u32[]{:S(2)}) collective-permute-start(bf16[336,768]{1,0:T(8,128)(2,1)S(1)} %get-tuple-element.27.refs_0_.block), channel_id=1, source_target_pairs={{0,16},{1,9},{2,18},{3,11},{4,20},{5,13},{6,22},{7,15},{8,24},{9,1... | collective-permute-start | bytes 1548296 | tf_op jit(solution)/shard_map/ppermute | solution.py:289
  13.5 2.3 %collective-permute-done.refs_1_ = bf16[160,768]{1,0:T(8,128)(2,1)S(1)} collective-permute-done((bf16[160,768]{1,0:T(8,128)(2,1)S(1)}, bf16[160,768]{1,0:T(8,128)(2,1)S(1)}, u32[]{:S(2)}, u32[]{:S(2)}) %collective-permute-start) | collective-permute-done | bytes 245792 | tf_op jit(solution)/shard_map/ppermute | solution.py:288
  15.8 2.0 %collective-permute-start.3 = (bf16[160,768]{1,0:T(8,128)(2,1)S(1)}, bf16[160,768]{1,0:T(8,128)(2,1)S(1)}, u32[]{:S(2)}, u32[]{:S(2)}) collective-permute-start(bf16[160,768]{1,0:T(8,128)(2,1)S(1)} %collective-permute-done.refs_1_), channel_id=1, source_target_pairs={{0,16},{1,9},{2,18},{3,11},{4,20},{5,13},{6,22},{7,15},{8,24},{9,1... | collective-permute-start | bytes 737288 | tf_op jit(solution)/shard_map/ppermute | solution.py:293
  17.9 1.9 %collective-permute-start.10 = (bf16[336,768]{1,0:T(8,128)(2,1)S(1)}, bf16[336,768]{1,0:T(8,128)(2,1)S(1)}, u32[]{:S(2)}, u32[]{:S(2)}) collective-permute-start(bf16[336,768]{1,0:T(8,128)(2,1)S(1)} %shard_map.40.partner), channel_id=1, source_target_pairs={{0,4},{6,2},{2,0},{1,7},{7,5},{5,3},{8,12},{14,10},{10,8},{9,15},{... | collective-permute-start | bytes 1548296 | tf_op jit(solution)/shard_map/ppermute | solution.py:292
  19.8 1.7 %collective-permute-done.1.refs_2_ = bf16[176,768]{1,0:T(8,128)(2,1)S(1)} collective-permute-done((bf16[176,768]{1,0:T(8,128)(2,1)S(1)}, bf16[176,768]{1,0:T(8,128)(2,1)S(1)}, u32[]{:S(2)}, u32[]{:S(2)}) %collective-permute-start.1) | collective-permute-done | bytes 270368 | tf_op jit(solution)/shard_map/ppermute | solution.py:288
  21.5 2.0 %collective-permute-start.4 = (bf16[176,768]{1,0:T(8,128)(2,1)S(1)}, bf16[176,768]{1,0:T(8,128)(2,1)S(1)}, u32[]{:S(2)}, u32[]{:S(2)}) collective-permute-start(bf16[176,768]{1,0:T(8,128)(2,1)S(1)} %collective-permute-done.1.refs_2_), channel_id=1, source_target_pairs={{0,16},{1,9},{2,18},{3,11},{4,20},{5,13},{6,22},{7,15},{8,24},{9,1... | collective-permute-start | bytes 811016 | tf_op jit(solution)/shard_map/ppermute | solution.py:293
  23.8 1.8 %collective-permute-done.3.refs_4_ = bf16[160,768]{1,0:T(8,128)(2,1)S(1)} collective-permute-done((bf16[160,768]{1,0:T(8,128)(2,1)S(1)}, bf16[160,768]{1,0:T(8,128)(2,1)S(1)}, u32[]{:S(2)}, u32[]{:S(2)}) %collective-permute-start.3) | collective-permute-done | bytes 245792 | tf_op jit(solution)/shard_map/ppermute | solution.py:293
  25.6 1.1 %collective-permute-start.7 = (bf16[160,768]{1,0:T(8,128)(2,1)S(1)}, bf16[160,768]{1,0:T(8,128)(2,1)S(1)}, u32[]{:S(2)}, u32[]{:S(2)}) collective-permute-start(bf16[160,768]{1,0:T(8,128)(2,1)S(1)} %get-tuple-element.32), channel_id=1, source_target_pairs={{0,1},{1,0},{2,3},{3,2},{4,5},{5,4},{6,7},{7,6},{8,9},{9,8},{10,11... | collective-permute-start | bytes 737288 | tf_op jit(solution)/shard_map/ppermute | solution.py:298
  26.6 1.8 %collective-permute-done.4.refs_5_ = bf16[176,768]{1,0:T(8,128)(2,1)S(1)} collective-permute-done((bf16[176,768]{1,0:T(8,128)(2,1)S(1)}, bf16[176,768]{1,0:T(8,128)(2,1)S(1)}, u32[]{:S(2)}, u32[]{:S(2)}) %collective-permute-start.4) | collective-permute-done | bytes 270368 | tf_op jit(solution)/shard_map/ppermute | solution.py:293
  29.3 1.6 %shard_map.41 = (f32[1,1280]{1,0:T(1,128)S(1)}, f32[1,320]{1,0:T(1,128)S(1)}) custom-call(bf16[336,768]{1,0:T(8,128)(2,1)S(1)} %get-tuple-element.27.refs_0_.block, bf16[336,768]{1,0:T(8,128)(2,1)S(1)} %shard_map.40.partner, bf16[1280,768]{1,0:T(8,128)(2,1)S(1)} %get-tuple-element.36.held.refs_2_.refs_3_, f32[1,1280]{1,0:T(1,128)S(1)} %get-tuple-element.37.row.refs_3_.refs_4_), custom_call_target="tpu_custom_call" | custom-call | flops 2516582400 | bytes 320 | tf_op jit(solution)/shard_map/pallas_call | solution.py:202
  31.0 0.8 %collective-permute-start.11 = (bf16[336,768]{1,0:T(8,128)(2,1)S(1)}, bf16[336,768]{1,0:T(8,128)(2,1)S(1)}, u32[]{:S(2)}, u32[]{:S(2)}) collective-permute-start(bf16[336,768]{1,0:T(8,128)(2,1)S(1)} %collective-permute-done.10.refs_1_), channel_id=1, source_target_pairs={{0,1},{1,0},{2,3},{3,2},{4,5},{5,4},{6,7},{7,6},{8,9},{9,8},{10,11... | collective-permute-start | bytes 1548296 | tf_op jit(solution)/shard_map/ppermute | solution.py:308
  31.8 1.9 %shard_map.42 = (f32[1,1280]{1,0:T(1,128)S(1)}, f32[1,640]{1,0:T(1,128)S(1)}) custom-call(bf16[320,768]{1,0:T(8,128)(2,1)S(1)} %get-tuple-element.40.refs_0_, bf16[336,768]{1,0:T(8,128)(2,1)S(1)} %collective-permute-done.10.refs_1_, bf16[1280,768]{1,0:T(8,128)(2,1)S(1)} %get-tuple-element.36.held.refs_2_.refs_3_, ...), custom_call_target="tpu_custom_call" | custom-call | flops 320 | bytes 320 | tf_op jit(solution)/shard_map/pallas_call | solution.py:216
  33.8 2.0 %shard_map.43 = (f32[1,320]{1,0:T(1,128)S(1)}, f32[1,640]{1,0:T(1,128)S(1)}, f32[1,320]{1,0:T(1,128)S(1)}, f32[1,640]{1,0:T(1,128)S(1)}) custom-call(bf16[160,768]{1,0:T(8,128)(2,1)S(1)} %copy-done.2, bf16[160,768]{1,0:T(8,128)(2,1)S(1)} %copy-done.4, bf16[336,768]{1,0:T(8,128)(2,1)S(1)} %collective-permute-done.11.refs_2_, ...), custom_call_target="tpu_custom_call" | custom-call | flops 320 | bytes 320 | tf_op jit(solution)/shard_map/pallas_call | solution.py:216
  35.8 1.8 %collective-permute-start.15 = (f32[1,640]{1,0:T(1,128)S(1)}, f32[1,640]{1,0:T(1,128)S(1)}, u32[]{:S(2)}, u32[]{:S(2)}) collective-permute-start(f32[1,640]{1,0:T(1,128)S(1)} %get-tuple-element.47), channel_id=1, source_target_pairs={{0,8},{1,17},{2,10},{3,19},{4,12},{5,21},{6,14},{7,23},{8,0},{9,25... | collective-permute-start | bytes 7688 | tf_op jit(solution)/shard_map/ppermute | solution.py:331
  37.6 2.2 %collective-permute-start.13 = (f32[1,640]{1,0:T(1,128)S(1)}, f32[1,640]{1,0:T(1,128)S(1)}, u32[]{:S(2)}, u32[]{:S(2)}) collective-permute-start(f32[1,640]{1,0:T(1,128)S(1)} %max.22), channel_id=1, source_target_pairs={{4,0},{2,6},{0,2},{7,1},{5,7},{3,5},{12,8},{10,14},{8,10},{15,9},{... | collective-permute-start | bytes 7688 | tf_op jit(solution)/shard_map/ppermute | solution.py:326
  39.9 1.6 %collective-permute-start.16 = (f32[1,320]{1,0:T(1,128)S(1)}, f32[1,320]{1,0:T(1,128)S(1)}, u32[]{:S(2)}, u32[]{:S(2)}) collective-permute-start(f32[1,320]{1,0:T(1,128)S(1)} %slice_maximum_fusion), channel_id=1, source_target_pairs={{0,16},{1,9},{2,18},{3,11},{4,20},{5,13},{6,22},{7,15},{8,24},{9,1... | collective-permute-start | bytes 3848 | tf_op jit(solution)/shard_map/ppermute | solution.py:334
  41.5 2.5 %collective-permute-done.13 = f32[1,640]{1,0:T(1,128)S(1)} collective-permute-done((f32[1,640]{1,0:T(1,128)S(1)}, f32[1,640]{1,0:T(1,128)S(1)}, u32[]{:S(2)}, u32[]{:S(2)}) %collective-permute-start.13) | collective-permute-done | bytes 2592 | tf_op jit(solution)/shard_map/ppermute | solution.py:326
  44.1 1.1 %collective-permute-done.14 = f32[1,320]{1,0:T(1,128)S(1)} collective-permute-done((f32[1,320]{1,0:T(1,128)S(1)}, f32[1,320]{1,0:T(1,128)S(1)}, u32[]{:S(2)}, u32[]{:S(2)}) %collective-permute-start.14) | collective-permute-done | bytes 1312 | tf_op jit(solution)/shard_map/ppermute | solution.py:330
  (34 shorter events, 3.0 us)
Async XLA Ops:
  0.0 23.5 %collective-permute-start.5 = (bf16[320,768]{1,0:T(8,128)(2,1)}, bf16[320,768]{1,0:T(8,128)(2,1)S(1)}, u32[]{:S(2)}, u32[]{:S(2)}) collective-permute-start(bf16[320,768]{1,0:T(8,128)(2,1)} %embeddings.1), channel_id=1, source_target_pairs={{0,4},{6,2},{2,0},{1,7},{7,5},{5,3},{8,12},{14,10},{10,8},{9,15},{... | collective-permute-start | bytes 1474568 | tf_op jit(solution)/shard_map/ppermute | solution.py:281
  5.9 11.8 %collective-permute-start.8 = (bf16[320,768]{1,0:T(8,128)(2,1)}, bf16[320,768]{1,0:T(8,128)(2,1)S(1)}, u32[]{:S(2)}, u32[]{:S(2)}) collective-permute-start(bf16[320,768]{1,0:T(8,128)(2,1)} %embeddings.1), channel_id=1, source_target_pairs={{0,1},{1,0},{2,3},{3,2},{4,5},{5,4},{6,7},{7,6},{8,9},{9,8},{10,11... | collective-permute-start | bytes 1474568 | tf_op jit(solution)/shard_map/ppermute | solution.py:280
  8.0 1.0 %copy-start = (bf16[320,768]{1,0:T(8,128)(2,1)S(1)}, bf16[320,768]{1,0:T(8,128)(2,1)}, u32[]{:S(2)}) copy-start(bf16[320,768]{1,0:T(8,128)(2,1)} %embeddings.1) | copy-start | bytes 1474564
  9.2 6.6 %collective-permute-start = (bf16[160,768]{1,0:T(8,128)(2,1)S(1)}, bf16[160,768]{1,0:T(8,128)(2,1)S(1)}, u32[]{:S(2)}, u32[]{:S(2)}) collective-permute-start(bf16[160,768]{1,0:T(8,128)(2,1)S(1)} %get-tuple-element.28), channel_id=1, source_target_pairs={{0,8},{1,17},{2,10},{3,19},{4,12},{5,21},{6,14},{7,23},{8,0},{9,25... | collective-permute-start | bytes 737288 | tf_op jit(solution)/shard_map/ppermute | solution.py:288
  10.8 1.3 %collective-permute-start.9 = (bf16[16,768]{1,0:T(8,128)(2,1)S(1)}, bf16[16,768]{1,0:T(8,128)(2,1)S(1)}, u32[]{:S(2)}, u32[]{:S(2)}) collective-permute-start(bf16[16,768]{1,0:T(8,128)(2,1)S(1)} %get-tuple-element.35.other_codes), channel_id=1, source_target_pairs={{0,1},{1,0},{2,3},{3,2},{4,5},{5,4},{6,7},{7,6},{8,9},{9,8},{10,11... | collective-permute-start | bytes 73736 | tf_op jit(solution)/shard_map/ppermute | solution.py:290
  10.8 10.8 %collective-permute-start.1 = (bf16[176,768]{1,0:T(8,128)(2,1)S(1)}, bf16[176,768]{1,0:T(8,128)(2,1)S(1)}, u32[]{:S(2)}, u32[]{:S(2)}) collective-permute-start(bf16[176,768]{1,0:T(8,128)(2,1)S(1)} %get-tuple-element.29), channel_id=1, source_target_pairs={{0,8},{1,17},{2,10},{3,19},{4,12},{5,21},{6,14},{7,23},{8,0},{9,25... | collective-permute-start | bytes 811016 | tf_op jit(solution)/shard_map/ppermute | solution.py:288
  12.0 14.6 %collective-permute-start.2 = (bf16[336,768]{1,0:T(8,128)(2,1)S(1)}, bf16[336,768]{1,0:T(8,128)(2,1)S(1)}, u32[]{:S(2)}, u32[]{:S(2)}) collective-permute-start(bf16[336,768]{1,0:T(8,128)(2,1)S(1)} %get-tuple-element.27.refs_0_.block), channel_id=1, source_target_pairs={{0,16},{1,9},{2,18},{3,11},{4,20},{5,13},{6,22},{7,15},{8,24},{9,1... | collective-permute-start | bytes 1548296 | tf_op jit(solution)/shard_map/ppermute | solution.py:289
  15.8 9.8 %collective-permute-start.3 = (bf16[160,768]{1,0:T(8,128)(2,1)S(1)}, bf16[160,768]{1,0:T(8,128)(2,1)S(1)}, u32[]{:S(2)}, u32[]{:S(2)}) collective-permute-start(bf16[160,768]{1,0:T(8,128)(2,1)S(1)} %collective-permute-done.refs_1_), channel_id=1, source_target_pairs={{0,16},{1,9},{2,18},{3,11},{4,20},{5,13},{6,22},{7,15},{8,24},{9,1... | collective-permute-start | bytes 737288 | tf_op jit(solution)/shard_map/ppermute | solution.py:293
  17.9 13.1 %collective-permute-start.10 = (bf16[336,768]{1,0:T(8,128)(2,1)S(1)}, bf16[336,768]{1,0:T(8,128)(2,1)S(1)}, u32[]{:S(2)}, u32[]{:S(2)}) collective-permute-start(bf16[336,768]{1,0:T(8,128)(2,1)S(1)} %shard_map.40.partner), channel_id=1, source_target_pairs={{0,4},{6,2},{2,0},{1,7},{7,5},{5,3},{8,12},{14,10},{10,8},{9,15},{... | collective-permute-start | bytes 1548296 | tf_op jit(solution)/shard_map/ppermute | solution.py:292
  21.5 6.9 %collective-permute-start.4 = (bf16[176,768]{1,0:T(8,128)(2,1)S(1)}, bf16[176,768]{1,0:T(8,128)(2,1)S(1)}, u32[]{:S(2)}, u32[]{:S(2)}) collective-permute-start(bf16[176,768]{1,0:T(8,128)(2,1)S(1)} %collective-permute-done.1.refs_2_), channel_id=1, source_target_pairs={{0,16},{1,9},{2,18},{3,11},{4,20},{5,13},{6,22},{7,15},{8,24},{9,1... | collective-permute-start | bytes 811016 | tf_op jit(solution)/shard_map/ppermute | solution.py:293
  23.7 4.9 %collective-permute-start.6 = (bf16[160,768]{1,0:T(8,128)(2,1)S(1)}, bf16[160,768]{1,0:T(8,128)(2,1)S(1)}, u32[]{:S(2)}, u32[]{:S(2)}) collective-permute-start(bf16[160,768]{1,0:T(8,128)(2,1)S(1)} %get-tuple-element.31), channel_id=1, source_target_pairs={{0,1},{1,0},{2,3},{3,2},{4,5},{5,4},{6,7},{7,6},{8,9},{9,8},{10,11... | collective-permute-start | bytes 737288 | tf_op jit(solution)/shard_map/ppermute | solution.py:298
  25.6 3.7 %collective-permute-start.7 = (bf16[160,768]{1,0:T(8,128)(2,1)S(1)}, bf16[160,768]{1,0:T(8,128)(2,1)S(1)}, u32[]{:S(2)}, u32[]{:S(2)}) collective-permute-start(bf16[160,768]{1,0:T(8,128)(2,1)S(1)} %get-tuple-element.32), channel_id=1, source_target_pairs={{0,1},{1,0},{2,3},{3,2},{4,5},{5,4},{6,7},{7,6},{8,9},{9,8},{10,11... | collective-permute-start | bytes 737288 | tf_op jit(solution)/shard_map/ppermute | solution.py:298
  28.6 0.7 %copy-start.1 = (bf16[160,768]{1,0:T(8,128)(2,1)}, bf16[160,768]{1,0:T(8,128)(2,1)S(1)}, u32[]{:S(2)}) copy-start(bf16[160,768]{1,0:T(8,128)(2,1)S(1)} %collective-permute-done.6.refs_0_) | copy-start | bytes 737284
  29.3 1.6 %copy-start.3 = (bf16[160,768]{1,0:T(8,128)(2,1)}, bf16[160,768]{1,0:T(8,128)(2,1)S(1)}, u32[]{:S(2)}) copy-start(bf16[160,768]{1,0:T(8,128)(2,1)S(1)} %collective-permute-done.7.refs_1_) | copy-start | bytes 737284
  31.0 2.8 %collective-permute-start.11 = (bf16[336,768]{1,0:T(8,128)(2,1)S(1)}, bf16[336,768]{1,0:T(8,128)(2,1)S(1)}, u32[]{:S(2)}, u32[]{:S(2)}) collective-permute-start(bf16[336,768]{1,0:T(8,128)(2,1)S(1)} %collective-permute-done.10.refs_1_), channel_id=1, source_target_pairs={{0,1},{1,0},{2,3},{3,2},{4,5},{5,4},{6,7},{7,6},{8,9},{9,8},{10,11... | collective-permute-start | bytes 1548296 | tf_op jit(solution)/shard_map/ppermute | solution.py:308
  31.8 1.9 %copy-start.2 = (bf16[160,768]{1,0:T(8,128)(2,1)S(1)}, bf16[160,768]{1,0:T(8,128)(2,1)}, u32[]{:S(2)}) copy-start(bf16[160,768]{1,0:T(8,128)(2,1)} %copy-done.1) | copy-start | bytes 737284
  31.8 1.9 %copy-start.4 = (bf16[160,768]{1,0:T(8,128)(2,1)S(1)}, bf16[160,768]{1,0:T(8,128)(2,1)}, u32[]{:S(2)}) copy-start(bf16[160,768]{1,0:T(8,128)(2,1)} %copy-done.3) | copy-start | bytes 737284
  35.7 1.9 %collective-permute-start.12 = (f32[1,640]{1,0:T(1,128)S(1)}, f32[1,640]{1,0:T(1,128)S(1)}, u32[]{:S(2)}, u32[]{:S(2)}) collective-permute-start(f32[1,640]{1,0:T(1,128)S(1)} %get-tuple-element.46), channel_id=1, source_target_pairs={{0,1},{1,0},{2,3},{3,2},{4,5},{5,4},{6,7},{7,6},{8,9},{9,8},{10,11... | collective-permute-start | bytes 7688 | tf_op jit(solution)/shard_map/ppermute | solution.py:323
  35.8 4.0 %collective-permute-start.15 = (f32[1,640]{1,0:T(1,128)S(1)}, f32[1,640]{1,0:T(1,128)S(1)}, u32[]{:S(2)}, u32[]{:S(2)}) collective-permute-start(f32[1,640]{1,0:T(1,128)S(1)} %get-tuple-element.47), channel_id=1, source_target_pairs={{0,8},{1,17},{2,10},{3,19},{4,12},{5,21},{6,14},{7,23},{8,0},{9,25... | collective-permute-start | bytes 7688 | tf_op jit(solution)/shard_map/ppermute | solution.py:331
  37.6 6.4 %collective-permute-start.13 = (f32[1,640]{1,0:T(1,128)S(1)}, f32[1,640]{1,0:T(1,128)S(1)}, u32[]{:S(2)}, u32[]{:S(2)}) collective-permute-start(f32[1,640]{1,0:T(1,128)S(1)} %max.22), channel_id=1, source_target_pairs={{4,0},{2,6},{0,2},{7,1},{5,7},{3,5},{12,8},{10,14},{8,10},{15,9},{... | collective-permute-start | bytes 7688 | tf_op jit(solution)/shard_map/ppermute | solution.py:326
  39.9 4.2 %collective-permute-start.16 = (f32[1,320]{1,0:T(1,128)S(1)}, f32[1,320]{1,0:T(1,128)S(1)}, u32[]{:S(2)}, u32[]{:S(2)}) collective-permute-start(f32[1,320]{1,0:T(1,128)S(1)} %slice_maximum_fusion), channel_id=1, source_target_pairs={{0,16},{1,9},{2,18},{3,11},{4,20},{5,13},{6,22},{7,15},{8,24},{9,1... | collective-permute-start | bytes 3848 | tf_op jit(solution)/shard_map/ppermute | solution.py:334
  44.1 1.2 %collective-permute-start.14 = (f32[1,320]{1,0:T(1,128)S(1)}, f32[1,320]{1,0:T(1,128)S(1)}, u32[]{:S(2)}, u32[]{:S(2)}) collective-permute-start(f32[1,320]{1,0:T(1,128)S(1)} %slice.17), channel_id=1, source_target_pairs={{0,1},{1,0},{2,3},{3,2},{4,5},{5,4},{6,7},{7,6},{8,9},{9,8},{10,11... | collective-permute-start | bytes 3848 | tf_op jit(solution)/shard_map/ppermute | solution.py:330

commit v13 on v12

--- a/solution.py
+++ b/solution.py
@@ -74,7 +74,7 @@
     return pl.pallas_call(
         kernel,
         out_shape=[jax.ShapeDtypeStruct((height, width), jnp.bfloat16) for height in heights],
-        compiler_params=pltpu.CompilerParams(vmem_limit_bytes=16 << 20),
+        compiler_params=pltpu.CompilerParams(vmem_limit_bytes=8 << 20),
         cost_estimate=pl.CostEstimate(flops=rows, bytes_accessed=rows, transcendentals=0),
     )(rows_of, *others)
 
@@ -153,7 +153,7 @@
             jax.ShapeDtypeStruct((total, width), jnp.bfloat16),
             jax.ShapeDtypeStruct((1, total), jnp.float32),
         ],
-        compiler_params=pltpu.CompilerParams(vmem_limit_bytes=16 << 20),
+        compiler_params=pltpu.CompilerParams(vmem_limit_bytes=8 << 20),
         cost_estimate=pl.CostEstimate(flops=rows, bytes_accessed=rows, transcendentals=0),
     )(*[piece for block in holds for piece in block])
 
@@ -205,8 +205,8 @@
             jax.ShapeDtypeStruct((1, total), jnp.float32),
             jax.ShapeDtypeStruct((1, rows), jnp.float32),
         ],
-        compiler_params=pltpu.CompilerParams(vmem_limit_bytes=32 << 20),
-        cost_estimate=pl.CostEstimate(flops=8 * rows * total * width, bytes_accessed=rows, transcendentals=0),
+        compiler_params=pltpu.CompilerParams(vmem_limit_bytes=12 << 20),
+        cost_estimate=pl.CostEstimate(flops=rows * total * width // 2, bytes_accessed=rows, transcendentals=0),
     )(block, partner, held, row)
 
 
@@ -217,7 +217,7 @@
         functools.partial(line_kernel, rows, span, len(pieces), together),
         out_shape=outs + [jax.ShapeDtypeStruct((1, 2 * rows), jnp.float32)],
         scratch_shapes=[pltpu.VMEM((rows, width), jnp.bfloat16)],
-        compiler_params=pltpu.CompilerParams(vmem_limit_bytes=32 << 20),
+        compiler_params=pltpu.CompilerParams(vmem_limit_bytes=12 << 20),
         cost_estimate=pl.CostEstimate(flops=rows, bytes_accessed=rows, transcendentals=0),
     )(*pieces, second, held, row, best)
     return bests, found

time: 46.1 us -> 46.1 us (level)
  starting transfers between devices: 24.3 us -> 22.1 us
  waiting for transfers between devices: 11.3 us -> 13.4 us
    ppermute x2, waiting for transfers between devices: 3.62 us -> 5.99 us  [shards(): from_corner = [lax.ppermute(part, BOTH, second) for part in from_first]]
    ppermute x2, starting transfers between devices: 1.14 us -> 0.07 us  [shards(): lax.ppermute(piece, BOTH, other_core)]
    ppermute x1, starting transfers between devices: 0.01 us -> 1.01 us  [shards(): other_codes = lax.ppermute(codes_of, BOTH, other_core)]
    ppermute x1, starting transfers between devices: 1.46 us -> 0.51 us  [shards(): from_second = [lax.ppermute(block, BOTH, second)]]
    ppermute x1, starting transfers between devices: 0.84 us -> 0.07 us  [shards(): second_far = lax.ppermute(second_near, BOTH, other_core)]
    ppermute x2, waiting for transfers between devices: 4 us -> 3.43 us  [shards(): from_first = [lax.ppermute(part, BOTH, first) for part in parts]]
where the time goes in v13:
time: 46.1 us; the launch traced here: 45.8 us
  starting transfers between devices  22.1 us (48%)
  waiting for transfers between devices  13.4 us (29%)
  Pallas kernels  6.22 us (13%)
  other arithmetic  2.07 us (4%)
  local copies, waits for them, and re-layouts  1.8 us (4%)
    ppermute x2, waiting for transfers between devices, shards(): from_corner = [lax.ppermute(part, BOTH, second) for part in from_first]  5.99 us
    ppermute x1, starting transfers between devices, shards(): raw = [lax.ppermute(embeddings, BOTH, pairs) for pairs in rounds]  5.49 us
    ppermute x2, starting transfers between devices, shards(): from_corner = [lax.ppermute(part, BOTH, second) for part in from_first]  4.13 us
    pallas_call x2, Pallas kernels, line(): pl.pallas_call(functools.partial(line_kernel, rows, span, len(pieces), to...  3.91 us
    ppermute x2, waiting for transfers between devices, shards(): from_first = [lax.ppermute(part, BOTH, first) for part in parts]  3.43 us
    ppermute x2, starting transfers between devices, shards(): from_first = [lax.ppermute(part, BOTH, first) for part in parts]  3.05 us
    ppermute x1, waiting for transfers between devices, shards(): lax.ppermute(kept[:, 2 * at * rows:2 * (at + 1) * rows], BOTH, back(pairs))  2.69 us
    ppermute x1, starting transfers between devices, shards(): near_other = [lax.ppermute(partner, BOTH, pairs) for pairs in rounds]  1.92 us
  transfers between devices with their start and end apart: 17, of which 6 were waited for; matrix products, arithmetic and copies ran while one was open for 3% of the time, Pallas kernels for 9%

profile of v13, /device:TPU:0, one launch (start us, length us, event | category | flops | bytes accessed | tf_op | source)
XLA Modules:
  0.0 45.8 jit_solution(13090658999018575593)
XLA Ops:
  0.5 5.5 %collective-permute-start.5 = (bf16[320,768]{1,0:T(8,128)(2,1)}, bf16[320,768]{1,0:T(8,128)(2,1)S(1)}, u32[]{:S(2)}, u32[]{:S(2)}) collective-permute-start(bf16[320,768]{1,0:T(8,128)(2,1)} %embeddings.1), channel_id=1, source_target_pairs={{0,4},{6,2},{2,0},{1,7},{7,5},{5,3},{8,12},{14,10},{10,8},{9,15},{... | collective-permute-start | bytes 1474568 | tf_op jit(solution)/shard_map/ppermute | solution.py:281
  5.9 0.7 %multiply_reduce_fusion = s32[320]{0:T(512)S(1)} fusion(s32[320,1]{0,1:T(1,128)} %param.4), kind=kLoop, calls=%fused_computation.6 | loop fusion | flops 640 | bytes 2560 | tf_op jit(solution)/shard_map/mul | solution.py:279
  6.6 0.7 %add.15.named = s32[320]{0:T(512)S(1)} add(s32[320]{0:T(512)S(1)} %multiply_reduce_fusion, s32[320]{0:T(512)} %param.5) | non-fusion elementwise | flops 320 | bytes 3840 | tf_op jit(solution)/shard_map/add | solution.py:279
  7.3 1.0 %copy-done = bf16[320,768]{1,0:T(8,128)(2,1)S(1)} copy-done((bf16[320,768]{1,0:T(8,128)(2,1)S(1)}, bf16[320,768]{1,0:T(8,128)(2,1)}, u32[]{:S(2)}) %copy-start) | copy-done | bytes 491544
  8.5 1.6 %collective-permute-start = (bf16[160,768]{1,0:T(8,128)(2,1)S(1)}, bf16[160,768]{1,0:T(8,128)(2,1)S(1)}, u32[]{:S(2)}, u32[]{:S(2)}) collective-permute-start(bf16[160,768]{1,0:T(8,128)(2,1)S(1)} %get-tuple-element.28), channel_id=1, source_target_pairs={{0,8},{1,17},{2,10},{3,19},{4,12},{5,21},{6,14},{7,23},{8,0},{9,25... | collective-permute-start | bytes 737288 | tf_op jit(solution)/shard_map/ppermute | solution.py:288
  10.1 1.0 %collective-permute-start.9 = (bf16[16,768]{1,0:T(8,128)(2,1)S(1)}, bf16[16,768]{1,0:T(8,128)(2,1)S(1)}, u32[]{:S(2)}, u32[]{:S(2)}) collective-permute-start(bf16[16,768]{1,0:T(8,128)(2,1)S(1)} %get-tuple-element.35.other_codes), channel_id=1, source_target_pairs={{0,1},{1,0},{2,3},{3,2},{4,5},{5,4},{6,7},{7,6},{8,9},{9,8},{10,11... | collective-permute-start | bytes 73736 | tf_op jit(solution)/shard_map/ppermute | solution.py:290
  11.1 1.5 %collective-permute-start.1 = (bf16[176,768]{1,0:T(8,128)(2,1)S(1)}, bf16[176,768]{1,0:T(8,128)(2,1)S(1)}, u32[]{:S(2)}, u32[]{:S(2)}) collective-permute-start(bf16[176,768]{1,0:T(8,128)(2,1)S(1)} %get-tuple-element.29), channel_id=1, source_target_pairs={{0,8},{1,17},{2,10},{3,19},{4,12},{5,21},{6,14},{7,23},{8,0},{9,25... | collective-permute-start | bytes 811016 | tf_op jit(solution)/shard_map/ppermute | solution.py:288
  12.6 0.5 %collective-permute-start.2 = (bf16[336,768]{1,0:T(8,128)(2,1)S(1)}, bf16[336,768]{1,0:T(8,128)(2,1)S(1)}, u32[]{:S(2)}, u32[]{:S(2)}) collective-permute-start(bf16[336,768]{1,0:T(8,128)(2,1)S(1)} %get-tuple-element.27.refs_0_.block), channel_id=1, source_target_pairs={{0,16},{1,9},{2,18},{3,11},{4,20},{5,13},{6,22},{7,15},{8,24},{9,1... | collective-permute-start | bytes 1548296 | tf_op jit(solution)/shard_map/ppermute | solution.py:289
  13.3 1.9 %collective-permute-start.10 = (bf16[336,768]{1,0:T(8,128)(2,1)S(1)}, bf16[336,768]{1,0:T(8,128)(2,1)S(1)}, u32[]{:S(2)}, u32[]{:S(2)}) collective-permute-start(bf16[336,768]{1,0:T(8,128)(2,1)S(1)} %shard_map.40.partner), channel_id=1, source_target_pairs={{0,4},{6,2},{2,0},{1,7},{7,5},{5,3},{8,12},{14,10},{10,8},{9,15},{... | collective-permute-start | bytes 1548296 | tf_op jit(solution)/shard_map/ppermute | solution.py:292
  15.2 1.8 %collective-permute-start.3 = (bf16[160,768]{1,0:T(8,128)(2,1)S(1)}, bf16[160,768]{1,0:T(8,128)(2,1)S(1)}, u32[]{:S(2)}, u32[]{:S(2)}) collective-permute-start(bf16[160,768]{1,0:T(8,128)(2,1)S(1)} %collective-permute-done.refs_1_), channel_id=1, source_target_pairs={{0,16},{1,9},{2,18},{3,11},{4,20},{5,13},{6,22},{7,15},{8,24},{9,1... | collective-permute-start | bytes 737288 | tf_op jit(solution)/shard_map/ppermute | solution.py:293
  17.0 3.4 %collective-permute-done.1.refs_2_ = bf16[176,768]{1,0:T(8,128)(2,1)S(1)} collective-permute-done((bf16[176,768]{1,0:T(8,128)(2,1)S(1)}, bf16[176,768]{1,0:T(8,128)(2,1)S(1)}, u32[]{:S(2)}, u32[]{:S(2)}) %collective-permute-start.1) | collective-permute-done | bytes 270368 | tf_op jit(solution)/shard_map/ppermute | solution.py:288
  20.4 2.4 %collective-permute-start.4 = (bf16[176,768]{1,0:T(8,128)(2,1)S(1)}, bf16[176,768]{1,0:T(8,128)(2,1)S(1)}, u32[]{:S(2)}, u32[]{:S(2)}) collective-permute-start(bf16[176,768]{1,0:T(8,128)(2,1)S(1)} %collective-permute-done.1.refs_2_), channel_id=1, source_target_pairs={{0,16},{1,9},{2,18},{3,11},{4,20},{5,13},{6,22},{7,15},{8,24},{9,1... | collective-permute-start | bytes 811016 | tf_op jit(solution)/shard_map/ppermute | solution.py:293
  23.1 3.1 %collective-permute-done.3.refs_4_ = bf16[160,768]{1,0:T(8,128)(2,1)S(1)} collective-permute-done((bf16[160,768]{1,0:T(8,128)(2,1)S(1)}, bf16[160,768]{1,0:T(8,128)(2,1)S(1)}, u32[]{:S(2)}, u32[]{:S(2)}) %collective-permute-start.3) | collective-permute-done | bytes 245792 | tf_op jit(solution)/shard_map/ppermute | solution.py:293
  26.2 2.9 %collective-permute-done.4.refs_5_ = bf16[176,768]{1,0:T(8,128)(2,1)S(1)} collective-permute-done((bf16[176,768]{1,0:T(8,128)(2,1)S(1)}, bf16[176,768]{1,0:T(8,128)(2,1)S(1)}, u32[]{:S(2)}, u32[]{:S(2)}) %collective-permute-start.4) | collective-permute-done | bytes 270368 | tf_op jit(solution)/shard_map/ppermute | solution.py:293
  29.2 0.7 %copy-done.1 = bf16[160,768]{1,0:T(8,128)(2,1)} copy-done((bf16[160,768]{1,0:T(8,128)(2,1)}, bf16[160,768]{1,0:T(8,128)(2,1)S(1)}, u32[]{:S(2)}) %copy-start.1) | copy-done | bytes 245784
  29.9 1.6 %shard_map.41 = (f32[1,1280]{1,0:T(1,128)S(1)}, f32[1,320]{1,0:T(1,128)S(1)}) custom-call(bf16[336,768]{1,0:T(8,128)(2,1)S(1)} %get-tuple-element.27.refs_0_.block, bf16[336,768]{1,0:T(8,128)(2,1)S(1)} %shard_map.40.partner, bf16[1280,768]{1,0:T(8,128)(2,1)S(1)} %get-tuple-element.36.held.refs_2_.refs_3_, f32[1,1280]{1,0:T(1,128)S(1)} %get-tuple-element.37.row.refs_3_.refs_4_), custom_call_target="tpu_custom_call" | custom-call | flops 157286400 | bytes 320 | tf_op jit(solution)/shard_map/pallas_call | solution.py:202
  31.7 1.9 %shard_map.42 = (f32[1,1280]{1,0:T(1,128)S(1)}, f32[1,640]{1,0:T(1,128)S(1)}) custom-call(bf16[320,768]{1,0:T(8,128)(2,1)S(1)} %get-tuple-element.40.refs_0_, bf16[336,768]{1,0:T(8,128)(2,1)S(1)} %collective-permute-done.10.refs_1_, bf16[1280,768]{1,0:T(8,128)(2,1)S(1)} %get-tuple-element.36.held.refs_2_.refs_3_, ...), custom_call_target="tpu_custom_call" | custom-call | flops 320 | bytes 320 | tf_op jit(solution)/shard_map/pallas_call | solution.py:216
  33.7 2.0 %shard_map.43 = (f32[1,320]{1,0:T(1,128)S(1)}, f32[1,640]{1,0:T(1,128)S(1)}, f32[1,320]{1,0:T(1,128)S(1)}, f32[1,640]{1,0:T(1,128)S(1)}) custom-call(bf16[160,768]{1,0:T(8,128)(2,1)S(1)} %copy-done.2, bf16[160,768]{1,0:T(8,128)(2,1)S(1)} %copy-done.4, bf16[336,768]{1,0:T(8,128)(2,1)S(1)} %collective-permute-done.11.refs_2_, ...), custom_call_target="tpu_custom_call" | custom-call | flops 320 | bytes 320 | tf_op jit(solution)/shard_map/pallas_call | solution.py:216
  36.1 1.5 %collective-permute-start.15 = (f32[1,640]{1,0:T(1,128)S(1)}, f32[1,640]{1,0:T(1,128)S(1)}, u32[]{:S(2)}, u32[]{:S(2)}) collective-permute-start(f32[1,640]{1,0:T(1,128)S(1)} %get-tuple-element.47), channel_id=1, source_target_pairs={{0,8},{1,17},{2,10},{3,19},{4,12},{5,21},{6,14},{7,23},{8,0},{9,25... | collective-permute-start | bytes 7688 | tf_op jit(solution)/shard_map/ppermute | solution.py:331
  37.6 1.9 %collective-permute-start.13 = (f32[1,640]{1,0:T(1,128)S(1)}, f32[1,640]{1,0:T(1,128)S(1)}, u32[]{:S(2)}, u32[]{:S(2)}) collective-permute-start(f32[1,640]{1,0:T(1,128)S(1)} %max.22), channel_id=1, source_target_pairs={{4,0},{2,6},{0,2},{7,1},{5,7},{3,5},{12,8},{10,14},{8,10},{15,9},{... | collective-permute-start | bytes 7688 | tf_op jit(solution)/shard_map/ppermute | solution.py:326
  39.8 1.5 %collective-permute-start.16 = (f32[1,320]{1,0:T(1,128)S(1)}, f32[1,320]{1,0:T(1,128)S(1)}, u32[]{:S(2)}, u32[]{:S(2)}) collective-permute-start(f32[1,320]{1,0:T(1,128)S(1)} %slice_maximum_fusion), channel_id=1, source_target_pairs={{0,16},{1,9},{2,18},{3,11},{4,20},{5,13},{6,22},{7,15},{8,24},{9,1... | collective-permute-start | bytes 3848 | tf_op jit(solution)/shard_map/ppermute | solution.py:334
  41.3 2.7 %collective-permute-done.13 = f32[1,640]{1,0:T(1,128)S(1)} collective-permute-done((f32[1,640]{1,0:T(1,128)S(1)}, f32[1,640]{1,0:T(1,128)S(1)}, u32[]{:S(2)}, u32[]{:S(2)}) %collective-permute-start.13) | collective-permute-done | bytes 2592 | tf_op jit(solution)/shard_map/ppermute | solution.py:326
  44.1 1.1 %collective-permute-done.14 = f32[1,320]{1,0:T(1,128)S(1)} collective-permute-done((f32[1,320]{1,0:T(1,128)S(1)}, f32[1,320]{1,0:T(1,128)S(1)}, u32[]{:S(2)}, u32[]{:S(2)}) %collective-permute-start.14) | collective-permute-done | bytes 1312 | tf_op jit(solution)/shard_map/ppermute | solution.py:330
  45.2 0.6 %fusion.2 = f32[320]{0:T(512)} fusion(f32[1,320]{1,0:T(1,128)S(1)} %collective-permute-done.16, f32[1,640]{1,0:T(1,128)S(1)} %collective-permute-done.15, f32[1,320]{1,0:T(1,128)S(1)} %collective-permute-done.14, f32[1,640]{1,0:T(1,128)S(1)} %broadcast_select_fusion, f32[1,320]{1,0:T(1,128)S(1)} %get-tuple-element.43, f32[1,320]{1,0:T(1,128)S(1)} %get-tuple-element.44), kind=kLoop, calls=%fused_computation.7 | loop fusion | flops 1600 | bytes 8960 | tf_op jit(solution)/shard_map/max | solution.py:335
  (34 shorter events, 2.1 us)
Async XLA Ops:
  0.0 13.1 %collective-permute-start.8 = (bf16[320,768]{1,0:T(8,128)(2,1)}, bf16[320,768]{1,0:T(8,128)(2,1)S(1)}, u32[]{:S(2)}, u32[]{:S(2)}) collective-permute-start(bf16[320,768]{1,0:T(8,128)(2,1)} %embeddings.1), channel_id=1, source_target_pairs={{0,1},{1,0},{2,3},{3,2},{4,5},{5,4},{6,7},{7,6},{8,9},{9,8},{10,11... | collective-permute-start | bytes 1474568 | tf_op jit(solution)/shard_map/ppermute | solution.py:280
  0.5 22.4 %collective-permute-start.5 = (bf16[320,768]{1,0:T(8,128)(2,1)}, bf16[320,768]{1,0:T(8,128)(2,1)S(1)}, u32[]{:S(2)}, u32[]{:S(2)}) collective-permute-start(bf16[320,768]{1,0:T(8,128)(2,1)} %embeddings.1), channel_id=1, source_target_pairs={{0,4},{6,2},{2,0},{1,7},{7,5},{5,3},{8,12},{14,10},{10,8},{9,15},{... | collective-permute-start | bytes 1474568 | tf_op jit(solution)/shard_map/ppermute | solution.py:281
  7.3 1.0 %copy-start = (bf16[320,768]{1,0:T(8,128)(2,1)S(1)}, bf16[320,768]{1,0:T(8,128)(2,1)}, u32[]{:S(2)}) copy-start(bf16[320,768]{1,0:T(8,128)(2,1)} %embeddings.1) | copy-start | bytes 1474564
  8.5 6.7 %collective-permute-start = (bf16[160,768]{1,0:T(8,128)(2,1)S(1)}, bf16[160,768]{1,0:T(8,128)(2,1)S(1)}, u32[]{:S(2)}, u32[]{:S(2)}) collective-permute-start(bf16[160,768]{1,0:T(8,128)(2,1)S(1)} %get-tuple-element.28), channel_id=1, source_target_pairs={{0,8},{1,17},{2,10},{3,19},{4,12},{5,21},{6,14},{7,23},{8,0},{9,25... | collective-permute-start | bytes 737288 | tf_op jit(solution)/shard_map/ppermute | solution.py:288
  10.1 2.5 %collective-permute-start.9 = (bf16[16,768]{1,0:T(8,128)(2,1)S(1)}, bf16[16,768]{1,0:T(8,128)(2,1)S(1)}, u32[]{:S(2)}, u32[]{:S(2)}) collective-permute-start(bf16[16,768]{1,0:T(8,128)(2,1)S(1)} %get-tuple-element.35.other_codes), channel_id=1, source_target_pairs={{0,1},{1,0},{2,3},{3,2},{4,5},{5,4},{6,7},{7,6},{8,9},{9,8},{10,11... | collective-permute-start | bytes 73736 | tf_op jit(solution)/shard_map/ppermute | solution.py:290
  11.1 9.3 %collective-permute-start.1 = (bf16[176,768]{1,0:T(8,128)(2,1)S(1)}, bf16[176,768]{1,0:T(8,128)(2,1)S(1)}, u32[]{:S(2)}, u32[]{:S(2)}) collective-permute-start(bf16[176,768]{1,0:T(8,128)(2,1)S(1)} %get-tuple-element.29), channel_id=1, source_target_pairs={{0,8},{1,17},{2,10},{3,19},{4,12},{5,21},{6,14},{7,23},{8,0},{9,25... | collective-permute-start | bytes 811016 | tf_op jit(solution)/shard_map/ppermute | solution.py:288
  12.6 13.6 %collective-permute-start.2 = (bf16[336,768]{1,0:T(8,128)(2,1)S(1)}, bf16[336,768]{1,0:T(8,128)(2,1)S(1)}, u32[]{:S(2)}, u32[]{:S(2)}) collective-permute-start(bf16[336,768]{1,0:T(8,128)(2,1)S(1)} %get-tuple-element.27.refs_0_.block), channel_id=1, source_target_pairs={{0,16},{1,9},{2,18},{3,11},{4,20},{5,13},{6,22},{7,15},{8,24},{9,1... | collective-permute-start | bytes 1548296 | tf_op jit(solution)/shard_map/ppermute | solution.py:289
  13.3 18.2 %collective-permute-start.10 = (bf16[336,768]{1,0:T(8,128)(2,1)S(1)}, bf16[336,768]{1,0:T(8,128)(2,1)S(1)}, u32[]{:S(2)}, u32[]{:S(2)}) collective-permute-start(bf16[336,768]{1,0:T(8,128)(2,1)S(1)} %shard_map.40.partner), channel_id=1, source_target_pairs={{0,4},{6,2},{2,0},{1,7},{7,5},{5,3},{8,12},{14,10},{10,8},{9,15},{... | collective-permute-start | bytes 1548296 | tf_op jit(solution)/shard_map/ppermute | solution.py:292
  15.2 10.9 %collective-permute-start.3 = (bf16[160,768]{1,0:T(8,128)(2,1)S(1)}, bf16[160,768]{1,0:T(8,128)(2,1)S(1)}, u32[]{:S(2)}, u32[]{:S(2)}) collective-permute-start(bf16[160,768]{1,0:T(8,128)(2,1)S(1)} %collective-permute-done.refs_1_), channel_id=1, source_target_pairs={{0,16},{1,9},{2,18},{3,11},{4,20},{5,13},{6,22},{7,15},{8,24},{9,1... | collective-permute-start | bytes 737288 | tf_op jit(solution)/shard_map/ppermute | solution.py:293
  20.4 8.6 %collective-permute-start.4 = (bf16[176,768]{1,0:T(8,128)(2,1)S(1)}, bf16[176,768]{1,0:T(8,128)(2,1)S(1)}, u32[]{:S(2)}, u32[]{:S(2)}) collective-permute-start(bf16[176,768]{1,0:T(8,128)(2,1)S(1)} %collective-permute-done.1.refs_2_), channel_id=1, source_target_pairs={{0,16},{1,9},{2,18},{3,11},{4,20},{5,13},{6,22},{7,15},{8,24},{9,1... | collective-permute-start | bytes 811016 | tf_op jit(solution)/shard_map/ppermute | solution.py:293
  23.0 6.2 %collective-permute-start.6 = (bf16[160,768]{1,0:T(8,128)(2,1)S(1)}, bf16[160,768]{1,0:T(8,128)(2,1)S(1)}, u32[]{:S(2)}, u32[]{:S(2)}) collective-permute-start(bf16[160,768]{1,0:T(8,128)(2,1)S(1)} %get-tuple-element.31), channel_id=1, source_target_pairs={{0,1},{1,0},{2,3},{3,2},{4,5},{5,4},{6,7},{7,6},{8,9},{9,8},{10,11... | collective-permute-start | bytes 737288 | tf_op jit(solution)/shard_map/ppermute | solution.py:298
  26.2 3.7 %collective-permute-start.7 = (bf16[160,768]{1,0:T(8,128)(2,1)S(1)}, bf16[160,768]{1,0:T(8,128)(2,1)S(1)}, u32[]{:S(2)}, u32[]{:S(2)}) collective-permute-start(bf16[160,768]{1,0:T(8,128)(2,1)S(1)} %get-tuple-element.32), channel_id=1, source_target_pairs={{0,1},{1,0},{2,3},{3,2},{4,5},{5,4},{6,7},{7,6},{8,9},{9,8},{10,11... | collective-permute-start | bytes 737288 | tf_op jit(solution)/shard_map/ppermute | solution.py:298
  29.2 0.7 %copy-start.1 = (bf16[160,768]{1,0:T(8,128)(2,1)}, bf16[160,768]{1,0:T(8,128)(2,1)S(1)}, u32[]{:S(2)}) copy-start(bf16[160,768]{1,0:T(8,128)(2,1)S(1)} %collective-permute-done.6.refs_0_) | copy-start | bytes 737284
  29.9 1.7 %copy-start.3 = (bf16[160,768]{1,0:T(8,128)(2,1)}, bf16[160,768]{1,0:T(8,128)(2,1)S(1)}, u32[]{:S(2)}) copy-start(bf16[160,768]{1,0:T(8,128)(2,1)S(1)} %collective-permute-done.7.refs_1_) | copy-start | bytes 737284
  31.6 2.1 %collective-permute-start.11 = (bf16[336,768]{1,0:T(8,128)(2,1)S(1)}, bf16[336,768]{1,0:T(8,128)(2,1)S(1)}, u32[]{:S(2)}, u32[]{:S(2)}) collective-permute-start(bf16[336,768]{1,0:T(8,128)(2,1)S(1)} %collective-permute-done.10.refs_1_), channel_id=1, source_target_pairs={{0,1},{1,0},{2,3},{3,2},{4,5},{5,4},{6,7},{7,6},{8,9},{9,8},{10,11... | collective-permute-start | bytes 1548296 | tf_op jit(solution)/shard_map/ppermute | solution.py:308
  31.7 2.0 %copy-start.2 = (bf16[160,768]{1,0:T(8,128)(2,1)S(1)}, bf16[160,768]{1,0:T(8,128)(2,1)}, u32[]{:S(2)}) copy-start(bf16[160,768]{1,0:T(8,128)(2,1)} %copy-done.1) | copy-start | bytes 737284
  31.7 2.0 %copy-start.4 = (bf16[160,768]{1,0:T(8,128)(2,1)S(1)}, bf16[160,768]{1,0:T(8,128)(2,1)}, u32[]{:S(2)}) copy-start(bf16[160,768]{1,0:T(8,128)(2,1)} %copy-done.3) | copy-start | bytes 737284
  35.6 2.0 %collective-permute-start.12 = (f32[1,640]{1,0:T(1,128)S(1)}, f32[1,640]{1,0:T(1,128)S(1)}, u32[]{:S(2)}, u32[]{:S(2)}) collective-permute-start(f32[1,640]{1,0:T(1,128)S(1)} %get-tuple-element.46), channel_id=1, source_target_pairs={{0,1},{1,0},{2,3},{3,2},{4,5},{5,4},{6,7},{7,6},{8,9},{9,8},{10,11... | collective-permute-start | bytes 7688 | tf_op jit(solution)/shard_map/ppermute | solution.py:323
  36.1 3.6 %collective-permute-start.15 = (f32[1,640]{1,0:T(1,128)S(1)}, f32[1,640]{1,0:T(1,128)S(1)}, u32[]{:S(2)}, u32[]{:S(2)}) collective-permute-start(f32[1,640]{1,0:T(1,128)S(1)} %get-tuple-element.47), channel_id=1, source_target_pairs={{0,8},{1,17},{2,10},{3,19},{4,12},{5,21},{6,14},{7,23},{8,0},{9,25... | collective-permute-start | bytes 7688 | tf_op jit(solution)/shard_map/ppermute | solution.py:331
  37.6 6.4 %collective-permute-start.13 = (f32[1,640]{1,0:T(1,128)S(1)}, f32[1,640]{1,0:T(1,128)S(1)}, u32[]{:S(2)}, u32[]{:S(2)}) collective-permute-start(f32[1,640]{1,0:T(1,128)S(1)} %max.22), channel_id=1, source_target_pairs={{4,0},{2,6},{0,2},{7,1},{5,7},{3,5},{12,8},{10,14},{8,10},{15,9},{... | collective-permute-start | bytes 7688 | tf_op jit(solution)/shard_map/ppermute | solution.py:326
  39.8 4.3 %collective-permute-start.16 = (f32[1,320]{1,0:T(1,128)S(1)}, f32[1,320]{1,0:T(1,128)S(1)}, u32[]{:S(2)}, u32[]{:S(2)}) collective-permute-start(f32[1,320]{1,0:T(1,128)S(1)} %slice_maximum_fusion), channel_id=1, source_target_pairs={{0,16},{1,9},{2,18},{3,11},{4,20},{5,13},{6,22},{7,15},{8,24},{9,1... | collective-permute-start | bytes 3848 | tf_op jit(solution)/shard_map/ppermute | solution.py:334
  44.1 1.2 %collective-permute-start.14 = (f32[1,320]{1,0:T(1,128)S(1)}, f32[1,320]{1,0:T(1,128)S(1)}, u32[]{:S(2)}, u32[]{:S(2)}) collective-permute-start(f32[1,320]{1,0:T(1,128)S(1)} %slice.17), channel_id=1, source_target_pairs={{0,1},{1,0},{2,3},{3,2},{4,5},{5,4},{6,7},{7,6},{8,9},{9,8},{10,11... | collective-permute-start | bytes 3848 | tf_op jit(solution)/shard_map/ppermute | solution.py:330

commit v14 on v13

--- a/solution.py
+++ b/solution.py
@@ -41,18 +41,17 @@
         out[...] = block[top : top + out.shape[0], :]
 
 
-def prepare_kernel(span, embeddings, named, block, *parts_out):
+def prepare_kernel(span, embeddings, named, block, codes_out, *parts_out):
     rows, width = embeddings.shape
     unit_rows(embeddings, block)
     names = named[...].reshape(1, rows)
     keys = names & (span - 1)
     parts = [keys >> 8, keys & 255, names >> (span.bit_length() - 1)]
     parts = [part.astype(jnp.float32) for part in parts]
-    parts = jnp.concatenate(parts + [jnp.zeros((EXTRA - 3, rows), jnp.float32)], axis=0)
+    parts = jnp.concatenate(parts + [jnp.zeros((EXTRA - CODES, rows), jnp.float32)], axis=0)
     parts = jnp.concatenate([parts, jnp.zeros((EXTRA, width - rows), jnp.float32)], axis=1)
     block[rows : rows + EXTRA, :] = parts.astype(jnp.bfloat16)
-    codes_out, *parts_out = parts_out
-    codes_out[0:EXTRA, :] = block[rows : rows + EXTRA, :]
+    codes_out[...] = block[rows : rows + EXTRA, :]
     give_parts(block, parts_out)
 
 
@@ -94,16 +93,17 @@
     partial = [jnp.full((CHUNK, LANES), -1.0, jnp.float32) for _ in starts]
     best_held = []
     for at in range(0, held.shape[0], TILE):
+        tile = min(TILE, held.shape[0] - at)
         sims = lax.dot_general(
             units,
-            held[at : at + TILE, :],
+            held[at : at + tile, :],
             (((1,), (1,)), ((), ())),
             preferred_element_type=jnp.float32,
         )
-        best = [jnp.full((CHUNK, LANES), -1.0, jnp.float32) for _ in range(0, TILE, LANES)]
+        best = [jnp.full((CHUNK, LANES), -1.0, jnp.float32) for _ in range(0, tile, LANES)]
         for place, top in enumerate(starts):
             mine = column[top : top + CHUNK]
-            for lane in range(0, TILE, LANES):
+            for lane in range(0, tile, LANES):
                 part = sims[top : top + CHUNK, lane : lane + LANES]
                 gap = mine - held_codes[:, at + lane : at + lane + LANES]
                 if to_block and to_held:
@@ -134,28 +134,40 @@
         whole[top + rows - height : top + rows, :] = last[0:height, :]
 
 
-def gather_kernel(rows, span, lengths, *refs):
-    *pieces, held, row = refs
-    holds = regrouped(pieces, lengths)
+def hold(holds, held, rows, span):
     for at, block in enumerate(holds):
         assemble(held, at * rows, rows, block, EXTRA)
-    row[...] = jnp.concatenate(
-        [codes(block[-1], rows, span)[:, :rows] for block in holds], axis=1
-    )
-
-
-def gather(holds, rows, span):
-    width = holds[0][0].shape[1]
+    row = [codes(block[-1], rows, span)[:, :rows] for block in holds]
+    rest = held.shape[0] - len(holds) * rows
+    if rest:
+        held[len(holds) * rows :, :] = jnp.zeros((rest, held.shape[1]), held.dtype)
+        row.append(jnp.zeros((1, rest), jnp.float32))
+    return jnp.concatenate(row, axis=1)
+
+
+def gather_kernel(rows, span, lengths, *refs):
+    *pieces, held, row, joined = refs
+    *holds, far = regrouped(pieces, lengths)
+    row[...] = hold(holds, held, rows, span)
+    assemble(joined, 0, rows, far, 0)
+
+
+def gather(holds, far, rows, span):
+    width = far[0].shape[1]
     total = len(holds) * rows
+    parts = [*holds, far]
     return pl.pallas_call(
-        functools.partial(gather_kernel, rows, span, [len(block) for block in holds]),
+        functools.partial(gather_kernel, rows, span, [len(part) for part in parts]),
         out_shape=[
             jax.ShapeDtypeStruct((total, width), jnp.bfloat16),
             jax.ShapeDtypeStruct((1, total), jnp.float32),
+            jax.ShapeDtypeStruct((rows, width), jnp.bfloat16),
         ],
         compiler_params=pltpu.CompilerParams(vmem_limit_bytes=8 << 20),
-        cost_estimate=pl.CostEstimate(flops=rows, bytes_accessed=rows, transcendentals=0),
-    )(*[piece for block in holds for piece in block])
+        cost_estimate=pl.CostEstimate(
+            flops=rows * total * width // 4, bytes_accessed=rows, transcendentals=0
+        ),
+    )(*[piece for part in parts for piece in part])
 
 
 def regrouped(flat, lengths):
@@ -163,20 +175,25 @@
     return [[next(flat) for _ in range(length)] for length in lengths]
 
 
-def plane_kernel(rows, span, block, partner, held, row, best, mine):
-    mine[...], _ = meet(
-        block[0:rows, :], codes(block, rows, span), rows, span, held, row[...], *OWN
-    )
-    _, best[...] = meet(
-        partner[0:rows, :], codes(partner, rows, span), rows, span, held, row[...], *HELD
-    )
-
-
-def line_kernel(rows, span, count, together, *refs):
-    pieces, (second, held, row, best, *outs, found, joined) = refs[:count], refs[count:]
-    if count > 1:
-        assemble(joined, 0, rows, pieces, 0)
-    units = joined if count > 1 else pieces[0]
+def plane_kernel(rows, span, lengths, block, partner, *refs):
+    *pieces, best, mine, held = refs
+    row = hold(regrouped(pieces, lengths), held, rows, span)
+    mine[...], _ = meet(block[0:rows, :], codes(block, rows, span), rows, span, held, row, *OWN)
+    _, theirs = meet(partner[0:rows, :], codes(partner, rows, span), rows, span, held, row, *HELD)
+    best[...] = theirs[:, : best.shape[1]]
+
+
+def rest_kernel(rows, span, block, partner, held, row, best, mine):
+    count = best.shape[1]
+    start = held.shape[0] - up(count, LANES)
+    held, row = held.at[start:, :], row[:, start:]
+    mine[...], _ = meet(block[0:rows, :], codes(block, rows, span), rows, span, held, row, *OWN)
+    _, theirs = meet(partner[0:rows, :], codes(partner, rows, span), rows, span, held, row, *HELD)
+    best[...] = theirs[:, row.shape[1] - count :]
+
+
+def line_kernel(rows, span, together, count, units, second, held, row, *refs):
+    bests, outs, found = refs[:count], refs[count:-1], refs[-1]
     results = [
         meet(
             block[0:rows, :],
@@ -190,36 +207,49 @@
         for block, place in ((units, CODES), (second, 0))
     ]
     found[...] = jnp.concatenate([mine for mine, _ in results], axis=1)
-    best = jnp.maximum(best[...], jnp.maximum(results[0][1], results[1][1]))
+    best = jnp.concatenate([best[...] for best in bests], axis=1)
+    best = jnp.maximum(best, jnp.maximum(results[0][1], results[1][1]))
     for out, places in zip(outs, together):
         out[...] = jnp.concatenate(
             [best[:, place * rows : (place + 1) * rows] for place in places], axis=1
         )
 
 
-def plane(block, partner, held, row, rows, span):
-    total, width = held.shape
+def plane(block, partner, holds, rows, span):
+    width = block.shape[1]
+    total = len(holds) * rows
     return pl.pallas_call(
-        functools.partial(plane_kernel, rows, span),
+        functools.partial(plane_kernel, rows, span, [len(part) for part in holds]),
         out_shape=[
             jax.ShapeDtypeStruct((1, total), jnp.float32),
             jax.ShapeDtypeStruct((1, rows), jnp.float32),
         ],
+        scratch_shapes=[pltpu.VMEM((up(total, LANES), width), jnp.bfloat16)],
         compiler_params=pltpu.CompilerParams(vmem_limit_bytes=12 << 20),
-        cost_estimate=pl.CostEstimate(flops=rows * total * width // 2, bytes_accessed=rows, transcendentals=0),
+        cost_estimate=pl.CostEstimate(flops=rows, bytes_accessed=rows, transcendentals=0),
+    )(block, partner, *[piece for part in holds for piece in part])
+
+
+def plane_rest(block, partner, held, row, count, rows, span):
+    return pl.pallas_call(
+        functools.partial(rest_kernel, rows, span),
+        out_shape=[
+            jax.ShapeDtypeStruct((1, count), jnp.float32),
+            jax.ShapeDtypeStruct((1, rows), jnp.float32),
+        ],
+        compiler_params=pltpu.CompilerParams(vmem_limit_bytes=12 << 20),
+        cost_estimate=pl.CostEstimate(flops=rows, bytes_accessed=rows, transcendentals=0),
     )(block, partner, held, row)
 
 
-def line(pieces, second, held, row, best, rows, span, together):
-    total, width = held.shape
+def line(units, second, held, row, bests, rows, span, together):
     outs = [jax.ShapeDtypeStruct((1, rows * len(some)), jnp.float32) for some in together]
     *bests, found = pl.pallas_call(
-        functools.partial(line_kernel, rows, span, len(pieces), together),
+        functools.partial(line_kernel, rows, span, together, len(bests)),
         out_shape=outs + [jax.ShapeDtypeStruct((1, 2 * rows), jnp.float32)],
-        scratch_shapes=[pltpu.VMEM((rows, width), jnp.bfloat16)],
         compiler_params=pltpu.CompilerParams(vmem_limit_bytes=12 << 20),
         cost_estimate=pl.CostEstimate(flops=rows, bytes_accessed=rows, transcendentals=0),
-    )(*pieces, second, held, row, best)
+    )(units, second, held, row, *bests)
     return bests, found
 
 
@@ -254,6 +284,7 @@
     other_core = everywhere(lambda p, g: (p, g ^ 1))
     first = everywhere(lambda p, g: (p ^ (1 + g % 2), g))
     second = everywhere(lambda p, g: (p ^ (2 - g % 2), g))
+    corner_pairs = everywhere(lambda p, g: (p ^ 3, g))
 
     rounds = line_rounds(chips)
     rounds += [[]] * (len(rounds) % 2)
@@ -276,9 +307,9 @@
         while span < rows * groups * members:
             span *= 2
         halves = (rows // 2, rows // 2 + EXTRA)
-        named = (cluster[:, 0] + 1) * span + order_key
         partner = lax.ppermute(embeddings, BOTH, other_core)
         raw = [lax.ppermute(embeddings, BOTH, pairs) for pairs in rounds]
+        named = (cluster[:, 0] + 1) * span + order_key
         block, codes_of, *parts = with_units(
             functools.partial(prepare_kernel, span),
             (rows + EXTRA, EXTRA, *halves),
@@ -298,40 +329,45 @@
         far = [[lax.ppermute(piece, BOTH, other_core) for piece in blocks[1:]] for blocks in near]
 
         results, kept, sent = [], [], []
-        held, row = gather([[block], from_first, from_second, from_corner], rows, span)
-        held, *far[0] = lax.optimization_barrier((held, *far[0]))
-        best, mine = plane(block, partner, held, row, rows, span)
+        best_two, mine = plane(block, partner, [[block], from_first], rows, span)
         results.append(mine)
-        whole, last = [tuple(range(groups))], [(0,), (1, 3), (2,)]
+        *from_corner, best_two = lax.optimization_barrier((*from_corner, best_two))
+        blocks = [[block], from_first, from_second, from_corner]
+        held, row, far_units = gather(blocks, far[0], rows, span)
+        best_rest, mine = plane_rest(block, partner, held, row, 2 * rows, rows, span)
+        results.append(mine)
+        bests = [best_two, best_rest]
+        far = [far_units] + [jnp.concatenate(pieces, axis=0) for pieces in far[1:]]
+        whole, last = [tuple(range(groups))], [(at,) for at in range(groups)]
         for at, second_near in enumerate(near_other):
-            second_near, best = lax.optimization_barrier((second_near, best))
+            second_near, *bests = lax.optimization_barrier((second_near, *bests))
             second_far = lax.ppermute(second_near, BOTH, other_core)
-            (best,), found = line(near[at][:1], second_near, held, row, best, rows, span, whole)
+            bests, found = line(near[at][0], second_near, held, row, bests, rows, span, whole)
             kept.append(found)
             bests, found = line(
                 far[at],
                 second_far,
                 held,
                 row,
-                best,
+                bests,
                 rows,
                 span,
                 last if at == len(rounds) - 1 else whole,
             )
-            best = bests[0]
             sent.append(found)
         sent = lax.ppermute(jnp.concatenate(sent, axis=1), BOTH, other_core)
         kept = jnp.maximum(jnp.concatenate(kept, axis=1), sent)
+        kept, *bests = lax.optimization_barrier((kept, *bests))
         for at, pairs in enumerate(rounds):
             found = lax.ppermute(kept[:, 2 * at * rows : 2 * (at + 1) * rows], BOTH, back(pairs))
             me = lax.axis_index(BOTH)
             sender = functools.reduce(jnp.logical_or, [me == source for source, _ in pairs])
             found = jnp.where(sender, found, -1.0)
             results += [found[:, :rows], lax.ppermute(found[:, rows:], BOTH, other_core)]
-        from_x = lax.ppermute(bests[1], BOTH, first)
-        results.append(from_x[:, :rows])
-        onward = jnp.maximum(bests[2], from_x[:, rows:])
-        results.append(lax.ppermute(onward, BOTH, second))
+        results += [
+            lax.ppermute(best, BOTH, pairs)
+            for best, pairs in zip(bests[1:], (first, second, corner_pairs))
+        ]
         return functools.reduce(jnp.maximum, results, bests[0]).reshape(rows)
 
     placed = (P(BOTH, None), P(BOTH, None), P(BOTH))

time: 46.1 us -> 46.6 us (1.011)
  waiting for transfers between devices: 13.4 us -> 15.4 us
  starting transfers between devices: 22.1 us -> 20.9 us
  local copies, waits for them, and re-layouts: 1.8 us -> 1.1 us
  Pallas kernels: 6.22 us -> 6.69 us
    ppermute x2 -> x3, waiting for transfers between devices: 0.17 us -> 3.48 us  [shards(): lax.ppermute(best, BOTH, pairs)]
    ppermute x1, waiting for transfers between devices: 2.69 us -> 0.34 us  [shards(): lax.ppermute(kept[:, 2 * at * rows:2 * (at + 1) * rows], BOTH, back(pairs))]
    ppermute x2, starting transfers between devices: 4.13 us -> 2.09 us  [shards(): from_corner = [lax.ppermute(part, BOTH, second) for part in from_first]]
    ppermute x1, waiting for transfers between devices: 1.13 us -> 0.01 us  [shards(): lax.ppermute(found[:, rows:], BOTH, other_core)]
    ppermute x1, starting transfers between devices: 0.51 us -> 1.52 us  [shards(): from_second = [lax.ppermute(block, BOTH, second)]]
    ppermute x2, starting transfers between devices: 3.05 us -> 2.09 us  [shards(): from_first = [lax.ppermute(part, BOTH, first) for part in parts]]
    ppermute x1, waiting for transfers between devices: 0.01 us -> 0.85 us  [shards(): other_codes = lax.ppermute(codes_of, BOTH, other_core)]
    ppermute x1, waiting for transfers between devices: 0.01 us -> 0.82 us  [shards(): sent = lax.ppermute(jnp.concatenate(sent, axis=1), BOTH, other_core)]
  transfers between devices with their start and end apart: 17 -> 18, of which waited for: 6 -> 8; matrix products, arithmetic and copies ran while one was open for 3% -> 3% of each run, Pallas kernels for 9% -> 10%
where the time goes in v14:
time: 46.6 us; the launch traced here: 46.3 us
  starting transfers between devices  20.9 us (45%)
  waiting for transfers between devices  15.4 us (33%)
  Pallas kernels  6.69 us (14%)
  other arithmetic  2 us (4%)
  local copies, waits for them, and re-layouts  1.1 us (2%)
    ppermute x2, waiting for transfers between devices, shards(): from_corner = [lax.ppermute(part, BOTH, second) for part in from_first]  6.04 us
    ppermute x1, starting transfers between devices, shards(): raw = [lax.ppermute(embeddings, BOTH, pairs) for pairs in rounds]  5.49 us
    pallas_call x2, Pallas kernels, line(): pl.pallas_call(functools.partial(line_kernel, rows, span, together, len(b...  3.95 us
    ppermute x2, waiting for transfers between devices, shards(): from_first = [lax.ppermute(part, BOTH, first) for part in parts]  3.8 us
    ppermute x3, starting transfers between devices, shards(): lax.ppermute(best, BOTH, pairs)  3.55 us
    ppermute x3, waiting for transfers between devices, shards(): lax.ppermute(best, BOTH, pairs)  3.48 us
    ppermute x1, starting transfers between devices, shards(): lax.ppermute(kept[:, 2 * at * rows:2 * (at + 1) * rows], BOTH, back(pairs))  2.38 us
    ppermute x2, starting transfers between devices, shards(): from_first = [lax.ppermute(part, BOTH, first) for part in parts]  2.09 us
  transfers between devices with their start and end apart: 18, of which 8 were waited for; matrix products, arithmetic and copies ran while one was open for 3% of the time, Pallas kernels for 10%

profile of v14, /device:TPU:0, one launch (start us, length us, event | category | flops | bytes accessed | tf_op | source)
XLA Modules:
  0.0 46.3 jit_solution(3121584521904610116)
XLA Ops:
  0.5 5.5 %collective-permute-start = (bf16[320,768]{1,0:T(8,128)(2,1)}, bf16[320,768]{1,0:T(8,128)(2,1)S(1)}, u32[]{:S(2)}, u32[]{:S(2)}) collective-permute-start(bf16[320,768]{1,0:T(8,128)(2,1)} %embeddings.1), channel_id=1, source_target_pairs={{0,4},{6,2},{2,0},{1,7},{7,5},{5,3},{8,12},{14,10},{10,8},{9,15},{... | collective-permute-start | bytes 1474568 | tf_op jit(solution)/shard_map/ppermute | solution.py:311
  5.9 0.7 %multiply_reduce_fusion = s32[320]{0:T(512)S(1)} fusion(s32[320,1]{0,1:T(1,128)} %param.4), kind=kLoop, calls=%fused_computation.5 | loop fusion | flops 640 | bytes 2560 | tf_op jit(solution)/shard_map/mul | solution.py:312
  6.6 0.7 %add.15.named = s32[320]{0:T(512)S(1)} add(s32[320]{0:T(512)S(1)} %multiply_reduce_fusion, s32[320]{0:T(512)} %param.5) | non-fusion elementwise | flops 320 | bytes 3840 | tf_op jit(solution)/shard_map/add | solution.py:312
  7.3 1.0 %copy-done = bf16[320,768]{1,0:T(8,128)(2,1)S(1)} copy-done((bf16[320,768]{1,0:T(8,128)(2,1)S(1)}, bf16[320,768]{1,0:T(8,128)(2,1)}, u32[]{:S(2)}) %copy-start) | copy-done | bytes 491544
  8.5 1.6 %collective-permute-start.4 = (bf16[160,768]{1,0:T(8,128)(2,1)S(1)}, bf16[160,768]{1,0:T(8,128)(2,1)S(1)}, u32[]{:S(2)}, u32[]{:S(2)}) collective-permute-start(bf16[160,768]{1,0:T(8,128)(2,1)S(1)} %get-tuple-element.39), channel_id=1, source_target_pairs={{0,8},{1,17},{2,10},{3,19},{4,12},{5,21},{6,14},{7,23},{8,0},{9,25... | collective-permute-start | bytes 737288 | tf_op jit(solution)/shard_map/ppermute | solution.py:319
  10.6 0.7 %collective-permute-start.2 = (bf16[16,768]{1,0:T(8,128)(2,1)S(1)}, bf16[16,768]{1,0:T(8,128)(2,1)S(1)}, u32[]{:S(2)}, u32[]{:S(2)}) collective-permute-start(bf16[16,768]{1,0:T(8,128)(2,1)S(1)} %get-tuple-element.38.other_codes), channel_id=1, source_target_pairs={{0,1},{1,0},{2,3},{3,2},{4,5},{5,4},{6,7},{7,6},{8,9},{9,8},{10,11... | collective-permute-start | bytes 73736 | tf_op jit(solution)/shard_map/ppermute | solution.py:321
  11.3 0.8 %collective-permute-done.2.codes_of = bf16[16,768]{1,0:T(8,128)(2,1)S(1)} collective-permute-done((bf16[16,768]{1,0:T(8,128)(2,1)S(1)}, bf16[16,768]{1,0:T(8,128)(2,1)S(1)}, u32[]{:S(2)}, u32[]{:S(2)}) %collective-permute-start.2) | collective-permute-done | bytes 24608 | tf_op jit(solution)/shard_map/ppermute | solution.py:321
  12.2 1.5 %collective-permute-start.8 = (bf16[336,768]{1,0:T(8,128)(2,1)S(1)}, bf16[336,768]{1,0:T(8,128)(2,1)S(1)}, u32[]{:S(2)}, u32[]{:S(2)}) collective-permute-start(bf16[336,768]{1,0:T(8,128)(2,1)S(1)} %get-tuple-element.41.block.refs_0_), channel_id=1, source_target_pairs={{0,16},{1,9},{2,18},{3,11},{4,20},{5,13},{6,22},{7,15},{8,24},{9,1... | collective-permute-start | bytes 1548296 | tf_op jit(solution)/shard_map/ppermute | solution.py:320
  13.9 1.9 %collective-permute-start.3 = (bf16[336,768]{1,0:T(8,128)(2,1)S(1)}, bf16[336,768]{1,0:T(8,128)(2,1)S(1)}, u32[]{:S(2)}, u32[]{:S(2)}) collective-permute-start(bf16[336,768]{1,0:T(8,128)(2,1)S(1)} %shard_map.39.partner), channel_id=1, source_target_pairs={{0,4},{6,2},{2,0},{1,7},{7,5},{5,3},{8,12},{14,10},{10,8},{9,15},{... | collective-permute-start | bytes 1548296 | tf_op jit(solution)/shard_map/ppermute | solution.py:323
  16.4 3.8 %collective-permute-done.6.refs_2_ = bf16[176,768]{1,0:T(8,128)(2,1)S(1)} collective-permute-done((bf16[176,768]{1,0:T(8,128)(2,1)S(1)}, bf16[176,768]{1,0:T(8,128)(2,1)S(1)}, u32[]{:S(2)}, u32[]{:S(2)}) %collective-permute-start.6) | collective-permute-done | bytes 270368 | tf_op jit(solution)/shard_map/ppermute | solution.py:319
  20.2 1.5 %collective-permute-start.7 = (bf16[176,768]{1,0:T(8,128)(2,1)S(1)}, bf16[176,768]{1,0:T(8,128)(2,1)S(1)}, u32[]{:S(2)}, u32[]{:S(2)}) collective-permute-start(bf16[176,768]{1,0:T(8,128)(2,1)S(1)} %collective-permute-done.6.refs_2_), channel_id=1, source_target_pairs={{0,16},{1,9},{2,18},{3,11},{4,20},{5,13},{6,22},{7,15},{8,24},{9,1... | collective-permute-start | bytes 811016 | tf_op jit(solution)/shard_map/ppermute | solution.py:324
  22.0 4.2 %collective-permute-done.5.refs_4_ = bf16[160,768]{1,0:T(8,128)(2,1)S(1)} collective-permute-done((bf16[160,768]{1,0:T(8,128)(2,1)S(1)}, bf16[160,768]{1,0:T(8,128)(2,1)S(1)}, u32[]{:S(2)}, u32[]{:S(2)}) %collective-permute-start.5) | collective-permute-done | bytes 245792 | tf_op jit(solution)/shard_map/ppermute | solution.py:324
  26.2 1.0 %shard_map.40 = (f32[1,640]{1,0:T(1,128)S(1)}, f32[1,320]{1,0:T(1,128)S(1)}) custom-call(bf16[336,768]{1,0:T(8,128)(2,1)S(1)} %get-tuple-element.41.block.refs_0_, bf16[336,768]{1,0:T(8,128)(2,1)S(1)} %shard_map.39.partner, bf16[336,768]{1,0:T(8,128)(2,1)S(1)} %get-tuple-element.41.block.refs_0_, bf16[160,768]{1,0:T(8,128)(2,1)S(1)} %collective-permute-done.4.refs_1_, ...), custom_call_target="tpu_custom_call" | custom-call | flops 320 | bytes 320 | tf_op jit(solution)/shard_map/pallas_call | solution.py:221
  27.2 1.9 %collective-permute-done.7.refs_5_ = bf16[176,768]{1,0:T(8,128)(2,1)S(1)} collective-permute-done((bf16[176,768]{1,0:T(8,128)(2,1)S(1)}, bf16[176,768]{1,0:T(8,128)(2,1)S(1)}, u32[]{:S(2)}, u32[]{:S(2)}) %collective-permute-start.7) | collective-permute-done | bytes 270368 | tf_op jit(solution)/shard_map/ppermute | solution.py:324
  29.2 1.0 %shard_map.42 = (f32[1,640]{1,0:T(1,128)S(1)}, f32[1,320]{1,0:T(1,128)S(1)}) custom-call(bf16[336,768]{1,0:T(8,128)(2,1)S(1)} %get-tuple-element.41.block.refs_0_, bf16[336,768]{1,0:T(8,128)(2,1)S(1)} %shard_map.39.partner, bf16[1280,768]{1,0:T(8,128)(2,1)S(1)} %get-tuple-element.48.held, f32[1,1280]{1,0:T(1,128)S(1)} %get-tuple-element.49.row), custom_call_target="tpu_custom_call" | custom-call | flops 320 | bytes 320 | tf_op jit(solution)/shard_map/pallas_call | solution.py:234
  30.4 2.0 %shard_map.43 = (f32[1,1280]{1,0:T(1,128)S(1)}, f32[1,640]{1,0:T(1,128)S(1)}) custom-call(bf16[320,768]{1,0:T(8,128)(2,1)S(1)} %get-tuple-element.37.units, bf16[336,768]{1,0:T(8,128)(2,1)S(1)} %collective-permute-done.3.second, bf16[1280,768]{1,0:T(8,128)(2,1)S(1)} %get-tuple-element.48.held, f32[1,1280]{1,0:T(1,128)S(1)} %get-tuple-element.49.row, ...), custom_call_target="tpu_custom_call" | custom-call | flops 320 | bytes 320 | tf_op jit(solution)/shard_map/pallas_call | solution.py:247
  32.3 2.0 %shard_map.44 = (f32[1,320]{1,0:T(1,128)S(1)}, f32[1,320]{1,0:T(1,128)S(1)}, f32[1,320]{1,0:T(1,128)S(1)}, f32[1,320]{1,0:T(1,128)S(1)}, f32[1,640]{1,0:T(1,128)S(1)}) custom-call(bf16[320,768]{1,0:T(8,128)(2,1)S(1)} %get-tuple-element.55.units, bf16[336,768]{1,0:T(8,128)(2,1)S(1)} %collective-permute-done.11.second, ...), custom_call_target="tpu_custom_call" | custom-call | flops 320 | bytes 320 | tf_op jit(solution)/shard_map/pallas_call | solution.py:247
  34.8 0.8 %collective-permute-done.12 = f32[1,640]{1,0:T(1,128)S(1)} collective-permute-done((f32[1,640]{1,0:T(1,128)S(1)}, f32[1,640]{1,0:T(1,128)S(1)}, u32[]{:S(2)}, u32[]{:S(2)}) %collective-permute-start.12) | collective-permute-done | bytes 2592 | tf_op jit(solution)/shard_map/ppermute | solution.py:358
  35.7 2.4 %collective-permute-start.13 = (f32[1,640]{1,0:T(1,128)S(1)}, f32[1,640]{1,0:T(1,128)S(1)}, u32[]{:S(2)}, u32[]{:S(2)}) collective-permute-start(f32[1,640]{1,0:T(1,128)S(1)} %max.24), channel_id=1, source_target_pairs={{4,0},{2,6},{0,2},{7,1},{5,7},{3,5},{12,8},{10,14},{8,10},{15,9},{... | collective-permute-start | bytes 7688 | tf_op jit(solution)/shard_map/ppermute | solution.py:362
  38.1 1.6 %collective-permute-start.15 = (f32[1,320]{1,0:T(1,128)S(1)}, f32[1,320]{1,0:T(1,128)S(1)}, u32[]{:S(2)}, u32[]{:S(2)}) collective-permute-start(f32[1,320]{1,0:T(1,128)S(1)} %get-tuple-element.66), channel_id=1, source_target_pairs={{0,8},{1,17},{2,10},{3,19},{4,12},{5,21},{6,14},{7,23},{8,0},{9,25... | collective-permute-start | bytes 3848 | tf_op jit(solution)/shard_map/ppermute | solution.py:368
  39.7 1.5 %collective-permute-start.16 = (f32[1,320]{1,0:T(1,128)S(1)}, f32[1,320]{1,0:T(1,128)S(1)}, u32[]{:S(2)}, u32[]{:S(2)}) collective-permute-start(f32[1,320]{1,0:T(1,128)S(1)} %get-tuple-element.67), channel_id=1, source_target_pairs={{0,16},{1,9},{2,18},{3,11},{4,20},{5,13},{6,22},{7,15},{8,24},{9,1... | collective-permute-start | bytes 3848 | tf_op jit(solution)/shard_map/ppermute | solution.py:368
  42.2 1.1 %collective-permute-done.16 = f32[1,320]{1,0:T(1,128)S(1)} collective-permute-done((f32[1,320]{1,0:T(1,128)S(1)}, f32[1,320]{1,0:T(1,128)S(1)}, u32[]{:S(2)}, u32[]{:S(2)}) %collective-permute-start.16) | collective-permute-done | bytes 1312 | tf_op jit(solution)/shard_map/ppermute | solution.py:368
  43.3 2.4 %collective-permute-done.17 = f32[1,320]{1,0:T(1,128)S(1)} collective-permute-done((f32[1,320]{1,0:T(1,128)S(1)}, f32[1,320]{1,0:T(1,128)S(1)}, u32[]{:S(2)}, u32[]{:S(2)}) %collective-permute-start.17) | collective-permute-done | bytes 1312 | tf_op jit(solution)/shard_map/ppermute | solution.py:368
  45.7 0.6 %maximum_reduce_fusion = f32[320]{0:T(512)} fusion(f32[1,320]{1,0:T(1,128)S(1)} %collective-permute-done.17, f32[1,320]{1,0:T(1,128)S(1)} %collective-permute-done.16, f32[1,320]{1,0:T(1,128)S(1)} %collective-permute-done.15, f32[1,320]{1,0:T(1,128)S(1)} %collective-permute-done.14, f32[1,640]{1,0:T(1,128)S(1)} %broadcast_select_fusion, ...), kind=kLoop, calls=%fused_computation.4 | loop fusion | flops 2240 | bytes 11520 | tf_op jit(solution)/shard_map/max | solution.py:371
  (28 shorter events, 3.9 us)
Async XLA Ops:
  0.0 13.7 %collective-permute-start.1 = (bf16[320,768]{1,0:T(8,128)(2,1)}, bf16[320,768]{1,0:T(8,128)(2,1)S(1)}, u32[]{:S(2)}, u32[]{:S(2)}) collective-permute-start(bf16[320,768]{1,0:T(8,128)(2,1)} %embeddings.1), channel_id=1, source_target_pairs={{0,1},{1,0},{2,3},{3,2},{4,5},{5,4},{6,7},{7,6},{8,9},{9,8},{10,11... | collective-permute-start | bytes 1474568 | tf_op jit(solution)/shard_map/ppermute | solution.py:310
  0.5 21.3 %collective-permute-start = (bf16[320,768]{1,0:T(8,128)(2,1)}, bf16[320,768]{1,0:T(8,128)(2,1)S(1)}, u32[]{:S(2)}, u32[]{:S(2)}) collective-permute-start(bf16[320,768]{1,0:T(8,128)(2,1)} %embeddings.1), channel_id=1, source_target_pairs={{0,4},{6,2},{2,0},{1,7},{7,5},{5,3},{8,12},{14,10},{10,8},{9,15},{... | collective-permute-start | bytes 1474568 | tf_op jit(solution)/shard_map/ppermute | solution.py:311
  7.3 1.0 %copy-start = (bf16[320,768]{1,0:T(8,128)(2,1)S(1)}, bf16[320,768]{1,0:T(8,128)(2,1)}, u32[]{:S(2)}) copy-start(bf16[320,768]{1,0:T(8,128)(2,1)} %embeddings.1) | copy-start | bytes 1474564
  8.5 7.3 %collective-permute-start.4 = (bf16[160,768]{1,0:T(8,128)(2,1)S(1)}, bf16[160,768]{1,0:T(8,128)(2,1)S(1)}, u32[]{:S(2)}, u32[]{:S(2)}) collective-permute-start(bf16[160,768]{1,0:T(8,128)(2,1)S(1)} %get-tuple-element.39), channel_id=1, source_target_pairs={{0,8},{1,17},{2,10},{3,19},{4,12},{5,21},{6,14},{7,23},{8,0},{9,25... | collective-permute-start | bytes 737288 | tf_op jit(solution)/shard_map/ppermute | solution.py:319
  10.1 10.1 %collective-permute-start.6 = (bf16[176,768]{1,0:T(8,128)(2,1)S(1)}, bf16[176,768]{1,0:T(8,128)(2,1)S(1)}, u32[]{:S(2)}, u32[]{:S(2)}) collective-permute-start(bf16[176,768]{1,0:T(8,128)(2,1)S(1)} %get-tuple-element.40), channel_id=1, source_target_pairs={{0,8},{1,17},{2,10},{3,19},{4,12},{5,21},{6,14},{7,23},{8,0},{9,25... | collective-permute-start | bytes 811016 | tf_op jit(solution)/shard_map/ppermute | solution.py:319
  10.6 1.6 %collective-permute-start.2 = (bf16[16,768]{1,0:T(8,128)(2,1)S(1)}, bf16[16,768]{1,0:T(8,128)(2,1)S(1)}, u32[]{:S(2)}, u32[]{:S(2)}) collective-permute-start(bf16[16,768]{1,0:T(8,128)(2,1)S(1)} %get-tuple-element.38.other_codes), channel_id=1, source_target_pairs={{0,1},{1,0},{2,3},{3,2},{4,5},{5,4},{6,7},{7,6},{8,9},{9,8},{10,11... | collective-permute-start | bytes 73736 | tf_op jit(solution)/shard_map/ppermute | solution.py:321
  12.2 16.9 %collective-permute-start.8 = (bf16[336,768]{1,0:T(8,128)(2,1)S(1)}, bf16[336,768]{1,0:T(8,128)(2,1)S(1)}, u32[]{:S(2)}, u32[]{:S(2)}) collective-permute-start(bf16[336,768]{1,0:T(8,128)(2,1)S(1)} %get-tuple-element.41.block.refs_0_), channel_id=1, source_target_pairs={{0,16},{1,9},{2,18},{3,11},{4,20},{5,13},{6,22},{7,15},{8,24},{9,1... | collective-permute-start | bytes 1548296 | tf_op jit(solution)/shard_map/ppermute | solution.py:320
  13.9 16.4 %collective-permute-start.3 = (bf16[336,768]{1,0:T(8,128)(2,1)S(1)}, bf16[336,768]{1,0:T(8,128)(2,1)S(1)}, u32[]{:S(2)}, u32[]{:S(2)}) collective-permute-start(bf16[336,768]{1,0:T(8,128)(2,1)S(1)} %shard_map.39.partner), channel_id=1, source_target_pairs={{0,4},{6,2},{2,0},{1,7},{7,5},{5,3},{8,12},{14,10},{10,8},{9,15},{... | collective-permute-start | bytes 1548296 | tf_op jit(solution)/shard_map/ppermute | solution.py:323
  15.8 10.3 %collective-permute-start.5 = (bf16[160,768]{1,0:T(8,128)(2,1)S(1)}, bf16[160,768]{1,0:T(8,128)(2,1)S(1)}, u32[]{:S(2)}, u32[]{:S(2)}) collective-permute-start(bf16[160,768]{1,0:T(8,128)(2,1)S(1)} %collective-permute-done.4.refs_1_), channel_id=1, source_target_pairs={{0,16},{1,9},{2,18},{3,11},{4,20},{5,13},{6,22},{7,15},{8,24},{9,1... | collective-permute-start | bytes 737288 | tf_op jit(solution)/shard_map/ppermute | solution.py:324
  20.2 8.9 %collective-permute-start.7 = (bf16[176,768]{1,0:T(8,128)(2,1)S(1)}, bf16[176,768]{1,0:T(8,128)(2,1)S(1)}, u32[]{:S(2)}, u32[]{:S(2)}) collective-permute-start(bf16[176,768]{1,0:T(8,128)(2,1)S(1)} %collective-permute-done.6.refs_2_), channel_id=1, source_target_pairs={{0,16},{1,9},{2,18},{3,11},{4,20},{5,13},{6,22},{7,15},{8,24},{9,1... | collective-permute-start | bytes 811016 | tf_op jit(solution)/shard_map/ppermute | solution.py:324
  21.9 7.2 %collective-permute-start.10 = (bf16[160,768]{1,0:T(8,128)(2,1)S(1)}, bf16[160,768]{1,0:T(8,128)(2,1)S(1)}, u32[]{:S(2)}, u32[]{:S(2)}) collective-permute-start(bf16[160,768]{1,0:T(8,128)(2,1)S(1)} %get-tuple-element.47), channel_id=1, source_target_pairs={{0,1},{1,0},{2,3},{3,2},{4,5},{5,4},{6,7},{7,6},{8,9},{9,8},{10,11... | collective-permute-start | bytes 737288 | tf_op jit(solution)/shard_map/ppermute | solution.py:329
  26.2 2.9 %collective-permute-start.9 = (bf16[160,768]{1,0:T(8,128)(2,1)S(1)}, bf16[160,768]{1,0:T(8,128)(2,1)S(1)}, u32[]{:S(2)}, u32[]{:S(2)}) collective-permute-start(bf16[160,768]{1,0:T(8,128)(2,1)S(1)} %get-tuple-element.46), channel_id=1, source_target_pairs={{0,1},{1,0},{2,3},{3,2},{4,5},{5,4},{6,7},{7,6},{8,9},{9,8},{10,11... | collective-permute-start | bytes 737288 | tf_op jit(solution)/shard_map/ppermute | solution.py:329
  30.3 2.1 %collective-permute-start.11 = (bf16[336,768]{1,0:T(8,128)(2,1)S(1)}, bf16[336,768]{1,0:T(8,128)(2,1)S(1)}, u32[]{:S(2)}, u32[]{:S(2)}) collective-permute-start(bf16[336,768]{1,0:T(8,128)(2,1)S(1)} %collective-permute-done.3.second), channel_id=1, source_target_pairs={{0,1},{1,0},{2,3},{3,2},{4,5},{5,4},{6,7},{7,6},{8,9},{9,8},{10,11... | collective-permute-start | bytes 1548296 | tf_op jit(solution)/shard_map/ppermute | solution.py:344
  34.3 1.3 %collective-permute-start.12 = (f32[1,640]{1,0:T(1,128)S(1)}, f32[1,640]{1,0:T(1,128)S(1)}, u32[]{:S(2)}, u32[]{:S(2)}) collective-permute-start(f32[1,640]{1,0:T(1,128)S(1)} %get-tuple-element.57), channel_id=1, source_target_pairs={{0,1},{1,0},{2,3},{3,2},{4,5},{5,4},{6,7},{7,6},{8,9},{9,8},{10,11... | collective-permute-start | bytes 7688 | tf_op jit(solution)/shard_map/ppermute | solution.py:358
  35.7 6.4 %collective-permute-start.13 = (f32[1,640]{1,0:T(1,128)S(1)}, f32[1,640]{1,0:T(1,128)S(1)}, u32[]{:S(2)}, u32[]{:S(2)}) collective-permute-start(f32[1,640]{1,0:T(1,128)S(1)} %max.24), channel_id=1, source_target_pairs={{4,0},{2,6},{0,2},{7,1},{5,7},{3,5},{12,8},{10,14},{8,10},{15,9},{... | collective-permute-start | bytes 7688 | tf_op jit(solution)/shard_map/ppermute | solution.py:362
  38.1 4.1 %collective-permute-start.15 = (f32[1,320]{1,0:T(1,128)S(1)}, f32[1,320]{1,0:T(1,128)S(1)}, u32[]{:S(2)}, u32[]{:S(2)}) collective-permute-start(f32[1,320]{1,0:T(1,128)S(1)} %get-tuple-element.66), channel_id=1, source_target_pairs={{0,8},{1,17},{2,10},{3,19},{4,12},{5,21},{6,14},{7,23},{8,0},{9,25... | collective-permute-start | bytes 3848 | tf_op jit(solution)/shard_map/ppermute | solution.py:368
  39.7 3.6 %collective-permute-start.16 = (f32[1,320]{1,0:T(1,128)S(1)}, f32[1,320]{1,0:T(1,128)S(1)}, u32[]{:S(2)}, u32[]{:S(2)}) collective-permute-start(f32[1,320]{1,0:T(1,128)S(1)} %get-tuple-element.67), channel_id=1, source_target_pairs={{0,16},{1,9},{2,18},{3,11},{4,20},{5,13},{6,22},{7,15},{8,24},{9,1... | collective-permute-start | bytes 3848 | tf_op jit(solution)/shard_map/ppermute | solution.py:368
  41.2 4.5 %collective-permute-start.17 = (f32[1,320]{1,0:T(1,128)S(1)}, f32[1,320]{1,0:T(1,128)S(1)}, u32[]{:S(2)}, u32[]{:S(2)}) collective-permute-start(f32[1,320]{1,0:T(1,128)S(1)} %get-tuple-element.68), channel_id=1, source_target_pairs={{0,24},{1,25},{2,26},{3,27},{4,28},{5,29},{6,30},{7,31},{8,16},{9,... | collective-permute-start | bytes 3848 | tf_op jit(solution)/shard_map/ppermute | solution.py:368
  42.1 3.6 %collective-permute-start.14 = (f32[1,320]{1,0:T(1,128)S(1)}, f32[1,320]{1,0:T(1,128)S(1)}, u32[]{:S(2)}, u32[]{:S(2)}) collective-permute-start(f32[1,320]{1,0:T(1,128)S(1)} %slice.9), channel_id=1, source_target_pairs={{0,1},{1,0},{2,3},{3,2},{4,5},{5,4},{6,7},{7,6},{8,9},{9,8},{10,11... | collective-permute-start | bytes 3848 | tf_op jit(solution)/shard_map/ppermute | solution.py:366

commit v15 on v14

--- a/solution.py
+++ b/solution.py
@@ -87,24 +87,26 @@
     return jnp.max(partial.T, axis=0, keepdims=True)[:, :rows]
 
 
-def meet(units, row, rows, span, held, held_codes, to_block, to_held):
-    column = turned_to_column(row, rows)
-    starts = range(0, rows, CHUNK)
-    partial = [jnp.full((CHUNK, LANES), -1.0, jnp.float32) for _ in starts]
+def meet(units, parts, rows, span, held, held_codes):
+    columns = [turned_to_column(row, rows) for row, _ in parts]
+    starts = [(block, top) for block in range(len(parts)) for top in range(0, rows, CHUNK)]
+    partial = {start: jnp.full((CHUNK, LANES), -1.0, jnp.float32) for start in starts}
     best_held = []
     for at in range(0, held.shape[0], TILE):
         tile = min(TILE, held.shape[0] - at)
         sims = lax.dot_general(
-            units,
+            units[...],
             held[at : at + tile, :],
             (((1,), (1,)), ((), ())),
             preferred_element_type=jnp.float32,
         )
         best = [jnp.full((CHUNK, LANES), -1.0, jnp.float32) for _ in range(0, tile, LANES)]
-        for place, top in enumerate(starts):
-            mine = column[top : top + CHUNK]
+        for block, top in starts:
+            to_block, to_held = parts[block][1]
+            mine = columns[block][top : top + CHUNK]
+            line = block * rows + top
             for lane in range(0, tile, LANES):
-                part = sims[top : top + CHUNK, lane : lane + LANES]
+                part = sims[line : line + CHUNK, lane : lane + LANES]
                 gap = mine - held_codes[:, at + lane : at + lane + LANES]
                 if to_block and to_held:
                     part = jnp.where(jnp.abs(gap) < span, part, -1.0)
@@ -115,14 +117,18 @@
                 else:
                     theirs = jnp.where((gap < 0.0) & (gap > -span), part, -1.0)
                 if to_block:
-                    partial[place] = jnp.maximum(partial[place], ours)
+                    partial[block, top] = jnp.maximum(partial[block, top], ours)
                 if to_held:
                     best[lane // LANES] = jnp.maximum(best[lane // LANES], theirs)
         best_held += [jnp.max(some, axis=0, keepdims=True) for some in best]
-    return (
-        row_from_partial(jnp.concatenate(partial, axis=0), rows) if to_block else None,
-        jnp.concatenate(best_held, axis=1) if to_held else None,
-    )
+    found = [
+        row_from_partial(
+            jnp.concatenate([partial[block, top] for top in range(0, rows, CHUNK)], axis=0), rows
+        )
+        for block, (_, (to_block, _)) in enumerate(parts)
+        if to_block
+    ]
+    return found, jnp.concatenate(best_held, axis=1)
 
 
 def assemble(whole, top, rows, pieces, extra):
@@ -175,40 +181,37 @@
     return [[next(flat) for _ in range(length)] for length in lengths]
 
 
+def pair(units, first, second, rows):
+    units[0:rows, :] = first[0:rows, :]
+    units[rows:, :] = second[0:rows, :]
+
+
 def plane_kernel(rows, span, lengths, block, partner, *refs):
-    *pieces, best, mine, held = refs
+    *pieces, best, mine, held, units = refs
     row = hold(regrouped(pieces, lengths), held, rows, span)
-    mine[...], _ = meet(block[0:rows, :], codes(block, rows, span), rows, span, held, row, *OWN)
-    _, theirs = meet(partner[0:rows, :], codes(partner, rows, span), rows, span, held, row, *HELD)
+    pair(units, block, partner, rows)
+    parts = [(codes(block, rows, span), OWN), (codes(partner, rows, span), HELD)]
+    (mine[...],), theirs = meet(units, parts, rows, span, held, row)
     best[...] = theirs[:, : best.shape[1]]
 
 
-def rest_kernel(rows, span, block, partner, held, row, best, mine):
+def rest_kernel(rows, span, block, partner, held, row, best, mine, units):
     count = best.shape[1]
     start = held.shape[0] - up(count, LANES)
     held, row = held.at[start:, :], row[:, start:]
-    mine[...], _ = meet(block[0:rows, :], codes(block, rows, span), rows, span, held, row, *OWN)
-    _, theirs = meet(partner[0:rows, :], codes(partner, rows, span), rows, span, held, row, *HELD)
+    pair(units, block, partner, rows)
+    parts = [(codes(block, rows, span), OWN), (codes(partner, rows, span), HELD)]
+    (mine[...],), theirs = meet(units, parts, rows, span, held, row)
     best[...] = theirs[:, row.shape[1] - count :]
 
 
-def line_kernel(rows, span, together, count, units, second, held, row, *refs):
-    bests, outs, found = refs[:count], refs[count:-1], refs[-1]
-    results = [
-        meet(
-            block[0:rows, :],
-            codes(second, rows, span, first=place),
-            rows,
-            span,
-            held,
-            row[...],
-            *TWO,
-        )
-        for block, place in ((units, CODES), (second, 0))
-    ]
-    found[...] = jnp.concatenate([mine for mine, _ in results], axis=1)
-    best = jnp.concatenate([best[...] for best in bests], axis=1)
-    best = jnp.maximum(best, jnp.maximum(results[0][1], results[1][1]))
+def line_kernel(rows, span, together, count, first, second, held, row, *refs):
+    bests, outs, (found, units) = refs[:count], refs[count:-2], refs[-2:]
+    pair(units, first, second, rows)
+    parts = [(codes(second, rows, span, first=place), TWO) for place in (CODES, 0)]
+    mine, theirs = meet(units, parts, rows, span, held, row[...])
+    found[...] = jnp.concatenate(mine, axis=1)
+    best = jnp.maximum(jnp.concatenate([best[...] for best in bests], axis=1), theirs)
     for out, places in zip(outs, together):
         out[...] = jnp.concatenate(
             [best[:, place * rows : (place + 1) * rows] for place in places], axis=1
@@ -224,7 +227,10 @@
             jax.ShapeDtypeStruct((1, total), jnp.float32),
             jax.ShapeDtypeStruct((1, rows), jnp.float32),
         ],
-        scratch_shapes=[pltpu.VMEM((up(total, LANES), width), jnp.bfloat16)],
+        scratch_shapes=[
+            pltpu.VMEM((up(total, LANES), width), jnp.bfloat16),
+            pltpu.VMEM((2 * rows, width), jnp.bfloat16),
+        ],
         compiler_params=pltpu.CompilerParams(vmem_limit_bytes=12 << 20),
         cost_estimate=pl.CostEstimate(flops=rows, bytes_accessed=rows, transcendentals=0),
     )(block, partner, *[piece for part in holds for piece in part])
@@ -237,19 +243,21 @@
             jax.ShapeDtypeStruct((1, count), jnp.float32),
             jax.ShapeDtypeStruct((1, rows), jnp.float32),
         ],
+        scratch_shapes=[pltpu.VMEM((2 * rows, block.shape[1]), jnp.bfloat16)],
         compiler_params=pltpu.CompilerParams(vmem_limit_bytes=12 << 20),
         cost_estimate=pl.CostEstimate(flops=rows, bytes_accessed=rows, transcendentals=0),
     )(block, partner, held, row)
 
 
-def line(units, second, held, row, bests, rows, span, together):
+def line(first, second, held, row, bests, rows, span, together):
     outs = [jax.ShapeDtypeStruct((1, rows * len(some)), jnp.float32) for some in together]
     *bests, found = pl.pallas_call(
         functools.partial(line_kernel, rows, span, together, len(bests)),
         out_shape=outs + [jax.ShapeDtypeStruct((1, 2 * rows), jnp.float32)],
+        scratch_shapes=[pltpu.VMEM((2 * rows, second.shape[1]), jnp.bfloat16)],
         compiler_params=pltpu.CompilerParams(vmem_limit_bytes=12 << 20),
         cost_estimate=pl.CostEstimate(flops=rows, bytes_accessed=rows, transcendentals=0),
-    )(units, second, held, row, *bests)
+    )(first, second, held, row, *bests)
     return bests, found
 
 
@@ -284,7 +292,6 @@
     other_core = everywhere(lambda p, g: (p, g ^ 1))
     first = everywhere(lambda p, g: (p ^ (1 + g % 2), g))
     second = everywhere(lambda p, g: (p ^ (2 - g % 2), g))
-    corner_pairs = everywhere(lambda p, g: (p ^ 3, g))
 
     rounds = line_rounds(chips)
     rounds += [[]] * (len(rounds) % 2)
@@ -338,7 +345,7 @@
         results.append(mine)
         bests = [best_two, best_rest]
         far = [far_units] + [jnp.concatenate(pieces, axis=0) for pieces in far[1:]]
-        whole, last = [tuple(range(groups))], [(at,) for at in range(groups)]
+        whole, last = [tuple(range(groups))], [(0,), (1, 3), (2,)]
         for at, second_near in enumerate(near_other):
             second_near, *bests = lax.optimization_barrier((second_near, *bests))
             second_far = lax.ppermute(second_near, BOTH, other_core)
@@ -357,17 +364,16 @@
             sent.append(found)
         sent = lax.ppermute(jnp.concatenate(sent, axis=1), BOTH, other_core)
         kept = jnp.maximum(jnp.concatenate(kept, axis=1), sent)
-        kept, *bests = lax.optimization_barrier((kept, *bests))
         for at, pairs in enumerate(rounds):
             found = lax.ppermute(kept[:, 2 * at * rows : 2 * (at + 1) * rows], BOTH, back(pairs))
             me = lax.axis_index(BOTH)
             sender = functools.reduce(jnp.logical_or, [me == source for source, _ in pairs])
             found = jnp.where(sender, found, -1.0)
             results += [found[:, :rows], lax.ppermute(found[:, rows:], BOTH, other_core)]
-        results += [
-            lax.ppermute(best, BOTH, pairs)
-            for best, pairs in zip(bests[1:], (first, second, corner_pairs))
-        ]
+        from_x = lax.ppermute(bests[1], BOTH, first)
+        results.append(from_x[:, :rows])
+        onward = jnp.maximum(bests[2], from_x[:, rows:])
+        results.append(lax.ppermute(onward, BOTH, second))
         return functools.reduce(jnp.maximum, results, bests[0]).reshape(rows)
 
     placed = (P(BOTH, None), P(BOTH, None), P(BOTH))

time: 46.6 us -> 44.9 us (0.964)
  waiting for transfers between devices: 15.4 us -> 14.2 us
  starting transfers between devices: 20.9 us -> 20.3 us
    ppermute x3 -> x2, waiting for transfers between devices: 3.48 us -> 0.01 us  [the longest x1 0.01 us: shards(): from_x = lax.ppermute(bests[1], BOTH, first)]
    ppermute x1, waiting for transfers between devices: 0.34 us -> 2.39 us  [shards(): lax.ppermute(kept[:, 2 * at * rows:2 * (at + 1) * rows], BOTH, back(pairs))]
    ppermute x1, waiting for transfers between devices: 0.01 us -> 1.13 us  [shards(): lax.ppermute(found[:, rows:], BOTH, other_core)]
    ppermute x1, waiting for transfers between devices: 0.82 us -> 0.01 us  [shards(): sent = lax.ppermute(jnp.concatenate(sent, axis=1), BOTH, other_core)]
    ppermute x3 -> x2, starting transfers between devices: 3.55 us -> 3.02 us  [the longest x1 1.51 us: shards(): results.append(lax.ppermute(onward, BOTH, second))]
    unnamed x2 -> x6, local copies, waits for them, and re-layouts: 1.03 us -> 1.04 us
  transfers between devices with their start and end apart: 18 -> 17, of which waited for: 8 -> 6; matrix products, arithmetic and copies ran while one was open for 3% -> 3% of each run, Pallas kernels for 10% -> 11%
where the time goes in v15:
time: 44.9 us; the launch traced here: 44.7 us
  starting transfers between devices  20.3 us (45%)
  waiting for transfers between devices  14.2 us (32%)
  Pallas kernels  6.76 us (15%)
  other arithmetic  2.07 us (5%)
  local copies, waits for them, and re-layouts  1.11 us (2%)
    ppermute x2, waiting for transfers between devices, shards(): from_corner = [lax.ppermute(part, BOTH, second) for part in from_first]  6.05 us
    ppermute x1, starting transfers between devices, shards(): raw = [lax.ppermute(embeddings, BOTH, pairs) for pairs in rounds]  5.49 us
    pallas_call x2, Pallas kernels, line(): pl.pallas_call(functools.partial(line_kernel, rows, span, together, len(b...  4.06 us
    ppermute x2, waiting for transfers between devices, shards(): from_first = [lax.ppermute(part, BOTH, first) for part in parts]  3.8 us
    ppermute x1, waiting for transfers between devices, shards(): lax.ppermute(kept[:, 2 * at * rows:2 * (at + 1) * rows], BOTH, back(pairs))  2.39 us
    ppermute x1, starting transfers between devices, shards(): lax.ppermute(kept[:, 2 * at * rows:2 * (at + 1) * rows], BOTH, back(pairs))  2.38 us
    ppermute x2, starting transfers between devices, shards(): from_first = [lax.ppermute(part, BOTH, first) for part in parts]  2.09 us
    ppermute x2, starting transfers between devices, shards(): from_corner = [lax.ppermute(part, BOTH, second) for part in from_first]  2.09 us
  transfers between devices with their start and end apart: 17, of which 6 were waited for; matrix products, arithmetic and copies ran while one was open for 3% of the time, Pallas kernels for 11%

profile of v15, /device:TPU:0, one launch (start us, length us, event | category | flops | bytes accessed | tf_op | source)
XLA Modules:
  0.0 44.7 jit_solution(6750125738940927284)
XLA Ops:
  0.5 5.5 %collective-permute-start.7 = (bf16[320,768]{1,0:T(8,128)(2,1)}, bf16[320,768]{1,0:T(8,128)(2,1)S(1)}, u32[]{:S(2)}, u32[]{:S(2)}) collective-permute-start(bf16[320,768]{1,0:T(8,128)(2,1)} %embeddings.1), channel_id=1, source_target_pairs={{0,4},{6,2},{2,0},{1,7},{7,5},{5,3},{8,12},{14,10},{10,8},{9,15},{... | collective-permute-start | bytes 1474568 | tf_op jit(solution)/shard_map/ppermute | solution.py:318
  5.9 0.7 %multiply_reduce_fusion = s32[320]{0:T(512)S(1)} fusion(s32[320,1]{0,1:T(1,128)} %param.4), kind=kLoop, calls=%fused_computation.6 | loop fusion | flops 640 | bytes 2560 | tf_op jit(solution)/shard_map/mul | solution.py:319
  6.6 0.7 %add.15.named = s32[320]{0:T(512)S(1)} add(s32[320]{0:T(512)S(1)} %multiply_reduce_fusion, s32[320]{0:T(512)} %param.5) | non-fusion elementwise | flops 320 | bytes 3840 | tf_op jit(solution)/shard_map/add | solution.py:319
  7.3 1.0 %copy-done.2 = bf16[320,768]{1,0:T(8,128)(2,1)S(1)} copy-done((bf16[320,768]{1,0:T(8,128)(2,1)S(1)}, bf16[320,768]{1,0:T(8,128)(2,1)}, u32[]{:S(2)}) %copy-start.2) | copy-done | bytes 491544
  8.5 1.6 %collective-permute-start = (bf16[160,768]{1,0:T(8,128)(2,1)S(1)}, bf16[160,768]{1,0:T(8,128)(2,1)S(1)}, u32[]{:S(2)}, u32[]{:S(2)}) collective-permute-start(bf16[160,768]{1,0:T(8,128)(2,1)S(1)} %get-tuple-element.32), channel_id=1, source_target_pairs={{0,8},{1,17},{2,10},{3,19},{4,12},{5,21},{6,14},{7,23},{8,0},{9,25... | collective-permute-start | bytes 737288 | tf_op jit(solution)/shard_map/ppermute | solution.py:326
  10.6 0.7 %collective-permute-start.6 = (bf16[16,768]{1,0:T(8,128)(2,1)S(1)}, bf16[16,768]{1,0:T(8,128)(2,1)S(1)}, u32[]{:S(2)}, u32[]{:S(2)}) collective-permute-start(bf16[16,768]{1,0:T(8,128)(2,1)S(1)} %get-tuple-element.34.other_codes), channel_id=1, source_target_pairs={{0,1},{1,0},{2,3},{3,2},{4,5},{5,4},{6,7},{7,6},{8,9},{9,8},{10,11... | collective-permute-start | bytes 73736 | tf_op jit(solution)/shard_map/ppermute | solution.py:328
  11.3 0.8 %collective-permute-done.6.codes_of = bf16[16,768]{1,0:T(8,128)(2,1)S(1)} collective-permute-done((bf16[16,768]{1,0:T(8,128)(2,1)S(1)}, bf16[16,768]{1,0:T(8,128)(2,1)S(1)}, u32[]{:S(2)}, u32[]{:S(2)}) %collective-permute-start.6) | collective-permute-done | bytes 24608 | tf_op jit(solution)/shard_map/ppermute | solution.py:328
  12.2 1.5 %collective-permute-start.2 = (bf16[336,768]{1,0:T(8,128)(2,1)S(1)}, bf16[336,768]{1,0:T(8,128)(2,1)S(1)}, u32[]{:S(2)}, u32[]{:S(2)}) collective-permute-start(bf16[336,768]{1,0:T(8,128)(2,1)S(1)} %get-tuple-element.31.block.refs_0_), channel_id=1, source_target_pairs={{0,16},{1,9},{2,18},{3,11},{4,20},{5,13},{6,22},{7,15},{8,24},{9,1... | collective-permute-start | bytes 1548296 | tf_op jit(solution)/shard_map/ppermute | solution.py:327
  13.9 1.9 %collective-permute-start.10 = (bf16[336,768]{1,0:T(8,128)(2,1)S(1)}, bf16[336,768]{1,0:T(8,128)(2,1)S(1)}, u32[]{:S(2)}, u32[]{:S(2)}) collective-permute-start(bf16[336,768]{1,0:T(8,128)(2,1)S(1)} %shard_map.38.partner), channel_id=1, source_target_pairs={{0,4},{6,2},{2,0},{1,7},{7,5},{5,3},{8,12},{14,10},{10,8},{9,15},{... | collective-permute-start | bytes 1548296 | tf_op jit(solution)/shard_map/ppermute | solution.py:330
  15.8 0.6 %collective-permute-start.3 = (bf16[160,768]{1,0:T(8,128)(2,1)S(1)}, bf16[160,768]{1,0:T(8,128)(2,1)S(1)}, u32[]{:S(2)}, u32[]{:S(2)}) collective-permute-start(bf16[160,768]{1,0:T(8,128)(2,1)S(1)} %collective-permute-done.refs_1_), channel_id=1, source_target_pairs={{0,16},{1,9},{2,18},{3,11},{4,20},{5,13},{6,22},{7,15},{8,24},{9,1... | collective-permute-start | bytes 737288 | tf_op jit(solution)/shard_map/ppermute | solution.py:331
  16.4 3.8 %collective-permute-done.1.refs_2_ = bf16[176,768]{1,0:T(8,128)(2,1)S(1)} collective-permute-done((bf16[176,768]{1,0:T(8,128)(2,1)S(1)}, bf16[176,768]{1,0:T(8,128)(2,1)S(1)}, u32[]{:S(2)}, u32[]{:S(2)}) %collective-permute-start.1) | collective-permute-done | bytes 270368 | tf_op jit(solution)/shard_map/ppermute | solution.py:326
  20.2 1.5 %collective-permute-start.4 = (bf16[176,768]{1,0:T(8,128)(2,1)S(1)}, bf16[176,768]{1,0:T(8,128)(2,1)S(1)}, u32[]{:S(2)}, u32[]{:S(2)}) collective-permute-start(bf16[176,768]{1,0:T(8,128)(2,1)S(1)} %collective-permute-done.1.refs_2_), channel_id=1, source_target_pairs={{0,16},{1,9},{2,18},{3,11},{4,20},{5,13},{6,22},{7,15},{8,24},{9,1... | collective-permute-start | bytes 811016 | tf_op jit(solution)/shard_map/ppermute | solution.py:331
  22.0 4.2 %collective-permute-done.3.refs_4_ = bf16[160,768]{1,0:T(8,128)(2,1)S(1)} collective-permute-done((bf16[160,768]{1,0:T(8,128)(2,1)S(1)}, bf16[160,768]{1,0:T(8,128)(2,1)S(1)}, u32[]{:S(2)}, u32[]{:S(2)}) %collective-permute-start.3) | collective-permute-done | bytes 245792 | tf_op jit(solution)/shard_map/ppermute | solution.py:331
  26.2 1.0 %shard_map.39 = (f32[1,640]{1,0:T(1,128)S(1)}, f32[1,320]{1,0:T(1,128)S(1)}) custom-call(bf16[336,768]{1,0:T(8,128)(2,1)S(1)} %get-tuple-element.31.block.refs_0_, bf16[336,768]{1,0:T(8,128)(2,1)S(1)} %shard_map.38.partner, bf16[336,768]{1,0:T(8,128)(2,1)S(1)} %get-tuple-element.31.block.refs_0_, bf16[160,768]{1,0:T(8,128)(2,1)S(1)} %collective-permute-done.refs_1_, ...), custom_call_target="tpu_custom_call" | custom-call | flops 320 | bytes 320 | tf_op jit(solution)/shard_map/pallas_call | solution.py:224
  27.2 1.9 %collective-permute-done.4.refs_5_ = bf16[176,768]{1,0:T(8,128)(2,1)S(1)} collective-permute-done((bf16[176,768]{1,0:T(8,128)(2,1)S(1)}, bf16[176,768]{1,0:T(8,128)(2,1)S(1)}, u32[]{:S(2)}, u32[]{:S(2)}) %collective-permute-start.4) | collective-permute-done | bytes 270368 | tf_op jit(solution)/shard_map/ppermute | solution.py:331
  29.3 1.0 %shard_map.42 = (f32[1,640]{1,0:T(1,128)S(1)}, f32[1,320]{1,0:T(1,128)S(1)}) custom-call(bf16[336,768]{1,0:T(8,128)(2,1)S(1)} %get-tuple-element.31.block.refs_0_, bf16[336,768]{1,0:T(8,128)(2,1)S(1)} %shard_map.38.partner, bf16[1280,768]{1,0:T(8,128)(2,1)S(1)} %get-tuple-element.42.held, f32[1,1280]{1,0:T(1,128)S(1)} %get-tuple-element.43.row), custom_call_target="tpu_custom_call" | custom-call | flops 320 | bytes 320 | tf_op jit(solution)/shard_map/pallas_call | solution.py:240
  30.4 2.0 %shard_map.43 = (f32[1,1280]{1,0:T(1,128)S(1)}, f32[1,640]{1,0:T(1,128)S(1)}) custom-call(bf16[320,768]{1,0:T(8,128)(2,1)S(1)} %get-tuple-element.46.first, bf16[336,768]{1,0:T(8,128)(2,1)S(1)} %collective-permute-done.10.second, bf16[1280,768]{1,0:T(8,128)(2,1)S(1)} %get-tuple-element.42.held, f32[1,1280]{1,0:T(1,128)S(1)} %get-tuple-element.43.row, ...), custom_call_target="tpu_custom_call" | custom-call | flops 320 | bytes 320 | tf_op jit(solution)/shard_map/pallas_call | solution.py:254
  32.4 2.0 %shard_map.44 = (f32[1,320]{1,0:T(1,128)S(1)}, f32[1,640]{1,0:T(1,128)S(1)}, f32[1,320]{1,0:T(1,128)S(1)}, f32[1,640]{1,0:T(1,128)S(1)}) custom-call(bf16[320,768]{1,0:T(8,128)(2,1)S(1)} %copy-done.1, bf16[336,768]{1,0:T(8,128)(2,1)S(1)} %collective-permute-done.11.second, bf16[1280,768]{1,0:T(8,128)(2,1)S(1)} %get-tuple-element.42.held, ...), custom_call_target="tpu_custom_call" | custom-call | flops 320 | bytes 320 | tf_op jit(solution)/shard_map/pallas_call | solution.py:254
  34.9 1.5 %collective-permute-start.15 = (f32[1,640]{1,0:T(1,128)S(1)}, f32[1,640]{1,0:T(1,128)S(1)}, u32[]{:S(2)}, u32[]{:S(2)}) collective-permute-start(f32[1,640]{1,0:T(1,128)S(1)} %get-tuple-element.55), channel_id=1, source_target_pairs={{0,8},{1,17},{2,10},{3,19},{4,12},{5,21},{6,14},{7,23},{8,0},{9,25... | collective-permute-start | bytes 7688 | tf_op jit(solution)/shard_map/ppermute | solution.py:373
  36.5 2.4 %collective-permute-start.13 = (f32[1,640]{1,0:T(1,128)S(1)}, f32[1,640]{1,0:T(1,128)S(1)}, u32[]{:S(2)}, u32[]{:S(2)}) collective-permute-start(f32[1,640]{1,0:T(1,128)S(1)} %max.26), channel_id=1, source_target_pairs={{4,0},{2,6},{0,2},{7,1},{5,7},{3,5},{12,8},{10,14},{8,10},{15,9},{... | collective-permute-start | bytes 7688 | tf_op jit(solution)/shard_map/ppermute | solution.py:368
  38.9 1.5 %collective-permute-start.16 = (f32[1,320]{1,0:T(1,128)S(1)}, f32[1,320]{1,0:T(1,128)S(1)}, u32[]{:S(2)}, u32[]{:S(2)}) collective-permute-start(f32[1,320]{1,0:T(1,128)S(1)} %slice_maximum_fusion), channel_id=1, source_target_pairs={{0,16},{1,9},{2,18},{3,11},{4,20},{5,13},{6,22},{7,15},{8,24},{9,1... | collective-permute-start | bytes 3848 | tf_op jit(solution)/shard_map/ppermute | solution.py:376
  40.4 2.4 %collective-permute-done.13 = f32[1,640]{1,0:T(1,128)S(1)} collective-permute-done((f32[1,640]{1,0:T(1,128)S(1)}, f32[1,640]{1,0:T(1,128)S(1)}, u32[]{:S(2)}, u32[]{:S(2)}) %collective-permute-start.13) | collective-permute-done | bytes 2592 | tf_op jit(solution)/shard_map/ppermute | solution.py:368
  42.9 1.1 %collective-permute-done.14 = f32[1,320]{1,0:T(1,128)S(1)} collective-permute-done((f32[1,320]{1,0:T(1,128)S(1)}, f32[1,320]{1,0:T(1,128)S(1)}, u32[]{:S(2)}, u32[]{:S(2)}) %collective-permute-start.14) | collective-permute-done | bytes 1312 | tf_op jit(solution)/shard_map/ppermute | solution.py:372
  44.1 0.6 %fusion.2 = f32[320]{0:T(512)} fusion(f32[1,320]{1,0:T(1,128)S(1)} %collective-permute-done.16, f32[1,640]{1,0:T(1,128)S(1)} %collective-permute-done.15, f32[1,320]{1,0:T(1,128)S(1)} %collective-permute-done.14, f32[1,640]{1,0:T(1,128)S(1)} %broadcast_select_fusion, f32[1,320]{1,0:T(1,128)S(1)} %get-tuple-element.52, f32[1,320]{1,0:T(1,128)S(1)} %get-tuple-element.50, ...), kind=kLoop, calls=%fused_computation.7 | loop fusion | flops 1920 | bytes 10240 | tf_op jit(solution)/shard_map/max | solution.py:377
  (31 shorter events, 2.5 us)
Async XLA Ops:
  0.0 13.7 %collective-permute-start.5 = (bf16[320,768]{1,0:T(8,128)(2,1)}, bf16[320,768]{1,0:T(8,128)(2,1)S(1)}, u32[]{:S(2)}, u32[]{:S(2)}) collective-permute-start(bf16[320,768]{1,0:T(8,128)(2,1)} %embeddings.1), channel_id=1, source_target_pairs={{0,1},{1,0},{2,3},{3,2},{4,5},{5,4},{6,7},{7,6},{8,9},{9,8},{10,11... | collective-permute-start | bytes 1474568 | tf_op jit(solution)/shard_map/ppermute | solution.py:317
  0.5 21.3 %collective-permute-start.7 = (bf16[320,768]{1,0:T(8,128)(2,1)}, bf16[320,768]{1,0:T(8,128)(2,1)S(1)}, u32[]{:S(2)}, u32[]{:S(2)}) collective-permute-start(bf16[320,768]{1,0:T(8,128)(2,1)} %embeddings.1), channel_id=1, source_target_pairs={{0,4},{6,2},{2,0},{1,7},{7,5},{5,3},{8,12},{14,10},{10,8},{9,15},{... | collective-permute-start | bytes 1474568 | tf_op jit(solution)/shard_map/ppermute | solution.py:318
  7.3 1.0 %copy-start.2 = (bf16[320,768]{1,0:T(8,128)(2,1)S(1)}, bf16[320,768]{1,0:T(8,128)(2,1)}, u32[]{:S(2)}) copy-start(bf16[320,768]{1,0:T(8,128)(2,1)} %embeddings.1) | copy-start | bytes 1474564
  8.5 7.3 %collective-permute-start = (bf16[160,768]{1,0:T(8,128)(2,1)S(1)}, bf16[160,768]{1,0:T(8,128)(2,1)S(1)}, u32[]{:S(2)}, u32[]{:S(2)}) collective-permute-start(bf16[160,768]{1,0:T(8,128)(2,1)S(1)} %get-tuple-element.32), channel_id=1, source_target_pairs={{0,8},{1,17},{2,10},{3,19},{4,12},{5,21},{6,14},{7,23},{8,0},{9,25... | collective-permute-start | bytes 737288 | tf_op jit(solution)/shard_map/ppermute | solution.py:326
  10.1 10.1 %collective-permute-start.1 = (bf16[176,768]{1,0:T(8,128)(2,1)S(1)}, bf16[176,768]{1,0:T(8,128)(2,1)S(1)}, u32[]{:S(2)}, u32[]{:S(2)}) collective-permute-start(bf16[176,768]{1,0:T(8,128)(2,1)S(1)} %get-tuple-element.33), channel_id=1, source_target_pairs={{0,8},{1,17},{2,10},{3,19},{4,12},{5,21},{6,14},{7,23},{8,0},{9,25... | collective-permute-start | bytes 811016 | tf_op jit(solution)/shard_map/ppermute | solution.py:326
  10.6 1.6 %collective-permute-start.6 = (bf16[16,768]{1,0:T(8,128)(2,1)S(1)}, bf16[16,768]{1,0:T(8,128)(2,1)S(1)}, u32[]{:S(2)}, u32[]{:S(2)}) collective-permute-start(bf16[16,768]{1,0:T(8,128)(2,1)S(1)} %get-tuple-element.34.other_codes), channel_id=1, source_target_pairs={{0,1},{1,0},{2,3},{3,2},{4,5},{5,4},{6,7},{7,6},{8,9},{9,8},{10,11... | collective-permute-start | bytes 73736 | tf_op jit(solution)/shard_map/ppermute | solution.py:328
  12.2 16.9 %collective-permute-start.2 = (bf16[336,768]{1,0:T(8,128)(2,1)S(1)}, bf16[336,768]{1,0:T(8,128)(2,1)S(1)}, u32[]{:S(2)}, u32[]{:S(2)}) collective-permute-start(bf16[336,768]{1,0:T(8,128)(2,1)S(1)} %get-tuple-element.31.block.refs_0_), channel_id=1, source_target_pairs={{0,16},{1,9},{2,18},{3,11},{4,20},{5,13},{6,22},{7,15},{8,24},{9,1... | collective-permute-start | bytes 1548296 | tf_op jit(solution)/shard_map/ppermute | solution.py:327
  13.9 16.4 %collective-permute-start.10 = (bf16[336,768]{1,0:T(8,128)(2,1)S(1)}, bf16[336,768]{1,0:T(8,128)(2,1)S(1)}, u32[]{:S(2)}, u32[]{:S(2)}) collective-permute-start(bf16[336,768]{1,0:T(8,128)(2,1)S(1)} %shard_map.38.partner), channel_id=1, source_target_pairs={{0,4},{6,2},{2,0},{1,7},{7,5},{5,3},{8,12},{14,10},{10,8},{9,15},{... | collective-permute-start | bytes 1548296 | tf_op jit(solution)/shard_map/ppermute | solution.py:330
  15.8 10.3 %collective-permute-start.3 = (bf16[160,768]{1,0:T(8,128)(2,1)S(1)}, bf16[160,768]{1,0:T(8,128)(2,1)S(1)}, u32[]{:S(2)}, u32[]{:S(2)}) collective-permute-start(bf16[160,768]{1,0:T(8,128)(2,1)S(1)} %collective-permute-done.refs_1_), channel_id=1, source_target_pairs={{0,16},{1,9},{2,18},{3,11},{4,20},{5,13},{6,22},{7,15},{8,24},{9,1... | collective-permute-start | bytes 737288 | tf_op jit(solution)/shard_map/ppermute | solution.py:331
  20.2 8.9 %collective-permute-start.4 = (bf16[176,768]{1,0:T(8,128)(2,1)S(1)}, bf16[176,768]{1,0:T(8,128)(2,1)S(1)}, u32[]{:S(2)}, u32[]{:S(2)}) collective-permute-start(bf16[176,768]{1,0:T(8,128)(2,1)S(1)} %collective-permute-done.1.refs_2_), channel_id=1, source_target_pairs={{0,16},{1,9},{2,18},{3,11},{4,20},{5,13},{6,22},{7,15},{8,24},{9,1... | collective-permute-start | bytes 811016 | tf_op jit(solution)/shard_map/ppermute | solution.py:331
  21.9 7.2 %collective-permute-start.8 = (bf16[160,768]{1,0:T(8,128)(2,1)S(1)}, bf16[160,768]{1,0:T(8,128)(2,1)S(1)}, u32[]{:S(2)}, u32[]{:S(2)}) collective-permute-start(bf16[160,768]{1,0:T(8,128)(2,1)S(1)} %get-tuple-element.38), channel_id=1, source_target_pairs={{0,1},{1,0},{2,3},{3,2},{4,5},{5,4},{6,7},{7,6},{8,9},{9,8},{10,11... | collective-permute-start | bytes 737288 | tf_op jit(solution)/shard_map/ppermute | solution.py:336
  26.2 2.9 %collective-permute-start.9 = (bf16[160,768]{1,0:T(8,128)(2,1)S(1)}, bf16[160,768]{1,0:T(8,128)(2,1)S(1)}, u32[]{:S(2)}, u32[]{:S(2)}) collective-permute-start(bf16[160,768]{1,0:T(8,128)(2,1)S(1)} %get-tuple-element.39), channel_id=1, source_target_pairs={{0,1},{1,0},{2,3},{3,2},{4,5},{5,4},{6,7},{7,6},{8,9},{9,8},{10,11... | collective-permute-start | bytes 737288 | tf_op jit(solution)/shard_map/ppermute | solution.py:336
  29.2 1.0 %copy-start = (bf16[320,768]{1,0:T(8,128)(2,1)}, bf16[320,768]{1,0:T(8,128)(2,1)S(1)}, u32[]{:S(2)}) copy-start(bf16[320,768]{1,0:T(8,128)(2,1)S(1)} %get-tuple-element.40.first) | copy-start | bytes 1474564
  30.3 2.1 %collective-permute-start.11 = (bf16[336,768]{1,0:T(8,128)(2,1)S(1)}, bf16[336,768]{1,0:T(8,128)(2,1)S(1)}, u32[]{:S(2)}, u32[]{:S(2)}) collective-permute-start(bf16[336,768]{1,0:T(8,128)(2,1)S(1)} %collective-permute-done.10.second), channel_id=1, source_target_pairs={{0,1},{1,0},{2,3},{3,2},{4,5},{5,4},{6,7},{7,6},{8,9},{9,8},{10,11... | collective-permute-start | bytes 1548296 | tf_op jit(solution)/shard_map/ppermute | solution.py:351
  30.4 2.0 %copy-start.1 = (bf16[320,768]{1,0:T(8,128)(2,1)S(1)}, bf16[320,768]{1,0:T(8,128)(2,1)}, u32[]{:S(2)}) copy-start(bf16[320,768]{1,0:T(8,128)(2,1)} %copy-done) | copy-start | bytes 1474564
  34.5 2.0 %collective-permute-start.12 = (f32[1,640]{1,0:T(1,128)S(1)}, f32[1,640]{1,0:T(1,128)S(1)}, u32[]{:S(2)}, u32[]{:S(2)}) collective-permute-start(f32[1,640]{1,0:T(1,128)S(1)} %get-tuple-element.54), channel_id=1, source_target_pairs={{0,1},{1,0},{2,3},{3,2},{4,5},{5,4},{6,7},{7,6},{8,9},{9,8},{10,11... | collective-permute-start | bytes 7688 | tf_op jit(solution)/shard_map/ppermute | solution.py:365
  34.9 3.9 %collective-permute-start.15 = (f32[1,640]{1,0:T(1,128)S(1)}, f32[1,640]{1,0:T(1,128)S(1)}, u32[]{:S(2)}, u32[]{:S(2)}) collective-permute-start(f32[1,640]{1,0:T(1,128)S(1)} %get-tuple-element.55), channel_id=1, source_target_pairs={{0,8},{1,17},{2,10},{3,19},{4,12},{5,21},{6,14},{7,23},{8,0},{9,25... | collective-permute-start | bytes 7688 | tf_op jit(solution)/shard_map/ppermute | solution.py:373
  36.5 6.4 %collective-permute-start.13 = (f32[1,640]{1,0:T(1,128)S(1)}, f32[1,640]{1,0:T(1,128)S(1)}, u32[]{:S(2)}, u32[]{:S(2)}) collective-permute-start(f32[1,640]{1,0:T(1,128)S(1)} %max.26), channel_id=1, source_target_pairs={{4,0},{2,6},{0,2},{7,1},{5,7},{3,5},{12,8},{10,14},{8,10},{15,9},{... | collective-permute-start | bytes 7688 | tf_op jit(solution)/shard_map/ppermute | solution.py:368
  38.9 4.0 %collective-permute-start.16 = (f32[1,320]{1,0:T(1,128)S(1)}, f32[1,320]{1,0:T(1,128)S(1)}, u32[]{:S(2)}, u32[]{:S(2)}) collective-permute-start(f32[1,320]{1,0:T(1,128)S(1)} %slice_maximum_fusion), channel_id=1, source_target_pairs={{0,16},{1,9},{2,18},{3,11},{4,20},{5,13},{6,22},{7,15},{8,24},{9,1... | collective-permute-start | bytes 3848 | tf_op jit(solution)/shard_map/ppermute | solution.py:376
  42.9 1.2 %collective-permute-start.14 = (f32[1,320]{1,0:T(1,128)S(1)}, f32[1,320]{1,0:T(1,128)S(1)}, u32[]{:S(2)}, u32[]{:S(2)}) collective-permute-start(f32[1,320]{1,0:T(1,128)S(1)} %slice.17), channel_id=1, source_target_pairs={{0,1},{1,0},{2,3},{3,2},{4,5},{5,4},{6,7},{7,6},{8,9},{9,8},{10,11... | collective-permute-start | bytes 3848 | tf_op jit(solution)/shard_map/ppermute | solution.py:372

commit v16 on v15

--- a/solution.py
+++ b/solution.py
@@ -87,26 +87,34 @@
     return jnp.max(partial.T, axis=0, keepdims=True)[:, :rows]
 
 
-def meet(units, parts, rows, span, held, held_codes):
+def meet(units, parts, rows, span, held, held_codes, sims):
     columns = [turned_to_column(row, rows) for row, _ in parts]
     starts = [(block, top) for block in range(len(parts)) for top in range(0, rows, CHUNK)]
     partial = {start: jnp.full((CHUNK, LANES), -1.0, jnp.float32) for start in starts}
     best_held = []
-    for at in range(0, held.shape[0], TILE):
-        tile = min(TILE, held.shape[0] - at)
-        sims = lax.dot_general(
+
+    def form(at):
+        end = min(at + TILE, held.shape[0])
+        sims[:, at:end] = lax.dot_general(
             units[...],
-            held[at : at + tile, :],
+            held[at:end, :],
             (((1,), (1,)), ((), ())),
             preferred_element_type=jnp.float32,
         )
+
+    total = held.shape[0]
+    form(0)
+    for at in range(0, total, TILE):
+        tile = min(TILE, total - at)
+        if at + TILE < total:
+            form(at + TILE)
         best = [jnp.full((CHUNK, LANES), -1.0, jnp.float32) for _ in range(0, tile, LANES)]
         for block, top in starts:
             to_block, to_held = parts[block][1]
             mine = columns[block][top : top + CHUNK]
             line = block * rows + top
             for lane in range(0, tile, LANES):
-                part = sims[line : line + CHUNK, lane : lane + LANES]
+                part = sims[line : line + CHUNK, at + lane : at + lane + LANES]
                 gap = mine - held_codes[:, at + lane : at + lane + LANES]
                 if to_block and to_held:
                     part = jnp.where(jnp.abs(gap) < span, part, -1.0)
@@ -187,29 +195,29 @@
 
 
 def plane_kernel(rows, span, lengths, block, partner, *refs):
-    *pieces, best, mine, held, units = refs
+    *pieces, best, mine, held, units, sims = refs
     row = hold(regrouped(pieces, lengths), held, rows, span)
     pair(units, block, partner, rows)
     parts = [(codes(block, rows, span), OWN), (codes(partner, rows, span), HELD)]
-    (mine[...],), theirs = meet(units, parts, rows, span, held, row)
+    (mine[...],), theirs = meet(units, parts, rows, span, held, row, sims)
     best[...] = theirs[:, : best.shape[1]]
 
 
-def rest_kernel(rows, span, block, partner, held, row, best, mine, units):
+def rest_kernel(rows, span, block, partner, held, row, best, mine, units, sims):
     count = best.shape[1]
     start = held.shape[0] - up(count, LANES)
     held, row = held.at[start:, :], row[:, start:]
     pair(units, block, partner, rows)
     parts = [(codes(block, rows, span), OWN), (codes(partner, rows, span), HELD)]
-    (mine[...],), theirs = meet(units, parts, rows, span, held, row)
+    (mine[...],), theirs = meet(units, parts, rows, span, held, row, sims)
     best[...] = theirs[:, row.shape[1] - count :]
 
 
 def line_kernel(rows, span, together, count, first, second, held, row, *refs):
-    bests, outs, (found, units) = refs[:count], refs[count:-2], refs[-2:]
+    bests, outs, (found, units, sims) = refs[:count], refs[count:-3], refs[-3:]
     pair(units, first, second, rows)
     parts = [(codes(second, rows, span, first=place), TWO) for place in (CODES, 0)]
-    mine, theirs = meet(units, parts, rows, span, held, row[...])
+    mine, theirs = meet(units, parts, rows, span, held, row[...], sims)
     found[...] = jnp.concatenate(mine, axis=1)
     best = jnp.maximum(jnp.concatenate([best[...] for best in bests], axis=1), theirs)
     for out, places in zip(outs, together):
@@ -230,6 +238,7 @@
         scratch_shapes=[
             pltpu.VMEM((up(total, LANES), width), jnp.bfloat16),
             pltpu.VMEM((2 * rows, width), jnp.bfloat16),
+            pltpu.VMEM((2 * rows, up(total, LANES)), jnp.float32),
         ],
         compiler_params=pltpu.CompilerParams(vmem_limit_bytes=12 << 20),
         cost_estimate=pl.CostEstimate(flops=rows, bytes_accessed=rows, transcendentals=0),
@@ -243,7 +252,10 @@
             jax.ShapeDtypeStruct((1, count), jnp.float32),
             jax.ShapeDtypeStruct((1, rows), jnp.float32),
         ],
-        scratch_shapes=[pltpu.VMEM((2 * rows, block.shape[1]), jnp.bfloat16)],
+        scratch_shapes=[
+            pltpu.VMEM((2 * rows, block.shape[1]), jnp.bfloat16),
+            pltpu.VMEM((2 * rows, up(count, LANES)), jnp.float32),
+        ],
         compiler_params=pltpu.CompilerParams(vmem_limit_bytes=12 << 20),
         cost_estimate=pl.CostEstimate(flops=rows, bytes_accessed=rows, transcendentals=0),
     )(block, partner, held, row)
@@ -254,7 +266,10 @@
     *bests, found = pl.pallas_call(
         functools.partial(line_kernel, rows, span, together, len(bests)),
         out_shape=outs + [jax.ShapeDtypeStruct((1, 2 * rows), jnp.float32)],
-        scratch_shapes=[pltpu.VMEM((2 * rows, second.shape[1]), jnp.bfloat16)],
+        scratch_shapes=[
+            pltpu.VMEM((2 * rows, second.shape[1]), jnp.bfloat16),
+            pltpu.VMEM((2 * rows, held.shape[0]), jnp.float32),
+        ],
         compiler_params=pltpu.CompilerParams(vmem_limit_bytes=12 << 20),
         cost_estimate=pl.CostEstimate(flops=rows, bytes_accessed=rows, transcendentals=0),
     )(first, second, held, row, *bests)

time: 44.9 us -> 44.9 us (level)
  no operation moved by 1% of the time
where the time goes in v16:
time: 44.9 us; the launch traced here: 44.7 us
  starting transfers between devices  20.3 us (45%)
  waiting for transfers between devices  14.2 us (32%)
  Pallas kernels  6.76 us (15%)
  other arithmetic  2.07 us (5%)
  local copies, waits for them, and re-layouts  1.11 us (2%)
    ppermute x2, waiting for transfers between devices, shards(): from_corner = [lax.ppermute(part, BOTH, second) for part in from_first]  6.05 us
    ppermute x1, starting transfers between devices, shards(): raw = [lax.ppermute(embeddings, BOTH, pairs) for pairs in rounds]  5.49 us
    pallas_call x2, Pallas kernels, line(): pl.pallas_call(functools.partial(line_kernel, rows, span, together, len(b...  4.06 us
    ppermute x2, waiting for transfers between devices, shards(): from_first = [lax.ppermute(part, BOTH, first) for part in parts]  3.8 us
    ppermute x1, waiting for transfers between devices, shards(): lax.ppermute(kept[:, 2 * at * rows:2 * (at + 1) * rows], BOTH, back(pairs))  2.39 us
    ppermute x1, starting transfers between devices, shards(): lax.ppermute(kept[:, 2 * at * rows:2 * (at + 1) * rows], BOTH, back(pairs))  2.38 us
    ppermute x2, starting transfers between devices, shards(): from_first = [lax.ppermute(part, BOTH, first) for part in parts]  2.09 us
    ppermute x2, starting transfers between devices, shards(): from_corner = [lax.ppermute(part, BOTH, second) for part in from_first]  2.09 us
  transfers between devices with their start and end apart: 17, of which 6 were waited for; matrix products, arithmetic and copies ran while one was open for 3% of the time, Pallas kernels for 11%

profile of v16, /device:TPU:0, one launch (start us, length us, event | category | flops | bytes accessed | tf_op | source)
XLA Modules:
  0.0 44.7 jit_solution(6750125738940927284)
XLA Ops:
  0.5 5.5 %collective-permute-start.7 = (bf16[320,768]{1,0:T(8,128)(2,1)}, bf16[320,768]{1,0:T(8,128)(2,1)S(1)}, u32[]{:S(2)}, u32[]{:S(2)}) collective-permute-start(bf16[320,768]{1,0:T(8,128)(2,1)} %embeddings.1), channel_id=1, source_target_pairs={{0,4},{6,2},{2,0},{1,7},{7,5},{5,3},{8,12},{14,10},{10,8},{9,15},{... | collective-permute-start | bytes 1474568 | tf_op jit(solution)/shard_map/ppermute | solution.py:333
  5.9 0.7 %multiply_reduce_fusion = s32[320]{0:T(512)S(1)} fusion(s32[320,1]{0,1:T(1,128)} %param.4), kind=kLoop, calls=%fused_computation.6 | loop fusion | flops 640 | bytes 2560 | tf_op jit(solution)/shard_map/mul | solution.py:334
  6.6 0.7 %add.15.named = s32[320]{0:T(512)S(1)} add(s32[320]{0:T(512)S(1)} %multiply_reduce_fusion, s32[320]{0:T(512)} %param.5) | non-fusion elementwise | flops 320 | bytes 3840 | tf_op jit(solution)/shard_map/add | solution.py:334
  7.3 1.0 %copy-done.2 = bf16[320,768]{1,0:T(8,128)(2,1)S(1)} copy-done((bf16[320,768]{1,0:T(8,128)(2,1)S(1)}, bf16[320,768]{1,0:T(8,128)(2,1)}, u32[]{:S(2)}) %copy-start.2) | copy-done | bytes 491544
  8.5 1.6 %collective-permute-start = (bf16[160,768]{1,0:T(8,128)(2,1)S(1)}, bf16[160,768]{1,0:T(8,128)(2,1)S(1)}, u32[]{:S(2)}, u32[]{:S(2)}) collective-permute-start(bf16[160,768]{1,0:T(8,128)(2,1)S(1)} %get-tuple-element.32), channel_id=1, source_target_pairs={{0,8},{1,17},{2,10},{3,19},{4,12},{5,21},{6,14},{7,23},{8,0},{9,25... | collective-permute-start | bytes 737288 | tf_op jit(solution)/shard_map/ppermute | solution.py:341
  10.6 0.7 %collective-permute-start.6 = (bf16[16,768]{1,0:T(8,128)(2,1)S(1)}, bf16[16,768]{1,0:T(8,128)(2,1)S(1)}, u32[]{:S(2)}, u32[]{:S(2)}) collective-permute-start(bf16[16,768]{1,0:T(8,128)(2,1)S(1)} %get-tuple-element.34.other_codes), channel_id=1, source_target_pairs={{0,1},{1,0},{2,3},{3,2},{4,5},{5,4},{6,7},{7,6},{8,9},{9,8},{10,11... | collective-permute-start | bytes 73736 | tf_op jit(solution)/shard_map/ppermute | solution.py:343
  11.3 0.8 %collective-permute-done.6.codes_of = bf16[16,768]{1,0:T(8,128)(2,1)S(1)} collective-permute-done((bf16[16,768]{1,0:T(8,128)(2,1)S(1)}, bf16[16,768]{1,0:T(8,128)(2,1)S(1)}, u32[]{:S(2)}, u32[]{:S(2)}) %collective-permute-start.6) | collective-permute-done | bytes 24608 | tf_op jit(solution)/shard_map/ppermute | solution.py:343
  12.2 1.5 %collective-permute-start.2 = (bf16[336,768]{1,0:T(8,128)(2,1)S(1)}, bf16[336,768]{1,0:T(8,128)(2,1)S(1)}, u32[]{:S(2)}, u32[]{:S(2)}) collective-permute-start(bf16[336,768]{1,0:T(8,128)(2,1)S(1)} %get-tuple-element.31.block.refs_0_), channel_id=1, source_target_pairs={{0,16},{1,9},{2,18},{3,11},{4,20},{5,13},{6,22},{7,15},{8,24},{9,1... | collective-permute-start | bytes 1548296 | tf_op jit(solution)/shard_map/ppermute | solution.py:342
  13.9 1.9 %collective-permute-start.10 = (bf16[336,768]{1,0:T(8,128)(2,1)S(1)}, bf16[336,768]{1,0:T(8,128)(2,1)S(1)}, u32[]{:S(2)}, u32[]{:S(2)}) collective-permute-start(bf16[336,768]{1,0:T(8,128)(2,1)S(1)} %shard_map.38.partner), channel_id=1, source_target_pairs={{0,4},{6,2},{2,0},{1,7},{7,5},{5,3},{8,12},{14,10},{10,8},{9,15},{... | collective-permute-start | bytes 1548296 | tf_op jit(solution)/shard_map/ppermute | solution.py:345
  15.8 0.6 %collective-permute-start.3 = (bf16[160,768]{1,0:T(8,128)(2,1)S(1)}, bf16[160,768]{1,0:T(8,128)(2,1)S(1)}, u32[]{:S(2)}, u32[]{:S(2)}) collective-permute-start(bf16[160,768]{1,0:T(8,128)(2,1)S(1)} %collective-permute-done.refs_1_), channel_id=1, source_target_pairs={{0,16},{1,9},{2,18},{3,11},{4,20},{5,13},{6,22},{7,15},{8,24},{9,1... | collective-permute-start | bytes 737288 | tf_op jit(solution)/shard_map/ppermute | solution.py:346
  16.4 3.8 %collective-permute-done.1.refs_2_ = bf16[176,768]{1,0:T(8,128)(2,1)S(1)} collective-permute-done((bf16[176,768]{1,0:T(8,128)(2,1)S(1)}, bf16[176,768]{1,0:T(8,128)(2,1)S(1)}, u32[]{:S(2)}, u32[]{:S(2)}) %collective-permute-start.1) | collective-permute-done | bytes 270368 | tf_op jit(solution)/shard_map/ppermute | solution.py:341
  20.2 1.5 %collective-permute-start.4 = (bf16[176,768]{1,0:T(8,128)(2,1)S(1)}, bf16[176,768]{1,0:T(8,128)(2,1)S(1)}, u32[]{:S(2)}, u32[]{:S(2)}) collective-permute-start(bf16[176,768]{1,0:T(8,128)(2,1)S(1)} %collective-permute-done.1.refs_2_), channel_id=1, source_target_pairs={{0,16},{1,9},{2,18},{3,11},{4,20},{5,13},{6,22},{7,15},{8,24},{9,1... | collective-permute-start | bytes 811016 | tf_op jit(solution)/shard_map/ppermute | solution.py:346
  22.0 4.2 %collective-permute-done.3.refs_4_ = bf16[160,768]{1,0:T(8,128)(2,1)S(1)} collective-permute-done((bf16[160,768]{1,0:T(8,128)(2,1)S(1)}, bf16[160,768]{1,0:T(8,128)(2,1)S(1)}, u32[]{:S(2)}, u32[]{:S(2)}) %collective-permute-start.3) | collective-permute-done | bytes 245792 | tf_op jit(solution)/shard_map/ppermute | solution.py:346
  26.2 1.0 %shard_map.39 = (f32[1,640]{1,0:T(1,128)S(1)}, f32[1,320]{1,0:T(1,128)S(1)}) custom-call(bf16[336,768]{1,0:T(8,128)(2,1)S(1)} %get-tuple-element.31.block.refs_0_, bf16[336,768]{1,0:T(8,128)(2,1)S(1)} %shard_map.38.partner, bf16[336,768]{1,0:T(8,128)(2,1)S(1)} %get-tuple-element.31.block.refs_0_, bf16[160,768]{1,0:T(8,128)(2,1)S(1)} %collective-permute-done.refs_1_, ...), custom_call_target="tpu_custom_call" | custom-call | flops 320 | bytes 320 | tf_op jit(solution)/shard_map/pallas_call | solution.py:232
  27.2 1.9 %collective-permute-done.4.refs_5_ = bf16[176,768]{1,0:T(8,128)(2,1)S(1)} collective-permute-done((bf16[176,768]{1,0:T(8,128)(2,1)S(1)}, bf16[176,768]{1,0:T(8,128)(2,1)S(1)}, u32[]{:S(2)}, u32[]{:S(2)}) %collective-permute-start.4) | collective-permute-done | bytes 270368 | tf_op jit(solution)/shard_map/ppermute | solution.py:346
  29.3 1.0 %shard_map.42 = (f32[1,640]{1,0:T(1,128)S(1)}, f32[1,320]{1,0:T(1,128)S(1)}) custom-call(bf16[336,768]{1,0:T(8,128)(2,1)S(1)} %get-tuple-element.31.block.refs_0_, bf16[336,768]{1,0:T(8,128)(2,1)S(1)} %shard_map.38.partner, bf16[1280,768]{1,0:T(8,128)(2,1)S(1)} %get-tuple-element.42.held, f32[1,1280]{1,0:T(1,128)S(1)} %get-tuple-element.43.row), custom_call_target="tpu_custom_call" | custom-call | flops 320 | bytes 320 | tf_op jit(solution)/shard_map/pallas_call | solution.py:249
  30.4 2.0 %shard_map.43 = (f32[1,1280]{1,0:T(1,128)S(1)}, f32[1,640]{1,0:T(1,128)S(1)}) custom-call(bf16[320,768]{1,0:T(8,128)(2,1)S(1)} %get-tuple-element.46.first, bf16[336,768]{1,0:T(8,128)(2,1)S(1)} %collective-permute-done.10.second, bf16[1280,768]{1,0:T(8,128)(2,1)S(1)} %get-tuple-element.42.held, f32[1,1280]{1,0:T(1,128)S(1)} %get-tuple-element.43.row, ...), custom_call_target="tpu_custom_call" | custom-call | flops 320 | bytes 320 | tf_op jit(solution)/shard_map/pallas_call | solution.py:266
  32.4 2.0 %shard_map.44 = (f32[1,320]{1,0:T(1,128)S(1)}, f32[1,640]{1,0:T(1,128)S(1)}, f32[1,320]{1,0:T(1,128)S(1)}, f32[1,640]{1,0:T(1,128)S(1)}) custom-call(bf16[320,768]{1,0:T(8,128)(2,1)S(1)} %copy-done.1, bf16[336,768]{1,0:T(8,128)(2,1)S(1)} %collective-permute-done.11.second, bf16[1280,768]{1,0:T(8,128)(2,1)S(1)} %get-tuple-element.42.held, ...), custom_call_target="tpu_custom_call" | custom-call | flops 320 | bytes 320 | tf_op jit(solution)/shard_map/pallas_call | solution.py:266
  34.9 1.5 %collective-permute-start.15 = (f32[1,640]{1,0:T(1,128)S(1)}, f32[1,640]{1,0:T(1,128)S(1)}, u32[]{:S(2)}, u32[]{:S(2)}) collective-permute-start(f32[1,640]{1,0:T(1,128)S(1)} %get-tuple-element.55), channel_id=1, source_target_pairs={{0,8},{1,17},{2,10},{3,19},{4,12},{5,21},{6,14},{7,23},{8,0},{9,25... | collective-permute-start | bytes 7688 | tf_op jit(solution)/shard_map/ppermute | solution.py:388
  36.5 2.4 %collective-permute-start.13 = (f32[1,640]{1,0:T(1,128)S(1)}, f32[1,640]{1,0:T(1,128)S(1)}, u32[]{:S(2)}, u32[]{:S(2)}) collective-permute-start(f32[1,640]{1,0:T(1,128)S(1)} %max.26), channel_id=1, source_target_pairs={{4,0},{2,6},{0,2},{7,1},{5,7},{3,5},{12,8},{10,14},{8,10},{15,9},{... | collective-permute-start | bytes 7688 | tf_op jit(solution)/shard_map/ppermute | solution.py:383
  38.9 1.5 %collective-permute-start.16 = (f32[1,320]{1,0:T(1,128)S(1)}, f32[1,320]{1,0:T(1,128)S(1)}, u32[]{:S(2)}, u32[]{:S(2)}) collective-permute-start(f32[1,320]{1,0:T(1,128)S(1)} %slice_maximum_fusion), channel_id=1, source_target_pairs={{0,16},{1,9},{2,18},{3,11},{4,20},{5,13},{6,22},{7,15},{8,24},{9,1... | collective-permute-start | bytes 3848 | tf_op jit(solution)/shard_map/ppermute | solution.py:391
  40.4 2.4 %collective-permute-done.13 = f32[1,640]{1,0:T(1,128)S(1)} collective-permute-done((f32[1,640]{1,0:T(1,128)S(1)}, f32[1,640]{1,0:T(1,128)S(1)}, u32[]{:S(2)}, u32[]{:S(2)}) %collective-permute-start.13) | collective-permute-done | bytes 2592 | tf_op jit(solution)/shard_map/ppermute | solution.py:383
  42.9 1.1 %collective-permute-done.14 = f32[1,320]{1,0:T(1,128)S(1)} collective-permute-done((f32[1,320]{1,0:T(1,128)S(1)}, f32[1,320]{1,0:T(1,128)S(1)}, u32[]{:S(2)}, u32[]{:S(2)}) %collective-permute-start.14) | collective-permute-done | bytes 1312 | tf_op jit(solution)/shard_map/ppermute | solution.py:387
  44.1 0.6 %fusion.2 = f32[320]{0:T(512)} fusion(f32[1,320]{1,0:T(1,128)S(1)} %collective-permute-done.16, f32[1,640]{1,0:T(1,128)S(1)} %collective-permute-done.15, f32[1,320]{1,0:T(1,128)S(1)} %collective-permute-done.14, f32[1,640]{1,0:T(1,128)S(1)} %broadcast_select_fusion, f32[1,320]{1,0:T(1,128)S(1)} %get-tuple-element.52, f32[1,320]{1,0:T(1,128)S(1)} %get-tuple-element.50, ...), kind=kLoop, calls=%fused_computation.7 | loop fusion | flops 1920 | bytes 10240 | tf_op jit(solution)/shard_map/max | solution.py:392
  (31 shorter events, 2.5 us)
Async XLA Ops:
  0.0 13.7 %collective-permute-start.5 = (bf16[320,768]{1,0:T(8,128)(2,1)}, bf16[320,768]{1,0:T(8,128)(2,1)S(1)}, u32[]{:S(2)}, u32[]{:S(2)}) collective-permute-start(bf16[320,768]{1,0:T(8,128)(2,1)} %embeddings.1), channel_id=1, source_target_pairs={{0,1},{1,0},{2,3},{3,2},{4,5},{5,4},{6,7},{7,6},{8,9},{9,8},{10,11... | collective-permute-start | bytes 1474568 | tf_op jit(solution)/shard_map/ppermute | solution.py:332
  0.5 21.3 %collective-permute-start.7 = (bf16[320,768]{1,0:T(8,128)(2,1)}, bf16[320,768]{1,0:T(8,128)(2,1)S(1)}, u32[]{:S(2)}, u32[]{:S(2)}) collective-permute-start(bf16[320,768]{1,0:T(8,128)(2,1)} %embeddings.1), channel_id=1, source_target_pairs={{0,4},{6,2},{2,0},{1,7},{7,5},{5,3},{8,12},{14,10},{10,8},{9,15},{... | collective-permute-start | bytes 1474568 | tf_op jit(solution)/shard_map/ppermute | solution.py:333
  7.3 1.0 %copy-start.2 = (bf16[320,768]{1,0:T(8,128)(2,1)S(1)}, bf16[320,768]{1,0:T(8,128)(2,1)}, u32[]{:S(2)}) copy-start(bf16[320,768]{1,0:T(8,128)(2,1)} %embeddings.1) | copy-start | bytes 1474564
  8.5 7.3 %collective-permute-start = (bf16[160,768]{1,0:T(8,128)(2,1)S(1)}, bf16[160,768]{1,0:T(8,128)(2,1)S(1)}, u32[]{:S(2)}, u32[]{:S(2)}) collective-permute-start(bf16[160,768]{1,0:T(8,128)(2,1)S(1)} %get-tuple-element.32), channel_id=1, source_target_pairs={{0,8},{1,17},{2,10},{3,19},{4,12},{5,21},{6,14},{7,23},{8,0},{9,25... | collective-permute-start | bytes 737288 | tf_op jit(solution)/shard_map/ppermute | solution.py:341
  10.1 10.1 %collective-permute-start.1 = (bf16[176,768]{1,0:T(8,128)(2,1)S(1)}, bf16[176,768]{1,0:T(8,128)(2,1)S(1)}, u32[]{:S(2)}, u32[]{:S(2)}) collective-permute-start(bf16[176,768]{1,0:T(8,128)(2,1)S(1)} %get-tuple-element.33), channel_id=1, source_target_pairs={{0,8},{1,17},{2,10},{3,19},{4,12},{5,21},{6,14},{7,23},{8,0},{9,25... | collective-permute-start | bytes 811016 | tf_op jit(solution)/shard_map/ppermute | solution.py:341
  10.6 1.6 %collective-permute-start.6 = (bf16[16,768]{1,0:T(8,128)(2,1)S(1)}, bf16[16,768]{1,0:T(8,128)(2,1)S(1)}, u32[]{:S(2)}, u32[]{:S(2)}) collective-permute-start(bf16[16,768]{1,0:T(8,128)(2,1)S(1)} %get-tuple-element.34.other_codes), channel_id=1, source_target_pairs={{0,1},{1,0},{2,3},{3,2},{4,5},{5,4},{6,7},{7,6},{8,9},{9,8},{10,11... | collective-permute-start | bytes 73736 | tf_op jit(solution)/shard_map/ppermute | solution.py:343
  12.2 16.9 %collective-permute-start.2 = (bf16[336,768]{1,0:T(8,128)(2,1)S(1)}, bf16[336,768]{1,0:T(8,128)(2,1)S(1)}, u32[]{:S(2)}, u32[]{:S(2)}) collective-permute-start(bf16[336,768]{1,0:T(8,128)(2,1)S(1)} %get-tuple-element.31.block.refs_0_), channel_id=1, source_target_pairs={{0,16},{1,9},{2,18},{3,11},{4,20},{5,13},{6,22},{7,15},{8,24},{9,1... | collective-permute-start | bytes 1548296 | tf_op jit(solution)/shard_map/ppermute | solution.py:342
  13.9 16.4 %collective-permute-start.10 = (bf16[336,768]{1,0:T(8,128)(2,1)S(1)}, bf16[336,768]{1,0:T(8,128)(2,1)S(1)}, u32[]{:S(2)}, u32[]{:S(2)}) collective-permute-start(bf16[336,768]{1,0:T(8,128)(2,1)S(1)} %shard_map.38.partner), channel_id=1, source_target_pairs={{0,4},{6,2},{2,0},{1,7},{7,5},{5,3},{8,12},{14,10},{10,8},{9,15},{... | collective-permute-start | bytes 1548296 | tf_op jit(solution)/shard_map/ppermute | solution.py:345
  15.8 10.3 %collective-permute-start.3 = (bf16[160,768]{1,0:T(8,128)(2,1)S(1)}, bf16[160,768]{1,0:T(8,128)(2,1)S(1)}, u32[]{:S(2)}, u32[]{:S(2)}) collective-permute-start(bf16[160,768]{1,0:T(8,128)(2,1)S(1)} %collective-permute-done.refs_1_), channel_id=1, source_target_pairs={{0,16},{1,9},{2,18},{3,11},{4,20},{5,13},{6,22},{7,15},{8,24},{9,1... | collective-permute-start | bytes 737288 | tf_op jit(solution)/shard_map/ppermute | solution.py:346
  20.2 8.9 %collective-permute-start.4 = (bf16[176,768]{1,0:T(8,128)(2,1)S(1)}, bf16[176,768]{1,0:T(8,128)(2,1)S(1)}, u32[]{:S(2)}, u32[]{:S(2)}) collective-permute-start(bf16[176,768]{1,0:T(8,128)(2,1)S(1)} %collective-permute-done.1.refs_2_), channel_id=1, source_target_pairs={{0,16},{1,9},{2,18},{3,11},{4,20},{5,13},{6,22},{7,15},{8,24},{9,1... | collective-permute-start | bytes 811016 | tf_op jit(solution)/shard_map/ppermute | solution.py:346
  21.9 7.2 %collective-permute-start.8 = (bf16[160,768]{1,0:T(8,128)(2,1)S(1)}, bf16[160,768]{1,0:T(8,128)(2,1)S(1)}, u32[]{:S(2)}, u32[]{:S(2)}) collective-permute-start(bf16[160,768]{1,0:T(8,128)(2,1)S(1)} %get-tuple-element.38), channel_id=1, source_target_pairs={{0,1},{1,0},{2,3},{3,2},{4,5},{5,4},{6,7},{7,6},{8,9},{9,8},{10,11... | collective-permute-start | bytes 737288 | tf_op jit(solution)/shard_map/ppermute | solution.py:351
  26.2 2.9 %collective-permute-start.9 = (bf16[160,768]{1,0:T(8,128)(2,1)S(1)}, bf16[160,768]{1,0:T(8,128)(2,1)S(1)}, u32[]{:S(2)}, u32[]{:S(2)}) collective-permute-start(bf16[160,768]{1,0:T(8,128)(2,1)S(1)} %get-tuple-element.39), channel_id=1, source_target_pairs={{0,1},{1,0},{2,3},{3,2},{4,5},{5,4},{6,7},{7,6},{8,9},{9,8},{10,11... | collective-permute-start | bytes 737288 | tf_op jit(solution)/shard_map/ppermute | solution.py:351
  29.2 1.0 %copy-start = (bf16[320,768]{1,0:T(8,128)(2,1)}, bf16[320,768]{1,0:T(8,128)(2,1)S(1)}, u32[]{:S(2)}) copy-start(bf16[320,768]{1,0:T(8,128)(2,1)S(1)} %get-tuple-element.40.first) | copy-start | bytes 1474564
  30.3 2.1 %collective-permute-start.11 = (bf16[336,768]{1,0:T(8,128)(2,1)S(1)}, bf16[336,768]{1,0:T(8,128)(2,1)S(1)}, u32[]{:S(2)}, u32[]{:S(2)}) collective-permute-start(bf16[336,768]{1,0:T(8,128)(2,1)S(1)} %collective-permute-done.10.second), channel_id=1, source_target_pairs={{0,1},{1,0},{2,3},{3,2},{4,5},{5,4},{6,7},{7,6},{8,9},{9,8},{10,11... | collective-permute-start | bytes 1548296 | tf_op jit(solution)/shard_map/ppermute | solution.py:366
  30.4 2.0 %copy-start.1 = (bf16[320,768]{1,0:T(8,128)(2,1)S(1)}, bf16[320,768]{1,0:T(8,128)(2,1)}, u32[]{:S(2)}) copy-start(bf16[320,768]{1,0:T(8,128)(2,1)} %copy-done) | copy-start | bytes 1474564
  34.5 2.0 %collective-permute-start.12 = (f32[1,640]{1,0:T(1,128)S(1)}, f32[1,640]{1,0:T(1,128)S(1)}, u32[]{:S(2)}, u32[]{:S(2)}) collective-permute-start(f32[1,640]{1,0:T(1,128)S(1)} %get-tuple-element.54), channel_id=1, source_target_pairs={{0,1},{1,0},{2,3},{3,2},{4,5},{5,4},{6,7},{7,6},{8,9},{9,8},{10,11... | collective-permute-start | bytes 7688 | tf_op jit(solution)/shard_map/ppermute | solution.py:380
  34.9 3.9 %collective-permute-start.15 = (f32[1,640]{1,0:T(1,128)S(1)}, f32[1,640]{1,0:T(1,128)S(1)}, u32[]{:S(2)}, u32[]{:S(2)}) collective-permute-start(f32[1,640]{1,0:T(1,128)S(1)} %get-tuple-element.55), channel_id=1, source_target_pairs={{0,8},{1,17},{2,10},{3,19},{4,12},{5,21},{6,14},{7,23},{8,0},{9,25... | collective-permute-start | bytes 7688 | tf_op jit(solution)/shard_map/ppermute | solution.py:388
  36.5 6.4 %collective-permute-start.13 = (f32[1,640]{1,0:T(1,128)S(1)}, f32[1,640]{1,0:T(1,128)S(1)}, u32[]{:S(2)}, u32[]{:S(2)}) collective-permute-start(f32[1,640]{1,0:T(1,128)S(1)} %max.26), channel_id=1, source_target_pairs={{4,0},{2,6},{0,2},{7,1},{5,7},{3,5},{12,8},{10,14},{8,10},{15,9},{... | collective-permute-start | bytes 7688 | tf_op jit(solution)/shard_map/ppermute | solution.py:383
  38.9 4.0 %collective-permute-start.16 = (f32[1,320]{1,0:T(1,128)S(1)}, f32[1,320]{1,0:T(1,128)S(1)}, u32[]{:S(2)}, u32[]{:S(2)}) collective-permute-start(f32[1,320]{1,0:T(1,128)S(1)} %slice_maximum_fusion), channel_id=1, source_target_pairs={{0,16},{1,9},{2,18},{3,11},{4,20},{5,13},{6,22},{7,15},{8,24},{9,1... | collective-permute-start | bytes 3848 | tf_op jit(solution)/shard_map/ppermute | solution.py:391
  42.9 1.2 %collective-permute-start.14 = (f32[1,320]{1,0:T(1,128)S(1)}, f32[1,320]{1,0:T(1,128)S(1)}, u32[]{:S(2)}, u32[]{:S(2)}) collective-permute-start(f32[1,320]{1,0:T(1,128)S(1)} %slice.17), channel_id=1, source_target_pairs={{0,1},{1,0},{2,3},{3,2},{4,5},{5,4},{6,7},{7,6},{8,9},{9,8},{10,11... | collective-permute-start | bytes 3848 | tf_op jit(solution)/shard_map/ppermute | solution.py:387

commit v17 on v15

--- a/solution.py
+++ b/solution.py
@@ -41,26 +41,26 @@
         out[...] = block[top : top + out.shape[0], :]
 
 
-def prepare_kernel(span, embeddings, named, block, codes_out, *parts_out):
+def prepare_kernel(embeddings, cluster, order_key, block, codes_out, *parts_out):
     rows, width = embeddings.shape
     unit_rows(embeddings, block)
-    names = named[...].reshape(1, rows)
-    keys = names & (span - 1)
-    parts = [keys >> 8, keys & 255, names >> (span.bit_length() - 1)]
+    keys = order_key[...].reshape(1, rows)
+    parts = [keys >> 8, keys & 255, cluster[...] + 1]
     parts = [part.astype(jnp.float32) for part in parts]
     parts = jnp.concatenate(parts + [jnp.zeros((EXTRA - CODES, rows), jnp.float32)], axis=0)
     parts = jnp.concatenate([parts, jnp.zeros((EXTRA, width - rows), jnp.float32)], axis=1)
     block[rows : rows + EXTRA, :] = parts.astype(jnp.bfloat16)
     codes_out[...] = block[rows : rows + EXTRA, :]
-    give_parts(block, parts_out)
-
-
-def complete_kernel(rows_of, codes_of, other_codes, block):
-    rows, width = rows_of.shape
-    unit_rows(rows_of, block)
-    named = [part[...].astype(jnp.float32)[0:CODES] for part in (codes_of, other_codes)]
-    named = jnp.concatenate(named + [jnp.zeros((EXTRA - 2 * CODES, width), jnp.float32)], axis=0)
-    block[rows:, :] = named.astype(jnp.bfloat16)
+    if parts_out:
+        give_parts(block, parts_out)
+
+
+def complete_kernel(block, other_codes, out):
+    rows = block.shape[0] - EXTRA
+    out[0:rows, :] = block[0:rows, :]
+    named = [part[...].astype(jnp.float32)[0:CODES] for part in (block.at[rows:, :], other_codes)]
+    rest = jnp.zeros((EXTRA - 2 * CODES, block.shape[1]), jnp.float32)
+    out[rows:, :] = jnp.concatenate(named + [rest], axis=0).astype(jnp.bfloat16)
 
 
 def unit_kernel(rows_of, block, *parts_out):
@@ -292,6 +292,7 @@
     other_core = everywhere(lambda p, g: (p, g ^ 1))
     first = everywhere(lambda p, g: (p ^ (1 + g % 2), g))
     second = everywhere(lambda p, g: (p ^ (2 - g % 2), g))
+    second_home = everywhere(lambda p, g: (p ^ (2 - g % 2), g ^ 1))
 
     rounds = line_rounds(chips)
     rounds += [[]] * (len(rounds) % 2)
@@ -314,20 +315,15 @@
         while span < rows * groups * members:
             span *= 2
         halves = (rows // 2, rows // 2 + EXTRA)
-        partner = lax.ppermute(embeddings, BOTH, other_core)
+        names = (cluster.reshape(1, rows), order_key)
         raw = [lax.ppermute(embeddings, BOTH, pairs) for pairs in rounds]
-        named = (cluster[:, 0] + 1) * span + order_key
-        block, codes_of, *parts = with_units(
-            functools.partial(prepare_kernel, span),
-            (rows + EXTRA, EXTRA, *halves),
-            embeddings,
-            named,
-        )
+        charge = [lax.ppermute(array, BOTH, other_core) for array in (embeddings, *names)]
+        block, _, *parts = with_units(prepare_kernel, (rows + EXTRA, EXTRA, *halves), *charge)
         from_first = [lax.ppermute(part, BOTH, first) for part in parts]
         from_second = [lax.ppermute(block, BOTH, second)]
-        other_codes = lax.ppermute(codes_of, BOTH, other_core)
-        (partner,) = with_units(complete_kernel, (rows + EXTRA,), partner, other_codes, codes_of)
-        near_other = [lax.ppermute(partner, BOTH, pairs) for pairs in rounds]
+        own, own_codes = with_units(prepare_kernel, (rows + EXTRA, EXTRA), embeddings, *names)
+        (both,) = with_units(complete_kernel, (rows + EXTRA,), block, own_codes)
+        near_other = [lax.ppermute(both, BOTH, pairs) for pairs in rounds]
         from_corner = [lax.ppermute(part, BOTH, second) for part in from_first]
         near = [
             list(with_units(unit_kernel, (rows, rows // 2, rows // 2), rows_of))
@@ -335,14 +331,14 @@
         ]
         far = [[lax.ppermute(piece, BOTH, other_core) for piece in blocks[1:]] for blocks in near]
 
-        results, kept, sent = [], [], []
-        best_two, mine = plane(block, partner, [[block], from_first], rows, span)
-        results.append(mine)
+        in_charge, results, kept, sent = [], [], [], []
+        best_two, mine = plane(block, own, [[block], from_first], rows, span)
+        in_charge.append(mine)
         *from_corner, best_two = lax.optimization_barrier((*from_corner, best_two))
         blocks = [[block], from_first, from_second, from_corner]
         held, row, far_units = gather(blocks, far[0], rows, span)
-        best_rest, mine = plane_rest(block, partner, held, row, 2 * rows, rows, span)
-        results.append(mine)
+        best_rest, mine = plane_rest(block, own, held, row, 2 * rows, rows, span)
+        in_charge.append(mine)
         bests = [best_two, best_rest]
         far = [far_units] + [jnp.concatenate(pieces, axis=0) for pieces in far[1:]]
         whole, last = [tuple(range(groups))], [(0,), (1, 3), (2,)]
@@ -371,10 +367,12 @@
             found = jnp.where(sender, found, -1.0)
             results += [found[:, :rows], lax.ppermute(found[:, rows:], BOTH, other_core)]
         from_x = lax.ppermute(bests[1], BOTH, first)
-        results.append(from_x[:, :rows])
+        in_charge += [bests[0], from_x[:, :rows]]
         onward = jnp.maximum(bests[2], from_x[:, rows:])
-        results.append(lax.ppermute(onward, BOTH, second))
-        return functools.reduce(jnp.maximum, results, bests[0]).reshape(rows)
+        results.append(lax.ppermute(onward, BOTH, second_home))
+        home = functools.reduce(jnp.maximum, in_charge)
+        results.append(lax.ppermute(home, BOTH, other_core))
+        return functools.reduce(jnp.maximum, results).reshape(rows)
 
     placed = (P(BOTH, None), P(BOTH, None), P(BOTH))
     return jax.shard_map(

time: 44.9 us -> 43.6 us (0.971)
  waiting for transfers between devices: 14.2 us -> 10.8 us
  starting transfers between devices: 20.3 us -> 21.9 us
  other arithmetic: 2.07 us -> 0.68 us
  local copies, waits for them, and re-layouts: 1.11 us -> 2.47 us
  Pallas kernels: 6.76 us -> 7.34 us
    ppermute x1, starting transfers between devices: 2.38 us -> 4.25 us  [shards(): lax.ppermute(kept[:, 2 * at * rows:2 * (at + 1) * rows], BOTH, back(pairs))]
    unnamed x6 -> x10, local copies, waits for them, and re-layouts: 1.04 us -> 2.4 us
    ppermute x2, waiting for transfers between devices: 6.05 us -> 4.74 us  [shards(): from_corner = [lax.ppermute(part, BOTH, second) for part in from_first]]
    ppermute x1, waiting for transfers between devices: 2.39 us -> 1.11 us  [shards(): lax.ppermute(kept[:, 2 * at * rows:2 * (at + 1) * rows], BOTH, back(pairs))]
    ppermute x1, waiting for transfers between devices: 1.13 us -> 0.32 us  [shards(): lax.ppermute(found[:, rows:], BOTH, other_core)]
    ppermute x4 -> x6, starting transfers between devices: 4.59 us -> 3.8 us  [the longest x1 1.92 us: shards(): near_other = [lax.ppermute(both, BOTH, pairs) for pairs in rounds]]
    mul x1 -> x0, other arithmetic: 0.7 us -> none  [shards(): named = (cluster[:, 0] + 1) * span + order_key]
    add x1 -> x0, other arithmetic: 0.68 us -> none  [shards(): named = (cluster[:, 0] + 1) * span + order_key]
  transfers between devices with their start and end apart: 17 -> 19, of which waited for: 6 -> 6; matrix products, arithmetic and copies ran while one was open for 3% -> 0% of each run, Pallas kernels for 11% -> 12%
where the time goes in v17:
time: 43.6 us; the launch traced here: 43.4 us
  starting transfers between devices  21.9 us (50%)
  waiting for transfers between devices  10.8 us (25%)
  Pallas kernels  7.34 us (17%)
  local copies, waits for them, and re-layouts  2.47 us (6%)
  other arithmetic  0.68 us (2%)
    ppermute x1, starting transfers between devices, shards(): raw = [lax.ppermute(embeddings, BOTH, pairs) for pairs in rounds]  5.49 us
    ppermute x2, waiting for transfers between devices, shards(): from_corner = [lax.ppermute(part, BOTH, second) for part in from_first]  4.74 us
    ppermute x1, starting transfers between devices, shards(): lax.ppermute(kept[:, 2 * at * rows:2 * (at + 1) * rows], BOTH, back(pairs))  4.25 us
    ppermute x2, waiting for transfers between devices, shards(): from_first = [lax.ppermute(part, BOTH, first) for part in parts]  4.11 us
    pallas_call x2, Pallas kernels, line(): pl.pallas_call(functools.partial(line_kernel, rows, span, together, len(b...  4.05 us
    unnamed x10, local copies, waits for them, and re-layouts  2.4 us
    ppermute x2, starting transfers between devices, shards(): from_corner = [lax.ppermute(part, BOTH, second) for part in from_first]  2.09 us
    ppermute x2, starting transfers between devices, shards(): from_first = [lax.ppermute(part, BOTH, first) for part in parts]  2.03 us
  transfers between devices with their start and end apart: 19, of which 6 were waited for; matrix products, arithmetic and copies ran while one was open for 0% of the time, Pallas kernels for 12%

profile of v17, /device:TPU:0, one launch (start us, length us, event | category | flops | bytes accessed | tf_op | source)
XLA Modules:
  0.0 43.4 jit_solution(560022935010582088)
XLA Ops:
  1.0 5.5 %collective-permute-start = (bf16[320,768]{1,0:T(8,128)(2,1)}, bf16[320,768]{1,0:T(8,128)(2,1)S(1)}, u32[]{:S(2)}, u32[]{:S(2)}) collective-permute-start(bf16[320,768]{1,0:T(8,128)(2,1)} %embeddings.1), channel_id=1, source_target_pairs={{0,4},{6,2},{2,0},{1,7},{7,5},{5,3},{8,12},{14,10},{10,8},{9,15},{... | collective-permute-start | bytes 1474568 | tf_op jit(solution)/shard_map/ppermute | solution.py:319
  6.5 0.7 %shard_map.38 = (bf16[336,768]{1,0:T(8,128)(2,1)S(1)}, bf16[16,768]{1,0:T(8,128)(2,1)}, bf16[160,768]{1,0:T(8,128)(2,1)S(1)}, bf16[176,768]{1,0:T(8,128)(2,1)S(1)}) custom-call(bf16[320,768]{1,0:T(8,128)(2,1)S(1)} %collective-permute-done.1.embeddings, s32[1,320]{1,0:T(1,128)S(1)} %collective-permute-done.2.cluster, s32[320]{0:T(512)S(1)} %collective-permute-done.3.order_key), custom_call_target="tpu_custom_call" | custom-call | flops 320 | bytes 320 | tf_op jit(solution)/shard_map/pallas_call | solution.py:73
  7.2 1.5 %collective-permute-start.5 = (bf16[160,768]{1,0:T(8,128)(2,1)S(1)}, bf16[160,768]{1,0:T(8,128)(2,1)S(1)}, u32[]{:S(2)}, u32[]{:S(2)}) collective-permute-start(bf16[160,768]{1,0:T(8,128)(2,1)S(1)} %get-tuple-element.35), channel_id=1, source_target_pairs={{0,8},{1,17},{2,10},{3,19},{4,12},{5,21},{6,14},{7,23},{8,0},{9,25... | collective-permute-start | bytes 737288 | tf_op jit(solution)/shard_map/ppermute | solution.py:322
  8.7 0.5 %collective-permute-start.7 = (bf16[176,768]{1,0:T(8,128)(2,1)S(1)}, bf16[176,768]{1,0:T(8,128)(2,1)S(1)}, u32[]{:S(2)}, u32[]{:S(2)}) collective-permute-start(bf16[176,768]{1,0:T(8,128)(2,1)S(1)} %get-tuple-element.36), channel_id=1, source_target_pairs={{0,8},{1,17},{2,10},{3,19},{4,12},{5,21},{6,14},{7,23},{8,0},{9,25... | collective-permute-start | bytes 811016 | tf_op jit(solution)/shard_map/ppermute | solution.py:322
  9.2 1.5 %collective-permute-start.9 = (bf16[336,768]{1,0:T(8,128)(2,1)S(1)}, bf16[336,768]{1,0:T(8,128)(2,1)S(1)}, u32[]{:S(2)}, u32[]{:S(2)}) collective-permute-start(bf16[336,768]{1,0:T(8,128)(2,1)S(1)} %get-tuple-element.33.block.refs_0_), channel_id=1, source_target_pairs={{0,16},{1,9},{2,18},{3,11},{4,20},{5,13},{6,22},{7,15},{8,24},{9,1... | collective-permute-start | bytes 1548296 | tf_op jit(solution)/shard_map/ppermute | solution.py:323
  10.8 1.0 %copy-done.2 = bf16[320,768]{1,0:T(8,128)(2,1)S(1)} copy-done((bf16[320,768]{1,0:T(8,128)(2,1)S(1)}, bf16[320,768]{1,0:T(8,128)(2,1)}, u32[]{:S(2)}) %copy-start.2) | copy-done | bytes 491544
  11.8 0.7 %copy-done.3 = s32[320]{0:T(512)S(1)} copy-done((s32[320]{0:T(512)S(1)}, s32[320]{0:T(512)}, u32[]{:S(2)}) %copy-start.3) | copy-done | bytes 1304
  12.5 0.7 %copy-done.4 = s32[320,1]{0,1:T(1,128)S(1)} copy-done((s32[320,1]{0,1:T(1,128)S(1)}, s32[320,1]{0,1:T(1,128)}, u32[]{:S(2)}) %copy-start.4) | copy-done | bytes 1304
  13.4 1.9 %collective-permute-start.4 = (bf16[336,768]{1,0:T(8,128)(2,1)S(1)}, bf16[336,768]{1,0:T(8,128)(2,1)S(1)}, u32[]{:S(2)}, u32[]{:S(2)}) collective-permute-start(bf16[336,768]{1,0:T(8,128)(2,1)S(1)} %shard_map.40), channel_id=1, source_target_pairs={{0,4},{6,2},{2,0},{1,7},{7,5},{5,3},{8,12},{14,10},{10,8},{9,15},{... | collective-permute-start | bytes 1548296 | tf_op jit(solution)/shard_map/ppermute | solution.py:326
  15.3 0.6 %collective-permute-start.6 = (bf16[160,768]{1,0:T(8,128)(2,1)S(1)}, bf16[160,768]{1,0:T(8,128)(2,1)S(1)}, u32[]{:S(2)}, u32[]{:S(2)}) collective-permute-start(bf16[160,768]{1,0:T(8,128)(2,1)S(1)} %collective-permute-done.5.refs_1_), channel_id=1, source_target_pairs={{0,16},{1,9},{2,18},{3,11},{4,20},{5,13},{6,22},{7,15},{8,24},{9,1... | collective-permute-start | bytes 737288 | tf_op jit(solution)/shard_map/ppermute | solution.py:327
  15.9 4.1 %collective-permute-done.7.refs_2_ = bf16[176,768]{1,0:T(8,128)(2,1)S(1)} collective-permute-done((bf16[176,768]{1,0:T(8,128)(2,1)S(1)}, bf16[176,768]{1,0:T(8,128)(2,1)S(1)}, u32[]{:S(2)}, u32[]{:S(2)}) %collective-permute-start.7) | collective-permute-done | bytes 270368 | tf_op jit(solution)/shard_map/ppermute | solution.py:322
  20.0 1.5 %collective-permute-start.8 = (bf16[176,768]{1,0:T(8,128)(2,1)S(1)}, bf16[176,768]{1,0:T(8,128)(2,1)S(1)}, u32[]{:S(2)}, u32[]{:S(2)}) collective-permute-start(bf16[176,768]{1,0:T(8,128)(2,1)S(1)} %collective-permute-done.7.refs_2_), channel_id=1, source_target_pairs={{0,16},{1,9},{2,18},{3,11},{4,20},{5,13},{6,22},{7,15},{8,24},{9,1... | collective-permute-start | bytes 811016 | tf_op jit(solution)/shard_map/ppermute | solution.py:327
  21.9 2.9 %collective-permute-done.6.refs_4_ = bf16[160,768]{1,0:T(8,128)(2,1)S(1)} collective-permute-done((bf16[160,768]{1,0:T(8,128)(2,1)S(1)}, bf16[160,768]{1,0:T(8,128)(2,1)S(1)}, u32[]{:S(2)}, u32[]{:S(2)}) %collective-permute-start.6) | collective-permute-done | bytes 245792 | tf_op jit(solution)/shard_map/ppermute | solution.py:327
  24.8 1.0 %shard_map.41 = (f32[1,640]{1,0:T(1,128)S(1)}, f32[1,320]{1,0:T(1,128)S(1)}) custom-call(bf16[336,768]{1,0:T(8,128)(2,1)S(1)} %get-tuple-element.33.block.refs_0_, bf16[336,768]{1,0:T(8,128)(2,1)S(1)} %get-tuple-element.37.partner, bf16[336,768]{1,0:T(8,128)(2,1)S(1)} %get-tuple-element.33.block.refs_0_, ...), custom_call_target="tpu_custom_call" | custom-call | flops 320 | bytes 320 | tf_op jit(solution)/shard_map/pallas_call | solution.py:224
  25.8 1.9 %collective-permute-done.8.refs_5_ = bf16[176,768]{1,0:T(8,128)(2,1)S(1)} collective-permute-done((bf16[176,768]{1,0:T(8,128)(2,1)S(1)}, bf16[176,768]{1,0:T(8,128)(2,1)S(1)}, u32[]{:S(2)}, u32[]{:S(2)}) %collective-permute-start.8) | collective-permute-done | bytes 270368 | tf_op jit(solution)/shard_map/ppermute | solution.py:327
  27.9 1.0 %shard_map.43 = (f32[1,640]{1,0:T(1,128)S(1)}, f32[1,320]{1,0:T(1,128)S(1)}) custom-call(bf16[336,768]{1,0:T(8,128)(2,1)S(1)} %get-tuple-element.33.block.refs_0_, bf16[336,768]{1,0:T(8,128)(2,1)S(1)} %get-tuple-element.37.partner, bf16[1280,768]{1,0:T(8,128)(2,1)S(1)} %get-tuple-element.44.held, f32[1,1280]{1,0:T(1,128)S(1)} %get-tuple-element.45.row), custom_call_target="tpu_custom_call" | custom-call | flops 320 | bytes 320 | tf_op jit(solution)/shard_map/pallas_call | solution.py:240
  28.9 0.5 %collective-permute-start.12 = (bf16[336,768]{1,0:T(8,128)(2,1)S(1)}, bf16[336,768]{1,0:T(8,128)(2,1)S(1)}, u32[]{:S(2)}, u32[]{:S(2)}) collective-permute-start(bf16[336,768]{1,0:T(8,128)(2,1)S(1)} %collective-permute-done.4.second), channel_id=1, source_target_pairs={{0,1},{1,0},{2,3},{3,2},{4,5},{5,4},{6,7},{7,6},{8,9},{9,8},{10,11... | collective-permute-start | bytes 1548296 | tf_op jit(solution)/shard_map/ppermute | solution.py:347
  29.4 2.0 %shard_map.44 = (f32[1,1280]{1,0:T(1,128)S(1)}, f32[1,640]{1,0:T(1,128)S(1)}) custom-call(bf16[320,768]{1,0:T(8,128)(2,1)S(1)} %get-tuple-element.32.first, bf16[336,768]{1,0:T(8,128)(2,1)S(1)} %collective-permute-done.4.second, bf16[1280,768]{1,0:T(8,128)(2,1)S(1)} %get-tuple-element.44.held, f32[1,1280]{1,0:T(1,128)S(1)} %get-tuple-element.45.row, ...), custom_call_target="tpu_custom_call" | custom-call | flops 320 | bytes 320 | tf_op jit(solution)/shard_map/pallas_call | solution.py:254
  31.5 2.0 %shard_map.45 = (f32[1,320]{1,0:T(1,128)S(1)}, f32[1,640]{1,0:T(1,128)S(1)}, f32[1,320]{1,0:T(1,128)S(1)}, f32[1,640]{1,0:T(1,128)S(1)}) custom-call(bf16[320,768]{1,0:T(8,128)(2,1)S(1)} %copy-done.1, bf16[336,768]{1,0:T(8,128)(2,1)S(1)} %collective-permute-done.12.second, bf16[1280,768]{1,0:T(8,128)(2,1)S(1)} %get-tuple-element.44.held, ...), custom_call_target="tpu_custom_call" | custom-call | flops 320 | bytes 320 | tf_op jit(solution)/shard_map/pallas_call | solution.py:254
  33.6 1.5 %collective-permute-start.16 = (f32[1,640]{1,0:T(1,128)S(1)}, f32[1,640]{1,0:T(1,128)S(1)}, u32[]{:S(2)}, u32[]{:S(2)}) collective-permute-start(f32[1,640]{1,0:T(1,128)S(1)} %get-tuple-element.55), channel_id=1, source_target_pairs={{0,8},{1,17},{2,10},{3,19},{4,12},{5,21},{6,14},{7,23},{8,0},{9,25... | collective-permute-start | bytes 7688 | tf_op jit(solution)/shard_map/ppermute | solution.py:369
  35.1 4.2 %collective-permute-start.14 = (f32[1,640]{1,0:T(1,128)S(1)}, f32[1,640]{1,0:T(1,128)S(1)}, u32[]{:S(2)}, u32[]{:S(2)}) collective-permute-start(f32[1,640]{1,0:T(1,128)S(1)} %max.24), channel_id=1, source_target_pairs={{4,0},{2,6},{0,2},{7,1},{5,7},{3,5},{12,8},{10,14},{8,10},{15,9},{... | collective-permute-start | bytes 7688 | tf_op jit(solution)/shard_map/ppermute | solution.py:364
  39.5 0.9 %collective-permute-start.18 = (f32[1,320]{1,0:T(1,128)S(1)}, f32[1,320]{1,0:T(1,128)S(1)}, u32[]{:S(2)}, u32[]{:S(2)}) collective-permute-start(f32[1,320]{1,0:T(1,128)S(1)} %get-tuple-element.60), channel_id=1, source_target_pairs={{0,1},{1,0},{2,3},{3,2},{4,5},{5,4},{6,7},{7,6},{8,9},{9,8},{10,11... | collective-permute-start | bytes 3848 | tf_op jit(solution)/shard_map/ppermute | solution.py:374
  40.4 1.1 %collective-permute-done.14 = f32[1,640]{1,0:T(1,128)S(1)} collective-permute-done((f32[1,640]{1,0:T(1,128)S(1)}, f32[1,640]{1,0:T(1,128)S(1)}, u32[]{:S(2)}, u32[]{:S(2)}) %collective-permute-start.14) | collective-permute-done | bytes 2592 | tf_op jit(solution)/shard_map/ppermute | solution.py:364
  42.8 0.6 %fusion.2 = f32[320]{0:T(512)} fusion(f32[1,320]{1,0:T(1,128)S(1)} %collective-permute-done.18, f32[1,320]{1,0:T(1,128)S(1)} %collective-permute-done.17, f32[1,320]{1,0:T(1,128)S(1)} %collective-permute-done.15, f32[1,640]{1,0:T(1,128)S(1)} %broadcast_select_fusion), kind=kLoop, calls=%fused_computation.6 | loop fusion | flops 960 | bytes 6400 | tf_op jit(solution)/shard_map/max | solution.py:375
  (38 shorter events, 3.2 us)
Async XLA Ops:
  0.0 6.5 %collective-permute-start.1 = (bf16[320,768]{1,0:T(8,128)(2,1)}, bf16[320,768]{1,0:T(8,128)(2,1)S(1)}, u32[]{:S(2)}, u32[]{:S(2)}) collective-permute-start(bf16[320,768]{1,0:T(8,128)(2,1)} %embeddings.1), channel_id=1, source_target_pairs={{0,1},{1,0},{2,3},{3,2},{4,5},{5,4},{6,7},{7,6},{8,9},{9,8},{10,11... | collective-permute-start | bytes 1474568 | tf_op jit(solution)/shard_map/ppermute | solution.py:320
  0.5 6.0 %collective-permute-start.2 = (s32[1,320]{1,0:T(1,128)}, s32[1,320]{1,0:T(1,128)S(1)}, u32[]{:S(2)}, u32[]{:S(2)}) collective-permute-start(s32[1,320]{1,0:T(1,128)} %bitcast.1), channel_id=1, source_target_pairs={{0,1},{1,0},{2,3},{3,2},{4,5},{5,4},{6,7},{7,6},{8,9},{9,8},{10,11... | collective-permute-start | bytes 3848 | tf_op jit(solution)/shard_map/ppermute | solution.py:320
  0.5 6.0 %collective-permute-start.3 = (s32[320]{0:T(512)}, s32[320]{0:T(512)S(1)}, u32[]{:S(2)}, u32[]{:S(2)}) collective-permute-start(s32[320]{0:T(512)} %order_key.1), channel_id=1, source_target_pairs={{0,1},{1,0},{2,3},{3,2},{4,5},{5,4},{6,7},{7,6},{8,9},{9,8},{10,11... | collective-permute-start | bytes 3848 | tf_op jit(solution)/shard_map/ppermute | solution.py:320
  1.0 20.6 %collective-permute-start = (bf16[320,768]{1,0:T(8,128)(2,1)}, bf16[320,768]{1,0:T(8,128)(2,1)S(1)}, u32[]{:S(2)}, u32[]{:S(2)}) collective-permute-start(bf16[320,768]{1,0:T(8,128)(2,1)} %embeddings.1), channel_id=1, source_target_pairs={{0,4},{6,2},{2,0},{1,7},{7,5},{5,3},{8,12},{14,10},{10,8},{9,15},{... | collective-permute-start | bytes 1474568 | tf_op jit(solution)/shard_map/ppermute | solution.py:319
  7.2 8.1 %collective-permute-start.5 = (bf16[160,768]{1,0:T(8,128)(2,1)S(1)}, bf16[160,768]{1,0:T(8,128)(2,1)S(1)}, u32[]{:S(2)}, u32[]{:S(2)}) collective-permute-start(bf16[160,768]{1,0:T(8,128)(2,1)S(1)} %get-tuple-element.35), channel_id=1, source_target_pairs={{0,8},{1,17},{2,10},{3,19},{4,12},{5,21},{6,14},{7,23},{8,0},{9,25... | collective-permute-start | bytes 737288 | tf_op jit(solution)/shard_map/ppermute | solution.py:322
  8.7 11.3 %collective-permute-start.7 = (bf16[176,768]{1,0:T(8,128)(2,1)S(1)}, bf16[176,768]{1,0:T(8,128)(2,1)S(1)}, u32[]{:S(2)}, u32[]{:S(2)}) collective-permute-start(bf16[176,768]{1,0:T(8,128)(2,1)S(1)} %get-tuple-element.36), channel_id=1, source_target_pairs={{0,8},{1,17},{2,10},{3,19},{4,12},{5,21},{6,14},{7,23},{8,0},{9,25... | collective-permute-start | bytes 811016 | tf_op jit(solution)/shard_map/ppermute | solution.py:322
  9.2 18.4 %collective-permute-start.9 = (bf16[336,768]{1,0:T(8,128)(2,1)S(1)}, bf16[336,768]{1,0:T(8,128)(2,1)S(1)}, u32[]{:S(2)}, u32[]{:S(2)}) collective-permute-start(bf16[336,768]{1,0:T(8,128)(2,1)S(1)} %get-tuple-element.33.block.refs_0_), channel_id=1, source_target_pairs={{0,16},{1,9},{2,18},{3,11},{4,20},{5,13},{6,22},{7,15},{8,24},{9,1... | collective-permute-start | bytes 1548296 | tf_op jit(solution)/shard_map/ppermute | solution.py:323
  10.8 1.0 %copy-start.2 = (bf16[320,768]{1,0:T(8,128)(2,1)S(1)}, bf16[320,768]{1,0:T(8,128)(2,1)}, u32[]{:S(2)}) copy-start(bf16[320,768]{1,0:T(8,128)(2,1)} %embeddings.1) | copy-start | bytes 1474564
  11.8 0.7 %copy-start.3 = (s32[320]{0:T(512)S(1)}, s32[320]{0:T(512)}, u32[]{:S(2)}) copy-start(s32[320]{0:T(512)} %order_key.1) | copy-start | bytes 3844
  12.5 0.7 %copy-start.4 = (s32[320,1]{0,1:T(1,128)S(1)}, s32[320,1]{0,1:T(1,128)}, u32[]{:S(2)}) copy-start(s32[320,1]{0,1:T(1,128)} %param.4) | copy-start | bytes 3844
  13.4 15.5 %collective-permute-start.4 = (bf16[336,768]{1,0:T(8,128)(2,1)S(1)}, bf16[336,768]{1,0:T(8,128)(2,1)S(1)}, u32[]{:S(2)}, u32[]{:S(2)}) collective-permute-start(bf16[336,768]{1,0:T(8,128)(2,1)S(1)} %shard_map.40), channel_id=1, source_target_pairs={{0,4},{6,2},{2,0},{1,7},{7,5},{5,3},{8,12},{14,10},{10,8},{9,15},{... | collective-permute-start | bytes 1548296 | tf_op jit(solution)/shard_map/ppermute | solution.py:326
  15.3 9.4 %collective-permute-start.6 = (bf16[160,768]{1,0:T(8,128)(2,1)S(1)}, bf16[160,768]{1,0:T(8,128)(2,1)S(1)}, u32[]{:S(2)}, u32[]{:S(2)}) collective-permute-start(bf16[160,768]{1,0:T(8,128)(2,1)S(1)} %collective-permute-done.5.refs_1_), channel_id=1, source_target_pairs={{0,16},{1,9},{2,18},{3,11},{4,20},{5,13},{6,22},{7,15},{8,24},{9,1... | collective-permute-start | bytes 737288 | tf_op jit(solution)/shard_map/ppermute | solution.py:327
  20.0 7.7 %collective-permute-start.8 = (bf16[176,768]{1,0:T(8,128)(2,1)S(1)}, bf16[176,768]{1,0:T(8,128)(2,1)S(1)}, u32[]{:S(2)}, u32[]{:S(2)}) collective-permute-start(bf16[176,768]{1,0:T(8,128)(2,1)S(1)} %collective-permute-done.7.refs_2_), channel_id=1, source_target_pairs={{0,16},{1,9},{2,18},{3,11},{4,20},{5,13},{6,22},{7,15},{8,24},{9,1... | collective-permute-start | bytes 811016 | tf_op jit(solution)/shard_map/ppermute | solution.py:327
  21.7 6.0 %collective-permute-start.10 = (bf16[160,768]{1,0:T(8,128)(2,1)S(1)}, bf16[160,768]{1,0:T(8,128)(2,1)S(1)}, u32[]{:S(2)}, u32[]{:S(2)}) collective-permute-start(bf16[160,768]{1,0:T(8,128)(2,1)S(1)} %get-tuple-element.42), channel_id=1, source_target_pairs={{0,1},{1,0},{2,3},{3,2},{4,5},{5,4},{6,7},{7,6},{8,9},{9,8},{10,11... | collective-permute-start | bytes 737288 | tf_op jit(solution)/shard_map/ppermute | solution.py:332
  24.8 2.9 %collective-permute-start.11 = (bf16[160,768]{1,0:T(8,128)(2,1)S(1)}, bf16[160,768]{1,0:T(8,128)(2,1)S(1)}, u32[]{:S(2)}, u32[]{:S(2)}) collective-permute-start(bf16[160,768]{1,0:T(8,128)(2,1)S(1)} %get-tuple-element.43), channel_id=1, source_target_pairs={{0,1},{1,0},{2,3},{3,2},{4,5},{5,4},{6,7},{7,6},{8,9},{9,8},{10,11... | collective-permute-start | bytes 737288 | tf_op jit(solution)/shard_map/ppermute | solution.py:332
  27.9 1.0 %copy-start = (bf16[320,768]{1,0:T(8,128)(2,1)}, bf16[320,768]{1,0:T(8,128)(2,1)S(1)}, u32[]{:S(2)}) copy-start(bf16[320,768]{1,0:T(8,128)(2,1)S(1)} %get-tuple-element.51.first) | copy-start | bytes 1474564
  28.9 2.6 %collective-permute-start.12 = (bf16[336,768]{1,0:T(8,128)(2,1)S(1)}, bf16[336,768]{1,0:T(8,128)(2,1)S(1)}, u32[]{:S(2)}, u32[]{:S(2)}) collective-permute-start(bf16[336,768]{1,0:T(8,128)(2,1)S(1)} %collective-permute-done.4.second), channel_id=1, source_target_pairs={{0,1},{1,0},{2,3},{3,2},{4,5},{5,4},{6,7},{7,6},{8,9},{9,8},{10,11... | collective-permute-start | bytes 1548296 | tf_op jit(solution)/shard_map/ppermute | solution.py:347
  29.4 2.0 %copy-start.1 = (bf16[320,768]{1,0:T(8,128)(2,1)S(1)}, bf16[320,768]{1,0:T(8,128)(2,1)}, u32[]{:S(2)}) copy-start(bf16[320,768]{1,0:T(8,128)(2,1)} %copy-done) | copy-start | bytes 1474564
  33.5 1.6 %collective-permute-start.13 = (f32[1,640]{1,0:T(1,128)S(1)}, f32[1,640]{1,0:T(1,128)S(1)}, u32[]{:S(2)}, u32[]{:S(2)}) collective-permute-start(f32[1,640]{1,0:T(1,128)S(1)} %get-tuple-element.53), channel_id=1, source_target_pairs={{0,1},{1,0},{2,3},{3,2},{4,5},{5,4},{6,7},{7,6},{8,9},{9,8},{10,11... | collective-permute-start | bytes 7688 | tf_op jit(solution)/shard_map/ppermute | solution.py:361
  33.6 5.8 %collective-permute-start.16 = (f32[1,640]{1,0:T(1,128)S(1)}, f32[1,640]{1,0:T(1,128)S(1)}, u32[]{:S(2)}, u32[]{:S(2)}) collective-permute-start(f32[1,640]{1,0:T(1,128)S(1)} %get-tuple-element.55), channel_id=1, source_target_pairs={{0,8},{1,17},{2,10},{3,19},{4,12},{5,21},{6,14},{7,23},{8,0},{9,25... | collective-permute-start | bytes 7688 | tf_op jit(solution)/shard_map/ppermute | solution.py:369
  35.1 6.4 %collective-permute-start.14 = (f32[1,640]{1,0:T(1,128)S(1)}, f32[1,640]{1,0:T(1,128)S(1)}, u32[]{:S(2)}, u32[]{:S(2)}) collective-permute-start(f32[1,640]{1,0:T(1,128)S(1)} %max.24), channel_id=1, source_target_pairs={{4,0},{2,6},{0,2},{7,1},{5,7},{3,5},{12,8},{10,14},{8,10},{15,9},{... | collective-permute-start | bytes 7688 | tf_op jit(solution)/shard_map/ppermute | solution.py:364
  39.4 3.0 %collective-permute-start.17 = (f32[1,320]{1,0:T(1,128)S(1)}, f32[1,320]{1,0:T(1,128)S(1)}, u32[]{:S(2)}, u32[]{:S(2)}) collective-permute-start(f32[1,320]{1,0:T(1,128)S(1)} %get-tuple-element.59), channel_id=1, source_target_pairs={{0,17},{1,8},{2,19},{3,10},{4,21},{5,12},{6,23},{7,14},{8,25},{9,0... | collective-permute-start | bytes 3848 | tf_op jit(solution)/shard_map/ppermute | solution.py:372
  39.5 3.0 %collective-permute-start.18 = (f32[1,320]{1,0:T(1,128)S(1)}, f32[1,320]{1,0:T(1,128)S(1)}, u32[]{:S(2)}, u32[]{:S(2)}) collective-permute-start(f32[1,320]{1,0:T(1,128)S(1)} %get-tuple-element.60), channel_id=1, source_target_pairs={{0,1},{1,0},{2,3},{3,2},{4,5},{5,4},{6,7},{7,6},{8,9},{9,8},{10,11... | collective-permute-start | bytes 3848 | tf_op jit(solution)/shard_map/ppermute | solution.py:374
  41.6 1.2 %collective-permute-start.15 = (f32[1,320]{1,0:T(1,128)S(1)}, f32[1,320]{1,0:T(1,128)S(1)}, u32[]{:S(2)}, u32[]{:S(2)}) collective-permute-start(f32[1,320]{1,0:T(1,128)S(1)} %slice.17), channel_id=1, source_target_pairs={{0,1},{1,0},{2,3},{3,2},{4,5},{5,4},{6,7},{7,6},{8,9},{9,8},{10,11... | collective-permute-start | bytes 3848 | tf_op jit(solution)/shard_map/ppermute | solution.py:368

commit v18 on v17

--- a/solution.py
+++ b/solution.py
@@ -87,26 +87,38 @@
     return jnp.max(partial.T, axis=0, keepdims=True)[:, :rows]
 
 
+def products(units, held, at, tile):
+    return lax.dot_general(
+        units,
+        held[at : at + tile, :],
+        (((1,), (1,)), ((), ())),
+        preferred_element_type=jnp.float32,
+    )
+
+
 def meet(units, parts, rows, span, held, held_codes):
-    columns = [turned_to_column(row, rows) for row, _ in parts]
+    columns = [turned_to_column(row, rows) for row, *_ in parts]
     starts = [(block, top) for block in range(len(parts)) for top in range(0, rows, CHUNK)]
     partial = {start: jnp.full((CHUNK, LANES), -1.0, jnp.float32) for start in starts}
+    places, count = [], 0
+    for part in parts:
+        places.append(part[3] if len(part) > 2 else count)
+        count += 0 if len(part) > 2 else rows
     best_held = []
     for at in range(0, held.shape[0], TILE):
         tile = min(TILE, held.shape[0] - at)
-        sims = lax.dot_general(
-            units[...],
-            held[at : at + tile, :],
-            (((1,), (1,)), ((), ())),
-            preferred_element_type=jnp.float32,
-        )
+        sims = products(units[...], held, at, tile)
         best = [jnp.full((CHUNK, LANES), -1.0, jnp.float32) for _ in range(0, tile, LANES)]
         for block, top in starts:
             to_block, to_held = parts[block][1]
             mine = columns[block][top : top + CHUNK]
-            line = block * rows + top
+            line = places[block] + top
             for lane in range(0, tile, LANES):
-                part = sims[line : line + CHUNK, lane : lane + LANES]
+                if len(parts[block]) > 2:
+                    left = at + lane
+                    part = parts[block][2][line : line + CHUNK, left : left + LANES]
+                else:
+                    part = sims[line : line + CHUNK, lane : lane + LANES]
                 gap = mine - held_codes[:, at + lane : at + lane + LANES]
                 if to_block and to_held:
                     part = jnp.where(jnp.abs(gap) < span, part, -1.0)
@@ -125,7 +137,7 @@
         row_from_partial(
             jnp.concatenate([partial[block, top] for top in range(0, rows, CHUNK)], axis=0), rows
         )
-        for block, (_, (to_block, _)) in enumerate(parts)
+        for block, (_, (to_block, _), *_) in enumerate(parts)
         if to_block
     ]
     return found, jnp.concatenate(best_held, axis=1)
@@ -205,11 +217,31 @@
     best[...] = theirs[:, row.shape[1] - count :]
 
 
-def line_kernel(rows, span, together, count, first, second, held, row, *refs):
-    bests, outs, (found, units) = refs[:count], refs[count:-2], refs[-2:]
+def products_kernel(rows, first, second, held, sims, units):
     pair(units, first, second, rows)
-    parts = [(codes(second, rows, span, first=place), TWO) for place in (CODES, 0)]
-    mine, theirs = meet(units, parts, rows, span, held, row[...])
+    for at in range(0, held.shape[0], TILE):
+        tile = min(TILE, held.shape[0] - at)
+        sims[:, at : at + tile] = products(units[...], held, at, tile)
+
+
+def all_products(first, second, held, rows):
+    total, width = held.shape
+    return pl.pallas_call(
+        functools.partial(products_kernel, rows),
+        out_shape=jax.ShapeDtypeStruct((2 * rows, total), jnp.float32),
+        scratch_shapes=[pltpu.VMEM((2 * rows, width), jnp.bfloat16)],
+        compiler_params=pltpu.CompilerParams(vmem_limit_bytes=8 << 20),
+        cost_estimate=pl.CostEstimate(flops=rows, bytes_accessed=rows, transcendentals=0),
+    )(first, second, held)
+
+
+def line_kernel(rows, span, together, count, start, sims, second, held, row, *refs):
+    bests, outs, found = refs[:count], refs[count:-1], refs[-1]
+    parts = [
+        (codes(second, rows, span, first=CODES), TWO, sims, start),
+        (codes(second, rows, span), TWO),
+    ]
+    mine, theirs = meet(second.at[0:rows, :], parts, rows, span, held, row[...])
     found[...] = jnp.concatenate(mine, axis=1)
     best = jnp.maximum(jnp.concatenate([best[...] for best in bests], axis=1), theirs)
     for out, places in zip(outs, together):
@@ -249,15 +281,14 @@
     )(block, partner, held, row)
 
 
-def line(first, second, held, row, bests, rows, span, together):
+def line(sims, start, second, held, row, bests, rows, span, together):
     outs = [jax.ShapeDtypeStruct((1, rows * len(some)), jnp.float32) for some in together]
     *bests, found = pl.pallas_call(
-        functools.partial(line_kernel, rows, span, together, len(bests)),
+        functools.partial(line_kernel, rows, span, together, len(bests), start),
         out_shape=outs + [jax.ShapeDtypeStruct((1, 2 * rows), jnp.float32)],
-        scratch_shapes=[pltpu.VMEM((2 * rows, second.shape[1]), jnp.bfloat16)],
-        compiler_params=pltpu.CompilerParams(vmem_limit_bytes=12 << 20),
+        compiler_params=pltpu.CompilerParams(vmem_limit_bytes=8 << 20),
         cost_estimate=pl.CostEstimate(flops=rows, bytes_accessed=rows, transcendentals=0),
-    )(first, second, held, row, *bests)
+    )(sims, second, held, row, *bests)
     return bests, found
 
 
@@ -343,12 +374,14 @@
         far = [far_units] + [jnp.concatenate(pieces, axis=0) for pieces in far[1:]]
         whole, last = [tuple(range(groups))], [(0,), (1, 3), (2,)]
         for at, second_near in enumerate(near_other):
-            second_near, *bests = lax.optimization_barrier((second_near, *bests))
+            sims = all_products(near[at][0], far[at], held, rows)
+            second_near, sims, *bests = lax.optimization_barrier((second_near, sims, *bests))
             second_far = lax.ppermute(second_near, BOTH, other_core)
-            bests, found = line(near[at][0], second_near, held, row, bests, rows, span, whole)
+            bests, found = line(sims, 0, second_near, held, row, bests, rows, span, whole)
             kept.append(found)
             bests, found = line(
-                far[at],
+                sims,
+                rows,
                 second_far,
                 held,
                 row,

time: 43.6 us -> 47.6 us (1.092)
  local copies, waits for them, and re-layouts: 2.47 us -> 6.05 us
  starting transfers between devices: 21.9 us -> 19.8 us
  waiting for transfers between devices: 10.8 us -> 12.7 us
  Pallas kernels: 7.34 us -> 7.86 us
    unnamed x10, local copies, waits for them, and re-layouts: 2.4 us -> 5.98 us
    ppermute x1, starting transfers between devices: 4.25 us -> 1.98 us  [shards(): lax.ppermute(kept[:, 2 * at * rows:2 * (at + 1) * rows], BOTH, back(pairs))]
    ppermute x1, waiting for transfers between devices: 1.11 us -> 2.6 us  [shards(): lax.ppermute(kept[:, 2 * at * rows:2 * (at + 1) * rows], BOTH, back(pairs))]
    pallas_call x0 -> x1, Pallas kernels: none -> 1.47 us  [all_products(): pl.pallas_call(functools.partial(products_kernel, rows), out_shape=jax.Sh...]
    pallas_call x2, Pallas kernels: 4.05 us -> 3.09 us  [line(): pl.pallas_call(functools.partial(line_kernel, rows, span, together, len(b...]
    ppermute x1, waiting for transfers between devices: 0.32 us -> 1.12 us  [shards(): lax.ppermute(found[:, rows:], BOTH, other_core)]
    ppermute x1, starting transfers between devices: 0.92 us -> 1.53 us  [shards(): results.append(lax.ppermute(home, BOTH, other_core))]
    ppermute x1, starting transfers between devices: 0.55 us -> 0.01 us  [shards(): second_far = lax.ppermute(second_near, BOTH, other_core)]
  transfers between devices with their start and end apart: 19 -> 19, of which waited for: 6 -> 6; matrix products, arithmetic and copies ran while one was open for 0% -> 0% of each run, Pallas kernels for 12% -> 13%
where the time goes in v18:
time: 47.6 us; the launch traced here: 47.3 us
  starting transfers between devices  19.8 us (42%)
  waiting for transfers between devices  12.7 us (27%)
  Pallas kernels  7.86 us (17%)
  local copies, waits for them, and re-layouts  6.05 us (13%)
  other arithmetic  0.68 us (1%)
    unnamed x10, local copies, waits for them, and re-layouts  5.98 us
    ppermute x1, starting transfers between devices, shards(): raw = [lax.ppermute(embeddings, BOTH, pairs) for pairs in rounds]  5.49 us
    ppermute x2, waiting for transfers between devices, shards(): from_corner = [lax.ppermute(part, BOTH, second) for part in from_first]  4.74 us
    ppermute x2, waiting for transfers between devices, shards(): from_first = [lax.ppermute(part, BOTH, first) for part in parts]  4.11 us
    pallas_call x2, Pallas kernels, line(): pl.pallas_call(functools.partial(line_kernel, rows, span, together, len(b...  3.09 us
    ppermute x1, waiting for transfers between devices, shards(): lax.ppermute(kept[:, 2 * at * rows:2 * (at + 1) * rows], BOTH, back(pairs))  2.6 us
    ppermute x2, starting transfers between devices, shards(): from_corner = [lax.ppermute(part, BOTH, second) for part in from_first]  2.09 us
    ppermute x2, starting transfers between devices, shards(): from_first = [lax.ppermute(part, BOTH, first) for part in parts]  2.03 us
  transfers between devices with their start and end apart: 19, of which 6 were waited for; matrix products, arithmetic and copies ran while one was open for 0% of the time, Pallas kernels for 13%

profile of v18, /device:TPU:0, one launch (start us, length us, event | category | flops | bytes accessed | tf_op | source)
XLA Modules:
  0.0 47.3 jit_solution(3865698052694375171)
XLA Ops:
  1.0 5.5 %collective-permute-start.4 = (bf16[320,768]{1,0:T(8,128)(2,1)}, bf16[320,768]{1,0:T(8,128)(2,1)S(1)}, u32[]{:S(2)}, u32[]{:S(2)}) collective-permute-start(bf16[320,768]{1,0:T(8,128)(2,1)} %embeddings.1), channel_id=1, source_target_pairs={{0,4},{6,2},{2,0},{1,7},{7,5},{5,3},{8,12},{14,10},{10,8},{9,15},{... | collective-permute-start | bytes 1474568 | tf_op jit(solution)/shard_map/ppermute | solution.py:350
  6.5 0.7 %shard_map.37 = (bf16[336,768]{1,0:T(8,128)(2,1)S(1)}, bf16[16,768]{1,0:T(8,128)(2,1)}, bf16[160,768]{1,0:T(8,128)(2,1)S(1)}, bf16[176,768]{1,0:T(8,128)(2,1)S(1)}) custom-call(bf16[320,768]{1,0:T(8,128)(2,1)S(1)} %collective-permute-done.embeddings, s32[1,320]{1,0:T(1,128)S(1)} %collective-permute-done.1.cluster, s32[320]{0:T(512)S(1)} %collective-permute-done.2.order_key), custom_call_target="tpu_custom_call" | custom-call | flops 320 | bytes 320 | tf_op jit(solution)/shard_map/pallas_call | solution.py:73
  7.2 1.5 %collective-permute-start.5 = (bf16[160,768]{1,0:T(8,128)(2,1)S(1)}, bf16[160,768]{1,0:T(8,128)(2,1)S(1)}, u32[]{:S(2)}, u32[]{:S(2)}) collective-permute-start(bf16[160,768]{1,0:T(8,128)(2,1)S(1)} %get-tuple-element.36), channel_id=1, source_target_pairs={{0,8},{1,17},{2,10},{3,19},{4,12},{5,21},{6,14},{7,23},{8,0},{9,25... | collective-permute-start | bytes 737288 | tf_op jit(solution)/shard_map/ppermute | solution.py:353
  9.2 1.5 %collective-permute-start.7 = (bf16[336,768]{1,0:T(8,128)(2,1)S(1)}, bf16[336,768]{1,0:T(8,128)(2,1)S(1)}, u32[]{:S(2)}, u32[]{:S(2)}) collective-permute-start(bf16[336,768]{1,0:T(8,128)(2,1)S(1)} %get-tuple-element.33.block.refs_0_), channel_id=1, source_target_pairs={{0,16},{1,9},{2,18},{3,11},{4,20},{5,13},{6,22},{7,15},{8,24},{9,1... | collective-permute-start | bytes 1548296 | tf_op jit(solution)/shard_map/ppermute | solution.py:354
  10.8 1.0 %copy-done.2 = bf16[320,768]{1,0:T(8,128)(2,1)S(1)} copy-done((bf16[320,768]{1,0:T(8,128)(2,1)S(1)}, bf16[320,768]{1,0:T(8,128)(2,1)}, u32[]{:S(2)}) %copy-start.2) | copy-done | bytes 491544
  11.8 0.7 %copy-done.3 = s32[320]{0:T(512)S(1)} copy-done((s32[320]{0:T(512)S(1)}, s32[320]{0:T(512)}, u32[]{:S(2)}) %copy-start.3) | copy-done | bytes 1304
  12.5 0.7 %copy-done.4 = s32[320,1]{0,1:T(1,128)S(1)} copy-done((s32[320,1]{0,1:T(1,128)S(1)}, s32[320,1]{0,1:T(1,128)}, u32[]{:S(2)}) %copy-start.4) | copy-done | bytes 1304
  13.4 1.9 %collective-permute-start.3 = (bf16[336,768]{1,0:T(8,128)(2,1)S(1)}, bf16[336,768]{1,0:T(8,128)(2,1)S(1)}, u32[]{:S(2)}, u32[]{:S(2)}) collective-permute-start(bf16[336,768]{1,0:T(8,128)(2,1)S(1)} %shard_map.39), channel_id=1, source_target_pairs={{0,4},{6,2},{2,0},{1,7},{7,5},{5,3},{8,12},{14,10},{10,8},{9,15},{... | collective-permute-start | bytes 1548296 | tf_op jit(solution)/shard_map/ppermute | solution.py:357
  15.9 4.1 %collective-permute-done.6.refs_2_ = bf16[176,768]{1,0:T(8,128)(2,1)S(1)} collective-permute-done((bf16[176,768]{1,0:T(8,128)(2,1)S(1)}, bf16[176,768]{1,0:T(8,128)(2,1)S(1)}, u32[]{:S(2)}, u32[]{:S(2)}) %collective-permute-start.6) | collective-permute-done | bytes 270368 | tf_op jit(solution)/shard_map/ppermute | solution.py:353
  20.0 1.5 %collective-permute-start.9 = (bf16[176,768]{1,0:T(8,128)(2,1)S(1)}, bf16[176,768]{1,0:T(8,128)(2,1)S(1)}, u32[]{:S(2)}, u32[]{:S(2)}) collective-permute-start(bf16[176,768]{1,0:T(8,128)(2,1)S(1)} %collective-permute-done.6.refs_2_), channel_id=1, source_target_pairs={{0,16},{1,9},{2,18},{3,11},{4,20},{5,13},{6,22},{7,15},{8,24},{9,1... | collective-permute-start | bytes 811016 | tf_op jit(solution)/shard_map/ppermute | solution.py:358
  21.9 2.9 %collective-permute-done.8.refs_4_ = bf16[160,768]{1,0:T(8,128)(2,1)S(1)} collective-permute-done((bf16[160,768]{1,0:T(8,128)(2,1)S(1)}, bf16[160,768]{1,0:T(8,128)(2,1)S(1)}, u32[]{:S(2)}, u32[]{:S(2)}) %collective-permute-start.8) | collective-permute-done | bytes 245792 | tf_op jit(solution)/shard_map/ppermute | solution.py:358
  24.8 1.0 %shard_map.41 = (f32[1,640]{1,0:T(1,128)S(1)}, f32[1,320]{1,0:T(1,128)S(1)}) custom-call(bf16[336,768]{1,0:T(8,128)(2,1)S(1)} %get-tuple-element.33.block.refs_0_, bf16[336,768]{1,0:T(8,128)(2,1)S(1)} %get-tuple-element.38.partner, bf16[336,768]{1,0:T(8,128)(2,1)S(1)} %get-tuple-element.33.block.refs_0_, ...), custom_call_target="tpu_custom_call" | custom-call | flops 320 | bytes 320 | tf_op jit(solution)/shard_map/pallas_call | solution.py:256
  25.8 1.9 %collective-permute-done.9.refs_5_ = bf16[176,768]{1,0:T(8,128)(2,1)S(1)} collective-permute-done((bf16[176,768]{1,0:T(8,128)(2,1)S(1)}, bf16[176,768]{1,0:T(8,128)(2,1)S(1)}, u32[]{:S(2)}, u32[]{:S(2)}) %collective-permute-start.9) | collective-permute-done | bytes 270368 | tf_op jit(solution)/shard_map/ppermute | solution.py:358
  27.9 1.0 %shard_map.44 = (f32[1,640]{1,0:T(1,128)S(1)}, f32[1,320]{1,0:T(1,128)S(1)}) custom-call(bf16[336,768]{1,0:T(8,128)(2,1)S(1)} %get-tuple-element.33.block.refs_0_, bf16[336,768]{1,0:T(8,128)(2,1)S(1)} %get-tuple-element.38.partner, bf16[1280,768]{1,0:T(8,128)(2,1)S(1)} %get-tuple-element.45.held, f32[1,1280]{1,0:T(1,128)S(1)} %get-tuple-element.47.row), custom_call_target="tpu_custom_call" | custom-call | flops 320 | bytes 320 | tf_op jit(solution)/shard_map/pallas_call | solution.py:272
  28.9 1.5 %shard_map.43.sims = f32[640,1280]{1,0:T(8,128)S(1)} custom-call(bf16[320,768]{1,0:T(8,128)(2,1)S(1)} %get-tuple-element.35.first, bf16[320,768]{1,0:T(8,128)(2,1)S(1)} %get-tuple-element.44.second, bf16[1280,768]{1,0:T(8,128)(2,1)S(1)} %get-tuple-element.45.held), custom_call_target="tpu_custom_call" | custom-call | flops 320 | bytes 320 | tf_op jit(solution)/shard_map/pallas_call | solution.py:229
  30.4 1.7 %copy-done = f32[640,1280]{1,0:T(8,128)} copy-done((f32[640,1280]{1,0:T(8,128)}, f32[640,1280]{1,0:T(8,128)S(1)}, u32[]{:S(2)}) %copy-start) | copy-done | bytes 3276824
  32.0 1.9 %copy-done.1 = f32[640,1280]{1,0:T(8,128)S(1)} copy-done((f32[640,1280]{1,0:T(8,128)S(1)}, f32[640,1280]{1,0:T(8,128)}, u32[]{:S(2)}) %copy-start.1) | copy-done | bytes 3276824
  33.9 1.5 %shard_map.45 = (f32[1,1280]{1,0:T(1,128)S(1)}, f32[1,640]{1,0:T(1,128)S(1)}) custom-call(f32[640,1280]{1,0:T(8,128)S(1)} %copy-done.1, bf16[336,768]{1,0:T(8,128)(2,1)S(1)} %collective-permute-done.3.second, bf16[1280,768]{1,0:T(8,128)(2,1)S(1)} %get-tuple-element.45.held, f32[1,1280]{1,0:T(1,128)S(1)} %get-tuple-element.47.row, ...), custom_call_target="tpu_custom_call" | custom-call | flops 320 | bytes 320 | tf_op jit(solution)/shard_map/pallas_call | solution.py:286
  35.5 1.6 %shard_map.46 = (f32[1,320]{1,0:T(1,128)S(1)}, f32[1,640]{1,0:T(1,128)S(1)}, f32[1,320]{1,0:T(1,128)S(1)}, f32[1,640]{1,0:T(1,128)S(1)}) custom-call(f32[640,1280]{1,0:T(8,128)S(1)} %copy-done.1, bf16[336,768]{1,0:T(8,128)(2,1)S(1)} %collective-permute-done.12.second, bf16[1280,768]{1,0:T(8,128)(2,1)S(1)} %get-tuple-element.45.held, ...), custom_call_target="tpu_custom_call" | custom-call | flops 320 | bytes 320 | tf_op jit(solution)/shard_map/pallas_call | solution.py:286
  37.6 1.5 %collective-permute-start.16 = (f32[1,640]{1,0:T(1,128)S(1)}, f32[1,640]{1,0:T(1,128)S(1)}, u32[]{:S(2)}, u32[]{:S(2)}) collective-permute-start(f32[1,640]{1,0:T(1,128)S(1)} %get-tuple-element.57), channel_id=1, source_target_pairs={{0,8},{1,17},{2,10},{3,19},{4,12},{5,21},{6,14},{7,23},{8,0},{9,25... | collective-permute-start | bytes 7688 | tf_op jit(solution)/shard_map/ppermute | solution.py:402
  39.1 2.0 %collective-permute-start.14 = (f32[1,640]{1,0:T(1,128)S(1)}, f32[1,640]{1,0:T(1,128)S(1)}, u32[]{:S(2)}, u32[]{:S(2)}) collective-permute-start(f32[1,640]{1,0:T(1,128)S(1)} %max.24), channel_id=1, source_target_pairs={{4,0},{2,6},{0,2},{7,1},{5,7},{3,5},{12,8},{10,14},{8,10},{15,9},{... | collective-permute-start | bytes 7688 | tf_op jit(solution)/shard_map/ppermute | solution.py:397
  41.3 1.5 %collective-permute-start.18 = (f32[1,320]{1,0:T(1,128)S(1)}, f32[1,320]{1,0:T(1,128)S(1)}, u32[]{:S(2)}, u32[]{:S(2)}) collective-permute-start(f32[1,320]{1,0:T(1,128)S(1)} %get-tuple-element.62), channel_id=1, source_target_pairs={{0,1},{1,0},{2,3},{3,2},{4,5},{5,4},{6,7},{7,6},{8,9},{9,8},{10,11... | collective-permute-start | bytes 3848 | tf_op jit(solution)/shard_map/ppermute | solution.py:407
  42.9 2.6 %collective-permute-done.14 = f32[1,640]{1,0:T(1,128)S(1)} collective-permute-done((f32[1,640]{1,0:T(1,128)S(1)}, f32[1,640]{1,0:T(1,128)S(1)}, u32[]{:S(2)}, u32[]{:S(2)}) %collective-permute-start.14) | collective-permute-done | bytes 2592 | tf_op jit(solution)/shard_map/ppermute | solution.py:397
  45.6 1.1 %collective-permute-done.15 = f32[1,320]{1,0:T(1,128)S(1)} collective-permute-done((f32[1,320]{1,0:T(1,128)S(1)}, f32[1,320]{1,0:T(1,128)S(1)}, u32[]{:S(2)}, u32[]{:S(2)}) %collective-permute-start.15) | collective-permute-done | bytes 1312 | tf_op jit(solution)/shard_map/ppermute | solution.py:401
  (39 shorter events, 4.4 us)
Async XLA Ops:
  0.0 6.5 %collective-permute-start = (bf16[320,768]{1,0:T(8,128)(2,1)}, bf16[320,768]{1,0:T(8,128)(2,1)S(1)}, u32[]{:S(2)}, u32[]{:S(2)}) collective-permute-start(bf16[320,768]{1,0:T(8,128)(2,1)} %embeddings.1), channel_id=1, source_target_pairs={{0,1},{1,0},{2,3},{3,2},{4,5},{5,4},{6,7},{7,6},{8,9},{9,8},{10,11... | collective-permute-start | bytes 1474568 | tf_op jit(solution)/shard_map/ppermute | solution.py:351
  0.5 6.0 %collective-permute-start.1 = (s32[1,320]{1,0:T(1,128)}, s32[1,320]{1,0:T(1,128)S(1)}, u32[]{:S(2)}, u32[]{:S(2)}) collective-permute-start(s32[1,320]{1,0:T(1,128)} %bitcast.1), channel_id=1, source_target_pairs={{0,1},{1,0},{2,3},{3,2},{4,5},{5,4},{6,7},{7,6},{8,9},{9,8},{10,11... | collective-permute-start | bytes 3848 | tf_op jit(solution)/shard_map/ppermute | solution.py:351
  0.5 6.0 %collective-permute-start.2 = (s32[320]{0:T(512)}, s32[320]{0:T(512)S(1)}, u32[]{:S(2)}, u32[]{:S(2)}) collective-permute-start(s32[320]{0:T(512)} %order_key.1), channel_id=1, source_target_pairs={{0,1},{1,0},{2,3},{3,2},{4,5},{5,4},{6,7},{7,6},{8,9},{9,8},{10,11... | collective-permute-start | bytes 3848 | tf_op jit(solution)/shard_map/ppermute | solution.py:351
  1.0 20.6 %collective-permute-start.4 = (bf16[320,768]{1,0:T(8,128)(2,1)}, bf16[320,768]{1,0:T(8,128)(2,1)S(1)}, u32[]{:S(2)}, u32[]{:S(2)}) collective-permute-start(bf16[320,768]{1,0:T(8,128)(2,1)} %embeddings.1), channel_id=1, source_target_pairs={{0,4},{6,2},{2,0},{1,7},{7,5},{5,3},{8,12},{14,10},{10,8},{9,15},{... | collective-permute-start | bytes 1474568 | tf_op jit(solution)/shard_map/ppermute | solution.py:350
  7.2 8.1 %collective-permute-start.5 = (bf16[160,768]{1,0:T(8,128)(2,1)S(1)}, bf16[160,768]{1,0:T(8,128)(2,1)S(1)}, u32[]{:S(2)}, u32[]{:S(2)}) collective-permute-start(bf16[160,768]{1,0:T(8,128)(2,1)S(1)} %get-tuple-element.36), channel_id=1, source_target_pairs={{0,8},{1,17},{2,10},{3,19},{4,12},{5,21},{6,14},{7,23},{8,0},{9,25... | collective-permute-start | bytes 737288 | tf_op jit(solution)/shard_map/ppermute | solution.py:353
  8.7 11.3 %collective-permute-start.6 = (bf16[176,768]{1,0:T(8,128)(2,1)S(1)}, bf16[176,768]{1,0:T(8,128)(2,1)S(1)}, u32[]{:S(2)}, u32[]{:S(2)}) collective-permute-start(bf16[176,768]{1,0:T(8,128)(2,1)S(1)} %get-tuple-element.37), channel_id=1, source_target_pairs={{0,8},{1,17},{2,10},{3,19},{4,12},{5,21},{6,14},{7,23},{8,0},{9,25... | collective-permute-start | bytes 811016 | tf_op jit(solution)/shard_map/ppermute | solution.py:353
  9.2 18.4 %collective-permute-start.7 = (bf16[336,768]{1,0:T(8,128)(2,1)S(1)}, bf16[336,768]{1,0:T(8,128)(2,1)S(1)}, u32[]{:S(2)}, u32[]{:S(2)}) collective-permute-start(bf16[336,768]{1,0:T(8,128)(2,1)S(1)} %get-tuple-element.33.block.refs_0_), channel_id=1, source_target_pairs={{0,16},{1,9},{2,18},{3,11},{4,20},{5,13},{6,22},{7,15},{8,24},{9,1... | collective-permute-start | bytes 1548296 | tf_op jit(solution)/shard_map/ppermute | solution.py:354
  10.8 1.0 %copy-start.2 = (bf16[320,768]{1,0:T(8,128)(2,1)S(1)}, bf16[320,768]{1,0:T(8,128)(2,1)}, u32[]{:S(2)}) copy-start(bf16[320,768]{1,0:T(8,128)(2,1)} %embeddings.1) | copy-start | bytes 1474564
  11.8 0.7 %copy-start.3 = (s32[320]{0:T(512)S(1)}, s32[320]{0:T(512)}, u32[]{:S(2)}) copy-start(s32[320]{0:T(512)} %order_key.1) | copy-start | bytes 3844
  12.5 0.7 %copy-start.4 = (s32[320,1]{0,1:T(1,128)S(1)}, s32[320,1]{0,1:T(1,128)}, u32[]{:S(2)}) copy-start(s32[320,1]{0,1:T(1,128)} %param.4) | copy-start | bytes 3844
  13.4 18.6 %collective-permute-start.3 = (bf16[336,768]{1,0:T(8,128)(2,1)S(1)}, bf16[336,768]{1,0:T(8,128)(2,1)S(1)}, u32[]{:S(2)}, u32[]{:S(2)}) collective-permute-start(bf16[336,768]{1,0:T(8,128)(2,1)S(1)} %shard_map.39), channel_id=1, source_target_pairs={{0,4},{6,2},{2,0},{1,7},{7,5},{5,3},{8,12},{14,10},{10,8},{9,15},{... | collective-permute-start | bytes 1548296 | tf_op jit(solution)/shard_map/ppermute | solution.py:357
  15.3 9.4 %collective-permute-start.8 = (bf16[160,768]{1,0:T(8,128)(2,1)S(1)}, bf16[160,768]{1,0:T(8,128)(2,1)S(1)}, u32[]{:S(2)}, u32[]{:S(2)}) collective-permute-start(bf16[160,768]{1,0:T(8,128)(2,1)S(1)} %collective-permute-done.5.refs_1_), channel_id=1, source_target_pairs={{0,16},{1,9},{2,18},{3,11},{4,20},{5,13},{6,22},{7,15},{8,24},{9,1... | collective-permute-start | bytes 737288 | tf_op jit(solution)/shard_map/ppermute | solution.py:358
  20.0 7.7 %collective-permute-start.9 = (bf16[176,768]{1,0:T(8,128)(2,1)S(1)}, bf16[176,768]{1,0:T(8,128)(2,1)S(1)}, u32[]{:S(2)}, u32[]{:S(2)}) collective-permute-start(bf16[176,768]{1,0:T(8,128)(2,1)S(1)} %collective-permute-done.6.refs_2_), channel_id=1, source_target_pairs={{0,16},{1,9},{2,18},{3,11},{4,20},{5,13},{6,22},{7,15},{8,24},{9,1... | collective-permute-start | bytes 811016 | tf_op jit(solution)/shard_map/ppermute | solution.py:358
  21.7 6.0 %collective-permute-start.10 = (bf16[160,768]{1,0:T(8,128)(2,1)S(1)}, bf16[160,768]{1,0:T(8,128)(2,1)S(1)}, u32[]{:S(2)}, u32[]{:S(2)}) collective-permute-start(bf16[160,768]{1,0:T(8,128)(2,1)S(1)} %get-tuple-element.42), channel_id=1, source_target_pairs={{0,1},{1,0},{2,3},{3,2},{4,5},{5,4},{6,7},{7,6},{8,9},{9,8},{10,11... | collective-permute-start | bytes 737288 | tf_op jit(solution)/shard_map/ppermute | solution.py:363
  24.8 2.9 %collective-permute-start.11 = (bf16[160,768]{1,0:T(8,128)(2,1)S(1)}, bf16[160,768]{1,0:T(8,128)(2,1)S(1)}, u32[]{:S(2)}, u32[]{:S(2)}) collective-permute-start(bf16[160,768]{1,0:T(8,128)(2,1)S(1)} %get-tuple-element.43), channel_id=1, source_target_pairs={{0,1},{1,0},{2,3},{3,2},{4,5},{5,4},{6,7},{7,6},{8,9},{9,8},{10,11... | collective-permute-start | bytes 737288 | tf_op jit(solution)/shard_map/ppermute | solution.py:363
  30.3 1.7 %copy-start = (f32[640,1280]{1,0:T(8,128)}, f32[640,1280]{1,0:T(8,128)S(1)}, u32[]{:S(2)}) copy-start(f32[640,1280]{1,0:T(8,128)S(1)} %shard_map.43.sims) | copy-start | bytes 9830404
  32.0 3.5 %collective-permute-start.12 = (bf16[336,768]{1,0:T(8,128)(2,1)S(1)}, bf16[336,768]{1,0:T(8,128)(2,1)S(1)}, u32[]{:S(2)}, u32[]{:S(2)}) collective-permute-start(bf16[336,768]{1,0:T(8,128)(2,1)S(1)} %collective-permute-done.3.second), channel_id=1, source_target_pairs={{0,1},{1,0},{2,3},{3,2},{4,5},{5,4},{6,7},{7,6},{8,9},{9,8},{10,11... | collective-permute-start | bytes 1548296 | tf_op jit(solution)/shard_map/ppermute | solution.py:379
  32.0 1.9 %copy-start.1 = (f32[640,1280]{1,0:T(8,128)S(1)}, f32[640,1280]{1,0:T(8,128)}, u32[]{:S(2)}) copy-start(f32[640,1280]{1,0:T(8,128)} %copy-done) | copy-start | bytes 9830404
  37.0 2.0 %collective-permute-start.13 = (f32[1,640]{1,0:T(1,128)S(1)}, f32[1,640]{1,0:T(1,128)S(1)}, u32[]{:S(2)}, u32[]{:S(2)}) collective-permute-start(f32[1,640]{1,0:T(1,128)S(1)} %get-tuple-element.55), channel_id=1, source_target_pairs={{0,1},{1,0},{2,3},{3,2},{4,5},{5,4},{6,7},{7,6},{8,9},{9,8},{10,11... | collective-permute-start | bytes 7688 | tf_op jit(solution)/shard_map/ppermute | solution.py:394
  37.6 3.6 %collective-permute-start.16 = (f32[1,640]{1,0:T(1,128)S(1)}, f32[1,640]{1,0:T(1,128)S(1)}, u32[]{:S(2)}, u32[]{:S(2)}) collective-permute-start(f32[1,640]{1,0:T(1,128)S(1)} %get-tuple-element.57), channel_id=1, source_target_pairs={{0,8},{1,17},{2,10},{3,19},{4,12},{5,21},{6,14},{7,23},{8,0},{9,25... | collective-permute-start | bytes 7688 | tf_op jit(solution)/shard_map/ppermute | solution.py:402
  39.1 6.4 %collective-permute-start.14 = (f32[1,640]{1,0:T(1,128)S(1)}, f32[1,640]{1,0:T(1,128)S(1)}, u32[]{:S(2)}, u32[]{:S(2)}) collective-permute-start(f32[1,640]{1,0:T(1,128)S(1)} %max.24), channel_id=1, source_target_pairs={{4,0},{2,6},{0,2},{7,1},{5,7},{3,5},{12,8},{10,14},{8,10},{15,9},{... | collective-permute-start | bytes 7688 | tf_op jit(solution)/shard_map/ppermute | solution.py:397
  41.3 4.3 %collective-permute-start.17 = (f32[1,320]{1,0:T(1,128)S(1)}, f32[1,320]{1,0:T(1,128)S(1)}, u32[]{:S(2)}, u32[]{:S(2)}) collective-permute-start(f32[1,320]{1,0:T(1,128)S(1)} %get-tuple-element.61), channel_id=1, source_target_pairs={{0,17},{1,8},{2,19},{3,10},{4,21},{5,12},{6,23},{7,14},{8,25},{9,0... | collective-permute-start | bytes 3848 | tf_op jit(solution)/shard_map/ppermute | solution.py:405
  41.3 4.2 %collective-permute-start.18 = (f32[1,320]{1,0:T(1,128)S(1)}, f32[1,320]{1,0:T(1,128)S(1)}, u32[]{:S(2)}, u32[]{:S(2)}) collective-permute-start(f32[1,320]{1,0:T(1,128)S(1)} %get-tuple-element.62), channel_id=1, source_target_pairs={{0,1},{1,0},{2,3},{3,2},{4,5},{5,4},{6,7},{7,6},{8,9},{9,8},{10,11... | collective-permute-start | bytes 3848 | tf_op jit(solution)/shard_map/ppermute | solution.py:407
  45.5 1.2 %collective-permute-start.15 = (f32[1,320]{1,0:T(1,128)S(1)}, f32[1,320]{1,0:T(1,128)S(1)}, u32[]{:S(2)}, u32[]{:S(2)}) collective-permute-start(f32[1,320]{1,0:T(1,128)S(1)} %slice.17), channel_id=1, source_target_pairs={{0,1},{1,0},{2,3},{3,2},{4,5},{5,4},{6,7},{7,6},{8,9},{9,8},{10,11... | collective-permute-start | bytes 3848 | tf_op jit(solution)/shard_map/ppermute | solution.py:401

commit v19 on v17

--- a/solution.py
+++ b/solution.py
@@ -268,7 +268,7 @@
 
 def line_rounds(chips):
     if chips == 4:
-        return [[(0, 2), (3, 1), (1, 0)], [(0, 3), (3, 2), (2, 1)]]
+        return [[(3, 1), (0, 2), (2, 3)], [(3, 0), (0, 1), (1, 2)]]
     rounds = []
     for shift in range(1, chips // 2 + 1):
         senders = chips // 2 if 2 * shift == chips else chips

time: 43.6 us -> 44.2 us (1.014)
  waiting for transfers between devices: 10.8 us -> 12 us
  starting transfers between devices: 21.9 us -> 21.2 us
    ppermute x1, starting transfers between devices: 4.25 us -> 1.29 us  [shards(): lax.ppermute(kept[:, 2 * at * rows:2 * (at + 1) * rows], BOTH, back(pairs))]
    ppermute x2, waiting for transfers between devices: 4.74 us -> 3.17 us  [shards(): from_corner = [lax.ppermute(part, BOTH, second) for part in from_first]]
    ppermute x1, starting transfers between devices: 1.92 us -> 3.49 us  [shards(): near_other = [lax.ppermute(both, BOTH, pairs) for pairs in rounds]]
    ppermute x1, waiting for transfers between devices: 1.11 us -> 2.6 us  [shards(): lax.ppermute(kept[:, 2 * at * rows:2 * (at + 1) * rows], BOTH, back(pairs))]
    ppermute x1, starting transfers between devices: 0.01 us -> 1.08 us  [shards(): results.append(lax.ppermute(onward, BOTH, second_home))]
    ppermute x1, waiting for transfers between devices: 0.32 us -> 1.12 us  [shards(): lax.ppermute(found[:, rows:], BOTH, other_core)]
    ppermute x1, waiting for transfers between devices: 0.01 us -> 0.78 us  [shards(): from_x = lax.ppermute(bests[1], BOTH, first)]
    ppermute x1, waiting for transfers between devices: 0.5 us -> 0.01 us  [shards(): results.append(lax.ppermute(onward, BOTH, second_home))]
  transfers between devices with their start and end apart: 19 -> 19, of which waited for: 6 -> 5; matrix products, arithmetic and copies ran while one was open for 0% -> 0% of each run, Pallas kernels for 12% -> 12%
where the time goes in v19:
time: 44.2 us; the launch traced here: 43.9 us
  starting transfers between devices  21.2 us (48%)
  waiting for transfers between devices  12 us (27%)
  Pallas kernels  7.35 us (17%)
  local copies, waits for them, and re-layouts  2.47 us (6%)
  other arithmetic  0.68 us (2%)
    ppermute x1, starting transfers between devices, shards(): raw = [lax.ppermute(embeddings, BOTH, pairs) for pairs in rounds]  5.51 us
    ppermute x2, waiting for transfers between devices, shards(): from_first = [lax.ppermute(part, BOTH, first) for part in parts]  4.28 us
    pallas_call x2, Pallas kernels, line(): pl.pallas_call(functools.partial(line_kernel, rows, span, together, len(b...  4.06 us
    ppermute x1, starting transfers between devices, shards(): near_other = [lax.ppermute(both, BOTH, pairs) for pairs in rounds]  3.49 us
    ppermute x2, waiting for transfers between devices, shards(): from_corner = [lax.ppermute(part, BOTH, second) for part in from_first]  3.17 us
    ppermute x1, waiting for transfers between devices, shards(): lax.ppermute(kept[:, 2 * at * rows:2 * (at + 1) * rows], BOTH, back(pairs))  2.6 us
    unnamed x10, local copies, waits for them, and re-layouts  2.4 us
    ppermute x2, starting transfers between devices, shards(): from_corner = [lax.ppermute(part, BOTH, second) for part in from_first]  2.19 us
  transfers between devices with their start and end apart: 19, of which 5 were waited for; matrix products, arithmetic and copies ran while one was open for 0% of the time, Pallas kernels for 12%

profile of v19, /device:TPU:0, one launch (start us, length us, event | category | flops | bytes accessed | tf_op | source)
XLA Modules:
  0.0 43.9 jit_solution(11614302794604658206)
XLA Ops:
  1.0 5.5 %collective-permute-start = (bf16[320,768]{1,0:T(8,128)(2,1)}, bf16[320,768]{1,0:T(8,128)(2,1)S(1)}, u32[]{:S(2)}, u32[]{:S(2)}) collective-permute-start(bf16[320,768]{1,0:T(8,128)(2,1)} %embeddings.1), channel_id=1, source_target_pairs={{6,2},{0,4},{4,6},{7,1},{1,3},{3,5},{14,10},{8,12},{12,14},{15,9},... | collective-permute-start | bytes 1474568 | tf_op jit(solution)/shard_map/ppermute | solution.py:319
  6.5 0.7 %shard_map.38 = (bf16[336,768]{1,0:T(8,128)(2,1)S(1)}, bf16[16,768]{1,0:T(8,128)(2,1)}, bf16[160,768]{1,0:T(8,128)(2,1)S(1)}, bf16[176,768]{1,0:T(8,128)(2,1)S(1)}) custom-call(bf16[320,768]{1,0:T(8,128)(2,1)S(1)} %collective-permute-done.1.embeddings, s32[1,320]{1,0:T(1,128)S(1)} %collective-permute-done.2.cluster, s32[320]{0:T(512)S(1)} %collective-permute-done.3.order_key), custom_call_target="tpu_custom_call" | custom-call | flops 320 | bytes 320 | tf_op jit(solution)/shard_map/pallas_call | solution.py:73
  7.2 1.5 %collective-permute-start.5 = (bf16[160,768]{1,0:T(8,128)(2,1)S(1)}, bf16[160,768]{1,0:T(8,128)(2,1)S(1)}, u32[]{:S(2)}, u32[]{:S(2)}) collective-permute-start(bf16[160,768]{1,0:T(8,128)(2,1)S(1)} %get-tuple-element.35), channel_id=1, source_target_pairs={{0,8},{1,17},{2,10},{3,19},{4,12},{5,21},{6,14},{7,23},{8,0},{9,25... | collective-permute-start | bytes 737288 | tf_op jit(solution)/shard_map/ppermute | solution.py:322
  9.3 1.5 %collective-permute-start.9 = (bf16[336,768]{1,0:T(8,128)(2,1)S(1)}, bf16[336,768]{1,0:T(8,128)(2,1)S(1)}, u32[]{:S(2)}, u32[]{:S(2)}) collective-permute-start(bf16[336,768]{1,0:T(8,128)(2,1)S(1)} %get-tuple-element.33.block.refs_0_), channel_id=1, source_target_pairs={{0,16},{1,9},{2,18},{3,11},{4,20},{5,13},{6,22},{7,15},{8,24},{9,1... | collective-permute-start | bytes 1548296 | tf_op jit(solution)/shard_map/ppermute | solution.py:323
  10.8 1.0 %copy-done.2 = bf16[320,768]{1,0:T(8,128)(2,1)S(1)} copy-done((bf16[320,768]{1,0:T(8,128)(2,1)S(1)}, bf16[320,768]{1,0:T(8,128)(2,1)}, u32[]{:S(2)}) %copy-start.2) | copy-done | bytes 491544
  11.8 0.7 %copy-done.3 = s32[320]{0:T(512)S(1)} copy-done((s32[320]{0:T(512)S(1)}, s32[320]{0:T(512)}, u32[]{:S(2)}) %copy-start.3) | copy-done | bytes 1304
  12.5 0.7 %copy-done.4 = s32[320,1]{0,1:T(1,128)S(1)} copy-done((s32[320,1]{0,1:T(1,128)S(1)}, s32[320,1]{0,1:T(1,128)}, u32[]{:S(2)}) %copy-start.4) | copy-done | bytes 1304
  13.4 3.5 %collective-permute-start.4 = (bf16[336,768]{1,0:T(8,128)(2,1)S(1)}, bf16[336,768]{1,0:T(8,128)(2,1)S(1)}, u32[]{:S(2)}, u32[]{:S(2)}) collective-permute-start(bf16[336,768]{1,0:T(8,128)(2,1)S(1)} %shard_map.40), channel_id=1, source_target_pairs={{6,2},{0,4},{4,6},{7,1},{1,3},{3,5},{14,10},{8,12},{12,14},{15,9},... | collective-permute-start | bytes 1548296 | tf_op jit(solution)/shard_map/ppermute | solution.py:326
  16.9 0.7 %collective-permute-start.6 = (bf16[160,768]{1,0:T(8,128)(2,1)S(1)}, bf16[160,768]{1,0:T(8,128)(2,1)S(1)}, u32[]{:S(2)}, u32[]{:S(2)}) collective-permute-start(bf16[160,768]{1,0:T(8,128)(2,1)S(1)} %collective-permute-done.5.refs_1_), channel_id=1, source_target_pairs={{0,16},{1,9},{2,18},{3,11},{4,20},{5,13},{6,22},{7,15},{8,24},{9,1... | collective-permute-start | bytes 737288 | tf_op jit(solution)/shard_map/ppermute | solution.py:327
  17.6 4.3 %collective-permute-done.7.refs_2_ = bf16[176,768]{1,0:T(8,128)(2,1)S(1)} collective-permute-done((bf16[176,768]{1,0:T(8,128)(2,1)S(1)}, bf16[176,768]{1,0:T(8,128)(2,1)S(1)}, u32[]{:S(2)}, u32[]{:S(2)}) %collective-permute-start.7) | collective-permute-done | bytes 270368 | tf_op jit(solution)/shard_map/ppermute | solution.py:322
  21.9 1.5 %collective-permute-start.8 = (bf16[176,768]{1,0:T(8,128)(2,1)S(1)}, bf16[176,768]{1,0:T(8,128)(2,1)S(1)}, u32[]{:S(2)}, u32[]{:S(2)}) collective-permute-start(bf16[176,768]{1,0:T(8,128)(2,1)S(1)} %collective-permute-done.7.refs_2_), channel_id=1, source_target_pairs={{0,16},{1,9},{2,18},{3,11},{4,20},{5,13},{6,22},{7,15},{8,24},{9,1... | collective-permute-start | bytes 811016 | tf_op jit(solution)/shard_map/ppermute | solution.py:327
  24.2 1.0 %shard_map.41 = (f32[1,640]{1,0:T(1,128)S(1)}, f32[1,320]{1,0:T(1,128)S(1)}) custom-call(bf16[336,768]{1,0:T(8,128)(2,1)S(1)} %get-tuple-element.33.block.refs_0_, bf16[336,768]{1,0:T(8,128)(2,1)S(1)} %get-tuple-element.37.partner, bf16[336,768]{1,0:T(8,128)(2,1)S(1)} %get-tuple-element.33.block.refs_0_, ...), custom_call_target="tpu_custom_call" | custom-call | flops 320 | bytes 320 | tf_op jit(solution)/shard_map/pallas_call | solution.py:224
  25.2 3.2 %collective-permute-done.8.refs_5_ = bf16[176,768]{1,0:T(8,128)(2,1)S(1)} collective-permute-done((bf16[176,768]{1,0:T(8,128)(2,1)S(1)}, bf16[176,768]{1,0:T(8,128)(2,1)S(1)}, u32[]{:S(2)}, u32[]{:S(2)}) %collective-permute-start.8) | collective-permute-done | bytes 270368 | tf_op jit(solution)/shard_map/ppermute | solution.py:327
  28.5 1.0 %shard_map.43 = (f32[1,640]{1,0:T(1,128)S(1)}, f32[1,320]{1,0:T(1,128)S(1)}) custom-call(bf16[336,768]{1,0:T(8,128)(2,1)S(1)} %get-tuple-element.33.block.refs_0_, bf16[336,768]{1,0:T(8,128)(2,1)S(1)} %get-tuple-element.37.partner, bf16[1280,768]{1,0:T(8,128)(2,1)S(1)} %get-tuple-element.44.held, f32[1,1280]{1,0:T(1,128)S(1)} %get-tuple-element.45.row), custom_call_target="tpu_custom_call" | custom-call | flops 320 | bytes 320 | tf_op jit(solution)/shard_map/pallas_call | solution.py:240
  29.7 2.0 %shard_map.44 = (f32[1,1280]{1,0:T(1,128)S(1)}, f32[1,640]{1,0:T(1,128)S(1)}) custom-call(bf16[320,768]{1,0:T(8,128)(2,1)S(1)} %get-tuple-element.32.first, bf16[336,768]{1,0:T(8,128)(2,1)S(1)} %collective-permute-done.4.second, bf16[1280,768]{1,0:T(8,128)(2,1)S(1)} %get-tuple-element.44.held, f32[1,1280]{1,0:T(1,128)S(1)} %get-tuple-element.45.row, ...), custom_call_target="tpu_custom_call" | custom-call | flops 320 | bytes 320 | tf_op jit(solution)/shard_map/pallas_call | solution.py:254
  31.7 2.0 %shard_map.45 = (f32[1,320]{1,0:T(1,128)S(1)}, f32[1,640]{1,0:T(1,128)S(1)}, f32[1,320]{1,0:T(1,128)S(1)}, f32[1,640]{1,0:T(1,128)S(1)}) custom-call(bf16[320,768]{1,0:T(8,128)(2,1)S(1)} %copy-done.1, bf16[336,768]{1,0:T(8,128)(2,1)S(1)} %collective-permute-done.12.second, bf16[1280,768]{1,0:T(8,128)(2,1)S(1)} %get-tuple-element.44.held, ...), custom_call_target="tpu_custom_call" | custom-call | flops 320 | bytes 320 | tf_op jit(solution)/shard_map/pallas_call | solution.py:254
  34.2 1.5 %collective-permute-start.16 = (f32[1,640]{1,0:T(1,128)S(1)}, f32[1,640]{1,0:T(1,128)S(1)}, u32[]{:S(2)}, u32[]{:S(2)}) collective-permute-start(f32[1,640]{1,0:T(1,128)S(1)} %get-tuple-element.55), channel_id=1, source_target_pairs={{0,8},{1,17},{2,10},{3,19},{4,12},{5,21},{6,14},{7,23},{8,0},{9,25... | collective-permute-start | bytes 7688 | tf_op jit(solution)/shard_map/ppermute | solution.py:369
  35.7 1.3 %collective-permute-start.14 = (f32[1,640]{1,0:T(1,128)S(1)}, f32[1,640]{1,0:T(1,128)S(1)}, u32[]{:S(2)}, u32[]{:S(2)}) collective-permute-start(f32[1,640]{1,0:T(1,128)S(1)} %max.24), channel_id=1, source_target_pairs={{2,6},{4,0},{6,4},{1,7},{3,1},{5,3},{10,14},{12,8},{14,12},{9,15},... | collective-permute-start | bytes 7688 | tf_op jit(solution)/shard_map/ppermute | solution.py:364
  37.0 0.8 %collective-permute-done.16 = f32[1,640]{1,0:T(1,128)S(1)} collective-permute-done((f32[1,640]{1,0:T(1,128)S(1)}, f32[1,640]{1,0:T(1,128)S(1)}, u32[]{:S(2)}, u32[]{:S(2)}) %collective-permute-start.16) | collective-permute-done | bytes 2592 | tf_op jit(solution)/shard_map/ppermute | solution.py:369
  37.9 1.1 %collective-permute-start.17 = (f32[1,320]{1,0:T(1,128)S(1)}, f32[1,320]{1,0:T(1,128)S(1)}, u32[]{:S(2)}, u32[]{:S(2)}) collective-permute-start(f32[1,320]{1,0:T(1,128)S(1)} %get-tuple-element.59), channel_id=1, source_target_pairs={{0,17},{1,8},{2,19},{3,10},{4,21},{5,12},{6,23},{7,14},{8,25},{9,0... | collective-permute-start | bytes 3848 | tf_op jit(solution)/shard_map/ppermute | solution.py:372
  39.0 0.5 %collective-permute-start.18 = (f32[1,320]{1,0:T(1,128)S(1)}, f32[1,320]{1,0:T(1,128)S(1)}, u32[]{:S(2)}, u32[]{:S(2)}) collective-permute-start(f32[1,320]{1,0:T(1,128)S(1)} %get-tuple-element.60), channel_id=1, source_target_pairs={{0,1},{1,0},{2,3},{3,2},{4,5},{5,4},{6,7},{7,6},{8,9},{9,8},{10,11... | collective-permute-start | bytes 3848 | tf_op jit(solution)/shard_map/ppermute | solution.py:374
  39.5 2.6 %collective-permute-done.14 = f32[1,640]{1,0:T(1,128)S(1)} collective-permute-done((f32[1,640]{1,0:T(1,128)S(1)}, f32[1,640]{1,0:T(1,128)S(1)}, u32[]{:S(2)}, u32[]{:S(2)}) %collective-permute-start.14) | collective-permute-done | bytes 2592 | tf_op jit(solution)/shard_map/ppermute | solution.py:364
  42.2 1.1 %collective-permute-done.15 = f32[1,320]{1,0:T(1,128)S(1)} collective-permute-done((f32[1,320]{1,0:T(1,128)S(1)}, f32[1,320]{1,0:T(1,128)S(1)}, u32[]{:S(2)}, u32[]{:S(2)}) %collective-permute-start.15) | collective-permute-done | bytes 1312 | tf_op jit(solution)/shard_map/ppermute | solution.py:368
  43.3 0.6 %fusion.2 = f32[320]{0:T(512)} fusion(f32[1,320]{1,0:T(1,128)S(1)} %collective-permute-done.18, f32[1,320]{1,0:T(1,128)S(1)} %collective-permute-done.17, f32[1,320]{1,0:T(1,128)S(1)} %collective-permute-done.15, f32[1,640]{1,0:T(1,128)S(1)} %broadcast_select_fusion), kind=kLoop, calls=%fused_computation.6 | loop fusion | flops 960 | bytes 6400 | tf_op jit(solution)/shard_map/max | solution.py:375
  (38 shorter events, 3.4 us)
Async XLA Ops:
  0.0 6.5 %collective-permute-start.1 = (bf16[320,768]{1,0:T(8,128)(2,1)}, bf16[320,768]{1,0:T(8,128)(2,1)S(1)}, u32[]{:S(2)}, u32[]{:S(2)}) collective-permute-start(bf16[320,768]{1,0:T(8,128)(2,1)} %embeddings.1), channel_id=1, source_target_pairs={{0,1},{1,0},{2,3},{3,2},{4,5},{5,4},{6,7},{7,6},{8,9},{9,8},{10,11... | collective-permute-start | bytes 1474568 | tf_op jit(solution)/shard_map/ppermute | solution.py:320
  0.5 6.0 %collective-permute-start.2 = (s32[1,320]{1,0:T(1,128)}, s32[1,320]{1,0:T(1,128)S(1)}, u32[]{:S(2)}, u32[]{:S(2)}) collective-permute-start(s32[1,320]{1,0:T(1,128)} %bitcast.1), channel_id=1, source_target_pairs={{0,1},{1,0},{2,3},{3,2},{4,5},{5,4},{6,7},{7,6},{8,9},{9,8},{10,11... | collective-permute-start | bytes 3848 | tf_op jit(solution)/shard_map/ppermute | solution.py:320
  0.5 6.0 %collective-permute-start.3 = (s32[320]{0:T(512)}, s32[320]{0:T(512)S(1)}, u32[]{:S(2)}, u32[]{:S(2)}) collective-permute-start(s32[320]{0:T(512)} %order_key.1), channel_id=1, source_target_pairs={{0,1},{1,0},{2,3},{3,2},{4,5},{5,4},{6,7},{7,6},{8,9},{9,8},{10,11... | collective-permute-start | bytes 3848 | tf_op jit(solution)/shard_map/ppermute | solution.py:320
  1.0 22.4 %collective-permute-start = (bf16[320,768]{1,0:T(8,128)(2,1)}, bf16[320,768]{1,0:T(8,128)(2,1)S(1)}, u32[]{:S(2)}, u32[]{:S(2)}) collective-permute-start(bf16[320,768]{1,0:T(8,128)(2,1)} %embeddings.1), channel_id=1, source_target_pairs={{6,2},{0,4},{4,6},{7,1},{1,3},{3,5},{14,10},{8,12},{12,14},{15,9},... | collective-permute-start | bytes 1474568 | tf_op jit(solution)/shard_map/ppermute | solution.py:319
  7.2 9.7 %collective-permute-start.5 = (bf16[160,768]{1,0:T(8,128)(2,1)S(1)}, bf16[160,768]{1,0:T(8,128)(2,1)S(1)}, u32[]{:S(2)}, u32[]{:S(2)}) collective-permute-start(bf16[160,768]{1,0:T(8,128)(2,1)S(1)} %get-tuple-element.35), channel_id=1, source_target_pairs={{0,8},{1,17},{2,10},{3,19},{4,12},{5,21},{6,14},{7,23},{8,0},{9,25... | collective-permute-start | bytes 737288 | tf_op jit(solution)/shard_map/ppermute | solution.py:322
  8.7 13.1 %collective-permute-start.7 = (bf16[176,768]{1,0:T(8,128)(2,1)S(1)}, bf16[176,768]{1,0:T(8,128)(2,1)S(1)}, u32[]{:S(2)}, u32[]{:S(2)}) collective-permute-start(bf16[176,768]{1,0:T(8,128)(2,1)S(1)} %get-tuple-element.36), channel_id=1, source_target_pairs={{0,8},{1,17},{2,10},{3,19},{4,12},{5,21},{6,14},{7,23},{8,0},{9,25... | collective-permute-start | bytes 811016 | tf_op jit(solution)/shard_map/ppermute | solution.py:322
  9.3 19.1 %collective-permute-start.9 = (bf16[336,768]{1,0:T(8,128)(2,1)S(1)}, bf16[336,768]{1,0:T(8,128)(2,1)S(1)}, u32[]{:S(2)}, u32[]{:S(2)}) collective-permute-start(bf16[336,768]{1,0:T(8,128)(2,1)S(1)} %get-tuple-element.33.block.refs_0_), channel_id=1, source_target_pairs={{0,16},{1,9},{2,18},{3,11},{4,20},{5,13},{6,22},{7,15},{8,24},{9,1... | collective-permute-start | bytes 1548296 | tf_op jit(solution)/shard_map/ppermute | solution.py:323
  10.8 1.0 %copy-start.2 = (bf16[320,768]{1,0:T(8,128)(2,1)S(1)}, bf16[320,768]{1,0:T(8,128)(2,1)}, u32[]{:S(2)}) copy-start(bf16[320,768]{1,0:T(8,128)(2,1)} %embeddings.1) | copy-start | bytes 1474564
  11.8 0.7 %copy-start.3 = (s32[320]{0:T(512)S(1)}, s32[320]{0:T(512)}, u32[]{:S(2)}) copy-start(s32[320]{0:T(512)} %order_key.1) | copy-start | bytes 3844
  12.5 0.7 %copy-start.4 = (s32[320,1]{0,1:T(1,128)S(1)}, s32[320,1]{0,1:T(1,128)}, u32[]{:S(2)}) copy-start(s32[320,1]{0,1:T(1,128)} %param.4) | copy-start | bytes 3844
  13.4 16.1 %collective-permute-start.4 = (bf16[336,768]{1,0:T(8,128)(2,1)S(1)}, bf16[336,768]{1,0:T(8,128)(2,1)S(1)}, u32[]{:S(2)}, u32[]{:S(2)}) collective-permute-start(bf16[336,768]{1,0:T(8,128)(2,1)S(1)} %shard_map.40), channel_id=1, source_target_pairs={{6,2},{0,4},{4,6},{7,1},{1,3},{3,5},{14,10},{8,12},{12,14},{15,9},... | collective-permute-start | bytes 1548296 | tf_op jit(solution)/shard_map/ppermute | solution.py:326
  16.9 6.7 %collective-permute-start.6 = (bf16[160,768]{1,0:T(8,128)(2,1)S(1)}, bf16[160,768]{1,0:T(8,128)(2,1)S(1)}, u32[]{:S(2)}, u32[]{:S(2)}) collective-permute-start(bf16[160,768]{1,0:T(8,128)(2,1)S(1)} %collective-permute-done.5.refs_1_), channel_id=1, source_target_pairs={{0,16},{1,9},{2,18},{3,11},{4,20},{5,13},{6,22},{7,15},{8,24},{9,1... | collective-permute-start | bytes 737288 | tf_op jit(solution)/shard_map/ppermute | solution.py:327
  21.9 6.5 %collective-permute-start.8 = (bf16[176,768]{1,0:T(8,128)(2,1)S(1)}, bf16[176,768]{1,0:T(8,128)(2,1)S(1)}, u32[]{:S(2)}, u32[]{:S(2)}) collective-permute-start(bf16[176,768]{1,0:T(8,128)(2,1)S(1)} %collective-permute-done.7.refs_2_), channel_id=1, source_target_pairs={{0,16},{1,9},{2,18},{3,11},{4,20},{5,13},{6,22},{7,15},{8,24},{9,1... | collective-permute-start | bytes 811016 | tf_op jit(solution)/shard_map/ppermute | solution.py:327
  23.6 4.8 %collective-permute-start.10 = (bf16[160,768]{1,0:T(8,128)(2,1)S(1)}, bf16[160,768]{1,0:T(8,128)(2,1)S(1)}, u32[]{:S(2)}, u32[]{:S(2)}) collective-permute-start(bf16[160,768]{1,0:T(8,128)(2,1)S(1)} %get-tuple-element.42), channel_id=1, source_target_pairs={{0,1},{1,0},{2,3},{3,2},{4,5},{5,4},{6,7},{7,6},{8,9},{9,8},{10,11... | collective-permute-start | bytes 737288 | tf_op jit(solution)/shard_map/ppermute | solution.py:332
  23.7 4.7 %collective-permute-start.11 = (bf16[160,768]{1,0:T(8,128)(2,1)S(1)}, bf16[160,768]{1,0:T(8,128)(2,1)S(1)}, u32[]{:S(2)}, u32[]{:S(2)}) collective-permute-start(bf16[160,768]{1,0:T(8,128)(2,1)S(1)} %get-tuple-element.43), channel_id=1, source_target_pairs={{0,1},{1,0},{2,3},{3,2},{4,5},{5,4},{6,7},{7,6},{8,9},{9,8},{10,11... | collective-permute-start | bytes 737288 | tf_op jit(solution)/shard_map/ppermute | solution.py:332
  28.5 1.0 %copy-start = (bf16[320,768]{1,0:T(8,128)(2,1)}, bf16[320,768]{1,0:T(8,128)(2,1)S(1)}, u32[]{:S(2)}) copy-start(bf16[320,768]{1,0:T(8,128)(2,1)S(1)} %get-tuple-element.51.first) | copy-start | bytes 1474564
  29.5 2.1 %collective-permute-start.12 = (bf16[336,768]{1,0:T(8,128)(2,1)S(1)}, bf16[336,768]{1,0:T(8,128)(2,1)S(1)}, u32[]{:S(2)}, u32[]{:S(2)}) collective-permute-start(bf16[336,768]{1,0:T(8,128)(2,1)S(1)} %collective-permute-done.4.second), channel_id=1, source_target_pairs={{0,1},{1,0},{2,3},{3,2},{4,5},{5,4},{6,7},{7,6},{8,9},{9,8},{10,11... | collective-permute-start | bytes 1548296 | tf_op jit(solution)/shard_map/ppermute | solution.py:347
  29.7 2.0 %copy-start.1 = (bf16[320,768]{1,0:T(8,128)(2,1)S(1)}, bf16[320,768]{1,0:T(8,128)(2,1)}, u32[]{:S(2)}) copy-start(bf16[320,768]{1,0:T(8,128)(2,1)} %copy-done) | copy-start | bytes 1474564
  33.7 2.0 %collective-permute-start.13 = (f32[1,640]{1,0:T(1,128)S(1)}, f32[1,640]{1,0:T(1,128)S(1)}, u32[]{:S(2)}, u32[]{:S(2)}) collective-permute-start(f32[1,640]{1,0:T(1,128)S(1)} %get-tuple-element.53), channel_id=1, source_target_pairs={{0,1},{1,0},{2,3},{3,2},{4,5},{5,4},{6,7},{7,6},{8,9},{9,8},{10,11... | collective-permute-start | bytes 7688 | tf_op jit(solution)/shard_map/ppermute | solution.py:361
  34.2 3.6 %collective-permute-start.16 = (f32[1,640]{1,0:T(1,128)S(1)}, f32[1,640]{1,0:T(1,128)S(1)}, u32[]{:S(2)}, u32[]{:S(2)}) collective-permute-start(f32[1,640]{1,0:T(1,128)S(1)} %get-tuple-element.55), channel_id=1, source_target_pairs={{0,8},{1,17},{2,10},{3,19},{4,12},{5,21},{6,14},{7,23},{8,0},{9,25... | collective-permute-start | bytes 7688 | tf_op jit(solution)/shard_map/ppermute | solution.py:369
  35.7 6.4 %collective-permute-start.14 = (f32[1,640]{1,0:T(1,128)S(1)}, f32[1,640]{1,0:T(1,128)S(1)}, u32[]{:S(2)}, u32[]{:S(2)}) collective-permute-start(f32[1,640]{1,0:T(1,128)S(1)} %max.24), channel_id=1, source_target_pairs={{2,6},{4,0},{6,4},{1,7},{3,1},{5,3},{10,14},{12,8},{14,12},{9,15},... | collective-permute-start | bytes 7688 | tf_op jit(solution)/shard_map/ppermute | solution.py:364
  37.9 4.3 %collective-permute-start.17 = (f32[1,320]{1,0:T(1,128)S(1)}, f32[1,320]{1,0:T(1,128)S(1)}, u32[]{:S(2)}, u32[]{:S(2)}) collective-permute-start(f32[1,320]{1,0:T(1,128)S(1)} %get-tuple-element.59), channel_id=1, source_target_pairs={{0,17},{1,8},{2,19},{3,10},{4,21},{5,12},{6,23},{7,14},{8,25},{9,0... | collective-permute-start | bytes 3848 | tf_op jit(solution)/shard_map/ppermute | solution.py:372
  39.0 3.3 %collective-permute-start.18 = (f32[1,320]{1,0:T(1,128)S(1)}, f32[1,320]{1,0:T(1,128)S(1)}, u32[]{:S(2)}, u32[]{:S(2)}) collective-permute-start(f32[1,320]{1,0:T(1,128)S(1)} %get-tuple-element.60), channel_id=1, source_target_pairs={{0,1},{1,0},{2,3},{3,2},{4,5},{5,4},{6,7},{7,6},{8,9},{9,8},{10,11... | collective-permute-start | bytes 3848 | tf_op jit(solution)/shard_map/ppermute | solution.py:374
  42.2 1.2 %collective-permute-start.15 = (f32[1,320]{1,0:T(1,128)S(1)}, f32[1,320]{1,0:T(1,128)S(1)}, u32[]{:S(2)}, u32[]{:S(2)}) collective-permute-start(f32[1,320]{1,0:T(1,128)S(1)} %slice.17), channel_id=1, source_target_pairs={{0,1},{1,0},{2,3},{3,2},{4,5},{5,4},{6,7},{7,6},{8,9},{9,8},{10,11... | collective-permute-start | bytes 3848 | tf_op jit(solution)/shard_map/ppermute | solution.py:368

commit v20 on v19

--- a/solution.py
+++ b/solution.py
@@ -268,7 +268,7 @@
 
 def line_rounds(chips):
     if chips == 4:
-        return [[(3, 1), (0, 2), (2, 3)], [(3, 0), (0, 1), (1, 2)]]
+        return [[(2, 0), (1, 3), (0, 1), (3, 2)], [(3, 0), (1, 2)]]
     rounds = []
     for shift in range(1, chips // 2 + 1):
         senders = chips // 2 if 2 * shift == chips else chips

time: 44.2 us -> 43.8 us (level)
  waiting for transfers between devices: 12 us -> 10.4 us
  starting transfers between devices: 21.2 us -> 22.5 us
    ppermute x1, waiting for transfers between devices: 2.6 us -> 0.84 us  [shards(): lax.ppermute(kept[:, 2 * at * rows:2 * (at + 1) * rows], BOTH, back(pairs))]
    ppermute x1, starting transfers between devices: 1.29 us -> 2.9 us  [shards(): lax.ppermute(kept[:, 2 * at * rows:2 * (at + 1) * rows], BOTH, back(pairs))]
    ppermute x1, waiting for transfers between devices: 0.01 us -> 1.25 us  [shards(): near_other = [lax.ppermute(both, BOTH, pairs) for pairs in rounds]]
    ppermute x1, starting transfers between devices: 5.51 us -> 4.47 us  [shards(): raw = [lax.ppermute(embeddings, BOTH, pairs) for pairs in rounds]]
    ppermute x1, starting transfers between devices: 3.49 us -> 4.5 us  [shards(): near_other = [lax.ppermute(both, BOTH, pairs) for pairs in rounds]]
    ppermute x2, waiting for transfers between devices: 4.28 us -> 3.41 us  [shards(): from_first = [lax.ppermute(part, BOTH, first) for part in parts]]
    ppermute x1, waiting for transfers between devices: 0.78 us -> 0.01 us  [shards(): from_x = lax.ppermute(bests[1], BOTH, first)]
    ppermute x1, starting transfers between devices: 1.08 us -> 1.64 us  [shards(): results.append(lax.ppermute(onward, BOTH, second_home))]
  transfers between devices with their start and end apart: 19 -> 19, of which waited for: 5 -> 7; matrix products, arithmetic and copies ran while one was open for 0% -> 0% of each run, Pallas kernels for 12% -> 12%
where the time goes in v20:
time: 43.8 us; the launch traced here: 43.5 us
  starting transfers between devices  22.5 us (51%)
  waiting for transfers between devices  10.4 us (24%)
  Pallas kernels  7.36 us (17%)
  local copies, waits for them, and re-layouts  2.47 us (6%)
  other arithmetic  0.68 us (2%)
    ppermute x1, starting transfers between devices, shards(): near_other = [lax.ppermute(both, BOTH, pairs) for pairs in rounds]  4.5 us
    ppermute x1, starting transfers between devices, shards(): raw = [lax.ppermute(embeddings, BOTH, pairs) for pairs in rounds]  4.47 us
    pallas_call x2, Pallas kernels, line(): pl.pallas_call(functools.partial(line_kernel, rows, span, together, len(b...  4.06 us
    ppermute x2, waiting for transfers between devices, shards(): from_corner = [lax.ppermute(part, BOTH, second) for part in from_first]  3.69 us
    ppermute x2, waiting for transfers between devices, shards(): from_first = [lax.ppermute(part, BOTH, first) for part in parts]  3.41 us
    ppermute x1, starting transfers between devices, shards(): lax.ppermute(kept[:, 2 * at * rows:2 * (at + 1) * rows], BOTH, back(pairs))  2.9 us
    unnamed x10, local copies, waits for them, and re-layouts  2.4 us
    ppermute x2, starting transfers between devices, shards(): from_corner = [lax.ppermute(part, BOTH, second) for part in from_first]  2.06 us
  transfers between devices with their start and end apart: 19, of which 7 were waited for; matrix products, arithmetic and copies ran while one was open for 0% of the time, Pallas kernels for 12%

profile of v20, /device:TPU:0, one launch (start us, length us, event | category | flops | bytes accessed | tf_op | source)
XLA Modules:
  0.0 43.5 jit_solution(11708568010071937635)
XLA Ops:
  1.0 4.5 %collective-permute-start = (bf16[320,768]{1,0:T(8,128)(2,1)}, bf16[320,768]{1,0:T(8,128)(2,1)S(1)}, u32[]{:S(2)}, u32[]{:S(2)}) collective-permute-start(bf16[320,768]{1,0:T(8,128)(2,1)} %embeddings.1), channel_id=1, source_target_pairs={{4,0},{2,6},{0,2},{6,4},{7,1},{3,5},{12,8},{10,14},{8,10},{14,12},... | collective-permute-start | bytes 1474568 | tf_op jit(solution)/shard_map/ppermute | solution.py:319
  5.5 0.7 %shard_map.38 = (bf16[336,768]{1,0:T(8,128)(2,1)S(1)}, bf16[16,768]{1,0:T(8,128)(2,1)}, bf16[160,768]{1,0:T(8,128)(2,1)S(1)}, bf16[176,768]{1,0:T(8,128)(2,1)S(1)}) custom-call(bf16[320,768]{1,0:T(8,128)(2,1)S(1)} %collective-permute-done.1.embeddings, s32[1,320]{1,0:T(1,128)S(1)} %collective-permute-done.2.cluster, s32[320]{0:T(512)S(1)} %collective-permute-done.3.order_key), custom_call_target="tpu_custom_call" | custom-call | flops 320 | bytes 320 | tf_op jit(solution)/shard_map/pallas_call | solution.py:73
  6.2 1.5 %collective-permute-start.5 = (bf16[160,768]{1,0:T(8,128)(2,1)S(1)}, bf16[160,768]{1,0:T(8,128)(2,1)S(1)}, u32[]{:S(2)}, u32[]{:S(2)}) collective-permute-start(bf16[160,768]{1,0:T(8,128)(2,1)S(1)} %get-tuple-element.35), channel_id=1, source_target_pairs={{0,8},{1,17},{2,10},{3,19},{4,12},{5,21},{6,14},{7,23},{8,0},{9,25... | collective-permute-start | bytes 737288 | tf_op jit(solution)/shard_map/ppermute | solution.py:322
  7.7 0.5 %collective-permute-start.7 = (bf16[176,768]{1,0:T(8,128)(2,1)S(1)}, bf16[176,768]{1,0:T(8,128)(2,1)S(1)}, u32[]{:S(2)}, u32[]{:S(2)}) collective-permute-start(bf16[176,768]{1,0:T(8,128)(2,1)S(1)} %get-tuple-element.36), channel_id=1, source_target_pairs={{0,8},{1,17},{2,10},{3,19},{4,12},{5,21},{6,14},{7,23},{8,0},{9,25... | collective-permute-start | bytes 811016 | tf_op jit(solution)/shard_map/ppermute | solution.py:322
  8.2 1.5 %collective-permute-start.9 = (bf16[336,768]{1,0:T(8,128)(2,1)S(1)}, bf16[336,768]{1,0:T(8,128)(2,1)S(1)}, u32[]{:S(2)}, u32[]{:S(2)}) collective-permute-start(bf16[336,768]{1,0:T(8,128)(2,1)S(1)} %get-tuple-element.33.block.refs_0_), channel_id=1, source_target_pairs={{0,16},{1,9},{2,18},{3,11},{4,20},{5,13},{6,22},{7,15},{8,24},{9,1... | collective-permute-start | bytes 1548296 | tf_op jit(solution)/shard_map/ppermute | solution.py:323
  9.8 1.0 %copy-done.2 = bf16[320,768]{1,0:T(8,128)(2,1)S(1)} copy-done((bf16[320,768]{1,0:T(8,128)(2,1)S(1)}, bf16[320,768]{1,0:T(8,128)(2,1)}, u32[]{:S(2)}) %copy-start.2) | copy-done | bytes 491544
  10.8 0.7 %copy-done.3 = s32[320]{0:T(512)S(1)} copy-done((s32[320]{0:T(512)S(1)}, s32[320]{0:T(512)}, u32[]{:S(2)}) %copy-start.3) | copy-done | bytes 1304
  11.5 0.7 %copy-done.4 = s32[320,1]{0,1:T(1,128)S(1)} copy-done((s32[320,1]{0,1:T(1,128)S(1)}, s32[320,1]{0,1:T(1,128)}, u32[]{:S(2)}) %copy-start.4) | copy-done | bytes 1304
  12.4 4.5 %collective-permute-start.4 = (bf16[336,768]{1,0:T(8,128)(2,1)S(1)}, bf16[336,768]{1,0:T(8,128)(2,1)S(1)}, u32[]{:S(2)}, u32[]{:S(2)}) collective-permute-start(bf16[336,768]{1,0:T(8,128)(2,1)S(1)} %shard_map.40), channel_id=1, source_target_pairs={{4,0},{2,6},{0,2},{6,4},{7,1},{3,5},{12,8},{10,14},{8,10},{14,12},... | collective-permute-start | bytes 1548296 | tf_op jit(solution)/shard_map/ppermute | solution.py:326
  16.9 0.6 %collective-permute-start.6 = (bf16[160,768]{1,0:T(8,128)(2,1)S(1)}, bf16[160,768]{1,0:T(8,128)(2,1)S(1)}, u32[]{:S(2)}, u32[]{:S(2)}) collective-permute-start(bf16[160,768]{1,0:T(8,128)(2,1)S(1)} %collective-permute-done.5.refs_1_), channel_id=1, source_target_pairs={{0,16},{1,9},{2,18},{3,11},{4,20},{5,13},{6,22},{7,15},{8,24},{9,1... | collective-permute-start | bytes 737288 | tf_op jit(solution)/shard_map/ppermute | solution.py:327
  17.5 3.4 %collective-permute-done.7.refs_2_ = bf16[176,768]{1,0:T(8,128)(2,1)S(1)} collective-permute-done((bf16[176,768]{1,0:T(8,128)(2,1)S(1)}, bf16[176,768]{1,0:T(8,128)(2,1)S(1)}, u32[]{:S(2)}, u32[]{:S(2)}) %collective-permute-start.7) | collective-permute-done | bytes 270368 | tf_op jit(solution)/shard_map/ppermute | solution.py:322
  20.9 1.5 %collective-permute-start.8 = (bf16[176,768]{1,0:T(8,128)(2,1)S(1)}, bf16[176,768]{1,0:T(8,128)(2,1)S(1)}, u32[]{:S(2)}, u32[]{:S(2)}) collective-permute-start(bf16[176,768]{1,0:T(8,128)(2,1)S(1)} %collective-permute-done.7.refs_2_), channel_id=1, source_target_pairs={{0,16},{1,9},{2,18},{3,11},{4,20},{5,13},{6,22},{7,15},{8,24},{9,1... | collective-permute-start | bytes 811016 | tf_op jit(solution)/shard_map/ppermute | solution.py:327
  23.2 1.0 %shard_map.41 = (f32[1,640]{1,0:T(1,128)S(1)}, f32[1,320]{1,0:T(1,128)S(1)}) custom-call(bf16[336,768]{1,0:T(8,128)(2,1)S(1)} %get-tuple-element.33.block.refs_0_, bf16[336,768]{1,0:T(8,128)(2,1)S(1)} %get-tuple-element.37.partner, bf16[336,768]{1,0:T(8,128)(2,1)S(1)} %get-tuple-element.33.block.refs_0_, ...), custom_call_target="tpu_custom_call" | custom-call | flops 320 | bytes 320 | tf_op jit(solution)/shard_map/pallas_call | solution.py:224
  24.2 3.2 %collective-permute-done.8.refs_5_ = bf16[176,768]{1,0:T(8,128)(2,1)S(1)} collective-permute-done((bf16[176,768]{1,0:T(8,128)(2,1)S(1)}, bf16[176,768]{1,0:T(8,128)(2,1)S(1)}, u32[]{:S(2)}, u32[]{:S(2)}) %collective-permute-start.8) | collective-permute-done | bytes 270368 | tf_op jit(solution)/shard_map/ppermute | solution.py:327
  27.5 1.0 %shard_map.43 = (f32[1,640]{1,0:T(1,128)S(1)}, f32[1,320]{1,0:T(1,128)S(1)}) custom-call(bf16[336,768]{1,0:T(8,128)(2,1)S(1)} %get-tuple-element.33.block.refs_0_, bf16[336,768]{1,0:T(8,128)(2,1)S(1)} %get-tuple-element.37.partner, bf16[1280,768]{1,0:T(8,128)(2,1)S(1)} %get-tuple-element.44.held, f32[1,1280]{1,0:T(1,128)S(1)} %get-tuple-element.45.row), custom_call_target="tpu_custom_call" | custom-call | flops 320 | bytes 320 | tf_op jit(solution)/shard_map/pallas_call | solution.py:240
  28.5 1.2 %collective-permute-done.4.second = bf16[336,768]{1,0:T(8,128)(2,1)S(1)} collective-permute-done((bf16[336,768]{1,0:T(8,128)(2,1)S(1)}, bf16[336,768]{1,0:T(8,128)(2,1)S(1)}, u32[]{:S(2)}, u32[]{:S(2)}) %collective-permute-start.4) | collective-permute-done | bytes 516128 | tf_op jit(solution)/shard_map/ppermute | solution.py:326
  29.8 2.0 %shard_map.44 = (f32[1,1280]{1,0:T(1,128)S(1)}, f32[1,640]{1,0:T(1,128)S(1)}) custom-call(bf16[320,768]{1,0:T(8,128)(2,1)S(1)} %get-tuple-element.32.first, bf16[336,768]{1,0:T(8,128)(2,1)S(1)} %collective-permute-done.4.second, bf16[1280,768]{1,0:T(8,128)(2,1)S(1)} %get-tuple-element.44.held, f32[1,1280]{1,0:T(1,128)S(1)} %get-tuple-element.45.row, ...), custom_call_target="tpu_custom_call" | custom-call | flops 320 | bytes 320 | tf_op jit(solution)/shard_map/pallas_call | solution.py:254
  31.8 2.0 %shard_map.45 = (f32[1,320]{1,0:T(1,128)S(1)}, f32[1,640]{1,0:T(1,128)S(1)}, f32[1,320]{1,0:T(1,128)S(1)}, f32[1,640]{1,0:T(1,128)S(1)}) custom-call(bf16[320,768]{1,0:T(8,128)(2,1)S(1)} %copy-done.1, bf16[336,768]{1,0:T(8,128)(2,1)S(1)} %collective-permute-done.12.second, bf16[1280,768]{1,0:T(8,128)(2,1)S(1)} %get-tuple-element.44.held, ...), custom_call_target="tpu_custom_call" | custom-call | flops 320 | bytes 320 | tf_op jit(solution)/shard_map/pallas_call | solution.py:254
  34.4 1.8 %collective-permute-start.16 = (f32[1,640]{1,0:T(1,128)S(1)}, f32[1,640]{1,0:T(1,128)S(1)}, u32[]{:S(2)}, u32[]{:S(2)}) collective-permute-start(f32[1,640]{1,0:T(1,128)S(1)} %get-tuple-element.55), channel_id=1, source_target_pairs={{0,8},{1,17},{2,10},{3,19},{4,12},{5,21},{6,14},{7,23},{8,0},{9,25... | collective-permute-start | bytes 7688 | tf_op jit(solution)/shard_map/ppermute | solution.py:369
  36.2 2.9 %collective-permute-start.14 = (f32[1,640]{1,0:T(1,128)S(1)}, f32[1,640]{1,0:T(1,128)S(1)}, u32[]{:S(2)}, u32[]{:S(2)}) collective-permute-start(f32[1,640]{1,0:T(1,128)S(1)} %max.24), channel_id=1, source_target_pairs={{0,4},{6,2},{2,0},{4,6},{1,7},{5,3},{8,12},{14,10},{10,8},{12,14},... | collective-permute-start | bytes 7688 | tf_op jit(solution)/shard_map/ppermute | solution.py:364
  39.2 1.6 %collective-permute-start.17 = (f32[1,320]{1,0:T(1,128)S(1)}, f32[1,320]{1,0:T(1,128)S(1)}, u32[]{:S(2)}, u32[]{:S(2)}) collective-permute-start(f32[1,320]{1,0:T(1,128)S(1)} %get-tuple-element.59), channel_id=1, source_target_pairs={{0,17},{1,8},{2,19},{3,10},{4,21},{5,12},{6,23},{7,14},{8,25},{9,0... | collective-permute-start | bytes 3848 | tf_op jit(solution)/shard_map/ppermute | solution.py:372
  40.8 0.8 %collective-permute-done.14 = f32[1,640]{1,0:T(1,128)S(1)} collective-permute-done((f32[1,640]{1,0:T(1,128)S(1)}, f32[1,640]{1,0:T(1,128)S(1)}, u32[]{:S(2)}, u32[]{:S(2)}) %collective-permute-start.14) | collective-permute-done | bytes 2592 | tf_op jit(solution)/shard_map/ppermute | solution.py:364
  42.2 0.7 %collective-permute-done.15 = f32[1,320]{1,0:T(1,128)S(1)} collective-permute-done((f32[1,320]{1,0:T(1,128)S(1)}, f32[1,320]{1,0:T(1,128)S(1)}, u32[]{:S(2)}, u32[]{:S(2)}) %collective-permute-start.15) | collective-permute-done | bytes 1312 | tf_op jit(solution)/shard_map/ppermute | solution.py:368
  42.9 0.6 %fusion.2 = f32[320]{0:T(512)} fusion(f32[1,320]{1,0:T(1,128)S(1)} %collective-permute-done.18, f32[1,320]{1,0:T(1,128)S(1)} %collective-permute-done.17, f32[1,320]{1,0:T(1,128)S(1)} %collective-permute-done.15, f32[1,640]{1,0:T(1,128)S(1)} %broadcast_select_fusion), kind=kLoop, calls=%fused_computation.6 | loop fusion | flops 960 | bytes 6400 | tf_op jit(solution)/shard_map/max | solution.py:375
  (38 shorter events, 3.3 us)
Async XLA Ops:
  0.0 5.5 %collective-permute-start.1 = (bf16[320,768]{1,0:T(8,128)(2,1)}, bf16[320,768]{1,0:T(8,128)(2,1)S(1)}, u32[]{:S(2)}, u32[]{:S(2)}) collective-permute-start(bf16[320,768]{1,0:T(8,128)(2,1)} %embeddings.1), channel_id=1, source_target_pairs={{0,1},{1,0},{2,3},{3,2},{4,5},{5,4},{6,7},{7,6},{8,9},{9,8},{10,11... | collective-permute-start | bytes 1474568 | tf_op jit(solution)/shard_map/ppermute | solution.py:320
  0.5 5.0 %collective-permute-start.2 = (s32[1,320]{1,0:T(1,128)}, s32[1,320]{1,0:T(1,128)S(1)}, u32[]{:S(2)}, u32[]{:S(2)}) collective-permute-start(s32[1,320]{1,0:T(1,128)} %bitcast.1), channel_id=1, source_target_pairs={{0,1},{1,0},{2,3},{3,2},{4,5},{5,4},{6,7},{7,6},{8,9},{9,8},{10,11... | collective-permute-start | bytes 3848 | tf_op jit(solution)/shard_map/ppermute | solution.py:320
  0.5 4.9 %collective-permute-start.3 = (s32[320]{0:T(512)}, s32[320]{0:T(512)S(1)}, u32[]{:S(2)}, u32[]{:S(2)}) collective-permute-start(s32[320]{0:T(512)} %order_key.1), channel_id=1, source_target_pairs={{0,1},{1,0},{2,3},{3,2},{4,5},{5,4},{6,7},{7,6},{8,9},{9,8},{10,11... | collective-permute-start | bytes 3848 | tf_op jit(solution)/shard_map/ppermute | solution.py:320
  1.0 21.4 %collective-permute-start = (bf16[320,768]{1,0:T(8,128)(2,1)}, bf16[320,768]{1,0:T(8,128)(2,1)S(1)}, u32[]{:S(2)}, u32[]{:S(2)}) collective-permute-start(bf16[320,768]{1,0:T(8,128)(2,1)} %embeddings.1), channel_id=1, source_target_pairs={{4,0},{2,6},{0,2},{6,4},{7,1},{3,5},{12,8},{10,14},{8,10},{14,12},... | collective-permute-start | bytes 1474568 | tf_op jit(solution)/shard_map/ppermute | solution.py:319
  6.2 10.7 %collective-permute-start.5 = (bf16[160,768]{1,0:T(8,128)(2,1)S(1)}, bf16[160,768]{1,0:T(8,128)(2,1)S(1)}, u32[]{:S(2)}, u32[]{:S(2)}) collective-permute-start(bf16[160,768]{1,0:T(8,128)(2,1)S(1)} %get-tuple-element.35), channel_id=1, source_target_pairs={{0,8},{1,17},{2,10},{3,19},{4,12},{5,21},{6,14},{7,23},{8,0},{9,25... | collective-permute-start | bytes 737288 | tf_op jit(solution)/shard_map/ppermute | solution.py:322
  7.7 13.2 %collective-permute-start.7 = (bf16[176,768]{1,0:T(8,128)(2,1)S(1)}, bf16[176,768]{1,0:T(8,128)(2,1)S(1)}, u32[]{:S(2)}, u32[]{:S(2)}) collective-permute-start(bf16[176,768]{1,0:T(8,128)(2,1)S(1)} %get-tuple-element.36), channel_id=1, source_target_pairs={{0,8},{1,17},{2,10},{3,19},{4,12},{5,21},{6,14},{7,23},{8,0},{9,25... | collective-permute-start | bytes 811016 | tf_op jit(solution)/shard_map/ppermute | solution.py:322
  8.2 19.1 %collective-permute-start.9 = (bf16[336,768]{1,0:T(8,128)(2,1)S(1)}, bf16[336,768]{1,0:T(8,128)(2,1)S(1)}, u32[]{:S(2)}, u32[]{:S(2)}) collective-permute-start(bf16[336,768]{1,0:T(8,128)(2,1)S(1)} %get-tuple-element.33.block.refs_0_), channel_id=1, source_target_pairs={{0,16},{1,9},{2,18},{3,11},{4,20},{5,13},{6,22},{7,15},{8,24},{9,1... | collective-permute-start | bytes 1548296 | tf_op jit(solution)/shard_map/ppermute | solution.py:323
  9.8 1.0 %copy-start.2 = (bf16[320,768]{1,0:T(8,128)(2,1)S(1)}, bf16[320,768]{1,0:T(8,128)(2,1)}, u32[]{:S(2)}) copy-start(bf16[320,768]{1,0:T(8,128)(2,1)} %embeddings.1) | copy-start | bytes 1474564
  10.8 0.7 %copy-start.3 = (s32[320]{0:T(512)S(1)}, s32[320]{0:T(512)}, u32[]{:S(2)}) copy-start(s32[320]{0:T(512)} %order_key.1) | copy-start | bytes 3844
  11.5 0.7 %copy-start.4 = (s32[320,1]{0,1:T(1,128)S(1)}, s32[320,1]{0,1:T(1,128)}, u32[]{:S(2)}) copy-start(s32[320,1]{0,1:T(1,128)} %param.4) | copy-start | bytes 3844
  12.4 17.4 %collective-permute-start.4 = (bf16[336,768]{1,0:T(8,128)(2,1)S(1)}, bf16[336,768]{1,0:T(8,128)(2,1)S(1)}, u32[]{:S(2)}, u32[]{:S(2)}) collective-permute-start(bf16[336,768]{1,0:T(8,128)(2,1)S(1)} %shard_map.40), channel_id=1, source_target_pairs={{4,0},{2,6},{0,2},{6,4},{7,1},{3,5},{12,8},{10,14},{8,10},{14,12},... | collective-permute-start | bytes 1548296 | tf_op jit(solution)/shard_map/ppermute | solution.py:326
  16.9 6.3 %collective-permute-start.6 = (bf16[160,768]{1,0:T(8,128)(2,1)S(1)}, bf16[160,768]{1,0:T(8,128)(2,1)S(1)}, u32[]{:S(2)}, u32[]{:S(2)}) collective-permute-start(bf16[160,768]{1,0:T(8,128)(2,1)S(1)} %collective-permute-done.5.refs_1_), channel_id=1, source_target_pairs={{0,16},{1,9},{2,18},{3,11},{4,20},{5,13},{6,22},{7,15},{8,24},{9,1... | collective-permute-start | bytes 737288 | tf_op jit(solution)/shard_map/ppermute | solution.py:327
  20.9 6.5 %collective-permute-start.8 = (bf16[176,768]{1,0:T(8,128)(2,1)S(1)}, bf16[176,768]{1,0:T(8,128)(2,1)S(1)}, u32[]{:S(2)}, u32[]{:S(2)}) collective-permute-start(bf16[176,768]{1,0:T(8,128)(2,1)S(1)} %collective-permute-done.7.refs_2_), channel_id=1, source_target_pairs={{0,16},{1,9},{2,18},{3,11},{4,20},{5,13},{6,22},{7,15},{8,24},{9,1... | collective-permute-start | bytes 811016 | tf_op jit(solution)/shard_map/ppermute | solution.py:327
  22.6 4.8 %collective-permute-start.10 = (bf16[160,768]{1,0:T(8,128)(2,1)S(1)}, bf16[160,768]{1,0:T(8,128)(2,1)S(1)}, u32[]{:S(2)}, u32[]{:S(2)}) collective-permute-start(bf16[160,768]{1,0:T(8,128)(2,1)S(1)} %get-tuple-element.42), channel_id=1, source_target_pairs={{0,1},{1,0},{2,3},{3,2},{4,5},{5,4},{6,7},{7,6},{8,9},{9,8},{10,11... | collective-permute-start | bytes 737288 | tf_op jit(solution)/shard_map/ppermute | solution.py:332
  23.2 4.2 %collective-permute-start.11 = (bf16[160,768]{1,0:T(8,128)(2,1)S(1)}, bf16[160,768]{1,0:T(8,128)(2,1)S(1)}, u32[]{:S(2)}, u32[]{:S(2)}) collective-permute-start(bf16[160,768]{1,0:T(8,128)(2,1)S(1)} %get-tuple-element.43), channel_id=1, source_target_pairs={{0,1},{1,0},{2,3},{3,2},{4,5},{5,4},{6,7},{7,6},{8,9},{9,8},{10,11... | collective-permute-start | bytes 737288 | tf_op jit(solution)/shard_map/ppermute | solution.py:332
  27.5 2.3 %copy-start = (bf16[320,768]{1,0:T(8,128)(2,1)}, bf16[320,768]{1,0:T(8,128)(2,1)S(1)}, u32[]{:S(2)}) copy-start(bf16[320,768]{1,0:T(8,128)(2,1)S(1)} %get-tuple-element.51.first) | copy-start | bytes 1474564
  29.8 2.0 %collective-permute-start.12 = (bf16[336,768]{1,0:T(8,128)(2,1)S(1)}, bf16[336,768]{1,0:T(8,128)(2,1)S(1)}, u32[]{:S(2)}, u32[]{:S(2)}) collective-permute-start(bf16[336,768]{1,0:T(8,128)(2,1)S(1)} %collective-permute-done.4.second), channel_id=1, source_target_pairs={{0,1},{1,0},{2,3},{3,2},{4,5},{5,4},{6,7},{7,6},{8,9},{9,8},{10,11... | collective-permute-start | bytes 1548296 | tf_op jit(solution)/shard_map/ppermute | solution.py:347
  29.8 2.0 %copy-start.1 = (bf16[320,768]{1,0:T(8,128)(2,1)S(1)}, bf16[320,768]{1,0:T(8,128)(2,1)}, u32[]{:S(2)}) copy-start(bf16[320,768]{1,0:T(8,128)(2,1)} %copy-done) | copy-start | bytes 1474564
  33.9 2.3 %collective-permute-start.13 = (f32[1,640]{1,0:T(1,128)S(1)}, f32[1,640]{1,0:T(1,128)S(1)}, u32[]{:S(2)}, u32[]{:S(2)}) collective-permute-start(f32[1,640]{1,0:T(1,128)S(1)} %get-tuple-element.53), channel_id=1, source_target_pairs={{0,1},{1,0},{2,3},{3,2},{4,5},{5,4},{6,7},{7,6},{8,9},{9,8},{10,11... | collective-permute-start | bytes 7688 | tf_op jit(solution)/shard_map/ppermute | solution.py:361
  34.4 4.7 %collective-permute-start.16 = (f32[1,640]{1,0:T(1,128)S(1)}, f32[1,640]{1,0:T(1,128)S(1)}, u32[]{:S(2)}, u32[]{:S(2)}) collective-permute-start(f32[1,640]{1,0:T(1,128)S(1)} %get-tuple-element.55), channel_id=1, source_target_pairs={{0,8},{1,17},{2,10},{3,19},{4,12},{5,21},{6,14},{7,23},{8,0},{9,25... | collective-permute-start | bytes 7688 | tf_op jit(solution)/shard_map/ppermute | solution.py:369
  36.2 5.5 %collective-permute-start.14 = (f32[1,640]{1,0:T(1,128)S(1)}, f32[1,640]{1,0:T(1,128)S(1)}, u32[]{:S(2)}, u32[]{:S(2)}) collective-permute-start(f32[1,640]{1,0:T(1,128)S(1)} %max.24), channel_id=1, source_target_pairs={{0,4},{6,2},{2,0},{4,6},{1,7},{5,3},{8,12},{14,10},{10,8},{12,14},... | collective-permute-start | bytes 7688 | tf_op jit(solution)/shard_map/ppermute | solution.py:364
  39.2 3.0 %collective-permute-start.17 = (f32[1,320]{1,0:T(1,128)S(1)}, f32[1,320]{1,0:T(1,128)S(1)}, u32[]{:S(2)}, u32[]{:S(2)}) collective-permute-start(f32[1,320]{1,0:T(1,128)S(1)} %get-tuple-element.59), channel_id=1, source_target_pairs={{0,17},{1,8},{2,19},{3,10},{4,21},{5,12},{6,23},{7,14},{8,25},{9,0... | collective-permute-start | bytes 3848 | tf_op jit(solution)/shard_map/ppermute | solution.py:372
  40.8 1.4 %collective-permute-start.18 = (f32[1,320]{1,0:T(1,128)S(1)}, f32[1,320]{1,0:T(1,128)S(1)}, u32[]{:S(2)}, u32[]{:S(2)}) collective-permute-start(f32[1,320]{1,0:T(1,128)S(1)} %get-tuple-element.60), channel_id=1, source_target_pairs={{0,1},{1,0},{2,3},{3,2},{4,5},{5,4},{6,7},{7,6},{8,9},{9,8},{10,11... | collective-permute-start | bytes 3848 | tf_op jit(solution)/shard_map/ppermute | solution.py:374
  41.8 1.2 %collective-permute-start.15 = (f32[1,320]{1,0:T(1,128)S(1)}, f32[1,320]{1,0:T(1,128)S(1)}, u32[]{:S(2)}, u32[]{:S(2)}) collective-permute-start(f32[1,320]{1,0:T(1,128)S(1)} %slice.17), channel_id=1, source_target_pairs={{0,1},{1,0},{2,3},{3,2},{4,5},{5,4},{6,7},{7,6},{8,9},{9,8},{10,11... | collective-permute-start | bytes 3848 | tf_op jit(solution)/shard_map/ppermute | solution.py:368

commit v21 on v17

--- a/solution.py
+++ b/solution.py
@@ -11,7 +11,7 @@
 EXTRA = 16
 CODES = 3
 LANES = 128
-TILE = 256
+TILE = 640
 CHUNK = 32
 BOTH = ("dp", "grid")
 

time: 43.6 us -> 44 us (level)
  no operation moved by 1% of the time
where the time goes in v21:
time: 44 us; the launch traced here: 43.7 us
  starting transfers between devices  21.9 us (50%)
  waiting for transfers between devices  10.8 us (25%)
  Pallas kernels  7.65 us (17%)
  local copies, waits for them, and re-layouts  2.47 us (6%)
  other arithmetic  0.68 us (2%)
    ppermute x1, starting transfers between devices, shards(): raw = [lax.ppermute(embeddings, BOTH, pairs) for pairs in rounds]  5.49 us
    ppermute x2, waiting for transfers between devices, shards(): from_corner = [lax.ppermute(part, BOTH, second) for part in from_first]  4.74 us
    pallas_call x2, Pallas kernels, line(): pl.pallas_call(functools.partial(line_kernel, rows, span, together, len(b...  4.36 us
    ppermute x1, starting transfers between devices, shards(): lax.ppermute(kept[:, 2 * at * rows:2 * (at + 1) * rows], BOTH, back(pairs))  4.22 us
    ppermute x2, waiting for transfers between devices, shards(): from_first = [lax.ppermute(part, BOTH, first) for part in parts]  4.11 us
    unnamed x10, local copies, waits for them, and re-layouts  2.4 us
    ppermute x2, starting transfers between devices, shards(): from_corner = [lax.ppermute(part, BOTH, second) for part in from_first]  2.09 us
    ppermute x2, starting transfers between devices, shards(): from_first = [lax.ppermute(part, BOTH, first) for part in parts]  2.03 us
  transfers between devices with their start and end apart: 19, of which 6 were waited for; matrix products, arithmetic and copies ran while one was open for 0% of the time, Pallas kernels for 12%

profile of v21, /device:TPU:0, one launch (start us, length us, event | category | flops | bytes accessed | tf_op | source)
XLA Modules:
  0.0 43.7 jit_solution(5026894112422749887)
XLA Ops:
  1.0 5.5 %collective-permute-start = (bf16[320,768]{1,0:T(8,128)(2,1)}, bf16[320,768]{1,0:T(8,128)(2,1)S(1)}, u32[]{:S(2)}, u32[]{:S(2)}) collective-permute-start(bf16[320,768]{1,0:T(8,128)(2,1)} %embeddings.1), channel_id=1, source_target_pairs={{0,4},{6,2},{2,0},{1,7},{7,5},{5,3},{8,12},{14,10},{10,8},{9,15},{... | collective-permute-start | bytes 1474568 | tf_op jit(solution)/shard_map/ppermute | solution.py:319
  6.5 0.7 %shard_map.38 = (bf16[336,768]{1,0:T(8,128)(2,1)S(1)}, bf16[16,768]{1,0:T(8,128)(2,1)}, bf16[160,768]{1,0:T(8,128)(2,1)S(1)}, bf16[176,768]{1,0:T(8,128)(2,1)S(1)}) custom-call(bf16[320,768]{1,0:T(8,128)(2,1)S(1)} %collective-permute-done.1.embeddings, s32[1,320]{1,0:T(1,128)S(1)} %collective-permute-done.2.cluster, s32[320]{0:T(512)S(1)} %collective-permute-done.3.order_key), custom_call_target="tpu_custom_call" | custom-call | flops 320 | bytes 320 | tf_op jit(solution)/shard_map/pallas_call | solution.py:73
  7.2 1.5 %collective-permute-start.5 = (bf16[160,768]{1,0:T(8,128)(2,1)S(1)}, bf16[160,768]{1,0:T(8,128)(2,1)S(1)}, u32[]{:S(2)}, u32[]{:S(2)}) collective-permute-start(bf16[160,768]{1,0:T(8,128)(2,1)S(1)} %get-tuple-element.35), channel_id=1, source_target_pairs={{0,8},{1,17},{2,10},{3,19},{4,12},{5,21},{6,14},{7,23},{8,0},{9,25... | collective-permute-start | bytes 737288 | tf_op jit(solution)/shard_map/ppermute | solution.py:322
  8.7 0.5 %collective-permute-start.7 = (bf16[176,768]{1,0:T(8,128)(2,1)S(1)}, bf16[176,768]{1,0:T(8,128)(2,1)S(1)}, u32[]{:S(2)}, u32[]{:S(2)}) collective-permute-start(bf16[176,768]{1,0:T(8,128)(2,1)S(1)} %get-tuple-element.36), channel_id=1, source_target_pairs={{0,8},{1,17},{2,10},{3,19},{4,12},{5,21},{6,14},{7,23},{8,0},{9,25... | collective-permute-start | bytes 811016 | tf_op jit(solution)/shard_map/ppermute | solution.py:322
  9.2 1.5 %collective-permute-start.9 = (bf16[336,768]{1,0:T(8,128)(2,1)S(1)}, bf16[336,768]{1,0:T(8,128)(2,1)S(1)}, u32[]{:S(2)}, u32[]{:S(2)}) collective-permute-start(bf16[336,768]{1,0:T(8,128)(2,1)S(1)} %get-tuple-element.33.block.refs_0_), channel_id=1, source_target_pairs={{0,16},{1,9},{2,18},{3,11},{4,20},{5,13},{6,22},{7,15},{8,24},{9,1... | collective-permute-start | bytes 1548296 | tf_op jit(solution)/shard_map/ppermute | solution.py:323
  10.8 1.0 %copy-done.2 = bf16[320,768]{1,0:T(8,128)(2,1)S(1)} copy-done((bf16[320,768]{1,0:T(8,128)(2,1)S(1)}, bf16[320,768]{1,0:T(8,128)(2,1)}, u32[]{:S(2)}) %copy-start.2) | copy-done | bytes 491544
  11.8 0.7 %copy-done.3 = s32[320]{0:T(512)S(1)} copy-done((s32[320]{0:T(512)S(1)}, s32[320]{0:T(512)}, u32[]{:S(2)}) %copy-start.3) | copy-done | bytes 1304
  12.5 0.7 %copy-done.4 = s32[320,1]{0,1:T(1,128)S(1)} copy-done((s32[320,1]{0,1:T(1,128)S(1)}, s32[320,1]{0,1:T(1,128)}, u32[]{:S(2)}) %copy-start.4) | copy-done | bytes 1304
  13.4 1.9 %collective-permute-start.4 = (bf16[336,768]{1,0:T(8,128)(2,1)S(1)}, bf16[336,768]{1,0:T(8,128)(2,1)S(1)}, u32[]{:S(2)}, u32[]{:S(2)}) collective-permute-start(bf16[336,768]{1,0:T(8,128)(2,1)S(1)} %shard_map.40), channel_id=1, source_target_pairs={{0,4},{6,2},{2,0},{1,7},{7,5},{5,3},{8,12},{14,10},{10,8},{9,15},{... | collective-permute-start | bytes 1548296 | tf_op jit(solution)/shard_map/ppermute | solution.py:326
  15.3 0.6 %collective-permute-start.6 = (bf16[160,768]{1,0:T(8,128)(2,1)S(1)}, bf16[160,768]{1,0:T(8,128)(2,1)S(1)}, u32[]{:S(2)}, u32[]{:S(2)}) collective-permute-start(bf16[160,768]{1,0:T(8,128)(2,1)S(1)} %collective-permute-done.5.refs_1_), channel_id=1, source_target_pairs={{0,16},{1,9},{2,18},{3,11},{4,20},{5,13},{6,22},{7,15},{8,24},{9,1... | collective-permute-start | bytes 737288 | tf_op jit(solution)/shard_map/ppermute | solution.py:327
  15.9 4.1 %collective-permute-done.7.refs_2_ = bf16[176,768]{1,0:T(8,128)(2,1)S(1)} collective-permute-done((bf16[176,768]{1,0:T(8,128)(2,1)S(1)}, bf16[176,768]{1,0:T(8,128)(2,1)S(1)}, u32[]{:S(2)}, u32[]{:S(2)}) %collective-permute-start.7) | collective-permute-done | bytes 270368 | tf_op jit(solution)/shard_map/ppermute | solution.py:322
  20.0 1.5 %collective-permute-start.8 = (bf16[176,768]{1,0:T(8,128)(2,1)S(1)}, bf16[176,768]{1,0:T(8,128)(2,1)S(1)}, u32[]{:S(2)}, u32[]{:S(2)}) collective-permute-start(bf16[176,768]{1,0:T(8,128)(2,1)S(1)} %collective-permute-done.7.refs_2_), channel_id=1, source_target_pairs={{0,16},{1,9},{2,18},{3,11},{4,20},{5,13},{6,22},{7,15},{8,24},{9,1... | collective-permute-start | bytes 811016 | tf_op jit(solution)/shard_map/ppermute | solution.py:327
  21.9 2.9 %collective-permute-done.6.refs_4_ = bf16[160,768]{1,0:T(8,128)(2,1)S(1)} collective-permute-done((bf16[160,768]{1,0:T(8,128)(2,1)S(1)}, bf16[160,768]{1,0:T(8,128)(2,1)S(1)}, u32[]{:S(2)}, u32[]{:S(2)}) %collective-permute-start.6) | collective-permute-done | bytes 245792 | tf_op jit(solution)/shard_map/ppermute | solution.py:327
  24.8 1.0 %shard_map.41 = (f32[1,640]{1,0:T(1,128)S(1)}, f32[1,320]{1,0:T(1,128)S(1)}) custom-call(bf16[336,768]{1,0:T(8,128)(2,1)S(1)} %get-tuple-element.33.block.refs_0_, bf16[336,768]{1,0:T(8,128)(2,1)S(1)} %get-tuple-element.37.partner, bf16[336,768]{1,0:T(8,128)(2,1)S(1)} %get-tuple-element.33.block.refs_0_, ...), custom_call_target="tpu_custom_call" | custom-call | flops 320 | bytes 320 | tf_op jit(solution)/shard_map/pallas_call | solution.py:224
  25.8 1.9 %collective-permute-done.8.refs_5_ = bf16[176,768]{1,0:T(8,128)(2,1)S(1)} collective-permute-done((bf16[176,768]{1,0:T(8,128)(2,1)S(1)}, bf16[176,768]{1,0:T(8,128)(2,1)S(1)}, u32[]{:S(2)}, u32[]{:S(2)}) %collective-permute-start.8) | collective-permute-done | bytes 270368 | tf_op jit(solution)/shard_map/ppermute | solution.py:327
  27.9 1.0 %shard_map.43 = (f32[1,640]{1,0:T(1,128)S(1)}, f32[1,320]{1,0:T(1,128)S(1)}) custom-call(bf16[336,768]{1,0:T(8,128)(2,1)S(1)} %get-tuple-element.33.block.refs_0_, bf16[336,768]{1,0:T(8,128)(2,1)S(1)} %get-tuple-element.37.partner, bf16[1280,768]{1,0:T(8,128)(2,1)S(1)} %get-tuple-element.44.held, f32[1,1280]{1,0:T(1,128)S(1)} %get-tuple-element.45.row), custom_call_target="tpu_custom_call" | custom-call | flops 320 | bytes 320 | tf_op jit(solution)/shard_map/pallas_call | solution.py:240
  28.9 0.5 %collective-permute-start.12 = (bf16[336,768]{1,0:T(8,128)(2,1)S(1)}, bf16[336,768]{1,0:T(8,128)(2,1)S(1)}, u32[]{:S(2)}, u32[]{:S(2)}) collective-permute-start(bf16[336,768]{1,0:T(8,128)(2,1)S(1)} %collective-permute-done.4.second), channel_id=1, source_target_pairs={{0,1},{1,0},{2,3},{3,2},{4,5},{5,4},{6,7},{7,6},{8,9},{9,8},{10,11... | collective-permute-start | bytes 1548296 | tf_op jit(solution)/shard_map/ppermute | solution.py:347
  29.4 2.2 %shard_map.44 = (f32[1,1280]{1,0:T(1,128)S(1)}, f32[1,640]{1,0:T(1,128)S(1)}) custom-call(bf16[320,768]{1,0:T(8,128)(2,1)S(1)} %get-tuple-element.32.first, bf16[336,768]{1,0:T(8,128)(2,1)S(1)} %collective-permute-done.4.second, bf16[1280,768]{1,0:T(8,128)(2,1)S(1)} %get-tuple-element.44.held, f32[1,1280]{1,0:T(1,128)S(1)} %get-tuple-element.45.row, ...), custom_call_target="tpu_custom_call" | custom-call | flops 320 | bytes 320 | tf_op jit(solution)/shard_map/pallas_call | solution.py:254
  31.6 2.2 %shard_map.45 = (f32[1,320]{1,0:T(1,128)S(1)}, f32[1,640]{1,0:T(1,128)S(1)}, f32[1,320]{1,0:T(1,128)S(1)}, f32[1,640]{1,0:T(1,128)S(1)}) custom-call(bf16[320,768]{1,0:T(8,128)(2,1)S(1)} %copy-done.1, bf16[336,768]{1,0:T(8,128)(2,1)S(1)} %collective-permute-done.12.second, bf16[1280,768]{1,0:T(8,128)(2,1)S(1)} %get-tuple-element.44.held, ...), custom_call_target="tpu_custom_call" | custom-call | flops 320 | bytes 320 | tf_op jit(solution)/shard_map/pallas_call | solution.py:254
  33.9 1.6 %collective-permute-start.16 = (f32[1,640]{1,0:T(1,128)S(1)}, f32[1,640]{1,0:T(1,128)S(1)}, u32[]{:S(2)}, u32[]{:S(2)}) collective-permute-start(f32[1,640]{1,0:T(1,128)S(1)} %get-tuple-element.55), channel_id=1, source_target_pairs={{0,8},{1,17},{2,10},{3,19},{4,12},{5,21},{6,14},{7,23},{8,0},{9,25... | collective-permute-start | bytes 7688 | tf_op jit(solution)/shard_map/ppermute | solution.py:369
  35.4 4.2 %collective-permute-start.14 = (f32[1,640]{1,0:T(1,128)S(1)}, f32[1,640]{1,0:T(1,128)S(1)}, u32[]{:S(2)}, u32[]{:S(2)}) collective-permute-start(f32[1,640]{1,0:T(1,128)S(1)} %max.24), channel_id=1, source_target_pairs={{4,0},{2,6},{0,2},{7,1},{5,7},{3,5},{12,8},{10,14},{8,10},{15,9},{... | collective-permute-start | bytes 7688 | tf_op jit(solution)/shard_map/ppermute | solution.py:364
  39.7 0.9 %collective-permute-start.18 = (f32[1,320]{1,0:T(1,128)S(1)}, f32[1,320]{1,0:T(1,128)S(1)}, u32[]{:S(2)}, u32[]{:S(2)}) collective-permute-start(f32[1,320]{1,0:T(1,128)S(1)} %get-tuple-element.60), channel_id=1, source_target_pairs={{0,1},{1,0},{2,3},{3,2},{4,5},{5,4},{6,7},{7,6},{8,9},{9,8},{10,11... | collective-permute-start | bytes 3848 | tf_op jit(solution)/shard_map/ppermute | solution.py:374
  40.7 1.1 %collective-permute-done.14 = f32[1,640]{1,0:T(1,128)S(1)} collective-permute-done((f32[1,640]{1,0:T(1,128)S(1)}, f32[1,640]{1,0:T(1,128)S(1)}, u32[]{:S(2)}, u32[]{:S(2)}) %collective-permute-start.14) | collective-permute-done | bytes 2592 | tf_op jit(solution)/shard_map/ppermute | solution.py:364
  43.1 0.6 %fusion.2 = f32[320]{0:T(512)} fusion(f32[1,320]{1,0:T(1,128)S(1)} %collective-permute-done.18, f32[1,320]{1,0:T(1,128)S(1)} %collective-permute-done.17, f32[1,320]{1,0:T(1,128)S(1)} %collective-permute-done.15, f32[1,640]{1,0:T(1,128)S(1)} %broadcast_select_fusion), kind=kLoop, calls=%fused_computation.6 | loop fusion | flops 960 | bytes 6400 | tf_op jit(solution)/shard_map/max | solution.py:375
  (38 shorter events, 3.2 us)
Async XLA Ops:
  0.0 6.5 %collective-permute-start.1 = (bf16[320,768]{1,0:T(8,128)(2,1)}, bf16[320,768]{1,0:T(8,128)(2,1)S(1)}, u32[]{:S(2)}, u32[]{:S(2)}) collective-permute-start(bf16[320,768]{1,0:T(8,128)(2,1)} %embeddings.1), channel_id=1, source_target_pairs={{0,1},{1,0},{2,3},{3,2},{4,5},{5,4},{6,7},{7,6},{8,9},{9,8},{10,11... | collective-permute-start | bytes 1474568 | tf_op jit(solution)/shard_map/ppermute | solution.py:320
  0.5 6.0 %collective-permute-start.2 = (s32[1,320]{1,0:T(1,128)}, s32[1,320]{1,0:T(1,128)S(1)}, u32[]{:S(2)}, u32[]{:S(2)}) collective-permute-start(s32[1,320]{1,0:T(1,128)} %bitcast.1), channel_id=1, source_target_pairs={{0,1},{1,0},{2,3},{3,2},{4,5},{5,4},{6,7},{7,6},{8,9},{9,8},{10,11... | collective-permute-start | bytes 3848 | tf_op jit(solution)/shard_map/ppermute | solution.py:320
  0.5 6.0 %collective-permute-start.3 = (s32[320]{0:T(512)}, s32[320]{0:T(512)S(1)}, u32[]{:S(2)}, u32[]{:S(2)}) collective-permute-start(s32[320]{0:T(512)} %order_key.1), channel_id=1, source_target_pairs={{0,1},{1,0},{2,3},{3,2},{4,5},{5,4},{6,7},{7,6},{8,9},{9,8},{10,11... | collective-permute-start | bytes 3848 | tf_op jit(solution)/shard_map/ppermute | solution.py:320
  1.0 20.6 %collective-permute-start = (bf16[320,768]{1,0:T(8,128)(2,1)}, bf16[320,768]{1,0:T(8,128)(2,1)S(1)}, u32[]{:S(2)}, u32[]{:S(2)}) collective-permute-start(bf16[320,768]{1,0:T(8,128)(2,1)} %embeddings.1), channel_id=1, source_target_pairs={{0,4},{6,2},{2,0},{1,7},{7,5},{5,3},{8,12},{14,10},{10,8},{9,15},{... | collective-permute-start | bytes 1474568 | tf_op jit(solution)/shard_map/ppermute | solution.py:319
  7.2 8.1 %collective-permute-start.5 = (bf16[160,768]{1,0:T(8,128)(2,1)S(1)}, bf16[160,768]{1,0:T(8,128)(2,1)S(1)}, u32[]{:S(2)}, u32[]{:S(2)}) collective-permute-start(bf16[160,768]{1,0:T(8,128)(2,1)S(1)} %get-tuple-element.35), channel_id=1, source_target_pairs={{0,8},{1,17},{2,10},{3,19},{4,12},{5,21},{6,14},{7,23},{8,0},{9,25... | collective-permute-start | bytes 737288 | tf_op jit(solution)/shard_map/ppermute | solution.py:322
  8.7 11.3 %collective-permute-start.7 = (bf16[176,768]{1,0:T(8,128)(2,1)S(1)}, bf16[176,768]{1,0:T(8,128)(2,1)S(1)}, u32[]{:S(2)}, u32[]{:S(2)}) collective-permute-start(bf16[176,768]{1,0:T(8,128)(2,1)S(1)} %get-tuple-element.36), channel_id=1, source_target_pairs={{0,8},{1,17},{2,10},{3,19},{4,12},{5,21},{6,14},{7,23},{8,0},{9,25... | collective-permute-start | bytes 811016 | tf_op jit(solution)/shard_map/ppermute | solution.py:322
  9.2 18.4 %collective-permute-start.9 = (bf16[336,768]{1,0:T(8,128)(2,1)S(1)}, bf16[336,768]{1,0:T(8,128)(2,1)S(1)}, u32[]{:S(2)}, u32[]{:S(2)}) collective-permute-start(bf16[336,768]{1,0:T(8,128)(2,1)S(1)} %get-tuple-element.33.block.refs_0_), channel_id=1, source_target_pairs={{0,16},{1,9},{2,18},{3,11},{4,20},{5,13},{6,22},{7,15},{8,24},{9,1... | collective-permute-start | bytes 1548296 | tf_op jit(solution)/shard_map/ppermute | solution.py:323
  10.8 1.0 %copy-start.2 = (bf16[320,768]{1,0:T(8,128)(2,1)S(1)}, bf16[320,768]{1,0:T(8,128)(2,1)}, u32[]{:S(2)}) copy-start(bf16[320,768]{1,0:T(8,128)(2,1)} %embeddings.1) | copy-start | bytes 1474564
  11.8 0.7 %copy-start.3 = (s32[320]{0:T(512)S(1)}, s32[320]{0:T(512)}, u32[]{:S(2)}) copy-start(s32[320]{0:T(512)} %order_key.1) | copy-start | bytes 3844
  12.5 0.7 %copy-start.4 = (s32[320,1]{0,1:T(1,128)S(1)}, s32[320,1]{0,1:T(1,128)}, u32[]{:S(2)}) copy-start(s32[320,1]{0,1:T(1,128)} %param.4) | copy-start | bytes 3844
  13.4 15.5 %collective-permute-start.4 = (bf16[336,768]{1,0:T(8,128)(2,1)S(1)}, bf16[336,768]{1,0:T(8,128)(2,1)S(1)}, u32[]{:S(2)}, u32[]{:S(2)}) collective-permute-start(bf16[336,768]{1,0:T(8,128)(2,1)S(1)} %shard_map.40), channel_id=1, source_target_pairs={{0,4},{6,2},{2,0},{1,7},{7,5},{5,3},{8,12},{14,10},{10,8},{9,15},{... | collective-permute-start | bytes 1548296 | tf_op jit(solution)/shard_map/ppermute | solution.py:326
  15.3 9.4 %collective-permute-start.6 = (bf16[160,768]{1,0:T(8,128)(2,1)S(1)}, bf16[160,768]{1,0:T(8,128)(2,1)S(1)}, u32[]{:S(2)}, u32[]{:S(2)}) collective-permute-start(bf16[160,768]{1,0:T(8,128)(2,1)S(1)} %collective-permute-done.5.refs_1_), channel_id=1, source_target_pairs={{0,16},{1,9},{2,18},{3,11},{4,20},{5,13},{6,22},{7,15},{8,24},{9,1... | collective-permute-start | bytes 737288 | tf_op jit(solution)/shard_map/ppermute | solution.py:327
  20.0 7.7 %collective-permute-start.8 = (bf16[176,768]{1,0:T(8,128)(2,1)S(1)}, bf16[176,768]{1,0:T(8,128)(2,1)S(1)}, u32[]{:S(2)}, u32[]{:S(2)}) collective-permute-start(bf16[176,768]{1,0:T(8,128)(2,1)S(1)} %collective-permute-done.7.refs_2_), channel_id=1, source_target_pairs={{0,16},{1,9},{2,18},{3,11},{4,20},{5,13},{6,22},{7,15},{8,24},{9,1... | collective-permute-start | bytes 811016 | tf_op jit(solution)/shard_map/ppermute | solution.py:327
  21.7 6.0 %collective-permute-start.10 = (bf16[160,768]{1,0:T(8,128)(2,1)S(1)}, bf16[160,768]{1,0:T(8,128)(2,1)S(1)}, u32[]{:S(2)}, u32[]{:S(2)}) collective-permute-start(bf16[160,768]{1,0:T(8,128)(2,1)S(1)} %get-tuple-element.42), channel_id=1, source_target_pairs={{0,1},{1,0},{2,3},{3,2},{4,5},{5,4},{6,7},{7,6},{8,9},{9,8},{10,11... | collective-permute-start | bytes 737288 | tf_op jit(solution)/shard_map/ppermute | solution.py:332
  24.8 2.9 %collective-permute-start.11 = (bf16[160,768]{1,0:T(8,128)(2,1)S(1)}, bf16[160,768]{1,0:T(8,128)(2,1)S(1)}, u32[]{:S(2)}, u32[]{:S(2)}) collective-permute-start(bf16[160,768]{1,0:T(8,128)(2,1)S(1)} %get-tuple-element.43), channel_id=1, source_target_pairs={{0,1},{1,0},{2,3},{3,2},{4,5},{5,4},{6,7},{7,6},{8,9},{9,8},{10,11... | collective-permute-start | bytes 737288 | tf_op jit(solution)/shard_map/ppermute | solution.py:332
  27.9 1.0 %copy-start = (bf16[320,768]{1,0:T(8,128)(2,1)}, bf16[320,768]{1,0:T(8,128)(2,1)S(1)}, u32[]{:S(2)}) copy-start(bf16[320,768]{1,0:T(8,128)(2,1)S(1)} %get-tuple-element.51.first) | copy-start | bytes 1474564
  28.9 2.7 %collective-permute-start.12 = (bf16[336,768]{1,0:T(8,128)(2,1)S(1)}, bf16[336,768]{1,0:T(8,128)(2,1)S(1)}, u32[]{:S(2)}, u32[]{:S(2)}) collective-permute-start(bf16[336,768]{1,0:T(8,128)(2,1)S(1)} %collective-permute-done.4.second), channel_id=1, source_target_pairs={{0,1},{1,0},{2,3},{3,2},{4,5},{5,4},{6,7},{7,6},{8,9},{9,8},{10,11... | collective-permute-start | bytes 1548296 | tf_op jit(solution)/shard_map/ppermute | solution.py:347
  29.4 2.2 %copy-start.1 = (bf16[320,768]{1,0:T(8,128)(2,1)S(1)}, bf16[320,768]{1,0:T(8,128)(2,1)}, u32[]{:S(2)}) copy-start(bf16[320,768]{1,0:T(8,128)(2,1)} %copy-done) | copy-start | bytes 1474564
  33.8 1.6 %collective-permute-start.13 = (f32[1,640]{1,0:T(1,128)S(1)}, f32[1,640]{1,0:T(1,128)S(1)}, u32[]{:S(2)}, u32[]{:S(2)}) collective-permute-start(f32[1,640]{1,0:T(1,128)S(1)} %get-tuple-element.53), channel_id=1, source_target_pairs={{0,1},{1,0},{2,3},{3,2},{4,5},{5,4},{6,7},{7,6},{8,9},{9,8},{10,11... | collective-permute-start | bytes 7688 | tf_op jit(solution)/shard_map/ppermute | solution.py:361
  33.9 5.8 %collective-permute-start.16 = (f32[1,640]{1,0:T(1,128)S(1)}, f32[1,640]{1,0:T(1,128)S(1)}, u32[]{:S(2)}, u32[]{:S(2)}) collective-permute-start(f32[1,640]{1,0:T(1,128)S(1)} %get-tuple-element.55), channel_id=1, source_target_pairs={{0,8},{1,17},{2,10},{3,19},{4,12},{5,21},{6,14},{7,23},{8,0},{9,25... | collective-permute-start | bytes 7688 | tf_op jit(solution)/shard_map/ppermute | solution.py:369
  35.4 6.4 %collective-permute-start.14 = (f32[1,640]{1,0:T(1,128)S(1)}, f32[1,640]{1,0:T(1,128)S(1)}, u32[]{:S(2)}, u32[]{:S(2)}) collective-permute-start(f32[1,640]{1,0:T(1,128)S(1)} %max.24), channel_id=1, source_target_pairs={{4,0},{2,6},{0,2},{7,1},{5,7},{3,5},{12,8},{10,14},{8,10},{15,9},{... | collective-permute-start | bytes 7688 | tf_op jit(solution)/shard_map/ppermute | solution.py:364
  39.7 3.0 %collective-permute-start.17 = (f32[1,320]{1,0:T(1,128)S(1)}, f32[1,320]{1,0:T(1,128)S(1)}, u32[]{:S(2)}, u32[]{:S(2)}) collective-permute-start(f32[1,320]{1,0:T(1,128)S(1)} %get-tuple-element.59), channel_id=1, source_target_pairs={{0,17},{1,8},{2,19},{3,10},{4,21},{5,12},{6,23},{7,14},{8,25},{9,0... | collective-permute-start | bytes 3848 | tf_op jit(solution)/shard_map/ppermute | solution.py:372
  39.7 3.0 %collective-permute-start.18 = (f32[1,320]{1,0:T(1,128)S(1)}, f32[1,320]{1,0:T(1,128)S(1)}, u32[]{:S(2)}, u32[]{:S(2)}) collective-permute-start(f32[1,320]{1,0:T(1,128)S(1)} %get-tuple-element.60), channel_id=1, source_target_pairs={{0,1},{1,0},{2,3},{3,2},{4,5},{5,4},{6,7},{7,6},{8,9},{9,8},{10,11... | collective-permute-start | bytes 3848 | tf_op jit(solution)/shard_map/ppermute | solution.py:374
  41.9 1.2 %collective-permute-start.15 = (f32[1,320]{1,0:T(1,128)S(1)}, f32[1,320]{1,0:T(1,128)S(1)}, u32[]{:S(2)}, u32[]{:S(2)}) collective-permute-start(f32[1,320]{1,0:T(1,128)S(1)} %slice.17), channel_id=1, source_target_pairs={{0,1},{1,0},{2,3},{3,2},{4,5},{5,4},{6,7},{7,6},{8,9},{9,8},{10,11... | collective-permute-start | bytes 3848 | tf_op jit(solution)/shard_map/ppermute | solution.py:368

commit v22 on v19

--- a/solution.py
+++ b/solution.py
@@ -207,15 +207,27 @@
 
 def line_kernel(rows, span, together, count, first, second, held, row, *refs):
     bests, outs, (found, units) = refs[:count], refs[count:-2], refs[-2:]
-    pair(units, first, second, rows)
     parts = [(codes(second, rows, span, first=place), TWO) for place in (CODES, 0)]
-    mine, theirs = meet(units, parts, rows, span, held, row[...])
-    found[...] = jnp.concatenate(mine, axis=1)
-    best = jnp.maximum(jnp.concatenate([best[...] for best in bests], axis=1), theirs)
-    for out, places in zip(outs, together):
-        out[...] = jnp.concatenate(
-            [best[:, place * rows : (place + 1) * rows] for place in places], axis=1
-        )
+
+    def give(best):
+        for out, places in zip(outs, together):
+            out[...] = jnp.concatenate(
+                [best[:, place * rows : (place + 1) * rows] for place in places], axis=1
+            )
+
+    arrived = jnp.max(parts[0][0]) > 0.0
+
+    @pl.when(arrived)
+    def _():
+        pair(units, first, second, rows)
+        mine, theirs = meet(units, parts, rows, span, held, row[...])
+        found[...] = jnp.concatenate(mine, axis=1)
+        give(jnp.maximum(jnp.concatenate([best[...] for best in bests], axis=1), theirs))
+
+    @pl.when(jnp.logical_not(arrived))
+    def _():
+        found[...] = jnp.full(found.shape, -1.0, jnp.float32)
+        give(jnp.concatenate([best[...] for best in bests], axis=1))
 
 
 def plane(block, partner, holds, rows, span):

time: 44.2 us -> 43.7 us (0.989)
  Pallas kernels: 7.35 us -> 5.59 us
  waiting for transfers between devices: 12 us -> 13.7 us
    pallas_call x2, Pallas kernels: 4.06 us -> 2.3 us  [line(): pl.pallas_call(functools.partial(line_kernel, rows, span, together, len(b...]
    ppermute x1, waiting for transfers between devices: 0.01 us -> 1.7 us  [shards(): second_far = lax.ppermute(second_near, BOTH, other_core)]
  transfers between devices with their start and end apart: 19 -> 19, of which waited for: 5 -> 6; matrix products, arithmetic and copies ran while one was open for 0% -> 0% of each run, Pallas kernels for 12% -> 8%
where the time goes in v22:
time: 43.7 us; the launch traced here: 43.5 us
  starting transfers between devices  20.8 us (48%)
  waiting for transfers between devices  13.7 us (31%)
  Pallas kernels  5.59 us (13%)
  local copies, waits for them, and re-layouts  2.47 us (6%)
  other arithmetic  0.68 us (2%)
    ppermute x1, starting transfers between devices, shards(): raw = [lax.ppermute(embeddings, BOTH, pairs) for pairs in rounds]  5.51 us
    ppermute x2, waiting for transfers between devices, shards(): from_first = [lax.ppermute(part, BOTH, first) for part in parts]  4.28 us
    ppermute x1, starting transfers between devices, shards(): near_other = [lax.ppermute(both, BOTH, pairs) for pairs in rounds]  3.49 us
    ppermute x2, waiting for transfers between devices, shards(): from_corner = [lax.ppermute(part, BOTH, second) for part in from_first]  3.17 us
    ppermute x1, waiting for transfers between devices, shards(): lax.ppermute(kept[:, 2 * at * rows:2 * (at + 1) * rows], BOTH, back(pairs))  2.6 us
    unnamed x10, local copies, waits for them, and re-layouts  2.4 us
    pallas_call x2, Pallas kernels, line(): pl.pallas_call(functools.partial(line_kernel, rows, span, together, len(b...  2.3 us
    ppermute x2, starting transfers between devices, shards(): from_corner = [lax.ppermute(part, BOTH, second) for part in from_first]  2.19 us
  transfers between devices with their start and end apart: 19, of which 6 were waited for; matrix products, arithmetic and copies ran while one was open for 0% of the time, Pallas kernels for 8%

profile of v22, /device:TPU:0, one launch (start us, length us, event | category | flops | bytes accessed | tf_op | source)
XLA Modules:
  0.0 43.5 jit_solution(162303502762520534)
XLA Ops:
  1.0 5.5 %collective-permute-start = (bf16[320,768]{1,0:T(8,128)(2,1)}, bf16[320,768]{1,0:T(8,128)(2,1)S(1)}, u32[]{:S(2)}, u32[]{:S(2)}) collective-permute-start(bf16[320,768]{1,0:T(8,128)(2,1)} %embeddings.1), channel_id=1, source_target_pairs={{6,2},{0,4},{4,6},{7,1},{1,3},{3,5},{14,10},{8,12},{12,14},{15,9},... | collective-permute-start | bytes 1474568 | tf_op jit(solution)/shard_map/ppermute | solution.py:331
  6.5 0.7 %shard_map.38 = (bf16[336,768]{1,0:T(8,128)(2,1)S(1)}, bf16[16,768]{1,0:T(8,128)(2,1)}, bf16[160,768]{1,0:T(8,128)(2,1)S(1)}, bf16[176,768]{1,0:T(8,128)(2,1)S(1)}) custom-call(bf16[320,768]{1,0:T(8,128)(2,1)S(1)} %collective-permute-done.1.embeddings, s32[1,320]{1,0:T(1,128)S(1)} %collective-permute-done.2.cluster, s32[320]{0:T(512)S(1)} %collective-permute-done.3.order_key), custom_call_target="tpu_custom_call" | custom-call | flops 320 | bytes 320 | tf_op jit(solution)/shard_map/pallas_call | solution.py:73
  7.2 1.5 %collective-permute-start.5 = (bf16[160,768]{1,0:T(8,128)(2,1)S(1)}, bf16[160,768]{1,0:T(8,128)(2,1)S(1)}, u32[]{:S(2)}, u32[]{:S(2)}) collective-permute-start(bf16[160,768]{1,0:T(8,128)(2,1)S(1)} %get-tuple-element.35), channel_id=1, source_target_pairs={{0,8},{1,17},{2,10},{3,19},{4,12},{5,21},{6,14},{7,23},{8,0},{9,25... | collective-permute-start | bytes 737288 | tf_op jit(solution)/shard_map/ppermute | solution.py:334
  8.7 0.5 %collective-permute-start.7 = (bf16[176,768]{1,0:T(8,128)(2,1)S(1)}, bf16[176,768]{1,0:T(8,128)(2,1)S(1)}, u32[]{:S(2)}, u32[]{:S(2)}) collective-permute-start(bf16[176,768]{1,0:T(8,128)(2,1)S(1)} %get-tuple-element.36), channel_id=1, source_target_pairs={{0,8},{1,17},{2,10},{3,19},{4,12},{5,21},{6,14},{7,23},{8,0},{9,25... | collective-permute-start | bytes 811016 | tf_op jit(solution)/shard_map/ppermute | solution.py:334
  9.3 1.5 %collective-permute-start.9 = (bf16[336,768]{1,0:T(8,128)(2,1)S(1)}, bf16[336,768]{1,0:T(8,128)(2,1)S(1)}, u32[]{:S(2)}, u32[]{:S(2)}) collective-permute-start(bf16[336,768]{1,0:T(8,128)(2,1)S(1)} %get-tuple-element.33.block.refs_0_), channel_id=1, source_target_pairs={{0,16},{1,9},{2,18},{3,11},{4,20},{5,13},{6,22},{7,15},{8,24},{9,1... | collective-permute-start | bytes 1548296 | tf_op jit(solution)/shard_map/ppermute | solution.py:335
  10.8 1.0 %copy-done.2 = bf16[320,768]{1,0:T(8,128)(2,1)S(1)} copy-done((bf16[320,768]{1,0:T(8,128)(2,1)S(1)}, bf16[320,768]{1,0:T(8,128)(2,1)}, u32[]{:S(2)}) %copy-start.2) | copy-done | bytes 491544
  11.8 0.7 %copy-done.3 = s32[320]{0:T(512)S(1)} copy-done((s32[320]{0:T(512)S(1)}, s32[320]{0:T(512)}, u32[]{:S(2)}) %copy-start.3) | copy-done | bytes 1304
  12.5 0.7 %copy-done.4 = s32[320,1]{0,1:T(1,128)S(1)} copy-done((s32[320,1]{0,1:T(1,128)S(1)}, s32[320,1]{0,1:T(1,128)}, u32[]{:S(2)}) %copy-start.4) | copy-done | bytes 1304
  13.4 3.5 %collective-permute-start.4 = (bf16[336,768]{1,0:T(8,128)(2,1)S(1)}, bf16[336,768]{1,0:T(8,128)(2,1)S(1)}, u32[]{:S(2)}, u32[]{:S(2)}) collective-permute-start(bf16[336,768]{1,0:T(8,128)(2,1)S(1)} %shard_map.40), channel_id=1, source_target_pairs={{6,2},{0,4},{4,6},{7,1},{1,3},{3,5},{14,10},{8,12},{12,14},{15,9},... | collective-permute-start | bytes 1548296 | tf_op jit(solution)/shard_map/ppermute | solution.py:338
  16.9 0.7 %collective-permute-start.6 = (bf16[160,768]{1,0:T(8,128)(2,1)S(1)}, bf16[160,768]{1,0:T(8,128)(2,1)S(1)}, u32[]{:S(2)}, u32[]{:S(2)}) collective-permute-start(bf16[160,768]{1,0:T(8,128)(2,1)S(1)} %collective-permute-done.5.refs_1_), channel_id=1, source_target_pairs={{0,16},{1,9},{2,18},{3,11},{4,20},{5,13},{6,22},{7,15},{8,24},{9,1... | collective-permute-start | bytes 737288 | tf_op jit(solution)/shard_map/ppermute | solution.py:339
  17.6 4.3 %collective-permute-done.7.refs_2_ = bf16[176,768]{1,0:T(8,128)(2,1)S(1)} collective-permute-done((bf16[176,768]{1,0:T(8,128)(2,1)S(1)}, bf16[176,768]{1,0:T(8,128)(2,1)S(1)}, u32[]{:S(2)}, u32[]{:S(2)}) %collective-permute-start.7) | collective-permute-done | bytes 270368 | tf_op jit(solution)/shard_map/ppermute | solution.py:334
  21.9 1.5 %collective-permute-start.8 = (bf16[176,768]{1,0:T(8,128)(2,1)S(1)}, bf16[176,768]{1,0:T(8,128)(2,1)S(1)}, u32[]{:S(2)}, u32[]{:S(2)}) collective-permute-start(bf16[176,768]{1,0:T(8,128)(2,1)S(1)} %collective-permute-done.7.refs_2_), channel_id=1, source_target_pairs={{0,16},{1,9},{2,18},{3,11},{4,20},{5,13},{6,22},{7,15},{8,24},{9,1... | collective-permute-start | bytes 811016 | tf_op jit(solution)/shard_map/ppermute | solution.py:339
  24.2 1.0 %shard_map.41 = (f32[1,640]{1,0:T(1,128)S(1)}, f32[1,320]{1,0:T(1,128)S(1)}) custom-call(bf16[336,768]{1,0:T(8,128)(2,1)S(1)} %get-tuple-element.33.block.refs_0_, bf16[336,768]{1,0:T(8,128)(2,1)S(1)} %get-tuple-element.37.partner, bf16[336,768]{1,0:T(8,128)(2,1)S(1)} %get-tuple-element.33.block.refs_0_, ...), custom_call_target="tpu_custom_call" | custom-call | flops 320 | bytes 320 | tf_op jit(solution)/shard_map/pallas_call | solution.py:236
  25.2 3.2 %collective-permute-done.8.refs_5_ = bf16[176,768]{1,0:T(8,128)(2,1)S(1)} collective-permute-done((bf16[176,768]{1,0:T(8,128)(2,1)S(1)}, bf16[176,768]{1,0:T(8,128)(2,1)S(1)}, u32[]{:S(2)}, u32[]{:S(2)}) %collective-permute-start.8) | collective-permute-done | bytes 270368 | tf_op jit(solution)/shard_map/ppermute | solution.py:339
  28.5 1.0 %shard_map.43 = (f32[1,640]{1,0:T(1,128)S(1)}, f32[1,320]{1,0:T(1,128)S(1)}) custom-call(bf16[336,768]{1,0:T(8,128)(2,1)S(1)} %get-tuple-element.33.block.refs_0_, bf16[336,768]{1,0:T(8,128)(2,1)S(1)} %get-tuple-element.37.partner, bf16[1280,768]{1,0:T(8,128)(2,1)S(1)} %get-tuple-element.44.held, f32[1,1280]{1,0:T(1,128)S(1)} %get-tuple-element.45.row), custom_call_target="tpu_custom_call" | custom-call | flops 320 | bytes 320 | tf_op jit(solution)/shard_map/pallas_call | solution.py:252
  29.8 1.7 %collective-permute-done.12.second = bf16[336,768]{1,0:T(8,128)(2,1)S(1)} collective-permute-done((bf16[336,768]{1,0:T(8,128)(2,1)S(1)}, bf16[336,768]{1,0:T(8,128)(2,1)S(1)}, u32[]{:S(2)}, u32[]{:S(2)}) %collective-permute-start.12) | collective-permute-done | bytes 516128 | tf_op jit(solution)/shard_map/ppermute | solution.py:359
  31.5 2.2 %shard_map.45 = (f32[1,320]{1,0:T(1,128)S(1)}, f32[1,640]{1,0:T(1,128)S(1)}, f32[1,320]{1,0:T(1,128)S(1)}, f32[1,640]{1,0:T(1,128)S(1)}) custom-call(bf16[320,768]{1,0:T(8,128)(2,1)S(1)} %copy-done.1, bf16[336,768]{1,0:T(8,128)(2,1)S(1)} %collective-permute-done.12.second, bf16[1280,768]{1,0:T(8,128)(2,1)S(1)} %get-tuple-element.44.held, ...), custom_call_target="tpu_custom_call" | custom-call | flops 320 | bytes 320 | tf_op jit(solution)/shard_map/pallas_call | solution.py:266
  33.7 1.6 %collective-permute-start.16 = (f32[1,640]{1,0:T(1,128)S(1)}, f32[1,640]{1,0:T(1,128)S(1)}, u32[]{:S(2)}, u32[]{:S(2)}) collective-permute-start(f32[1,640]{1,0:T(1,128)S(1)} %get-tuple-element.55), channel_id=1, source_target_pairs={{0,8},{1,17},{2,10},{3,19},{4,12},{5,21},{6,14},{7,23},{8,0},{9,25... | collective-permute-start | bytes 7688 | tf_op jit(solution)/shard_map/ppermute | solution.py:381
  35.3 1.3 %collective-permute-start.14 = (f32[1,640]{1,0:T(1,128)S(1)}, f32[1,640]{1,0:T(1,128)S(1)}, u32[]{:S(2)}, u32[]{:S(2)}) collective-permute-start(f32[1,640]{1,0:T(1,128)S(1)} %max.24), channel_id=1, source_target_pairs={{2,6},{4,0},{6,4},{1,7},{3,1},{5,3},{10,14},{12,8},{14,12},{9,15},... | collective-permute-start | bytes 7688 | tf_op jit(solution)/shard_map/ppermute | solution.py:376
  36.6 0.8 %collective-permute-done.16 = f32[1,640]{1,0:T(1,128)S(1)} collective-permute-done((f32[1,640]{1,0:T(1,128)S(1)}, f32[1,640]{1,0:T(1,128)S(1)}, u32[]{:S(2)}, u32[]{:S(2)}) %collective-permute-start.16) | collective-permute-done | bytes 2592 | tf_op jit(solution)/shard_map/ppermute | solution.py:381
  37.5 1.1 %collective-permute-start.17 = (f32[1,320]{1,0:T(1,128)S(1)}, f32[1,320]{1,0:T(1,128)S(1)}, u32[]{:S(2)}, u32[]{:S(2)}) collective-permute-start(f32[1,320]{1,0:T(1,128)S(1)} %get-tuple-element.59), channel_id=1, source_target_pairs={{0,17},{1,8},{2,19},{3,10},{4,21},{5,12},{6,23},{7,14},{8,25},{9,0... | collective-permute-start | bytes 3848 | tf_op jit(solution)/shard_map/ppermute | solution.py:384
  39.1 2.6 %collective-permute-done.14 = f32[1,640]{1,0:T(1,128)S(1)} collective-permute-done((f32[1,640]{1,0:T(1,128)S(1)}, f32[1,640]{1,0:T(1,128)S(1)}, u32[]{:S(2)}, u32[]{:S(2)}) %collective-permute-start.14) | collective-permute-done | bytes 2592 | tf_op jit(solution)/shard_map/ppermute | solution.py:376
  41.8 1.1 %collective-permute-done.15 = f32[1,320]{1,0:T(1,128)S(1)} collective-permute-done((f32[1,320]{1,0:T(1,128)S(1)}, f32[1,320]{1,0:T(1,128)S(1)}, u32[]{:S(2)}, u32[]{:S(2)}) %collective-permute-start.15) | collective-permute-done | bytes 1312 | tf_op jit(solution)/shard_map/ppermute | solution.py:380
  42.9 0.6 %fusion.2 = f32[320]{0:T(512)} fusion(f32[1,320]{1,0:T(1,128)S(1)} %collective-permute-done.18, f32[1,320]{1,0:T(1,128)S(1)} %collective-permute-done.17, f32[1,320]{1,0:T(1,128)S(1)} %collective-permute-done.15, f32[1,640]{1,0:T(1,128)S(1)} %broadcast_select_fusion), kind=kLoop, calls=%fused_computation.6 | loop fusion | flops 960 | bytes 6400 | tf_op jit(solution)/shard_map/max | solution.py:387
  (38 shorter events, 3.0 us)
Async XLA Ops:
  0.0 6.5 %collective-permute-start.1 = (bf16[320,768]{1,0:T(8,128)(2,1)}, bf16[320,768]{1,0:T(8,128)(2,1)S(1)}, u32[]{:S(2)}, u32[]{:S(2)}) collective-permute-start(bf16[320,768]{1,0:T(8,128)(2,1)} %embeddings.1), channel_id=1, source_target_pairs={{0,1},{1,0},{2,3},{3,2},{4,5},{5,4},{6,7},{7,6},{8,9},{9,8},{10,11... | collective-permute-start | bytes 1474568 | tf_op jit(solution)/shard_map/ppermute | solution.py:332
  0.5 6.0 %collective-permute-start.2 = (s32[1,320]{1,0:T(1,128)}, s32[1,320]{1,0:T(1,128)S(1)}, u32[]{:S(2)}, u32[]{:S(2)}) collective-permute-start(s32[1,320]{1,0:T(1,128)} %bitcast.1), channel_id=1, source_target_pairs={{0,1},{1,0},{2,3},{3,2},{4,5},{5,4},{6,7},{7,6},{8,9},{9,8},{10,11... | collective-permute-start | bytes 3848 | tf_op jit(solution)/shard_map/ppermute | solution.py:332
  0.5 6.0 %collective-permute-start.3 = (s32[320]{0:T(512)}, s32[320]{0:T(512)S(1)}, u32[]{:S(2)}, u32[]{:S(2)}) collective-permute-start(s32[320]{0:T(512)} %order_key.1), channel_id=1, source_target_pairs={{0,1},{1,0},{2,3},{3,2},{4,5},{5,4},{6,7},{7,6},{8,9},{9,8},{10,11... | collective-permute-start | bytes 3848 | tf_op jit(solution)/shard_map/ppermute | solution.py:332
  1.0 22.4 %collective-permute-start = (bf16[320,768]{1,0:T(8,128)(2,1)}, bf16[320,768]{1,0:T(8,128)(2,1)S(1)}, u32[]{:S(2)}, u32[]{:S(2)}) collective-permute-start(bf16[320,768]{1,0:T(8,128)(2,1)} %embeddings.1), channel_id=1, source_target_pairs={{6,2},{0,4},{4,6},{7,1},{1,3},{3,5},{14,10},{8,12},{12,14},{15,9},... | collective-permute-start | bytes 1474568 | tf_op jit(solution)/shard_map/ppermute | solution.py:331
  7.2 9.7 %collective-permute-start.5 = (bf16[160,768]{1,0:T(8,128)(2,1)S(1)}, bf16[160,768]{1,0:T(8,128)(2,1)S(1)}, u32[]{:S(2)}, u32[]{:S(2)}) collective-permute-start(bf16[160,768]{1,0:T(8,128)(2,1)S(1)} %get-tuple-element.35), channel_id=1, source_target_pairs={{0,8},{1,17},{2,10},{3,19},{4,12},{5,21},{6,14},{7,23},{8,0},{9,25... | collective-permute-start | bytes 737288 | tf_op jit(solution)/shard_map/ppermute | solution.py:334
  8.7 13.1 %collective-permute-start.7 = (bf16[176,768]{1,0:T(8,128)(2,1)S(1)}, bf16[176,768]{1,0:T(8,128)(2,1)S(1)}, u32[]{:S(2)}, u32[]{:S(2)}) collective-permute-start(bf16[176,768]{1,0:T(8,128)(2,1)S(1)} %get-tuple-element.36), channel_id=1, source_target_pairs={{0,8},{1,17},{2,10},{3,19},{4,12},{5,21},{6,14},{7,23},{8,0},{9,25... | collective-permute-start | bytes 811016 | tf_op jit(solution)/shard_map/ppermute | solution.py:334
  9.3 19.1 %collective-permute-start.9 = (bf16[336,768]{1,0:T(8,128)(2,1)S(1)}, bf16[336,768]{1,0:T(8,128)(2,1)S(1)}, u32[]{:S(2)}, u32[]{:S(2)}) collective-permute-start(bf16[336,768]{1,0:T(8,128)(2,1)S(1)} %get-tuple-element.33.block.refs_0_), channel_id=1, source_target_pairs={{0,16},{1,9},{2,18},{3,11},{4,20},{5,13},{6,22},{7,15},{8,24},{9,1... | collective-permute-start | bytes 1548296 | tf_op jit(solution)/shard_map/ppermute | solution.py:335
  10.8 1.0 %copy-start.2 = (bf16[320,768]{1,0:T(8,128)(2,1)S(1)}, bf16[320,768]{1,0:T(8,128)(2,1)}, u32[]{:S(2)}) copy-start(bf16[320,768]{1,0:T(8,128)(2,1)} %embeddings.1) | copy-start | bytes 1474564
  11.8 0.7 %copy-start.3 = (s32[320]{0:T(512)S(1)}, s32[320]{0:T(512)}, u32[]{:S(2)}) copy-start(s32[320]{0:T(512)} %order_key.1) | copy-start | bytes 3844
  12.5 0.7 %copy-start.4 = (s32[320,1]{0,1:T(1,128)S(1)}, s32[320,1]{0,1:T(1,128)}, u32[]{:S(2)}) copy-start(s32[320,1]{0,1:T(1,128)} %param.4) | copy-start | bytes 3844
  13.4 16.1 %collective-permute-start.4 = (bf16[336,768]{1,0:T(8,128)(2,1)S(1)}, bf16[336,768]{1,0:T(8,128)(2,1)S(1)}, u32[]{:S(2)}, u32[]{:S(2)}) collective-permute-start(bf16[336,768]{1,0:T(8,128)(2,1)S(1)} %shard_map.40), channel_id=1, source_target_pairs={{6,2},{0,4},{4,6},{7,1},{1,3},{3,5},{14,10},{8,12},{12,14},{15,9},... | collective-permute-start | bytes 1548296 | tf_op jit(solution)/shard_map/ppermute | solution.py:338
  16.9 6.7 %collective-permute-start.6 = (bf16[160,768]{1,0:T(8,128)(2,1)S(1)}, bf16[160,768]{1,0:T(8,128)(2,1)S(1)}, u32[]{:S(2)}, u32[]{:S(2)}) collective-permute-start(bf16[160,768]{1,0:T(8,128)(2,1)S(1)} %collective-permute-done.5.refs_1_), channel_id=1, source_target_pairs={{0,16},{1,9},{2,18},{3,11},{4,20},{5,13},{6,22},{7,15},{8,24},{9,1... | collective-permute-start | bytes 737288 | tf_op jit(solution)/shard_map/ppermute | solution.py:339
  21.9 6.5 %collective-permute-start.8 = (bf16[176,768]{1,0:T(8,128)(2,1)S(1)}, bf16[176,768]{1,0:T(8,128)(2,1)S(1)}, u32[]{:S(2)}, u32[]{:S(2)}) collective-permute-start(bf16[176,768]{1,0:T(8,128)(2,1)S(1)} %collective-permute-done.7.refs_2_), channel_id=1, source_target_pairs={{0,16},{1,9},{2,18},{3,11},{4,20},{5,13},{6,22},{7,15},{8,24},{9,1... | collective-permute-start | bytes 811016 | tf_op jit(solution)/shard_map/ppermute | solution.py:339
  23.6 4.8 %collective-permute-start.10 = (bf16[160,768]{1,0:T(8,128)(2,1)S(1)}, bf16[160,768]{1,0:T(8,128)(2,1)S(1)}, u32[]{:S(2)}, u32[]{:S(2)}) collective-permute-start(bf16[160,768]{1,0:T(8,128)(2,1)S(1)} %get-tuple-element.42), channel_id=1, source_target_pairs={{0,1},{1,0},{2,3},{3,2},{4,5},{5,4},{6,7},{7,6},{8,9},{9,8},{10,11... | collective-permute-start | bytes 737288 | tf_op jit(solution)/shard_map/ppermute | solution.py:344
  23.7 4.7 %collective-permute-start.11 = (bf16[160,768]{1,0:T(8,128)(2,1)S(1)}, bf16[160,768]{1,0:T(8,128)(2,1)S(1)}, u32[]{:S(2)}, u32[]{:S(2)}) collective-permute-start(bf16[160,768]{1,0:T(8,128)(2,1)S(1)} %get-tuple-element.43), channel_id=1, source_target_pairs={{0,1},{1,0},{2,3},{3,2},{4,5},{5,4},{6,7},{7,6},{8,9},{9,8},{10,11... | collective-permute-start | bytes 737288 | tf_op jit(solution)/shard_map/ppermute | solution.py:344
  28.5 1.0 %copy-start = (bf16[320,768]{1,0:T(8,128)(2,1)}, bf16[320,768]{1,0:T(8,128)(2,1)S(1)}, u32[]{:S(2)}) copy-start(bf16[320,768]{1,0:T(8,128)(2,1)S(1)} %get-tuple-element.51.first) | copy-start | bytes 1474564
  29.5 2.0 %collective-permute-start.12 = (bf16[336,768]{1,0:T(8,128)(2,1)S(1)}, bf16[336,768]{1,0:T(8,128)(2,1)S(1)}, u32[]{:S(2)}, u32[]{:S(2)}) collective-permute-start(bf16[336,768]{1,0:T(8,128)(2,1)S(1)} %collective-permute-done.4.second), channel_id=1, source_target_pairs={{0,1},{1,0},{2,3},{3,2},{4,5},{5,4},{6,7},{7,6},{8,9},{9,8},{10,11... | collective-permute-start | bytes 1548296 | tf_op jit(solution)/shard_map/ppermute | solution.py:359
  29.7 1.9 %copy-start.1 = (bf16[320,768]{1,0:T(8,128)(2,1)S(1)}, bf16[320,768]{1,0:T(8,128)(2,1)}, u32[]{:S(2)}) copy-start(bf16[320,768]{1,0:T(8,128)(2,1)} %copy-done) | copy-start | bytes 1474564
  33.7 1.6 %collective-permute-start.13 = (f32[1,640]{1,0:T(1,128)S(1)}, f32[1,640]{1,0:T(1,128)S(1)}, u32[]{:S(2)}, u32[]{:S(2)}) collective-permute-start(f32[1,640]{1,0:T(1,128)S(1)} %get-tuple-element.53), channel_id=1, source_target_pairs={{0,1},{1,0},{2,3},{3,2},{4,5},{5,4},{6,7},{7,6},{8,9},{9,8},{10,11... | collective-permute-start | bytes 7688 | tf_op jit(solution)/shard_map/ppermute | solution.py:373
  33.7 3.7 %collective-permute-start.16 = (f32[1,640]{1,0:T(1,128)S(1)}, f32[1,640]{1,0:T(1,128)S(1)}, u32[]{:S(2)}, u32[]{:S(2)}) collective-permute-start(f32[1,640]{1,0:T(1,128)S(1)} %get-tuple-element.55), channel_id=1, source_target_pairs={{0,8},{1,17},{2,10},{3,19},{4,12},{5,21},{6,14},{7,23},{8,0},{9,25... | collective-permute-start | bytes 7688 | tf_op jit(solution)/shard_map/ppermute | solution.py:381
  35.3 6.4 %collective-permute-start.14 = (f32[1,640]{1,0:T(1,128)S(1)}, f32[1,640]{1,0:T(1,128)S(1)}, u32[]{:S(2)}, u32[]{:S(2)}) collective-permute-start(f32[1,640]{1,0:T(1,128)S(1)} %max.24), channel_id=1, source_target_pairs={{2,6},{4,0},{6,4},{1,7},{3,1},{5,3},{10,14},{12,8},{14,12},{9,15},... | collective-permute-start | bytes 7688 | tf_op jit(solution)/shard_map/ppermute | solution.py:376
  37.5 4.3 %collective-permute-start.17 = (f32[1,320]{1,0:T(1,128)S(1)}, f32[1,320]{1,0:T(1,128)S(1)}, u32[]{:S(2)}, u32[]{:S(2)}) collective-permute-start(f32[1,320]{1,0:T(1,128)S(1)} %get-tuple-element.59), channel_id=1, source_target_pairs={{0,17},{1,8},{2,19},{3,10},{4,21},{5,12},{6,23},{7,14},{8,25},{9,0... | collective-permute-start | bytes 3848 | tf_op jit(solution)/shard_map/ppermute | solution.py:384
  38.6 3.2 %collective-permute-start.18 = (f32[1,320]{1,0:T(1,128)S(1)}, f32[1,320]{1,0:T(1,128)S(1)}, u32[]{:S(2)}, u32[]{:S(2)}) collective-permute-start(f32[1,320]{1,0:T(1,128)S(1)} %get-tuple-element.60), channel_id=1, source_target_pairs={{0,1},{1,0},{2,3},{3,2},{4,5},{5,4},{6,7},{7,6},{8,9},{9,8},{10,11... | collective-permute-start | bytes 3848 | tf_op jit(solution)/shard_map/ppermute | solution.py:386
  41.7 1.2 %collective-permute-start.15 = (f32[1,320]{1,0:T(1,128)S(1)}, f32[1,320]{1,0:T(1,128)S(1)}, u32[]{:S(2)}, u32[]{:S(2)}) collective-permute-start(f32[1,320]{1,0:T(1,128)S(1)} %slice.17), channel_id=1, source_target_pairs={{0,1},{1,0},{2,3},{3,2},{4,5},{5,4},{6,7},{7,6},{8,9},{9,8},{10,11... | collective-permute-start | bytes 3848 | tf_op jit(solution)/shard_map/ppermute | solution.py:380

commit v23 on v22

--- a/solution.py
+++ b/solution.py
@@ -304,7 +304,11 @@
     other_core = everywhere(lambda p, g: (p, g ^ 1))
     first = everywhere(lambda p, g: (p ^ (1 + g % 2), g))
     second = everywhere(lambda p, g: (p ^ (2 - g % 2), g))
-    second_home = everywhere(lambda p, g: (p ^ (2 - g % 2), g ^ 1))
+    homes = [
+        everywhere(lambda p, g: (p ^ (1 + g % 2), g ^ 1)),
+        everywhere(lambda p, g: (p ^ (2 - g % 2), g ^ 1)),
+        everywhere(lambda p, g: (p ^ 3, g ^ 1)),
+    ]
 
     rounds = line_rounds(chips)
     rounds += [[]] * (len(rounds) % 2)
@@ -353,7 +357,7 @@
         in_charge.append(mine)
         bests = [best_two, best_rest]
         far = [far_units] + [jnp.concatenate(pieces, axis=0) for pieces in far[1:]]
-        whole, last = [tuple(range(groups))], [(0,), (1, 3), (2,)]
+        whole, last = [tuple(range(groups))], [(at,) for at in range(groups)]
         for at, second_near in enumerate(near_other):
             second_near, *bests = lax.optimization_barrier((second_near, *bests))
             second_far = lax.ppermute(second_near, BOTH, other_core)
@@ -372,16 +376,17 @@
             sent.append(found)
         sent = lax.ppermute(jnp.concatenate(sent, axis=1), BOTH, other_core)
         kept = jnp.maximum(jnp.concatenate(kept, axis=1), sent)
+        kept, *bests = lax.optimization_barrier((kept, *bests))
         for at, pairs in enumerate(rounds):
             found = lax.ppermute(kept[:, 2 * at * rows : 2 * (at + 1) * rows], BOTH, back(pairs))
             me = lax.axis_index(BOTH)
             sender = functools.reduce(jnp.logical_or, [me == source for source, _ in pairs])
             found = jnp.where(sender, found, -1.0)
             results += [found[:, :rows], lax.ppermute(found[:, rows:], BOTH, other_core)]
-        from_x = lax.ppermute(bests[1], BOTH, first)
-        in_charge += [bests[0], from_x[:, :rows]]
-        onward = jnp.maximum(bests[2], from_x[:, rows:])
-        results.append(lax.ppermute(onward, BOTH, second_home))
+        results += [
+            lax.ppermute(best, BOTH, pairs) for best, pairs in zip(bests[1:], homes)
+        ]
+        in_charge.append(bests[0])
         home = functools.reduce(jnp.maximum, in_charge)
         results.append(lax.ppermute(home, BOTH, other_core))
         return functools.reduce(jnp.maximum, results).reshape(rows)

time: 43.7 us -> 44.1 us (level)
  starting transfers between devices: 20.8 us -> 23.2 us
  waiting for transfers between devices: 13.7 us -> 11.7 us
    ppermute x1, waiting for transfers between devices: 2.6 us -> 0.01 us  [shards(): lax.ppermute(kept[:, 2 * at * rows:2 * (at + 1) * rows], BOTH, back(pairs))]
    ppermute x1, waiting for transfers between devices: 1.12 us -> 0.01 us  [shards(): lax.ppermute(found[:, rows:], BOTH, other_core)]
    ppermute x1, waiting for transfers between devices: 0.01 us -> 1.06 us  [shards(): sent = lax.ppermute(jnp.concatenate(sent, axis=1), BOTH, other_core)]
    ppermute x1, starting transfers between devices: 0.48 us -> 1.49 us  [shards(): results.append(lax.ppermute(home, BOTH, other_core))]
    ppermute x2 -> x3, starting transfers between devices: 2.68 us -> 3.64 us  [shards(): lax.ppermute(best, BOTH, pairs)]
    ppermute x2 -> x3, waiting for transfers between devices: 0.8 us -> 1.47 us  [shards(): lax.ppermute(best, BOTH, pairs)]
    ppermute x1, starting transfers between devices: 0.01 us -> 0.45 us  [shards(): lax.ppermute(found[:, rows:], BOTH, other_core)]
  transfers between devices with their start and end apart: 19 -> 20, of which waited for: 6 -> 5; matrix products, arithmetic and copies ran while one was open for 0% -> 0% of each run, Pallas kernels for 8% -> 8%
where the time goes in v23:
time: 44.1 us; the launch traced here: 43.9 us
  starting transfers between devices  23.2 us (53%)
  waiting for transfers between devices  11.7 us (27%)
  Pallas kernels  5.57 us (13%)
  local copies, waits for them, and re-layouts  2.47 us (6%)
  other arithmetic  0.62 us (1%)
    ppermute x1, starting transfers between devices, shards(): raw = [lax.ppermute(embeddings, BOTH, pairs) for pairs in rounds]  5.51 us
    ppermute x2, waiting for transfers between devices, shards(): from_first = [lax.ppermute(part, BOTH, first) for part in parts]  4.28 us
    ppermute x3, starting transfers between devices, shards(): lax.ppermute(best, BOTH, pairs)  3.64 us
    ppermute x1, starting transfers between devices, shards(): near_other = [lax.ppermute(both, BOTH, pairs) for pairs in rounds]  3.49 us
    ppermute x2, waiting for transfers between devices, shards(): from_corner = [lax.ppermute(part, BOTH, second) for part in from_first]  3.17 us
    unnamed x10, local copies, waits for them, and re-layouts  2.4 us
    pallas_call x2, Pallas kernels, line(): pl.pallas_call(functools.partial(line_kernel, rows, span, together, len(b...  2.28 us
    ppermute x2, starting transfers between devices, shards(): from_corner = [lax.ppermute(part, BOTH, second) for part in from_first]  2.19 us
  transfers between devices with their start and end apart: 20, of which 5 were waited for; matrix products, arithmetic and copies ran while one was open for 0% of the time, Pallas kernels for 8%

profile of v23, /device:TPU:0, one launch (start us, length us, event | category | flops | bytes accessed | tf_op | source)
XLA Modules:
  0.0 43.9 jit_solution(5728211126400843389)
XLA Ops:
  1.0 5.5 %collective-permute-start = (bf16[320,768]{1,0:T(8,128)(2,1)}, bf16[320,768]{1,0:T(8,128)(2,1)S(1)}, u32[]{:S(2)}, u32[]{:S(2)}) collective-permute-start(bf16[320,768]{1,0:T(8,128)(2,1)} %embeddings.1), channel_id=1, source_target_pairs={{6,2},{0,4},{4,6},{7,1},{1,3},{3,5},{14,10},{8,12},{12,14},{15,9},... | collective-permute-start | bytes 1474568 | tf_op jit(solution)/shard_map/ppermute | solution.py:335
  6.5 0.7 %shard_map.38 = (bf16[336,768]{1,0:T(8,128)(2,1)S(1)}, bf16[16,768]{1,0:T(8,128)(2,1)}, bf16[160,768]{1,0:T(8,128)(2,1)S(1)}, bf16[176,768]{1,0:T(8,128)(2,1)S(1)}) custom-call(bf16[320,768]{1,0:T(8,128)(2,1)S(1)} %collective-permute-done.1.embeddings, s32[1,320]{1,0:T(1,128)S(1)} %collective-permute-done.2.cluster, s32[320]{0:T(512)S(1)} %collective-permute-done.3.order_key), custom_call_target="tpu_custom_call" | custom-call | flops 320 | bytes 320 | tf_op jit(solution)/shard_map/pallas_call | solution.py:73
  7.2 1.5 %collective-permute-start.5 = (bf16[160,768]{1,0:T(8,128)(2,1)S(1)}, bf16[160,768]{1,0:T(8,128)(2,1)S(1)}, u32[]{:S(2)}, u32[]{:S(2)}) collective-permute-start(bf16[160,768]{1,0:T(8,128)(2,1)S(1)} %get-tuple-element.41), channel_id=1, source_target_pairs={{0,8},{1,17},{2,10},{3,19},{4,12},{5,21},{6,14},{7,23},{8,0},{9,25... | collective-permute-start | bytes 737288 | tf_op jit(solution)/shard_map/ppermute | solution.py:338
  9.3 1.5 %collective-permute-start.9 = (bf16[336,768]{1,0:T(8,128)(2,1)S(1)}, bf16[336,768]{1,0:T(8,128)(2,1)S(1)}, u32[]{:S(2)}, u32[]{:S(2)}) collective-permute-start(bf16[336,768]{1,0:T(8,128)(2,1)S(1)} %get-tuple-element.39.block.refs_0_), channel_id=1, source_target_pairs={{0,16},{1,9},{2,18},{3,11},{4,20},{5,13},{6,22},{7,15},{8,24},{9,1... | collective-permute-start | bytes 1548296 | tf_op jit(solution)/shard_map/ppermute | solution.py:339
  10.8 1.0 %copy-done.2 = bf16[320,768]{1,0:T(8,128)(2,1)S(1)} copy-done((bf16[320,768]{1,0:T(8,128)(2,1)S(1)}, bf16[320,768]{1,0:T(8,128)(2,1)}, u32[]{:S(2)}) %copy-start.2) | copy-done | bytes 491544
  11.8 0.7 %copy-done.3 = s32[320]{0:T(512)S(1)} copy-done((s32[320]{0:T(512)S(1)}, s32[320]{0:T(512)}, u32[]{:S(2)}) %copy-start.3) | copy-done | bytes 1304
  12.5 0.7 %copy-done.4 = s32[320,1]{0,1:T(1,128)S(1)} copy-done((s32[320,1]{0,1:T(1,128)S(1)}, s32[320,1]{0,1:T(1,128)}, u32[]{:S(2)}) %copy-start.4) | copy-done | bytes 1304
  13.4 3.5 %collective-permute-start.4 = (bf16[336,768]{1,0:T(8,128)(2,1)S(1)}, bf16[336,768]{1,0:T(8,128)(2,1)S(1)}, u32[]{:S(2)}, u32[]{:S(2)}) collective-permute-start(bf16[336,768]{1,0:T(8,128)(2,1)S(1)} %shard_map.40), channel_id=1, source_target_pairs={{6,2},{0,4},{4,6},{7,1},{1,3},{3,5},{14,10},{8,12},{12,14},{15,9},... | collective-permute-start | bytes 1548296 | tf_op jit(solution)/shard_map/ppermute | solution.py:342
  16.9 0.7 %collective-permute-start.6 = (bf16[160,768]{1,0:T(8,128)(2,1)S(1)}, bf16[160,768]{1,0:T(8,128)(2,1)S(1)}, u32[]{:S(2)}, u32[]{:S(2)}) collective-permute-start(bf16[160,768]{1,0:T(8,128)(2,1)S(1)} %collective-permute-done.5.refs_1_), channel_id=1, source_target_pairs={{0,16},{1,9},{2,18},{3,11},{4,20},{5,13},{6,22},{7,15},{8,24},{9,1... | collective-permute-start | bytes 737288 | tf_op jit(solution)/shard_map/ppermute | solution.py:343
  17.6 4.3 %collective-permute-done.7.refs_2_ = bf16[176,768]{1,0:T(8,128)(2,1)S(1)} collective-permute-done((bf16[176,768]{1,0:T(8,128)(2,1)S(1)}, bf16[176,768]{1,0:T(8,128)(2,1)S(1)}, u32[]{:S(2)}, u32[]{:S(2)}) %collective-permute-start.7) | collective-permute-done | bytes 270368 | tf_op jit(solution)/shard_map/ppermute | solution.py:338
  21.9 1.5 %collective-permute-start.8 = (bf16[176,768]{1,0:T(8,128)(2,1)S(1)}, bf16[176,768]{1,0:T(8,128)(2,1)S(1)}, u32[]{:S(2)}, u32[]{:S(2)}) collective-permute-start(bf16[176,768]{1,0:T(8,128)(2,1)S(1)} %collective-permute-done.7.refs_2_), channel_id=1, source_target_pairs={{0,16},{1,9},{2,18},{3,11},{4,20},{5,13},{6,22},{7,15},{8,24},{9,1... | collective-permute-start | bytes 811016 | tf_op jit(solution)/shard_map/ppermute | solution.py:343
  24.2 1.0 %shard_map.41 = (f32[1,640]{1,0:T(1,128)S(1)}, f32[1,320]{1,0:T(1,128)S(1)}) custom-call(bf16[336,768]{1,0:T(8,128)(2,1)S(1)} %get-tuple-element.39.block.refs_0_, bf16[336,768]{1,0:T(8,128)(2,1)S(1)} %get-tuple-element.43.partner, bf16[336,768]{1,0:T(8,128)(2,1)S(1)} %get-tuple-element.39.block.refs_0_, ...), custom_call_target="tpu_custom_call" | custom-call | flops 320 | bytes 320 | tf_op jit(solution)/shard_map/pallas_call | solution.py:236
  25.2 3.2 %collective-permute-done.8.refs_5_ = bf16[176,768]{1,0:T(8,128)(2,1)S(1)} collective-permute-done((bf16[176,768]{1,0:T(8,128)(2,1)S(1)}, bf16[176,768]{1,0:T(8,128)(2,1)S(1)}, u32[]{:S(2)}, u32[]{:S(2)}) %collective-permute-start.8) | collective-permute-done | bytes 270368 | tf_op jit(solution)/shard_map/ppermute | solution.py:343
  28.5 1.0 %shard_map.43 = (f32[1,640]{1,0:T(1,128)S(1)}, f32[1,320]{1,0:T(1,128)S(1)}) custom-call(bf16[336,768]{1,0:T(8,128)(2,1)S(1)} %get-tuple-element.39.block.refs_0_, bf16[336,768]{1,0:T(8,128)(2,1)S(1)} %get-tuple-element.43.partner, bf16[1280,768]{1,0:T(8,128)(2,1)S(1)} %get-tuple-element.50.held, f32[1,1280]{1,0:T(1,128)S(1)} %get-tuple-element.51.row), custom_call_target="tpu_custom_call" | custom-call | flops 320 | bytes 320 | tf_op jit(solution)/shard_map/pallas_call | solution.py:252
  29.8 1.7 %collective-permute-done.12.second = bf16[336,768]{1,0:T(8,128)(2,1)S(1)} collective-permute-done((bf16[336,768]{1,0:T(8,128)(2,1)S(1)}, bf16[336,768]{1,0:T(8,128)(2,1)S(1)}, u32[]{:S(2)}, u32[]{:S(2)}) %collective-permute-start.12) | collective-permute-done | bytes 516128 | tf_op jit(solution)/shard_map/ppermute | solution.py:363
  31.5 2.1 %shard_map.45 = (f32[1,320]{1,0:T(1,128)S(1)}, f32[1,320]{1,0:T(1,128)S(1)}, f32[1,320]{1,0:T(1,128)S(1)}, f32[1,320]{1,0:T(1,128)S(1)}, f32[1,640]{1,0:T(1,128)S(1)}) custom-call(bf16[320,768]{1,0:T(8,128)(2,1)S(1)} %copy-done.1, bf16[336,768]{1,0:T(8,128)(2,1)S(1)} %collective-permute-done.12.second, bf16[1280,768]{1,0:T(8,128)(2,1)S(1)} %get-tuple-element.50.held, ...), custom_call_target="tpu_custom_call" | custom-call | flops 320 | bytes 320 | tf_op jit(solution)/shard_map/pallas_call | solution.py:266
  33.8 1.1 %collective-permute-done.13 = f32[1,640]{1,0:T(1,128)S(1)} collective-permute-done((f32[1,640]{1,0:T(1,128)S(1)}, f32[1,640]{1,0:T(1,128)S(1)}, u32[]{:S(2)}, u32[]{:S(2)}) %collective-permute-start.13) | collective-permute-done | bytes 2592 | tf_op jit(solution)/shard_map/ppermute | solution.py:377
  34.8 1.3 %collective-permute-start.14 = (f32[1,640]{1,0:T(1,128)S(1)}, f32[1,640]{1,0:T(1,128)S(1)}, u32[]{:S(2)}, u32[]{:S(2)}) collective-permute-start(f32[1,640]{1,0:T(1,128)S(1)} %max.24), channel_id=1, source_target_pairs={{2,6},{4,0},{6,4},{1,7},{3,1},{5,3},{10,14},{12,8},{14,12},{9,15},... | collective-permute-start | bytes 7688 | tf_op jit(solution)/shard_map/ppermute | solution.py:381
  36.1 1.5 %collective-permute-start.19 = (f32[1,320]{1,0:T(1,128)S(1)}, f32[1,320]{1,0:T(1,128)S(1)}, u32[]{:S(2)}, u32[]{:S(2)}) collective-permute-start(f32[1,320]{1,0:T(1,128)S(1)} %maximum_maximum_fusion), channel_id=1, source_target_pairs={{0,1},{1,0},{2,3},{3,2},{4,5},{5,4},{6,7},{7,6},{8,9},{9,8},{10,11... | collective-permute-start | bytes 3848 | tf_op jit(solution)/shard_map/ppermute | solution.py:391
  37.6 0.9 %collective-permute-start.16 = (f32[1,320]{1,0:T(1,128)S(1)}, f32[1,320]{1,0:T(1,128)S(1)}, u32[]{:S(2)}, u32[]{:S(2)}) collective-permute-start(f32[1,320]{1,0:T(1,128)S(1)} %get-tuple-element.65), channel_id=1, source_target_pairs={{0,9},{1,16},{2,11},{3,18},{4,13},{5,20},{6,15},{7,22},{8,1},{9,24... | collective-permute-start | bytes 3848 | tf_op jit(solution)/shard_map/ppermute | solution.py:387
  38.6 0.8 %collective-permute-start.17 = (f32[1,320]{1,0:T(1,128)S(1)}, f32[1,320]{1,0:T(1,128)S(1)}, u32[]{:S(2)}, u32[]{:S(2)}) collective-permute-start(f32[1,320]{1,0:T(1,128)S(1)} %get-tuple-element.66), channel_id=1, source_target_pairs={{0,17},{1,8},{2,19},{3,10},{4,21},{5,12},{6,23},{7,14},{8,25},{9,0... | collective-permute-start | bytes 3848 | tf_op jit(solution)/shard_map/ppermute | solution.py:387
  39.4 1.9 %collective-permute-start.18 = (f32[1,320]{1,0:T(1,128)S(1)}, f32[1,320]{1,0:T(1,128)S(1)}, u32[]{:S(2)}, u32[]{:S(2)}) collective-permute-start(f32[1,320]{1,0:T(1,128)S(1)} %get-tuple-element.67), channel_id=1, source_target_pairs={{0,25},{1,24},{2,27},{3,26},{4,29},{5,28},{6,31},{7,30},{8,17},{9,... | collective-permute-start | bytes 3848 | tf_op jit(solution)/shard_map/ppermute | solution.py:387
  41.8 1.5 %collective-permute-done.18 = f32[1,320]{1,0:T(1,128)S(1)} collective-permute-done((f32[1,320]{1,0:T(1,128)S(1)}, f32[1,320]{1,0:T(1,128)S(1)}, u32[]{:S(2)}, u32[]{:S(2)}) %collective-permute-start.18) | collective-permute-done | bytes 1312 | tf_op jit(solution)/shard_map/ppermute | solution.py:387
  43.3 0.6 %maximum_reduce_fusion = f32[320]{0:T(512)} fusion(f32[1,320]{1,0:T(1,128)S(1)} %collective-permute-done.19, f32[1,320]{1,0:T(1,128)S(1)} %collective-permute-done.18, f32[1,320]{1,0:T(1,128)S(1)} %collective-permute-done.17, f32[1,320]{1,0:T(1,128)S(1)} %collective-permute-done.16, f32[1,320]{1,0:T(1,128)S(1)} %collective-permute-done.15, ...), kind=kLoop, calls=%fused_computation.4 | loop fusion | flops 1600 | bytes 8960 | tf_op jit(solution)/shard_map/max | solution.py:392
  (40 shorter events, 3.5 us)
Async XLA Ops:
  0.0 6.5 %collective-permute-start.1 = (bf16[320,768]{1,0:T(8,128)(2,1)}, bf16[320,768]{1,0:T(8,128)(2,1)S(1)}, u32[]{:S(2)}, u32[]{:S(2)}) collective-permute-start(bf16[320,768]{1,0:T(8,128)(2,1)} %embeddings.1), channel_id=1, source_target_pairs={{0,1},{1,0},{2,3},{3,2},{4,5},{5,4},{6,7},{7,6},{8,9},{9,8},{10,11... | collective-permute-start | bytes 1474568 | tf_op jit(solution)/shard_map/ppermute | solution.py:336
  0.5 6.0 %collective-permute-start.2 = (s32[1,320]{1,0:T(1,128)}, s32[1,320]{1,0:T(1,128)S(1)}, u32[]{:S(2)}, u32[]{:S(2)}) collective-permute-start(s32[1,320]{1,0:T(1,128)} %bitcast.1), channel_id=1, source_target_pairs={{0,1},{1,0},{2,3},{3,2},{4,5},{5,4},{6,7},{7,6},{8,9},{9,8},{10,11... | collective-permute-start | bytes 3848 | tf_op jit(solution)/shard_map/ppermute | solution.py:336
  0.5 6.0 %collective-permute-start.3 = (s32[320]{0:T(512)}, s32[320]{0:T(512)S(1)}, u32[]{:S(2)}, u32[]{:S(2)}) collective-permute-start(s32[320]{0:T(512)} %order_key.1), channel_id=1, source_target_pairs={{0,1},{1,0},{2,3},{3,2},{4,5},{5,4},{6,7},{7,6},{8,9},{9,8},{10,11... | collective-permute-start | bytes 3848 | tf_op jit(solution)/shard_map/ppermute | solution.py:336
  1.0 22.4 %collective-permute-start = (bf16[320,768]{1,0:T(8,128)(2,1)}, bf16[320,768]{1,0:T(8,128)(2,1)S(1)}, u32[]{:S(2)}, u32[]{:S(2)}) collective-permute-start(bf16[320,768]{1,0:T(8,128)(2,1)} %embeddings.1), channel_id=1, source_target_pairs={{6,2},{0,4},{4,6},{7,1},{1,3},{3,5},{14,10},{8,12},{12,14},{15,9},... | collective-permute-start | bytes 1474568 | tf_op jit(solution)/shard_map/ppermute | solution.py:335
  7.2 9.7 %collective-permute-start.5 = (bf16[160,768]{1,0:T(8,128)(2,1)S(1)}, bf16[160,768]{1,0:T(8,128)(2,1)S(1)}, u32[]{:S(2)}, u32[]{:S(2)}) collective-permute-start(bf16[160,768]{1,0:T(8,128)(2,1)S(1)} %get-tuple-element.41), channel_id=1, source_target_pairs={{0,8},{1,17},{2,10},{3,19},{4,12},{5,21},{6,14},{7,23},{8,0},{9,25... | collective-permute-start | bytes 737288 | tf_op jit(solution)/shard_map/ppermute | solution.py:338
  8.7 13.1 %collective-permute-start.7 = (bf16[176,768]{1,0:T(8,128)(2,1)S(1)}, bf16[176,768]{1,0:T(8,128)(2,1)S(1)}, u32[]{:S(2)}, u32[]{:S(2)}) collective-permute-start(bf16[176,768]{1,0:T(8,128)(2,1)S(1)} %get-tuple-element.42), channel_id=1, source_target_pairs={{0,8},{1,17},{2,10},{3,19},{4,12},{5,21},{6,14},{7,23},{8,0},{9,25... | collective-permute-start | bytes 811016 | tf_op jit(solution)/shard_map/ppermute | solution.py:338
  9.3 19.1 %collective-permute-start.9 = (bf16[336,768]{1,0:T(8,128)(2,1)S(1)}, bf16[336,768]{1,0:T(8,128)(2,1)S(1)}, u32[]{:S(2)}, u32[]{:S(2)}) collective-permute-start(bf16[336,768]{1,0:T(8,128)(2,1)S(1)} %get-tuple-element.39.block.refs_0_), channel_id=1, source_target_pairs={{0,16},{1,9},{2,18},{3,11},{4,20},{5,13},{6,22},{7,15},{8,24},{9,1... | collective-permute-start | bytes 1548296 | tf_op jit(solution)/shard_map/ppermute | solution.py:339
  10.8 1.0 %copy-start.2 = (bf16[320,768]{1,0:T(8,128)(2,1)S(1)}, bf16[320,768]{1,0:T(8,128)(2,1)}, u32[]{:S(2)}) copy-start(bf16[320,768]{1,0:T(8,128)(2,1)} %embeddings.1) | copy-start | bytes 1474564
  11.8 0.7 %copy-start.3 = (s32[320]{0:T(512)S(1)}, s32[320]{0:T(512)}, u32[]{:S(2)}) copy-start(s32[320]{0:T(512)} %order_key.1) | copy-start | bytes 3844
  13.4 16.1 %collective-permute-start.4 = (bf16[336,768]{1,0:T(8,128)(2,1)S(1)}, bf16[336,768]{1,0:T(8,128)(2,1)S(1)}, u32[]{:S(2)}, u32[]{:S(2)}) collective-permute-start(bf16[336,768]{1,0:T(8,128)(2,1)S(1)} %shard_map.40), channel_id=1, source_target_pairs={{6,2},{0,4},{4,6},{7,1},{1,3},{3,5},{14,10},{8,12},{12,14},{15,9},... | collective-permute-start | bytes 1548296 | tf_op jit(solution)/shard_map/ppermute | solution.py:342
  16.9 6.7 %collective-permute-start.6 = (bf16[160,768]{1,0:T(8,128)(2,1)S(1)}, bf16[160,768]{1,0:T(8,128)(2,1)S(1)}, u32[]{:S(2)}, u32[]{:S(2)}) collective-permute-start(bf16[160,768]{1,0:T(8,128)(2,1)S(1)} %collective-permute-done.5.refs_1_), channel_id=1, source_target_pairs={{0,16},{1,9},{2,18},{3,11},{4,20},{5,13},{6,22},{7,15},{8,24},{9,1... | collective-permute-start | bytes 737288 | tf_op jit(solution)/shard_map/ppermute | solution.py:343
  21.9 6.5 %collective-permute-start.8 = (bf16[176,768]{1,0:T(8,128)(2,1)S(1)}, bf16[176,768]{1,0:T(8,128)(2,1)S(1)}, u32[]{:S(2)}, u32[]{:S(2)}) collective-permute-start(bf16[176,768]{1,0:T(8,128)(2,1)S(1)} %collective-permute-done.7.refs_2_), channel_id=1, source_target_pairs={{0,16},{1,9},{2,18},{3,11},{4,20},{5,13},{6,22},{7,15},{8,24},{9,1... | collective-permute-start | bytes 811016 | tf_op jit(solution)/shard_map/ppermute | solution.py:343
  23.6 4.8 %collective-permute-start.10 = (bf16[160,768]{1,0:T(8,128)(2,1)S(1)}, bf16[160,768]{1,0:T(8,128)(2,1)S(1)}, u32[]{:S(2)}, u32[]{:S(2)}) collective-permute-start(bf16[160,768]{1,0:T(8,128)(2,1)S(1)} %get-tuple-element.48), channel_id=1, source_target_pairs={{0,1},{1,0},{2,3},{3,2},{4,5},{5,4},{6,7},{7,6},{8,9},{9,8},{10,11... | collective-permute-start | bytes 737288 | tf_op jit(solution)/shard_map/ppermute | solution.py:348
  23.7 4.7 %collective-permute-start.11 = (bf16[160,768]{1,0:T(8,128)(2,1)S(1)}, bf16[160,768]{1,0:T(8,128)(2,1)S(1)}, u32[]{:S(2)}, u32[]{:S(2)}) collective-permute-start(bf16[160,768]{1,0:T(8,128)(2,1)S(1)} %get-tuple-element.49), channel_id=1, source_target_pairs={{0,1},{1,0},{2,3},{3,2},{4,5},{5,4},{6,7},{7,6},{8,9},{9,8},{10,11... | collective-permute-start | bytes 737288 | tf_op jit(solution)/shard_map/ppermute | solution.py:348
  28.5 1.0 %copy-start = (bf16[320,768]{1,0:T(8,128)(2,1)}, bf16[320,768]{1,0:T(8,128)(2,1)S(1)}, u32[]{:S(2)}) copy-start(bf16[320,768]{1,0:T(8,128)(2,1)S(1)} %get-tuple-element.57.first) | copy-start | bytes 1474564
  29.5 2.0 %collective-permute-start.12 = (bf16[336,768]{1,0:T(8,128)(2,1)S(1)}, bf16[336,768]{1,0:T(8,128)(2,1)S(1)}, u32[]{:S(2)}, u32[]{:S(2)}) collective-permute-start(bf16[336,768]{1,0:T(8,128)(2,1)S(1)} %collective-permute-done.4.second), channel_id=1, source_target_pairs={{0,1},{1,0},{2,3},{3,2},{4,5},{5,4},{6,7},{7,6},{8,9},{9,8},{10,11... | collective-permute-start | bytes 1548296 | tf_op jit(solution)/shard_map/ppermute | solution.py:363
  29.7 1.9 %copy-start.1 = (bf16[320,768]{1,0:T(8,128)(2,1)S(1)}, bf16[320,768]{1,0:T(8,128)(2,1)}, u32[]{:S(2)}) copy-start(bf16[320,768]{1,0:T(8,128)(2,1)} %copy-done) | copy-start | bytes 1474564
  33.7 1.2 %collective-permute-start.13 = (f32[1,640]{1,0:T(1,128)S(1)}, f32[1,640]{1,0:T(1,128)S(1)}, u32[]{:S(2)}, u32[]{:S(2)}) collective-permute-start(f32[1,640]{1,0:T(1,128)S(1)} %get-tuple-element.59), channel_id=1, source_target_pairs={{0,1},{1,0},{2,3},{3,2},{4,5},{5,4},{6,7},{7,6},{8,9},{9,8},{10,11... | collective-permute-start | bytes 7688 | tf_op jit(solution)/shard_map/ppermute | solution.py:377
  34.8 6.4 %collective-permute-start.14 = (f32[1,640]{1,0:T(1,128)S(1)}, f32[1,640]{1,0:T(1,128)S(1)}, u32[]{:S(2)}, u32[]{:S(2)}) collective-permute-start(f32[1,640]{1,0:T(1,128)S(1)} %max.24), channel_id=1, source_target_pairs={{2,6},{4,0},{6,4},{1,7},{3,1},{5,3},{10,14},{12,8},{14,12},{9,15},... | collective-permute-start | bytes 7688 | tf_op jit(solution)/shard_map/ppermute | solution.py:381
  36.1 5.7 %collective-permute-start.19 = (f32[1,320]{1,0:T(1,128)S(1)}, f32[1,320]{1,0:T(1,128)S(1)}, u32[]{:S(2)}, u32[]{:S(2)}) collective-permute-start(f32[1,320]{1,0:T(1,128)S(1)} %maximum_maximum_fusion), channel_id=1, source_target_pairs={{0,1},{1,0},{2,3},{3,2},{4,5},{5,4},{6,7},{7,6},{8,9},{9,8},{10,11... | collective-permute-start | bytes 3848 | tf_op jit(solution)/shard_map/ppermute | solution.py:391
  37.6 4.2 %collective-permute-start.16 = (f32[1,320]{1,0:T(1,128)S(1)}, f32[1,320]{1,0:T(1,128)S(1)}, u32[]{:S(2)}, u32[]{:S(2)}) collective-permute-start(f32[1,320]{1,0:T(1,128)S(1)} %get-tuple-element.65), channel_id=1, source_target_pairs={{0,9},{1,16},{2,11},{3,18},{4,13},{5,20},{6,15},{7,22},{8,1},{9,24... | collective-permute-start | bytes 3848 | tf_op jit(solution)/shard_map/ppermute | solution.py:387
  38.6 3.2 %collective-permute-start.17 = (f32[1,320]{1,0:T(1,128)S(1)}, f32[1,320]{1,0:T(1,128)S(1)}, u32[]{:S(2)}, u32[]{:S(2)}) collective-permute-start(f32[1,320]{1,0:T(1,128)S(1)} %get-tuple-element.66), channel_id=1, source_target_pairs={{0,17},{1,8},{2,19},{3,10},{4,21},{5,12},{6,23},{7,14},{8,25},{9,0... | collective-permute-start | bytes 3848 | tf_op jit(solution)/shard_map/ppermute | solution.py:387
  39.4 3.9 %collective-permute-start.18 = (f32[1,320]{1,0:T(1,128)S(1)}, f32[1,320]{1,0:T(1,128)S(1)}, u32[]{:S(2)}, u32[]{:S(2)}) collective-permute-start(f32[1,320]{1,0:T(1,128)S(1)} %get-tuple-element.67), channel_id=1, source_target_pairs={{0,25},{1,24},{2,27},{3,26},{4,29},{5,28},{6,31},{7,30},{8,17},{9,... | collective-permute-start | bytes 3848 | tf_op jit(solution)/shard_map/ppermute | solution.py:387
  41.4 1.9 %collective-permute-start.15 = (f32[1,320]{1,0:T(1,128)S(1)}, f32[1,320]{1,0:T(1,128)S(1)}, u32[]{:S(2)}, u32[]{:S(2)}) collective-permute-start(f32[1,320]{1,0:T(1,128)S(1)} %slice.9), channel_id=1, source_target_pairs={{0,1},{1,0},{2,3},{3,2},{4,5},{5,4},{6,7},{7,6},{8,9},{9,8},{10,11... | collective-permute-start | bytes 3848 | tf_op jit(solution)/shard_map/ppermute | solution.py:385
  (1 other events, 0.7 us)

commit v24 on v22

--- a/solution.py
+++ b/solution.py
@@ -41,18 +41,30 @@
         out[...] = block[top : top + out.shape[0], :]
 
 
-def prepare_kernel(embeddings, cluster, order_key, block, codes_out, *parts_out):
-    rows, width = embeddings.shape
-    unit_rows(embeddings, block)
+def code_rows(cluster, order_key, width):
+    rows = order_key.shape[0]
     keys = order_key[...].reshape(1, rows)
     parts = [keys >> 8, keys & 255, cluster[...] + 1]
     parts = [part.astype(jnp.float32) for part in parts]
     parts = jnp.concatenate(parts + [jnp.zeros((EXTRA - CODES, rows), jnp.float32)], axis=0)
     parts = jnp.concatenate([parts, jnp.zeros((EXTRA, width - rows), jnp.float32)], axis=1)
-    block[rows : rows + EXTRA, :] = parts.astype(jnp.bfloat16)
-    codes_out[...] = block[rows : rows + EXTRA, :]
-    if parts_out:
-        give_parts(block, parts_out)
+    return parts.astype(jnp.bfloat16)
+
+
+def prepare_kernel(embeddings, cluster, order_key, block, *parts_out):
+    rows, width = embeddings.shape
+    unit_rows(embeddings, block)
+    block[rows : rows + EXTRA, :] = code_rows(cluster, order_key, width)
+    give_parts(block, parts_out)
+
+
+def codes_kernel(cluster, order_key, out):
+    out[...] = code_rows(cluster, order_key, out.shape[1])
+
+
+def own_kernel(embeddings, own_codes, block):
+    unit_rows(embeddings, block)
+    block[embeddings.shape[0] :, :] = own_codes[...]
 
 
 def complete_kernel(block, other_codes, out):
@@ -68,14 +80,13 @@
     give_parts(block, parts_out)
 
 
-def with_units(kernel, heights, rows_of, *others):
-    rows, width = rows_of.shape
+def with_units(kernel, heights, width, *inputs):
     return pl.pallas_call(
         kernel,
         out_shape=[jax.ShapeDtypeStruct((height, width), jnp.bfloat16) for height in heights],
         compiler_params=pltpu.CompilerParams(vmem_limit_bytes=8 << 20),
-        cost_estimate=pl.CostEstimate(flops=rows, bytes_accessed=rows, transcendentals=0),
-    )(rows_of, *others)
+        cost_estimate=pl.CostEstimate(flops=width, bytes_accessed=width, transcendentals=0),
+    )(*inputs)
 
 
 def row_from_partial(partial, rows):
@@ -330,15 +341,18 @@
         names = (cluster.reshape(1, rows), order_key)
         raw = [lax.ppermute(embeddings, BOTH, pairs) for pairs in rounds]
         charge = [lax.ppermute(array, BOTH, other_core) for array in (embeddings, *names)]
-        block, _, *parts = with_units(prepare_kernel, (rows + EXTRA, EXTRA, *halves), *charge)
+        width = embeddings.shape[1]
+        block, *parts = with_units(prepare_kernel, (rows + EXTRA, *halves), width, *charge)
         from_first = [lax.ppermute(part, BOTH, first) for part in parts]
-        from_second = [lax.ppermute(block, BOTH, second)]
-        own, own_codes = with_units(prepare_kernel, (rows + EXTRA, EXTRA), embeddings, *names)
-        (both,) = with_units(complete_kernel, (rows + EXTRA,), block, own_codes)
+        (own_codes,) = with_units(codes_kernel, (EXTRA,), width, *names)
+        later, own_codes = lax.optimization_barrier((block, own_codes))
+        from_second = [lax.ppermute(later, BOTH, second)]
+        (both,) = with_units(complete_kernel, (rows + EXTRA,), width, block, own_codes)
+        (own,) = with_units(own_kernel, (rows + EXTRA,), width, embeddings, own_codes)
         near_other = [lax.ppermute(both, BOTH, pairs) for pairs in rounds]
         from_corner = [lax.ppermute(part, BOTH, second) for part in from_first]
         near = [
-            list(with_units(unit_kernel, (rows, rows // 2, rows // 2), rows_of))
+            list(with_units(unit_kernel, (rows, rows // 2, rows // 2), width, rows_of))
             for rows_of in raw
         ]
         far = [[lax.ppermute(piece, BOTH, other_core) for piece in blocks[1:]] for blocks in near]

time: 43.7 us -> 43.5 us (level)
  starting transfers between devices: 20.8 us -> 24.7 us
  waiting for transfers between devices: 13.7 us -> 11.2 us
  local copies, waits for them, and re-layouts: 2.47 us -> 1.45 us
  Pallas kernels: 5.59 us -> 5.06 us
    ppermute x2, waiting for transfers between devices: 3.17 us -> 1.52 us  [shards(): from_corner = [lax.ppermute(part, BOTH, second) for part in from_first]]
    ppermute x2, starting transfers between devices: 0.56 us -> 2.03 us  [shards(): lax.ppermute(piece, BOTH, other_core)]
    ppermute x1, starting transfers between devices: 1.55 us -> 2.74 us  [shards(): from_x = lax.ppermute(bests[1], BOTH, first)]
    unnamed x10, local copies, waits for them, and re-layouts: 2.4 us -> 1.37 us
    pallas_call x4 -> x5, Pallas kernels: 1.13 us -> 0.59 us  [with_units(): pl.pallas_call(kernel, out_shape=[jax.ShapeDtypeStruct((height, width), j...]
    ppermute x1, waiting for transfers between devices: 0.8 us -> 0.27 us  [shards(): from_x = lax.ppermute(bests[1], BOTH, first)]
    ppermute x1, starting transfers between devices: 1.12 us -> 1.61 us  [shards(): results.append(lax.ppermute(onward, BOTH, second_home))]
    ppermute x1, starting transfers between devices: 0.07 us -> 0.53 us  [shards(): second_far = lax.ppermute(second_near, BOTH, other_core)]
  transfers between devices with their start and end apart: 19 -> 19, of which waited for: 6 -> 7; matrix products, arithmetic and copies ran while one was open for 0% -> 0% of each run, Pallas kernels for 8% -> 7%
where the time goes in v24:
time: 43.5 us; the launch traced here: 43.3 us
  starting transfers between devices  24.7 us (57%)
  waiting for transfers between devices  11.2 us (26%)
  Pallas kernels  5.06 us (12%)
  local copies, waits for them, and re-layouts  1.45 us (3%)
  other arithmetic  0.68 us (2%)
    ppermute x1, starting transfers between devices, shards(): raw = [lax.ppermute(embeddings, BOTH, pairs) for pairs in rounds]  5.57 us
    ppermute x2, waiting for transfers between devices, shards(): from_first = [lax.ppermute(part, BOTH, first) for part in parts]  4.28 us
    ppermute x1, starting transfers between devices, shards(): near_other = [lax.ppermute(both, BOTH, pairs) for pairs in rounds]  3.49 us
    ppermute x1, starting transfers between devices, shards(): from_x = lax.ppermute(bests[1], BOTH, first)  2.74 us
    ppermute x1, waiting for transfers between devices, shards(): lax.ppermute(kept[:, 2 * at * rows:2 * (at + 1) * rows], BOTH, back(pairs))  2.6 us
    pallas_call x2, Pallas kernels, line(): pl.pallas_call(functools.partial(line_kernel, rows, span, together, len(b...  2.29 us
    ppermute x2, starting transfers between devices, shards(): from_corner = [lax.ppermute(part, BOTH, second) for part in from_first]  2.26 us
    ppermute x2, starting transfers between devices, shards(): from_first = [lax.ppermute(part, BOTH, first) for part in parts]  2.09 us
  transfers between devices with their start and end apart: 19, of which 7 were waited for; matrix products, arithmetic and copies ran while one was open for 0% of the time, Pallas kernels for 7%

profile of v24, /device:TPU:0, one launch (start us, length us, event | category | flops | bytes accessed | tf_op | source)
XLA Modules:
  0.0 43.3 jit_solution(18186130620176883173)
XLA Ops:
  1.0 5.6 %collective-permute-start = (bf16[320,768]{1,0:T(8,128)(2,1)}, bf16[320,768]{1,0:T(8,128)(2,1)S(1)}, u32[]{:S(2)}, u32[]{:S(2)}) collective-permute-start(bf16[320,768]{1,0:T(8,128)(2,1)} %embeddings.1), channel_id=1, source_target_pairs={{6,2},{0,4},{4,6},{7,1},{1,3},{3,5},{14,10},{8,12},{12,14},{15,9},... | collective-permute-start | bytes 1474568 | tf_op jit(solution)/shard_map/ppermute | solution.py:342
  6.8 1.6 %collective-permute-start.5 = (bf16[160,768]{1,0:T(8,128)(2,1)S(1)}, bf16[160,768]{1,0:T(8,128)(2,1)S(1)}, u32[]{:S(2)}, u32[]{:S(2)}) collective-permute-start(bf16[160,768]{1,0:T(8,128)(2,1)S(1)} %get-tuple-element.35), channel_id=1, source_target_pairs={{0,8},{1,17},{2,10},{3,19},{4,12},{5,21},{6,14},{7,23},{8,0},{9,25... | collective-permute-start | bytes 737288 | tf_op jit(solution)/shard_map/ppermute | solution.py:346
  8.3 0.5 %collective-permute-start.7 = (bf16[176,768]{1,0:T(8,128)(2,1)S(1)}, bf16[176,768]{1,0:T(8,128)(2,1)S(1)}, u32[]{:S(2)}, u32[]{:S(2)}) collective-permute-start(bf16[176,768]{1,0:T(8,128)(2,1)S(1)} %get-tuple-element.36), channel_id=1, source_target_pairs={{0,8},{1,17},{2,10},{3,19},{4,12},{5,21},{6,14},{7,23},{8,0},{9,25... | collective-permute-start | bytes 811016 | tf_op jit(solution)/shard_map/ppermute | solution.py:346
  8.9 0.7 %copy-done.3 = s32[320]{0:T(512)S(1)} copy-done((s32[320]{0:T(512)S(1)}, s32[320]{0:T(512)}, u32[]{:S(2)}) %copy-start.3) | copy-done | bytes 1304
  9.5 0.7 %copy-done.4 = s32[320,1]{0,1:T(1,128)S(1)} copy-done((s32[320,1]{0,1:T(1,128)S(1)}, s32[320,1]{0,1:T(1,128)}, u32[]{:S(2)}) %copy-start.4) | copy-done | bytes 1304
  10.2 1.6 %collective-permute-start.9 = (bf16[336,768]{1,0:T(8,128)(2,1)S(1)}, bf16[336,768]{1,0:T(8,128)(2,1)S(1)}, u32[]{:S(2)}, u32[]{:S(2)}) collective-permute-start(bf16[336,768]{1,0:T(8,128)(2,1)S(1)} %get-tuple-element.39.block.refs_0_), channel_id=1, source_target_pairs={{0,16},{1,9},{2,18},{3,11},{4,20},{5,13},{6,22},{7,15},{8,24},{9,1... | collective-permute-start | bytes 1548296 | tf_op jit(solution)/shard_map/ppermute | solution.py:349
  11.9 3.5 %collective-permute-start.4 = (bf16[336,768]{1,0:T(8,128)(2,1)S(1)}, bf16[336,768]{1,0:T(8,128)(2,1)S(1)}, u32[]{:S(2)}, u32[]{:S(2)}) collective-permute-start(bf16[336,768]{1,0:T(8,128)(2,1)S(1)} %shard_map.40), channel_id=1, source_target_pairs={{6,2},{0,4},{4,6},{7,1},{1,3},{3,5},{14,10},{8,12},{12,14},{15,9},... | collective-permute-start | bytes 1548296 | tf_op jit(solution)/shard_map/ppermute | solution.py:352
  15.4 0.7 %collective-permute-start.6 = (bf16[160,768]{1,0:T(8,128)(2,1)S(1)}, bf16[160,768]{1,0:T(8,128)(2,1)S(1)}, u32[]{:S(2)}, u32[]{:S(2)}) collective-permute-start(bf16[160,768]{1,0:T(8,128)(2,1)S(1)} %collective-permute-done.5.refs_1_), channel_id=1, source_target_pairs={{0,16},{1,9},{2,18},{3,11},{4,20},{5,13},{6,22},{7,15},{8,24},{9,1... | collective-permute-start | bytes 737288 | tf_op jit(solution)/shard_map/ppermute | solution.py:353
  16.1 4.3 %collective-permute-done.7.refs_2_ = bf16[176,768]{1,0:T(8,128)(2,1)S(1)} collective-permute-done((bf16[176,768]{1,0:T(8,128)(2,1)S(1)}, bf16[176,768]{1,0:T(8,128)(2,1)S(1)}, u32[]{:S(2)}, u32[]{:S(2)}) %collective-permute-start.7) | collective-permute-done | bytes 270368 | tf_op jit(solution)/shard_map/ppermute | solution.py:346
  20.4 1.5 %collective-permute-start.8 = (bf16[176,768]{1,0:T(8,128)(2,1)S(1)}, bf16[176,768]{1,0:T(8,128)(2,1)S(1)}, u32[]{:S(2)}, u32[]{:S(2)}) collective-permute-start(bf16[176,768]{1,0:T(8,128)(2,1)S(1)} %collective-permute-done.7.refs_2_), channel_id=1, source_target_pairs={{0,16},{1,9},{2,18},{3,11},{4,20},{5,13},{6,22},{7,15},{8,24},{9,1... | collective-permute-start | bytes 811016 | tf_op jit(solution)/shard_map/ppermute | solution.py:353
  22.2 2.0 %collective-permute-start.11 = (bf16[160,768]{1,0:T(8,128)(2,1)S(1)}, bf16[160,768]{1,0:T(8,128)(2,1)S(1)}, u32[]{:S(2)}, u32[]{:S(2)}) collective-permute-start(bf16[160,768]{1,0:T(8,128)(2,1)S(1)} %get-tuple-element.43), channel_id=1, source_target_pairs={{0,1},{1,0},{2,3},{3,2},{4,5},{5,4},{6,7},{7,6},{8,9},{9,8},{10,11... | collective-permute-start | bytes 737288 | tf_op jit(solution)/shard_map/ppermute | solution.py:358
  24.4 1.0 %shard_map.42 = (f32[1,640]{1,0:T(1,128)S(1)}, f32[1,320]{1,0:T(1,128)S(1)}) custom-call(bf16[336,768]{1,0:T(8,128)(2,1)S(1)} %get-tuple-element.39.block.refs_0_, bf16[336,768]{1,0:T(8,128)(2,1)S(1)} %shard_map.41.partner, bf16[336,768]{1,0:T(8,128)(2,1)S(1)} %get-tuple-element.39.block.refs_0_, bf16[160,768]{1,0:T(8,128)(2,1)S(1)} %collective-permute-done.5.refs_1_, ...), custom_call_target="tpu_custom_call" | custom-call | flops 320 | bytes 320 | tf_op jit(solution)/shard_map/pallas_call | solution.py:247
  25.4 1.4 %collective-permute-done.8.refs_5_ = bf16[176,768]{1,0:T(8,128)(2,1)S(1)} collective-permute-done((bf16[176,768]{1,0:T(8,128)(2,1)S(1)}, bf16[176,768]{1,0:T(8,128)(2,1)S(1)}, u32[]{:S(2)}, u32[]{:S(2)}) %collective-permute-start.8) | collective-permute-done | bytes 270368 | tf_op jit(solution)/shard_map/ppermute | solution.py:353
  27.0 1.0 %shard_map.44 = (f32[1,640]{1,0:T(1,128)S(1)}, f32[1,320]{1,0:T(1,128)S(1)}) custom-call(bf16[336,768]{1,0:T(8,128)(2,1)S(1)} %get-tuple-element.39.block.refs_0_, bf16[336,768]{1,0:T(8,128)(2,1)S(1)} %shard_map.41.partner, bf16[1280,768]{1,0:T(8,128)(2,1)S(1)} %get-tuple-element.44.held, f32[1,1280]{1,0:T(1,128)S(1)} %get-tuple-element.45.row), custom_call_target="tpu_custom_call" | custom-call | flops 320 | bytes 320 | tf_op jit(solution)/shard_map/pallas_call | solution.py:263
  28.1 0.5 %collective-permute-start.12 = (bf16[336,768]{1,0:T(8,128)(2,1)S(1)}, bf16[336,768]{1,0:T(8,128)(2,1)S(1)}, u32[]{:S(2)}, u32[]{:S(2)}) collective-permute-start(bf16[336,768]{1,0:T(8,128)(2,1)S(1)} %collective-permute-done.4.second), channel_id=1, source_target_pairs={{0,1},{1,0},{2,3},{3,2},{4,5},{5,4},{6,7},{7,6},{8,9},{9,8},{10,11... | collective-permute-start | bytes 1548296 | tf_op jit(solution)/shard_map/ppermute | solution.py:373
  28.7 1.4 %collective-permute-done.12.second = bf16[336,768]{1,0:T(8,128)(2,1)S(1)} collective-permute-done((bf16[336,768]{1,0:T(8,128)(2,1)S(1)}, bf16[336,768]{1,0:T(8,128)(2,1)S(1)}, u32[]{:S(2)}, u32[]{:S(2)}) %collective-permute-start.12) | collective-permute-done | bytes 516128 | tf_op jit(solution)/shard_map/ppermute | solution.py:373
  30.1 2.2 %shard_map.46 = (f32[1,320]{1,0:T(1,128)S(1)}, f32[1,640]{1,0:T(1,128)S(1)}, f32[1,320]{1,0:T(1,128)S(1)}, f32[1,640]{1,0:T(1,128)S(1)}) custom-call(bf16[320,768]{1,0:T(8,128)(2,1)S(1)} %copy-done.1, bf16[336,768]{1,0:T(8,128)(2,1)S(1)} %collective-permute-done.12.second, bf16[1280,768]{1,0:T(8,128)(2,1)S(1)} %get-tuple-element.44.held, ...), custom_call_target="tpu_custom_call" | custom-call | flops 320 | bytes 320 | tf_op jit(solution)/shard_map/pallas_call | solution.py:277
  32.3 2.7 %collective-permute-start.16 = (f32[1,640]{1,0:T(1,128)S(1)}, f32[1,640]{1,0:T(1,128)S(1)}, u32[]{:S(2)}, u32[]{:S(2)}) collective-permute-start(f32[1,640]{1,0:T(1,128)S(1)} %get-tuple-element.55), channel_id=1, source_target_pairs={{0,8},{1,17},{2,10},{3,19},{4,12},{5,21},{6,14},{7,23},{8,0},{9,25... | collective-permute-start | bytes 7688 | tf_op jit(solution)/shard_map/ppermute | solution.py:395
  35.1 1.3 %collective-permute-start.14 = (f32[1,640]{1,0:T(1,128)S(1)}, f32[1,640]{1,0:T(1,128)S(1)}, u32[]{:S(2)}, u32[]{:S(2)}) collective-permute-start(f32[1,640]{1,0:T(1,128)S(1)} %max.24), channel_id=1, source_target_pairs={{2,6},{4,0},{6,4},{1,7},{3,1},{5,3},{10,14},{12,8},{14,12},{9,15},... | collective-permute-start | bytes 7688 | tf_op jit(solution)/shard_map/ppermute | solution.py:390
  36.7 1.6 %collective-permute-start.17 = (f32[1,320]{1,0:T(1,128)S(1)}, f32[1,320]{1,0:T(1,128)S(1)}, u32[]{:S(2)}, u32[]{:S(2)}) collective-permute-start(f32[1,320]{1,0:T(1,128)S(1)} %get-tuple-element.59), channel_id=1, source_target_pairs={{0,17},{1,8},{2,19},{3,10},{4,21},{5,12},{6,23},{7,14},{8,25},{9,0... | collective-permute-start | bytes 3848 | tf_op jit(solution)/shard_map/ppermute | solution.py:398
  38.3 0.5 %collective-permute-start.18 = (f32[1,320]{1,0:T(1,128)S(1)}, f32[1,320]{1,0:T(1,128)S(1)}, u32[]{:S(2)}, u32[]{:S(2)}) collective-permute-start(f32[1,320]{1,0:T(1,128)S(1)} %get-tuple-element.60), channel_id=1, source_target_pairs={{0,1},{1,0},{2,3},{3,2},{4,5},{5,4},{6,7},{7,6},{8,9},{9,8},{10,11... | collective-permute-start | bytes 3848 | tf_op jit(solution)/shard_map/ppermute | solution.py:400
  38.8 2.6 %collective-permute-done.14 = f32[1,640]{1,0:T(1,128)S(1)} collective-permute-done((f32[1,640]{1,0:T(1,128)S(1)}, f32[1,640]{1,0:T(1,128)S(1)}, u32[]{:S(2)}, u32[]{:S(2)}) %collective-permute-start.14) | collective-permute-done | bytes 2592 | tf_op jit(solution)/shard_map/ppermute | solution.py:390
  41.6 1.1 %collective-permute-done.15 = f32[1,320]{1,0:T(1,128)S(1)} collective-permute-done((f32[1,320]{1,0:T(1,128)S(1)}, f32[1,320]{1,0:T(1,128)S(1)}, u32[]{:S(2)}, u32[]{:S(2)}) %collective-permute-start.15) | collective-permute-done | bytes 1312 | tf_op jit(solution)/shard_map/ppermute | solution.py:394
  42.7 0.6 %fusion.2 = f32[320]{0:T(512)} fusion(f32[1,320]{1,0:T(1,128)S(1)} %collective-permute-done.18, f32[1,320]{1,0:T(1,128)S(1)} %collective-permute-done.17, f32[1,320]{1,0:T(1,128)S(1)} %collective-permute-done.15, f32[1,640]{1,0:T(1,128)S(1)} %broadcast_select_fusion), kind=kLoop, calls=%fused_computation.6 | loop fusion | flops 960 | bytes 6400 | tf_op jit(solution)/shard_map/max | solution.py:401
  (39 shorter events, 2.5 us)
Async XLA Ops:
  0.0 24.2 %copy-start.2 = (bf16[320,768]{1,0:T(8,128)(2,1)S(1)}, bf16[320,768]{1,0:T(8,128)(2,1)}, u32[]{:S(2)}) copy-start(bf16[320,768]{1,0:T(8,128)(2,1)} %embeddings.1) | copy-start | bytes 1474564
  0.0 6.6 %collective-permute-start.1 = (bf16[320,768]{1,0:T(8,128)(2,1)}, bf16[320,768]{1,0:T(8,128)(2,1)S(1)}, u32[]{:S(2)}, u32[]{:S(2)}) collective-permute-start(bf16[320,768]{1,0:T(8,128)(2,1)} %embeddings.1), channel_id=1, source_target_pairs={{0,1},{1,0},{2,3},{3,2},{4,5},{5,4},{6,7},{7,6},{8,9},{9,8},{10,11... | collective-permute-start | bytes 1474568 | tf_op jit(solution)/shard_map/ppermute | solution.py:343
  0.5 6.1 %collective-permute-start.2 = (s32[1,320]{1,0:T(1,128)}, s32[1,320]{1,0:T(1,128)S(1)}, u32[]{:S(2)}, u32[]{:S(2)}) collective-permute-start(s32[1,320]{1,0:T(1,128)} %bitcast.1), channel_id=1, source_target_pairs={{0,1},{1,0},{2,3},{3,2},{4,5},{5,4},{6,7},{7,6},{8,9},{9,8},{10,11... | collective-permute-start | bytes 3848 | tf_op jit(solution)/shard_map/ppermute | solution.py:343
  0.5 6.0 %collective-permute-start.3 = (s32[320]{0:T(512)}, s32[320]{0:T(512)S(1)}, u32[]{:S(2)}, u32[]{:S(2)}) collective-permute-start(s32[320]{0:T(512)} %order_key.1), channel_id=1, source_target_pairs={{0,1},{1,0},{2,3},{3,2},{4,5},{5,4},{6,7},{7,6},{8,9},{9,8},{10,11... | collective-permute-start | bytes 3848 | tf_op jit(solution)/shard_map/ppermute | solution.py:343
  1.0 20.9 %collective-permute-start = (bf16[320,768]{1,0:T(8,128)(2,1)}, bf16[320,768]{1,0:T(8,128)(2,1)S(1)}, u32[]{:S(2)}, u32[]{:S(2)}) collective-permute-start(bf16[320,768]{1,0:T(8,128)(2,1)} %embeddings.1), channel_id=1, source_target_pairs={{6,2},{0,4},{4,6},{7,1},{1,3},{3,5},{14,10},{8,12},{12,14},{15,9},... | collective-permute-start | bytes 1474568 | tf_op jit(solution)/shard_map/ppermute | solution.py:342
  6.8 8.6 %collective-permute-start.5 = (bf16[160,768]{1,0:T(8,128)(2,1)S(1)}, bf16[160,768]{1,0:T(8,128)(2,1)S(1)}, u32[]{:S(2)}, u32[]{:S(2)}) collective-permute-start(bf16[160,768]{1,0:T(8,128)(2,1)S(1)} %get-tuple-element.35), channel_id=1, source_target_pairs={{0,8},{1,17},{2,10},{3,19},{4,12},{5,21},{6,14},{7,23},{8,0},{9,25... | collective-permute-start | bytes 737288 | tf_op jit(solution)/shard_map/ppermute | solution.py:346
  8.3 12.1 %collective-permute-start.7 = (bf16[176,768]{1,0:T(8,128)(2,1)S(1)}, bf16[176,768]{1,0:T(8,128)(2,1)S(1)}, u32[]{:S(2)}, u32[]{:S(2)}) collective-permute-start(bf16[176,768]{1,0:T(8,128)(2,1)S(1)} %get-tuple-element.36), channel_id=1, source_target_pairs={{0,8},{1,17},{2,10},{3,19},{4,12},{5,21},{6,14},{7,23},{8,0},{9,25... | collective-permute-start | bytes 811016 | tf_op jit(solution)/shard_map/ppermute | solution.py:346
  8.9 0.7 %copy-start.3 = (s32[320]{0:T(512)S(1)}, s32[320]{0:T(512)}, u32[]{:S(2)}) copy-start(s32[320]{0:T(512)} %order_key.1) | copy-start | bytes 3844
  9.5 0.7 %copy-start.4 = (s32[320,1]{0,1:T(1,128)S(1)}, s32[320,1]{0,1:T(1,128)}, u32[]{:S(2)}) copy-start(s32[320,1]{0,1:T(1,128)} %param.4) | copy-start | bytes 3844
  10.2 16.6 %collective-permute-start.9 = (bf16[336,768]{1,0:T(8,128)(2,1)S(1)}, bf16[336,768]{1,0:T(8,128)(2,1)S(1)}, u32[]{:S(2)}, u32[]{:S(2)}) collective-permute-start(bf16[336,768]{1,0:T(8,128)(2,1)S(1)} %get-tuple-element.39.block.refs_0_), channel_id=1, source_target_pairs={{0,16},{1,9},{2,18},{3,11},{4,20},{5,13},{6,22},{7,15},{8,24},{9,1... | collective-permute-start | bytes 1548296 | tf_op jit(solution)/shard_map/ppermute | solution.py:349
  11.9 16.2 %collective-permute-start.4 = (bf16[336,768]{1,0:T(8,128)(2,1)S(1)}, bf16[336,768]{1,0:T(8,128)(2,1)S(1)}, u32[]{:S(2)}, u32[]{:S(2)}) collective-permute-start(bf16[336,768]{1,0:T(8,128)(2,1)S(1)} %shard_map.40), channel_id=1, source_target_pairs={{6,2},{0,4},{4,6},{7,1},{1,3},{3,5},{14,10},{8,12},{12,14},{15,9},... | collective-permute-start | bytes 1548296 | tf_op jit(solution)/shard_map/ppermute | solution.py:352
  15.4 6.9 %collective-permute-start.6 = (bf16[160,768]{1,0:T(8,128)(2,1)S(1)}, bf16[160,768]{1,0:T(8,128)(2,1)S(1)}, u32[]{:S(2)}, u32[]{:S(2)}) collective-permute-start(bf16[160,768]{1,0:T(8,128)(2,1)S(1)} %collective-permute-done.5.refs_1_), channel_id=1, source_target_pairs={{0,16},{1,9},{2,18},{3,11},{4,20},{5,13},{6,22},{7,15},{8,24},{9,1... | collective-permute-start | bytes 737288 | tf_op jit(solution)/shard_map/ppermute | solution.py:353
  20.4 6.5 %collective-permute-start.8 = (bf16[176,768]{1,0:T(8,128)(2,1)S(1)}, bf16[176,768]{1,0:T(8,128)(2,1)S(1)}, u32[]{:S(2)}, u32[]{:S(2)}) collective-permute-start(bf16[176,768]{1,0:T(8,128)(2,1)S(1)} %collective-permute-done.7.refs_2_), channel_id=1, source_target_pairs={{0,16},{1,9},{2,18},{3,11},{4,20},{5,13},{6,22},{7,15},{8,24},{9,1... | collective-permute-start | bytes 811016 | tf_op jit(solution)/shard_map/ppermute | solution.py:353
  22.1 4.8 %collective-permute-start.10 = (bf16[160,768]{1,0:T(8,128)(2,1)S(1)}, bf16[160,768]{1,0:T(8,128)(2,1)S(1)}, u32[]{:S(2)}, u32[]{:S(2)}) collective-permute-start(bf16[160,768]{1,0:T(8,128)(2,1)S(1)} %get-tuple-element.42), channel_id=1, source_target_pairs={{0,1},{1,0},{2,3},{3,2},{4,5},{5,4},{6,7},{7,6},{8,9},{9,8},{10,11... | collective-permute-start | bytes 737288 | tf_op jit(solution)/shard_map/ppermute | solution.py:358
  22.2 4.6 %collective-permute-start.11 = (bf16[160,768]{1,0:T(8,128)(2,1)S(1)}, bf16[160,768]{1,0:T(8,128)(2,1)S(1)}, u32[]{:S(2)}, u32[]{:S(2)}) collective-permute-start(bf16[160,768]{1,0:T(8,128)(2,1)S(1)} %get-tuple-element.43), channel_id=1, source_target_pairs={{0,1},{1,0},{2,3},{3,2},{4,5},{5,4},{6,7},{7,6},{8,9},{9,8},{10,11... | collective-permute-start | bytes 737288 | tf_op jit(solution)/shard_map/ppermute | solution.py:358
  27.0 1.0 %copy-start = (bf16[320,768]{1,0:T(8,128)(2,1)}, bf16[320,768]{1,0:T(8,128)(2,1)S(1)}, u32[]{:S(2)}) copy-start(bf16[320,768]{1,0:T(8,128)(2,1)S(1)} %get-tuple-element.51.first) | copy-start | bytes 1474564
  28.1 2.1 %collective-permute-start.12 = (bf16[336,768]{1,0:T(8,128)(2,1)S(1)}, bf16[336,768]{1,0:T(8,128)(2,1)S(1)}, u32[]{:S(2)}, u32[]{:S(2)}) collective-permute-start(bf16[336,768]{1,0:T(8,128)(2,1)S(1)} %collective-permute-done.4.second), channel_id=1, source_target_pairs={{0,1},{1,0},{2,3},{3,2},{4,5},{5,4},{6,7},{7,6},{8,9},{9,8},{10,11... | collective-permute-start | bytes 1548296 | tf_op jit(solution)/shard_map/ppermute | solution.py:373
  28.6 1.5 %copy-start.1 = (bf16[320,768]{1,0:T(8,128)(2,1)S(1)}, bf16[320,768]{1,0:T(8,128)(2,1)}, u32[]{:S(2)}) copy-start(bf16[320,768]{1,0:T(8,128)(2,1)} %copy-done) | copy-start | bytes 1474564
  32.3 2.8 %collective-permute-start.13 = (f32[1,640]{1,0:T(1,128)S(1)}, f32[1,640]{1,0:T(1,128)S(1)}, u32[]{:S(2)}, u32[]{:S(2)}) collective-permute-start(f32[1,640]{1,0:T(1,128)S(1)} %get-tuple-element.53), channel_id=1, source_target_pairs={{0,1},{1,0},{2,3},{3,2},{4,5},{5,4},{6,7},{7,6},{8,9},{9,8},{10,11... | collective-permute-start | bytes 7688 | tf_op jit(solution)/shard_map/ppermute | solution.py:387
  32.3 4.3 %collective-permute-start.16 = (f32[1,640]{1,0:T(1,128)S(1)}, f32[1,640]{1,0:T(1,128)S(1)}, u32[]{:S(2)}, u32[]{:S(2)}) collective-permute-start(f32[1,640]{1,0:T(1,128)S(1)} %get-tuple-element.55), channel_id=1, source_target_pairs={{0,8},{1,17},{2,10},{3,19},{4,12},{5,21},{6,14},{7,23},{8,0},{9,25... | collective-permute-start | bytes 7688 | tf_op jit(solution)/shard_map/ppermute | solution.py:395
  35.1 6.4 %collective-permute-start.14 = (f32[1,640]{1,0:T(1,128)S(1)}, f32[1,640]{1,0:T(1,128)S(1)}, u32[]{:S(2)}, u32[]{:S(2)}) collective-permute-start(f32[1,640]{1,0:T(1,128)S(1)} %max.24), channel_id=1, source_target_pairs={{2,6},{4,0},{6,4},{1,7},{3,1},{5,3},{10,14},{12,8},{14,12},{9,15},... | collective-permute-start | bytes 7688 | tf_op jit(solution)/shard_map/ppermute | solution.py:390
  36.7 4.8 %collective-permute-start.17 = (f32[1,320]{1,0:T(1,128)S(1)}, f32[1,320]{1,0:T(1,128)S(1)}, u32[]{:S(2)}, u32[]{:S(2)}) collective-permute-start(f32[1,320]{1,0:T(1,128)S(1)} %get-tuple-element.59), channel_id=1, source_target_pairs={{0,17},{1,8},{2,19},{3,10},{4,21},{5,12},{6,23},{7,14},{8,25},{9,0... | collective-permute-start | bytes 3848 | tf_op jit(solution)/shard_map/ppermute | solution.py:398
  38.3 3.2 %collective-permute-start.18 = (f32[1,320]{1,0:T(1,128)S(1)}, f32[1,320]{1,0:T(1,128)S(1)}, u32[]{:S(2)}, u32[]{:S(2)}) collective-permute-start(f32[1,320]{1,0:T(1,128)S(1)} %get-tuple-element.60), channel_id=1, source_target_pairs={{0,1},{1,0},{2,3},{3,2},{4,5},{5,4},{6,7},{7,6},{8,9},{9,8},{10,11... | collective-permute-start | bytes 3848 | tf_op jit(solution)/shard_map/ppermute | solution.py:400
  41.5 1.2 %collective-permute-start.15 = (f32[1,320]{1,0:T(1,128)S(1)}, f32[1,320]{1,0:T(1,128)S(1)}, u32[]{:S(2)}, u32[]{:S(2)}) collective-permute-start(f32[1,320]{1,0:T(1,128)S(1)} %slice.17), channel_id=1, source_target_pairs={{0,1},{1,0},{2,3},{3,2},{4,5},{5,4},{6,7},{7,6},{8,9},{9,8},{10,11... | collective-permute-start | bytes 3848 | tf_op jit(solution)/shard_map/ppermute | solution.py:394

commit v25 on v24

--- a/solution.py
+++ b/solution.py
@@ -315,7 +315,11 @@
     other_core = everywhere(lambda p, g: (p, g ^ 1))
     first = everywhere(lambda p, g: (p ^ (1 + g % 2), g))
     second = everywhere(lambda p, g: (p ^ (2 - g % 2), g))
-    second_home = everywhere(lambda p, g: (p ^ (2 - g % 2), g ^ 1))
+    homes = [
+        everywhere(lambda p, g: (p ^ (1 + g % 2), g ^ 1)),
+        everywhere(lambda p, g: (p ^ (2 - g % 2), g ^ 1)),
+        everywhere(lambda p, g: (p ^ 3, g ^ 1)),
+    ]
 
     rounds = line_rounds(chips)
     rounds += [[]] * (len(rounds) % 2)
@@ -367,7 +371,7 @@
         in_charge.append(mine)
         bests = [best_two, best_rest]
         far = [far_units] + [jnp.concatenate(pieces, axis=0) for pieces in far[1:]]
-        whole, last = [tuple(range(groups))], [(0,), (1, 3), (2,)]
+        whole, last = [tuple(range(groups))], [(at,) for at in range(groups)]
         for at, second_near in enumerate(near_other):
             second_near, *bests = lax.optimization_barrier((second_near, *bests))
             second_far = lax.ppermute(second_near, BOTH, other_core)
@@ -386,16 +390,18 @@
             sent.append(found)
         sent = lax.ppermute(jnp.concatenate(sent, axis=1), BOTH, other_core)
         kept = jnp.maximum(jnp.concatenate(kept, axis=1), sent)
+        kept, *bests = lax.optimization_barrier((kept, *bests))
         for at, pairs in enumerate(rounds):
             found = lax.ppermute(kept[:, 2 * at * rows : 2 * (at + 1) * rows], BOTH, back(pairs))
             me = lax.axis_index(BOTH)
             sender = functools.reduce(jnp.logical_or, [me == source for source, _ in pairs])
             found = jnp.where(sender, found, -1.0)
-            results += [found[:, :rows], lax.ppermute(found[:, rows:], BOTH, other_core)]
-        from_x = lax.ppermute(bests[1], BOTH, first)
-        in_charge += [bests[0], from_x[:, :rows]]
-        onward = jnp.maximum(bests[2], from_x[:, rows:])
-        results.append(lax.ppermute(onward, BOTH, second_home))
+            results.append(found[:, :rows])
+            in_charge.append(found[:, rows:])
+        results += [
+            lax.ppermute(best, BOTH, pairs) for best, pairs in zip(bests[1:], homes)
+        ]
+        in_charge.append(bests[0])
         home = functools.reduce(jnp.maximum, in_charge)
         results.append(lax.ppermute(home, BOTH, other_core))
         return functools.reduce(jnp.maximum, results).reshape(rows)

time: 43.5 us -> 43.2 us (level)
  waiting for transfers between devices: 11.2 us -> 9.51 us
  starting transfers between devices: 24.7 us -> 26 us
    ppermute x1, waiting for transfers between devices: 2.6 us -> 0.01 us  [shards(): lax.ppermute(kept[:, 2 * at * rows:2 * (at + 1) * rows], BOTH, back(pairs))]
    ppermute x3, starting transfers between devices: 4.36 us -> 6.2 us  [shards(): lax.ppermute(best, BOTH, pairs)]
    ppermute x1, waiting for transfers between devices: 0.01 us -> 1.11 us  [shards(): sent = lax.ppermute(jnp.concatenate(sent, axis=1), BOTH, other_core)]
    ppermute x1, starting transfers between devices: 0.52 us -> 0.01 us  [shards(): results.append(lax.ppermute(home, BOTH, other_core))]
    unnamed x10 -> x6, local copies, waits for them, and re-layouts: 1.37 us -> 1.36 us
where the time goes in v25:
time: 43.2 us; the launch traced here: 42.9 us
  starting transfers between devices  26 us (60%)
  waiting for transfers between devices  9.51 us (22%)
  Pallas kernels  5.01 us (12%)
  local copies, waits for them, and re-layouts  1.36 us (3%)
  other arithmetic  0.69 us (2%)
    ppermute x3, starting transfers between devices, shards(): lax.ppermute(best, BOTH, pairs)  6.2 us
    ppermute x1, starting transfers between devices, shards(): raw = [lax.ppermute(embeddings, BOTH, pairs) for pairs in rounds]  5.57 us
    ppermute x2, waiting for transfers between devices, shards(): from_first = [lax.ppermute(part, BOTH, first) for part in parts]  4.28 us
    ppermute x1, starting transfers between devices, shards(): near_other = [lax.ppermute(both, BOTH, pairs) for pairs in rounds]  3.49 us
    ppermute x2, starting transfers between devices, shards(): from_corner = [lax.ppermute(part, BOTH, second) for part in from_first]  2.26 us
    pallas_call x2, Pallas kernels, line(): pl.pallas_call(functools.partial(line_kernel, rows, span, together, len(b...  2.26 us
    ppermute x2, starting transfers between devices, shards(): from_first = [lax.ppermute(part, BOTH, first) for part in parts]  2.09 us
    ppermute x2, starting transfers between devices, shards(): lax.ppermute(piece, BOTH, other_core)  2.03 us
  transfers between devices with their start and end apart: 19, of which 7 were waited for; matrix products, arithmetic and copies ran while one was open for 0% of the time, Pallas kernels for 7%

profile of v25, /device:TPU:0, one launch (start us, length us, event | category | flops | bytes accessed | tf_op | source)
XLA Modules:
  0.0 42.9 jit_solution(14031008316122043716)
XLA Ops:
  0.0 0.5 %collective-permute-start.1 = (bf16[320,768]{1,0:T(8,128)(2,1)}, bf16[320,768]{1,0:T(8,128)(2,1)S(1)}, u32[]{:S(2)}, u32[]{:S(2)}) collective-permute-start(bf16[320,768]{1,0:T(8,128)(2,1)} %embeddings.1), channel_id=1, source_target_pairs={{0,1},{1,0},{2,3},{3,2},{4,5},{5,4},{6,7},{7,6},{8,9},{9,8},{10,11... | collective-permute-start | bytes 1474568 | tf_op jit(solution)/shard_map/ppermute | solution.py:347
  1.0 5.6 %collective-permute-start = (bf16[320,768]{1,0:T(8,128)(2,1)}, bf16[320,768]{1,0:T(8,128)(2,1)S(1)}, u32[]{:S(2)}, u32[]{:S(2)}) collective-permute-start(bf16[320,768]{1,0:T(8,128)(2,1)} %embeddings.1), channel_id=1, source_target_pairs={{6,2},{0,4},{4,6},{7,1},{1,3},{3,5},{14,10},{8,12},{12,14},{15,9},... | collective-permute-start | bytes 1474568 | tf_op jit(solution)/shard_map/ppermute | solution.py:346
  6.8 1.6 %collective-permute-start.5 = (bf16[160,768]{1,0:T(8,128)(2,1)S(1)}, bf16[160,768]{1,0:T(8,128)(2,1)S(1)}, u32[]{:S(2)}, u32[]{:S(2)}) collective-permute-start(bf16[160,768]{1,0:T(8,128)(2,1)S(1)} %get-tuple-element.41), channel_id=1, source_target_pairs={{0,8},{1,17},{2,10},{3,19},{4,12},{5,21},{6,14},{7,23},{8,0},{9,25... | collective-permute-start | bytes 737288 | tf_op jit(solution)/shard_map/ppermute | solution.py:350
  8.3 0.5 %collective-permute-start.7 = (bf16[176,768]{1,0:T(8,128)(2,1)S(1)}, bf16[176,768]{1,0:T(8,128)(2,1)S(1)}, u32[]{:S(2)}, u32[]{:S(2)}) collective-permute-start(bf16[176,768]{1,0:T(8,128)(2,1)S(1)} %get-tuple-element.42), channel_id=1, source_target_pairs={{0,8},{1,17},{2,10},{3,19},{4,12},{5,21},{6,14},{7,23},{8,0},{9,25... | collective-permute-start | bytes 811016 | tf_op jit(solution)/shard_map/ppermute | solution.py:350
  8.9 0.7 %copy-done.1 = s32[320]{0:T(512)S(1)} copy-done((s32[320]{0:T(512)S(1)}, s32[320]{0:T(512)}, u32[]{:S(2)}) %copy-start.1) | copy-done | bytes 1304
  9.5 0.7 %copy-done.2 = s32[320,1]{0,1:T(1,128)S(1)} copy-done((s32[320,1]{0,1:T(1,128)S(1)}, s32[320,1]{0,1:T(1,128)}, u32[]{:S(2)}) %copy-start.2) | copy-done | bytes 1304
  10.2 1.6 %collective-permute-start.9 = (bf16[336,768]{1,0:T(8,128)(2,1)S(1)}, bf16[336,768]{1,0:T(8,128)(2,1)S(1)}, u32[]{:S(2)}, u32[]{:S(2)}) collective-permute-start(bf16[336,768]{1,0:T(8,128)(2,1)S(1)} %get-tuple-element.45.block.refs_0_), channel_id=1, source_target_pairs={{0,16},{1,9},{2,18},{3,11},{4,20},{5,13},{6,22},{7,15},{8,24},{9,1... | collective-permute-start | bytes 1548296 | tf_op jit(solution)/shard_map/ppermute | solution.py:353
  11.9 3.5 %collective-permute-start.4 = (bf16[336,768]{1,0:T(8,128)(2,1)S(1)}, bf16[336,768]{1,0:T(8,128)(2,1)S(1)}, u32[]{:S(2)}, u32[]{:S(2)}) collective-permute-start(bf16[336,768]{1,0:T(8,128)(2,1)S(1)} %shard_map.40), channel_id=1, source_target_pairs={{6,2},{0,4},{4,6},{7,1},{1,3},{3,5},{14,10},{8,12},{12,14},{15,9},... | collective-permute-start | bytes 1548296 | tf_op jit(solution)/shard_map/ppermute | solution.py:356
  15.4 0.7 %collective-permute-start.6 = (bf16[160,768]{1,0:T(8,128)(2,1)S(1)}, bf16[160,768]{1,0:T(8,128)(2,1)S(1)}, u32[]{:S(2)}, u32[]{:S(2)}) collective-permute-start(bf16[160,768]{1,0:T(8,128)(2,1)S(1)} %collective-permute-done.5.refs_1_), channel_id=1, source_target_pairs={{0,16},{1,9},{2,18},{3,11},{4,20},{5,13},{6,22},{7,15},{8,24},{9,1... | collective-permute-start | bytes 737288 | tf_op jit(solution)/shard_map/ppermute | solution.py:357
  16.1 4.3 %collective-permute-done.7.refs_2_ = bf16[176,768]{1,0:T(8,128)(2,1)S(1)} collective-permute-done((bf16[176,768]{1,0:T(8,128)(2,1)S(1)}, bf16[176,768]{1,0:T(8,128)(2,1)S(1)}, u32[]{:S(2)}, u32[]{:S(2)}) %collective-permute-start.7) | collective-permute-done | bytes 270368 | tf_op jit(solution)/shard_map/ppermute | solution.py:350
  20.4 1.5 %collective-permute-start.8 = (bf16[176,768]{1,0:T(8,128)(2,1)S(1)}, bf16[176,768]{1,0:T(8,128)(2,1)S(1)}, u32[]{:S(2)}, u32[]{:S(2)}) collective-permute-start(bf16[176,768]{1,0:T(8,128)(2,1)S(1)} %collective-permute-done.7.refs_2_), channel_id=1, source_target_pairs={{0,16},{1,9},{2,18},{3,11},{4,20},{5,13},{6,22},{7,15},{8,24},{9,1... | collective-permute-start | bytes 811016 | tf_op jit(solution)/shard_map/ppermute | solution.py:357
  22.2 2.0 %collective-permute-start.11 = (bf16[160,768]{1,0:T(8,128)(2,1)S(1)}, bf16[160,768]{1,0:T(8,128)(2,1)S(1)}, u32[]{:S(2)}, u32[]{:S(2)}) collective-permute-start(bf16[160,768]{1,0:T(8,128)(2,1)S(1)} %get-tuple-element.49), channel_id=1, source_target_pairs={{0,1},{1,0},{2,3},{3,2},{4,5},{5,4},{6,7},{7,6},{8,9},{9,8},{10,11... | collective-permute-start | bytes 737288 | tf_op jit(solution)/shard_map/ppermute | solution.py:362
  24.4 1.0 %shard_map.42 = (f32[1,640]{1,0:T(1,128)S(1)}, f32[1,320]{1,0:T(1,128)S(1)}) custom-call(bf16[336,768]{1,0:T(8,128)(2,1)S(1)} %get-tuple-element.45.block.refs_0_, bf16[336,768]{1,0:T(8,128)(2,1)S(1)} %shard_map.41.partner, bf16[336,768]{1,0:T(8,128)(2,1)S(1)} %get-tuple-element.45.block.refs_0_, bf16[160,768]{1,0:T(8,128)(2,1)S(1)} %collective-permute-done.5.refs_1_, ...), custom_call_target="tpu_custom_call" | custom-call | flops 320 | bytes 320 | tf_op jit(solution)/shard_map/pallas_call | solution.py:247
  25.4 1.4 %collective-permute-done.8.refs_5_ = bf16[176,768]{1,0:T(8,128)(2,1)S(1)} collective-permute-done((bf16[176,768]{1,0:T(8,128)(2,1)S(1)}, bf16[176,768]{1,0:T(8,128)(2,1)S(1)}, u32[]{:S(2)}, u32[]{:S(2)}) %collective-permute-start.8) | collective-permute-done | bytes 270368 | tf_op jit(solution)/shard_map/ppermute | solution.py:357
  27.0 1.0 %shard_map.44 = (f32[1,640]{1,0:T(1,128)S(1)}, f32[1,320]{1,0:T(1,128)S(1)}) custom-call(bf16[336,768]{1,0:T(8,128)(2,1)S(1)} %get-tuple-element.45.block.refs_0_, bf16[336,768]{1,0:T(8,128)(2,1)S(1)} %shard_map.41.partner, bf16[1280,768]{1,0:T(8,128)(2,1)S(1)} %get-tuple-element.50.held, f32[1,1280]{1,0:T(1,128)S(1)} %get-tuple-element.51.row), custom_call_target="tpu_custom_call" | custom-call | flops 320 | bytes 320 | tf_op jit(solution)/shard_map/pallas_call | solution.py:263
  28.0 0.6 %collective-permute-start.12 = (bf16[336,768]{1,0:T(8,128)(2,1)S(1)}, bf16[336,768]{1,0:T(8,128)(2,1)S(1)}, u32[]{:S(2)}, u32[]{:S(2)}) collective-permute-start(bf16[336,768]{1,0:T(8,128)(2,1)S(1)} %collective-permute-done.4.second), channel_id=1, source_target_pairs={{0,1},{1,0},{2,3},{3,2},{4,5},{5,4},{6,7},{7,6},{8,9},{9,8},{10,11... | collective-permute-start | bytes 1548296 | tf_op jit(solution)/shard_map/ppermute | solution.py:377
  28.7 1.4 %collective-permute-done.12.second = bf16[336,768]{1,0:T(8,128)(2,1)S(1)} collective-permute-done((bf16[336,768]{1,0:T(8,128)(2,1)S(1)}, bf16[336,768]{1,0:T(8,128)(2,1)S(1)}, u32[]{:S(2)}, u32[]{:S(2)}) %collective-permute-start.12) | collective-permute-done | bytes 516128 | tf_op jit(solution)/shard_map/ppermute | solution.py:377
  30.1 2.1 %shard_map.46 = (f32[1,320]{1,0:T(1,128)S(1)}, f32[1,320]{1,0:T(1,128)S(1)}, f32[1,320]{1,0:T(1,128)S(1)}, f32[1,320]{1,0:T(1,128)S(1)}, f32[1,640]{1,0:T(1,128)S(1)}) custom-call(bf16[320,768]{1,0:T(8,128)(2,1)S(1)} %get-tuple-element.57.first, bf16[336,768]{1,0:T(8,128)(2,1)S(1)} %collective-permute-done.12.second, ...), custom_call_target="tpu_custom_call" | custom-call | flops 320 | bytes 320 | tf_op jit(solution)/shard_map/pallas_call | solution.py:277
  32.3 1.1 %collective-permute-done.13 = f32[1,640]{1,0:T(1,128)S(1)} collective-permute-done((f32[1,640]{1,0:T(1,128)S(1)}, f32[1,640]{1,0:T(1,128)S(1)}, u32[]{:S(2)}, u32[]{:S(2)}) %collective-permute-start.13) | collective-permute-done | bytes 2592 | tf_op jit(solution)/shard_map/ppermute | solution.py:391
  33.4 1.3 %collective-permute-start.14 = (f32[1,640]{1,0:T(1,128)S(1)}, f32[1,640]{1,0:T(1,128)S(1)}, u32[]{:S(2)}, u32[]{:S(2)}) collective-permute-start(f32[1,640]{1,0:T(1,128)S(1)} %max.24), channel_id=1, source_target_pairs={{2,6},{4,0},{6,4},{1,7},{3,1},{5,3},{10,14},{12,8},{14,12},{9,15},... | collective-permute-start | bytes 7688 | tf_op jit(solution)/shard_map/ppermute | solution.py:395
  34.8 3.5 %collective-permute-start.15 = (f32[1,320]{1,0:T(1,128)S(1)}, f32[1,320]{1,0:T(1,128)S(1)}, u32[]{:S(2)}, u32[]{:S(2)}) collective-permute-start(f32[1,320]{1,0:T(1,128)S(1)} %get-tuple-element.65), channel_id=1, source_target_pairs={{0,9},{1,16},{2,11},{3,18},{4,13},{5,20},{6,15},{7,22},{8,1},{9,24... | collective-permute-start | bytes 3848 | tf_op jit(solution)/shard_map/ppermute | solution.py:402
  38.4 2.6 %collective-permute-start.17 = (f32[1,320]{1,0:T(1,128)S(1)}, f32[1,320]{1,0:T(1,128)S(1)}, u32[]{:S(2)}, u32[]{:S(2)}) collective-permute-start(f32[1,320]{1,0:T(1,128)S(1)} %get-tuple-element.67), channel_id=1, source_target_pairs={{0,25},{1,24},{2,27},{3,26},{4,29},{5,28},{6,31},{7,30},{8,17},{9,... | collective-permute-start | bytes 3848 | tf_op jit(solution)/shard_map/ppermute | solution.py:402
  41.3 1.0 %collective-permute-done.17 = f32[1,320]{1,0:T(1,128)S(1)} collective-permute-done((f32[1,320]{1,0:T(1,128)S(1)}, f32[1,320]{1,0:T(1,128)S(1)}, u32[]{:S(2)}, u32[]{:S(2)}) %collective-permute-start.17) | collective-permute-done | bytes 1312 | tf_op jit(solution)/shard_map/ppermute | solution.py:402
  42.3 0.6 %maximum_reduce_fusion = f32[320]{0:T(512)} fusion(f32[1,320]{1,0:T(1,128)S(1)} %collective-permute-done.18, f32[1,320]{1,0:T(1,128)S(1)} %collective-permute-done.17, f32[1,320]{1,0:T(1,128)S(1)} %collective-permute-done.16, f32[1,320]{1,0:T(1,128)S(1)} %collective-permute-done.15, f32[1,640]{1,0:T(1,128)S(1)} %broadcast_select_fusion), kind=kLoop, calls=%fused_computation.6 | loop fusion | flops 1280 | bytes 7680 | tf_op jit(solution)/shard_map/max | solution.py:407
  (34 shorter events, 2.0 us)
Async XLA Ops:
  0.0 24.2 %copy-start = (bf16[320,768]{1,0:T(8,128)(2,1)S(1)}, bf16[320,768]{1,0:T(8,128)(2,1)}, u32[]{:S(2)}) copy-start(bf16[320,768]{1,0:T(8,128)(2,1)} %embeddings.1) | copy-start | bytes 1474564
  0.0 6.6 %collective-permute-start.1 = (bf16[320,768]{1,0:T(8,128)(2,1)}, bf16[320,768]{1,0:T(8,128)(2,1)S(1)}, u32[]{:S(2)}, u32[]{:S(2)}) collective-permute-start(bf16[320,768]{1,0:T(8,128)(2,1)} %embeddings.1), channel_id=1, source_target_pairs={{0,1},{1,0},{2,3},{3,2},{4,5},{5,4},{6,7},{7,6},{8,9},{9,8},{10,11... | collective-permute-start | bytes 1474568 | tf_op jit(solution)/shard_map/ppermute | solution.py:347
  0.5 6.1 %collective-permute-start.2 = (s32[1,320]{1,0:T(1,128)}, s32[1,320]{1,0:T(1,128)S(1)}, u32[]{:S(2)}, u32[]{:S(2)}) collective-permute-start(s32[1,320]{1,0:T(1,128)} %bitcast.1), channel_id=1, source_target_pairs={{0,1},{1,0},{2,3},{3,2},{4,5},{5,4},{6,7},{7,6},{8,9},{9,8},{10,11... | collective-permute-start | bytes 3848 | tf_op jit(solution)/shard_map/ppermute | solution.py:347
  0.5 6.0 %collective-permute-start.3 = (s32[320]{0:T(512)}, s32[320]{0:T(512)S(1)}, u32[]{:S(2)}, u32[]{:S(2)}) collective-permute-start(s32[320]{0:T(512)} %order_key.1), channel_id=1, source_target_pairs={{0,1},{1,0},{2,3},{3,2},{4,5},{5,4},{6,7},{7,6},{8,9},{9,8},{10,11... | collective-permute-start | bytes 3848 | tf_op jit(solution)/shard_map/ppermute | solution.py:347
  1.0 20.9 %collective-permute-start = (bf16[320,768]{1,0:T(8,128)(2,1)}, bf16[320,768]{1,0:T(8,128)(2,1)S(1)}, u32[]{:S(2)}, u32[]{:S(2)}) collective-permute-start(bf16[320,768]{1,0:T(8,128)(2,1)} %embeddings.1), channel_id=1, source_target_pairs={{6,2},{0,4},{4,6},{7,1},{1,3},{3,5},{14,10},{8,12},{12,14},{15,9},... | collective-permute-start | bytes 1474568 | tf_op jit(solution)/shard_map/ppermute | solution.py:346
  6.8 8.6 %collective-permute-start.5 = (bf16[160,768]{1,0:T(8,128)(2,1)S(1)}, bf16[160,768]{1,0:T(8,128)(2,1)S(1)}, u32[]{:S(2)}, u32[]{:S(2)}) collective-permute-start(bf16[160,768]{1,0:T(8,128)(2,1)S(1)} %get-tuple-element.41), channel_id=1, source_target_pairs={{0,8},{1,17},{2,10},{3,19},{4,12},{5,21},{6,14},{7,23},{8,0},{9,25... | collective-permute-start | bytes 737288 | tf_op jit(solution)/shard_map/ppermute | solution.py:350
  8.3 12.1 %collective-permute-start.7 = (bf16[176,768]{1,0:T(8,128)(2,1)S(1)}, bf16[176,768]{1,0:T(8,128)(2,1)S(1)}, u32[]{:S(2)}, u32[]{:S(2)}) collective-permute-start(bf16[176,768]{1,0:T(8,128)(2,1)S(1)} %get-tuple-element.42), channel_id=1, source_target_pairs={{0,8},{1,17},{2,10},{3,19},{4,12},{5,21},{6,14},{7,23},{8,0},{9,25... | collective-permute-start | bytes 811016 | tf_op jit(solution)/shard_map/ppermute | solution.py:350
  8.9 0.7 %copy-start.1 = (s32[320]{0:T(512)S(1)}, s32[320]{0:T(512)}, u32[]{:S(2)}) copy-start(s32[320]{0:T(512)} %order_key.1) | copy-start | bytes 3844
  9.5 0.7 %copy-start.2 = (s32[320,1]{0,1:T(1,128)S(1)}, s32[320,1]{0,1:T(1,128)}, u32[]{:S(2)}) copy-start(s32[320,1]{0,1:T(1,128)} %param.4) | copy-start | bytes 3844
  10.2 16.6 %collective-permute-start.9 = (bf16[336,768]{1,0:T(8,128)(2,1)S(1)}, bf16[336,768]{1,0:T(8,128)(2,1)S(1)}, u32[]{:S(2)}, u32[]{:S(2)}) collective-permute-start(bf16[336,768]{1,0:T(8,128)(2,1)S(1)} %get-tuple-element.45.block.refs_0_), channel_id=1, source_target_pairs={{0,16},{1,9},{2,18},{3,11},{4,20},{5,13},{6,22},{7,15},{8,24},{9,1... | collective-permute-start | bytes 1548296 | tf_op jit(solution)/shard_map/ppermute | solution.py:353
  11.9 16.2 %collective-permute-start.4 = (bf16[336,768]{1,0:T(8,128)(2,1)S(1)}, bf16[336,768]{1,0:T(8,128)(2,1)S(1)}, u32[]{:S(2)}, u32[]{:S(2)}) collective-permute-start(bf16[336,768]{1,0:T(8,128)(2,1)S(1)} %shard_map.40), channel_id=1, source_target_pairs={{6,2},{0,4},{4,6},{7,1},{1,3},{3,5},{14,10},{8,12},{12,14},{15,9},... | collective-permute-start | bytes 1548296 | tf_op jit(solution)/shard_map/ppermute | solution.py:356
  15.4 6.9 %collective-permute-start.6 = (bf16[160,768]{1,0:T(8,128)(2,1)S(1)}, bf16[160,768]{1,0:T(8,128)(2,1)S(1)}, u32[]{:S(2)}, u32[]{:S(2)}) collective-permute-start(bf16[160,768]{1,0:T(8,128)(2,1)S(1)} %collective-permute-done.5.refs_1_), channel_id=1, source_target_pairs={{0,16},{1,9},{2,18},{3,11},{4,20},{5,13},{6,22},{7,15},{8,24},{9,1... | collective-permute-start | bytes 737288 | tf_op jit(solution)/shard_map/ppermute | solution.py:357
  20.4 6.5 %collective-permute-start.8 = (bf16[176,768]{1,0:T(8,128)(2,1)S(1)}, bf16[176,768]{1,0:T(8,128)(2,1)S(1)}, u32[]{:S(2)}, u32[]{:S(2)}) collective-permute-start(bf16[176,768]{1,0:T(8,128)(2,1)S(1)} %collective-permute-done.7.refs_2_), channel_id=1, source_target_pairs={{0,16},{1,9},{2,18},{3,11},{4,20},{5,13},{6,22},{7,15},{8,24},{9,1... | collective-permute-start | bytes 811016 | tf_op jit(solution)/shard_map/ppermute | solution.py:357
  22.1 4.8 %collective-permute-start.10 = (bf16[160,768]{1,0:T(8,128)(2,1)S(1)}, bf16[160,768]{1,0:T(8,128)(2,1)S(1)}, u32[]{:S(2)}, u32[]{:S(2)}) collective-permute-start(bf16[160,768]{1,0:T(8,128)(2,1)S(1)} %get-tuple-element.48), channel_id=1, source_target_pairs={{0,1},{1,0},{2,3},{3,2},{4,5},{5,4},{6,7},{7,6},{8,9},{9,8},{10,11... | collective-permute-start | bytes 737288 | tf_op jit(solution)/shard_map/ppermute | solution.py:362
  22.2 4.6 %collective-permute-start.11 = (bf16[160,768]{1,0:T(8,128)(2,1)S(1)}, bf16[160,768]{1,0:T(8,128)(2,1)S(1)}, u32[]{:S(2)}, u32[]{:S(2)}) collective-permute-start(bf16[160,768]{1,0:T(8,128)(2,1)S(1)} %get-tuple-element.49), channel_id=1, source_target_pairs={{0,1},{1,0},{2,3},{3,2},{4,5},{5,4},{6,7},{7,6},{8,9},{9,8},{10,11... | collective-permute-start | bytes 737288 | tf_op jit(solution)/shard_map/ppermute | solution.py:362
  28.0 2.1 %collective-permute-start.12 = (bf16[336,768]{1,0:T(8,128)(2,1)S(1)}, bf16[336,768]{1,0:T(8,128)(2,1)S(1)}, u32[]{:S(2)}, u32[]{:S(2)}) collective-permute-start(bf16[336,768]{1,0:T(8,128)(2,1)S(1)} %collective-permute-done.4.second), channel_id=1, source_target_pairs={{0,1},{1,0},{2,3},{3,2},{4,5},{5,4},{6,7},{7,6},{8,9},{9,8},{10,11... | collective-permute-start | bytes 1548296 | tf_op jit(solution)/shard_map/ppermute | solution.py:377
  32.2 1.2 %collective-permute-start.13 = (f32[1,640]{1,0:T(1,128)S(1)}, f32[1,640]{1,0:T(1,128)S(1)}, u32[]{:S(2)}, u32[]{:S(2)}) collective-permute-start(f32[1,640]{1,0:T(1,128)S(1)} %get-tuple-element.59), channel_id=1, source_target_pairs={{0,1},{1,0},{2,3},{3,2},{4,5},{5,4},{6,7},{7,6},{8,9},{9,8},{10,11... | collective-permute-start | bytes 7688 | tf_op jit(solution)/shard_map/ppermute | solution.py:391
  33.4 7.6 %collective-permute-start.14 = (f32[1,640]{1,0:T(1,128)S(1)}, f32[1,640]{1,0:T(1,128)S(1)}, u32[]{:S(2)}, u32[]{:S(2)}) collective-permute-start(f32[1,640]{1,0:T(1,128)S(1)} %max.24), channel_id=1, source_target_pairs={{2,6},{4,0},{6,4},{1,7},{3,1},{5,3},{10,14},{12,8},{14,12},{9,15},... | collective-permute-start | bytes 7688 | tf_op jit(solution)/shard_map/ppermute | solution.py:395
  34.8 6.3 %collective-permute-start.15 = (f32[1,320]{1,0:T(1,128)S(1)}, f32[1,320]{1,0:T(1,128)S(1)}, u32[]{:S(2)}, u32[]{:S(2)}) collective-permute-start(f32[1,320]{1,0:T(1,128)S(1)} %get-tuple-element.65), channel_id=1, source_target_pairs={{0,9},{1,16},{2,11},{3,18},{4,13},{5,20},{6,15},{7,22},{8,1},{9,24... | collective-permute-start | bytes 3848 | tf_op jit(solution)/shard_map/ppermute | solution.py:402
  38.3 3.0 %collective-permute-start.16 = (f32[1,320]{1,0:T(1,128)S(1)}, f32[1,320]{1,0:T(1,128)S(1)}, u32[]{:S(2)}, u32[]{:S(2)}) collective-permute-start(f32[1,320]{1,0:T(1,128)S(1)} %get-tuple-element.66), channel_id=1, source_target_pairs={{0,17},{1,8},{2,19},{3,10},{4,21},{5,12},{6,23},{7,14},{8,25},{9,0... | collective-permute-start | bytes 3848 | tf_op jit(solution)/shard_map/ppermute | solution.py:402
  38.4 3.9 %collective-permute-start.17 = (f32[1,320]{1,0:T(1,128)S(1)}, f32[1,320]{1,0:T(1,128)S(1)}, u32[]{:S(2)}, u32[]{:S(2)}) collective-permute-start(f32[1,320]{1,0:T(1,128)S(1)} %get-tuple-element.67), channel_id=1, source_target_pairs={{0,25},{1,24},{2,27},{3,26},{4,29},{5,28},{6,31},{7,30},{8,17},{9,... | collective-permute-start | bytes 3848 | tf_op jit(solution)/shard_map/ppermute | solution.py:402
  41.1 1.2 %collective-permute-start.18 = (f32[1,320]{1,0:T(1,128)S(1)}, f32[1,320]{1,0:T(1,128)S(1)}, u32[]{:S(2)}, u32[]{:S(2)}) collective-permute-start(f32[1,320]{1,0:T(1,128)S(1)} %fusion), channel_id=1, source_target_pairs={{0,1},{1,0},{2,3},{3,2},{4,5},{5,4},{6,7},{7,6},{8,9},{9,8},{10,11... | collective-permute-start | bytes 3848 | tf_op jit(solution)/shard_map/ppermute | solution.py:406

commit v26 on v25

--- a/solution.py
+++ b/solution.py
@@ -398,9 +398,7 @@
             found = jnp.where(sender, found, -1.0)
             results.append(found[:, :rows])
             in_charge.append(found[:, rows:])
-        results += [
-            lax.ppermute(best, BOTH, pairs) for best, pairs in zip(bests[1:], homes)
-        ]
+        results += [lax.ppermute(bests[at], BOTH, homes[at - 1]) for at in (3, 1, 2)]
         in_charge.append(bests[0])
         home = functools.reduce(jnp.maximum, in_charge)
         results.append(lax.ppermute(home, BOTH, other_core))

time: 43.2 us -> 43.3 us (level)
  transfers between devices with their start and end apart: 19 -> 19, of which waited for: 7 -> 6; matrix products, arithmetic and copies ran while one was open for 0% -> 0% of each run, Pallas kernels for 7% -> 7%
where the time goes in v26:
time: 43.3 us; the launch traced here: 42.9 us
  starting transfers between devices  26.1 us (60%)
  waiting for transfers between devices  9.51 us (22%)
  Pallas kernels  5.01 us (12%)
  local copies, waits for them, and re-layouts  1.36 us (3%)
  other arithmetic  0.69 us (2%)
    ppermute x3, starting transfers between devices, shards(): lax.ppermute(bests[at], BOTH, homes[at - 1])  6.21 us
    ppermute x1, starting transfers between devices, shards(): raw = [lax.ppermute(embeddings, BOTH, pairs) for pairs in rounds]  5.57 us
    ppermute x2, waiting for transfers between devices, shards(): from_first = [lax.ppermute(part, BOTH, first) for part in parts]  4.28 us
    ppermute x1, starting transfers between devices, shards(): near_other = [lax.ppermute(both, BOTH, pairs) for pairs in rounds]  3.49 us
    ppermute x2, starting transfers between devices, shards(): from_corner = [lax.ppermute(part, BOTH, second) for part in from_first]  2.26 us
    pallas_call x2, Pallas kernels, line(): pl.pallas_call(functools.partial(line_kernel, rows, span, together, len(b...  2.26 us
    ppermute x2, starting transfers between devices, shards(): from_first = [lax.ppermute(part, BOTH, first) for part in parts]  2.09 us
    ppermute x2, starting transfers between devices, shards(): lax.ppermute(piece, BOTH, other_core)  2.03 us
  transfers between devices with their start and end apart: 19, of which 6 were waited for; matrix products, arithmetic and copies ran while one was open for 0% of the time, Pallas kernels for 7%

profile of v26, /device:TPU:0, one launch (start us, length us, event | category | flops | bytes accessed | tf_op | source)
XLA Modules:
  0.0 42.9 jit_solution(15968498527044409304)
XLA Ops:
  0.0 0.5 %collective-permute-start.1 = (bf16[320,768]{1,0:T(8,128)(2,1)}, bf16[320,768]{1,0:T(8,128)(2,1)S(1)}, u32[]{:S(2)}, u32[]{:S(2)}) collective-permute-start(bf16[320,768]{1,0:T(8,128)(2,1)} %embeddings.1), channel_id=1, source_target_pairs={{0,1},{1,0},{2,3},{3,2},{4,5},{5,4},{6,7},{7,6},{8,9},{9,8},{10,11... | collective-permute-start | bytes 1474568 | tf_op jit(solution)/shard_map/ppermute | solution.py:347
  1.0 5.6 %collective-permute-start = (bf16[320,768]{1,0:T(8,128)(2,1)}, bf16[320,768]{1,0:T(8,128)(2,1)S(1)}, u32[]{:S(2)}, u32[]{:S(2)}) collective-permute-start(bf16[320,768]{1,0:T(8,128)(2,1)} %embeddings.1), channel_id=1, source_target_pairs={{6,2},{0,4},{4,6},{7,1},{1,3},{3,5},{14,10},{8,12},{12,14},{15,9},... | collective-permute-start | bytes 1474568 | tf_op jit(solution)/shard_map/ppermute | solution.py:346
  6.8 1.6 %collective-permute-start.5 = (bf16[160,768]{1,0:T(8,128)(2,1)S(1)}, bf16[160,768]{1,0:T(8,128)(2,1)S(1)}, u32[]{:S(2)}, u32[]{:S(2)}) collective-permute-start(bf16[160,768]{1,0:T(8,128)(2,1)S(1)} %get-tuple-element.41), channel_id=1, source_target_pairs={{0,8},{1,17},{2,10},{3,19},{4,12},{5,21},{6,14},{7,23},{8,0},{9,25... | collective-permute-start | bytes 737288 | tf_op jit(solution)/shard_map/ppermute | solution.py:350
  8.3 0.5 %collective-permute-start.7 = (bf16[176,768]{1,0:T(8,128)(2,1)S(1)}, bf16[176,768]{1,0:T(8,128)(2,1)S(1)}, u32[]{:S(2)}, u32[]{:S(2)}) collective-permute-start(bf16[176,768]{1,0:T(8,128)(2,1)S(1)} %get-tuple-element.42), channel_id=1, source_target_pairs={{0,8},{1,17},{2,10},{3,19},{4,12},{5,21},{6,14},{7,23},{8,0},{9,25... | collective-permute-start | bytes 811016 | tf_op jit(solution)/shard_map/ppermute | solution.py:350
  8.9 0.7 %copy-done.1 = s32[320]{0:T(512)S(1)} copy-done((s32[320]{0:T(512)S(1)}, s32[320]{0:T(512)}, u32[]{:S(2)}) %copy-start.1) | copy-done | bytes 1304
  9.5 0.7 %copy-done.2 = s32[320,1]{0,1:T(1,128)S(1)} copy-done((s32[320,1]{0,1:T(1,128)S(1)}, s32[320,1]{0,1:T(1,128)}, u32[]{:S(2)}) %copy-start.2) | copy-done | bytes 1304
  10.2 1.6 %collective-permute-start.9 = (bf16[336,768]{1,0:T(8,128)(2,1)S(1)}, bf16[336,768]{1,0:T(8,128)(2,1)S(1)}, u32[]{:S(2)}, u32[]{:S(2)}) collective-permute-start(bf16[336,768]{1,0:T(8,128)(2,1)S(1)} %get-tuple-element.45.block.refs_0_), channel_id=1, source_target_pairs={{0,16},{1,9},{2,18},{3,11},{4,20},{5,13},{6,22},{7,15},{8,24},{9,1... | collective-permute-start | bytes 1548296 | tf_op jit(solution)/shard_map/ppermute | solution.py:353
  11.9 3.5 %collective-permute-start.4 = (bf16[336,768]{1,0:T(8,128)(2,1)S(1)}, bf16[336,768]{1,0:T(8,128)(2,1)S(1)}, u32[]{:S(2)}, u32[]{:S(2)}) collective-permute-start(bf16[336,768]{1,0:T(8,128)(2,1)S(1)} %shard_map.40), channel_id=1, source_target_pairs={{6,2},{0,4},{4,6},{7,1},{1,3},{3,5},{14,10},{8,12},{12,14},{15,9},... | collective-permute-start | bytes 1548296 | tf_op jit(solution)/shard_map/ppermute | solution.py:356
  15.4 0.7 %collective-permute-start.6 = (bf16[160,768]{1,0:T(8,128)(2,1)S(1)}, bf16[160,768]{1,0:T(8,128)(2,1)S(1)}, u32[]{:S(2)}, u32[]{:S(2)}) collective-permute-start(bf16[160,768]{1,0:T(8,128)(2,1)S(1)} %collective-permute-done.5.refs_1_), channel_id=1, source_target_pairs={{0,16},{1,9},{2,18},{3,11},{4,20},{5,13},{6,22},{7,15},{8,24},{9,1... | collective-permute-start | bytes 737288 | tf_op jit(solution)/shard_map/ppermute | solution.py:357
  16.1 4.3 %collective-permute-done.7.refs_2_ = bf16[176,768]{1,0:T(8,128)(2,1)S(1)} collective-permute-done((bf16[176,768]{1,0:T(8,128)(2,1)S(1)}, bf16[176,768]{1,0:T(8,128)(2,1)S(1)}, u32[]{:S(2)}, u32[]{:S(2)}) %collective-permute-start.7) | collective-permute-done | bytes 270368 | tf_op jit(solution)/shard_map/ppermute | solution.py:350
  20.4 1.5 %collective-permute-start.8 = (bf16[176,768]{1,0:T(8,128)(2,1)S(1)}, bf16[176,768]{1,0:T(8,128)(2,1)S(1)}, u32[]{:S(2)}, u32[]{:S(2)}) collective-permute-start(bf16[176,768]{1,0:T(8,128)(2,1)S(1)} %collective-permute-done.7.refs_2_), channel_id=1, source_target_pairs={{0,16},{1,9},{2,18},{3,11},{4,20},{5,13},{6,22},{7,15},{8,24},{9,1... | collective-permute-start | bytes 811016 | tf_op jit(solution)/shard_map/ppermute | solution.py:357
  22.2 2.0 %collective-permute-start.11 = (bf16[160,768]{1,0:T(8,128)(2,1)S(1)}, bf16[160,768]{1,0:T(8,128)(2,1)S(1)}, u32[]{:S(2)}, u32[]{:S(2)}) collective-permute-start(bf16[160,768]{1,0:T(8,128)(2,1)S(1)} %get-tuple-element.49), channel_id=1, source_target_pairs={{0,1},{1,0},{2,3},{3,2},{4,5},{5,4},{6,7},{7,6},{8,9},{9,8},{10,11... | collective-permute-start | bytes 737288 | tf_op jit(solution)/shard_map/ppermute | solution.py:362
  24.4 1.0 %shard_map.42 = (f32[1,640]{1,0:T(1,128)S(1)}, f32[1,320]{1,0:T(1,128)S(1)}) custom-call(bf16[336,768]{1,0:T(8,128)(2,1)S(1)} %get-tuple-element.45.block.refs_0_, bf16[336,768]{1,0:T(8,128)(2,1)S(1)} %shard_map.41.partner, bf16[336,768]{1,0:T(8,128)(2,1)S(1)} %get-tuple-element.45.block.refs_0_, bf16[160,768]{1,0:T(8,128)(2,1)S(1)} %collective-permute-done.5.refs_1_, ...), custom_call_target="tpu_custom_call" | custom-call | flops 320 | bytes 320 | tf_op jit(solution)/shard_map/pallas_call | solution.py:247
  25.4 1.4 %collective-permute-done.8.refs_5_ = bf16[176,768]{1,0:T(8,128)(2,1)S(1)} collective-permute-done((bf16[176,768]{1,0:T(8,128)(2,1)S(1)}, bf16[176,768]{1,0:T(8,128)(2,1)S(1)}, u32[]{:S(2)}, u32[]{:S(2)}) %collective-permute-start.8) | collective-permute-done | bytes 270368 | tf_op jit(solution)/shard_map/ppermute | solution.py:357
  27.0 1.0 %shard_map.44 = (f32[1,640]{1,0:T(1,128)S(1)}, f32[1,320]{1,0:T(1,128)S(1)}) custom-call(bf16[336,768]{1,0:T(8,128)(2,1)S(1)} %get-tuple-element.45.block.refs_0_, bf16[336,768]{1,0:T(8,128)(2,1)S(1)} %shard_map.41.partner, bf16[1280,768]{1,0:T(8,128)(2,1)S(1)} %get-tuple-element.50.held, f32[1,1280]{1,0:T(1,128)S(1)} %get-tuple-element.51.row), custom_call_target="tpu_custom_call" | custom-call | flops 320 | bytes 320 | tf_op jit(solution)/shard_map/pallas_call | solution.py:263
  28.0 0.6 %collective-permute-start.12 = (bf16[336,768]{1,0:T(8,128)(2,1)S(1)}, bf16[336,768]{1,0:T(8,128)(2,1)S(1)}, u32[]{:S(2)}, u32[]{:S(2)}) collective-permute-start(bf16[336,768]{1,0:T(8,128)(2,1)S(1)} %collective-permute-done.4.second), channel_id=1, source_target_pairs={{0,1},{1,0},{2,3},{3,2},{4,5},{5,4},{6,7},{7,6},{8,9},{9,8},{10,11... | collective-permute-start | bytes 1548296 | tf_op jit(solution)/shard_map/ppermute | solution.py:377
  28.7 1.4 %collective-permute-done.12.second = bf16[336,768]{1,0:T(8,128)(2,1)S(1)} collective-permute-done((bf16[336,768]{1,0:T(8,128)(2,1)S(1)}, bf16[336,768]{1,0:T(8,128)(2,1)S(1)}, u32[]{:S(2)}, u32[]{:S(2)}) %collective-permute-start.12) | collective-permute-done | bytes 516128 | tf_op jit(solution)/shard_map/ppermute | solution.py:377
  30.1 2.1 %shard_map.46 = (f32[1,320]{1,0:T(1,128)S(1)}, f32[1,320]{1,0:T(1,128)S(1)}, f32[1,320]{1,0:T(1,128)S(1)}, f32[1,320]{1,0:T(1,128)S(1)}, f32[1,640]{1,0:T(1,128)S(1)}) custom-call(bf16[320,768]{1,0:T(8,128)(2,1)S(1)} %get-tuple-element.57.first, bf16[336,768]{1,0:T(8,128)(2,1)S(1)} %collective-permute-done.12.second, ...), custom_call_target="tpu_custom_call" | custom-call | flops 320 | bytes 320 | tf_op jit(solution)/shard_map/pallas_call | solution.py:277
  32.3 1.1 %collective-permute-done.13 = f32[1,640]{1,0:T(1,128)S(1)} collective-permute-done((f32[1,640]{1,0:T(1,128)S(1)}, f32[1,640]{1,0:T(1,128)S(1)}, u32[]{:S(2)}, u32[]{:S(2)}) %collective-permute-start.13) | collective-permute-done | bytes 2592 | tf_op jit(solution)/shard_map/ppermute | solution.py:391
  33.4 1.3 %collective-permute-start.14 = (f32[1,640]{1,0:T(1,128)S(1)}, f32[1,640]{1,0:T(1,128)S(1)}, u32[]{:S(2)}, u32[]{:S(2)}) collective-permute-start(f32[1,640]{1,0:T(1,128)S(1)} %max.24), channel_id=1, source_target_pairs={{2,6},{4,0},{6,4},{1,7},{3,1},{5,3},{10,14},{12,8},{14,12},{9,15},... | collective-permute-start | bytes 7688 | tf_op jit(solution)/shard_map/ppermute | solution.py:395
  34.8 4.5 %collective-permute-start.15 = (f32[1,320]{1,0:T(1,128)S(1)}, f32[1,320]{1,0:T(1,128)S(1)}, u32[]{:S(2)}, u32[]{:S(2)}) collective-permute-start(f32[1,320]{1,0:T(1,128)S(1)} %get-tuple-element.65), channel_id=1, source_target_pairs={{0,25},{1,24},{2,27},{3,26},{4,29},{5,28},{6,31},{7,30},{8,17},{9,... | collective-permute-start | bytes 3848 | tf_op jit(solution)/shard_map/ppermute | solution.py:401
  39.3 1.7 %collective-permute-start.17 = (f32[1,320]{1,0:T(1,128)S(1)}, f32[1,320]{1,0:T(1,128)S(1)}, u32[]{:S(2)}, u32[]{:S(2)}) collective-permute-start(f32[1,320]{1,0:T(1,128)S(1)} %get-tuple-element.67), channel_id=1, source_target_pairs={{0,17},{1,8},{2,19},{3,10},{4,21},{5,12},{6,23},{7,14},{8,25},{9,0... | collective-permute-start | bytes 3848 | tf_op jit(solution)/shard_map/ppermute | solution.py:401
  41.1 1.1 %collective-permute-done.16 = f32[1,320]{1,0:T(1,128)S(1)} collective-permute-done((f32[1,320]{1,0:T(1,128)S(1)}, f32[1,320]{1,0:T(1,128)S(1)}, u32[]{:S(2)}, u32[]{:S(2)}) %collective-permute-start.16) | collective-permute-done | bytes 1312 | tf_op jit(solution)/shard_map/ppermute | solution.py:401
  42.3 0.6 %maximum_reduce_fusion = f32[320]{0:T(512)} fusion(f32[1,320]{1,0:T(1,128)S(1)} %collective-permute-done.18, f32[1,320]{1,0:T(1,128)S(1)} %collective-permute-done.17, f32[1,320]{1,0:T(1,128)S(1)} %collective-permute-done.16, f32[1,320]{1,0:T(1,128)S(1)} %collective-permute-done.15, f32[1,640]{1,0:T(1,128)S(1)} %broadcast_select_fusion), kind=kLoop, calls=%fused_computation.6 | loop fusion | flops 1280 | bytes 7680 | tf_op jit(solution)/shard_map/max | solution.py:405
  (34 shorter events, 1.8 us)
Async XLA Ops:
  0.0 24.2 %copy-start = (bf16[320,768]{1,0:T(8,128)(2,1)S(1)}, bf16[320,768]{1,0:T(8,128)(2,1)}, u32[]{:S(2)}) copy-start(bf16[320,768]{1,0:T(8,128)(2,1)} %embeddings.1) | copy-start | bytes 1474564
  0.0 6.6 %collective-permute-start.1 = (bf16[320,768]{1,0:T(8,128)(2,1)}, bf16[320,768]{1,0:T(8,128)(2,1)S(1)}, u32[]{:S(2)}, u32[]{:S(2)}) collective-permute-start(bf16[320,768]{1,0:T(8,128)(2,1)} %embeddings.1), channel_id=1, source_target_pairs={{0,1},{1,0},{2,3},{3,2},{4,5},{5,4},{6,7},{7,6},{8,9},{9,8},{10,11... | collective-permute-start | bytes 1474568 | tf_op jit(solution)/shard_map/ppermute | solution.py:347
  0.5 6.1 %collective-permute-start.2 = (s32[1,320]{1,0:T(1,128)}, s32[1,320]{1,0:T(1,128)S(1)}, u32[]{:S(2)}, u32[]{:S(2)}) collective-permute-start(s32[1,320]{1,0:T(1,128)} %bitcast.1), channel_id=1, source_target_pairs={{0,1},{1,0},{2,3},{3,2},{4,5},{5,4},{6,7},{7,6},{8,9},{9,8},{10,11... | collective-permute-start | bytes 3848 | tf_op jit(solution)/shard_map/ppermute | solution.py:347
  0.5 6.0 %collective-permute-start.3 = (s32[320]{0:T(512)}, s32[320]{0:T(512)S(1)}, u32[]{:S(2)}, u32[]{:S(2)}) collective-permute-start(s32[320]{0:T(512)} %order_key.1), channel_id=1, source_target_pairs={{0,1},{1,0},{2,3},{3,2},{4,5},{5,4},{6,7},{7,6},{8,9},{9,8},{10,11... | collective-permute-start | bytes 3848 | tf_op jit(solution)/shard_map/ppermute | solution.py:347
  1.0 20.9 %collective-permute-start = (bf16[320,768]{1,0:T(8,128)(2,1)}, bf16[320,768]{1,0:T(8,128)(2,1)S(1)}, u32[]{:S(2)}, u32[]{:S(2)}) collective-permute-start(bf16[320,768]{1,0:T(8,128)(2,1)} %embeddings.1), channel_id=1, source_target_pairs={{6,2},{0,4},{4,6},{7,1},{1,3},{3,5},{14,10},{8,12},{12,14},{15,9},... | collective-permute-start | bytes 1474568 | tf_op jit(solution)/shard_map/ppermute | solution.py:346
  6.8 8.6 %collective-permute-start.5 = (bf16[160,768]{1,0:T(8,128)(2,1)S(1)}, bf16[160,768]{1,0:T(8,128)(2,1)S(1)}, u32[]{:S(2)}, u32[]{:S(2)}) collective-permute-start(bf16[160,768]{1,0:T(8,128)(2,1)S(1)} %get-tuple-element.41), channel_id=1, source_target_pairs={{0,8},{1,17},{2,10},{3,19},{4,12},{5,21},{6,14},{7,23},{8,0},{9,25... | collective-permute-start | bytes 737288 | tf_op jit(solution)/shard_map/ppermute | solution.py:350
  8.3 12.1 %collective-permute-start.7 = (bf16[176,768]{1,0:T(8,128)(2,1)S(1)}, bf16[176,768]{1,0:T(8,128)(2,1)S(1)}, u32[]{:S(2)}, u32[]{:S(2)}) collective-permute-start(bf16[176,768]{1,0:T(8,128)(2,1)S(1)} %get-tuple-element.42), channel_id=1, source_target_pairs={{0,8},{1,17},{2,10},{3,19},{4,12},{5,21},{6,14},{7,23},{8,0},{9,25... | collective-permute-start | bytes 811016 | tf_op jit(solution)/shard_map/ppermute | solution.py:350
  8.9 0.7 %copy-start.1 = (s32[320]{0:T(512)S(1)}, s32[320]{0:T(512)}, u32[]{:S(2)}) copy-start(s32[320]{0:T(512)} %order_key.1) | copy-start | bytes 3844
  9.5 0.7 %copy-start.2 = (s32[320,1]{0,1:T(1,128)S(1)}, s32[320,1]{0,1:T(1,128)}, u32[]{:S(2)}) copy-start(s32[320,1]{0,1:T(1,128)} %param.4) | copy-start | bytes 3844
  10.2 16.6 %collective-permute-start.9 = (bf16[336,768]{1,0:T(8,128)(2,1)S(1)}, bf16[336,768]{1,0:T(8,128)(2,1)S(1)}, u32[]{:S(2)}, u32[]{:S(2)}) collective-permute-start(bf16[336,768]{1,0:T(8,128)(2,1)S(1)} %get-tuple-element.45.block.refs_0_), channel_id=1, source_target_pairs={{0,16},{1,9},{2,18},{3,11},{4,20},{5,13},{6,22},{7,15},{8,24},{9,1... | collective-permute-start | bytes 1548296 | tf_op jit(solution)/shard_map/ppermute | solution.py:353
  11.9 16.2 %collective-permute-start.4 = (bf16[336,768]{1,0:T(8,128)(2,1)S(1)}, bf16[336,768]{1,0:T(8,128)(2,1)S(1)}, u32[]{:S(2)}, u32[]{:S(2)}) collective-permute-start(bf16[336,768]{1,0:T(8,128)(2,1)S(1)} %shard_map.40), channel_id=1, source_target_pairs={{6,2},{0,4},{4,6},{7,1},{1,3},{3,5},{14,10},{8,12},{12,14},{15,9},... | collective-permute-start | bytes 1548296 | tf_op jit(solution)/shard_map/ppermute | solution.py:356
  15.4 6.9 %collective-permute-start.6 = (bf16[160,768]{1,0:T(8,128)(2,1)S(1)}, bf16[160,768]{1,0:T(8,128)(2,1)S(1)}, u32[]{:S(2)}, u32[]{:S(2)}) collective-permute-start(bf16[160,768]{1,0:T(8,128)(2,1)S(1)} %collective-permute-done.5.refs_1_), channel_id=1, source_target_pairs={{0,16},{1,9},{2,18},{3,11},{4,20},{5,13},{6,22},{7,15},{8,24},{9,1... | collective-permute-start | bytes 737288 | tf_op jit(solution)/shard_map/ppermute | solution.py:357
  20.4 6.5 %collective-permute-start.8 = (bf16[176,768]{1,0:T(8,128)(2,1)S(1)}, bf16[176,768]{1,0:T(8,128)(2,1)S(1)}, u32[]{:S(2)}, u32[]{:S(2)}) collective-permute-start(bf16[176,768]{1,0:T(8,128)(2,1)S(1)} %collective-permute-done.7.refs_2_), channel_id=1, source_target_pairs={{0,16},{1,9},{2,18},{3,11},{4,20},{5,13},{6,22},{7,15},{8,24},{9,1... | collective-permute-start | bytes 811016 | tf_op jit(solution)/shard_map/ppermute | solution.py:357
  22.1 4.8 %collective-permute-start.10 = (bf16[160,768]{1,0:T(8,128)(2,1)S(1)}, bf16[160,768]{1,0:T(8,128)(2,1)S(1)}, u32[]{:S(2)}, u32[]{:S(2)}) collective-permute-start(bf16[160,768]{1,0:T(8,128)(2,1)S(1)} %get-tuple-element.48), channel_id=1, source_target_pairs={{0,1},{1,0},{2,3},{3,2},{4,5},{5,4},{6,7},{7,6},{8,9},{9,8},{10,11... | collective-permute-start | bytes 737288 | tf_op jit(solution)/shard_map/ppermute | solution.py:362
  22.2 4.6 %collective-permute-start.11 = (bf16[160,768]{1,0:T(8,128)(2,1)S(1)}, bf16[160,768]{1,0:T(8,128)(2,1)S(1)}, u32[]{:S(2)}, u32[]{:S(2)}) collective-permute-start(bf16[160,768]{1,0:T(8,128)(2,1)S(1)} %get-tuple-element.49), channel_id=1, source_target_pairs={{0,1},{1,0},{2,3},{3,2},{4,5},{5,4},{6,7},{7,6},{8,9},{9,8},{10,11... | collective-permute-start | bytes 737288 | tf_op jit(solution)/shard_map/ppermute | solution.py:362
  28.0 2.1 %collective-permute-start.12 = (bf16[336,768]{1,0:T(8,128)(2,1)S(1)}, bf16[336,768]{1,0:T(8,128)(2,1)S(1)}, u32[]{:S(2)}, u32[]{:S(2)}) collective-permute-start(bf16[336,768]{1,0:T(8,128)(2,1)S(1)} %collective-permute-done.4.second), channel_id=1, source_target_pairs={{0,1},{1,0},{2,3},{3,2},{4,5},{5,4},{6,7},{7,6},{8,9},{9,8},{10,11... | collective-permute-start | bytes 1548296 | tf_op jit(solution)/shard_map/ppermute | solution.py:377
  32.2 1.2 %collective-permute-start.13 = (f32[1,640]{1,0:T(1,128)S(1)}, f32[1,640]{1,0:T(1,128)S(1)}, u32[]{:S(2)}, u32[]{:S(2)}) collective-permute-start(f32[1,640]{1,0:T(1,128)S(1)} %get-tuple-element.59), channel_id=1, source_target_pairs={{0,1},{1,0},{2,3},{3,2},{4,5},{5,4},{6,7},{7,6},{8,9},{9,8},{10,11... | collective-permute-start | bytes 7688 | tf_op jit(solution)/shard_map/ppermute | solution.py:391
  33.4 7.6 %collective-permute-start.14 = (f32[1,640]{1,0:T(1,128)S(1)}, f32[1,640]{1,0:T(1,128)S(1)}, u32[]{:S(2)}, u32[]{:S(2)}) collective-permute-start(f32[1,640]{1,0:T(1,128)S(1)} %max.24), channel_id=1, source_target_pairs={{2,6},{4,0},{6,4},{1,7},{3,1},{5,3},{10,14},{12,8},{14,12},{9,15},... | collective-permute-start | bytes 7688 | tf_op jit(solution)/shard_map/ppermute | solution.py:395
  34.8 6.3 %collective-permute-start.15 = (f32[1,320]{1,0:T(1,128)S(1)}, f32[1,320]{1,0:T(1,128)S(1)}, u32[]{:S(2)}, u32[]{:S(2)}) collective-permute-start(f32[1,320]{1,0:T(1,128)S(1)} %get-tuple-element.65), channel_id=1, source_target_pairs={{0,25},{1,24},{2,27},{3,26},{4,29},{5,28},{6,31},{7,30},{8,17},{9,... | collective-permute-start | bytes 3848 | tf_op jit(solution)/shard_map/ppermute | solution.py:401
  39.3 3.0 %collective-permute-start.16 = (f32[1,320]{1,0:T(1,128)S(1)}, f32[1,320]{1,0:T(1,128)S(1)}, u32[]{:S(2)}, u32[]{:S(2)}) collective-permute-start(f32[1,320]{1,0:T(1,128)S(1)} %get-tuple-element.66), channel_id=1, source_target_pairs={{0,9},{1,16},{2,11},{3,18},{4,13},{5,20},{6,15},{7,22},{8,1},{9,24... | collective-permute-start | bytes 3848 | tf_op jit(solution)/shard_map/ppermute | solution.py:401
  39.3 3.0 %collective-permute-start.17 = (f32[1,320]{1,0:T(1,128)S(1)}, f32[1,320]{1,0:T(1,128)S(1)}, u32[]{:S(2)}, u32[]{:S(2)}) collective-permute-start(f32[1,320]{1,0:T(1,128)S(1)} %get-tuple-element.67), channel_id=1, source_target_pairs={{0,17},{1,8},{2,19},{3,10},{4,21},{5,12},{6,23},{7,14},{8,25},{9,0... | collective-permute-start | bytes 3848 | tf_op jit(solution)/shard_map/ppermute | solution.py:401
  41.1 1.2 %collective-permute-start.18 = (f32[1,320]{1,0:T(1,128)S(1)}, f32[1,320]{1,0:T(1,128)S(1)}, u32[]{:S(2)}, u32[]{:S(2)}) collective-permute-start(f32[1,320]{1,0:T(1,128)S(1)} %fusion), channel_id=1, source_target_pairs={{0,1},{1,0},{2,3},{3,2},{4,5},{5,4},{6,7},{7,6},{8,9},{9,8},{10,11... | collective-permute-start | bytes 3848 | tf_op jit(solution)/shard_map/ppermute | solution.py:404

commit v27 on v25

--- a/solution.py
+++ b/solution.py
@@ -12,7 +12,7 @@
 CODES = 3
 LANES = 128
 TILE = 256
-CHUNK = 32
+CHUNK = 64
 BOTH = ("dp", "grid")
 
 

time: 43.2 us -> 43.2 us (level)
  no operation moved by 1% of the time
where the time goes in v27:
time: 43.2 us; the launch traced here: 42.9 us
  starting transfers between devices  26 us (60%)
  waiting for transfers between devices  9.51 us (22%)
  Pallas kernels  5.03 us (12%)
  local copies, waits for them, and re-layouts  1.36 us (3%)
  other arithmetic  0.69 us (2%)
    ppermute x3, starting transfers between devices, shards(): lax.ppermute(best, BOTH, pairs)  6.2 us
    ppermute x1, starting transfers between devices, shards(): raw = [lax.ppermute(embeddings, BOTH, pairs) for pairs in rounds]  5.57 us
    ppermute x2, waiting for transfers between devices, shards(): from_first = [lax.ppermute(part, BOTH, first) for part in parts]  4.28 us
    ppermute x1, starting transfers between devices, shards(): near_other = [lax.ppermute(both, BOTH, pairs) for pairs in rounds]  3.49 us
    pallas_call x2, Pallas kernels, line(): pl.pallas_call(functools.partial(line_kernel, rows, span, together, len(b...  2.27 us
    ppermute x2, starting transfers between devices, shards(): from_corner = [lax.ppermute(part, BOTH, second) for part in from_first]  2.26 us
    ppermute x2, starting transfers between devices, shards(): from_first = [lax.ppermute(part, BOTH, first) for part in parts]  2.09 us
    ppermute x2, starting transfers between devices, shards(): lax.ppermute(piece, BOTH, other_core)  2.03 us
  transfers between devices with their start and end apart: 19, of which 7 were waited for; matrix products, arithmetic and copies ran while one was open for 0% of the time, Pallas kernels for 7%

profile of v27, /device:TPU:0, one launch (start us, length us, event | category | flops | bytes accessed | tf_op | source)
XLA Modules:
  0.0 42.9 jit_solution(3810464883552295485)
XLA Ops:
  0.0 0.5 %collective-permute-start.1 = (bf16[320,768]{1,0:T(8,128)(2,1)}, bf16[320,768]{1,0:T(8,128)(2,1)S(1)}, u32[]{:S(2)}, u32[]{:S(2)}) collective-permute-start(bf16[320,768]{1,0:T(8,128)(2,1)} %embeddings.1), channel_id=1, source_target_pairs={{0,1},{1,0},{2,3},{3,2},{4,5},{5,4},{6,7},{7,6},{8,9},{9,8},{10,11... | collective-permute-start | bytes 1474568 | tf_op jit(solution)/shard_map/ppermute | solution.py:347
  1.0 5.6 %collective-permute-start = (bf16[320,768]{1,0:T(8,128)(2,1)}, bf16[320,768]{1,0:T(8,128)(2,1)S(1)}, u32[]{:S(2)}, u32[]{:S(2)}) collective-permute-start(bf16[320,768]{1,0:T(8,128)(2,1)} %embeddings.1), channel_id=1, source_target_pairs={{6,2},{0,4},{4,6},{7,1},{1,3},{3,5},{14,10},{8,12},{12,14},{15,9},... | collective-permute-start | bytes 1474568 | tf_op jit(solution)/shard_map/ppermute | solution.py:346
  6.8 1.6 %collective-permute-start.5 = (bf16[160,768]{1,0:T(8,128)(2,1)S(1)}, bf16[160,768]{1,0:T(8,128)(2,1)S(1)}, u32[]{:S(2)}, u32[]{:S(2)}) collective-permute-start(bf16[160,768]{1,0:T(8,128)(2,1)S(1)} %get-tuple-element.41), channel_id=1, source_target_pairs={{0,8},{1,17},{2,10},{3,19},{4,12},{5,21},{6,14},{7,23},{8,0},{9,25... | collective-permute-start | bytes 737288 | tf_op jit(solution)/shard_map/ppermute | solution.py:350
  8.3 0.5 %collective-permute-start.7 = (bf16[176,768]{1,0:T(8,128)(2,1)S(1)}, bf16[176,768]{1,0:T(8,128)(2,1)S(1)}, u32[]{:S(2)}, u32[]{:S(2)}) collective-permute-start(bf16[176,768]{1,0:T(8,128)(2,1)S(1)} %get-tuple-element.42), channel_id=1, source_target_pairs={{0,8},{1,17},{2,10},{3,19},{4,12},{5,21},{6,14},{7,23},{8,0},{9,25... | collective-permute-start | bytes 811016 | tf_op jit(solution)/shard_map/ppermute | solution.py:350
  8.9 0.7 %copy-done.1 = s32[320]{0:T(512)S(1)} copy-done((s32[320]{0:T(512)S(1)}, s32[320]{0:T(512)}, u32[]{:S(2)}) %copy-start.1) | copy-done | bytes 1304
  9.5 0.7 %copy-done.2 = s32[320,1]{0,1:T(1,128)S(1)} copy-done((s32[320,1]{0,1:T(1,128)S(1)}, s32[320,1]{0,1:T(1,128)}, u32[]{:S(2)}) %copy-start.2) | copy-done | bytes 1304
  10.2 1.6 %collective-permute-start.9 = (bf16[336,768]{1,0:T(8,128)(2,1)S(1)}, bf16[336,768]{1,0:T(8,128)(2,1)S(1)}, u32[]{:S(2)}, u32[]{:S(2)}) collective-permute-start(bf16[336,768]{1,0:T(8,128)(2,1)S(1)} %get-tuple-element.45.block.refs_0_), channel_id=1, source_target_pairs={{0,16},{1,9},{2,18},{3,11},{4,20},{5,13},{6,22},{7,15},{8,24},{9,1... | collective-permute-start | bytes 1548296 | tf_op jit(solution)/shard_map/ppermute | solution.py:353
  11.9 3.5 %collective-permute-start.4 = (bf16[336,768]{1,0:T(8,128)(2,1)S(1)}, bf16[336,768]{1,0:T(8,128)(2,1)S(1)}, u32[]{:S(2)}, u32[]{:S(2)}) collective-permute-start(bf16[336,768]{1,0:T(8,128)(2,1)S(1)} %shard_map.40), channel_id=1, source_target_pairs={{6,2},{0,4},{4,6},{7,1},{1,3},{3,5},{14,10},{8,12},{12,14},{15,9},... | collective-permute-start | bytes 1548296 | tf_op jit(solution)/shard_map/ppermute | solution.py:356
  15.4 0.7 %collective-permute-start.6 = (bf16[160,768]{1,0:T(8,128)(2,1)S(1)}, bf16[160,768]{1,0:T(8,128)(2,1)S(1)}, u32[]{:S(2)}, u32[]{:S(2)}) collective-permute-start(bf16[160,768]{1,0:T(8,128)(2,1)S(1)} %collective-permute-done.5.refs_1_), channel_id=1, source_target_pairs={{0,16},{1,9},{2,18},{3,11},{4,20},{5,13},{6,22},{7,15},{8,24},{9,1... | collective-permute-start | bytes 737288 | tf_op jit(solution)/shard_map/ppermute | solution.py:357
  16.1 4.3 %collective-permute-done.7.refs_2_ = bf16[176,768]{1,0:T(8,128)(2,1)S(1)} collective-permute-done((bf16[176,768]{1,0:T(8,128)(2,1)S(1)}, bf16[176,768]{1,0:T(8,128)(2,1)S(1)}, u32[]{:S(2)}, u32[]{:S(2)}) %collective-permute-start.7) | collective-permute-done | bytes 270368 | tf_op jit(solution)/shard_map/ppermute | solution.py:350
  20.4 1.5 %collective-permute-start.8 = (bf16[176,768]{1,0:T(8,128)(2,1)S(1)}, bf16[176,768]{1,0:T(8,128)(2,1)S(1)}, u32[]{:S(2)}, u32[]{:S(2)}) collective-permute-start(bf16[176,768]{1,0:T(8,128)(2,1)S(1)} %collective-permute-done.7.refs_2_), channel_id=1, source_target_pairs={{0,16},{1,9},{2,18},{3,11},{4,20},{5,13},{6,22},{7,15},{8,24},{9,1... | collective-permute-start | bytes 811016 | tf_op jit(solution)/shard_map/ppermute | solution.py:357
  22.2 2.0 %collective-permute-start.11 = (bf16[160,768]{1,0:T(8,128)(2,1)S(1)}, bf16[160,768]{1,0:T(8,128)(2,1)S(1)}, u32[]{:S(2)}, u32[]{:S(2)}) collective-permute-start(bf16[160,768]{1,0:T(8,128)(2,1)S(1)} %get-tuple-element.49), channel_id=1, source_target_pairs={{0,1},{1,0},{2,3},{3,2},{4,5},{5,4},{6,7},{7,6},{8,9},{9,8},{10,11... | collective-permute-start | bytes 737288 | tf_op jit(solution)/shard_map/ppermute | solution.py:362
  24.4 1.0 %shard_map.42 = (f32[1,640]{1,0:T(1,128)S(1)}, f32[1,320]{1,0:T(1,128)S(1)}) custom-call(bf16[336,768]{1,0:T(8,128)(2,1)S(1)} %get-tuple-element.45.block.refs_0_, bf16[336,768]{1,0:T(8,128)(2,1)S(1)} %shard_map.41.partner, bf16[336,768]{1,0:T(8,128)(2,1)S(1)} %get-tuple-element.45.block.refs_0_, bf16[160,768]{1,0:T(8,128)(2,1)S(1)} %collective-permute-done.5.refs_1_, ...), custom_call_target="tpu_custom_call" | custom-call | flops 320 | bytes 320 | tf_op jit(solution)/shard_map/pallas_call | solution.py:247
  25.4 1.4 %collective-permute-done.8.refs_5_ = bf16[176,768]{1,0:T(8,128)(2,1)S(1)} collective-permute-done((bf16[176,768]{1,0:T(8,128)(2,1)S(1)}, bf16[176,768]{1,0:T(8,128)(2,1)S(1)}, u32[]{:S(2)}, u32[]{:S(2)}) %collective-permute-start.8) | collective-permute-done | bytes 270368 | tf_op jit(solution)/shard_map/ppermute | solution.py:357
  27.0 1.0 %shard_map.44 = (f32[1,640]{1,0:T(1,128)S(1)}, f32[1,320]{1,0:T(1,128)S(1)}) custom-call(bf16[336,768]{1,0:T(8,128)(2,1)S(1)} %get-tuple-element.45.block.refs_0_, bf16[336,768]{1,0:T(8,128)(2,1)S(1)} %shard_map.41.partner, bf16[1280,768]{1,0:T(8,128)(2,1)S(1)} %get-tuple-element.50.held, f32[1,1280]{1,0:T(1,128)S(1)} %get-tuple-element.51.row), custom_call_target="tpu_custom_call" | custom-call | flops 320 | bytes 320 | tf_op jit(solution)/shard_map/pallas_call | solution.py:263
  28.0 0.5 %collective-permute-start.12 = (bf16[336,768]{1,0:T(8,128)(2,1)S(1)}, bf16[336,768]{1,0:T(8,128)(2,1)S(1)}, u32[]{:S(2)}, u32[]{:S(2)}) collective-permute-start(bf16[336,768]{1,0:T(8,128)(2,1)S(1)} %collective-permute-done.4.second), channel_id=1, source_target_pairs={{0,1},{1,0},{2,3},{3,2},{4,5},{5,4},{6,7},{7,6},{8,9},{9,8},{10,11... | collective-permute-start | bytes 1548296 | tf_op jit(solution)/shard_map/ppermute | solution.py:377
  28.7 1.4 %collective-permute-done.12.second = bf16[336,768]{1,0:T(8,128)(2,1)S(1)} collective-permute-done((bf16[336,768]{1,0:T(8,128)(2,1)S(1)}, bf16[336,768]{1,0:T(8,128)(2,1)S(1)}, u32[]{:S(2)}, u32[]{:S(2)}) %collective-permute-start.12) | collective-permute-done | bytes 516128 | tf_op jit(solution)/shard_map/ppermute | solution.py:377
  30.1 2.1 %shard_map.46 = (f32[1,320]{1,0:T(1,128)S(1)}, f32[1,320]{1,0:T(1,128)S(1)}, f32[1,320]{1,0:T(1,128)S(1)}, f32[1,320]{1,0:T(1,128)S(1)}, f32[1,640]{1,0:T(1,128)S(1)}) custom-call(bf16[320,768]{1,0:T(8,128)(2,1)S(1)} %get-tuple-element.57.first, bf16[336,768]{1,0:T(8,128)(2,1)S(1)} %collective-permute-done.12.second, ...), custom_call_target="tpu_custom_call" | custom-call | flops 320 | bytes 320 | tf_op jit(solution)/shard_map/pallas_call | solution.py:277
  32.3 1.1 %collective-permute-done.13 = f32[1,640]{1,0:T(1,128)S(1)} collective-permute-done((f32[1,640]{1,0:T(1,128)S(1)}, f32[1,640]{1,0:T(1,128)S(1)}, u32[]{:S(2)}, u32[]{:S(2)}) %collective-permute-start.13) | collective-permute-done | bytes 2592 | tf_op jit(solution)/shard_map/ppermute | solution.py:391
  33.4 1.3 %collective-permute-start.14 = (f32[1,640]{1,0:T(1,128)S(1)}, f32[1,640]{1,0:T(1,128)S(1)}, u32[]{:S(2)}, u32[]{:S(2)}) collective-permute-start(f32[1,640]{1,0:T(1,128)S(1)} %max.24), channel_id=1, source_target_pairs={{2,6},{4,0},{6,4},{1,7},{3,1},{5,3},{10,14},{12,8},{14,12},{9,15},... | collective-permute-start | bytes 7688 | tf_op jit(solution)/shard_map/ppermute | solution.py:395
  34.8 3.5 %collective-permute-start.15 = (f32[1,320]{1,0:T(1,128)S(1)}, f32[1,320]{1,0:T(1,128)S(1)}, u32[]{:S(2)}, u32[]{:S(2)}) collective-permute-start(f32[1,320]{1,0:T(1,128)S(1)} %get-tuple-element.65), channel_id=1, source_target_pairs={{0,9},{1,16},{2,11},{3,18},{4,13},{5,20},{6,15},{7,22},{8,1},{9,24... | collective-permute-start | bytes 3848 | tf_op jit(solution)/shard_map/ppermute | solution.py:402
  38.4 2.6 %collective-permute-start.17 = (f32[1,320]{1,0:T(1,128)S(1)}, f32[1,320]{1,0:T(1,128)S(1)}, u32[]{:S(2)}, u32[]{:S(2)}) collective-permute-start(f32[1,320]{1,0:T(1,128)S(1)} %get-tuple-element.67), channel_id=1, source_target_pairs={{0,25},{1,24},{2,27},{3,26},{4,29},{5,28},{6,31},{7,30},{8,17},{9,... | collective-permute-start | bytes 3848 | tf_op jit(solution)/shard_map/ppermute | solution.py:402
  41.3 1.0 %collective-permute-done.17 = f32[1,320]{1,0:T(1,128)S(1)} collective-permute-done((f32[1,320]{1,0:T(1,128)S(1)}, f32[1,320]{1,0:T(1,128)S(1)}, u32[]{:S(2)}, u32[]{:S(2)}) %collective-permute-start.17) | collective-permute-done | bytes 1312 | tf_op jit(solution)/shard_map/ppermute | solution.py:402
  42.3 0.6 %maximum_reduce_fusion = f32[320]{0:T(512)} fusion(f32[1,320]{1,0:T(1,128)S(1)} %collective-permute-done.18, f32[1,320]{1,0:T(1,128)S(1)} %collective-permute-done.17, f32[1,320]{1,0:T(1,128)S(1)} %collective-permute-done.16, f32[1,320]{1,0:T(1,128)S(1)} %collective-permute-done.15, f32[1,640]{1,0:T(1,128)S(1)} %broadcast_select_fusion), kind=kLoop, calls=%fused_computation.6 | loop fusion | flops 1280 | bytes 7680 | tf_op jit(solution)/shard_map/max | solution.py:407
  (34 shorter events, 2.0 us)
Async XLA Ops:
  0.0 24.2 %copy-start = (bf16[320,768]{1,0:T(8,128)(2,1)S(1)}, bf16[320,768]{1,0:T(8,128)(2,1)}, u32[]{:S(2)}) copy-start(bf16[320,768]{1,0:T(8,128)(2,1)} %embeddings.1) | copy-start | bytes 1474564
  0.0 6.6 %collective-permute-start.1 = (bf16[320,768]{1,0:T(8,128)(2,1)}, bf16[320,768]{1,0:T(8,128)(2,1)S(1)}, u32[]{:S(2)}, u32[]{:S(2)}) collective-permute-start(bf16[320,768]{1,0:T(8,128)(2,1)} %embeddings.1), channel_id=1, source_target_pairs={{0,1},{1,0},{2,3},{3,2},{4,5},{5,4},{6,7},{7,6},{8,9},{9,8},{10,11... | collective-permute-start | bytes 1474568 | tf_op jit(solution)/shard_map/ppermute | solution.py:347
  0.5 6.1 %collective-permute-start.2 = (s32[1,320]{1,0:T(1,128)}, s32[1,320]{1,0:T(1,128)S(1)}, u32[]{:S(2)}, u32[]{:S(2)}) collective-permute-start(s32[1,320]{1,0:T(1,128)} %bitcast.1), channel_id=1, source_target_pairs={{0,1},{1,0},{2,3},{3,2},{4,5},{5,4},{6,7},{7,6},{8,9},{9,8},{10,11... | collective-permute-start | bytes 3848 | tf_op jit(solution)/shard_map/ppermute | solution.py:347
  0.5 6.0 %collective-permute-start.3 = (s32[320]{0:T(512)}, s32[320]{0:T(512)S(1)}, u32[]{:S(2)}, u32[]{:S(2)}) collective-permute-start(s32[320]{0:T(512)} %order_key.1), channel_id=1, source_target_pairs={{0,1},{1,0},{2,3},{3,2},{4,5},{5,4},{6,7},{7,6},{8,9},{9,8},{10,11... | collective-permute-start | bytes 3848 | tf_op jit(solution)/shard_map/ppermute | solution.py:347
  1.0 20.9 %collective-permute-start = (bf16[320,768]{1,0:T(8,128)(2,1)}, bf16[320,768]{1,0:T(8,128)(2,1)S(1)}, u32[]{:S(2)}, u32[]{:S(2)}) collective-permute-start(bf16[320,768]{1,0:T(8,128)(2,1)} %embeddings.1), channel_id=1, source_target_pairs={{6,2},{0,4},{4,6},{7,1},{1,3},{3,5},{14,10},{8,12},{12,14},{15,9},... | collective-permute-start | bytes 1474568 | tf_op jit(solution)/shard_map/ppermute | solution.py:346
  6.8 8.6 %collective-permute-start.5 = (bf16[160,768]{1,0:T(8,128)(2,1)S(1)}, bf16[160,768]{1,0:T(8,128)(2,1)S(1)}, u32[]{:S(2)}, u32[]{:S(2)}) collective-permute-start(bf16[160,768]{1,0:T(8,128)(2,1)S(1)} %get-tuple-element.41), channel_id=1, source_target_pairs={{0,8},{1,17},{2,10},{3,19},{4,12},{5,21},{6,14},{7,23},{8,0},{9,25... | collective-permute-start | bytes 737288 | tf_op jit(solution)/shard_map/ppermute | solution.py:350
  8.3 12.1 %collective-permute-start.7 = (bf16[176,768]{1,0:T(8,128)(2,1)S(1)}, bf16[176,768]{1,0:T(8,128)(2,1)S(1)}, u32[]{:S(2)}, u32[]{:S(2)}) collective-permute-start(bf16[176,768]{1,0:T(8,128)(2,1)S(1)} %get-tuple-element.42), channel_id=1, source_target_pairs={{0,8},{1,17},{2,10},{3,19},{4,12},{5,21},{6,14},{7,23},{8,0},{9,25... | collective-permute-start | bytes 811016 | tf_op jit(solution)/shard_map/ppermute | solution.py:350
  8.9 0.7 %copy-start.1 = (s32[320]{0:T(512)S(1)}, s32[320]{0:T(512)}, u32[]{:S(2)}) copy-start(s32[320]{0:T(512)} %order_key.1) | copy-start | bytes 3844
  9.5 0.7 %copy-start.2 = (s32[320,1]{0,1:T(1,128)S(1)}, s32[320,1]{0,1:T(1,128)}, u32[]{:S(2)}) copy-start(s32[320,1]{0,1:T(1,128)} %param.4) | copy-start | bytes 3844
  10.2 16.6 %collective-permute-start.9 = (bf16[336,768]{1,0:T(8,128)(2,1)S(1)}, bf16[336,768]{1,0:T(8,128)(2,1)S(1)}, u32[]{:S(2)}, u32[]{:S(2)}) collective-permute-start(bf16[336,768]{1,0:T(8,128)(2,1)S(1)} %get-tuple-element.45.block.refs_0_), channel_id=1, source_target_pairs={{0,16},{1,9},{2,18},{3,11},{4,20},{5,13},{6,22},{7,15},{8,24},{9,1... | collective-permute-start | bytes 1548296 | tf_op jit(solution)/shard_map/ppermute | solution.py:353
  11.9 16.2 %collective-permute-start.4 = (bf16[336,768]{1,0:T(8,128)(2,1)S(1)}, bf16[336,768]{1,0:T(8,128)(2,1)S(1)}, u32[]{:S(2)}, u32[]{:S(2)}) collective-permute-start(bf16[336,768]{1,0:T(8,128)(2,1)S(1)} %shard_map.40), channel_id=1, source_target_pairs={{6,2},{0,4},{4,6},{7,1},{1,3},{3,5},{14,10},{8,12},{12,14},{15,9},... | collective-permute-start | bytes 1548296 | tf_op jit(solution)/shard_map/ppermute | solution.py:356
  15.4 6.9 %collective-permute-start.6 = (bf16[160,768]{1,0:T(8,128)(2,1)S(1)}, bf16[160,768]{1,0:T(8,128)(2,1)S(1)}, u32[]{:S(2)}, u32[]{:S(2)}) collective-permute-start(bf16[160,768]{1,0:T(8,128)(2,1)S(1)} %collective-permute-done.5.refs_1_), channel_id=1, source_target_pairs={{0,16},{1,9},{2,18},{3,11},{4,20},{5,13},{6,22},{7,15},{8,24},{9,1... | collective-permute-start | bytes 737288 | tf_op jit(solution)/shard_map/ppermute | solution.py:357
  20.4 6.5 %collective-permute-start.8 = (bf16[176,768]{1,0:T(8,128)(2,1)S(1)}, bf16[176,768]{1,0:T(8,128)(2,1)S(1)}, u32[]{:S(2)}, u32[]{:S(2)}) collective-permute-start(bf16[176,768]{1,0:T(8,128)(2,1)S(1)} %collective-permute-done.7.refs_2_), channel_id=1, source_target_pairs={{0,16},{1,9},{2,18},{3,11},{4,20},{5,13},{6,22},{7,15},{8,24},{9,1... | collective-permute-start | bytes 811016 | tf_op jit(solution)/shard_map/ppermute | solution.py:357
  22.1 4.8 %collective-permute-start.10 = (bf16[160,768]{1,0:T(8,128)(2,1)S(1)}, bf16[160,768]{1,0:T(8,128)(2,1)S(1)}, u32[]{:S(2)}, u32[]{:S(2)}) collective-permute-start(bf16[160,768]{1,0:T(8,128)(2,1)S(1)} %get-tuple-element.48), channel_id=1, source_target_pairs={{0,1},{1,0},{2,3},{3,2},{4,5},{5,4},{6,7},{7,6},{8,9},{9,8},{10,11... | collective-permute-start | bytes 737288 | tf_op jit(solution)/shard_map/ppermute | solution.py:362
  22.2 4.6 %collective-permute-start.11 = (bf16[160,768]{1,0:T(8,128)(2,1)S(1)}, bf16[160,768]{1,0:T(8,128)(2,1)S(1)}, u32[]{:S(2)}, u32[]{:S(2)}) collective-permute-start(bf16[160,768]{1,0:T(8,128)(2,1)S(1)} %get-tuple-element.49), channel_id=1, source_target_pairs={{0,1},{1,0},{2,3},{3,2},{4,5},{5,4},{6,7},{7,6},{8,9},{9,8},{10,11... | collective-permute-start | bytes 737288 | tf_op jit(solution)/shard_map/ppermute | solution.py:362
  28.0 2.1 %collective-permute-start.12 = (bf16[336,768]{1,0:T(8,128)(2,1)S(1)}, bf16[336,768]{1,0:T(8,128)(2,1)S(1)}, u32[]{:S(2)}, u32[]{:S(2)}) collective-permute-start(bf16[336,768]{1,0:T(8,128)(2,1)S(1)} %collective-permute-done.4.second), channel_id=1, source_target_pairs={{0,1},{1,0},{2,3},{3,2},{4,5},{5,4},{6,7},{7,6},{8,9},{9,8},{10,11... | collective-permute-start | bytes 1548296 | tf_op jit(solution)/shard_map/ppermute | solution.py:377
  32.3 1.2 %collective-permute-start.13 = (f32[1,640]{1,0:T(1,128)S(1)}, f32[1,640]{1,0:T(1,128)S(1)}, u32[]{:S(2)}, u32[]{:S(2)}) collective-permute-start(f32[1,640]{1,0:T(1,128)S(1)} %get-tuple-element.59), channel_id=1, source_target_pairs={{0,1},{1,0},{2,3},{3,2},{4,5},{5,4},{6,7},{7,6},{8,9},{9,8},{10,11... | collective-permute-start | bytes 7688 | tf_op jit(solution)/shard_map/ppermute | solution.py:391
  33.4 7.6 %collective-permute-start.14 = (f32[1,640]{1,0:T(1,128)S(1)}, f32[1,640]{1,0:T(1,128)S(1)}, u32[]{:S(2)}, u32[]{:S(2)}) collective-permute-start(f32[1,640]{1,0:T(1,128)S(1)} %max.24), channel_id=1, source_target_pairs={{2,6},{4,0},{6,4},{1,7},{3,1},{5,3},{10,14},{12,8},{14,12},{9,15},... | collective-permute-start | bytes 7688 | tf_op jit(solution)/shard_map/ppermute | solution.py:395
  34.8 6.3 %collective-permute-start.15 = (f32[1,320]{1,0:T(1,128)S(1)}, f32[1,320]{1,0:T(1,128)S(1)}, u32[]{:S(2)}, u32[]{:S(2)}) collective-permute-start(f32[1,320]{1,0:T(1,128)S(1)} %get-tuple-element.65), channel_id=1, source_target_pairs={{0,9},{1,16},{2,11},{3,18},{4,13},{5,20},{6,15},{7,22},{8,1},{9,24... | collective-permute-start | bytes 3848 | tf_op jit(solution)/shard_map/ppermute | solution.py:402
  38.3 3.0 %collective-permute-start.16 = (f32[1,320]{1,0:T(1,128)S(1)}, f32[1,320]{1,0:T(1,128)S(1)}, u32[]{:S(2)}, u32[]{:S(2)}) collective-permute-start(f32[1,320]{1,0:T(1,128)S(1)} %get-tuple-element.66), channel_id=1, source_target_pairs={{0,17},{1,8},{2,19},{3,10},{4,21},{5,12},{6,23},{7,14},{8,25},{9,0... | collective-permute-start | bytes 3848 | tf_op jit(solution)/shard_map/ppermute | solution.py:402
  38.4 3.9 %collective-permute-start.17 = (f32[1,320]{1,0:T(1,128)S(1)}, f32[1,320]{1,0:T(1,128)S(1)}, u32[]{:S(2)}, u32[]{:S(2)}) collective-permute-start(f32[1,320]{1,0:T(1,128)S(1)} %get-tuple-element.67), channel_id=1, source_target_pairs={{0,25},{1,24},{2,27},{3,26},{4,29},{5,28},{6,31},{7,30},{8,17},{9,... | collective-permute-start | bytes 3848 | tf_op jit(solution)/shard_map/ppermute | solution.py:402
  41.1 1.2 %collective-permute-start.18 = (f32[1,320]{1,0:T(1,128)S(1)}, f32[1,320]{1,0:T(1,128)S(1)}, u32[]{:S(2)}, u32[]{:S(2)}) collective-permute-start(f32[1,320]{1,0:T(1,128)S(1)} %fusion), channel_id=1, source_target_pairs={{0,1},{1,0},{2,3},{3,2},{4,5},{5,4},{6,7},{7,6},{8,9},{9,8},{10,11... | collective-permute-start | bytes 3848 | tf_op jit(solution)/shard_map/ppermute | solution.py:406

commit v28 on v25

--- a/solution.py
+++ b/solution.py
@@ -99,38 +99,40 @@
 
 
 def meet(units, parts, rows, span, held, held_codes):
-    columns = [turned_to_column(row, rows) for row, _ in parts]
+    low = -(2**31)
+    columns = [turned_to_column(row, rows).astype(jnp.int32) for row, _ in parts]
+    after = [column + (2**31 - 1) for column in columns]
+    before = [column + (low + 1) for column in columns]
+    held_codes = held_codes.astype(jnp.int32)
+    limit = low + span - 1
     starts = [(block, top) for block in range(len(parts)) for top in range(0, rows, CHUNK)]
     partial = {start: jnp.full((CHUNK, LANES), -1.0, jnp.float32) for start in starts}
     best_held = []
     for at in range(0, held.shape[0], TILE):
         tile = min(TILE, held.shape[0] - at)
-        sims = lax.dot_general(
-            units[...],
-            held[at : at + tile, :],
-            (((1,), (1,)), ((), ())),
-            preferred_element_type=jnp.float32,
-        )
+        sims = [
+            lax.dot_general(
+                some[0:rows, :],
+                held[at : at + tile, :],
+                (((1,), (1,)), ((), ())),
+                preferred_element_type=jnp.float32,
+            )
+            for some in units
+        ]
         best = [jnp.full((CHUNK, LANES), -1.0, jnp.float32) for _ in range(0, tile, LANES)]
         for block, top in starts:
             to_block, to_held = parts[block][1]
-            mine = columns[block][top : top + CHUNK]
-            line = block * rows + top
             for lane in range(0, tile, LANES):
-                part = sims[line : line + CHUNK, lane : lane + LANES]
-                gap = mine - held_codes[:, at + lane : at + lane + LANES]
-                if to_block and to_held:
-                    part = jnp.where(jnp.abs(gap) < span, part, -1.0)
-                    later = gap > 0.0
-                    ours, theirs = jnp.where(later, part, -1.0), jnp.where(later, -1.0, part)
-                elif to_block:
-                    ours = jnp.where((gap > 0.0) & (gap < span), part, -1.0)
-                else:
-                    theirs = jnp.where((gap < 0.0) & (gap > -span), part, -1.0)
+                part = sims[block][top : top + CHUNK, lane : lane + LANES]
+                theirs = held_codes[:, at + lane : at + lane + LANES]
                 if to_block:
+                    earlier = after[block][top : top + CHUNK] - theirs < limit
+                    ours = jnp.where(earlier, part, -1.0)
                     partial[block, top] = jnp.maximum(partial[block, top], ours)
                 if to_held:
-                    best[lane // LANES] = jnp.maximum(best[lane // LANES], theirs)
+                    earlier = theirs - before[block][top : top + CHUNK] < limit
+                    other = jnp.where(earlier, part, -1.0)
+                    best[lane // LANES] = jnp.maximum(best[lane // LANES], other)
         best_held += [jnp.max(some, axis=0, keepdims=True) for some in best]
     found = [
         row_from_partial(
@@ -192,32 +194,27 @@
     return [[next(flat) for _ in range(length)] for length in lengths]
 
 
-def pair(units, first, second, rows):
-    units[0:rows, :] = first[0:rows, :]
-    units[rows:, :] = second[0:rows, :]
-
-
 def plane_kernel(rows, span, lengths, block, partner, *refs):
-    *pieces, best, mine, held, units = refs
+    *pieces, best, mine, held = refs
     row = hold(regrouped(pieces, lengths), held, rows, span)
-    pair(units, block, partner, rows)
+    units = (block, partner)
     parts = [(codes(block, rows, span), OWN), (codes(partner, rows, span), HELD)]
     (mine[...],), theirs = meet(units, parts, rows, span, held, row)
     best[...] = theirs[:, : best.shape[1]]
 
 
-def rest_kernel(rows, span, block, partner, held, row, best, mine, units):
+def rest_kernel(rows, span, block, partner, held, row, best, mine):
     count = best.shape[1]
     start = held.shape[0] - up(count, LANES)
     held, row = held.at[start:, :], row[:, start:]
-    pair(units, block, partner, rows)
+    units = (block, partner)
     parts = [(codes(block, rows, span), OWN), (codes(partner, rows, span), HELD)]
     (mine[...],), theirs = meet(units, parts, rows, span, held, row)
     best[...] = theirs[:, row.shape[1] - count :]
 
 
 def line_kernel(rows, span, together, count, first, second, held, row, *refs):
-    bests, outs, (found, units) = refs[:count], refs[count:-2], refs[-2:]
+    bests, outs, found = refs[:count], refs[count:-1], refs[-1]
     parts = [(codes(second, rows, span, first=place), TWO) for place in (CODES, 0)]
 
     def give(best):
@@ -230,7 +227,7 @@
 
     @pl.when(arrived)
     def _():
-        pair(units, first, second, rows)
+        units = (first, second)
         mine, theirs = meet(units, parts, rows, span, held, row[...])
         found[...] = jnp.concatenate(mine, axis=1)
         give(jnp.maximum(jnp.concatenate([best[...] for best in bests], axis=1), theirs))
@@ -252,7 +249,6 @@
         ],
         scratch_shapes=[
             pltpu.VMEM((up(total, LANES), width), jnp.bfloat16),
-            pltpu.VMEM((2 * rows, width), jnp.bfloat16),
         ],
         compiler_params=pltpu.CompilerParams(vmem_limit_bytes=12 << 20),
         cost_estimate=pl.CostEstimate(flops=rows, bytes_accessed=rows, transcendentals=0),
@@ -266,7 +262,6 @@
             jax.ShapeDtypeStruct((1, count), jnp.float32),
             jax.ShapeDtypeStruct((1, rows), jnp.float32),
         ],
-        scratch_shapes=[pltpu.VMEM((2 * rows, block.shape[1]), jnp.bfloat16)],
         compiler_params=pltpu.CompilerParams(vmem_limit_bytes=12 << 20),
         cost_estimate=pl.CostEstimate(flops=rows, bytes_accessed=rows, transcendentals=0),
     )(block, partner, held, row)
@@ -277,7 +272,6 @@
     *bests, found = pl.pallas_call(
         functools.partial(line_kernel, rows, span, together, len(bests)),
         out_shape=outs + [jax.ShapeDtypeStruct((1, 2 * rows), jnp.float32)],
-        scratch_shapes=[pltpu.VMEM((2 * rows, second.shape[1]), jnp.bfloat16)],
         compiler_params=pltpu.CompilerParams(vmem_limit_bytes=12 << 20),
         cost_estimate=pl.CostEstimate(flops=rows, bytes_accessed=rows, transcendentals=0),
     )(first, second, held, row, *bests)

time: 43.2 us -> 43.3 us (level)
  no operation moved by 1% of the time
where the time goes in v28:
time: 43.3 us; the launch traced here: 43.1 us
  starting transfers between devices  25.9 us (60%)
  waiting for transfers between devices  9.41 us (22%)
  Pallas kernels  5.41 us (12%)
  local copies, waits for them, and re-layouts  1.36 us (3%)
  other arithmetic  0.69 us (2%)
    ppermute x3, starting transfers between devices, shards(): lax.ppermute(best, BOTH, pairs)  6.2 us
    ppermute x1, starting transfers between devices, shards(): raw = [lax.ppermute(embeddings, BOTH, pairs) for pairs in rounds]  5.57 us
    ppermute x2, waiting for transfers between devices, shards(): from_first = [lax.ppermute(part, BOTH, first) for part in parts]  4.28 us
    ppermute x1, starting transfers between devices, shards(): near_other = [lax.ppermute(both, BOTH, pairs) for pairs in rounds]  3.49 us
    pallas_call x2, Pallas kernels, line(): pl.pallas_call(functools.partial(line_kernel, rows, span, together, len(b...  2.43 us
    ppermute x2, starting transfers between devices, shards(): from_corner = [lax.ppermute(part, BOTH, second) for part in from_first]  2.26 us
    ppermute x2, starting transfers between devices, shards(): from_first = [lax.ppermute(part, BOTH, first) for part in parts]  2.09 us
    ppermute x2, starting transfers between devices, shards(): lax.ppermute(piece, BOTH, other_core)  2.03 us
  transfers between devices with their start and end apart: 19, of which 7 were waited for; matrix products, arithmetic and copies ran while one was open for 0% of the time, Pallas kernels for 7%

profile of v28, /device:TPU:0, one launch (start us, length us, event | category | flops | bytes accessed | tf_op | source)
XLA Modules:
  0.0 43.1 jit_solution(1028204520908871868)
XLA Ops:
  0.0 0.5 %collective-permute-start.1 = (bf16[320,768]{1,0:T(8,128)(2,1)}, bf16[320,768]{1,0:T(8,128)(2,1)S(1)}, u32[]{:S(2)}, u32[]{:S(2)}) collective-permute-start(bf16[320,768]{1,0:T(8,128)(2,1)} %embeddings.1), channel_id=1, source_target_pairs={{0,1},{1,0},{2,3},{3,2},{4,5},{5,4},{6,7},{7,6},{8,9},{9,8},{10,11... | collective-permute-start | bytes 1474568 | tf_op jit(solution)/shard_map/ppermute | solution.py:341
  0.5 0.4 %collective-permute-start.3 = (s32[320]{0:T(512)}, s32[320]{0:T(512)S(1)}, u32[]{:S(2)}, u32[]{:S(2)}) collective-permute-start(s32[320]{0:T(512)} %order_key.1), channel_id=1, source_target_pairs={{0,1},{1,0},{2,3},{3,2},{4,5},{5,4},{6,7},{7,6},{8,9},{9,8},{10,11... | collective-permute-start | bytes 3848 | tf_op jit(solution)/shard_map/ppermute | solution.py:341
  1.0 5.6 %collective-permute-start = (bf16[320,768]{1,0:T(8,128)(2,1)}, bf16[320,768]{1,0:T(8,128)(2,1)S(1)}, u32[]{:S(2)}, u32[]{:S(2)}) collective-permute-start(bf16[320,768]{1,0:T(8,128)(2,1)} %embeddings.1), channel_id=1, source_target_pairs={{6,2},{0,4},{4,6},{7,1},{1,3},{3,5},{14,10},{8,12},{12,14},{15,9},... | collective-permute-start | bytes 1474568 | tf_op jit(solution)/shard_map/ppermute | solution.py:340
  6.8 1.6 %collective-permute-start.5 = (bf16[160,768]{1,0:T(8,128)(2,1)S(1)}, bf16[160,768]{1,0:T(8,128)(2,1)S(1)}, u32[]{:S(2)}, u32[]{:S(2)}) collective-permute-start(bf16[160,768]{1,0:T(8,128)(2,1)S(1)} %get-tuple-element.41), channel_id=1, source_target_pairs={{0,8},{1,17},{2,10},{3,19},{4,12},{5,21},{6,14},{7,23},{8,0},{9,25... | collective-permute-start | bytes 737288 | tf_op jit(solution)/shard_map/ppermute | solution.py:344
  8.3 0.5 %collective-permute-start.7 = (bf16[176,768]{1,0:T(8,128)(2,1)S(1)}, bf16[176,768]{1,0:T(8,128)(2,1)S(1)}, u32[]{:S(2)}, u32[]{:S(2)}) collective-permute-start(bf16[176,768]{1,0:T(8,128)(2,1)S(1)} %get-tuple-element.42), channel_id=1, source_target_pairs={{0,8},{1,17},{2,10},{3,19},{4,12},{5,21},{6,14},{7,23},{8,0},{9,25... | collective-permute-start | bytes 811016 | tf_op jit(solution)/shard_map/ppermute | solution.py:344
  8.9 0.7 %copy-done.1 = s32[320]{0:T(512)S(1)} copy-done((s32[320]{0:T(512)S(1)}, s32[320]{0:T(512)}, u32[]{:S(2)}) %copy-start.1) | copy-done | bytes 1304
  9.5 0.7 %copy-done.2 = s32[320,1]{0,1:T(1,128)S(1)} copy-done((s32[320,1]{0,1:T(1,128)S(1)}, s32[320,1]{0,1:T(1,128)}, u32[]{:S(2)}) %copy-start.2) | copy-done | bytes 1304
  10.2 1.6 %collective-permute-start.9 = (bf16[336,768]{1,0:T(8,128)(2,1)S(1)}, bf16[336,768]{1,0:T(8,128)(2,1)S(1)}, u32[]{:S(2)}, u32[]{:S(2)}) collective-permute-start(bf16[336,768]{1,0:T(8,128)(2,1)S(1)} %get-tuple-element.45.block.refs_0_), channel_id=1, source_target_pairs={{0,16},{1,9},{2,18},{3,11},{4,20},{5,13},{6,22},{7,15},{8,24},{9,1... | collective-permute-start | bytes 1548296 | tf_op jit(solution)/shard_map/ppermute | solution.py:347
  11.9 3.5 %collective-permute-start.4 = (bf16[336,768]{1,0:T(8,128)(2,1)S(1)}, bf16[336,768]{1,0:T(8,128)(2,1)S(1)}, u32[]{:S(2)}, u32[]{:S(2)}) collective-permute-start(bf16[336,768]{1,0:T(8,128)(2,1)S(1)} %shard_map.40), channel_id=1, source_target_pairs={{6,2},{0,4},{4,6},{7,1},{1,3},{3,5},{14,10},{8,12},{12,14},{15,9},... | collective-permute-start | bytes 1548296 | tf_op jit(solution)/shard_map/ppermute | solution.py:350
  15.4 0.7 %collective-permute-start.6 = (bf16[160,768]{1,0:T(8,128)(2,1)S(1)}, bf16[160,768]{1,0:T(8,128)(2,1)S(1)}, u32[]{:S(2)}, u32[]{:S(2)}) collective-permute-start(bf16[160,768]{1,0:T(8,128)(2,1)S(1)} %collective-permute-done.5.refs_1_), channel_id=1, source_target_pairs={{0,16},{1,9},{2,18},{3,11},{4,20},{5,13},{6,22},{7,15},{8,24},{9,1... | collective-permute-start | bytes 737288 | tf_op jit(solution)/shard_map/ppermute | solution.py:351
  16.1 4.3 %collective-permute-done.7.refs_2_ = bf16[176,768]{1,0:T(8,128)(2,1)S(1)} collective-permute-done((bf16[176,768]{1,0:T(8,128)(2,1)S(1)}, bf16[176,768]{1,0:T(8,128)(2,1)S(1)}, u32[]{:S(2)}, u32[]{:S(2)}) %collective-permute-start.7) | collective-permute-done | bytes 270368 | tf_op jit(solution)/shard_map/ppermute | solution.py:344
  20.4 1.5 %collective-permute-start.8 = (bf16[176,768]{1,0:T(8,128)(2,1)S(1)}, bf16[176,768]{1,0:T(8,128)(2,1)S(1)}, u32[]{:S(2)}, u32[]{:S(2)}) collective-permute-start(bf16[176,768]{1,0:T(8,128)(2,1)S(1)} %collective-permute-done.7.refs_2_), channel_id=1, source_target_pairs={{0,16},{1,9},{2,18},{3,11},{4,20},{5,13},{6,22},{7,15},{8,24},{9,1... | collective-permute-start | bytes 811016 | tf_op jit(solution)/shard_map/ppermute | solution.py:351
  22.2 2.0 %collective-permute-start.11 = (bf16[160,768]{1,0:T(8,128)(2,1)S(1)}, bf16[160,768]{1,0:T(8,128)(2,1)S(1)}, u32[]{:S(2)}, u32[]{:S(2)}) collective-permute-start(bf16[160,768]{1,0:T(8,128)(2,1)S(1)} %get-tuple-element.49), channel_id=1, source_target_pairs={{0,1},{1,0},{2,3},{3,2},{4,5},{5,4},{6,7},{7,6},{8,9},{9,8},{10,11... | collective-permute-start | bytes 737288 | tf_op jit(solution)/shard_map/ppermute | solution.py:356
  24.4 1.1 %shard_map.42 = (f32[1,640]{1,0:T(1,128)S(1)}, f32[1,320]{1,0:T(1,128)S(1)}) custom-call(bf16[336,768]{1,0:T(8,128)(2,1)S(1)} %get-tuple-element.45.block.refs_0_, bf16[336,768]{1,0:T(8,128)(2,1)S(1)} %shard_map.41.partner, bf16[336,768]{1,0:T(8,128)(2,1)S(1)} %get-tuple-element.45.block.refs_0_, bf16[160,768]{1,0:T(8,128)(2,1)S(1)} %collective-permute-done.5.refs_1_, ...), custom_call_target="tpu_custom_call" | custom-call | flops 320 | bytes 320 | tf_op jit(solution)/shard_map/pallas_call | solution.py:244
  25.5 1.3 %collective-permute-done.8.refs_5_ = bf16[176,768]{1,0:T(8,128)(2,1)S(1)} collective-permute-done((bf16[176,768]{1,0:T(8,128)(2,1)S(1)}, bf16[176,768]{1,0:T(8,128)(2,1)S(1)}, u32[]{:S(2)}, u32[]{:S(2)}) %collective-permute-start.8) | collective-permute-done | bytes 270368 | tf_op jit(solution)/shard_map/ppermute | solution.py:351
  27.0 1.1 %shard_map.44 = (f32[1,640]{1,0:T(1,128)S(1)}, f32[1,320]{1,0:T(1,128)S(1)}) custom-call(bf16[336,768]{1,0:T(8,128)(2,1)S(1)} %get-tuple-element.45.block.refs_0_, bf16[336,768]{1,0:T(8,128)(2,1)S(1)} %shard_map.41.partner, bf16[1280,768]{1,0:T(8,128)(2,1)S(1)} %get-tuple-element.50.held, f32[1,1280]{1,0:T(1,128)S(1)} %get-tuple-element.51.row), custom_call_target="tpu_custom_call" | custom-call | flops 320 | bytes 320 | tf_op jit(solution)/shard_map/pallas_call | solution.py:259
  28.7 1.4 %collective-permute-done.12.second = bf16[336,768]{1,0:T(8,128)(2,1)S(1)} collective-permute-done((bf16[336,768]{1,0:T(8,128)(2,1)S(1)}, bf16[336,768]{1,0:T(8,128)(2,1)S(1)}, u32[]{:S(2)}, u32[]{:S(2)}) %collective-permute-start.12) | collective-permute-done | bytes 516128 | tf_op jit(solution)/shard_map/ppermute | solution.py:371
  30.1 2.3 %shard_map.46 = (f32[1,320]{1,0:T(1,128)S(1)}, f32[1,320]{1,0:T(1,128)S(1)}, f32[1,320]{1,0:T(1,128)S(1)}, f32[1,320]{1,0:T(1,128)S(1)}, f32[1,640]{1,0:T(1,128)S(1)}) custom-call(bf16[320,768]{1,0:T(8,128)(2,1)S(1)} %get-tuple-element.57.first, bf16[336,768]{1,0:T(8,128)(2,1)S(1)} %collective-permute-done.12.second, ...), custom_call_target="tpu_custom_call" | custom-call | flops 320 | bytes 320 | tf_op jit(solution)/shard_map/pallas_call | solution.py:272
  32.5 1.1 %collective-permute-done.13 = f32[1,640]{1,0:T(1,128)S(1)} collective-permute-done((f32[1,640]{1,0:T(1,128)S(1)}, f32[1,640]{1,0:T(1,128)S(1)}, u32[]{:S(2)}, u32[]{:S(2)}) %collective-permute-start.13) | collective-permute-done | bytes 2592 | tf_op jit(solution)/shard_map/ppermute | solution.py:385
  33.6 1.3 %collective-permute-start.14 = (f32[1,640]{1,0:T(1,128)S(1)}, f32[1,640]{1,0:T(1,128)S(1)}, u32[]{:S(2)}, u32[]{:S(2)}) collective-permute-start(f32[1,640]{1,0:T(1,128)S(1)} %max.24), channel_id=1, source_target_pairs={{2,6},{4,0},{6,4},{1,7},{3,1},{5,3},{10,14},{12,8},{14,12},{9,15},... | collective-permute-start | bytes 7688 | tf_op jit(solution)/shard_map/ppermute | solution.py:389
  35.0 3.5 %collective-permute-start.15 = (f32[1,320]{1,0:T(1,128)S(1)}, f32[1,320]{1,0:T(1,128)S(1)}, u32[]{:S(2)}, u32[]{:S(2)}) collective-permute-start(f32[1,320]{1,0:T(1,128)S(1)} %get-tuple-element.65), channel_id=1, source_target_pairs={{0,9},{1,16},{2,11},{3,18},{4,13},{5,20},{6,15},{7,22},{8,1},{9,24... | collective-permute-start | bytes 3848 | tf_op jit(solution)/shard_map/ppermute | solution.py:396
  38.6 2.6 %collective-permute-start.17 = (f32[1,320]{1,0:T(1,128)S(1)}, f32[1,320]{1,0:T(1,128)S(1)}, u32[]{:S(2)}, u32[]{:S(2)}) collective-permute-start(f32[1,320]{1,0:T(1,128)S(1)} %get-tuple-element.67), channel_id=1, source_target_pairs={{0,25},{1,24},{2,27},{3,26},{4,29},{5,28},{6,31},{7,30},{8,17},{9,... | collective-permute-start | bytes 3848 | tf_op jit(solution)/shard_map/ppermute | solution.py:396
  41.5 1.0 %collective-permute-done.17 = f32[1,320]{1,0:T(1,128)S(1)} collective-permute-done((f32[1,320]{1,0:T(1,128)S(1)}, f32[1,320]{1,0:T(1,128)S(1)}, u32[]{:S(2)}, u32[]{:S(2)}) %collective-permute-start.17) | collective-permute-done | bytes 1312 | tf_op jit(solution)/shard_map/ppermute | solution.py:396
  42.5 0.6 %maximum_reduce_fusion = f32[320]{0:T(512)} fusion(f32[1,320]{1,0:T(1,128)S(1)} %collective-permute-done.18, f32[1,320]{1,0:T(1,128)S(1)} %collective-permute-done.17, f32[1,320]{1,0:T(1,128)S(1)} %collective-permute-done.16, f32[1,320]{1,0:T(1,128)S(1)} %collective-permute-done.15, f32[1,640]{1,0:T(1,128)S(1)} %broadcast_select_fusion), kind=kLoop, calls=%fused_computation.6 | loop fusion | flops 1280 | bytes 7680 | tf_op jit(solution)/shard_map/max | solution.py:401
  (34 shorter events, 2.0 us)
Async XLA Ops:
  0.0 24.2 %copy-start = (bf16[320,768]{1,0:T(8,128)(2,1)S(1)}, bf16[320,768]{1,0:T(8,128)(2,1)}, u32[]{:S(2)}) copy-start(bf16[320,768]{1,0:T(8,128)(2,1)} %embeddings.1) | copy-start | bytes 1474564
  0.0 6.6 %collective-permute-start.1 = (bf16[320,768]{1,0:T(8,128)(2,1)}, bf16[320,768]{1,0:T(8,128)(2,1)S(1)}, u32[]{:S(2)}, u32[]{:S(2)}) collective-permute-start(bf16[320,768]{1,0:T(8,128)(2,1)} %embeddings.1), channel_id=1, source_target_pairs={{0,1},{1,0},{2,3},{3,2},{4,5},{5,4},{6,7},{7,6},{8,9},{9,8},{10,11... | collective-permute-start | bytes 1474568 | tf_op jit(solution)/shard_map/ppermute | solution.py:341
  0.5 6.1 %collective-permute-start.2 = (s32[1,320]{1,0:T(1,128)}, s32[1,320]{1,0:T(1,128)S(1)}, u32[]{:S(2)}, u32[]{:S(2)}) collective-permute-start(s32[1,320]{1,0:T(1,128)} %bitcast.1), channel_id=1, source_target_pairs={{0,1},{1,0},{2,3},{3,2},{4,5},{5,4},{6,7},{7,6},{8,9},{9,8},{10,11... | collective-permute-start | bytes 3848 | tf_op jit(solution)/shard_map/ppermute | solution.py:341
  0.5 6.0 %collective-permute-start.3 = (s32[320]{0:T(512)}, s32[320]{0:T(512)S(1)}, u32[]{:S(2)}, u32[]{:S(2)}) collective-permute-start(s32[320]{0:T(512)} %order_key.1), channel_id=1, source_target_pairs={{0,1},{1,0},{2,3},{3,2},{4,5},{5,4},{6,7},{7,6},{8,9},{9,8},{10,11... | collective-permute-start | bytes 3848 | tf_op jit(solution)/shard_map/ppermute | solution.py:341
  1.0 20.9 %collective-permute-start = (bf16[320,768]{1,0:T(8,128)(2,1)}, bf16[320,768]{1,0:T(8,128)(2,1)S(1)}, u32[]{:S(2)}, u32[]{:S(2)}) collective-permute-start(bf16[320,768]{1,0:T(8,128)(2,1)} %embeddings.1), channel_id=1, source_target_pairs={{6,2},{0,4},{4,6},{7,1},{1,3},{3,5},{14,10},{8,12},{12,14},{15,9},... | collective-permute-start | bytes 1474568 | tf_op jit(solution)/shard_map/ppermute | solution.py:340
  6.8 8.6 %collective-permute-start.5 = (bf16[160,768]{1,0:T(8,128)(2,1)S(1)}, bf16[160,768]{1,0:T(8,128)(2,1)S(1)}, u32[]{:S(2)}, u32[]{:S(2)}) collective-permute-start(bf16[160,768]{1,0:T(8,128)(2,1)S(1)} %get-tuple-element.41), channel_id=1, source_target_pairs={{0,8},{1,17},{2,10},{3,19},{4,12},{5,21},{6,14},{7,23},{8,0},{9,25... | collective-permute-start | bytes 737288 | tf_op jit(solution)/shard_map/ppermute | solution.py:344
  8.3 12.1 %collective-permute-start.7 = (bf16[176,768]{1,0:T(8,128)(2,1)S(1)}, bf16[176,768]{1,0:T(8,128)(2,1)S(1)}, u32[]{:S(2)}, u32[]{:S(2)}) collective-permute-start(bf16[176,768]{1,0:T(8,128)(2,1)S(1)} %get-tuple-element.42), channel_id=1, source_target_pairs={{0,8},{1,17},{2,10},{3,19},{4,12},{5,21},{6,14},{7,23},{8,0},{9,25... | collective-permute-start | bytes 811016 | tf_op jit(solution)/shard_map/ppermute | solution.py:344
  8.9 0.7 %copy-start.1 = (s32[320]{0:T(512)S(1)}, s32[320]{0:T(512)}, u32[]{:S(2)}) copy-start(s32[320]{0:T(512)} %order_key.1) | copy-start | bytes 3844
  9.5 0.7 %copy-start.2 = (s32[320,1]{0,1:T(1,128)S(1)}, s32[320,1]{0,1:T(1,128)}, u32[]{:S(2)}) copy-start(s32[320,1]{0,1:T(1,128)} %param.4) | copy-start | bytes 3844
  10.2 16.6 %collective-permute-start.9 = (bf16[336,768]{1,0:T(8,128)(2,1)S(1)}, bf16[336,768]{1,0:T(8,128)(2,1)S(1)}, u32[]{:S(2)}, u32[]{:S(2)}) collective-permute-start(bf16[336,768]{1,0:T(8,128)(2,1)S(1)} %get-tuple-element.45.block.refs_0_), channel_id=1, source_target_pairs={{0,16},{1,9},{2,18},{3,11},{4,20},{5,13},{6,22},{7,15},{8,24},{9,1... | collective-permute-start | bytes 1548296 | tf_op jit(solution)/shard_map/ppermute | solution.py:347
  11.9 16.3 %collective-permute-start.4 = (bf16[336,768]{1,0:T(8,128)(2,1)S(1)}, bf16[336,768]{1,0:T(8,128)(2,1)S(1)}, u32[]{:S(2)}, u32[]{:S(2)}) collective-permute-start(bf16[336,768]{1,0:T(8,128)(2,1)S(1)} %shard_map.40), channel_id=1, source_target_pairs={{6,2},{0,4},{4,6},{7,1},{1,3},{3,5},{14,10},{8,12},{12,14},{15,9},... | collective-permute-start | bytes 1548296 | tf_op jit(solution)/shard_map/ppermute | solution.py:350
  15.4 6.9 %collective-permute-start.6 = (bf16[160,768]{1,0:T(8,128)(2,1)S(1)}, bf16[160,768]{1,0:T(8,128)(2,1)S(1)}, u32[]{:S(2)}, u32[]{:S(2)}) collective-permute-start(bf16[160,768]{1,0:T(8,128)(2,1)S(1)} %collective-permute-done.5.refs_1_), channel_id=1, source_target_pairs={{0,16},{1,9},{2,18},{3,11},{4,20},{5,13},{6,22},{7,15},{8,24},{9,1... | collective-permute-start | bytes 737288 | tf_op jit(solution)/shard_map/ppermute | solution.py:351
  20.4 6.5 %collective-permute-start.8 = (bf16[176,768]{1,0:T(8,128)(2,1)S(1)}, bf16[176,768]{1,0:T(8,128)(2,1)S(1)}, u32[]{:S(2)}, u32[]{:S(2)}) collective-permute-start(bf16[176,768]{1,0:T(8,128)(2,1)S(1)} %collective-permute-done.7.refs_2_), channel_id=1, source_target_pairs={{0,16},{1,9},{2,18},{3,11},{4,20},{5,13},{6,22},{7,15},{8,24},{9,1... | collective-permute-start | bytes 811016 | tf_op jit(solution)/shard_map/ppermute | solution.py:351
  22.1 4.8 %collective-permute-start.10 = (bf16[160,768]{1,0:T(8,128)(2,1)S(1)}, bf16[160,768]{1,0:T(8,128)(2,1)S(1)}, u32[]{:S(2)}, u32[]{:S(2)}) collective-permute-start(bf16[160,768]{1,0:T(8,128)(2,1)S(1)} %get-tuple-element.48), channel_id=1, source_target_pairs={{0,1},{1,0},{2,3},{3,2},{4,5},{5,4},{6,7},{7,6},{8,9},{9,8},{10,11... | collective-permute-start | bytes 737288 | tf_op jit(solution)/shard_map/ppermute | solution.py:356
  22.2 4.6 %collective-permute-start.11 = (bf16[160,768]{1,0:T(8,128)(2,1)S(1)}, bf16[160,768]{1,0:T(8,128)(2,1)S(1)}, u32[]{:S(2)}, u32[]{:S(2)}) collective-permute-start(bf16[160,768]{1,0:T(8,128)(2,1)S(1)} %get-tuple-element.49), channel_id=1, source_target_pairs={{0,1},{1,0},{2,3},{3,2},{4,5},{5,4},{6,7},{7,6},{8,9},{9,8},{10,11... | collective-permute-start | bytes 737288 | tf_op jit(solution)/shard_map/ppermute | solution.py:356
  28.1 2.0 %collective-permute-start.12 = (bf16[336,768]{1,0:T(8,128)(2,1)S(1)}, bf16[336,768]{1,0:T(8,128)(2,1)S(1)}, u32[]{:S(2)}, u32[]{:S(2)}) collective-permute-start(bf16[336,768]{1,0:T(8,128)(2,1)S(1)} %collective-permute-done.4.second), channel_id=1, source_target_pairs={{0,1},{1,0},{2,3},{3,2},{4,5},{5,4},{6,7},{7,6},{8,9},{9,8},{10,11... | collective-permute-start | bytes 1548296 | tf_op jit(solution)/shard_map/ppermute | solution.py:371
  32.4 1.2 %collective-permute-start.13 = (f32[1,640]{1,0:T(1,128)S(1)}, f32[1,640]{1,0:T(1,128)S(1)}, u32[]{:S(2)}, u32[]{:S(2)}) collective-permute-start(f32[1,640]{1,0:T(1,128)S(1)} %get-tuple-element.59), channel_id=1, source_target_pairs={{0,1},{1,0},{2,3},{3,2},{4,5},{5,4},{6,7},{7,6},{8,9},{9,8},{10,11... | collective-permute-start | bytes 7688 | tf_op jit(solution)/shard_map/ppermute | solution.py:385
  33.6 7.6 %collective-permute-start.14 = (f32[1,640]{1,0:T(1,128)S(1)}, f32[1,640]{1,0:T(1,128)S(1)}, u32[]{:S(2)}, u32[]{:S(2)}) collective-permute-start(f32[1,640]{1,0:T(1,128)S(1)} %max.24), channel_id=1, source_target_pairs={{2,6},{4,0},{6,4},{1,7},{3,1},{5,3},{10,14},{12,8},{14,12},{9,15},... | collective-permute-start | bytes 7688 | tf_op jit(solution)/shard_map/ppermute | solution.py:389
  35.0 6.3 %collective-permute-start.15 = (f32[1,320]{1,0:T(1,128)S(1)}, f32[1,320]{1,0:T(1,128)S(1)}, u32[]{:S(2)}, u32[]{:S(2)}) collective-permute-start(f32[1,320]{1,0:T(1,128)S(1)} %get-tuple-element.65), channel_id=1, source_target_pairs={{0,9},{1,16},{2,11},{3,18},{4,13},{5,20},{6,15},{7,22},{8,1},{9,24... | collective-permute-start | bytes 3848 | tf_op jit(solution)/shard_map/ppermute | solution.py:396
  38.5 3.0 %collective-permute-start.16 = (f32[1,320]{1,0:T(1,128)S(1)}, f32[1,320]{1,0:T(1,128)S(1)}, u32[]{:S(2)}, u32[]{:S(2)}) collective-permute-start(f32[1,320]{1,0:T(1,128)S(1)} %get-tuple-element.66), channel_id=1, source_target_pairs={{0,17},{1,8},{2,19},{3,10},{4,21},{5,12},{6,23},{7,14},{8,25},{9,0... | collective-permute-start | bytes 3848 | tf_op jit(solution)/shard_map/ppermute | solution.py:396
  38.6 3.9 %collective-permute-start.17 = (f32[1,320]{1,0:T(1,128)S(1)}, f32[1,320]{1,0:T(1,128)S(1)}, u32[]{:S(2)}, u32[]{:S(2)}) collective-permute-start(f32[1,320]{1,0:T(1,128)S(1)} %get-tuple-element.67), channel_id=1, source_target_pairs={{0,25},{1,24},{2,27},{3,26},{4,29},{5,28},{6,31},{7,30},{8,17},{9,... | collective-permute-start | bytes 3848 | tf_op jit(solution)/shard_map/ppermute | solution.py:396
  41.3 1.2 %collective-permute-start.18 = (f32[1,320]{1,0:T(1,128)S(1)}, f32[1,320]{1,0:T(1,128)S(1)}, u32[]{:S(2)}, u32[]{:S(2)}) collective-permute-start(f32[1,320]{1,0:T(1,128)S(1)} %fusion), channel_id=1, source_target_pairs={{0,1},{1,0},{2,3},{3,2},{4,5},{5,4},{6,7},{7,6},{8,9},{9,8},{10,11... | collective-permute-start | bytes 3848 | tf_op jit(solution)/shard_map/ppermute | solution.py:400

commit v29 on v28

--- a/solution.py
+++ b/solution.py
@@ -99,12 +99,7 @@
 
 
 def meet(units, parts, rows, span, held, held_codes):
-    low = -(2**31)
-    columns = [turned_to_column(row, rows).astype(jnp.int32) for row, _ in parts]
-    after = [column + (2**31 - 1) for column in columns]
-    before = [column + (low + 1) for column in columns]
-    held_codes = held_codes.astype(jnp.int32)
-    limit = low + span - 1
+    columns = [turned_to_column(row, rows) for row, _ in parts]
     starts = [(block, top) for block in range(len(parts)) for top in range(0, rows, CHUNK)]
     partial = {start: jnp.full((CHUNK, LANES), -1.0, jnp.float32) for start in starts}
     best_held = []
@@ -122,17 +117,22 @@
         best = [jnp.full((CHUNK, LANES), -1.0, jnp.float32) for _ in range(0, tile, LANES)]
         for block, top in starts:
             to_block, to_held = parts[block][1]
+            mine = columns[block][top : top + CHUNK]
             for lane in range(0, tile, LANES):
                 part = sims[block][top : top + CHUNK, lane : lane + LANES]
-                theirs = held_codes[:, at + lane : at + lane + LANES]
+                gap = mine - held_codes[:, at + lane : at + lane + LANES]
+                if to_block and to_held:
+                    part = jnp.where(jnp.abs(gap) < span, part, -1.0)
+                    later = gap > 0.0
+                    ours, theirs = jnp.where(later, part, -1.0), jnp.where(later, -1.0, part)
+                elif to_block:
+                    ours = jnp.where((gap > 0.0) & (gap < span), part, -1.0)
+                else:
+                    theirs = jnp.where((gap < 0.0) & (gap > -span), part, -1.0)
                 if to_block:
-                    earlier = after[block][top : top + CHUNK] - theirs < limit
-                    ours = jnp.where(earlier, part, -1.0)
                     partial[block, top] = jnp.maximum(partial[block, top], ours)
                 if to_held:
-                    earlier = theirs - before[block][top : top + CHUNK] < limit
-                    other = jnp.where(earlier, part, -1.0)
-                    best[lane // LANES] = jnp.maximum(best[lane // LANES], other)
+                    best[lane // LANES] = jnp.maximum(best[lane // LANES], theirs)
         best_held += [jnp.max(some, axis=0, keepdims=True) for some in best]
     found = [
         row_from_partial(

time: 43.3 us -> 43.1 us (level)
  no operation moved by 1% of the time
where the time goes in v29:
time: 43.1 us; the launch traced here: 42.9 us
  starting transfers between devices  25.9 us (60%)
  waiting for transfers between devices  9.41 us (22%)
  Pallas kernels  5.29 us (12%)
  local copies, waits for them, and re-layouts  1.36 us (3%)
  other arithmetic  0.69 us (2%)
    ppermute x3, starting transfers between devices, shards(): lax.ppermute(best, BOTH, pairs)  6.15 us
    ppermute x1, starting transfers between devices, shards(): raw = [lax.ppermute(embeddings, BOTH, pairs) for pairs in rounds]  5.57 us
    ppermute x2, waiting for transfers between devices, shards(): from_first = [lax.ppermute(part, BOTH, first) for part in parts]  4.28 us
    ppermute x1, starting transfers between devices, shards(): near_other = [lax.ppermute(both, BOTH, pairs) for pairs in rounds]  3.49 us
    ppermute x2, starting transfers between devices, shards(): from_corner = [lax.ppermute(part, BOTH, second) for part in from_first]  2.26 us
    pallas_call x2, Pallas kernels, line(): pl.pallas_call(functools.partial(line_kernel, rows, span, together, len(b...  2.26 us
    ppermute x2, starting transfers between devices, shards(): from_first = [lax.ppermute(part, BOTH, first) for part in parts]  2.09 us
    ppermute x2, starting transfers between devices, shards(): lax.ppermute(piece, BOTH, other_core)  2.03 us
  transfers between devices with their start and end apart: 19, of which 7 were waited for; matrix products, arithmetic and copies ran while one was open for 0% of the time, Pallas kernels for 7%

profile of v29, /device:TPU:0, one launch (start us, length us, event | category | flops | bytes accessed | tf_op | source)
XLA Modules:
  0.0 42.9 jit_solution(5083985048942765735)
XLA Ops:
  0.0 0.5 %collective-permute-start.1 = (bf16[320,768]{1,0:T(8,128)(2,1)}, bf16[320,768]{1,0:T(8,128)(2,1)S(1)}, u32[]{:S(2)}, u32[]{:S(2)}) collective-permute-start(bf16[320,768]{1,0:T(8,128)(2,1)} %embeddings.1), channel_id=1, source_target_pairs={{0,1},{1,0},{2,3},{3,2},{4,5},{5,4},{6,7},{7,6},{8,9},{9,8},{10,11... | collective-permute-start | bytes 1474568 | tf_op jit(solution)/shard_map/ppermute | solution.py:341
  0.5 0.4 %collective-permute-start.3 = (s32[320]{0:T(512)}, s32[320]{0:T(512)S(1)}, u32[]{:S(2)}, u32[]{:S(2)}) collective-permute-start(s32[320]{0:T(512)} %order_key.1), channel_id=1, source_target_pairs={{0,1},{1,0},{2,3},{3,2},{4,5},{5,4},{6,7},{7,6},{8,9},{9,8},{10,11... | collective-permute-start | bytes 3848 | tf_op jit(solution)/shard_map/ppermute | solution.py:341
  1.0 5.6 %collective-permute-start = (bf16[320,768]{1,0:T(8,128)(2,1)}, bf16[320,768]{1,0:T(8,128)(2,1)S(1)}, u32[]{:S(2)}, u32[]{:S(2)}) collective-permute-start(bf16[320,768]{1,0:T(8,128)(2,1)} %embeddings.1), channel_id=1, source_target_pairs={{6,2},{0,4},{4,6},{7,1},{1,3},{3,5},{14,10},{8,12},{12,14},{15,9},... | collective-permute-start | bytes 1474568 | tf_op jit(solution)/shard_map/ppermute | solution.py:340
  6.8 1.6 %collective-permute-start.5 = (bf16[160,768]{1,0:T(8,128)(2,1)S(1)}, bf16[160,768]{1,0:T(8,128)(2,1)S(1)}, u32[]{:S(2)}, u32[]{:S(2)}) collective-permute-start(bf16[160,768]{1,0:T(8,128)(2,1)S(1)} %get-tuple-element.41), channel_id=1, source_target_pairs={{0,8},{1,17},{2,10},{3,19},{4,12},{5,21},{6,14},{7,23},{8,0},{9,25... | collective-permute-start | bytes 737288 | tf_op jit(solution)/shard_map/ppermute | solution.py:344
  8.3 0.5 %collective-permute-start.7 = (bf16[176,768]{1,0:T(8,128)(2,1)S(1)}, bf16[176,768]{1,0:T(8,128)(2,1)S(1)}, u32[]{:S(2)}, u32[]{:S(2)}) collective-permute-start(bf16[176,768]{1,0:T(8,128)(2,1)S(1)} %get-tuple-element.42), channel_id=1, source_target_pairs={{0,8},{1,17},{2,10},{3,19},{4,12},{5,21},{6,14},{7,23},{8,0},{9,25... | collective-permute-start | bytes 811016 | tf_op jit(solution)/shard_map/ppermute | solution.py:344
  8.9 0.7 %copy-done.1 = s32[320]{0:T(512)S(1)} copy-done((s32[320]{0:T(512)S(1)}, s32[320]{0:T(512)}, u32[]{:S(2)}) %copy-start.1) | copy-done | bytes 1304
  9.5 0.7 %copy-done.2 = s32[320,1]{0,1:T(1,128)S(1)} copy-done((s32[320,1]{0,1:T(1,128)S(1)}, s32[320,1]{0,1:T(1,128)}, u32[]{:S(2)}) %copy-start.2) | copy-done | bytes 1304
  10.2 1.6 %collective-permute-start.9 = (bf16[336,768]{1,0:T(8,128)(2,1)S(1)}, bf16[336,768]{1,0:T(8,128)(2,1)S(1)}, u32[]{:S(2)}, u32[]{:S(2)}) collective-permute-start(bf16[336,768]{1,0:T(8,128)(2,1)S(1)} %get-tuple-element.45.block.refs_0_), channel_id=1, source_target_pairs={{0,16},{1,9},{2,18},{3,11},{4,20},{5,13},{6,22},{7,15},{8,24},{9,1... | collective-permute-start | bytes 1548296 | tf_op jit(solution)/shard_map/ppermute | solution.py:347
  11.9 3.5 %collective-permute-start.4 = (bf16[336,768]{1,0:T(8,128)(2,1)S(1)}, bf16[336,768]{1,0:T(8,128)(2,1)S(1)}, u32[]{:S(2)}, u32[]{:S(2)}) collective-permute-start(bf16[336,768]{1,0:T(8,128)(2,1)S(1)} %shard_map.40), channel_id=1, source_target_pairs={{6,2},{0,4},{4,6},{7,1},{1,3},{3,5},{14,10},{8,12},{12,14},{15,9},... | collective-permute-start | bytes 1548296 | tf_op jit(solution)/shard_map/ppermute | solution.py:350
  15.4 0.7 %collective-permute-start.6 = (bf16[160,768]{1,0:T(8,128)(2,1)S(1)}, bf16[160,768]{1,0:T(8,128)(2,1)S(1)}, u32[]{:S(2)}, u32[]{:S(2)}) collective-permute-start(bf16[160,768]{1,0:T(8,128)(2,1)S(1)} %collective-permute-done.5.refs_1_), channel_id=1, source_target_pairs={{0,16},{1,9},{2,18},{3,11},{4,20},{5,13},{6,22},{7,15},{8,24},{9,1... | collective-permute-start | bytes 737288 | tf_op jit(solution)/shard_map/ppermute | solution.py:351
  16.1 4.3 %collective-permute-done.7.refs_2_ = bf16[176,768]{1,0:T(8,128)(2,1)S(1)} collective-permute-done((bf16[176,768]{1,0:T(8,128)(2,1)S(1)}, bf16[176,768]{1,0:T(8,128)(2,1)S(1)}, u32[]{:S(2)}, u32[]{:S(2)}) %collective-permute-start.7) | collective-permute-done | bytes 270368 | tf_op jit(solution)/shard_map/ppermute | solution.py:344
  20.4 1.5 %collective-permute-start.8 = (bf16[176,768]{1,0:T(8,128)(2,1)S(1)}, bf16[176,768]{1,0:T(8,128)(2,1)S(1)}, u32[]{:S(2)}, u32[]{:S(2)}) collective-permute-start(bf16[176,768]{1,0:T(8,128)(2,1)S(1)} %collective-permute-done.7.refs_2_), channel_id=1, source_target_pairs={{0,16},{1,9},{2,18},{3,11},{4,20},{5,13},{6,22},{7,15},{8,24},{9,1... | collective-permute-start | bytes 811016 | tf_op jit(solution)/shard_map/ppermute | solution.py:351
  22.2 2.0 %collective-permute-start.11 = (bf16[160,768]{1,0:T(8,128)(2,1)S(1)}, bf16[160,768]{1,0:T(8,128)(2,1)S(1)}, u32[]{:S(2)}, u32[]{:S(2)}) collective-permute-start(bf16[160,768]{1,0:T(8,128)(2,1)S(1)} %get-tuple-element.49), channel_id=1, source_target_pairs={{0,1},{1,0},{2,3},{3,2},{4,5},{5,4},{6,7},{7,6},{8,9},{9,8},{10,11... | collective-permute-start | bytes 737288 | tf_op jit(solution)/shard_map/ppermute | solution.py:356
  24.4 1.1 %shard_map.42 = (f32[1,640]{1,0:T(1,128)S(1)}, f32[1,320]{1,0:T(1,128)S(1)}) custom-call(bf16[336,768]{1,0:T(8,128)(2,1)S(1)} %get-tuple-element.45.block.refs_0_, bf16[336,768]{1,0:T(8,128)(2,1)S(1)} %shard_map.41.partner, bf16[336,768]{1,0:T(8,128)(2,1)S(1)} %get-tuple-element.45.block.refs_0_, bf16[160,768]{1,0:T(8,128)(2,1)S(1)} %collective-permute-done.5.refs_1_, ...), custom_call_target="tpu_custom_call" | custom-call | flops 320 | bytes 320 | tf_op jit(solution)/shard_map/pallas_call | solution.py:244
  25.5 1.3 %collective-permute-done.8.refs_5_ = bf16[176,768]{1,0:T(8,128)(2,1)S(1)} collective-permute-done((bf16[176,768]{1,0:T(8,128)(2,1)S(1)}, bf16[176,768]{1,0:T(8,128)(2,1)S(1)}, u32[]{:S(2)}, u32[]{:S(2)}) %collective-permute-start.8) | collective-permute-done | bytes 270368 | tf_op jit(solution)/shard_map/ppermute | solution.py:351
  27.0 1.1 %shard_map.44 = (f32[1,640]{1,0:T(1,128)S(1)}, f32[1,320]{1,0:T(1,128)S(1)}) custom-call(bf16[336,768]{1,0:T(8,128)(2,1)S(1)} %get-tuple-element.45.block.refs_0_, bf16[336,768]{1,0:T(8,128)(2,1)S(1)} %shard_map.41.partner, bf16[1280,768]{1,0:T(8,128)(2,1)S(1)} %get-tuple-element.50.held, f32[1,1280]{1,0:T(1,128)S(1)} %get-tuple-element.51.row), custom_call_target="tpu_custom_call" | custom-call | flops 320 | bytes 320 | tf_op jit(solution)/shard_map/pallas_call | solution.py:259
  28.7 1.4 %collective-permute-done.12.second = bf16[336,768]{1,0:T(8,128)(2,1)S(1)} collective-permute-done((bf16[336,768]{1,0:T(8,128)(2,1)S(1)}, bf16[336,768]{1,0:T(8,128)(2,1)S(1)}, u32[]{:S(2)}, u32[]{:S(2)}) %collective-permute-start.12) | collective-permute-done | bytes 516128 | tf_op jit(solution)/shard_map/ppermute | solution.py:371
  30.1 2.1 %shard_map.46 = (f32[1,320]{1,0:T(1,128)S(1)}, f32[1,320]{1,0:T(1,128)S(1)}, f32[1,320]{1,0:T(1,128)S(1)}, f32[1,320]{1,0:T(1,128)S(1)}, f32[1,640]{1,0:T(1,128)S(1)}) custom-call(bf16[320,768]{1,0:T(8,128)(2,1)S(1)} %get-tuple-element.57.first, bf16[336,768]{1,0:T(8,128)(2,1)S(1)} %collective-permute-done.12.second, ...), custom_call_target="tpu_custom_call" | custom-call | flops 320 | bytes 320 | tf_op jit(solution)/shard_map/pallas_call | solution.py:272
  32.3 1.1 %collective-permute-done.13 = f32[1,640]{1,0:T(1,128)S(1)} collective-permute-done((f32[1,640]{1,0:T(1,128)S(1)}, f32[1,640]{1,0:T(1,128)S(1)}, u32[]{:S(2)}, u32[]{:S(2)}) %collective-permute-start.13) | collective-permute-done | bytes 2592 | tf_op jit(solution)/shard_map/ppermute | solution.py:385
  33.5 1.3 %collective-permute-start.14 = (f32[1,640]{1,0:T(1,128)S(1)}, f32[1,640]{1,0:T(1,128)S(1)}, u32[]{:S(2)}, u32[]{:S(2)}) collective-permute-start(f32[1,640]{1,0:T(1,128)S(1)} %max.24), channel_id=1, source_target_pairs={{2,6},{4,0},{6,4},{1,7},{3,1},{5,3},{10,14},{12,8},{14,12},{9,15},... | collective-permute-start | bytes 7688 | tf_op jit(solution)/shard_map/ppermute | solution.py:389
  34.8 3.5 %collective-permute-start.15 = (f32[1,320]{1,0:T(1,128)S(1)}, f32[1,320]{1,0:T(1,128)S(1)}, u32[]{:S(2)}, u32[]{:S(2)}) collective-permute-start(f32[1,320]{1,0:T(1,128)S(1)} %get-tuple-element.65), channel_id=1, source_target_pairs={{0,9},{1,16},{2,11},{3,18},{4,13},{5,20},{6,15},{7,22},{8,1},{9,24... | collective-permute-start | bytes 3848 | tf_op jit(solution)/shard_map/ppermute | solution.py:396
  38.4 2.6 %collective-permute-start.17 = (f32[1,320]{1,0:T(1,128)S(1)}, f32[1,320]{1,0:T(1,128)S(1)}, u32[]{:S(2)}, u32[]{:S(2)}) collective-permute-start(f32[1,320]{1,0:T(1,128)S(1)} %get-tuple-element.67), channel_id=1, source_target_pairs={{0,25},{1,24},{2,27},{3,26},{4,29},{5,28},{6,31},{7,30},{8,17},{9,... | collective-permute-start | bytes 3848 | tf_op jit(solution)/shard_map/ppermute | solution.py:396
  41.3 1.0 %collective-permute-done.17 = f32[1,320]{1,0:T(1,128)S(1)} collective-permute-done((f32[1,320]{1,0:T(1,128)S(1)}, f32[1,320]{1,0:T(1,128)S(1)}, u32[]{:S(2)}, u32[]{:S(2)}) %collective-permute-start.17) | collective-permute-done | bytes 1312 | tf_op jit(solution)/shard_map/ppermute | solution.py:396
  42.3 0.6 %maximum_reduce_fusion = f32[320]{0:T(512)} fusion(f32[1,320]{1,0:T(1,128)S(1)} %collective-permute-done.18, f32[1,320]{1,0:T(1,128)S(1)} %collective-permute-done.17, f32[1,320]{1,0:T(1,128)S(1)} %collective-permute-done.16, f32[1,320]{1,0:T(1,128)S(1)} %collective-permute-done.15, f32[1,640]{1,0:T(1,128)S(1)} %broadcast_select_fusion), kind=kLoop, calls=%fused_computation.6 | loop fusion | flops 1280 | bytes 7680 | tf_op jit(solution)/shard_map/max | solution.py:401
  (34 shorter events, 2.0 us)
Async XLA Ops:
  0.0 24.2 %copy-start = (bf16[320,768]{1,0:T(8,128)(2,1)S(1)}, bf16[320,768]{1,0:T(8,128)(2,1)}, u32[]{:S(2)}) copy-start(bf16[320,768]{1,0:T(8,128)(2,1)} %embeddings.1) | copy-start | bytes 1474564
  0.0 6.6 %collective-permute-start.1 = (bf16[320,768]{1,0:T(8,128)(2,1)}, bf16[320,768]{1,0:T(8,128)(2,1)S(1)}, u32[]{:S(2)}, u32[]{:S(2)}) collective-permute-start(bf16[320,768]{1,0:T(8,128)(2,1)} %embeddings.1), channel_id=1, source_target_pairs={{0,1},{1,0},{2,3},{3,2},{4,5},{5,4},{6,7},{7,6},{8,9},{9,8},{10,11... | collective-permute-start | bytes 1474568 | tf_op jit(solution)/shard_map/ppermute | solution.py:341
  0.5 6.1 %collective-permute-start.2 = (s32[1,320]{1,0:T(1,128)}, s32[1,320]{1,0:T(1,128)S(1)}, u32[]{:S(2)}, u32[]{:S(2)}) collective-permute-start(s32[1,320]{1,0:T(1,128)} %bitcast.1), channel_id=1, source_target_pairs={{0,1},{1,0},{2,3},{3,2},{4,5},{5,4},{6,7},{7,6},{8,9},{9,8},{10,11... | collective-permute-start | bytes 3848 | tf_op jit(solution)/shard_map/ppermute | solution.py:341
  0.5 6.0 %collective-permute-start.3 = (s32[320]{0:T(512)}, s32[320]{0:T(512)S(1)}, u32[]{:S(2)}, u32[]{:S(2)}) collective-permute-start(s32[320]{0:T(512)} %order_key.1), channel_id=1, source_target_pairs={{0,1},{1,0},{2,3},{3,2},{4,5},{5,4},{6,7},{7,6},{8,9},{9,8},{10,11... | collective-permute-start | bytes 3848 | tf_op jit(solution)/shard_map/ppermute | solution.py:341
  1.0 20.9 %collective-permute-start = (bf16[320,768]{1,0:T(8,128)(2,1)}, bf16[320,768]{1,0:T(8,128)(2,1)S(1)}, u32[]{:S(2)}, u32[]{:S(2)}) collective-permute-start(bf16[320,768]{1,0:T(8,128)(2,1)} %embeddings.1), channel_id=1, source_target_pairs={{6,2},{0,4},{4,6},{7,1},{1,3},{3,5},{14,10},{8,12},{12,14},{15,9},... | collective-permute-start | bytes 1474568 | tf_op jit(solution)/shard_map/ppermute | solution.py:340
  6.8 8.6 %collective-permute-start.5 = (bf16[160,768]{1,0:T(8,128)(2,1)S(1)}, bf16[160,768]{1,0:T(8,128)(2,1)S(1)}, u32[]{:S(2)}, u32[]{:S(2)}) collective-permute-start(bf16[160,768]{1,0:T(8,128)(2,1)S(1)} %get-tuple-element.41), channel_id=1, source_target_pairs={{0,8},{1,17},{2,10},{3,19},{4,12},{5,21},{6,14},{7,23},{8,0},{9,25... | collective-permute-start | bytes 737288 | tf_op jit(solution)/shard_map/ppermute | solution.py:344
  8.3 12.1 %collective-permute-start.7 = (bf16[176,768]{1,0:T(8,128)(2,1)S(1)}, bf16[176,768]{1,0:T(8,128)(2,1)S(1)}, u32[]{:S(2)}, u32[]{:S(2)}) collective-permute-start(bf16[176,768]{1,0:T(8,128)(2,1)S(1)} %get-tuple-element.42), channel_id=1, source_target_pairs={{0,8},{1,17},{2,10},{3,19},{4,12},{5,21},{6,14},{7,23},{8,0},{9,25... | collective-permute-start | bytes 811016 | tf_op jit(solution)/shard_map/ppermute | solution.py:344
  8.9 0.7 %copy-start.1 = (s32[320]{0:T(512)S(1)}, s32[320]{0:T(512)}, u32[]{:S(2)}) copy-start(s32[320]{0:T(512)} %order_key.1) | copy-start | bytes 3844
  9.5 0.7 %copy-start.2 = (s32[320,1]{0,1:T(1,128)S(1)}, s32[320,1]{0,1:T(1,128)}, u32[]{:S(2)}) copy-start(s32[320,1]{0,1:T(1,128)} %param.4) | copy-start | bytes 3844
  10.2 16.6 %collective-permute-start.9 = (bf16[336,768]{1,0:T(8,128)(2,1)S(1)}, bf16[336,768]{1,0:T(8,128)(2,1)S(1)}, u32[]{:S(2)}, u32[]{:S(2)}) collective-permute-start(bf16[336,768]{1,0:T(8,128)(2,1)S(1)} %get-tuple-element.45.block.refs_0_), channel_id=1, source_target_pairs={{0,16},{1,9},{2,18},{3,11},{4,20},{5,13},{6,22},{7,15},{8,24},{9,1... | collective-permute-start | bytes 1548296 | tf_op jit(solution)/shard_map/ppermute | solution.py:347
  11.9 16.3 %collective-permute-start.4 = (bf16[336,768]{1,0:T(8,128)(2,1)S(1)}, bf16[336,768]{1,0:T(8,128)(2,1)S(1)}, u32[]{:S(2)}, u32[]{:S(2)}) collective-permute-start(bf16[336,768]{1,0:T(8,128)(2,1)S(1)} %shard_map.40), channel_id=1, source_target_pairs={{6,2},{0,4},{4,6},{7,1},{1,3},{3,5},{14,10},{8,12},{12,14},{15,9},... | collective-permute-start | bytes 1548296 | tf_op jit(solution)/shard_map/ppermute | solution.py:350
  15.4 6.9 %collective-permute-start.6 = (bf16[160,768]{1,0:T(8,128)(2,1)S(1)}, bf16[160,768]{1,0:T(8,128)(2,1)S(1)}, u32[]{:S(2)}, u32[]{:S(2)}) collective-permute-start(bf16[160,768]{1,0:T(8,128)(2,1)S(1)} %collective-permute-done.5.refs_1_), channel_id=1, source_target_pairs={{0,16},{1,9},{2,18},{3,11},{4,20},{5,13},{6,22},{7,15},{8,24},{9,1... | collective-permute-start | bytes 737288 | tf_op jit(solution)/shard_map/ppermute | solution.py:351
  20.4 6.5 %collective-permute-start.8 = (bf16[176,768]{1,0:T(8,128)(2,1)S(1)}, bf16[176,768]{1,0:T(8,128)(2,1)S(1)}, u32[]{:S(2)}, u32[]{:S(2)}) collective-permute-start(bf16[176,768]{1,0:T(8,128)(2,1)S(1)} %collective-permute-done.7.refs_2_), channel_id=1, source_target_pairs={{0,16},{1,9},{2,18},{3,11},{4,20},{5,13},{6,22},{7,15},{8,24},{9,1... | collective-permute-start | bytes 811016 | tf_op jit(solution)/shard_map/ppermute | solution.py:351
  22.1 4.8 %collective-permute-start.10 = (bf16[160,768]{1,0:T(8,128)(2,1)S(1)}, bf16[160,768]{1,0:T(8,128)(2,1)S(1)}, u32[]{:S(2)}, u32[]{:S(2)}) collective-permute-start(bf16[160,768]{1,0:T(8,128)(2,1)S(1)} %get-tuple-element.48), channel_id=1, source_target_pairs={{0,1},{1,0},{2,3},{3,2},{4,5},{5,4},{6,7},{7,6},{8,9},{9,8},{10,11... | collective-permute-start | bytes 737288 | tf_op jit(solution)/shard_map/ppermute | solution.py:356
  22.2 4.6 %collective-permute-start.11 = (bf16[160,768]{1,0:T(8,128)(2,1)S(1)}, bf16[160,768]{1,0:T(8,128)(2,1)S(1)}, u32[]{:S(2)}, u32[]{:S(2)}) collective-permute-start(bf16[160,768]{1,0:T(8,128)(2,1)S(1)} %get-tuple-element.49), channel_id=1, source_target_pairs={{0,1},{1,0},{2,3},{3,2},{4,5},{5,4},{6,7},{7,6},{8,9},{9,8},{10,11... | collective-permute-start | bytes 737288 | tf_op jit(solution)/shard_map/ppermute | solution.py:356
  28.2 2.0 %collective-permute-start.12 = (bf16[336,768]{1,0:T(8,128)(2,1)S(1)}, bf16[336,768]{1,0:T(8,128)(2,1)S(1)}, u32[]{:S(2)}, u32[]{:S(2)}) collective-permute-start(bf16[336,768]{1,0:T(8,128)(2,1)S(1)} %collective-permute-done.4.second), channel_id=1, source_target_pairs={{0,1},{1,0},{2,3},{3,2},{4,5},{5,4},{6,7},{7,6},{8,9},{9,8},{10,11... | collective-permute-start | bytes 1548296 | tf_op jit(solution)/shard_map/ppermute | solution.py:371
  32.3 1.2 %collective-permute-start.13 = (f32[1,640]{1,0:T(1,128)S(1)}, f32[1,640]{1,0:T(1,128)S(1)}, u32[]{:S(2)}, u32[]{:S(2)}) collective-permute-start(f32[1,640]{1,0:T(1,128)S(1)} %get-tuple-element.59), channel_id=1, source_target_pairs={{0,1},{1,0},{2,3},{3,2},{4,5},{5,4},{6,7},{7,6},{8,9},{9,8},{10,11... | collective-permute-start | bytes 7688 | tf_op jit(solution)/shard_map/ppermute | solution.py:385
  33.5 7.5 %collective-permute-start.14 = (f32[1,640]{1,0:T(1,128)S(1)}, f32[1,640]{1,0:T(1,128)S(1)}, u32[]{:S(2)}, u32[]{:S(2)}) collective-permute-start(f32[1,640]{1,0:T(1,128)S(1)} %max.24), channel_id=1, source_target_pairs={{2,6},{4,0},{6,4},{1,7},{3,1},{5,3},{10,14},{12,8},{14,12},{9,15},... | collective-permute-start | bytes 7688 | tf_op jit(solution)/shard_map/ppermute | solution.py:389
  34.8 6.3 %collective-permute-start.15 = (f32[1,320]{1,0:T(1,128)S(1)}, f32[1,320]{1,0:T(1,128)S(1)}, u32[]{:S(2)}, u32[]{:S(2)}) collective-permute-start(f32[1,320]{1,0:T(1,128)S(1)} %get-tuple-element.65), channel_id=1, source_target_pairs={{0,9},{1,16},{2,11},{3,18},{4,13},{5,20},{6,15},{7,22},{8,1},{9,24... | collective-permute-start | bytes 3848 | tf_op jit(solution)/shard_map/ppermute | solution.py:396
  38.3 3.0 %collective-permute-start.16 = (f32[1,320]{1,0:T(1,128)S(1)}, f32[1,320]{1,0:T(1,128)S(1)}, u32[]{:S(2)}, u32[]{:S(2)}) collective-permute-start(f32[1,320]{1,0:T(1,128)S(1)} %get-tuple-element.66), channel_id=1, source_target_pairs={{0,17},{1,8},{2,19},{3,10},{4,21},{5,12},{6,23},{7,14},{8,25},{9,0... | collective-permute-start | bytes 3848 | tf_op jit(solution)/shard_map/ppermute | solution.py:396
  38.4 3.9 %collective-permute-start.17 = (f32[1,320]{1,0:T(1,128)S(1)}, f32[1,320]{1,0:T(1,128)S(1)}, u32[]{:S(2)}, u32[]{:S(2)}) collective-permute-start(f32[1,320]{1,0:T(1,128)S(1)} %get-tuple-element.67), channel_id=1, source_target_pairs={{0,25},{1,24},{2,27},{3,26},{4,29},{5,28},{6,31},{7,30},{8,17},{9,... | collective-permute-start | bytes 3848 | tf_op jit(solution)/shard_map/ppermute | solution.py:396
  41.1 1.2 %collective-permute-start.18 = (f32[1,320]{1,0:T(1,128)S(1)}, f32[1,320]{1,0:T(1,128)S(1)}, u32[]{:S(2)}, u32[]{:S(2)}) collective-permute-start(f32[1,320]{1,0:T(1,128)S(1)} %fusion), channel_id=1, source_target_pairs={{0,1},{1,0},{2,3},{3,2},{4,5},{5,4},{6,7},{7,6},{8,9},{9,8},{10,11... | collective-permute-start | bytes 3848 | tf_op jit(solution)/shard_map/ppermute | solution.py:400
